TPU v7x, 32 devices: a whole 2x2x4 slice. The times are simulated.
32 devices in a mesh: parts: 2 (over y), tensor: 4 (over z), example: 2 (over x), test: 2 (over core).
Axes of the slice: x: 2, y: 2, z: 4, core: 2. Of those that a mesh axis runs over, the one named last changes fastest.
Arguments:
- activations: bfloat16 [8, 128, 5120], P(('parts', 'example'), None, 'tensor'), parts along dimension 0, may hold values from -6 to 6
- out_grad: bfloat16 [8, 128, 5120], P(('parts', 'example'), None, 'tensor'), parts along dimension 0, may hold values from -6 to 6
- w_gate: bfloat16 [5120, 16384], P(('example', 'test'), 'tensor'), may hold values from -0.078125 to 0.078125
- w_up: bfloat16 [5120, 16384], P(('example', 'test'), 'tensor'), may hold values from -0.078125 to 0.078125
- w_down: bfloat16 [16384, 5120], P('tensor', ('example', 'test')), may hold values from -0.046875 to 0.046875
- proj_model: bfloat16 [5120, 192], P('tensor'), may hold values from -0.078125 to 0.078125
- proj_hidden: bfloat16 [16384, 192], P('tensor'), may hold values from -0.046875 to 0.046875
- test_grads: bfloat16 [3, 64, 64, 1024], P(None, 'tensor', None, 'test'), may hold values from -0.0048828125 to 0.0048828125
- lengths: int32 [8], P(('parts', 'example')), parts along dimension 0, may hold values from 1 to 128, as said below
- groups: int32 [8], P(('parts', 'example')), parts along dimension 0, may hold values from 0 to 3, as said below
Outputs:
- scores: float32 [8, 1024], P(('parts', 'example'), 'test'), parts along dimension 0
- group_scores: float32 [8, 1024], P('parts', 'test'), parts along dimension 0
There are 2 independent parts, one for each index of `parts`. A program takes and returns all parts, laid end to end along the dimension named above; an argument that names none is the same for every part. Nothing has to cross between parts.
Inputs may be any that keep to these rules, and one draw needn't show every extreme that they name: `lengths`: at least one example of each draw has all 128 tokens valid. At least two different groups occur in each draw.
All inputs are finite; a program needn't handle non-finite values.
Results may differ from a plain program's by a relative error of at most 0.003.
Values may be sent and summed in bfloat16 or wider, within the bound.
No kernel may reach another device: no remote copies, remote signals or barrier semaphores. Data moves between devices by JAX's collectives and lax.ppermute only.
A program may use at most 256 MiB of HBM per device.

v0:
```python
import jax
import jax.numpy as jnp
from jax import lax
from jax.sharding import PartitionSpec as P

NGROUP = 4


def fold_gate_up(model_rows, pieces):
    return (
        jnp.dot(model_rows, pieces[0], preferred_element_type=jnp.float32),
        jnp.dot(model_rows, pieces[1], preferred_element_type=jnp.float32),
    )


def fold_down(model_rows, weight_piece):
    return lax.dot_general(
        model_rows, weight_piece, (((1,), (1,)), ((), ())), preferred_element_type=jnp.float32
    )


def on_device(
    activations,
    out_grad,
    w_gate,
    w_up,
    w_down,
    proj_model,
    proj_hidden,
    test_grads,
    lengths,
    groups,
):
    ex_loc, seq_len, d_local = activations.shape
    tok_rows = ex_loc * seq_len
    proj_width = proj_model.shape[1] // 3
    flat_acts = activations.reshape(tok_rows, d_local)
    flat_grad = out_grad.reshape(tok_rows, d_local)
    acts_full, grad_full = (
        lax.all_gather(flat_acts, "tensor", axis=1, tiled=True),
        lax.all_gather(flat_grad, "tensor", axis=1, tiled=True),
    )
    n_cores = lax.axis_size("test")
    core_index = lax.axis_index("test")
    hid_part = w_gate.shape[1] // n_cores
    d_part = d_local // n_cores
    gate_rows, up_rows = (
        lax.all_to_all(w_gate, "test", split_axis=1, concat_axis=0, tiled=True),
        lax.all_to_all(w_up, "test", split_axis=1, concat_axis=0, tiled=True),
    )
    gate_act, up_act = fold_gate_up(
        acts_full,
        (
            lax.all_gather(gate_rows, "example", axis=0, tiled=True),
            lax.all_gather(up_rows, "example", axis=0, tiled=True),
        ),
    )
    down_cols = lax.all_to_all(w_down, "test", split_axis=0, concat_axis=1, tiled=True)
    d_hidden = fold_down(grad_full, lax.all_gather(down_cols, "example", axis=1, tiled=True))
    hid_proj = lax.dynamic_slice_in_dim(proj_hidden, core_index * hid_part, hid_part, 0)
    acts_cols = lax.dynamic_slice_in_dim(flat_acts, core_index * d_part, d_part, 1)
    grad_cols = lax.dynamic_slice_in_dim(flat_grad, core_index * d_part, d_part, 1)
    model_proj = lax.dynamic_slice_in_dim(proj_model, core_index * d_part, d_part, 0)
    sigmoid_gate = jax.nn.sigmoid(gate_act)
    silu_gate = gate_act * sigmoid_gate
    hidden = (silu_gate * up_act).astype(jnp.bfloat16)
    d_gate = (d_hidden * up_act * sigmoid_gate * (1.0 + gate_act * (1.0 - sigmoid_gate))).astype(
        jnp.bfloat16
    )
    d_up = (d_hidden * silu_gate).astype(jnp.bfloat16)
    in_model = jnp.dot(
        acts_cols, model_proj[:, : 2 * proj_width], preferred_element_type=jnp.float32
    )
    out_model = jnp.dot(
        grad_cols, model_proj[:, 2 * proj_width :], preferred_element_type=jnp.float32
    )
    in_hidden = jnp.dot(hidden, hid_proj[:, 2 * proj_width :], preferred_element_type=jnp.float32)
    out_gate = jnp.dot(d_gate, hid_proj[:, :proj_width], preferred_element_type=jnp.float32)
    out_up = jnp.dot(
        d_up, hid_proj[:, proj_width : 2 * proj_width], preferred_element_type=jnp.float32
    )
    inputs_part = jnp.concatenate([in_model, in_hidden], 1)
    outputs_part = jnp.concatenate([out_gate, out_up, out_model], 1)
    inputs_part, outputs_part = lax.psum((inputs_part, outputs_part), "test")
    k_share = proj_width // lax.axis_size("tensor")
    inputs_sum, outputs_all = lax.psum((inputs_part, outputs_part), "tensor")
    outputs_mine = lax.dynamic_slice_in_dim(
        outputs_all.reshape(tok_rows, 3, proj_width), lax.axis_index("tensor") * k_share, k_share, 2
    )
    inputs_sum = inputs_sum.reshape(ex_loc, seq_len, 3, proj_width)
    outputs_mine = outputs_mine.reshape(ex_loc, seq_len, 3, k_share)
    positions = jnp.arange(seq_len, dtype=jnp.int32)
    token_mask = (positions[None, :] < lengths[:, None]).astype(jnp.float32)
    example_grads = jnp.einsum(
        "bsli,bslj->blij",
        outputs_mine * token_mask[:, :, None, None],
        inputs_sum,
        precision=lax.Precision.HIGHEST,
    )
    partial_scores = jnp.einsum(
        "blij,lijn->bn",
        example_grads,
        test_grads.astype(jnp.float32),
        precision=lax.Precision.HIGHEST,
    )
    group_onehot = (groups[:, None] == jnp.arange(NGROUP, dtype=jnp.int32)[None, :]).astype(
        jnp.float32
    )
    scores = lax.psum(partial_scores, "tensor")
    group_scores = lax.psum(
        jnp.dot(group_onehot.T, scores, precision=lax.Precision.HIGHEST), "example"
    )
    return (scores, group_scores)


def solution(mesh):
    placed = (
        P(("parts", "example"), None, "tensor"),
        P(("parts", "example"), None, "tensor"),
        P(("example", "test"), "tensor"),
        P(("example", "test"), "tensor"),
        P("tensor", ("example", "test")),
        P("tensor", None),
        P("tensor", None),
        P(None, "tensor", None, "test"),
        P(("parts", "example")),
        P(("parts", "example")),
    )
    return jax.shard_map(
        on_device,
        mesh=mesh,
        in_specs=placed,
        out_specs=(P(("parts", "example"), "test"), P("parts", "test")),
        check_vma=False,
    )
```

profile of v0, /device:TPU:0, one launch (start us, length us, event | category | flops | bytes accessed | tf_op | source)
XLA Modules:
  0.0 968.8 jit_solution(12904874922844044041)
XLA Ops:
  7.2 0.0 all-gather.10.cloned.1.call-start
  7.2 0.7 all-gather.10.cloned.1.call-update
  7.9 0.0 all-gather.14.cloned.1.call-start
  8.0 14.6 %copy.25 = bf16[1280,4096]{0,1:T(8,128)(2,1)} copy(bf16[1280,4096]{1,0:T(8,128)(2,1)} %param.12) | data formatting | bytes 20971520 | tf_op args[2]
  22.5 21.8 %all_to_all.57 = bf16[1280,2,2048]{0,2,1:T(8,128)(2,1)} all-to-all(bf16[1280,2,2048]{0,2,1:T(8,128)(2,1)} %bitcast.36), channel_id=1, replica_groups=mesh['parts'=2,'tensor'=4,'example'=2,'test'=2] {'test'}, dimensions={1} | all-to-all | bytes 20971520 | tf_op jit(solution)/shard_map/all_to_all | solution.py:48
  44.3 14.5 %copy.26 = bf16[2,1280,2048]{2,1,0:T(8,128)(2,1)} copy(bf16[2,1280,2048]{1,2,0:T(8,128)(2,1)} %bitcast.34) | data formatting | bytes 20971520 | tf_op jit(solution)/shard_map/all_to_all | solution.py:48
  58.8 0.0 all-gather.14.cloned.1.call-update
  58.8 0.0 all-gather.12.cloned.1.call-start
  58.9 14.4 %copy.23 = bf16[1280,4096]{0,1:T(8,128)(2,1)} copy(bf16[1280,4096]{1,0:T(8,128)(2,1)} %param.13) | data formatting | bytes 20971520 | tf_op args[3]
  73.2 22.6 %all_to_all.58 = bf16[1280,2,2048]{0,2,1:T(8,128)(2,1)} all-to-all(bf16[1280,2,2048]{0,2,1:T(8,128)(2,1)} %bitcast.37), channel_id=1, replica_groups=mesh['parts'=2,'tensor'=4,'example'=2,'test'=2] {'test'}, dimensions={1} | all-to-all | bytes 20971520 | tf_op jit(solution)/shard_map/all_to_all | solution.py:49
  95.8 14.6 %copy.24 = bf16[2,1280,2048]{2,1,0:T(8,128)(2,1)} copy(bf16[2,1280,2048]{1,2,0:T(8,128)(2,1)} %bitcast.35) | data formatting | bytes 20971520 | tf_op jit(solution)/shard_map/all_to_all | solution.py:49
  110.5 0.0 all-gather.12.cloned.1.call-update
  110.5 0.0 all-gather.6.cloned.1.call-start
  110.5 0.5 all-gather.6.cloned.1.call-update
  111.1 0.0 all-gather.8.cloned.1.call-start
  111.1 21.8 %all_to_all.59 = bf16[2,2048,1280]{2,1,0:T(8,128)(2,1)} all-to-all(bf16[2,2048,1280]{2,1,0:T(8,128)(2,1)} %bitcast.39), channel_id=1, replica_groups=mesh['parts'=2,'tensor'=4,'example'=2,'test'=2] {'test'}, dimensions={0} | all-to-all | bytes 20971520 | tf_op jit(solution)/shard_map/all_to_all | solution.py:58
  132.9 14.4 %copy.22 = bf16[2048,2,1280]{0,2,1:T(8,128)(2,1)} copy(bf16[2048,2,1280]{2,0,1:T(8,128)(2,1)} %bitcast.38) | data formatting | bytes 20971520 | tf_op jit(solution)/shard_map/all_to_all | solution.py:58
  147.3 0.0 all-gather.8.cloned.1.call-update
  147.4 0.0 all-reduce.7.cloned.1.call-start
  147.4 1.2 fusion.13
  148.6 1.3 fusion.11
  149.9 0.0 all-gather.10.cloned.1.call-done
  149.9 164.9 %all-gather.14.cloned.1.call-done = bf16[5120,2048]{1,0:T(8,128)(2,1)} async-done(((bf16[2560,2048]{1,0:T(8,128)(2,1)}), bf16[5120,2048]{1,0:T(8,128)(2,1)}) %all-gather.14.cloned.1.call-update) | async-done | bytes 20971536 | tf_op jit(solution)/shard_map/all_gather | solution.py:54
  314.9 11.8 %fusion.35 = f32[256,2048]{1,0:T(8,128)} fusion(bf16[256,5120]{1,0:T(8,128)(2,1)} %all-gather.10.cloned.1.call-done, bf16[5120,2048]{1,0:T(8,128)(2,1)} %all-gather.14.cloned.1.call-done), kind=kOutput, calls=%fused_computation.40 | convolution fusion | flops 5368709120 | bytes 25690112 | tf_op jit(solution)/shard_map/dot_general | solution.py:11
  326.7 237.1 %all-gather.12.cloned.1.call-done = bf16[5120,2048]{1,0:T(8,128)(2,1)} async-done(((bf16[2560,2048]{1,0:T(8,128)(2,1)}), bf16[5120,2048]{1,0:T(8,128)(2,1)}) %all-gather.12.cloned.1.call-update) | async-done | bytes 20971536 | tf_op jit(solution)/shard_map/all_gather | solution.py:55
  563.8 10.7 %fusion.34 = f32[256,2048]{1,0:T(8,128)S(1)} fusion(bf16[256,5120]{1,0:T(8,128)(2,1)} %all-gather.10.cloned.1.call-done, bf16[5120,2048]{1,0:T(8,128)(2,1)} %all-gather.12.cloned.1.call-done), kind=kOutput, calls=%fused_computation.39 | convolution fusion | flops 5368709120 | bytes 25690112 | tf_op jit(solution)/shard_map/dot_general | solution.py:12
  574.6 1.3 copy-done.6
  576.0 1.7 fusion.7
  577.6 42.5 %all-gather.6.cloned.1.call-done = bf16[256,5120]{1,0:T(8,128)(2,1)} async-done(((bf16[256,1280]{1,0:T(8,128)(2,1)}), bf16[256,5120]{1,0:T(8,128)(2,1)}) %all-gather.6.cloned.1.call-update) | async-done | bytes 2621456 | tf_op jit(solution)/shard_map/all_gather | solution.py:41
  620.1 247.6 %all-gather.8.cloned.1.call-done = bf16[2048,5120]{0,1:T(8,128)(2,1)} async-done(((bf16[2048,2560]{0,1:T(8,128)(2,1)}), bf16[2048,5120]{0,1:T(8,128)(2,1)}) %all-gather.8.cloned.1.call-update) | async-done | bytes 20971536 | tf_op jit(solution)/shard_map/all_gather | solution.py:59
  867.7 10.7 %fusion.33 = f32[256,2048]{1,0:T(8,128)S(1)} fusion(bf16[256,5120]{1,0:T(8,128)(2,1)} %all-gather.6.cloned.1.call-done, bf16[2048,5120]{0,1:T(8,128)(2,1)} %all-gather.8.cloned.1.call-done), kind=kOutput, calls=%fused_computation.38 | convolution fusion | flops 5368709120 | bytes 25690112 | tf_op jit(solution)/shard_map/dot_general | solution.py:17
  878.5 1.9 fusion.8
  880.4 1.7 fusion.6
  882.0 0.8 pad_maximum_fusion
  882.8 0.0 all-reduce.7.cloned.1.call-update
  882.8 0.0 all-reduce.5.cloned.1.call-start
  882.9 18.6 %all-reduce.7.cloned.1.call-done = (f32[256,192]{0,1:T(8,128)}, f32[256,192]{0,1:T(8,128)}) async-done(((f32[256,192]{0,1:T(8,128)}, f32[256,192]{0,1:T(8,128)}), (f32[256,192]{0,1:T(8,128)}, f32[256,192]{0,1:T(8,128)})) %all-reduce.7.cloned.1.call-update) | async-done | bytes 393232 | tf_op jit(solution)/shard_map/psum | solution.py:84
  901.5 1.0 reshape.55
  902.6 0.7 copy.27
  903.3 0.0 all-reduce.5.cloned.1.call-update
  903.3 0.1 compare_convert_fusion
  903.4 39.0 %all-reduce.5.cloned.1.call-done = (f32[2,128,3,64]{1,3,2,0:T(8,128)}, f32[256,3,64]{0,2,1:T(8,128)}) async-done(((f32[2,128,3,64]{1,3,2,0:T(8,128)}, f32[256,3,64]{0,2,1:T(8,128)}), (f32[2,128,3,64]{1,3,2,0:T(8,128)}, f32[256,3,64]{0,2,1:T(8,128)})) %all-reduce.5.cloned.1.call-update) | async-done | bytes 393232 | tf_op jit(solution)/shard_map/psum | solution.py:86
  942.4 0.8 constant_dynamic-slice_fusion
  943.2 1.3 fusion.21
  944.6 1.4 fusion.3
  946.0 10.2 %psum.46 = f32[2,512]{1,0:T(2,128)S(1)} all-reduce(f32[2,512]{1,0:T(2,128)S(1)} %fusion.3), channel_id=1, replica_groups=mesh['parts'=2,'tensor'=4,'example'=2,'test'=2] {'tensor'}, use_global_device_ids=true, to_apply=%region_4.0 | all-reduce | flops 1024 | bytes 8192 | tf_op jit(solution)/shard_map/psum | solution.py:109
  956.2 0.3 fusion.23
  956.4 5.6 psum.47
  (18 shorter events, 0.1 us)
Async XLA Ops:
  7.2 937.4 %copy-start = (bf16[3,16,64,512]{3,2,1,0:T(8,128)(2,1)S(1)}, bf16[3,16,64,512]{3,2,1,0:T(8,128)(2,1)}, u32[]{:S(2)}) copy-start(bf16[3,16,64,512]{3,2,1,0:T(8,128)(2,1)} %param.17) | copy-start | bytes 9437188
  7.2 142.7 %all-gather.10.cloned.1.call-start = ((), (), s32[]{:S(2)}) async-start(), calls=%async_computation.5 | async-start | bytes 3276800 | tf_op jit(solution)/shard_map/all_gather | solution.py:40
  7.9 307.0 %all-gather.14.cloned.1.call-start = ((), (), s32[]{:S(2)}) async-start(), calls=%async_computation.7 | async-start | bytes 31457280 | tf_op jit(solution)/shard_map/all_gather | solution.py:54
  58.8 505.0 %all-gather.12.cloned.1.call-start = ((), (), s32[]{:S(2)}) async-start(), calls=%async_computation.6 | async-start | bytes 31457280 | tf_op jit(solution)/shard_map/all_gather | solution.py:55
  110.5 509.6 %all-gather.6.cloned.1.call-start = ((), (), s32[]{:S(2)}) async-start(), calls=%async_computation.3 | async-start | bytes 3276800 | tf_op jit(solution)/shard_map/all_gather | solution.py:41
  111.1 756.6 %all-gather.8.cloned.1.call-start = ((), (), s32[]{:S(2)}) async-start(), calls=%async_computation.4 | async-start | bytes 31457280 | tf_op jit(solution)/shard_map/all_gather | solution.py:59
  147.4 754.2 %all-reduce.7.cloned.1.call-start = ((), (), s32[]{:S(2)}) async-start(), calls=%async_computation.9 | async-start | bytes 786432 | tf_op jit(solution)/shard_map/psum | solution.py:84
  563.8 12.1 %copy-start.4 = (f32[256,2048]{1,0:T(8,128)S(1)}, f32[256,2048]{1,0:T(8,128)}, u32[]{:S(2)}) copy-start(f32[256,2048]{1,0:T(8,128)} %fusion.35) | copy-start | bytes 6291460
  574.6 1.4 copy-start.6
  867.7 10.8 %copy-start.5 = (f32[256,2048]{1,0:T(8,128)S(1)}, f32[256,2048]{1,0:T(8,128)}, u32[]{:S(2)}) copy-start(f32[256,2048]{1,0:T(8,128)} %fusion.35) | copy-start | bytes 6291460
  867.7 10.8 %copy-start.7 = (f32[256,2048]{1,0:T(8,128)S(1)}, f32[256,2048]{1,0:T(8,128)}, u32[]{:S(2)}) copy-start(f32[256,2048]{1,0:T(8,128)} %copy-done.6) | copy-start | bytes 6291460
  882.0 21.3 %copy-start.2 = (s32[2]{0:T(128)S(1)}, s32[2]{0:T(128)}, u32[]{:S(2)}) copy-start(s32[2]{0:T(128)} %param.18) | copy-start | bytes 28
  882.8 59.5 %all-reduce.5.cloned.1.call-start = ((), (), s32[]{:S(2)}) async-start(), calls=%async_computation.8 | async-start | bytes 786432 | tf_op jit(solution)/shard_map/psum | solution.py:86
  903.3 52.9 %copy-start.3 = (s32[2]{0:T(128)S(1)}, s32[2]{0:T(128)}, u32[]{:S(2)}) copy-start(s32[2]{0:T(128)} %param.19) | copy-start | bytes 28
  956.2 5.8 copy-start.1
Sparse Core Ops, SparseCore 0:
  9.6 57.4 all-gather.9
  68.6 246.1 all-gather.13
  316.4 247.3 all-gather.11
  565.3 54.8 all-gather.5
  621.5 246.1 all-gather.7
  883.0 18.5 all-reduce.6
  904.1 38.2 all-reduce.4
where the time goes:
time: 972 us; the launch traced here: 969 us
  waiting for transfers between devices  751 us (77%)
  blocking collectives  81.9 us (8%)
  local copies, waits for them, and re-layouts  76.4 us (8%)
  matrix products  44 us (5%)
  between operations  14.3 us (1%)
    all_gather x1, waiting for transfers between devices, on_device(): lax.all_gather(down_cols, 'example', axis=1, tiled=True)  248 us
    all_gather x1, waiting for transfers between devices, on_device(): lax.all_gather(up_rows, 'example', axis=0, tiled=True)  237 us
    all_gather x1, waiting for transfers between devices, on_device(): lax.all_gather(gate_rows, 'example', axis=0, tiled=True)  165 us
    all_gather x1, waiting for transfers between devices, on_device(): lax.all_gather(flat_grad, 'tensor', axis=1, tiled=True)  42.5 us
    psum x1, waiting for transfers between devices, on_device(): inputs_sum, outputs_all = lax.psum((inputs_part, outputs_part), 'tensor')  39 us
    unnamed x19, local copies, waits for them, and re-layouts  30.3 us
    all_to_all x1, blocking collectives, on_device(): lax.all_to_all(w_up, 'test', split_axis=1, concat_axis=0, tiled=True)  22.6 us
    all_to_all x1, blocking collectives, on_device(): lax.all_to_all(w_gate, 'test', split_axis=1, concat_axis=0, tiled=True)  21.8 us
  transfers between devices with their start and end apart: 7, of which 6 were waited for; matrix products, arithmetic and copies ran while one was open for 10% of the time, Pallas kernels for 0%

commit v1 on v0

v1 whole, which is shorter than its diff:
```python
import jax
import jax.numpy as jnp
from jax import lax
from jax.sharding import PartitionSpec as P

NGROUP = 4
F32 = jnp.float32
SEND_SCALE = 16.0


def shift(value, axis, step):
    n = lax.axis_size(axis)
    return lax.ppermute(value, axis, [(i, (i + step) % n) for i in range(n)])


def pack(value):
    return (value * SEND_SCALE).astype(jnp.float16)


def unpack(value):
    return value.astype(F32) * (1.0 / SEND_SCALE)


def gather_in_order(value, axis):
    n = lax.axis_size(axis)
    if n == 1:
        return value[None]
    if n > 8:
        return lax.all_gather(value, axis, axis=0)
    got = [shift(value, axis, step) for step in range(n - 1, 0, -1)] + [value]
    return lax.dynamic_slice_in_dim(
        jnp.stack(got + got), n - 1 - lax.axis_index(axis), n, 0
    )


def scatter_sum(value, axis, dim):
    n = lax.axis_size(axis)
    if n > 8:
        return lax.psum_scatter(value, axis, scatter_dimension=dim, tiled=True)
    me = lax.axis_index(axis)
    width = value.shape[dim] // n
    total = lax.dynamic_slice_in_dim(value, me * width, width, dim)
    for step in range(1, n):
        block = lax.dynamic_slice_in_dim(value, lax.rem(me + step, n) * width, width, dim)
        total = total + shift(block, axis, step)
    return total


def on_device(
    activations,
    out_grad,
    w_gate,
    w_up,
    w_down,
    proj_model,
    proj_hidden,
    test_grads,
    lengths,
    groups,
):
    ex_loc, seq_len, d_local = activations.shape
    tok_rows = ex_loc * seq_len
    width = proj_model.shape[1] // 3
    n_cores = lax.axis_size("test")
    core = lax.axis_index("test")
    n_ex = lax.axis_size("example")
    ex_index = lax.axis_index("example")
    hid_part = w_gate.shape[1] // n_cores
    rows_part = tok_rows // n_cores
    flat_acts = activations.reshape(tok_rows, d_local)
    flat_grad = out_grad.reshape(tok_rows, d_local)

    def features_here(flat):
        mine = lax.dynamic_slice_in_dim(flat, core * rows_part, rows_part, 0)
        whole = lax.all_gather(mine, "tensor", axis=1, tiled=True)
        return lax.all_to_all(whole, ("example", "test"), split_axis=1, concat_axis=0, tiled=True)

    acts_here = features_here(flat_acts)
    grad_here = features_here(flat_grad)

    def core_sum(product):
        kept = lax.dynamic_slice_in_dim(product, core * hid_part, hid_part, 1)
        for step in range(1, n_cores):
            to = lax.rem(core + step, n_cores)
            sent = pack(lax.dynamic_slice_in_dim(product, to * hid_part, hid_part, 1))
            kept = kept + unpack(shift(sent, "test", step))
        return kept

    def rows_of(tokens, owner):
        return lax.dynamic_slice_in_dim(tokens, owner * tok_rows, tok_rows, 0)

    def forward(tokens, weight):
        return jnp.dot(tokens, weight, preferred_element_type=F32)

    def backward(tokens, weight):
        return lax.dot_general(tokens, weight, (((1,), (1,)), ((), ())), preferred_element_type=F32)

    jobs = (
        (forward, acts_here, w_gate),
        (forward, acts_here, w_up),
        (backward, grad_here, w_down),
    )
    arrived = [[], [], []]
    for step in range(1, n_ex):
        owner = lax.rem(ex_index + step, n_ex)
        for place, (product, tokens, weight) in enumerate(jobs):
            partial = core_sum(product(rows_of(tokens, owner), weight))
            arrived[place].append(shift(pack(partial), "example", step))
    own = [
        core_sum(product(rows_of(tokens, ex_index), weight)) for product, tokens, weight in jobs
    ]
    for place in range(3):
        for received in arrived[place]:
            own[place] = own[place] + unpack(received)
    gate_act, up_act, d_hidden = own

    model_part = jnp.concatenate(
        [
            jnp.dot(flat_acts, proj_model[:, : 2 * width], preferred_element_type=F32),
            jnp.dot(flat_grad, proj_model[:, 2 * width :], preferred_element_type=F32),
        ],
        1,
    )
    model_sum = lax.psum(model_part, "tensor")

    sigmoid_gate = jax.nn.sigmoid(gate_act)
    silu_gate = gate_act * sigmoid_gate
    hidden = (silu_gate * up_act).astype(jnp.bfloat16)
    d_gate = (d_hidden * up_act * sigmoid_gate * (1.0 + gate_act * (1.0 - sigmoid_gate))).astype(
        jnp.bfloat16
    )
    d_up = (d_hidden * silu_gate).astype(jnp.bfloat16)
    hid_proj = lax.dynamic_slice_in_dim(proj_hidden, core * hid_part, hid_part, 0)
    out_gate = jnp.dot(d_gate, hid_proj[:, :width], preferred_element_type=F32)
    out_up = jnp.dot(d_up, hid_proj[:, width : 2 * width], preferred_element_type=F32)
    in_hidden = jnp.dot(hidden, hid_proj[:, 2 * width :], preferred_element_type=F32)

    positions = jnp.arange(seq_len, dtype=jnp.int32)
    token_mask = (positions[None, :] < lengths[:, None]).astype(F32)[:, :, None]
    model_sum = model_sum.reshape(ex_loc, seq_len, 3, width)

    def outer(outputs, inputs):
        return jnp.einsum(
            "bsi,bsj->bij", outputs * token_mask, inputs, precision=lax.Precision.HIGHEST
        )

    grads_part = jnp.stack(
        [
            outer(out_gate.reshape(ex_loc, seq_len, width), model_sum[:, :, 0]),
            outer(out_up.reshape(ex_loc, seq_len, width), model_sum[:, :, 1]),
            outer(model_sum[:, :, 2], in_hidden.reshape(ex_loc, seq_len, width)),
        ],
        1,
    )
    grads_half = scatter_sum(grads_part, "tensor", 2)
    grads_mine = grads_half
    for step in range(1, n_cores):
        grads_mine = grads_mine + shift(grads_half, "test", step)
    partial_scores = jnp.einsum(
        "blij,lijn->bn",
        grads_mine,
        test_grads.astype(F32),
        precision=lax.Precision.HIGHEST,
    )
    scores = jnp.sum(gather_in_order(partial_scores, "tensor"), 0)
    group_onehot = (groups[:, None] == jnp.arange(NGROUP, dtype=jnp.int32)[None, :]).astype(F32)
    group_part = jnp.dot(group_onehot.T, scores, precision=lax.Precision.HIGHEST)
    group_scores = jnp.sum(gather_in_order(group_part, "example"), 0)
    return (scores, group_scores)


def solution(mesh):
    placed = (
        P(("parts", "example"), None, "tensor"),
        P(("parts", "example"), None, "tensor"),
        P(("example", "test"), "tensor"),
        P(("example", "test"), "tensor"),
        P("tensor", ("example", "test")),
        P("tensor", None),
        P("tensor", None),
        P(None, "tensor", None, "test"),
        P(("parts", "example")),
        P(("parts", "example")),
    )
    return jax.shard_map(
        on_device,
        mesh=mesh,
        in_specs=placed,
        out_specs=(P(("parts", "example"), "test"), P("parts", "test")),
        check_vma=False,
    )
```

time: 972 us -> 258 us (0.27)
  waiting for transfers between devices: 751 us -> 138 us
  blocking collectives: 81.9 us -> 0 us
  local copies, waits for them, and re-layouts: 76.4 us -> 13.8 us
  starting transfers between devices: 0.28 us -> 23.5 us
  matrix products: 44 us -> 58.9 us
    all_gather x5 -> x2, waiting for transfers between devices: 692 us -> 62.7 us  [features_here(): whole = lax.all_gather(mine, 'tensor', axis=1, tiled=True)]
    ppermute x0 -> x17, waiting for transfers between devices: none -> 74.9 us  [shift(): return lax.ppermute(value, axis, [(i, (i + step) % n) for i in range(n)])]
    all_to_all x3 -> x0, blocking collectives: 66.2 us -> none  [the longest x1 22.6 us: on_device(): lax.all_to_all(w_up, 'test', split_axis=1, concat_axis=0, tiled=True)]
    psum x2 -> x1, waiting for transfers between devices: 57.6 us -> 0.02 us  [on_device(): model_sum = lax.psum(model_part, 'tensor')]
    all_to_all x3 -> x2, local copies, waits for them, and re-layouts: 43.5 us -> 4.83 us  [features_here(): lax.all_to_all(whole, ('example', 'test'), split_axis=1, concat_axis=0, t...]
    unnamed x19 -> x57, local copies, waits for them, and re-layouts: 30.3 us -> 5.95 us
    psum x2 -> x0, blocking collectives: 15.8 us -> none  [the longest x1 10.2 us: on_device(): scores = lax.psum(partial_scores, 'tensor')]
    dot_general x10 -> x15, matrix products: 43.7 us -> 58.6 us  [the longest x4 26.6 us: forward(): return jnp.dot(tokens, weight, preferred_element_type=F32)]
  transfers between devices with their start and end apart: 7 -> 22, of which waited for: 6 -> 13; matrix products, arithmetic and copies ran while one was open for 10% -> 19% of each run, Pallas kernels for 0% -> 0%
where the time goes in v1:
time: 258 us; the launch traced here: 257 us
  waiting for transfers between devices  138 us (53%)
  matrix products  58.9 us (23%)
  starting transfers between devices  23.5 us (9%)
  between operations  14.2 us (6%)
  local copies, waits for them, and re-layouts  13.8 us (5%)
  other arithmetic  8.91 us (3%)
    ppermute x17, waiting for transfers between devices, shift(): return lax.ppermute(value, axis, [(i, (i + step) % n) for i in range(n)])  74.9 us
    all_gather x2, waiting for transfers between devices, features_here(): whole = lax.all_gather(mine, 'tensor', axis=1, tiled=True)  62.7 us
    dot_general x4, matrix products, forward(): return jnp.dot(tokens, weight, preferred_element_type=F32)  26.6 us
    ppermute x17, starting transfers between devices, shift(): return lax.ppermute(value, axis, [(i, (i + step) % n) for i in range(n)])  14.8 us
    dot_general x2, matrix products, backward(): lax.dot_general(tokens, weight, (((1,), (1,)), ((), ())), preferred_eleme...  11.9 us
    all_to_all x2, starting transfers between devices, features_here(): lax.all_to_all(whole, ('example', 'test'), split_axis=1, concat_axis=0, t...  8.59 us
    convert_element_type x9, other arithmetic, pack(): return (value * SEND_SCALE).astype(jnp.float16)  7.31 us
    dot_general x1, matrix products, on_device(): out_gate = jnp.dot(d_gate, hid_proj[:, :width], preferred_element_type=F32)  6.76 us
  transfers between devices with their start and end apart: 22, of which 13 were waited for; matrix products, arithmetic and copies ran while one was open for 19% of the time, Pallas kernels for 0%

profile of v1, /device:TPU:0, one launch (start us, length us, event | category | flops | bytes accessed | tf_op | source)
XLA Modules:
  0.0 257.0 jit_solution(9820273494791947157)
XLA Ops:
  7.2 1.1 constant_dynamic-slice_fusion.3
  8.4 0.9 copy.37
  9.3 1.0 constant_dynamic-slice_fusion.4
  10.4 0.9 copy.36
  11.3 33.7 %all-gather.5.cloned.1.call-done = bf16[128,5120]{0,1:T(8,128)(2,1)} async-done(((bf16[128,1280]{0,1:T(8,128)(2,1)}), bf16[128,5120]{0,1:T(8,128)(2,1)}) %all-gather.5.cloned.1.call-update) | async-done | bytes 1310736 | tf_op jit(solution)/shard_map/all_gather | solution.py:75
  45.0 4.3 %all-to-all-start.1 = ((bf16[128,4,1280]{0,2,1:T(8,128)(2,1)}), bf16[128,4,1280]{0,2,1:T(8,128)(2,1)}, u32[]{:S(2)}, u32[]{:S(2)}) async-start(bf16[128,4,1280]{0,2,1:T(8,128)(2,1)} %bitcast.74), calls=%async_computation.1 | async-start | bytes 2621440 | tf_op jit(solution)/shard_map/all_to_all | solution.py:76
  49.3 29.0 %all-gather.3.cloned.1.call-done = bf16[128,5120]{0,1:T(8,128)(2,1)} async-done(((bf16[128,1280]{0,1:T(8,128)(2,1)}), bf16[128,5120]{0,1:T(8,128)(2,1)}) %all-gather.3.cloned.1.call-update) | async-done | bytes 1310736 | tf_op jit(solution)/shard_map/all_gather | solution.py:75
  78.3 4.3 %all-to-all-start = ((bf16[128,4,1280]{0,2,1:T(8,128)(2,1)}), bf16[128,4,1280]{0,2,1:T(8,128)(2,1)}, u32[]{:S(2)}, u32[]{:S(2)}) async-start(bf16[128,4,1280]{0,2,1:T(8,128)(2,1)} %bitcast.73), calls=%async_computation | async-start | bytes 2621440 | tf_op jit(solution)/shard_map/all_to_all | solution.py:76
  82.7 2.4 copy.26
  85.1 9.1 %fusion.7 = f32[256,4096]{1,0:T(8,128)} fusion(bf16[1280,4096]{1,0:T(8,128)(2,1)} %param.12, bf16[512,1280]{1,0:T(8,128)(2,1)} %bitcast.75, s32[]{:T(128)S(6)} %select_n.26), kind=kOutput, calls=%fused_computation.29 | convolution fusion | flops 2684354560 | bytes 15335428 | tf_op jit(solution)/shard_map/dot_general | solution.py:93
  94.3 8.6 %fusion.9 = f32[256,4096]{1,0:T(8,128)} fusion(bf16[1280,4096]{1,0:T(8,128)(2,1)} %param.13, bf16[512,1280]{1,0:T(8,128)(2,1)S(1)} %bitcast.76, s32[]{:T(128)S(6)} %select_n.26), kind=kOutput, calls=%fused_computation.31 | convolution fusion | flops 2684354560 | bytes 15335428 | tf_op jit(solution)/shard_map/dot_general | solution.py:93
  102.9 4.4 %fusion.11 = f32[256,4096]{1,0:T(8,128)} fusion(bf16[1280,4096]{1,0:T(8,128)(2,1)S(1)} %bitcast.87, bf16[512,1280]{1,0:T(8,128)(2,1)S(1)} %bitcast.77, s32[]{:T(128)S(6)} %select_n.23), kind=kOutput, calls=%fused_computation.33 | convolution fusion | flops 2684354560 | bytes 15335428 | tf_op jit(solution)/shard_map/dot_general | solution.py:93
  107.3 4.4 %fusion.13 = f32[256,4096]{1,0:T(8,128)} fusion(bf16[1280,4096]{1,0:T(8,128)(2,1)S(1)} %bitcast.89, bf16[512,1280]{1,0:T(8,128)(2,1)S(1)} %bitcast.78, s32[]{:T(128)S(6)} %select_n.23), kind=kOutput, calls=%fused_computation.35 | convolution fusion | flops 2684354560 | bytes 15335428 | tf_op jit(solution)/shard_map/dot_general | solution.py:93
  111.8 2.4 copy.24
  114.2 5.9 %fusion.3 = f32[256,4096]{1,0:T(8,128)S(1)} fusion(bf16[4096,1280]{1,0:T(8,128)(2,1)} %param.14, bf16[512,1280]{1,0:T(8,128)(2,1)} %bitcast.79, s32[]{:T(128)S(6)} %select_n.26), kind=kOutput, calls=%fused_computation.25 | convolution fusion | flops 2684354560 | bytes 15335428 | tf_op jit(solution)/shard_map/dot_general | solution.py:96
  120.1 6.0 %fusion.5 = f32[256,4096]{1,0:T(8,128)S(1)} fusion(bf16[4096,1280]{1,0:T(8,128)(2,1)} %param.14, bf16[512,1280]{1,0:T(8,128)(2,1)S(1)} %bitcast.80, s32[]{:T(128)S(6)} %select_n.23), kind=kOutput, calls=%fused_computation.27 | convolution fusion | flops 2684354560 | bytes 15335428 | tf_op jit(solution)/shard_map/dot_general | solution.py:96
  127.1 2.6 %copy-done.1 = f32[256,4096]{1,0:T(8,128)S(1)} copy-done((f32[256,4096]{1,0:T(8,128)S(1)}, f32[256,4096]{1,0:T(8,128)}, u32[]{:S(2)}) %copy-start.1) | copy-done | bytes 4194328
  131.7 0.8 copy-done.9
  132.5 1.2 multiply_convert_fusion.8
  134.0 1.2 multiply_convert_fusion.11
  135.3 1.4 multiply_convert_fusion.9
  136.7 3.2 %collective-permute-start.2 = (f16[256,2048]{1,0:T(8,128)(2,1)}, f16[256,2048]{1,0:T(8,128)(2,1)}, u32[]{:S(2)}, u32[]{:S(2)}) collective-permute-start(f16[256,2048]{1,0:T(8,128)(2,1)} %multiply_convert_fusion.9), channel_id=1, source_target_pairs={{0,2},{2,0},{1,3},{3,1},{4,6},{6,4},{5,7},{7,5},{8,10},{10,8},{9,1... | collective-permute-start | bytes 3145736 | tf_op jit(solution)/shard_map/ppermute | solution.py:13
  140.0 1.4 multiply_convert_fusion.3
  141.4 1.4 multiply_convert_fusion.6
  142.8 2.0 collective-permute-start.5
  145.7 0.7 copy.28
  146.6 17.7 %collective-permute-done.2 = f16[256,2048]{1,0:T(8,128)(2,1)} collective-permute-done((f16[256,2048]{1,0:T(8,128)(2,1)}, f16[256,2048]{1,0:T(8,128)(2,1)}, u32[]{:S(2)}, u32[]{:S(2)}) %collective-permute-start.2) | collective-permute-done | bytes 1048608 | tf_op jit(solution)/shard_map/ppermute | solution.py:13
  164.2 22.5 %collective-permute-done.8 = f16[256,2048]{1,0:T(8,128)(2,1)} collective-permute-done((f16[256,2048]{1,0:T(8,128)(2,1)}, f16[256,2048]{1,0:T(8,128)(2,1)}, u32[]{:S(2)}, u32[]{:S(2)}) %collective-permute-start.8) | collective-permute-done | bytes 1048608 | tf_op jit(solution)/shard_map/ppermute | solution.py:13
  186.7 22.0 %collective-permute-done.5 = f16[256,2048]{1,0:T(8,128)(2,1)} collective-permute-done((f16[256,2048]{1,0:T(8,128)(2,1)}, f16[256,2048]{1,0:T(8,128)(2,1)}, u32[]{:S(2)}, u32[]{:S(2)}) %collective-permute-start.5) | collective-permute-done | bytes 1048608 | tf_op jit(solution)/shard_map/ppermute | solution.py:13
  208.7 6.8 %convolution_bitcast_fusion.5 = f32[8,2,8,128]{3,2,1,0:T(8,128)S(1)} fusion(f16[256,2048]{1,0:T(8,128)(2,1)} %collective-permute-done.2, f16[256,2048]{1,0:T(8,128)(2,1)} %collective-permute-done, f32[256,4096]{1,0:T(8,128)} %copy-done.10, s32[]{:T(128)S(6)} %select_n.24, f16[256,2048]{1,0:T(8,128)(2,1)} %collective-permute-done.5, ...), kind=kOutput, calls=%fused_computation.24 | convolution fusion | flops 81788928 | bytes 12911616 | tf_op jit(solution)/shard_map/dot_general | solution.py:134
  215.5 3.4 %convolution_bitcast_fusion.3 = f32[8,2,8,128]{3,2,1,0:T(8,128)S(1)} fusion(f16[256,2048]{1,0:T(8,128)(2,1)} %collective-permute-done.2, f16[256,2048]{1,0:T(8,128)(2,1)} %collective-permute-done, f32[256,4096]{1,0:T(8,128)S(1)} %copy-done.11, s32[]{:T(128)S(6)} %select_n.24, bf16[4096,192]{0,1:T(8,128)(2,1)} %param.16, s32[]{:T(128)S(6)} %add.149, ...), kind=kOutput, calls=%fused_computation.22 | convolution fusion | flops 76546048 | bytes 8717824 | tf_op jit(solution)/shard_map/dot_general | solution.py:135
  218.9 1.1 convolution_bitcast_fusion.4
  220.0 1.1 convolution_bitcast_fusion.2
  221.1 4.8 %convolution_bitcast_fusion.1 = f32[8,2,8,128]{3,2,1,0:T(8,128)S(1)} fusion(f16[256,2048]{1,0:T(8,128)(2,1)} %collective-permute-done.5, f16[256,2048]{1,0:T(8,128)(2,1)} %collective-permute-done.3, f32[256,4096]{1,0:T(8,128)} %fusion.13, s32[]{:T(128)S(6)} %select_n.24, bf16[4096,192]{0,1:T(8,128)(2,1)} %param.16, s32[]{:T(128)S(6)} %add.150, ...), kind=kOutput, calls=%fused_computation.20 | convolution fusion | flops 76546048 | bytes 8717824 | tf_op jit(solution)/shard_map/dot_general | solution.py:136
  225.9 1.1 convolution_bitcast_fusion
  227.0 1.5 collective-permute-start.10
  228.5 1.7 collective-permute-start.11
  230.5 2.4 collective-permute-done.10
  233.1 3.1 %collective-permute-done.9 = f32[2,3,16,64]{3,2,0,1:T(8,128)} collective-permute-done((f32[2,3,16,64]{3,2,0,1:T(8,128)S(1)}, f32[2,3,16,64]{3,2,0,1:T(8,128)}, u32[]{:S(2)}, u32[]{:S(2)}) %collective-permute-start.9) | collective-permute-done | bytes 24608 | tf_op jit(solution)/shard_map/ppermute | solution.py:13
  236.2 0.8 add_add_fusion
  237.1 1.2 collective-permute-done.12
  238.4 1.4 fusion
  240.0 1.8 collective-permute-start.15
  241.8 1.6 collective-permute-done.13
  243.4 1.0 collective-permute-done.14
  244.4 1.4 collective-permute-done.15
  246.1 1.7 collective-permute-start.16
  247.9 1.9 collective-permute-done.16
  (98 shorter events, 6.5 us)
Async XLA Ops:
  7.2 231.2 %copy-start = (bf16[3,16,64,512]{3,2,1,0:T(8,128)(2,1)S(1)}, bf16[3,16,64,512]{3,2,1,0:T(8,128)(2,1)}, u32[]{:S(2)}) copy-start(bf16[3,16,64,512]{3,2,1,0:T(8,128)(2,1)} %param.17) | copy-start | bytes 9437188
  7.2 37.8 %all-gather.5.cloned.1.call-start = ((), (), s32[]{:S(2)}) async-start(), calls=%async_computation.3 | async-start | bytes 1638400 | tf_op jit(solution)/shard_map/all_gather | solution.py:75
  9.3 69.0 %all-gather.3.cloned.1.call-start = ((), (), s32[]{:S(2)}) async-start(), calls=%async_computation.2 | async-start | bytes 1638400 | tf_op jit(solution)/shard_map/all_gather | solution.py:75
  45.0 33.3 %all-to-all-start.1 = ((bf16[128,4,1280]{0,2,1:T(8,128)(2,1)}), bf16[128,4,1280]{0,2,1:T(8,128)(2,1)}, u32[]{:S(2)}, u32[]{:S(2)}) async-start(bf16[128,4,1280]{0,2,1:T(8,128)(2,1)} %bitcast.74), calls=%async_computation.1 | async-start | bytes 2621440 | tf_op jit(solution)/shard_map/all_to_all | solution.py:76
  78.3 33.4 %all-to-all-start = ((bf16[128,4,1280]{0,2,1:T(8,128)(2,1)}), bf16[128,4,1280]{0,2,1:T(8,128)(2,1)}, u32[]{:S(2)}, u32[]{:S(2)}) async-start(bf16[128,4,1280]{0,2,1:T(8,128)(2,1)} %bitcast.73), calls=%async_computation | async-start | bytes 2621440 | tf_op jit(solution)/shard_map/all_to_all | solution.py:76
  82.6 136.3 %all-reduce.2.cloned.1.call-start = ((), (), s32[]{:S(2)}) async-start(), calls=%async_computation.4 | async-start | bytes 393216 | tf_op jit(solution)/shard_map/psum | solution.py:124
  85.1 9.1 %copy-start.5 = (bf16[4,128,1280]{2,1,0:T(8,128)(2,1)S(1)}, bf16[4,128,1280]{2,1,0:T(8,128)(2,1)}, u32[]{:S(2)}) copy-start(bf16[4,128,1280]{2,1,0:T(8,128)(2,1)} %copy.26) | copy-start | bytes 3932164
  85.1 17.7 %slice-start = ((s8[10485760]{0:T(1024)(128)(4,1)}), s8[4194304]{0:T(1024)(128)(4,1)S(1)}, s32[]{:S(2)}) async-start(s8[10485760]{0:T(1024)(128)(4,1)} %bitcast.86), calls=%async_computation.5 | async-start | bytes 8388608
  85.1 17.7 %slice-start.1 = ((s8[10485760]{0:T(1024)(128)(4,1)}), s8[4194304]{0:T(1024)(128)(4,1)S(1)}, s32[]{:S(2)}) async-start(s8[10485760]{0:T(1024)(128)(4,1)} %bitcast.86), calls=%async_computation.6 | async-start | bytes 8388608
  94.2 8.6 %slice-start.2 = ((s8[10485760]{0:T(1024)(128)(4,1)}), s8[2097152]{0:T(1024)(128)(4,1)S(1)}, s32[]{:S(2)}) async-start(s8[10485760]{0:T(1024)(128)(4,1)} %bitcast.86), calls=%async_computation.7 | async-start | bytes 4194304
  94.2 13.0 %slice-start.3 = ((s8[10485760]{0:T(1024)(128)(4,1)}), s8[4194304]{0:T(1024)(128)(4,1)S(1)}, s32[]{:S(2)}) async-start(s8[10485760]{0:T(1024)(128)(4,1)} %bitcast.88), calls=%async_computation.8 | async-start | bytes 8388608
  94.2 13.0 %slice-start.4 = ((s8[10485760]{0:T(1024)(128)(4,1)}), s8[4194304]{0:T(1024)(128)(4,1)S(1)}, s32[]{:S(2)}) async-start(s8[10485760]{0:T(1024)(128)(4,1)} %bitcast.88), calls=%async_computation.9 | async-start | bytes 8388608
  102.8 4.5 %slice-start.5 = ((s8[10485760]{0:T(1024)(128)(4,1)}), s8[2097152]{0:T(1024)(128)(4,1)S(1)}, s32[]{:S(2)}) async-start(s8[10485760]{0:T(1024)(128)(4,1)} %bitcast.88), calls=%async_computation.10 | async-start | bytes 4194304
  114.2 5.9 %copy-start.6 = (bf16[4,128,1280]{2,1,0:T(8,128)(2,1)S(1)}, bf16[4,128,1280]{2,1,0:T(8,128)(2,1)}, u32[]{:S(2)}) copy-start(bf16[4,128,1280]{2,1,0:T(8,128)(2,1)} %copy.24) | copy-start | bytes 3932164
  120.1 6.7 %copy-start.2 = (f32[256,4096]{1,0:T(8,128)S(1)}, f32[256,4096]{1,0:T(8,128)}, u32[]{:S(2)}) copy-start(f32[256,4096]{1,0:T(8,128)} %fusion.7) | copy-start | bytes 12582916
  126.1 8.0 %copy-start.10 = (f32[256,4096]{1,0:T(8,128)}, f32[256,4096]{1,0:T(8,128)S(1)}, u32[]{:S(2)}) copy-start(f32[256,4096]{1,0:T(8,128)S(1)} %fusion.5) | copy-start | bytes 12582916
  126.1 3.7 %copy-start.1 = (f32[256,4096]{1,0:T(8,128)S(1)}, f32[256,4096]{1,0:T(8,128)}, u32[]{:S(2)}) copy-start(f32[256,4096]{1,0:T(8,128)} %fusion.9) | copy-start | bytes 12582916
  126.3 8.9 %collective-permute-start.1 = (f16[256,2048]{1,0:T(8,128)(2,1)S(1)}, f16[256,2048]{1,0:T(8,128)(2,1)S(1)}, u32[]{:S(2)}, u32[]{:S(2)}) collective-permute-start(f16[256,2048]{1,0:T(8,128)(2,1)S(1)} %multiply_convert_fusion.10), channel_id=1, source_target_pairs={{0,1},{1,0},{2,3},{3,2},{4,5},{5,4},{6,7},{7,6},{8,9},{9,8},{10,11... | collective-permute-start | bytes 3145736 | tf_op jit(solution)/shard_map/ppermute | solution.py:13
  126.8 4.3 %copy-start.7 = (f32[256,4096]{1,0:T(8,128)S(1)}, f32[256,4096]{1,0:T(8,128)}, u32[]{:S(2)}) copy-start(f32[256,4096]{1,0:T(8,128)} %fusion.11) | copy-start | bytes 12582916
  127.0 9.8 %collective-permute-start.7 = (f16[256,2048]{1,0:T(8,128)(2,1)S(1)}, f16[256,2048]{1,0:T(8,128)(2,1)S(1)}, u32[]{:S(2)}, u32[]{:S(2)}) collective-permute-start(f16[256,2048]{1,0:T(8,128)(2,1)S(1)} %multiply_convert_fusion.4), channel_id=1, source_target_pairs={{0,1},{1,0},{2,3},{3,2},{4,5},{5,4},{6,7},{7,6},{8,9},{9,8},{10,11... | collective-permute-start | bytes 3145736 | tf_op jit(solution)/shard_map/ppermute | solution.py:13
  129.8 2.7 %copy-start.9 = (f32[256,4096]{1,0:T(8,128)S(1)}, f32[256,4096]{1,0:T(8,128)}, u32[]{:S(2)}) copy-start(f32[256,4096]{1,0:T(8,128)} %fusion.13) | copy-start | bytes 12582916
  130.0 11.4 %collective-permute-start.4 = (f16[256,2048]{1,0:T(8,128)(2,1)S(1)}, f16[256,2048]{1,0:T(8,128)(2,1)S(1)}, u32[]{:S(2)}, u32[]{:S(2)}) collective-permute-start(f16[256,2048]{1,0:T(8,128)(2,1)S(1)} %multiply_convert_fusion.7), channel_id=1, source_target_pairs={{0,1},{1,0},{2,3},{3,2},{4,5},{5,4},{6,7},{7,6},{8,9},{9,8},{10,11... | collective-permute-start | bytes 3145736 | tf_op jit(solution)/shard_map/ppermute | solution.py:13
  131.2 11.6 %collective-permute-start.6 = (f16[256,2048]{1,0:T(8,128)(2,1)S(1)}, f16[256,2048]{1,0:T(8,128)(2,1)S(1)}, u32[]{:S(2)}, u32[]{:S(2)}) collective-permute-start(f16[256,2048]{1,0:T(8,128)(2,1)S(1)} %multiply_convert_fusion.5), channel_id=1, source_target_pairs={{0,1},{1,0},{2,3},{3,2},{4,5},{5,4},{6,7},{7,6},{8,9},{9,8},{10,11... | collective-permute-start | bytes 3145736 | tf_op jit(solution)/shard_map/ppermute | solution.py:13
  133.6 12.9 %collective-permute-start.3 = (f16[256,2048]{1,0:T(8,128)(2,1)}, f16[256,2048]{1,0:T(8,128)(2,1)}, u32[]{:S(2)}, u32[]{:S(2)}) collective-permute-start(f16[256,2048]{1,0:T(8,128)(2,1)} %multiply_convert_fusion.8), channel_id=1, source_target_pairs={{0,1},{1,0},{2,3},{3,2},{4,5},{5,4},{6,7},{7,6},{8,9},{9,8},{10,11... | collective-permute-start | bytes 3145736 | tf_op jit(solution)/shard_map/ppermute | solution.py:13
  135.2 11.3 %collective-permute-start = (f16[256,2048]{1,0:T(8,128)(2,1)}, f16[256,2048]{1,0:T(8,128)(2,1)}, u32[]{:S(2)}, u32[]{:S(2)}) collective-permute-start(f16[256,2048]{1,0:T(8,128)(2,1)} %multiply_convert_fusion.11), channel_id=1, source_target_pairs={{0,1},{1,0},{2,3},{3,2},{4,5},{5,4},{6,7},{7,6},{8,9},{9,8},{10,11... | collective-permute-start | bytes 3145736 | tf_op jit(solution)/shard_map/ppermute | solution.py:13
  136.7 27.5 %collective-permute-start.2 = (f16[256,2048]{1,0:T(8,128)(2,1)}, f16[256,2048]{1,0:T(8,128)(2,1)}, u32[]{:S(2)}, u32[]{:S(2)}) collective-permute-start(f16[256,2048]{1,0:T(8,128)(2,1)} %multiply_convert_fusion.9), channel_id=1, source_target_pairs={{0,2},{2,0},{1,3},{3,1},{4,6},{6,4},{5,7},{7,5},{8,10},{10,8},{9,1... | collective-permute-start | bytes 3145736 | tf_op jit(solution)/shard_map/ppermute | solution.py:13
  141.4 3.5 %copy-start.3 = (bf16[2,128,1280]{2,1,0:T(8,128)(2,1)S(1)}, bf16[2,128,1280]{2,1,0:T(8,128)(2,1)}, u32[]{:S(2)}) copy-start(bf16[2,128,1280]{2,1,0:T(8,128)(2,1)} %param.11) | copy-start | bytes 1966084
  141.4 3.5 %copy-start.12 = (bf16[1280,192]{0,1:T(8,128)(2,1)S(1)}, bf16[1280,192]{0,1:T(8,128)(2,1)}, u32[]{:S(2)}) copy-start(bf16[1280,192]{0,1:T(8,128)(2,1)} %param.15) | copy-start | bytes 1474564
  141.4 3.8 %copy-start.4 = (bf16[2,128,1280]{2,1,0:T(8,128)(2,1)S(1)}, bf16[2,128,1280]{2,1,0:T(8,128)(2,1)}, u32[]{:S(2)}) copy-start(bf16[2,128,1280]{2,1,0:T(8,128)(2,1)} %param.10) | copy-start | bytes 1966084
  141.4 45.3 %collective-permute-start.8 = (f16[256,2048]{1,0:T(8,128)(2,1)}, f16[256,2048]{1,0:T(8,128)(2,1)}, u32[]{:S(2)}, u32[]{:S(2)}) collective-permute-start(f16[256,2048]{1,0:T(8,128)(2,1)} %multiply_convert_fusion.3), channel_id=1, source_target_pairs={{0,2},{2,0},{1,3},{3,1},{4,6},{6,4},{5,7},{7,5},{8,10},{10,8},{9,1... | collective-permute-start | bytes 3145736 | tf_op jit(solution)/shard_map/ppermute | solution.py:13
  142.8 3.6 %copy-start.16 = (s32[2]{0:T(128)S(1)}, s32[2]{0:T(128)}, u32[]{:S(2)}) copy-start(s32[2]{0:T(128)} %param.18) | copy-start | bytes 28
  142.8 2.7 %copy-start.14 = (f16[256,2048]{1,0:T(8,128)(2,1)}, f16[256,2048]{1,0:T(8,128)(2,1)S(1)}, u32[]{:S(2)}) copy-start(f16[256,2048]{1,0:T(8,128)(2,1)S(1)} %collective-permute-done.6) | copy-start | bytes 3145732
  142.8 65.9 %collective-permute-start.5 = (f16[256,2048]{1,0:T(8,128)(2,1)}, f16[256,2048]{1,0:T(8,128)(2,1)}, u32[]{:S(2)}, u32[]{:S(2)}) collective-permute-start(f16[256,2048]{1,0:T(8,128)(2,1)} %multiply_convert_fusion.6), channel_id=1, source_target_pairs={{0,2},{2,0},{1,3},{3,1},{4,6},{6,4},{5,7},{7,5},{8,10},{10,8},{9,1... | collective-permute-start | bytes 3145736 | tf_op jit(solution)/shard_map/ppermute | solution.py:13
  146.5 68.9 %copy-start.8 = (f32[256,4096]{1,0:T(8,128)S(1)}, f32[256,4096]{1,0:T(8,128)}, u32[]{:S(2)}) copy-start(f32[256,4096]{1,0:T(8,128)} %fusion.11) | copy-start | bytes 12582916
  146.5 68.9 %copy-start.11 = (f32[256,4096]{1,0:T(8,128)S(1)}, f32[256,4096]{1,0:T(8,128)}, u32[]{:S(2)}) copy-start(f32[256,4096]{1,0:T(8,128)} %copy-done.10) | copy-start | bytes 12582916
  146.5 69.0 %copy-start.15 = (f16[256,2048]{1,0:T(8,128)(2,1)S(1)}, f16[256,2048]{1,0:T(8,128)(2,1)}, u32[]{:S(2)}) copy-start(f16[256,2048]{1,0:T(8,128)(2,1)} %copy-done.14) | copy-start | bytes 3145732
  227.0 18.9 %copy-start.17 = (s32[2]{0:T(128)S(1)}, s32[2]{0:T(128)}, u32[]{:S(2)}) copy-start(s32[2]{0:T(128)} %param.19) | copy-start | bytes 28
  227.0 5.9 %collective-permute-start.10 = (f32[2,3,16,64]{3,2,0,1:T(8,128)S(1)}, f32[2,3,16,64]{3,2,0,1:T(8,128)S(1)}, u32[]{:S(2)}, u32[]{:S(2)}) collective-permute-start(f32[2,3,16,64]{3,2,0,1:T(8,128)S(1)} %get-tuple-element.4), channel_id=1, source_target_pairs={{0,8},{4,12},{8,0},{12,4},{1,9},{5,13},{9,1},{13,5},{2,10},{6,14},... | collective-permute-start | bytes 73736 | tf_op jit(solution)/shard_map/ppermute | solution.py:13
  228.5 4.6 %collective-permute-start.11 = (f32[2,3,16,64]{3,2,0,1:T(8,128)S(1)}, f32[2,3,16,64]{3,2,0,1:T(8,128)}, u32[]{:S(2)}, u32[]{:S(2)}) collective-permute-start(f32[2,3,16,64]{3,2,0,1:T(8,128)S(1)} %get-tuple-element.3), channel_id=1, source_target_pairs={{0,12},{4,0},{8,4},{12,8},{1,13},{5,1},{9,5},{13,9},{2,14},{6,2},{... | collective-permute-start | bytes 73736 | tf_op jit(solution)/shard_map/ppermute | solution.py:13
  230.2 6.0 %collective-permute-start.9 = (f32[2,3,16,64]{3,2,0,1:T(8,128)S(1)}, f32[2,3,16,64]{3,2,0,1:T(8,128)}, u32[]{:S(2)}, u32[]{:S(2)}) collective-permute-start(f32[2,3,16,64]{3,2,0,1:T(8,128)S(1)} %get-tuple-element.2), channel_id=1, source_target_pairs={{0,4},{4,8},{8,12},{12,0},{1,5},{5,9},{9,13},{13,1},{2,6},{6,10},{... | collective-permute-start | bytes 73736 | tf_op jit(solution)/shard_map/ppermute | solution.py:13
  237.1 1.3 collective-permute-start.12
  239.8 3.6 %collective-permute-start.13 = (f32[2,512]{1,0:T(2,128)S(1)}, f32[2,512]{1,0:T(2,128)S(1)}, u32[]{:S(2)}, u32[]{:S(2)}) collective-permute-start(f32[2,512]{1,0:T(2,128)S(1)} %bitcast.81), channel_id=1, source_target_pairs={{0,12},{4,0},{8,4},{12,8},{1,13},{5,1},{9,5},{13,9},{2,14},{6,2},{... | collective-permute-start | bytes 12296 | tf_op jit(solution)/shard_map/ppermute | solution.py:13
  239.9 4.5 %collective-permute-start.14 = (f32[2,512]{1,0:T(2,128)S(1)}, f32[2,512]{1,0:T(2,128)S(1)}, u32[]{:S(2)}, u32[]{:S(2)}) collective-permute-start(f32[2,512]{1,0:T(2,128)S(1)} %bitcast.82), channel_id=1, source_target_pairs={{0,8},{4,12},{8,0},{12,4},{1,9},{5,13},{9,1},{13,5},{2,10},{6,14},... | collective-permute-start | bytes 12296 | tf_op jit(solution)/shard_map/ppermute | solution.py:13
  240.0 5.8 %collective-permute-start.15 = (f32[2,512]{1,0:T(2,128)S(1)}, f32[2,512]{1,0:T(2,128)S(1)}, u32[]{:S(2)}, u32[]{:S(2)}) collective-permute-start(f32[2,512]{1,0:T(2,128)S(1)} %bitcast.83), channel_id=1, source_target_pairs={{0,4},{4,8},{8,12},{12,0},{1,5},{5,9},{9,13},{13,1},{2,6},{6,10},{... | collective-permute-start | bytes 12296 | tf_op jit(solution)/shard_map/ppermute | solution.py:13
  245.9 4.6 %copy-start.13 = (f32[2,512]{1,0:T(2,128)}, f32[2,512]{1,0:T(2,128)S(1)}, u32[]{:S(2)}) copy-start(f32[2,512]{1,0:T(2,128)S(1)} %dynamic-slice_reduce_fusion) | copy-start | bytes 12292
  246.1 3.7 %collective-permute-start.16 = (f32[4,512]{1,0:T(4,128)S(1)}, f32[4,512]{1,0:T(4,128)S(1)}, u32[]{:S(2)}, u32[]{:S(2)}) collective-permute-start(f32[4,512]{1,0:T(4,128)S(1)} %fusion.45), channel_id=1, source_target_pairs={{0,2},{2,0},{1,3},{3,1},{4,6},{6,4},{5,7},{7,5},{8,10},{10,8},{9,1... | collective-permute-start | bytes 24584 | tf_op jit(solution)/shard_map/ppermute | solution.py:13
Sparse Core Ops, SparseCore 0:
  9.6 35.3 all-gather.4
  46.6 31.6 all-gather.2
  146.6 32.8 all-reduce.1

commit v2 on v1

v2 whole, which is shorter than its diff:
```python
import jax
import jax.numpy as jnp
from jax import lax
from jax.sharding import PartitionSpec as P

NGROUP = 4
F32 = jnp.float32
SEND_SCALE = 16.0


def shift(value, axis, step):
    n = lax.axis_size(axis)
    return lax.ppermute(value, axis, [(i, (i + step) % n) for i in range(n)])


def pack(value):
    return (value * SEND_SCALE).astype(jnp.float16)


def unpack(value):
    return value.astype(F32) * (1.0 / SEND_SCALE)


def gather_in_order(value, axis):
    n = lax.axis_size(axis)
    if n == 1:
        return value[None]
    if n > 8:
        return lax.all_gather(value, axis, axis=0)
    return in_order([value] + [shift(value, axis, step) for step in range(1, n)], axis)


def scatter_sum(value, axis, dim):
    n = lax.axis_size(axis)
    if n > 8:
        return lax.psum_scatter(value, axis, scatter_dimension=dim, tiled=True)
    me = lax.axis_index(axis)
    width = value.shape[dim] // n
    total = lax.dynamic_slice_in_dim(value, me * width, width, dim)
    for step in range(1, n):
        block = lax.dynamic_slice_in_dim(value, lax.rem(me + step, n) * width, width, dim)
        total = total + shift(block, axis, step)
    return total


def after(value, *earlier):
    return lax.optimization_barrier((value,) + earlier)[0]


def in_order(pieces, axis):
    n = len(pieces)
    back = pieces[:0:-1] + pieces[:1]
    return lax.dynamic_slice_in_dim(jnp.stack(back + back), n - 1 - lax.axis_index(axis), n, 0)


def gather_features(mine, marks=()):
    n = lax.axis_size("tensor")
    if n > 8:
        return lax.all_gather(mine, "tensor", axis=0)
    pieces = [mine]
    for step in range(1, n):
        start = after(mine, marks[min(step, len(marks)) - 1]) if marks else mine
        pieces.append(shift(start, "tensor", step))
    return in_order(pieces, "tensor")


def features_here(blocks):
    peers = lax.axis_size("example") * lax.axis_size("test")
    n, rows, d_local = blocks.shape
    if n == peers == 4:
        return swap_features(blocks)
    whole = jnp.transpose(blocks, (1, 0, 2)).reshape(rows, n * d_local)
    return lax.all_to_all(whole, ("example", "test"), split_axis=1, concat_axis=0, tiled=True)


def swap_features(blocks):
    ex_index, core = lax.axis_index("example"), lax.axis_index("test")
    got = {}
    for ex_step in (1, 0):
        for core_step in (0, 1):
            wanted = ((ex_index + ex_step) % 2) * 2 + (core + core_step) % 2
            piece = lax.dynamic_index_in_dim(blocks, wanted, 0, keepdims=False)
            if ex_step or core_step:
                pairs = [
                    (2 * e + c, 2 * ((e + ex_step) % 2) + (c + core_step) % 2)
                    for e in range(2)
                    for c in range(2)
                ]
                piece = lax.ppermute(piece, ("example", "test"), pairs)
            got[ex_step, core_step] = piece
    halves = [
        jnp.concatenate(
            [
                jnp.where(core == 0, got[ex_step, 0], got[ex_step, 1]),
                jnp.where(core == 0, got[ex_step, 1], got[ex_step, 0]),
            ]
        )
        for ex_step in (0, 1)
    ]
    return halves


def on_device(
    activations,
    out_grad,
    w_gate,
    w_up,
    w_down,
    proj_model,
    proj_hidden,
    test_grads,
    lengths,
    groups,
):
    ex_loc, seq_len, d_local = activations.shape
    tok_rows = ex_loc * seq_len
    width = proj_model.shape[1] // 3
    n_cores = lax.axis_size("test")
    core = lax.axis_index("test")
    n_ex = lax.axis_size("example")
    ex_index = lax.axis_index("example")
    hid_part = w_gate.shape[1] // n_cores
    rows_part = tok_rows // n_cores
    flat_acts = activations.reshape(tok_rows, d_local)
    flat_grad = out_grad.reshape(tok_rows, d_local)

    acts_mine = lax.dynamic_slice_in_dim(flat_acts, core * rows_part, rows_part, 0)
    grad_mine = lax.dynamic_slice_in_dim(flat_grad, core * rows_part, rows_part, 0)
    acts_blocks = gather_features(acts_mine)
    model_part = jnp.concatenate(
        [
            jnp.dot(flat_acts, proj_model[:, : 2 * width], preferred_element_type=F32),
            jnp.dot(flat_grad, proj_model[:, 2 * width :], preferred_element_type=F32),
        ],
        1,
    )
    model_sum = lax.psum(after(model_part, acts_blocks), "tensor")
    acts_here = features_here(acts_blocks)

    def rows_of(tokens, step):
        if isinstance(tokens, list):
            return tokens[step]
        owner = lax.rem(ex_index + step, n_ex)
        return lax.dynamic_slice_in_dim(tokens, owner * tok_rows, tok_rows, 0)

    def core_sum(product):
        kept = unpack(lax.dynamic_slice_in_dim(product, core * hid_part, hid_part, 1))
        for step in range(1, n_cores):
            to = lax.rem(core + step, n_cores)
            sent = lax.dynamic_slice_in_dim(product, to * hid_part, hid_part, 1)
            kept = kept + unpack(shift(sent, "test", step))
        return kept

    def forward(tokens, weight):
        return pack(jnp.dot(tokens, weight, preferred_element_type=F32))

    def backward(tokens, weight):
        return pack(
            lax.dot_general(tokens, weight, (((1,), (1,)), ((), ())), preferred_element_type=F32)
        )

    jobs = [(forward, acts_here, w_gate), (forward, acts_here, w_up)]

    def products(place, step, *earlier):
        product, tokens, weight = jobs[place]
        return product(after(rows_of(tokens, step), *earlier), weight)

    def send(place, step, whole):
        sent = pack(core_sum(whole))
        arrived[place].append(shift(sent, "example", step))
        return sent

    arrived = [[], [], []]
    last = acts_mine
    marks = [acts_blocks]
    for step in range(1, n_ex):
        gate_far = products(0, step, last)
        up_far = products(1, step, gate_far)
        gate_sent = send(0, step, gate_far)
        up_sent = send(1, step, up_far)
        last = up_far
        marks += [gate_far, gate_sent]
    grad_blocks = gather_features(grad_mine, marks)
    gate_near = products(0, 0, last, gate_sent)
    up_near = products(1, 0, gate_near, up_sent)
    last = up_near
    jobs.append((backward, features_here(grad_blocks), w_down))
    for step in range(1, n_ex):
        down_far = products(2, step, last, *arrived[0])
        down_sent = send(2, step, down_far)
        last = down_far
    down_near = products(2, 0, last)
    own = [core_sum(gate_near), core_sum(up_near), core_sum(down_near)]
    gate_act, up_act, d_hidden = [
        kept + sum(unpack(received) for received in got) for kept, got in zip(own, arrived)
    ]

    sigmoid_gate = jax.nn.sigmoid(gate_act)
    silu_gate = gate_act * sigmoid_gate
    hidden = (silu_gate * up_act).astype(jnp.bfloat16)
    d_gate = (d_hidden * up_act * sigmoid_gate * (1.0 + gate_act * (1.0 - sigmoid_gate))).astype(
        jnp.bfloat16
    )
    d_up = (d_hidden * silu_gate).astype(jnp.bfloat16)
    hid_proj = lax.dynamic_slice_in_dim(proj_hidden, core * hid_part, hid_part, 0)
    out_gate = jnp.dot(d_gate, hid_proj[:, :width], preferred_element_type=F32)
    out_up = jnp.dot(d_up, hid_proj[:, width : 2 * width], preferred_element_type=F32)
    in_hidden = jnp.dot(hidden, hid_proj[:, 2 * width :], preferred_element_type=F32)

    positions = jnp.arange(seq_len, dtype=jnp.int32)
    token_mask = (positions[None, :] < lengths[:, None]).astype(F32)[:, :, None]
    masked = model_sum.reshape(ex_loc, seq_len, 3 * width) * token_mask

    def outer(outputs, inputs):
        return jnp.einsum("bsi,bsj->bij", outputs, inputs, precision=lax.Precision.HIGHEST)

    by_token = (ex_loc, seq_len, width)
    grads_part = jnp.stack(
        [
            outer(out_gate.reshape(by_token), masked[:, :, :width]),
            outer(out_up.reshape(by_token), masked[:, :, width : 2 * width]),
            outer(masked[:, :, 2 * width :], in_hidden.reshape(by_token)),
        ],
        1,
    )
    grads_part = scatter_sum(grads_part, "tensor", 2)
    by_example = []
    for ex_step in range(n_ex):
        total = None
        for core_step in range(n_cores):
            piece = grads_part
            if ex_step or core_step:
                pairs = [
                    (e * n_cores + c, (e + ex_step) % n_ex * n_cores + (c + core_step) % n_cores)
                    for e in range(n_ex)
                    for c in range(n_cores)
                ]
                piece = lax.ppermute(piece, ("example", "test"), pairs)
            total = piece if total is None else total + piece
        by_example.append(total)
    grads_all = in_order(by_example, "example").reshape((n_ex * ex_loc,) + grads_part.shape[1:])
    partial_scores = jnp.einsum(
        "blij,lijn->bn",
        grads_all,
        test_grads.astype(F32),
        precision=lax.Precision.HIGHEST,
    )
    all_scores = jnp.sum(gather_in_order(partial_scores, "tensor"), 0)
    scores = lax.dynamic_slice_in_dim(all_scores, ex_index * ex_loc, ex_loc, 0)
    all_groups = gather_in_order(groups, "example").reshape(-1)
    group_onehot = (all_groups[:, None] == jnp.arange(NGROUP, dtype=jnp.int32)[None, :]).astype(F32)
    group_scores = jnp.dot(group_onehot.T, all_scores, precision=lax.Precision.HIGHEST)
    return (scores, group_scores)


def solution(mesh):
    placed = (
        P(("parts", "example"), None, "tensor"),
        P(("parts", "example"), None, "tensor"),
        P(("example", "test"), "tensor"),
        P(("example", "test"), "tensor"),
        P("tensor", ("example", "test")),
        P("tensor", None),
        P("tensor", None),
        P(None, "tensor", None, "test"),
        P(("parts", "example")),
        P(("parts", "example")),
    )
    return jax.shard_map(
        on_device,
        mesh=mesh,
        in_specs=placed,
        out_specs=(P(("parts", "example"), "test"), P("parts", "test")),
        check_vma=False,
    )
```

time: 258 us -> 237 us (0.919)
  waiting for transfers between devices: 138 us -> 91.9 us
  starting transfers between devices: 23.5 us -> 46.4 us
  local copies, waits for them, and re-layouts: 13.8 us -> 16.6 us
    all_gather x2 -> x0, waiting for transfers between devices: 62.7 us -> none  [features_here(): whole = lax.all_gather(mine, 'tensor', axis=1, tiled=True)]
    ppermute x0 -> x9, waiting for transfers between devices: none -> 47.2 us  [the longest x6 43.7 us: swap_features(): piece = lax.ppermute(piece, ('example', 'test'), pairs)]
    ppermute x17 -> x22, waiting for transfers between devices: 74.9 us -> 44.6 us  [shift(): return lax.ppermute(value, axis, [(i, (i + step) % n) for i in range(n)])]
    ppermute x17 -> x22, starting transfers between devices: 14.8 us -> 40 us  [shift(): return lax.ppermute(value, axis, [(i, (i + step) % n) for i in range(n)])]
    dot_general x9, matrix products: 31.4 us -> 19.6 us  [the longest x4 16.6 us: forward(): return pack(jnp.dot(tokens, weight, preferred_element_type=F32))]
    dot_general x2, matrix products: 11.9 us -> 22.6 us  [backward(): lax.dot_general(tokens, weight, (((1,), (1,)), ((), ())), preferred_eleme...]
    all_to_all x2 -> x0, starting transfers between devices: 8.59 us -> none  [features_here(): lax.all_to_all(whole, ('example', 'test'), split_axis=1, concat_axis=0, t...]
    dynamic_slice x2 -> x11, local copies, waits for them, and re-layouts: 2.15 us -> 8.79 us  [the longest x6 4.55 us: core_sum(): sent = lax.dynamic_slice_in_dim(product, to * hid_part, hid_part, 1)]
  transfers between devices with their start and end apart: 22 -> 32, of which waited for: 13 -> 14; matrix products, arithmetic and copies ran while one was open for 19% -> 28% of each run, Pallas kernels for 0% -> 0%
where the time goes in v2:
time: 237 us
  waiting for transfers between devices  91.9 us (39%)
  matrix products  58.3 us (25%)
  starting transfers between devices  46.4 us (20%)
  local copies, waits for them, and re-layouts  16.6 us (7%)
  between operations  14.8 us (6%)
  other arithmetic  8.81 us (4%)
    ppermute x22, waiting for transfers between devices, shift(): return lax.ppermute(value, axis, [(i, (i + step) % n) for i in range(n)])  44.6 us
    ppermute x6, waiting for transfers between devices, swap_features(): piece = lax.ppermute(piece, ('example', 'test'), pairs)  43.7 us
    ppermute x22, starting transfers between devices, shift(): return lax.ppermute(value, axis, [(i, (i + step) % n) for i in range(n)])  40 us
    dot_general x2, matrix products, backward(): lax.dot_general(tokens, weight, (((1,), (1,)), ((), ())), preferred_eleme...  22.6 us
    dot_general x4, matrix products, forward(): return pack(jnp.dot(tokens, weight, preferred_element_type=F32))  16.6 us
    unnamed x63, local copies, waits for them, and re-layouts  5.89 us
  transfers between devices with their start and end apart: 32, of which 14 were waited for; matrix products, arithmetic and copies ran while one was open for 28% of the time, Pallas kernels for 0%

profile of v2, /device:TPU:0, one launch (start us, length us, event | category | flops | bytes accessed | tf_op | source)
XLA Modules:
  0.0 236.7 jit_solution(7999679165813966037)
XLA Ops:
  7.2 1.9 constant_dynamic-slice_fusion.12
  9.1 3.0 %collective-permute-start.2 = (bf16[128,1280]{1,0:T(8,128)(2,1)}, bf16[128,1280]{1,0:T(8,128)(2,1)S(1)}, u32[]{:S(2)}, u32[]{:S(2)}) collective-permute-start(bf16[128,1280]{1,0:T(8,128)(2,1)} %constant_dynamic-slice_fusion.12), channel_id=1, source_target_pairs={{0,4},{4,8},{8,12},{12,0},{1,5},{5,9},{9,13},{13,1},{2,6},{6,10},{... | collective-permute-start | bytes 983048 | tf_op jit(solution)/shard_map/ppermute | solution.py:13
  12.1 2.6 %collective-permute-start.1 = (bf16[128,1280]{1,0:T(8,128)(2,1)}, bf16[128,1280]{1,0:T(8,128)(2,1)}, u32[]{:S(2)}, u32[]{:S(2)}) collective-permute-start(bf16[128,1280]{1,0:T(8,128)(2,1)} %constant_dynamic-slice_fusion.12), channel_id=1, source_target_pairs={{0,8},{4,12},{8,0},{12,4},{1,9},{5,13},{9,1},{13,5},{2,10},{6,14},... | collective-permute-start | bytes 983048 | tf_op jit(solution)/shard_map/ppermute | solution.py:13
  14.7 1.3 collective-permute-start
  16.1 2.2 fusion.14
  18.2 1.4 fusion.19
  20.7 1.7 constant_dynamic-slice_fusion.13
  22.4 11.1 %collective-permute-done = bf16[128,1280]{1,0:T(8,128)(2,1)} collective-permute-done((bf16[128,1280]{1,0:T(8,128)(2,1)}, bf16[128,1280]{1,0:T(8,128)(2,1)}, u32[]{:S(2)}, u32[]{:S(2)}) %collective-permute-start) | collective-permute-done | bytes 327712 | tf_op jit(solution)/shard_map/ppermute | solution.py:13
  34.5 1.9 collective-permute-done.1
  39.5 1.5 copy-done.3
  42.0 1.0 collective-permute-start.4
  44.6 8.6 %collective-permute-start.8 = (bf16[128,1280]{1,0:T(8,128)(2,1)S(1)}, bf16[128,1280]{1,0:T(8,128)(2,1)S(1)}, u32[]{:S(2)}, u32[]{:S(2)}) collective-permute-start(bf16[128,1280]{1,0:T(8,128)(2,1)S(1)} %copy-done.10), channel_id=1, source_target_pairs={{0,4},{4,8},{8,12},{12,0},{1,5},{5,9},{9,13},{13,1},{2,6},{6,10},{... | collective-permute-start | bytes 983048 | tf_op jit(solution)/shard_map/ppermute | solution.py:13
  53.1 6.2 %collective-permute-done.3 = bf16[128,1280]{1,0:T(8,128)(2,1)} collective-permute-done((bf16[128,1280]{1,0:T(8,128)(2,1)}, bf16[128,1280]{1,0:T(8,128)(2,1)}, u32[]{:S(2)}, u32[]{:S(2)}) %collective-permute-start.3) | collective-permute-done | bytes 327712 | tf_op jit(solution)/shard_map/ppermute | solution.py:89
  59.4 1.1 broadcast_select_fusion.3
  60.6 7.4 %fusion = f16[256,4096]{1,0:T(8,128)(2,1)S(1)} fusion(bf16[256,1280]{1,0:T(8,128)(2,1)S(1)} %pad_maximum_fusion, bf16[1280,4096]{1,0:T(8,128)(2,1)} %param.12), kind=kOutput, calls=%fused_computation.6 | convolution fusion | flops 2686451712 | bytes 13238272 | tf_op jit(solution)/shard_map/dot_general | solution.py:155
  67.9 7.5 %collective-permute-start.7 = (bf16[128,1280]{1,0:T(8,128)(2,1)S(1)}, bf16[128,1280]{1,0:T(8,128)(2,1)S(1)}, u32[]{:S(2)}, u32[]{:S(2)}) collective-permute-start(bf16[128,1280]{1,0:T(8,128)(2,1)S(1)} %copy-done.10), channel_id=1, source_target_pairs={{0,8},{4,12},{8,0},{12,4},{1,9},{5,13},{9,1},{13,5},{2,10},{6,14},... | collective-permute-start | bytes 983048 | tf_op jit(solution)/shard_map/ppermute | solution.py:13
  75.9 3.1 %fusion.1 = f16[256,4096]{1,0:T(8,128)(2,1)S(1)} fusion(bf16[256,1280]{1,0:T(8,128)(2,1)S(1)} %pad_maximum_fusion, bf16[1280,4096]{1,0:T(8,128)(2,1)S(1)} %bitcast.125), kind=kOutput, calls=%fused_computation.7 | convolution fusion | flops 2686451712 | bytes 13238272 | tf_op jit(solution)/shard_map/dot_general | solution.py:155
  79.7 1.1 bitcast_select_fusion.1
  81.4 1.6 collective-permute-start.14
  83.0 3.4 %collective-permute-start.6 = (bf16[128,1280]{1,0:T(8,128)(2,1)S(1)}, bf16[128,1280]{1,0:T(8,128)(2,1)S(1)}, u32[]{:S(2)}, u32[]{:S(2)}) collective-permute-start(bf16[128,1280]{1,0:T(8,128)(2,1)S(1)} %copy-done.10), channel_id=1, source_target_pairs={{0,12},{4,0},{8,4},{12,8},{1,13},{5,1},{9,5},{13,9},{2,14},{6,2},{... | collective-permute-start | bytes 983048 | tf_op jit(solution)/shard_map/ppermute | solution.py:13
  86.4 1.4 add_convert_fusion.1
  88.3 3.1 %fusion.2 = f16[256,4096]{1,0:T(8,128)(2,1)S(1)} fusion(bf16[256,1280]{1,0:T(8,128)(2,1)S(1)} %pad_maximum_fusion.3, bf16[1280,4096]{1,0:T(8,128)(2,1)S(1)} %bitcast.123), kind=kOutput, calls=%fused_computation.8 | convolution fusion | flops 2686451712 | bytes 13238272 | tf_op jit(solution)/shard_map/dot_general | solution.py:155
  91.4 1.2 constant_dynamic-slice_fusion.5
  92.6 5.2 %collective-permute-done.6 = bf16[128,1280]{1,0:T(8,128)(2,1)S(1)} collective-permute-done((bf16[128,1280]{1,0:T(8,128)(2,1)S(1)}, bf16[128,1280]{1,0:T(8,128)(2,1)S(1)}, u32[]{:S(2)}, u32[]{:S(2)}) %collective-permute-start.6) | collective-permute-done | bytes 327712 | tf_op jit(solution)/shard_map/ppermute | solution.py:13
  98.8 3.1 %fusion.3 = f16[256,4096]{1,0:T(8,128)(2,1)S(1)} fusion(bf16[256,1280]{1,0:T(8,128)(2,1)S(1)} %pad_maximum_fusion.3, bf16[1280,4096]{1,0:T(8,128)(2,1)S(1)} %bitcast.125), kind=kOutput, calls=%fused_computation.9 | convolution fusion | flops 2686451712 | bytes 13238272 | tf_op jit(solution)/shard_map/dot_general | solution.py:155
  101.9 1.3 constant_dynamic-slice_fusion.6
  103.5 1.4 collective-permute-start.10
  105.0 31.0 %collective-permute-done.11 = bf16[128,1280]{1,0:T(8,128)(2,1)S(1)} collective-permute-done((bf16[128,1280]{1,0:T(8,128)(2,1)S(1)}, bf16[128,1280]{1,0:T(8,128)(2,1)S(1)}, u32[]{:S(2)}, u32[]{:S(2)}) %collective-permute-start.11) | collective-permute-done | bytes 327712 | tf_op jit(solution)/shard_map/ppermute | solution.py:89
  136.8 6.5 %collective-permute-done.10 = bf16[128,1280]{1,0:T(8,128)(2,1)S(1)} collective-permute-done((bf16[128,1280]{1,0:T(8,128)(2,1)S(1)}, bf16[128,1280]{1,0:T(8,128)(2,1)S(1)}, u32[]{:S(2)}, u32[]{:S(2)}) %collective-permute-start.10) | collective-permute-done | bytes 327712 | tf_op jit(solution)/shard_map/ppermute | solution.py:89
  143.4 11.4 %fusion.4 = f16[256,4096]{1,0:T(8,128)(2,1)S(1)} fusion(bf16[256,1280]{1,0:T(8,128)(2,1)S(1)} %pad_maximum_fusion.2, bf16[4096,1280]{1,0:T(8,128)(2,1)} %param.14), kind=kOutput, calls=%fused_computation.10 | convolution fusion | flops 2686451712 | bytes 13238272 | tf_op jit(solution)/shard_map/dot_general | solution.py:159
  155.1 11.2 %fusion.5 = f16[256,4096]{1,0:T(8,128)(2,1)S(1)} fusion(bf16[256,1280]{1,0:T(8,128)(2,1)S(1)} %pad_maximum_fusion.1, bf16[4096,1280]{1,0:T(8,128)(2,1)} %param.14), kind=kOutput, calls=%fused_computation.11 | convolution fusion | flops 2686451712 | bytes 13238272 | tf_op jit(solution)/shard_map/dot_general | solution.py:159
  166.4 1.4 constant_dynamic-slice_fusion.8
  168.2 1.5 add_convert_fusion
  169.7 1.5 collective-permute-start.17
  172.3 4.5 %convolution_bitcast_fusion.1 = f32[8,2,8,128]{3,2,1,0:T(8,128)S(1)} fusion(f16[256,2048]{1,0:T(8,128)(2,1)} %collective-permute-done.19, f16[256,2048]{1,0:T(8,128)(2,1)} %collective-permute-done.18, f16[256,4096]{1,0:T(8,128)(2,1)} %copy-done.6, s32[]{:T(128)S(6)} %select_n.164, bf16[4096,192]{0,1:T(8,128)(2,1)} %param.16, s32[]{:T(128)S(6)} %add.253, ...), kind=kOutput, calls=%fused_computation.26 | convolution fusion | flops 76546048 | bytes 6620672 | tf_op jit(solution)/shard_map/dot_general | solution.py:208
  177.0 18.1 %collective-permute-done.17 = f16[256,2048]{1,0:T(8,128)(2,1)} collective-permute-done((f16[256,2048]{1,0:T(8,128)(2,1)}, f16[256,2048]{1,0:T(8,128)(2,1)}, u32[]{:S(2)}, u32[]{:S(2)}) %collective-permute-start.17) | collective-permute-done | bytes 1048608 | tf_op jit(solution)/shard_map/ppermute | solution.py:13
  195.1 3.4 %convolution_bitcast_fusion.3 = f32[8,2,8,128]{3,2,1,0:T(8,128)S(1)} fusion(f16[256,2048]{1,0:T(8,128)(2,1)} %collective-permute-done.17, f16[256,2048]{1,0:T(8,128)(2,1)} %collective-permute-done.15, f16[256,4096]{1,0:T(8,128)(2,1)S(1)} %copy-done.9, s32[]{:T(128)S(6)} %select_n.164, bf16[4096,192]{0,1:T(8,128)(2,1)} %param.16, s32[]{:T(128)S(6)} %add.252, ...), kind=kOutput, calls=%fused_computation.28 | convolution fusion | flops 76546048 | bytes 6620672 | tf_op jit(solution)/shard_map/dot_general | solution.py:207
  198.7 4.7 %convolution_bitcast_fusion.5 = f32[8,2,8,128]{3,2,1,0:T(8,128)S(1)} fusion(f16[256,2048]{1,0:T(8,128)(2,1)} %collective-permute-done.17, f16[256,2048]{1,0:T(8,128)(2,1)} %collective-permute-done.15, f16[256,2048]{1,0:T(8,128)(2,1)} %collective-permute-done.19, f16[256,2048]{1,0:T(8,128)(2,1)} %collective-permute-done.18, ...), kind=kOutput, calls=%fused_computation.30 | convolution fusion | flops 81788928 | bytes 9765888 | tf_op jit(solution)/shard_map/dot_general | solution.py:206
  203.7 1.6 collective-permute-start.21
  205.4 2.2 collective-permute-start.23
  207.7 1.5 collective-permute-start.30
  210.2 2.5 %collective-permute-done.22 = f32[2,3,16,64]{3,2,0,1:T(8,128)} collective-permute-done((f32[2,3,16,64]{3,2,0,1:T(8,128)S(1)}, f32[2,3,16,64]{3,2,0,1:T(8,128)}, u32[]{:S(2)}, u32[]{:S(2)}) %collective-permute-start.22) | collective-permute-done | bytes 24608 | tf_op jit(solution)/shard_map/ppermute | solution.py:13
  213.6 1.7 collective-permute-start.25
  215.8 1.5 collective-permute-done.25
  217.3 2.1 collective-permute-done.24
  219.5 1.4 fusion.6
  220.8 2.0 collective-permute-start.27
  224.5 3.0 %collective-permute-done.28 = f32[4,512]{1,0:T(4,128)S(1)} collective-permute-done((f32[4,512]{1,0:T(4,128)S(1)}, f32[4,512]{1,0:T(4,128)S(1)}, u32[]{:S(2)}, u32[]{:S(2)}) %collective-permute-start.28) | collective-permute-done | bytes 8224 | tf_op jit(solution)/shard_map/ppermute | solution.py:13
  (138 shorter events, 21.4 us)
Async XLA Ops:
  7.2 212.3 %copy-start = (bf16[3,16,64,512]{3,2,1,0:T(8,128)(2,1)S(1)}, bf16[3,16,64,512]{3,2,1,0:T(8,128)(2,1)}, u32[]{:S(2)}) copy-start(bf16[3,16,64,512]{3,2,1,0:T(8,128)(2,1)} %param.17) | copy-start | bytes 9437188
  7.2 164.1 %all-reduce.2.cloned.1.call-start = ((), (), s32[]{:S(2)}) async-start(), calls=%async_computation | async-start | bytes 393216 | tf_op jit(solution)/shard_map/psum | solution.py:137
  9.1 28.3 %collective-permute-start.2 = (bf16[128,1280]{1,0:T(8,128)(2,1)}, bf16[128,1280]{1,0:T(8,128)(2,1)S(1)}, u32[]{:S(2)}, u32[]{:S(2)}) collective-permute-start(bf16[128,1280]{1,0:T(8,128)(2,1)} %constant_dynamic-slice_fusion.12), channel_id=1, source_target_pairs={{0,4},{4,8},{8,12},{12,0},{1,5},{5,9},{9,13},{13,1},{2,6},{6,10},{... | collective-permute-start | bytes 983048 | tf_op jit(solution)/shard_map/ppermute | solution.py:13
  12.1 24.2 %collective-permute-start.1 = (bf16[128,1280]{1,0:T(8,128)(2,1)}, bf16[128,1280]{1,0:T(8,128)(2,1)}, u32[]{:S(2)}, u32[]{:S(2)}) collective-permute-start(bf16[128,1280]{1,0:T(8,128)(2,1)} %constant_dynamic-slice_fusion.12), channel_id=1, source_target_pairs={{0,8},{4,12},{8,0},{12,4},{1,9},{5,13},{9,1},{13,5},{2,10},{6,14},... | collective-permute-start | bytes 983048 | tf_op jit(solution)/shard_map/ppermute | solution.py:13
  14.7 18.8 %collective-permute-start = (bf16[128,1280]{1,0:T(8,128)(2,1)}, bf16[128,1280]{1,0:T(8,128)(2,1)}, u32[]{:S(2)}, u32[]{:S(2)}) collective-permute-start(bf16[128,1280]{1,0:T(8,128)(2,1)} %constant_dynamic-slice_fusion.12), channel_id=1, source_target_pairs={{0,12},{4,0},{8,4},{12,8},{1,13},{5,1},{9,5},{13,9},{2,14},{6,2},{... | collective-permute-start | bytes 983048 | tf_op jit(solution)/shard_map/ppermute | solution.py:13
  19.7 17.7 %copy-start.1 = (bf16[2,128,1280]{2,1,0:T(8,128)(2,1)S(1)}, bf16[2,128,1280]{2,1,0:T(8,128)(2,1)}, u32[]{:S(2)}) copy-start(bf16[2,128,1280]{2,1,0:T(8,128)(2,1)} %param.10) | copy-start | bytes 1966084
  42.0 11.1 %collective-permute-start.4 = (bf16[128,1280]{1,0:T(8,128)(2,1)}, bf16[128,1280]{1,0:T(8,128)(2,1)}, u32[]{:S(2)}, u32[]{:S(2)}) collective-permute-start(bf16[128,1280]{1,0:T(8,128)(2,1)} %get-tuple-element.30), channel_id=1, source_target_pairs={{0,3},{1,2},{2,1},{3,0},{4,7},{5,6},{6,5},{7,4},{8,11},{9,10},{10,... | collective-permute-start | bytes 983048 | tf_op jit(solution)/shard_map/ppermute | solution.py:89
  43.0 16.3 %collective-permute-start.3 = (bf16[128,1280]{1,0:T(8,128)(2,1)}, bf16[128,1280]{1,0:T(8,128)(2,1)}, u32[]{:S(2)}, u32[]{:S(2)}) collective-permute-start(bf16[128,1280]{1,0:T(8,128)(2,1)} %get-tuple-element.31), channel_id=1, source_target_pairs={{0,2},{1,3},{2,0},{3,1},{4,6},{5,7},{6,4},{7,5},{8,10},{9,11},{10,... | collective-permute-start | bytes 983048 | tf_op jit(solution)/shard_map/ppermute | solution.py:89
  43.6 36.2 %collective-permute-start.12 = (bf16[128,1280]{1,0:T(8,128)(2,1)}, bf16[128,1280]{1,0:T(8,128)(2,1)}, u32[]{:S(2)}, u32[]{:S(2)}) collective-permute-start(bf16[128,1280]{1,0:T(8,128)(2,1)} %get-tuple-element.29), channel_id=1, source_target_pairs={{0,1},{1,0},{2,3},{3,2},{4,5},{5,4},{6,7},{7,6},{8,9},{9,8},{10,11... | collective-permute-start | bytes 983048 | tf_op jit(solution)/shard_map/ppermute | solution.py:89
  44.6 53.3 %collective-permute-start.8 = (bf16[128,1280]{1,0:T(8,128)(2,1)S(1)}, bf16[128,1280]{1,0:T(8,128)(2,1)S(1)}, u32[]{:S(2)}, u32[]{:S(2)}) collective-permute-start(bf16[128,1280]{1,0:T(8,128)(2,1)S(1)} %copy-done.10), channel_id=1, source_target_pairs={{0,4},{4,8},{8,12},{12,0},{1,5},{5,9},{9,13},{13,1},{2,6},{6,10},{... | collective-permute-start | bytes 983048 | tf_op jit(solution)/shard_map/ppermute | solution.py:13
  60.5 15.3 %slice-start.3 = ((s8[10485760]{0:T(1024)(128)(4,1)}), s8[4194304]{0:T(1024)(128)(4,1)S(1)}, s32[]{:S(2)}) async-start(s8[10485760]{0:T(1024)(128)(4,1)} %bitcast.124), calls=%async_computation.4 | async-start | bytes 8388608
  60.5 15.3 %slice-start.4 = ((s8[10485760]{0:T(1024)(128)(4,1)}), s8[4194304]{0:T(1024)(128)(4,1)S(1)}, s32[]{:S(2)}) async-start(s8[10485760]{0:T(1024)(128)(4,1)} %bitcast.124), calls=%async_computation.5 | async-start | bytes 8388608
  60.6 15.3 %slice-start.5 = ((s8[10485760]{0:T(1024)(128)(4,1)}), s8[2097152]{0:T(1024)(128)(4,1)S(1)}, s32[]{:S(2)}) async-start(s8[10485760]{0:T(1024)(128)(4,1)} %bitcast.124), calls=%async_computation.6 | async-start | bytes 4194304
  67.9 29.9 %collective-permute-start.7 = (bf16[128,1280]{1,0:T(8,128)(2,1)S(1)}, bf16[128,1280]{1,0:T(8,128)(2,1)S(1)}, u32[]{:S(2)}, u32[]{:S(2)}) collective-permute-start(bf16[128,1280]{1,0:T(8,128)(2,1)S(1)} %copy-done.10), channel_id=1, source_target_pairs={{0,8},{4,12},{8,0},{12,4},{1,9},{5,13},{9,1},{13,5},{2,10},{6,14},... | collective-permute-start | bytes 983048 | tf_op jit(solution)/shard_map/ppermute | solution.py:13
  75.7 5.2 %collective-permute-start.5 = (f16[256,2048]{1,0:T(8,128)(2,1)S(1)}, f16[256,2048]{1,0:T(8,128)(2,1)S(1)}, u32[]{:S(2)}, u32[]{:S(2)}) collective-permute-start(f16[256,2048]{1,0:T(8,128)(2,1)S(1)} %constant_dynamic-slice_fusion.11), channel_id=1, source_target_pairs={{0,1},{1,0},{2,3},{3,2},{4,5},{5,4},{6,7},{7,6},{8,9},{9,8},{10,11... | collective-permute-start | bytes 3145736 | tf_op jit(solution)/shard_map/ppermute | solution.py:13
  75.8 12.5 %slice-start = ((s8[10485760]{0:T(1024)(128)(4,1)}), s8[4194304]{0:T(1024)(128)(4,1)S(1)}, s32[]{:S(2)}) async-start(s8[10485760]{0:T(1024)(128)(4,1)} %bitcast.122), calls=%async_computation.1 | async-start | bytes 8388608
  75.8 12.5 %slice-start.1 = ((s8[10485760]{0:T(1024)(128)(4,1)}), s8[4194304]{0:T(1024)(128)(4,1)S(1)}, s32[]{:S(2)}) async-start(s8[10485760]{0:T(1024)(128)(4,1)} %bitcast.122), calls=%async_computation.2 | async-start | bytes 8388608
  79.0 9.3 %slice-start.2 = ((s8[10485760]{0:T(1024)(128)(4,1)}), s8[2097152]{0:T(1024)(128)(4,1)S(1)}, s32[]{:S(2)}) async-start(s8[10485760]{0:T(1024)(128)(4,1)} %bitcast.122), calls=%async_computation.3 | async-start | bytes 4194304
  79.2 7.1 %collective-permute-start.13 = (f16[256,2048]{1,0:T(8,128)(2,1)S(1)}, f16[256,2048]{1,0:T(8,128)(2,1)S(1)}, u32[]{:S(2)}, u32[]{:S(2)}) collective-permute-start(f16[256,2048]{1,0:T(8,128)(2,1)S(1)} %constant_dynamic-slice_fusion.9), channel_id=1, source_target_pairs={{0,1},{1,0},{2,3},{3,2},{4,5},{5,4},{6,7},{7,6},{8,9},{9,8},{10,11... | collective-permute-start | bytes 3145736 | tf_op jit(solution)/shard_map/ppermute | solution.py:13
  81.4 62.0 %collective-permute-start.14 = (f16[256,2048]{1,0:T(8,128)(2,1)S(1)}, f16[256,2048]{1,0:T(8,128)(2,1)S(1)}, u32[]{:S(2)}, u32[]{:S(2)}) collective-permute-start(f16[256,2048]{1,0:T(8,128)(2,1)S(1)} %add_convert_fusion.2), channel_id=1, source_target_pairs={{0,2},{2,0},{1,3},{3,1},{4,6},{6,4},{5,7},{7,5},{8,10},{10,8},{9,1... | collective-permute-start | bytes 3145736 | tf_op jit(solution)/shard_map/ppermute | solution.py:13
  83.0 14.8 %collective-permute-start.6 = (bf16[128,1280]{1,0:T(8,128)(2,1)S(1)}, bf16[128,1280]{1,0:T(8,128)(2,1)S(1)}, u32[]{:S(2)}, u32[]{:S(2)}) collective-permute-start(bf16[128,1280]{1,0:T(8,128)(2,1)S(1)} %copy-done.10), channel_id=1, source_target_pairs={{0,12},{4,0},{8,4},{12,8},{1,13},{5,1},{9,5},{13,9},{2,14},{6,2},{... | collective-permute-start | bytes 983048 | tf_op jit(solution)/shard_map/ppermute | solution.py:13
  87.8 84.5 %collective-permute-start.19 = (f16[256,2048]{1,0:T(8,128)(2,1)}, f16[256,2048]{1,0:T(8,128)(2,1)}, u32[]{:S(2)}, u32[]{:S(2)}) collective-permute-start(f16[256,2048]{1,0:T(8,128)(2,1)} %add_convert_fusion.1), channel_id=1, source_target_pairs={{0,2},{2,0},{1,3},{3,1},{4,6},{6,4},{5,7},{7,5},{8,10},{10,8},{9,1... | collective-permute-start | bytes 3145736 | tf_op jit(solution)/shard_map/ppermute | solution.py:13
  91.4 6.4 %copy-start.4 = (f16[256,4096]{1,0:T(8,128)(2,1)}, f16[256,4096]{1,0:T(8,128)(2,1)S(1)}, u32[]{:S(2)}) copy-start(f16[256,4096]{1,0:T(8,128)(2,1)S(1)} %fusion.2) | copy-start | bytes 6291460
  91.4 6.5 %copy-start.2 = (bf16[2,128,1280]{2,1,0:T(8,128)(2,1)S(1)}, bf16[2,128,1280]{2,1,0:T(8,128)(2,1)}, u32[]{:S(2)}) copy-start(bf16[2,128,1280]{2,1,0:T(8,128)(2,1)} %param.11) | copy-start | bytes 1966084
  97.8 74.4 %collective-permute-start.20 = (f16[256,2048]{1,0:T(8,128)(2,1)}, f16[256,2048]{1,0:T(8,128)(2,1)}, u32[]{:S(2)}, u32[]{:S(2)}) collective-permute-start(f16[256,2048]{1,0:T(8,128)(2,1)} %constant_dynamic-slice_fusion.5), channel_id=1, source_target_pairs={{0,1},{1,0},{2,3},{3,2},{4,5},{5,4},{6,7},{7,6},{8,9},{9,8},{10,11... | collective-permute-start | bytes 3145736 | tf_op jit(solution)/shard_map/ppermute | solution.py:13
  98.2 5.3 %collective-permute-start.9 = (bf16[128,1280]{1,0:T(8,128)(2,1)S(1)}, bf16[128,1280]{1,0:T(8,128)(2,1)S(1)}, u32[]{:S(2)}, u32[]{:S(2)}) collective-permute-start(bf16[128,1280]{1,0:T(8,128)(2,1)S(1)} %get-tuple-element.26), channel_id=1, source_target_pairs={{0,1},{1,0},{2,3},{3,2},{4,5},{5,4},{6,7},{7,6},{8,9},{9,8},{10,11... | collective-permute-start | bytes 983048 | tf_op jit(solution)/shard_map/ppermute | solution.py:89
  103.2 32.8 %collective-permute-start.11 = (bf16[128,1280]{1,0:T(8,128)(2,1)S(1)}, bf16[128,1280]{1,0:T(8,128)(2,1)S(1)}, u32[]{:S(2)}, u32[]{:S(2)}) collective-permute-start(bf16[128,1280]{1,0:T(8,128)(2,1)S(1)} %get-tuple-element.27), channel_id=1, source_target_pairs={{0,3},{1,2},{2,1},{3,0},{4,7},{5,6},{6,5},{7,4},{8,11},{9,10},{10,... | collective-permute-start | bytes 983048 | tf_op jit(solution)/shard_map/ppermute | solution.py:89
  103.5 39.8 %collective-permute-start.10 = (bf16[128,1280]{1,0:T(8,128)(2,1)S(1)}, bf16[128,1280]{1,0:T(8,128)(2,1)S(1)}, u32[]{:S(2)}, u32[]{:S(2)}) collective-permute-start(bf16[128,1280]{1,0:T(8,128)(2,1)S(1)} %get-tuple-element.28), channel_id=1, source_target_pairs={{0,2},{1,3},{2,0},{3,1},{4,6},{5,7},{6,4},{7,5},{8,10},{9,11},{10,... | collective-permute-start | bytes 983048 | tf_op jit(solution)/shard_map/ppermute | solution.py:89
  136.0 36.2 %collective-permute-start.18 = (f16[256,2048]{1,0:T(8,128)(2,1)}, f16[256,2048]{1,0:T(8,128)(2,1)}, u32[]{:S(2)}, u32[]{:S(2)}) collective-permute-start(f16[256,2048]{1,0:T(8,128)(2,1)} %constant_dynamic-slice_fusion.6), channel_id=1, source_target_pairs={{0,1},{1,0},{2,3},{3,2},{4,5},{5,4},{6,7},{7,6},{8,9},{9,8},{10,11... | collective-permute-start | bytes 3145736 | tf_op jit(solution)/shard_map/ppermute | solution.py:13
  143.4 11.4 %copy-start.12 = (f16[256,2048]{1,0:T(8,128)(2,1)}, f16[256,2048]{1,0:T(8,128)(2,1)S(1)}, u32[]{:S(2)}) copy-start(f16[256,2048]{1,0:T(8,128)(2,1)S(1)} %collective-permute-done.14) | copy-start | bytes 3145732
  155.0 13.2 %collective-permute-start.16 = (f16[256,2048]{1,0:T(8,128)(2,1)S(1)}, f16[256,2048]{1,0:T(8,128)(2,1)S(1)}, u32[]{:S(2)}, u32[]{:S(2)}) collective-permute-start(f16[256,2048]{1,0:T(8,128)(2,1)S(1)} %constant_dynamic-slice_fusion.7), channel_id=1, source_target_pairs={{0,1},{1,0},{2,3},{3,2},{4,5},{5,4},{6,7},{7,6},{8,9},{9,8},{10,11... | collective-permute-start | bytes 3145736 | tf_op jit(solution)/shard_map/ppermute | solution.py:13
  167.7 9.2 %collective-permute-start.15 = (f16[256,2048]{1,0:T(8,128)(2,1)}, f16[256,2048]{1,0:T(8,128)(2,1)}, u32[]{:S(2)}, u32[]{:S(2)}) collective-permute-start(f16[256,2048]{1,0:T(8,128)(2,1)} %constant_dynamic-slice_fusion.8), channel_id=1, source_target_pairs={{0,1},{1,0},{2,3},{3,2},{4,5},{5,4},{6,7},{7,6},{8,9},{9,8},{10,11... | collective-permute-start | bytes 3145736 | tf_op jit(solution)/shard_map/ppermute | solution.py:13
  169.7 25.4 %collective-permute-start.17 = (f16[256,2048]{1,0:T(8,128)(2,1)}, f16[256,2048]{1,0:T(8,128)(2,1)}, u32[]{:S(2)}, u32[]{:S(2)}) collective-permute-start(f16[256,2048]{1,0:T(8,128)(2,1)} %add_convert_fusion), channel_id=1, source_target_pairs={{0,2},{2,0},{1,3},{3,1},{4,6},{6,4},{5,7},{7,5},{8,10},{10,8},{9,1... | collective-permute-start | bytes 3145736 | tf_op jit(solution)/shard_map/ppermute | solution.py:13
  172.2 22.9 %copy-start.5 = (f16[256,4096]{1,0:T(8,128)(2,1)S(1)}, f16[256,4096]{1,0:T(8,128)(2,1)}, u32[]{:S(2)}) copy-start(f16[256,4096]{1,0:T(8,128)(2,1)} %copy-done.4) | copy-start | bytes 6291460
  172.2 22.9 %copy-start.9 = (f16[256,4096]{1,0:T(8,128)(2,1)S(1)}, f16[256,4096]{1,0:T(8,128)(2,1)}, u32[]{:S(2)}) copy-start(f16[256,4096]{1,0:T(8,128)(2,1)} %copy-done.8) | copy-start | bytes 6291460
  172.2 22.9 %copy-start.13 = (f16[256,2048]{1,0:T(8,128)(2,1)S(1)}, f16[256,2048]{1,0:T(8,128)(2,1)}, u32[]{:S(2)}) copy-start(f16[256,2048]{1,0:T(8,128)(2,1)} %copy-done.12) | copy-start | bytes 3145732
  176.9 21.8 %copy-start.7 = (f16[256,4096]{1,0:T(8,128)(2,1)S(1)}, f16[256,4096]{1,0:T(8,128)(2,1)}, u32[]{:S(2)}) copy-start(f16[256,4096]{1,0:T(8,128)(2,1)} %copy-done.6) | copy-start | bytes 6291460
  198.7 9.0 %copy-start.11 = (s32[2]{0:T(128)S(1)}, s32[2]{0:T(128)}, u32[]{:S(2)}) copy-start(s32[2]{0:T(128)} %param.19) | copy-start | bytes 28
  203.7 6.5 %collective-permute-start.21 = (f32[2,3,16,64]{3,2,0,1:T(8,128)S(1)}, f32[2,3,16,64]{3,2,0,1:T(8,128)S(1)}, u32[]{:S(2)}, u32[]{:S(2)}) collective-permute-start(f32[2,3,16,64]{3,2,0,1:T(8,128)S(1)} %get-tuple-element.36), channel_id=1, source_target_pairs={{0,4},{4,8},{8,12},{12,0},{1,5},{5,9},{9,13},{13,1},{2,6},{6,10},{... | collective-permute-start | bytes 73736 | tf_op jit(solution)/shard_map/ppermute | solution.py:13
  205.4 4.8 %collective-permute-start.23 = (f32[2,3,16,64]{3,2,0,1:T(8,128)S(1)}, f32[2,3,16,64]{3,2,0,1:T(8,128)}, u32[]{:S(2)}, u32[]{:S(2)}) collective-permute-start(f32[2,3,16,64]{3,2,0,1:T(8,128)S(1)} %get-tuple-element.37), channel_id=1, source_target_pairs={{0,12},{4,0},{8,4},{12,8},{1,13},{5,1},{9,5},{13,9},{2,14},{6,2},{... | collective-permute-start | bytes 73736 | tf_op jit(solution)/shard_map/ppermute | solution.py:13
  207.6 5.1 %collective-permute-start.22 = (f32[2,3,16,64]{3,2,0,1:T(8,128)S(1)}, f32[2,3,16,64]{3,2,0,1:T(8,128)}, u32[]{:S(2)}, u32[]{:S(2)}) collective-permute-start(f32[2,3,16,64]{3,2,0,1:T(8,128)S(1)} %get-tuple-element.38), channel_id=1, source_target_pairs={{0,8},{4,12},{8,0},{12,4},{1,9},{5,13},{9,1},{13,5},{2,10},{6,14},... | collective-permute-start | bytes 73736 | tf_op jit(solution)/shard_map/ppermute | solution.py:13
  207.7 5.9 %collective-permute-start.30 = (s32[2]{0:T(128)S(1)}, s32[2]{0:T(128)S(1)}, u32[]{:S(2)}, u32[]{:S(2)}) collective-permute-start(s32[2]{0:T(128)S(1)} %copy-done.11), channel_id=1, source_target_pairs={{0,2},{2,0},{1,3},{3,1},{4,6},{6,4},{5,7},{7,5},{8,10},{10,8},{9,1... | collective-permute-start | bytes 32 | tf_op jit(solution)/shard_map/ppermute | solution.py:13
  213.5 2.3 collective-permute-start.26
  213.6 3.6 %collective-permute-start.25 = (f32[2,3,16,64]{3,2,0,1:T(8,128)S(1)}, f32[2,3,16,64]{3,2,0,1:T(8,128)S(1)}, u32[]{:S(2)}, u32[]{:S(2)}) collective-permute-start(f32[2,3,16,64]{3,2,0,1:T(8,128)S(1)} %add_add_fusion), channel_id=1, source_target_pairs={{0,3},{1,2},{2,1},{3,0},{4,7},{5,6},{6,5},{7,4},{8,11},{9,10},{10,... | collective-permute-start | bytes 73736 | tf_op jit(solution)/shard_map/ppermute | solution.py:238
  215.3 4.1 %collective-permute-start.24 = (f32[2,3,16,64]{3,2,0,1:T(8,128)S(1)}, f32[2,3,16,64]{3,2,0,1:T(8,128)S(1)}, u32[]{:S(2)}, u32[]{:S(2)}) collective-permute-start(f32[2,3,16,64]{3,2,0,1:T(8,128)S(1)} %add_add_fusion), channel_id=1, source_target_pairs={{0,2},{1,3},{2,0},{3,1},{4,6},{5,7},{6,4},{7,5},{8,10},{9,11},{10,... | collective-permute-start | bytes 73736 | tf_op jit(solution)/shard_map/ppermute | solution.py:238
  220.8 3.7 %collective-permute-start.27 = (f32[4,512]{1,0:T(4,128)S(1)}, f32[4,512]{1,0:T(4,128)S(1)}, u32[]{:S(2)}, u32[]{:S(2)}) collective-permute-start(f32[4,512]{1,0:T(4,128)S(1)} %bitcast.117), channel_id=1, source_target_pairs={{0,12},{4,0},{8,4},{12,8},{1,13},{5,1},{9,5},{13,9},{2,14},{6,2},{... | collective-permute-start | bytes 24584 | tf_op jit(solution)/shard_map/ppermute | solution.py:13
  222.9 5.4 %collective-permute-start.29 = (f32[4,512]{1,0:T(4,128)S(1)}, f32[4,512]{1,0:T(4,128)S(1)}, u32[]{:S(2)}, u32[]{:S(2)}) collective-permute-start(f32[4,512]{1,0:T(4,128)S(1)} %bitcast.118), channel_id=1, source_target_pairs={{0,4},{4,8},{8,12},{12,0},{1,5},{5,9},{9,13},{13,1},{2,6},{6,10},{... | collective-permute-start | bytes 24584 | tf_op jit(solution)/shard_map/ppermute | solution.py:13
  223.0 4.5 %collective-permute-start.28 = (f32[4,512]{1,0:T(4,128)S(1)}, f32[4,512]{1,0:T(4,128)S(1)}, u32[]{:S(2)}, u32[]{:S(2)}) collective-permute-start(f32[4,512]{1,0:T(4,128)S(1)} %bitcast.119), channel_id=1, source_target_pairs={{0,8},{4,12},{8,0},{12,4},{1,9},{5,13},{9,1},{13,5},{2,10},{6,14},... | collective-permute-start | bytes 24584 | tf_op jit(solution)/shard_map/ppermute | solution.py:13
  (5 other events, 16.4 us)
Sparse Core Ops, SparseCore 0:
  44.7 49.1 all-reduce.1

commit v3 on v2

--- a/solution.py
+++ b/solution.py
@@ -1,6 +1,8 @@
 import jax
 import jax.numpy as jnp
 from jax import lax
+from jax.experimental import pallas as pl
+from jax.experimental.pallas import tpu as pltpu
 from jax.sharding import PartitionSpec as P
 
 NGROUP = 4
@@ -53,51 +55,75 @@
     return lax.dynamic_slice_in_dim(jnp.stack(back + back), n - 1 - lax.axis_index(axis), n, 0)
 
 
-def gather_features(mine, marks=()):
-    n = lax.axis_size("tensor")
-    if n > 8:
-        return lax.all_gather(mine, "tensor", axis=0)
-    pieces = [mine]
-    for step in range(1, n):
-        start = after(mine, marks[min(step, len(marks)) - 1]) if marks else mine
-        pieces.append(shift(start, "tensor", step))
-    return in_order(pieces, "tensor")
-
-
-def features_here(blocks):
-    peers = lax.axis_size("example") * lax.axis_size("test")
-    n, rows, d_local = blocks.shape
-    if n == peers == 4:
-        return swap_features(blocks)
-    whole = jnp.transpose(blocks, (1, 0, 2)).reshape(rows, n * d_local)
-    return lax.all_to_all(whole, ("example", "test"), split_axis=1, concat_axis=0, tiled=True)
-
-
-def swap_features(blocks):
-    ex_index, core = lax.axis_index("example"), lax.axis_index("test")
-    got = {}
-    for ex_step in (1, 0):
-        for core_step in (0, 1):
-            wanted = ((ex_index + ex_step) % 2) * 2 + (core + core_step) % 2
-            piece = lax.dynamic_index_in_dim(blocks, wanted, 0, keepdims=False)
-            if ex_step or core_step:
-                pairs = [
-                    (2 * e + c, 2 * ((e + ex_step) % 2) + (c + core_step) % 2)
-                    for e in range(2)
-                    for c in range(2)
-                ]
-                piece = lax.ppermute(piece, ("example", "test"), pairs)
-            got[ex_step, core_step] = piece
-    halves = [
-        jnp.concatenate(
-            [
-                jnp.where(core == 0, got[ex_step, 0], got[ex_step, 1]),
-                jnp.where(core == 0, got[ex_step, 1], got[ex_step, 0]),
-            ]
+class Features:
+    def __init__(self, flat):
+        self.flat = flat
+        self.n_ex, self.n_cores = lax.axis_size("example"), lax.axis_size("test")
+        self.blocks = [None] * self.n_ex
+        self.direct = (lax.axis_size("tensor"), self.n_ex, self.n_cores) == (4, 2, 2)
+
+    def far(self, marks):
+        if self.direct:
+            self.blocks[1] = direct_features(self.flat, 1, marks)
+            return
+        rows = self.flat.shape[0]
+        part = rows // self.n_cores
+        mine = lax.dynamic_slice_in_dim(self.flat, lax.axis_index("test") * part, part, 0)
+        whole = lax.all_gather(after(mine, marks[0]), "tensor", axis=1, tiled=True)
+        whole = lax.all_to_all(
+            whole, ("example", "test"), split_axis=1, concat_axis=0, tiled=True
         )
-        for ex_step in (0, 1)
-    ]
-    return halves
+        for step in range(self.n_ex):
+            owner = lax.rem(lax.axis_index("example") + step, self.n_ex)
+            self.blocks[step] = lax.dynamic_slice_in_dim(whole, owner * rows, rows, 0)
+
+    def near(self, marks):
+        if self.direct:
+            self.blocks[0] = direct_features(self.flat, 0, marks)
+
+
+def direct_features(flat, ex_step, marks):
+    pieces = []
+    for turn in range(2):
+        pairs = []
+        for block in range(4):
+            example, core = block // 2, block % 2
+            for source_core in range(2):
+                target = block ^ (2 * turn + (source_core ^ core))
+                source = block * 4 + (example ^ ex_step) * 2 + source_core
+                pairs.append((source, target * 4 + example * 2 + core))
+        start = after(flat, marks[min(turn, len(marks) - 1)])
+        pieces.append(lax.ppermute(start, ("tensor", "example", "test"), pairs))
+    block = lax.axis_index("example") * 2 + lax.axis_index("test")
+    return jnp.where((lax.axis_index("tensor") ^ block) < 2, pieces[0], pieces[1])
+
+
+def dot_rows_kernel(tokens_ref, weight_ref, out_ref):
+    out_ref[...] = lax.dot_general(
+        tokens_ref[...], weight_ref[...], (((1,), (1,)), ((), ())), preferred_element_type=F32
+    )
+
+
+def dot_rows(tokens, weight):
+    rows, depth = tokens.shape
+    hidden = weight.shape[0]
+    tile = min(512, hidden)
+    return pl.pallas_call(
+        dot_rows_kernel,
+        out_shape=jax.ShapeDtypeStruct((rows, hidden), F32),
+        grid=(hidden // tile,),
+        in_specs=[
+            pl.BlockSpec((rows, depth), lambda i: (0, 0)),
+            pl.BlockSpec((tile, depth), lambda i: (i, 0)),
+        ],
+        out_specs=pl.BlockSpec((rows, tile), lambda i: (0, i)),
+        compiler_params=pltpu.CompilerParams(vmem_limit_bytes=16 * 2**20),
+        cost_estimate=pl.CostEstimate(
+            flops=2 * rows * depth * hidden,
+            bytes_accessed=2 * hidden * depth + 4 * rows * hidden,
+            transcendentals=0,
+        ),
+    )(tokens, weight)
 
 
 def on_device(
@@ -120,13 +146,29 @@
     n_ex = lax.axis_size("example")
     ex_index = lax.axis_index("example")
     hid_part = w_gate.shape[1] // n_cores
-    rows_part = tok_rows // n_cores
     flat_acts = activations.reshape(tok_rows, d_local)
     flat_grad = out_grad.reshape(tok_rows, d_local)
 
-    acts_mine = lax.dynamic_slice_in_dim(flat_acts, core * rows_part, rows_part, 0)
-    grad_mine = lax.dynamic_slice_in_dim(flat_grad, core * rows_part, rows_part, 0)
-    acts_blocks = gather_features(acts_mine)
+    def forward(tokens, weight):
+        return jnp.dot(tokens, weight, preferred_element_type=F32)
+
+    def core_sum(product):
+        kept = lax.dynamic_slice_in_dim(product, core * hid_part, hid_part, 1)
+        for step in range(1, n_cores):
+            to = lax.rem(core + step, n_cores)
+            sent = pack(lax.dynamic_slice_in_dim(product, to * hid_part, hid_part, 1))
+            kept = kept + unpack(shift(sent, "test", step))
+        return kept
+
+    def send(place, step, whole):
+        sent = pack(core_sum(whole))
+        arrived[place].append(shift(sent, "example", step))
+        return sent
+
+    arrived = [[], [], []]
+    begin = lengths
+    acts = Features(flat_acts)
+    acts.far([begin])
     model_part = jnp.concatenate(
         [
             jnp.dot(flat_acts, proj_model[:, : 2 * width], preferred_element_type=F32),
@@ -134,62 +176,26 @@
         ],
         1,
     )
-    model_sum = lax.psum(after(model_part, acts_blocks), "tensor")
-    acts_here = features_here(acts_blocks)
-
-    def rows_of(tokens, step):
-        if isinstance(tokens, list):
-            return tokens[step]
-        owner = lax.rem(ex_index + step, n_ex)
-        return lax.dynamic_slice_in_dim(tokens, owner * tok_rows, tok_rows, 0)
-
-    def core_sum(product):
-        kept = unpack(lax.dynamic_slice_in_dim(product, core * hid_part, hid_part, 1))
-        for step in range(1, n_cores):
-            to = lax.rem(core + step, n_cores)
-            sent = lax.dynamic_slice_in_dim(product, to * hid_part, hid_part, 1)
-            kept = kept + unpack(shift(sent, "test", step))
-        return kept
-
-    def forward(tokens, weight):
-        return pack(jnp.dot(tokens, weight, preferred_element_type=F32))
-
-    def backward(tokens, weight):
-        return pack(
-            lax.dot_general(tokens, weight, (((1,), (1,)), ((), ())), preferred_element_type=F32)
-        )
-
-    jobs = [(forward, acts_here, w_gate), (forward, acts_here, w_up)]
-
-    def products(place, step, *earlier):
-        product, tokens, weight = jobs[place]
-        return product(after(rows_of(tokens, step), *earlier), weight)
-
-    def send(place, step, whole):
-        sent = pack(core_sum(whole))
-        arrived[place].append(shift(sent, "example", step))
-        return sent
-
-    arrived = [[], [], []]
-    last = acts_mine
-    marks = [acts_blocks]
+    last = begin
     for step in range(1, n_ex):
-        gate_far = products(0, step, last)
-        up_far = products(1, step, gate_far)
+        gate_far = forward(after(acts.blocks[step], last), w_gate)
+        up_far = forward(after(acts.blocks[step], gate_far), w_up)
         gate_sent = send(0, step, gate_far)
         up_sent = send(1, step, up_far)
         last = up_far
-        marks += [gate_far, gate_sent]
-    grad_blocks = gather_features(grad_mine, marks)
-    gate_near = products(0, 0, last, gate_sent)
-    up_near = products(1, 0, gate_near, up_sent)
+    grad = Features(flat_grad)
+    grad.far([acts.blocks[1], gate_sent])
+    acts.near([gate_far, gate_sent])
+    model_sum = lax.psum(after(model_part, gate_sent), "tensor")
+    gate_near = forward(after(acts.blocks[0], last, gate_sent), w_gate)
+    up_near = forward(after(acts.blocks[0], gate_near, up_sent), w_up)
+    grad.near([up_sent, up_near])
     last = up_near
-    jobs.append((backward, features_here(grad_blocks), w_down))
     for step in range(1, n_ex):
-        down_far = products(2, step, last, *arrived[0])
+        down_far = dot_rows(after(grad.blocks[step], last, *arrived[0]), w_down)
         down_sent = send(2, step, down_far)
         last = down_far
-    down_near = products(2, 0, last)
+    down_near = dot_rows(after(grad.blocks[0], last, down_sent, *arrived[1]), w_down)
     own = [core_sum(gate_near), core_sum(up_near), core_sum(down_near)]
     gate_act, up_act, d_hidden = [
         kept + sum(unpack(received) for received in got) for kept, got in zip(own, arrived)

time: 237 us -> 203 us (0.86)
  waiting for transfers between devices: 91.9 us -> 67.6 us
  matrix products: 58.3 us -> 36.3 us
  Pallas kernels: 0 us -> 9.24 us
  other arithmetic: 8.81 us -> 17.7 us
  local copies, waits for them, and re-layouts: 16.6 us -> 11.1 us
    ppermute x22 -> x16, starting transfers between devices: 40 us -> 14 us  [shift(): return lax.ppermute(value, axis, [(i, (i + step) % n) for i in range(n)])]
    ppermute x6 -> x8, starting transfers between devices: 4.1 us -> 29.7 us  [direct_features(): pieces.append(lax.ppermute(start, ('tensor', 'example', 'test'), pairs))]
    dot_general x6 -> x4, matrix products: 39.3 us -> 17.5 us  [forward(): return jnp.dot(tokens, weight, preferred_element_type=F32)]
    ppermute x22 -> x16, waiting for transfers between devices: 44.6 us -> 25.9 us  [shift(): return lax.ppermute(value, axis, [(i, (i + step) % n) for i in range(n)])]
    ppermute x6 -> x8, waiting for transfers between devices: 43.7 us -> 28.1 us  [direct_features(): pieces.append(lax.ppermute(start, ('tensor', 'example', 'test'), pairs))]
    psum x1, waiting for transfers between devices: 0.01 us -> 10.1 us  [on_device(): model_sum = lax.psum(after(model_part, gate_sent), 'tensor')]
    convert_element_type x3 -> x9, other arithmetic: 3.34 us -> 13 us  [pack(): return (value * SEND_SCALE).astype(jnp.float16)]
    pallas_call x0 -> x2, Pallas kernels: none -> 9.24 us  [dot_rows(): pl.pallas_call(dot_rows_kernel, out_shape=jax.ShapeDtypeStruct((rows, hid...]
  transfers between devices with their start and end apart: 32 -> 28, of which waited for: 14 -> 11; matrix products, arithmetic and copies ran while one was open for 28% -> 18% of each run, Pallas kernels for 0% -> 5%
where the time goes in v3:
time: 203 us
  waiting for transfers between devices  67.6 us (33%)
  starting transfers between devices  46.1 us (23%)
  matrix products  36.3 us (18%)
  other arithmetic  17.7 us (9%)
  between operations  14.6 us (7%)
  local copies, waits for them, and re-layouts  11.1 us (5%)
  Pallas kernels  9.24 us (5%)
    ppermute x8, starting transfers between devices, direct_features(): pieces.append(lax.ppermute(start, ('tensor', 'example', 'test'), pairs))  29.7 us
    ppermute x8, waiting for transfers between devices, direct_features(): pieces.append(lax.ppermute(start, ('tensor', 'example', 'test'), pairs))  28.1 us
    ppermute x16, waiting for transfers between devices, shift(): return lax.ppermute(value, axis, [(i, (i + step) % n) for i in range(n)])  25.9 us
    dot_general x4, matrix products, forward(): return jnp.dot(tokens, weight, preferred_element_type=F32)  17.5 us
    ppermute x16, starting transfers between devices, shift(): return lax.ppermute(value, axis, [(i, (i + step) % n) for i in range(n)])  14 us
    convert_element_type x9, other arithmetic, pack(): return (value * SEND_SCALE).astype(jnp.float16)  13 us
    psum x1, waiting for transfers between devices, on_device(): model_sum = lax.psum(after(model_part, gate_sent), 'tensor')  10.1 us
    unnamed x49, local copies, waits for them, and re-layouts  9.65 us
  transfers between devices with their start and end apart: 28, of which 11 were waited for; matrix products, arithmetic and copies ran while one was open for 18% of the time, Pallas kernels for 5%

profile of v3, /device:TPU:0, one launch (start us, length us, event | category | flops | bytes accessed | tf_op | source)
XLA Modules:
  0.0 202.5 jit_solution(570435167113300680)
XLA Ops:
  7.2 1.6 collective-permute-start.1
  8.9 1.3 collective-permute-start
  10.2 21.3 %collective-permute-done = bf16[256,1280]{1,0:T(8,128)(2,1)} collective-permute-done((bf16[256,1280]{1,0:T(8,128)(2,1)}, bf16[256,1280]{1,0:T(8,128)(2,1)}, u32[]{:S(2)}, u32[]{:S(2)}) %collective-permute-start) | collective-permute-done | bytes 655392 | tf_op jit(solution)/shard_map/ppermute | solution.py:96
  31.5 1.3 broadcast_select_fusion.3
  32.9 5.7 %fusion.34 = f32[256,4096]{1,0:T(8,128)S(1)} fusion(bf16[256,1280]{1,0:T(8,128)(2,1)S(1)} %broadcast_select_fusion.3, bf16[1280,4096]{1,0:T(8,128)(2,1)} %param.12), kind=kOutput, calls=%fused_computation.86 | convolution fusion | flops 2684354560 | bytes 15335424 | tf_op jit(solution)/shard_map/dot_general | solution.py:153
  39.1 2.9 %fusion.35 = f32[256,4096]{1,0:T(8,128)S(1)} fusion(bf16[256,1280]{1,0:T(8,128)(2,1)S(1)} %broadcast_select_fusion.3, bf16[1280,4096]{1,0:T(8,128)(2,1)S(1)} %bitcast.78), kind=kOutput, calls=%fused_computation.87 | convolution fusion | flops 2684354560 | bytes 15335424 | tf_op jit(solution)/shard_map/dot_general | solution.py:153
  44.7 15.5 %collective-permute-start.6 = (bf16[256,1280]{1,0:T(8,128)(2,1)S(1)}, bf16[256,1280]{1,0:T(8,128)(2,1)S(1)}, u32[]{:S(2)}, u32[]{:S(2)}) collective-permute-start(bf16[256,1280]{1,0:T(8,128)(2,1)S(1)} %bitcast.68), channel_id=1, source_target_pairs={{0,8},{1,12},{4,9},{5,13},{10,2},{11,6},{14,3},{15,7},{16,24},{17,... | collective-permute-start | bytes 1966088 | tf_op jit(solution)/shard_map/ppermute | solution.py:96
  60.2 1.4 fusion.8
  61.6 1.3 collective-permute-start.8
  62.9 2.7 %collective-permute-start.10 = (f16[256,2048]{1,0:T(8,128)(2,1)S(1)}, f16[256,2048]{1,0:T(8,128)(2,1)}, u32[]{:S(2)}, u32[]{:S(2)}) collective-permute-start(f16[256,2048]{1,0:T(8,128)(2,1)S(1)} %multiply_convert_fusion.8), channel_id=1, source_target_pairs={{0,2},{2,0},{1,3},{3,1},{4,6},{6,4},{5,7},{7,5},{8,10},{10,8},{9,1... | collective-permute-start | bytes 3145736 | tf_op jit(solution)/shard_map/ppermute | solution.py:15
  65.7 1.4 multiply_convert_fusion.10
  67.9 6.8 %collective-permute-done.6 = bf16[256,1280]{1,0:T(8,128)(2,1)S(1)} collective-permute-done((bf16[256,1280]{1,0:T(8,128)(2,1)S(1)}, bf16[256,1280]{1,0:T(8,128)(2,1)S(1)}, u32[]{:S(2)}, u32[]{:S(2)}) %collective-permute-start.6) | collective-permute-done | bytes 655392 | tf_op jit(solution)/shard_map/ppermute | solution.py:96
  74.7 6.5 %collective-permute-start.3 = (bf16[256,1280]{1,0:T(8,128)(2,1)}, bf16[256,1280]{1,0:T(8,128)(2,1)}, u32[]{:S(2)}, u32[]{:S(2)}) collective-permute-start(bf16[256,1280]{1,0:T(8,128)(2,1)} %bitcast), channel_id=1, source_target_pairs={{0,0},{1,4},{4,1},{5,5},{10,10},{11,14},{14,11},{15,15},{16,16},{1... | collective-permute-start | bytes 1966088 | tf_op jit(solution)/shard_map/ppermute | solution.py:96
  81.3 4.4 %fusion.36 = f32[256,4096]{1,0:T(8,128)} fusion(bf16[256,1280]{1,0:T(8,128)(2,1)S(1)} %broadcast_select_fusion.2, bf16[1280,4096]{1,0:T(8,128)(2,1)S(1)} %bitcast.76), kind=kOutput, calls=%fused_computation.88 | convolution fusion | flops 2684354560 | bytes 15335424 | tf_op jit(solution)/shard_map/dot_general | solution.py:153
  85.7 4.5 %fusion.37 = f32[256,4096]{1,0:T(8,128)} fusion(bf16[256,1280]{1,0:T(8,128)(2,1)S(1)} %broadcast_select_fusion.2, bf16[1280,4096]{1,0:T(8,128)(2,1)S(1)} %bitcast.78), kind=kOutput, calls=%fused_computation.89 | convolution fusion | flops 2684354560 | bytes 15335424 | tf_op jit(solution)/shard_map/dot_general | solution.py:153
  90.2 2.1 %collective-permute-start.7 = (bf16[256,1280]{1,0:T(8,128)(2,1)}, bf16[256,1280]{1,0:T(8,128)(2,1)}, u32[]{:S(2)}, u32[]{:S(2)}) collective-permute-start(bf16[256,1280]{1,0:T(8,128)(2,1)} %bitcast), channel_id=1, source_target_pairs={{0,8},{1,12},{4,9},{5,13},{10,2},{11,6},{14,3},{15,7},{16,24},{17,... | collective-permute-start | bytes 1966088 | tf_op jit(solution)/shard_map/ppermute | solution.py:96
  92.4 18.5 %collective-permute-done.10 = f16[256,2048]{1,0:T(8,128)(2,1)} collective-permute-done((f16[256,2048]{1,0:T(8,128)(2,1)S(1)}, f16[256,2048]{1,0:T(8,128)(2,1)}, u32[]{:S(2)}, u32[]{:S(2)}) %collective-permute-start.10) | collective-permute-done | bytes 1048608 | tf_op jit(solution)/shard_map/ppermute | solution.py:15
  111.0 4.6 %shard_map.113 = f32[256,4096]{1,0:T(8,128)S(1)} custom-call(bf16[256,1280]{1,0:T(8,128)(2,1)S(1)} %broadcast_select_fusion.tokens_ref, bf16[4096,1280]{1,0:T(8,128)(2,1)S(1)} %bitcast.63), custom_call_target="tpu_custom_call" | custom-call | flops 2684354560 | bytes 14680064 | tf_op jit(solution)/shard_map/pallas_call | solution.py:111
  115.6 2.1 %copy-done.2 = f32[256,4096]{1,0:T(8,128)} copy-done((f32[256,4096]{1,0:T(8,128)}, f32[256,4096]{1,0:T(8,128)S(1)}, u32[]{:S(2)}) %copy-start.2) | copy-done | bytes 4194328
  117.7 1.2 multiply_convert_fusion.7
  119.6 2.8 %multiply_convert_fusion.3 = f16[256,2048]{1,0:T(8,128)(2,1)} fusion(f32[256,4096]{1,0:T(8,128)} %fusion.36, s32[]{:T(128)S(6)} %select_n.62), kind=kLoop, calls=%fused_computation.8 | loop fusion | flops 1048576 | bytes 3145732 | tf_op jit(solution)/shard_map/convert_element_type | solution.py:19
  122.4 2.9 %multiply_convert_fusion.4 = f16[256,2048]{1,0:T(8,128)(2,1)} fusion(f32[256,4096]{1,0:T(8,128)} %fusion.37, s32[]{:T(128)S(6)} %select_n.62), kind=kLoop, calls=%fused_computation.10 | loop fusion | flops 1048576 | bytes 3145732 | tf_op jit(solution)/shard_map/convert_element_type | solution.py:19
  125.8 1.2 broadcast_select_fusion.1.tokens_ref
  127.0 2.7 %multiply_convert_fusion.6 = f16[256,2048]{1,0:T(8,128)(2,1)} fusion(f16[256,2048]{1,0:T(8,128)(2,1)} %collective-permute-done.11, f32[256,4096]{1,0:T(8,128)S(1)} %copy-done.3, s32[]{:T(128)S(6)} %select_n.61), kind=kLoop, calls=%fused_computation.13 | loop fusion | flops 2621440 | bytes 4194308 | tf_op jit(solution)/shard_map/convert_element_type | solution.py:19
  129.7 2.0 %collective-permute-start.14 = (f16[256,2048]{1,0:T(8,128)(2,1)}, f16[256,2048]{1,0:T(8,128)(2,1)}, u32[]{:S(2)}, u32[]{:S(2)}) collective-permute-start(f16[256,2048]{1,0:T(8,128)(2,1)} %multiply_convert_fusion.6), channel_id=1, source_target_pairs={{0,2},{2,0},{1,3},{3,1},{4,6},{6,4},{5,7},{7,5},{8,10},{10,8},{9,1... | collective-permute-start | bytes 3145736 | tf_op jit(solution)/shard_map/ppermute | solution.py:15
  131.7 4.0 %copy-done.1 = bf16[4096,1280]{1,0:T(8,128)(2,1)S(1)} copy-done((bf16[4096,1280]{1,0:T(8,128)(2,1)S(1)}, bf16[4096,1280]{1,0:T(8,128)(2,1)}, u32[]{:S(2)}) %copy-start.1) | copy-done | bytes 10485784
  135.7 4.6 %shard_map.114 = f32[256,4096]{1,0:T(8,128)S(1)} custom-call(bf16[256,1280]{1,0:T(8,128)(2,1)S(1)} %broadcast_select_fusion.1.tokens_ref, bf16[4096,1280]{1,0:T(8,128)(2,1)S(1)} %copy-done.1), custom_call_target="tpu_custom_call" | custom-call | flops 2684354560 | bytes 14680064 | tf_op jit(solution)/shard_map/pallas_call | solution.py:111
  140.4 2.1 %copy-done.4 = f32[256,4096]{1,0:T(8,128)} copy-done((f32[256,4096]{1,0:T(8,128)}, f32[256,4096]{1,0:T(8,128)S(1)}, u32[]{:S(2)}) %copy-start.4) | copy-done | bytes 4194328
  142.4 1.2 multiply_convert_fusion.5
  143.7 10.1 %all-reduce.2.cloned.1.call-done = f32[2,128,192]{1,2,0:T(8,128)} async-done(((f32[2,128,192]{1,2,0:T(8,128)}), f32[2,128,192]{1,2,0:T(8,128)}) %all-reduce.2.cloned.1.call-update) | async-done | bytes 196624 | tf_op jit(solution)/shard_map/psum | solution.py:189
  153.7 0.9 broadcast_multiply_fusion
  154.7 5.0 %convolution_bitcast_fusion.1 = f32[8,2,8,128]{3,2,1,0:T(8,128)S(1)} fusion(f16[256,2048]{1,0:T(8,128)(2,1)} %collective-permute-done.12, f16[256,2048]{1,0:T(8,128)(2,1)} %collective-permute-done.15, f32[256,4096]{1,0:T(8,128)} %fusion.37, s32[]{:T(128)S(6)} %select_n.61, bf16[4096,192]{0,1:T(8,128)(2,1)} %param.16, s32[]{:T(128)S(6)} %add.148, ...), kind=kOutput, calls=%fused_computation.20 | convolution fusion | flops 76546048 | bytes 8717824 | tf_op jit(solution)/shard_map/dot_general | solution.py:214
  160.7 4.0 %convolution_bitcast_fusion.3 = f32[8,2,8,128]{3,2,1,0:T(8,128)S(1)} fusion(f16[256,2048]{1,0:T(8,128)(2,1)} %collective-permute-done.14, f16[256,2048]{1,0:T(8,128)(2,1)} %collective-permute-done.13, f32[256,4096]{1,0:T(8,128)S(1)} %copy-done.5, s32[]{:T(128)S(6)} %select_n.61, bf16[4096,192]{0,1:T(8,128)(2,1)} %param.16, s32[]{:T(128)S(6)} %add.147, ...), kind=kOutput, calls=%fused_computation.22 | convolution fusion | flops 76546048 | bytes 8717824 | tf_op jit(solution)/shard_map/dot_general | solution.py:213
  165.0 5.1 %convolution_bitcast_fusion.5 = f32[8,2,8,128]{3,2,1,0:T(8,128)S(1)} fusion(f16[256,2048]{1,0:T(8,128)(2,1)} %collective-permute-done.14, f16[256,2048]{1,0:T(8,128)(2,1)} %collective-permute-done.13, f32[256,4096]{1,0:T(8,128)S(1)} %copy-done.5, s32[]{:T(128)S(6)} %select_n.61, f16[256,2048]{1,0:T(8,128)(2,1)} %collective-permute-done.12, ...), kind=kOutput, calls=%fused_computation.24 | convolution fusion | flops 81788928 | bytes 12911616 | tf_op jit(solution)/shard_map/dot_general | solution.py:212
  170.3 1.4 collective-permute-start.17
  171.7 2.5 %collective-permute-start.19 = (f32[2,3,16,64]{3,2,0,1:T(8,128)S(1)}, f32[2,3,16,64]{3,2,0,1:T(8,128)}, u32[]{:S(2)}, u32[]{:S(2)}) collective-permute-start(f32[2,3,16,64]{3,2,0,1:T(8,128)S(1)} %get-tuple-element.31), channel_id=1, source_target_pairs={{0,12},{4,0},{8,4},{12,8},{1,13},{5,1},{9,5},{13,9},{2,14},{6,2},{... | collective-permute-start | bytes 73736 | tf_op jit(solution)/shard_map/ppermute | solution.py:15
  174.5 1.4 collective-permute-start.26
  176.8 2.5 %collective-permute-done.18 = f32[2,3,16,64]{3,2,0,1:T(8,128)} collective-permute-done((f32[2,3,16,64]{3,2,0,1:T(8,128)S(1)}, f32[2,3,16,64]{3,2,0,1:T(8,128)}, u32[]{:S(2)}, u32[]{:S(2)}) %collective-permute-start.18) | collective-permute-done | bytes 24608 | tf_op jit(solution)/shard_map/ppermute | solution.py:15
  179.3 0.8 add_add_fusion
  180.2 1.6 collective-permute-start.21
  182.4 1.4 collective-permute-done.21
  183.8 2.1 %collective-permute-done.20 = f32[2,3,16,64]{3,2,0,1:T(8,128)S(1)} collective-permute-done((f32[2,3,16,64]{3,2,0,1:T(8,128)S(1)}, f32[2,3,16,64]{3,2,0,1:T(8,128)S(1)}, u32[]{:S(2)}, u32[]{:S(2)}) %collective-permute-start.20) | collective-permute-done | bytes 24608 | tf_op jit(solution)/shard_map/ppermute | solution.py:244
  186.0 1.4 fusion
  187.4 0.9 collective-permute-start.23
  188.4 1.1 collective-permute-start.25
  190.1 1.0 collective-permute-done.23
  191.1 3.0 %collective-permute-done.24 = f32[4,512]{1,0:T(4,128)S(1)} collective-permute-done((f32[4,512]{1,0:T(4,128)S(1)}, f32[4,512]{1,0:T(4,128)S(1)}, u32[]{:S(2)}, u32[]{:S(2)}) %collective-permute-start.24) | collective-permute-done | bytes 8224 | tf_op jit(solution)/shard_map/ppermute | solution.py:15
  194.8 0.9 fusion.26
  (107 shorter events, 10.1 us)
Async XLA Ops:
  7.2 178.9 %copy-start = (bf16[3,16,64,512]{3,2,1,0:T(8,128)(2,1)S(1)}, bf16[3,16,64,512]{3,2,1,0:T(8,128)(2,1)}, u32[]{:S(2)}) copy-start(bf16[3,16,64,512]{3,2,1,0:T(8,128)(2,1)} %param.17) | copy-start | bytes 9437188
  7.2 146.6 %all-reduce.2.cloned.1.call-start = ((), (), s32[]{:S(2)}) async-start(), calls=%async_computation | async-start | bytes 393216 | tf_op jit(solution)/shard_map/psum | solution.py:189
  7.2 3.0 %collective-permute-start.1 = (bf16[256,1280]{1,0:T(8,128)(2,1)}, bf16[256,1280]{1,0:T(8,128)(2,1)}, u32[]{:S(2)}, u32[]{:S(2)}) collective-permute-start(bf16[256,1280]{1,0:T(8,128)(2,1)} %bitcast.64), channel_id=1, source_target_pairs={{2,8},{3,12},{6,9},{7,13},{8,2},{9,6},{12,3},{13,7},{18,24},{19,28... | collective-permute-start | bytes 1966088 | tf_op jit(solution)/shard_map/ppermute | solution.py:96
  8.9 22.7 %collective-permute-start = (bf16[256,1280]{1,0:T(8,128)(2,1)}, bf16[256,1280]{1,0:T(8,128)(2,1)}, u32[]{:S(2)}, u32[]{:S(2)}) collective-permute-start(bf16[256,1280]{1,0:T(8,128)(2,1)} %bitcast.65), channel_id=1, source_target_pairs={{2,0},{3,4},{6,1},{7,5},{8,10},{9,14},{12,11},{13,15},{18,16},{19,... | collective-permute-start | bytes 1966088 | tf_op jit(solution)/shard_map/ppermute | solution.py:96
  31.5 7.4 %slice-start.6 = ((s8[10485760]{0:T(1024)(128)(4,1)}), s8[4194304]{0:T(1024)(128)(4,1)S(1)}, s32[]{:S(2)}) async-start(s8[10485760]{0:T(1024)(128)(4,1)} %bitcast.77), calls=%async_computation.7 | async-start | bytes 8388608
  32.8 6.1 %slice-start.7 = ((s8[10485760]{0:T(1024)(128)(4,1)}), s8[4194304]{0:T(1024)(128)(4,1)S(1)}, s32[]{:S(2)}) async-start(s8[10485760]{0:T(1024)(128)(4,1)} %bitcast.77), calls=%async_computation.8 | async-start | bytes 8388608
  32.9 6.2 %slice-start.8 = ((s8[10485760]{0:T(1024)(128)(4,1)}), s8[2097152]{0:T(1024)(128)(4,1)S(1)}, s32[]{:S(2)}) async-start(s8[10485760]{0:T(1024)(128)(4,1)} %bitcast.77), calls=%async_computation.9 | async-start | bytes 4194304
  38.8 5.4 %collective-permute-start.5 = (f16[256,2048]{1,0:T(8,128)(2,1)S(1)}, f16[256,2048]{1,0:T(8,128)(2,1)S(1)}, u32[]{:S(2)}, u32[]{:S(2)}) collective-permute-start(f16[256,2048]{1,0:T(8,128)(2,1)S(1)} %multiply_convert_fusion.9), channel_id=1, source_target_pairs={{0,1},{1,0},{2,3},{3,2},{4,5},{5,4},{6,7},{7,6},{8,9},{9,8},{10,11... | collective-permute-start | bytes 3145736 | tf_op jit(solution)/shard_map/ppermute | solution.py:15
  39.1 42.2 %slice-start.3 = ((s8[10485760]{0:T(1024)(128)(4,1)}), s8[4194304]{0:T(1024)(128)(4,1)S(1)}, s32[]{:S(2)}) async-start(s8[10485760]{0:T(1024)(128)(4,1)} %bitcast.75), calls=%async_computation.4 | async-start | bytes 8388608
  39.1 42.2 %slice-start.4 = ((s8[10485760]{0:T(1024)(128)(4,1)}), s8[4194304]{0:T(1024)(128)(4,1)S(1)}, s32[]{:S(2)}) async-start(s8[10485760]{0:T(1024)(128)(4,1)} %bitcast.75), calls=%async_computation.5 | async-start | bytes 8388608
  42.0 1.2 copy-start.9
  42.2 39.1 %slice-start.5 = ((s8[10485760]{0:T(1024)(128)(4,1)}), s8[2097152]{0:T(1024)(128)(4,1)S(1)}, s32[]{:S(2)}) async-start(s8[10485760]{0:T(1024)(128)(4,1)} %bitcast.75), calls=%async_computation.6 | async-start | bytes 4194304
  42.2 23.5 %collective-permute-start.2 = (f16[256,2048]{1,0:T(8,128)(2,1)S(1)}, f16[256,2048]{1,0:T(8,128)(2,1)S(1)}, u32[]{:S(2)}, u32[]{:S(2)}) collective-permute-start(f16[256,2048]{1,0:T(8,128)(2,1)S(1)} %multiply_convert_fusion.11), channel_id=1, source_target_pairs={{0,1},{1,0},{2,3},{3,2},{4,5},{5,4},{6,7},{7,6},{8,9},{9,8},{10,11... | collective-permute-start | bytes 3145736 | tf_op jit(solution)/shard_map/ppermute | solution.py:15
  43.5 23.6 %collective-permute-start.4 = (bf16[256,1280]{1,0:T(8,128)(2,1)S(1)}, bf16[256,1280]{1,0:T(8,128)(2,1)S(1)}, u32[]{:S(2)}, u32[]{:S(2)}) collective-permute-start(bf16[256,1280]{1,0:T(8,128)(2,1)S(1)} %bitcast.67), channel_id=1, source_target_pairs={{0,0},{1,4},{4,1},{5,5},{10,10},{11,14},{14,11},{15,15},{16,16},{1... | collective-permute-start | bytes 1966088 | tf_op jit(solution)/shard_map/ppermute | solution.py:96
  44.7 30.0 %collective-permute-start.6 = (bf16[256,1280]{1,0:T(8,128)(2,1)S(1)}, bf16[256,1280]{1,0:T(8,128)(2,1)S(1)}, u32[]{:S(2)}, u32[]{:S(2)}) collective-permute-start(bf16[256,1280]{1,0:T(8,128)(2,1)S(1)} %bitcast.68), channel_id=1, source_target_pairs={{0,8},{1,12},{4,9},{5,13},{10,2},{11,6},{14,3},{15,7},{16,24},{17,... | collective-permute-start | bytes 1966088 | tf_op jit(solution)/shard_map/ppermute | solution.py:96
  61.6 28.6 %collective-permute-start.8 = (bf16[256,1280]{1,0:T(8,128)(2,1)}, bf16[256,1280]{1,0:T(8,128)(2,1)S(1)}, u32[]{:S(2)}, u32[]{:S(2)}) collective-permute-start(bf16[256,1280]{1,0:T(8,128)(2,1)} %bitcast), channel_id=1, source_target_pairs={{2,0},{3,4},{6,1},{7,5},{8,10},{9,14},{12,11},{13,15},{18,16},{19,... | collective-permute-start | bytes 1966088 | tf_op jit(solution)/shard_map/ppermute | solution.py:96
  62.9 48.0 %collective-permute-start.10 = (f16[256,2048]{1,0:T(8,128)(2,1)S(1)}, f16[256,2048]{1,0:T(8,128)(2,1)}, u32[]{:S(2)}, u32[]{:S(2)}) collective-permute-start(f16[256,2048]{1,0:T(8,128)(2,1)S(1)} %multiply_convert_fusion.8), channel_id=1, source_target_pairs={{0,2},{2,0},{1,3},{3,1},{4,6},{6,4},{5,7},{7,5},{8,10},{10,8},{9,1... | collective-permute-start | bytes 3145736 | tf_op jit(solution)/shard_map/ppermute | solution.py:15
  67.1 64.6 %collective-permute-start.12 = (f16[256,2048]{1,0:T(8,128)(2,1)}, f16[256,2048]{1,0:T(8,128)(2,1)}, u32[]{:S(2)}, u32[]{:S(2)}) collective-permute-start(f16[256,2048]{1,0:T(8,128)(2,1)} %multiply_convert_fusion.10), channel_id=1, source_target_pairs={{0,2},{2,0},{1,3},{3,1},{4,6},{6,4},{5,7},{7,5},{8,10},{10,8},{9,1... | collective-permute-start | bytes 3145736 | tf_op jit(solution)/shard_map/ppermute | solution.py:15
  67.2 25.2 %collective-permute-start.9 = (bf16[256,1280]{1,0:T(8,128)(2,1)}, bf16[256,1280]{1,0:T(8,128)(2,1)S(1)}, u32[]{:S(2)}, u32[]{:S(2)}) collective-permute-start(bf16[256,1280]{1,0:T(8,128)(2,1)} %bitcast), channel_id=1, source_target_pairs={{2,8},{3,12},{6,9},{7,13},{8,2},{9,6},{12,3},{13,7},{18,24},{19,28... | collective-permute-start | bytes 1966088 | tf_op jit(solution)/shard_map/ppermute | solution.py:96
  74.7 51.1 %collective-permute-start.3 = (bf16[256,1280]{1,0:T(8,128)(2,1)}, bf16[256,1280]{1,0:T(8,128)(2,1)}, u32[]{:S(2)}, u32[]{:S(2)}) collective-permute-start(bf16[256,1280]{1,0:T(8,128)(2,1)} %bitcast), channel_id=1, source_target_pairs={{0,0},{1,4},{4,1},{5,5},{10,10},{11,14},{14,11},{15,15},{16,16},{1... | collective-permute-start | bytes 1966088 | tf_op jit(solution)/shard_map/ppermute | solution.py:96
  81.3 29.7 %slice-start = ((s8[10485760]{0:T(1024)(128)(4,1)}), s8[4194304]{0:T(1024)(128)(4,1)S(1)}, s32[]{:S(2)}) async-start(s8[10485760]{0:T(1024)(128)(4,1)} %bitcast.62), calls=%async_computation.1 | async-start | bytes 8388608
  81.3 29.7 %slice-start.1 = ((s8[10485760]{0:T(1024)(128)(4,1)}), s8[4194304]{0:T(1024)(128)(4,1)S(1)}, s32[]{:S(2)}) async-start(s8[10485760]{0:T(1024)(128)(4,1)} %bitcast.62), calls=%async_computation.2 | async-start | bytes 8388608
  85.7 25.2 %slice-start.2 = ((s8[10485760]{0:T(1024)(128)(4,1)}), s8[2097152]{0:T(1024)(128)(4,1)S(1)}, s32[]{:S(2)}) async-start(s8[10485760]{0:T(1024)(128)(4,1)} %bitcast.62), calls=%async_computation.3 | async-start | bytes 4194304
  90.2 35.6 %collective-permute-start.7 = (bf16[256,1280]{1,0:T(8,128)(2,1)}, bf16[256,1280]{1,0:T(8,128)(2,1)}, u32[]{:S(2)}, u32[]{:S(2)}) collective-permute-start(bf16[256,1280]{1,0:T(8,128)(2,1)} %bitcast), channel_id=1, source_target_pairs={{0,8},{1,12},{4,9},{5,13},{10,2},{11,6},{14,3},{15,7},{16,24},{17,... | collective-permute-start | bytes 1966088 | tf_op jit(solution)/shard_map/ppermute | solution.py:96
  115.6 2.1 %copy-start.2 = (f32[256,4096]{1,0:T(8,128)}, f32[256,4096]{1,0:T(8,128)S(1)}, u32[]{:S(2)}) copy-start(f32[256,4096]{1,0:T(8,128)S(1)} %shard_map.113) | copy-start | bytes 12582916
  118.9 8.1 %collective-permute-start.11 = (f16[256,2048]{1,0:T(8,128)(2,1)}, f16[256,2048]{1,0:T(8,128)(2,1)}, u32[]{:S(2)}, u32[]{:S(2)}) collective-permute-start(f16[256,2048]{1,0:T(8,128)(2,1)} %multiply_convert_fusion.7), channel_id=1, source_target_pairs={{0,1},{1,0},{2,3},{3,2},{4,5},{5,4},{6,7},{7,6},{8,9},{9,8},{10,11... | collective-permute-start | bytes 3145736 | tf_op jit(solution)/shard_map/ppermute | solution.py:15
  122.4 4.6 %copy-start.3 = (f32[256,4096]{1,0:T(8,128)S(1)}, f32[256,4096]{1,0:T(8,128)}, u32[]{:S(2)}) copy-start(f32[256,4096]{1,0:T(8,128)} %copy-done.2) | copy-start | bytes 12582916
  125.3 29.4 %collective-permute-start.16 = (f16[256,2048]{1,0:T(8,128)(2,1)}, f16[256,2048]{1,0:T(8,128)(2,1)}, u32[]{:S(2)}, u32[]{:S(2)}) collective-permute-start(f16[256,2048]{1,0:T(8,128)(2,1)} %multiply_convert_fusion.3), channel_id=1, source_target_pairs={{0,1},{1,0},{2,3},{3,2},{4,5},{5,4},{6,7},{7,6},{8,9},{9,8},{10,11... | collective-permute-start | bytes 3145736 | tf_op jit(solution)/shard_map/ppermute | solution.py:15
  125.8 28.9 %collective-permute-start.15 = (f16[256,2048]{1,0:T(8,128)(2,1)}, f16[256,2048]{1,0:T(8,128)(2,1)}, u32[]{:S(2)}, u32[]{:S(2)}) collective-permute-start(f16[256,2048]{1,0:T(8,128)(2,1)} %multiply_convert_fusion.4), channel_id=1, source_target_pairs={{0,1},{1,0},{2,3},{3,2},{4,5},{5,4},{6,7},{7,6},{8,9},{9,8},{10,11... | collective-permute-start | bytes 3145736 | tf_op jit(solution)/shard_map/ppermute | solution.py:15
  129.7 30.3 %collective-permute-start.14 = (f16[256,2048]{1,0:T(8,128)(2,1)}, f16[256,2048]{1,0:T(8,128)(2,1)}, u32[]{:S(2)}, u32[]{:S(2)}) collective-permute-start(f16[256,2048]{1,0:T(8,128)(2,1)} %multiply_convert_fusion.6), channel_id=1, source_target_pairs={{0,2},{2,0},{1,3},{3,1},{4,6},{6,4},{5,7},{7,5},{8,10},{10,8},{9,1... | collective-permute-start | bytes 3145736 | tf_op jit(solution)/shard_map/ppermute | solution.py:15
  131.7 4.0 %copy-start.1 = (bf16[4096,1280]{1,0:T(8,128)(2,1)S(1)}, bf16[4096,1280]{1,0:T(8,128)(2,1)}, u32[]{:S(2)}) copy-start(bf16[4096,1280]{1,0:T(8,128)(2,1)} %weight_ref.3) | copy-start | bytes 31457284
  140.3 2.1 %copy-start.4 = (f32[256,4096]{1,0:T(8,128)}, f32[256,4096]{1,0:T(8,128)S(1)}, u32[]{:S(2)}) copy-start(f32[256,4096]{1,0:T(8,128)S(1)} %shard_map.114) | copy-start | bytes 12582916
  142.4 1.2 copy-start.11
  143.6 16.4 %collective-permute-start.13 = (f16[256,2048]{1,0:T(8,128)(2,1)}, f16[256,2048]{1,0:T(8,128)(2,1)}, u32[]{:S(2)}, u32[]{:S(2)}) collective-permute-start(f16[256,2048]{1,0:T(8,128)(2,1)} %multiply_convert_fusion.5), channel_id=1, source_target_pairs={{0,1},{1,0},{2,3},{3,2},{4,5},{5,4},{6,7},{7,6},{8,9},{9,8},{10,11... | collective-permute-start | bytes 3145736 | tf_op jit(solution)/shard_map/ppermute | solution.py:15
  154.7 5.3 %copy-start.5 = (f32[256,4096]{1,0:T(8,128)S(1)}, f32[256,4096]{1,0:T(8,128)}, u32[]{:S(2)}) copy-start(f32[256,4096]{1,0:T(8,128)} %copy-done.4) | copy-start | bytes 12582916
  154.7 6.0 %copy-start.6 = (f32[256,4096]{1,0:T(8,128)S(1)}, f32[256,4096]{1,0:T(8,128)}, u32[]{:S(2)}) copy-start(f32[256,4096]{1,0:T(8,128)} %fusion.36) | copy-start | bytes 12582916
  159.9 5.0 %copy-start.7 = (f32[256,4096]{1,0:T(8,128)S(1)}, f32[256,4096]{1,0:T(8,128)}, u32[]{:S(2)}) copy-start(f32[256,4096]{1,0:T(8,128)} %fusion.37) | copy-start | bytes 12582916
  164.9 9.6 %copy-start.10 = (s32[2]{0:T(128)S(1)}, s32[2]{0:T(128)}, u32[]{:S(2)}) copy-start(s32[2]{0:T(128)} %param.19) | copy-start | bytes 28
  170.3 6.0 %collective-permute-start.17 = (f32[2,3,16,64]{3,2,0,1:T(8,128)S(1)}, f32[2,3,16,64]{3,2,0,1:T(8,128)S(1)}, u32[]{:S(2)}, u32[]{:S(2)}) collective-permute-start(f32[2,3,16,64]{3,2,0,1:T(8,128)S(1)} %get-tuple-element.30), channel_id=1, source_target_pairs={{0,4},{4,8},{8,12},{12,0},{1,5},{5,9},{9,13},{13,1},{2,6},{6,10},{... | collective-permute-start | bytes 73736 | tf_op jit(solution)/shard_map/ppermute | solution.py:15
  171.7 5.0 %collective-permute-start.19 = (f32[2,3,16,64]{3,2,0,1:T(8,128)S(1)}, f32[2,3,16,64]{3,2,0,1:T(8,128)}, u32[]{:S(2)}, u32[]{:S(2)}) collective-permute-start(f32[2,3,16,64]{3,2,0,1:T(8,128)S(1)} %get-tuple-element.31), channel_id=1, source_target_pairs={{0,12},{4,0},{8,4},{12,8},{1,13},{5,1},{9,5},{13,9},{2,14},{6,2},{... | collective-permute-start | bytes 73736 | tf_op jit(solution)/shard_map/ppermute | solution.py:15
  174.2 5.1 %collective-permute-start.18 = (f32[2,3,16,64]{3,2,0,1:T(8,128)S(1)}, f32[2,3,16,64]{3,2,0,1:T(8,128)}, u32[]{:S(2)}, u32[]{:S(2)}) collective-permute-start(f32[2,3,16,64]{3,2,0,1:T(8,128)S(1)} %get-tuple-element.32), channel_id=1, source_target_pairs={{0,8},{4,12},{8,0},{12,4},{1,9},{5,13},{9,1},{13,5},{2,10},{6,14},... | collective-permute-start | bytes 73736 | tf_op jit(solution)/shard_map/ppermute | solution.py:15
  174.5 5.7 %collective-permute-start.26 = (s32[2]{0:T(128)S(1)}, s32[2]{0:T(128)S(1)}, u32[]{:S(2)}, u32[]{:S(2)}) collective-permute-start(s32[2]{0:T(128)S(1)} %copy-done.10), channel_id=1, source_target_pairs={{0,2},{2,0},{1,3},{3,1},{4,6},{6,4},{5,7},{7,5},{8,10},{10,8},{9,1... | collective-permute-start | bytes 32 | tf_op jit(solution)/shard_map/ppermute | solution.py:15
  180.1 2.3 %collective-permute-start.22 = (f32[2,3,16,64]{3,2,0,1:T(8,128)S(1)}, f32[2,3,16,64]{3,2,0,1:T(8,128)S(1)}, u32[]{:S(2)}, u32[]{:S(2)}) collective-permute-start(f32[2,3,16,64]{3,2,0,1:T(8,128)S(1)} %add_add_fusion), channel_id=1, source_target_pairs={{0,1},{1,0},{2,3},{3,2},{4,5},{5,4},{6,7},{7,6},{8,9},{9,8},{10,11... | collective-permute-start | bytes 73736 | tf_op jit(solution)/shard_map/ppermute | solution.py:244
  180.2 3.6 %collective-permute-start.21 = (f32[2,3,16,64]{3,2,0,1:T(8,128)S(1)}, f32[2,3,16,64]{3,2,0,1:T(8,128)S(1)}, u32[]{:S(2)}, u32[]{:S(2)}) collective-permute-start(f32[2,3,16,64]{3,2,0,1:T(8,128)S(1)} %add_add_fusion), channel_id=1, source_target_pairs={{0,3},{1,2},{2,1},{3,0},{4,7},{5,6},{6,5},{7,4},{8,11},{9,10},{10,... | collective-permute-start | bytes 73736 | tf_op jit(solution)/shard_map/ppermute | solution.py:244
  181.9 4.1 %collective-permute-start.20 = (f32[2,3,16,64]{3,2,0,1:T(8,128)S(1)}, f32[2,3,16,64]{3,2,0,1:T(8,128)S(1)}, u32[]{:S(2)}, u32[]{:S(2)}) collective-permute-start(f32[2,3,16,64]{3,2,0,1:T(8,128)S(1)} %add_add_fusion), channel_id=1, source_target_pairs={{0,2},{1,3},{2,0},{3,1},{4,6},{5,7},{6,4},{7,5},{8,10},{9,11},{10,... | collective-permute-start | bytes 73736 | tf_op jit(solution)/shard_map/ppermute | solution.py:244
  187.4 3.7 %collective-permute-start.23 = (f32[4,512]{1,0:T(4,128)S(1)}, f32[4,512]{1,0:T(4,128)S(1)}, u32[]{:S(2)}, u32[]{:S(2)}) collective-permute-start(f32[4,512]{1,0:T(4,128)S(1)} %bitcast.70), channel_id=1, source_target_pairs={{0,12},{4,0},{8,4},{12,8},{1,13},{5,1},{9,5},{13,9},{2,14},{6,2},{... | collective-permute-start | bytes 24584 | tf_op jit(solution)/shard_map/ppermute | solution.py:15
  188.4 5.7 %collective-permute-start.25 = (f32[4,512]{1,0:T(4,128)S(1)}, f32[4,512]{1,0:T(4,128)S(1)}, u32[]{:S(2)}, u32[]{:S(2)}) collective-permute-start(f32[4,512]{1,0:T(4,128)S(1)} %bitcast.71), channel_id=1, source_target_pairs={{0,4},{4,8},{8,12},{12,0},{1,5},{5,9},{9,13},{13,1},{2,6},{6,10},{... | collective-permute-start | bytes 24584 | tf_op jit(solution)/shard_map/ppermute | solution.py:15
  189.6 4.5 %collective-permute-start.24 = (f32[4,512]{1,0:T(4,128)S(1)}, f32[4,512]{1,0:T(4,128)S(1)}, u32[]{:S(2)}, u32[]{:S(2)}) collective-permute-start(f32[4,512]{1,0:T(4,128)S(1)} %bitcast.72), channel_id=1, source_target_pairs={{0,8},{4,12},{8,0},{12,4},{1,9},{5,13},{9,1},{13,5},{2,10},{6,14},... | collective-permute-start | bytes 24584 | tf_op jit(solution)/shard_map/ppermute | solution.py:15
  (1 other events, 1.1 us)
Sparse Core Ops, SparseCore 0:
  119.7 33.9 all-reduce.1

commit v4 on v1

v4 whole, which is shorter than its diff:
```python
import functools

import jax
import jax.numpy as jnp
from jax import lax
from jax.experimental import pallas as pl
from jax.experimental.pallas import tpu as pltpu
from jax.sharding import PartitionSpec as P

NGROUP = 4
F32 = jnp.float32
SEND_SCALE = 16.0


def shift(value, axis, step):
    n = lax.axis_size(axis)
    return lax.ppermute(value, axis, [(i, (i + step) % n) for i in range(n)])


def pack(value):
    return (value * SEND_SCALE).astype(jnp.float16)


def unpack(value):
    return value.astype(F32) * (1.0 / SEND_SCALE)


def exchange(blocks, axis):
    return lax.all_to_all(blocks, axis, split_axis=0, concat_axis=0, tiled=True)


def share(value, axis, n):
    return exchange(jnp.broadcast_to(value[None], (n,) + value.shape), axis)


def token(value):
    corner = value[(0,) * (value.ndim - 2)]
    return corner[:16, :128].astype(F32) if value.dtype == jnp.float16 else value


def after(value, *earlier):
    earlier = [token(one) for one in earlier]
    anywhere = pl.BlockSpec(memory_space=pl.ANY)
    return pl.pallas_call(
        lambda *refs: None,
        out_shape=jax.ShapeDtypeStruct(value.shape, value.dtype),
        in_specs=[anywhere] * (1 + len(earlier)),
        out_specs=anywhere,
        input_output_aliases={0: 0},
        cost_estimate=pl.CostEstimate(flops=1, bytes_accessed=1, transcendentals=0),
    )(value, *earlier)


def direct_features(starts, ex_step):
    pieces = []
    for turn in range(2):
        pairs = []
        for block in range(4):
            example, core = block // 2, block % 2
            for source_core in range(2):
                target = block ^ (2 * turn + (source_core ^ core))
                source = block * 4 + (example ^ ex_step) * 2 + source_core
                pairs.append((source, target * 4 + example * 2 + core))
        pieces.append(lax.ppermute(starts[turn], ("tensor", "example", "test"), pairs))
    return pieces


def gathered_features(flat, n_ex, n_cores):
    rows = flat.shape[0]
    part = rows // n_cores
    mine = lax.dynamic_slice_in_dim(flat, lax.axis_index("test") * part, part, 0)
    whole = lax.all_gather(mine, "tensor", axis=1, tiled=True)
    whole = lax.all_to_all(whole, ("example", "test"), split_axis=1, concat_axis=0, tiled=True)
    owners = [lax.rem(lax.axis_index("example") + step, n_ex) for step in range(n_ex)]
    return [lax.dynamic_slice_in_dim(whole, owner * rows, rows, 0) for owner in owners]


def products_kernel(by_rows, n_pieces, n_weights, place_ref, *refs):
    pieces, refs = refs[:n_pieces], refs[n_pieces:]
    weight_refs, refs = refs[:n_weights], refs[n_weights:]
    kept_refs, sent_refs = refs[-1 - 2 * n_weights : -1 : 2], refs[-2 * n_weights : -1 : 2]
    tokens_ref = refs[-1]
    keep = pl.program_id(0) == pl.num_programs(0) - 1

    @pl.when((pl.program_id(0) == 0) & (pl.program_id(1) == 0))
    def _():
        for place, piece in enumerate(pieces):

            @pl.when(place_ref[1] == place)
            def _():
                tokens_ref[...] = piece[...]

    contract = (((1,), (1 if by_rows else 0,)), ((), ()))
    for weight_ref, kept_ref, sent_ref in zip(weight_refs, kept_refs, sent_refs):
        product = lax.dot_general(
            tokens_ref[...], weight_ref[...], contract, preferred_element_type=F32
        )

        @pl.when(keep)
        def _():
            kept_ref[...] = product

        @pl.when(jnp.logical_not(keep))
        def _():
            sent_ref[0] = product


def products(pieces, weights, by_rows, n_cores, *earlier):
    earlier = [token(one) for one in earlier]
    rows, depth = pieces[0].shape
    hidden = weights[0].shape[0 if by_rows else 1] // n_cores
    tile = min(512, hidden)
    tiles = hidden // tile

    def weight_block(turn, i, place_ref):
        block = lax.rem(place_ref[0] + turn + 1, n_cores) * tiles + i
        return (block, 0) if by_rows else (0, block)

    core = lax.axis_index("test")
    holder = lax.axis_index("example") * n_cores + core
    piece = (lax.axis_index("tensor") ^ holder) // 2 if len(pieces) == 2 else 0 * core

    def kept_block(turn, i, place_ref):
        return (0, jnp.where(turn == n_cores - 1, i, 0))

    def sent_block(turn, i, place_ref):
        return (jnp.minimum(turn, n_cores - 2), 0, jnp.where(turn == n_cores - 1, tiles - 1, i))

    outs = pl.pallas_call(
        functools.partial(products_kernel, by_rows, len(pieces), len(weights)),
        out_shape=[
            jax.ShapeDtypeStruct((rows, hidden), F32),
            jax.ShapeDtypeStruct((n_cores - 1, rows, hidden), F32),
        ]
        * len(weights),
        grid_spec=pltpu.PrefetchScalarGridSpec(
            num_scalar_prefetch=1,
            grid=(n_cores, tiles),
            in_specs=[pl.BlockSpec((rows, depth), lambda turn, i, place_ref: (0, 0))] * len(pieces)
            + [pl.BlockSpec((tile, depth) if by_rows else (depth, tile), weight_block)]
            * len(weights)
            + [pl.BlockSpec(memory_space=pl.ANY)] * len(earlier),
            out_specs=[
                pl.BlockSpec((rows, tile), kept_block),
                pl.BlockSpec((1, rows, tile), sent_block),
            ]
            * len(weights),
            scratch_shapes=[pltpu.VMEM((rows, depth), jnp.bfloat16)],
        ),
        compiler_params=pltpu.CompilerParams(vmem_limit_bytes=24 * 2**20),
        cost_estimate=pl.CostEstimate(flops=1, bytes_accessed=1, transcendentals=0),
    )(jnp.stack([core, piece]), *pieces, *weights, *earlier)
    return list(zip(outs[::2], outs[1::2]))


def on_device(
    activations,
    out_grad,
    w_gate,
    w_up,
    w_down,
    proj_model,
    proj_hidden,
    test_grads,
    lengths,
    groups,
):
    ex_loc, seq_len, d_local = activations.shape
    tok_rows = ex_loc * seq_len
    width = proj_model.shape[1] // 3
    n_z = lax.axis_size("tensor")
    n_cores = lax.axis_size("test")
    core = lax.axis_index("test")
    n_ex = lax.axis_size("example")
    ex_index = lax.axis_index("example")
    hid_part = w_gate.shape[1] // n_cores

    def core_swap(product):
        kept, others = product
        packed = [pack(others[step - 1]) for step in range(1, n_cores)]
        got = [shift(sent, "test", step + 1) for step, sent in enumerate(packed)]
        return kept, packed, got

    def core_sum(kept, got):
        return kept + sum(unpack(one) for one in got)

    arrived = [[[] for _ in range(ex_loc)] for _ in range(3)]
    queue = []

    def send(which, e, step, kept, got, *earlier):
        earlier = queue[-2:-1] + list(earlier)
        if earlier:
            kept = after(kept, *earlier)
        sent = pack(core_sum(kept, got))
        queue.append(shift(sent, "example", step))
        arrived[which][e].append(queue[-1])
        return sent

    flat_acts = activations.reshape(tok_rows, d_local)
    flat_grad = out_grad.reshape(tok_rows, d_local)
    model_part = jnp.concatenate(
        [
            jnp.dot(flat_acts, proj_model[:, : 2 * width], preferred_element_type=F32),
            jnp.dot(flat_grad, proj_model[:, 2 * width :], preferred_element_type=F32),
        ],
        1,
    )
    direct = (n_z, n_ex, n_cores) == (4, 2, 2)
    examples = [slice(e * seq_len, (e + 1) * seq_len) for e in range(ex_loc)]
    if direct:
        acts_far = [[direct_features([activations[e]] * 2, 1) for e in range(ex_loc)]]
    else:
        acts_here = gathered_features(flat_acts, n_ex, n_cores)
        grad_here = gathered_features(flat_grad, n_ex, n_cores)
        acts_far = [[[block[rows]] for rows in examples] for block in acts_here[1:]]
    earlier = []
    marks = []
    for e in range(ex_loc):
        for step in range(1, n_ex):
            far = products(acts_far[step - 1][e], (w_gate, w_up), False, n_cores, *earlier)
            swapped = [core_swap(one) for one in far]
            earlier = [packed[-1] for _, packed, _ in swapped]
            marks.append(earlier)
            for which, (kept, _, got) in enumerate(swapped):
                sent = send(which, e, step, kept, got)
    model_sum = lax.psum(after(model_part, marks[0][0]), "tensor")
    if direct:
        start = after(flat_grad, marks[0][1])
        later = after(start, marks[-1][0])
        grad_far = [direct_features([start, later], 1)]
        start = after(flat_acts, marks[-1][1])
        acts_near = direct_features([start, start], 0)
        acts_near = [after(piece, *marks[-1]) for piece in acts_near]
    else:
        grad_far = [[block] for block in grad_here[1:]]
        acts_near = acts_here[:1]
    acts_near = products(acts_near, (w_gate, w_up), False, n_cores, *marks[-1])
    grad_far = [[after(piece, acts_near[0][0]) for piece in pieces] for pieces in grad_far]
    for step in range(1, n_ex):
        (far,) = products(grad_far[step - 1], (w_down,), True, n_cores)
        kept, packed, got = core_swap(far)
        for e, rows in enumerate(examples):
            sent = send(2, e, step, kept[rows], [one[rows] for one in got])
    if direct:
        start = after(flat_grad, acts_near[0][0])
        grad_near = direct_features([start, start], 0)
        grad_near = [after(piece, packed[-1]) for piece in grad_near]
    else:
        grad_near = grad_here[:1]
    (grad_near,) = products(grad_near, (w_down,), True, n_cores, packed[-1])
    model_sum = after(model_sum, grad_near[0])
    own = []
    for near in (*acts_near, grad_near):
        kept, _, got = core_swap(near)
        own.append(lax.optimization_barrier(core_sum(kept, got)))

    def total(which, e):
        kept = own[which][e * seq_len : (e + 1) * seq_len]
        return kept + sum(unpack(one) for one in arrived[which][e])

    hid_proj = lax.dynamic_slice_in_dim(proj_hidden, core * hid_part, hid_part, 0)
    positions = jnp.arange(seq_len, dtype=jnp.int32)
    token_mask = (positions[None, :] < lengths[:, None]).astype(F32)[:, :, None]
    masked = model_sum.reshape(ex_loc, seq_len, 3 * width) * token_mask

    def outer(outputs, inputs):
        product = lax.dot_general(
            outputs, inputs, (((0,), (0,)), ((), ())), precision=lax.Precision.HIGHEST
        )
        return product.reshape(n_z, width // n_z, width)

    factors, hidden_grads = [], []
    for e in range(ex_loc):
        gate_act, up_act = total(0, e), total(1, e)
        sigmoid_gate = jax.nn.sigmoid(gate_act)
        silu_gate = gate_act * sigmoid_gate
        hidden = (silu_gate * up_act).astype(jnp.bfloat16)
        gate_factor = up_act * sigmoid_gate * (1.0 + gate_act * (1.0 - sigmoid_gate))
        factors.append(lax.optimization_barrier((gate_factor, silu_gate)))
        in_hidden = jnp.dot(hidden, hid_proj[:, 2 * width :], preferred_element_type=F32)
        hidden_grads.append(outer(masked[e, :, 2 * width :], in_hidden))
    grads = []
    for e in range(ex_loc):
        d_hidden = total(2, e)
        d_gate = (d_hidden * factors[e][0]).astype(jnp.bfloat16)
        d_up = (d_hidden * factors[e][1]).astype(jnp.bfloat16)
        out_gate = jnp.dot(d_gate, hid_proj[:, :width], preferred_element_type=F32)
        out_up = jnp.dot(d_up, hid_proj[:, width : 2 * width], preferred_element_type=F32)
        grads += [
            outer(out_gate, masked[e, :, :width]),
            outer(out_up, masked[e, :, width : 2 * width]),
            hidden_grads[e],
        ]
    grads = jnp.sum(exchange(jnp.stack(grads, 1), "tensor"), 0)
    grads = share(grads, ("example", "test"), n_ex * n_cores)
    grads = jnp.sum(grads.reshape((n_ex, n_cores) + grads.shape[1:]), 1)
    partial_scores = lax.dot_general(
        grads.reshape(n_ex * ex_loc, -1),
        test_grads.astype(F32).reshape(-1, test_grads.shape[-1]),
        (((1,), (0,)), ((), ())),
        precision=lax.Precision.HIGHEST,
    )
    all_scores = jnp.sum(share(partial_scores, "tensor", n_z), 0)
    scores = lax.dynamic_slice_in_dim(all_scores, ex_index * ex_loc, ex_loc, 0)
    all_groups = [groups] + [shift(groups, "example", step) for step in range(1, n_ex)]
    owners = jnp.stack([lax.rem(ex_index + n_ex - step, n_ex) for step in range(n_ex)])
    all_groups = jnp.zeros((n_ex, ex_loc), jnp.int32).at[owners].set(jnp.stack(all_groups))
    group_onehot = (
        all_groups.reshape(-1)[:, None] == jnp.arange(NGROUP, dtype=jnp.int32)[None, :]
    ).astype(F32)
    group_scores = jnp.dot(group_onehot.T, all_scores, precision=lax.Precision.HIGHEST)
    return (scores, group_scores)


def solution(mesh):
    placed = (
        P(("parts", "example"), None, "tensor"),
        P(("parts", "example"), None, "tensor"),
        P(("example", "test"), "tensor"),
        P(("example", "test"), "tensor"),
        P("tensor", ("example", "test")),
        P("tensor", None),
        P("tensor", None),
        P(None, "tensor", None, "test"),
        P(("parts", "example")),
        P(("parts", "example")),
    )
    return jax.shard_map(
        on_device,
        mesh=mesh,
        in_specs=placed,
        out_specs=(P(("parts", "example"), "test"), P("parts", "test")),
        check_vma=False,
    )
```

time: 258 us -> 309 us (1.20)
  waiting for transfers between devices: 138 us -> 44.1 us
  starting transfers between devices: 23.5 us -> 86.3 us
  matrix products: 58.9 us -> 10.8 us
  Pallas kernels: 0 us -> 46.4 us
  local copies, waits for them, and re-layouts: 13.8 us -> 52.3 us
  other arithmetic: 8.91 us -> 44 us
  blocking collectives: 0 us -> 8.43 us
    all_gather x2 -> x0, waiting for transfers between devices: 62.7 us -> none  [features_here(): whole = lax.all_gather(mine, 'tensor', axis=1, tiled=True)]
    ppermute x17 -> x15, waiting for transfers between devices: 74.9 us -> 21.6 us  [shift(): return lax.ppermute(value, axis, [(i, (i + step) % n) for i in range(n)])]
    pallas_call x0 -> x21, Pallas kernels: none -> 46.4 us  [the longest x5 46.4 us: products(): pl.pallas_call(functools.partial(products_kernel, by_rows, len(pieces), l...]
    dot_general x11 -> x8, matrix products: 43.3 us -> 3.27 us  [the longest x1 1.32 us: on_device(): lax.dot_general(grads.reshape(n_ex * ex_loc, -1), test_grads.astype(F32)....]
    ppermute x0 -> x10, starting transfers between devices: none -> 39.6 us  [direct_features(): lax.ppermute(starts[turn], ('tensor', 'example', 'test'), pairs)]
    unnamed x57 -> x79, local copies, waits for them, and re-layouts: 5.95 us -> 45.2 us
    ppermute x17 -> x15, starting transfers between devices: 14.8 us -> 40.1 us  [shift(): return lax.ppermute(value, axis, [(i, (i + step) % n) for i in range(n)])]
    ppermute x0 -> x10, waiting for transfers between devices: none -> 15.3 us  [direct_features(): lax.ppermute(starts[turn], ('tensor', 'example', 'test'), pairs)]
  transfers between devices with their start and end apart: 22 -> 28, of which waited for: 13 -> 5; matrix products, arithmetic and copies ran while one was open for 19% -> 19% of each run, Pallas kernels for 0% -> 15%
where the time goes in v4:
time: 309 us; the launch traced here: 307 us
  starting transfers between devices  86.3 us (28%)
  local copies, waits for them, and re-layouts  52.3 us (17%)
  Pallas kernels  46.4 us (15%)
  waiting for transfers between devices  44.1 us (14%)
  other arithmetic  44 us (14%)
  between operations  14.7 us (5%)
  matrix products  10.8 us (3%)
  blocking collectives  8.43 us (3%)
    pallas_call x5, Pallas kernels, products(): pl.pallas_call(functools.partial(products_kernel, by_rows, len(pieces), l...  46.4 us
    unnamed x79, local copies, waits for them, and re-layouts  45.2 us
    ppermute x15, starting transfers between devices, shift(): return lax.ppermute(value, axis, [(i, (i + step) % n) for i in range(n)])  40.1 us
    ppermute x10, starting transfers between devices, direct_features(): lax.ppermute(starts[turn], ('tensor', 'example', 'test'), pairs)  39.6 us
    ppermute x15, waiting for transfers between devices, shift(): return lax.ppermute(value, axis, [(i, (i + step) % n) for i in range(n)])  21.6 us
    convert_element_type x13, other arithmetic, pack(): return (value * SEND_SCALE).astype(jnp.float16)  21.6 us
    ppermute x10, waiting for transfers between devices, direct_features(): lax.ppermute(starts[turn], ('tensor', 'example', 'test'), pairs)  15.3 us
    convert_element_type x9, other arithmetic, token(): corner[:16, :128].astype(F32)  9.68 us
  transfers between devices with their start and end apart: 28, of which 5 were waited for; matrix products, arithmetic and copies ran while one was open for 19% of the time, Pallas kernels for 15%

profile of v4, /device:TPU:0, one launch (start us, length us, event | category | flops | bytes accessed | tf_op | source)
XLA Modules:
  0.0 307.0 jit_solution(16195542631897495169)
XLA Ops:
  8.5 2.3 copy.66
  16.5 2.1 copy.52.refs_0_
  18.6 2.1 fusion.30
  21.6 1.7 pad_maximum_fusion.refs_0_
  23.5 12.3 %collective-permute-done.2.refs_0_ = bf16[128,1280]{1,0:T(8,128)(2,1)} collective-permute-done((bf16[128,1280]{1,0:T(8,128)(2,1)}, bf16[128,1280]{1,0:T(8,128)(2,1)}, u32[]{:S(2)}, u32[]{:S(2)}) %collective-permute-start.2) | collective-permute-done | bytes 327712 | tf_op jit(solution)/shard_map/ppermute | solution.py:64
  35.8 4.0 %copy-done.1 = bf16[1280,4096]{1,0:T(8,128)(2,1)S(1)} copy-done((bf16[1280,4096]{1,0:T(8,128)(2,1)S(1)}, bf16[1280,4096]{1,0:T(8,128)(2,1)}, u32[]{:S(2)}) %copy-start.1) | copy-done | bytes 10485784
  39.8 4.0 %copy-done.4 = bf16[1280,4096]{1,0:T(8,128)(2,1)S(1)} copy-done((bf16[1280,4096]{1,0:T(8,128)(2,1)S(1)}, bf16[1280,4096]{1,0:T(8,128)(2,1)}, u32[]{:S(2)}) %copy-start.4) | copy-done | bytes 10485784
  43.8 9.9 %shard_map.113 = (f32[128,2048]{1,0:T(8,128)S(1)}, f32[1,128,2048]{2,1,0:T(8,128)S(1)}, f32[128,2048]{1,0:T(8,128)S(1)}, f32[1,128,2048]{2,1,0:T(8,128)S(1)}) custom-call(s32[2]{0:T(128)S(1)} %pad_add_fusion.place_ref, bf16[128,1280]{1,0:T(8,128)(2,1)} %collective-permute-done.2.refs_0_, bf16[128,1280]{1,0:T(8,128)(2,1)} %collective-permute-done.3.refs_1_, ...), custom_call_target="tpu_custom_call" | custom-call | flops 1 | bytes 1 | tf_op jit(solution)/shard_map/pallas_call | solution.py:129
  57.5 4.0 %copy-done.5 = bf16[1280,4096]{1,0:T(8,128)(2,1)S(1)} copy-done((bf16[1280,4096]{1,0:T(8,128)(2,1)S(1)}, bf16[1280,4096]{1,0:T(8,128)(2,1)}, u32[]{:S(2)}) %copy-start.5) | copy-done | bytes 10485784
  61.5 9.5 %shard_map.114 = (f32[128,2048]{1,0:T(8,128)S(1)}, f32[1,128,2048]{2,1,0:T(8,128)S(1)}, f32[128,2048]{1,0:T(8,128)S(1)}, f32[1,128,2048]{2,1,0:T(8,128)S(1)}) custom-call(s32[2]{0:T(128)S(1)} %pad_add_fusion.place_ref, bf16[128,1280]{1,0:T(8,128)(2,1)} %collective-permute-done.refs_0_, bf16[128,1280]{1,0:T(8,128)(2,1)S(1)} %collective-permute-done.1.refs_1_, ...), custom_call_target="tpu_custom_call" | custom-call | flops 1 | bytes 1 | tf_op jit(solution)/shard_map/pallas_call | solution.py:129
  77.4 16.4 %collective-permute-start.5 = (bf16[256,1280]{1,0:T(8,128)(2,1)}, bf16[256,1280]{1,0:T(8,128)(2,1)}, u32[]{:S(2)}, u32[]{:S(2)}) collective-permute-start(bf16[256,1280]{1,0:T(8,128)(2,1)} %shard_map.115), channel_id=1, source_target_pairs={{0,8},{1,12},{4,9},{5,13},{10,2},{11,6},{14,3},{15,7},{16,24},{17,... | collective-permute-start | bytes 1966088 | tf_op jit(solution)/shard_map/ppermute | solution.py:64
  93.8 6.6 %collective-permute-start.4 = (bf16[256,1280]{1,0:T(8,128)(2,1)}, bf16[256,1280]{1,0:T(8,128)(2,1)}, u32[]{:S(2)}, u32[]{:S(2)}) collective-permute-start(bf16[256,1280]{1,0:T(8,128)(2,1)} %shard_map.115), channel_id=1, source_target_pairs={{0,0},{1,4},{4,1},{5,5},{10,10},{11,14},{14,11},{15,15},{16,16},{1... | collective-permute-start | bytes 1966088 | tf_op jit(solution)/shard_map/ppermute | solution.py:64
  100.4 1.4 collective-permute-start.7
  101.8 2.3 multiply_convert_fusion.12
  104.2 2.0 multiply_convert_fusion.15
  106.2 3.0 collective-permute-done.5.refs_0_
  109.2 19.4 %collective-permute-start.19 = (f16[128,2048]{1,0:T(8,128)(2,1)}, f16[128,2048]{1,0:T(8,128)(2,1)}, u32[]{:S(2)}, u32[]{:S(2)}) collective-permute-start(f16[128,2048]{1,0:T(8,128)(2,1)} %multiply_convert_fusion.12), channel_id=1, source_target_pairs={{0,2},{2,0},{1,3},{3,1},{4,6},{6,4},{5,7},{7,5},{8,10},{10,8},{9,1... | collective-permute-start | bytes 1572872 | tf_op jit(solution)/shard_map/ppermute | solution.py:17
  128.7 4.0 %copy-done.3 = bf16[1280,4096]{1,0:T(8,128)(2,1)S(1)} copy-done((bf16[1280,4096]{1,0:T(8,128)(2,1)S(1)}, bf16[1280,4096]{1,0:T(8,128)(2,1)}, u32[]{:S(2)}) %copy-start.3) | copy-done | bytes 10485784
  132.7 4.0 %copy-done.6 = bf16[1280,4096]{1,0:T(8,128)(2,1)S(1)} copy-done((bf16[1280,4096]{1,0:T(8,128)(2,1)S(1)}, bf16[1280,4096]{1,0:T(8,128)(2,1)}, u32[]{:S(2)}) %copy-start.6) | copy-done | bytes 10485784
  136.7 12.9 %shard_map.118 = (f32[256,2048]{1,0:T(8,128)S(1)}, f32[1,256,2048]{2,1,0:T(8,128)S(1)}, f32[256,2048]{1,0:T(8,128)S(1)}, f32[1,256,2048]{2,1,0:T(8,128)S(1)}) custom-call(s32[2]{0:T(128)S(1)} %pad_add_fusion.place_ref, bf16[256,1280]{1,0:T(8,128)(2,1)} %shard_map.116.refs_0_, bf16[256,1280]{1,0:T(8,128)(2,1)} %shard_map.117.refs_1_, ...), custom_call_target="tpu_custom_call" | custom-call | flops 1 | bytes 1 | tf_op jit(solution)/shard_map/pallas_call | solution.py:129
  155.1 2.3 collective-permute-start.9
  157.4 2.8 fusion.8
  160.2 2.8 fusion.9
  163.0 6.5 %collective-permute-start.6 = (bf16[256,1280]{1,0:T(8,128)(2,1)}, bf16[256,1280]{1,0:T(8,128)(2,1)}, u32[]{:S(2)}, u32[]{:S(2)}) collective-permute-start(bf16[256,1280]{1,0:T(8,128)(2,1)} %shard_map.119), channel_id=1, source_target_pairs={{0,0},{1,4},{4,1},{5,5},{10,10},{11,14},{14,11},{15,15},{16,16},{1... | collective-permute-start | bytes 1966088 | tf_op jit(solution)/shard_map/ppermute | solution.py:64
  170.8 1.5 collective-permute-start.8
  172.3 2.4 multiply_convert_fusion.14
  176.5 2.4 multiply_convert_fusion.8
  178.8 14.9 %collective-permute-start.14 = (f16[128,2048]{1,0:T(8,128)(2,1)}, f16[128,2048]{1,0:T(8,128)(2,1)}, u32[]{:S(2)}, u32[]{:S(2)}) collective-permute-start(f16[128,2048]{1,0:T(8,128)(2,1)} %multiply_convert_fusion.14), channel_id=1, source_target_pairs={{0,2},{2,0},{1,3},{3,1},{4,6},{6,4},{5,7},{7,5},{8,10},{10,8},{9,1... | collective-permute-start | bytes 1572872 | tf_op jit(solution)/shard_map/ppermute | solution.py:17
  193.7 4.0 %copy-done.7 = bf16[4096,1280]{1,0:T(8,128)(2,1)S(1)} copy-done((bf16[4096,1280]{1,0:T(8,128)(2,1)S(1)}, bf16[4096,1280]{1,0:T(8,128)(2,1)}, u32[]{:S(2)}) %copy-start.7) | copy-done | bytes 10485784
  197.7 7.0 %shard_map.124 = (f32[256,2048]{1,0:T(8,128)S(1)}, f32[1,256,2048]{2,1,0:T(8,128)S(1)}) custom-call(s32[2]{0:T(128)S(1)} %pad_add_fusion.place_ref, bf16[256,1280]{1,0:T(8,128)(2,1)} %shard_map.121.refs_0_, bf16[256,1280]{1,0:T(8,128)(2,1)} %shard_map.123.refs_1_, bf16[4096,1280]{1,0:T(8,128)(2,1)S(1)} %copy-done.7), custom_call_target="tpu_custom_call" | custom-call | flops 1 | bytes 1 | tf_op jit(solution)/shard_map/pallas_call | solution.py:129
  207.2 3.1 %fusion.48 = (f32[128,2048]{1,0:T(8,128)}, f32[128,2048]{1,0:T(8,128)}) fusion(f32[256,2048]{1,0:T(8,128)} %copy-done.18), kind=kLoop, calls=%fused_computation.113 | loop fusion | bytes 4194304 | tf_op jit(solution)/shard_map/slice | solution.py:243
  210.3 4.0 %copy-done.8 = bf16[4096,1280]{1,0:T(8,128)(2,1)S(1)} copy-done((bf16[4096,1280]{1,0:T(8,128)(2,1)S(1)}, bf16[4096,1280]{1,0:T(8,128)(2,1)}, u32[]{:S(2)}) %copy-start.8) | copy-done | bytes 10485784
  214.3 7.0 %shard_map.127 = (f32[256,2048]{1,0:T(8,128)S(1)}, f32[1,256,2048]{2,1,0:T(8,128)S(1)}) custom-call(s32[2]{0:T(128)S(1)} %pad_add_fusion.place_ref, bf16[256,1280]{1,0:T(8,128)(2,1)} %shard_map.125.refs_0_, bf16[256,1280]{1,0:T(8,128)(2,1)} %shard_map.126.refs_1_, bf16[4096,1280]{1,0:T(8,128)(2,1)S(1)} %copy-done.8, f32[16,128]{1,0:T(8,128)S(1)} %copy-done.24), custom_call_target="tpu_custom_call" | custom-call | flops 1 | bytes 1 | tf_op jit(solution)/shard_map/pallas_call | solution.py:129
  228.1 2.3 multiply_add_fusion
  230.6 1.6 multiply_add_fusion.1
  232.3 2.8 add_multiply_fusion
  235.1 1.4 convolution_bitcast_fusion.1
  236.5 1.6 convolution_bitcast_fusion.5
  238.2 1.8 multiply_convert_fusion.7
  240.0 2.0 collective-permute-start.23
  242.1 1.7 multiply_add_fusion.2
  243.8 21.6 %collective-permute-done.16 = f16[128,2048]{1,0:T(8,128)(2,1)S(1)} collective-permute-done((f16[128,2048]{1,0:T(8,128)(2,1)S(1)}, f16[128,2048]{1,0:T(8,128)(2,1)S(1)}, u32[]{:S(2)}, u32[]{:S(2)}) %collective-permute-start.16) | collective-permute-done | bytes 524320 | tf_op jit(solution)/shard_map/ppermute | solution.py:17
  268.3 8.4 %all_to_all.15 = f32[4,1,6144]{2,1,0:T(1,128)S(1)} all-to-all(f32[4,1,6144]{2,1,0:T(1,128)S(1)} %reshape.220), channel_id=1, replica_groups=mesh['parts'=2,'tensor'=4,'example'=2,'test'=2] {'tensor'}, dimensions={0} | all-to-all | bytes 196608 | tf_op jit(solution)/shard_map/all_to_all | solution.py:29
  279.1 3.3 %all-to-all-start.1 = ((f32[4,1,6144]{2,1,0:T(1,128)}), f32[4,1,6144]{2,1,0:T(1,128)S(1)}, u32[]{:S(2)}, u32[]{:S(2)}) async-start(f32[4,1,6144]{2,1,0:T(1,128)} %reshape.222), calls=%async_computation.1 | async-start | bytes 196608 | tf_op jit(solution)/shard_map/all_to_all | solution.py:29
  282.4 2.0 collective-permute-start.24
  284.4 2.3 all-to-all-done.1
  289.8 3.3 %all-to-all-start.2 = ((f32[4,4,512]{2,1,0:T(4,128)}), f32[4,4,512]{2,1,0:T(4,128)S(1)}, u32[]{:S(2)}, u32[]{:S(2)}) async-start(f32[4,4,512]{2,1,0:T(4,128)} %broadcast_in_dim.5), calls=%async_computation.2 | async-start | bytes 65536 | tf_op jit(solution)/shard_map/all_to_all | solution.py:29
  293.8 4.9 %all-to-all-done.2 = f32[4,4,512]{2,1,0:T(4,128)S(1)} async-done(((f32[4,4,512]{2,1,0:T(4,128)}), f32[4,4,512]{2,1,0:T(4,128)S(1)}, u32[]{:S(2)}, u32[]{:S(2)}) %all-to-all-start.2) | async-done | bytes 32800 | tf_op jit(solution)/shard_map/all_to_all | solution.py:29
  (174 shorter events, 46.9 us)
Async XLA Ops:
  7.2 280.7 %copy-start = (bf16[3,16,64,512]{3,2,1,0:T(8,128)(2,1)S(1)}, bf16[3,16,64,512]{3,2,1,0:T(8,128)(2,1)}, u32[]{:S(2)}) copy-start(bf16[3,16,64,512]{3,2,1,0:T(8,128)(2,1)} %param.17) | copy-start | bytes 9437188
  7.2 216.6 %all-reduce.2.cloned.1.call-start = ((), (), s32[]{:S(2)}) async-start(), calls=%async_computation.3 | async-start | bytes 524288 | tf_op jit(solution)/shard_map/psum | solution.py:226
  11.6 11.8 %copy-start.35 = (s32[2]{0:T(128)S(1)}, s32[2]{0:T(128)}, u32[]{:S(2)}) copy-start(s32[2]{0:T(128)} %param.18) | copy-start | bytes 28
  11.6 45.9 %collective-permute-start.1 = (bf16[128,1280]{1,0:T(8,128)(2,1)}, bf16[128,1280]{1,0:T(8,128)(2,1)S(1)}, u32[]{:S(2)}, u32[]{:S(2)}) collective-permute-start(bf16[128,1280]{1,0:T(8,128)(2,1)} %get-tuple-element.50), channel_id=1, source_target_pairs={{2,8},{3,12},{6,9},{7,13},{8,2},{9,6},{12,3},{13,7},{18,24},{19,28... | collective-permute-start | bytes 983048 | tf_op jit(solution)/shard_map/ppermute | solution.py:64
  12.5 45.1 %collective-permute-start = (bf16[128,1280]{1,0:T(8,128)(2,1)}, bf16[128,1280]{1,0:T(8,128)(2,1)}, u32[]{:S(2)}, u32[]{:S(2)}) collective-permute-start(bf16[128,1280]{1,0:T(8,128)(2,1)} %get-tuple-element.50), channel_id=1, source_target_pairs={{2,0},{3,4},{6,1},{7,5},{8,10},{9,14},{12,11},{13,15},{18,16},{19,... | collective-permute-start | bytes 983048 | tf_op jit(solution)/shard_map/ppermute | solution.py:64
  13.8 9.7 %collective-permute-start.3 = (bf16[128,1280]{1,0:T(8,128)(2,1)}, bf16[128,1280]{1,0:T(8,128)(2,1)}, u32[]{:S(2)}, u32[]{:S(2)}) collective-permute-start(bf16[128,1280]{1,0:T(8,128)(2,1)} %get-tuple-element.51), channel_id=1, source_target_pairs={{2,8},{3,12},{6,9},{7,13},{8,2},{9,6},{12,3},{13,7},{18,24},{19,28... | collective-permute-start | bytes 983048 | tf_op jit(solution)/shard_map/ppermute | solution.py:64
  15.1 20.7 %collective-permute-start.2 = (bf16[128,1280]{1,0:T(8,128)(2,1)}, bf16[128,1280]{1,0:T(8,128)(2,1)}, u32[]{:S(2)}, u32[]{:S(2)}) collective-permute-start(bf16[128,1280]{1,0:T(8,128)(2,1)} %get-tuple-element.51), channel_id=1, source_target_pairs={{2,0},{3,4},{6,1},{7,5},{8,10},{9,14},{12,11},{13,15},{18,16},{19,... | collective-permute-start | bytes 983048 | tf_op jit(solution)/shard_map/ppermute | solution.py:64
  16.5 4.2 %copy-start.28 = (bf16[2,128,1280]{2,1,0:T(8,128)(2,1)S(1)}, bf16[2,128,1280]{2,1,0:T(8,128)(2,1)}, u32[]{:S(2)}) copy-start(bf16[2,128,1280]{2,1,0:T(8,128)(2,1)} %copy-done.27) | copy-start | bytes 1966084
  16.5 4.2 %copy-start.33 = (bf16[1280,192]{0,1:T(8,128)(2,1)S(1)}, bf16[1280,192]{0,1:T(8,128)(2,1)}, u32[]{:S(2)}) copy-start(bf16[1280,192]{0,1:T(8,128)(2,1)} %param.15) | copy-start | bytes 1474564
  35.8 4.0 %copy-start.1 = (bf16[1280,4096]{1,0:T(8,128)(2,1)S(1)}, bf16[1280,4096]{1,0:T(8,128)(2,1)}, u32[]{:S(2)}) copy-start(bf16[1280,4096]{1,0:T(8,128)(2,1)} %refs_2_.7) | copy-start | bytes 31457284
  39.8 4.0 %copy-start.4 = (bf16[1280,4096]{1,0:T(8,128)(2,1)S(1)}, bf16[1280,4096]{1,0:T(8,128)(2,1)}, u32[]{:S(2)}) copy-start(bf16[1280,4096]{1,0:T(8,128)(2,1)} %refs_3_.5) | copy-start | bytes 31457284
  43.8 13.8 %copy-start.2 = (bf16[1280,4096]{1,0:T(8,128)(2,1)S(1)}, bf16[1280,4096]{1,0:T(8,128)(2,1)}, u32[]{:S(2)}) copy-start(bf16[1280,4096]{1,0:T(8,128)(2,1)} %refs_2_.7) | copy-start | bytes 31457284
  53.7 17.3 %copy-start.19 = (f32[128,2048]{1,0:T(8,128)}, f32[128,2048]{1,0:T(8,128)S(1)}, u32[]{:S(2)}) copy-start(f32[128,2048]{1,0:T(8,128)S(1)} %get-tuple-element.32) | copy-start | bytes 3145732
  53.7 17.3 %copy-start.21 = (f32[128,2048]{1,0:T(8,128)}, f32[128,2048]{1,0:T(8,128)S(1)}, u32[]{:S(2)}) copy-start(f32[128,2048]{1,0:T(8,128)S(1)} %get-tuple-element.35) | copy-start | bytes 3145732
  55.4 15.6 %copy-start.25 = (f32[16,128]{1,0:T(8,128)}, f32[16,128]{1,0:T(8,128)S(1)}, u32[]{:S(2)}) copy-start(f32[16,128]{1,0:T(8,128)S(1)} %slice_convert_fusion.8.refs_4_.refs_1_) | copy-start | bytes 24580
  55.4 48.8 %collective-permute-start.11 = (f16[128,2048]{1,0:T(8,128)(2,1)}, f16[128,2048]{1,0:T(8,128)(2,1)}, u32[]{:S(2)}, u32[]{:S(2)}) collective-permute-start(f16[128,2048]{1,0:T(8,128)(2,1)} %fusion.12), channel_id=1, source_target_pairs={{0,1},{1,0},{2,3},{3,2},{4,5},{5,4},{6,7},{7,6},{8,9},{9,8},{10,11... | collective-permute-start | bytes 1572872 | tf_op jit(solution)/shard_map/ppermute | solution.py:17
  56.3 44.1 %collective-permute-start.18 = (f16[128,2048]{1,0:T(8,128)(2,1)}, f16[128,2048]{1,0:T(8,128)(2,1)}, u32[]{:S(2)}, u32[]{:S(2)}) collective-permute-start(f16[128,2048]{1,0:T(8,128)(2,1)} %fusion.13), channel_id=1, source_target_pairs={{0,1},{1,0},{2,3},{3,2},{4,5},{5,4},{6,7},{7,6},{8,9},{9,8},{10,11... | collective-permute-start | bytes 1572872 | tf_op jit(solution)/shard_map/ppermute | solution.py:17
  57.5 13.5 %copy-start.26 = (f32[16,128]{1,0:T(8,128)}, f32[16,128]{1,0:T(8,128)S(1)}, u32[]{:S(2)}) copy-start(f32[16,128]{1,0:T(8,128)S(1)} %slice_convert_fusion.7.refs_5_.refs_1_) | copy-start | bytes 24580
  57.5 4.0 %copy-start.5 = (bf16[1280,4096]{1,0:T(8,128)(2,1)S(1)}, bf16[1280,4096]{1,0:T(8,128)(2,1)}, u32[]{:S(2)}) copy-start(bf16[1280,4096]{1,0:T(8,128)(2,1)} %refs_3_.5) | copy-start | bytes 31457284
  77.4 93.4 %collective-permute-start.13 = (f16[128,2048]{1,0:T(8,128)(2,1)}, f16[128,2048]{1,0:T(8,128)(2,1)}, u32[]{:S(2)}, u32[]{:S(2)}) collective-permute-start(f16[128,2048]{1,0:T(8,128)(2,1)} %fusion.15), channel_id=1, source_target_pairs={{0,1},{1,0},{2,3},{3,2},{4,5},{5,4},{6,7},{7,6},{8,9},{9,8},{10,11... | collective-permute-start | bytes 1572872 | tf_op jit(solution)/shard_map/ppermute | solution.py:17
  77.4 31.9 %collective-permute-start.5 = (bf16[256,1280]{1,0:T(8,128)(2,1)}, bf16[256,1280]{1,0:T(8,128)(2,1)}, u32[]{:S(2)}, u32[]{:S(2)}) collective-permute-start(bf16[256,1280]{1,0:T(8,128)(2,1)} %shard_map.115), channel_id=1, source_target_pairs={{0,8},{1,12},{4,9},{5,13},{10,2},{11,6},{14,3},{15,7},{16,24},{17,... | collective-permute-start | bytes 1966088 | tf_op jit(solution)/shard_map/ppermute | solution.py:64
  93.8 34.8 %collective-permute-start.4 = (bf16[256,1280]{1,0:T(8,128)(2,1)}, bf16[256,1280]{1,0:T(8,128)(2,1)}, u32[]{:S(2)}, u32[]{:S(2)}) collective-permute-start(bf16[256,1280]{1,0:T(8,128)(2,1)} %shard_map.115), channel_id=1, source_target_pairs={{0,0},{1,4},{4,1},{5,5},{10,10},{11,14},{14,11},{15,15},{16,16},{1... | collective-permute-start | bytes 1966088 | tf_op jit(solution)/shard_map/ppermute | solution.py:64
  100.4 28.3 %collective-permute-start.7 = (bf16[256,1280]{1,0:T(8,128)(2,1)}, bf16[256,1280]{1,0:T(8,128)(2,1)}, u32[]{:S(2)}, u32[]{:S(2)}) collective-permute-start(bf16[256,1280]{1,0:T(8,128)(2,1)} %shard_map.120.refs_0_), channel_id=1, source_target_pairs={{2,0},{3,4},{6,1},{7,5},{8,10},{9,14},{12,11},{13,15},{18,16},{19,... | collective-permute-start | bytes 1966088 | tf_op jit(solution)/shard_map/ppermute | solution.py:64
  104.2 71.8 %collective-permute-start.21 = (f16[128,2048]{1,0:T(8,128)(2,1)}, f16[128,2048]{1,0:T(8,128)(2,1)}, u32[]{:S(2)}, u32[]{:S(2)}) collective-permute-start(f16[128,2048]{1,0:T(8,128)(2,1)} %fusion.14), channel_id=1, source_target_pairs={{0,1},{1,0},{2,3},{3,2},{4,5},{5,4},{6,7},{7,6},{8,9},{9,8},{10,11... | collective-permute-start | bytes 1572872 | tf_op jit(solution)/shard_map/ppermute | solution.py:17
  106.2 22.5 %copy-start.22 = (f32[16,128]{1,0:T(8,128)S(1)}, f32[16,128]{1,0:T(8,128)}, u32[]{:S(2)}) copy-start(f32[16,128]{1,0:T(8,128)} %slice_convert_fusion.6.refs_1_.refs_2_.refs_5_) | copy-start | bytes 24580
  106.2 22.5 %copy-start.23 = (f32[16,128]{1,0:T(8,128)S(1)}, f32[16,128]{1,0:T(8,128)}, u32[]{:S(2)}) copy-start(f32[16,128]{1,0:T(8,128)} %slice_convert_fusion.5.refs_1_.refs_4_) | copy-start | bytes 24580
  109.2 65.5 %collective-permute-start.19 = (f16[128,2048]{1,0:T(8,128)(2,1)}, f16[128,2048]{1,0:T(8,128)(2,1)}, u32[]{:S(2)}, u32[]{:S(2)}) collective-permute-start(f16[128,2048]{1,0:T(8,128)(2,1)} %multiply_convert_fusion.12), channel_id=1, source_target_pairs={{0,2},{2,0},{1,3},{3,1},{4,6},{6,4},{5,7},{7,5},{8,10},{10,8},{9,1... | collective-permute-start | bytes 1572872 | tf_op jit(solution)/shard_map/ppermute | solution.py:17
  128.6 34.4 %collective-permute-start.12 = (f16[128,2048]{1,0:T(8,128)(2,1)}, f16[128,2048]{1,0:T(8,128)(2,1)}, u32[]{:S(2)}, u32[]{:S(2)}) collective-permute-start(f16[128,2048]{1,0:T(8,128)(2,1)} %multiply_convert_fusion.15), channel_id=1, source_target_pairs={{0,2},{2,0},{1,3},{3,1},{4,6},{6,4},{5,7},{7,5},{8,10},{10,8},{9,1... | collective-permute-start | bytes 1572872 | tf_op jit(solution)/shard_map/ppermute | solution.py:17
  128.7 4.0 %copy-start.3 = (bf16[1280,4096]{1,0:T(8,128)(2,1)S(1)}, bf16[1280,4096]{1,0:T(8,128)(2,1)}, u32[]{:S(2)}) copy-start(bf16[1280,4096]{1,0:T(8,128)(2,1)} %refs_2_.7) | copy-start | bytes 31457284
  132.7 4.0 %copy-start.6 = (bf16[1280,4096]{1,0:T(8,128)(2,1)S(1)}, bf16[1280,4096]{1,0:T(8,128)(2,1)}, u32[]{:S(2)}) copy-start(bf16[1280,4096]{1,0:T(8,128)(2,1)} %refs_3_.5) | copy-start | bytes 31457284
  155.1 52.0 %collective-permute-start.9 = (bf16[256,1280]{1,0:T(8,128)(2,1)}, bf16[256,1280]{1,0:T(8,128)(2,1)}, u32[]{:S(2)}, u32[]{:S(2)}) collective-permute-start(bf16[256,1280]{1,0:T(8,128)(2,1)} %shard_map.119), channel_id=1, source_target_pairs={{0,8},{1,12},{4,9},{5,13},{10,2},{11,6},{14,3},{15,7},{16,24},{17,... | collective-permute-start | bytes 1966088 | tf_op jit(solution)/shard_map/ppermute | solution.py:64
  163.0 44.1 %collective-permute-start.6 = (bf16[256,1280]{1,0:T(8,128)(2,1)}, bf16[256,1280]{1,0:T(8,128)(2,1)}, u32[]{:S(2)}, u32[]{:S(2)}) collective-permute-start(bf16[256,1280]{1,0:T(8,128)(2,1)} %shard_map.119), channel_id=1, source_target_pairs={{0,0},{1,4},{4,1},{5,5},{10,10},{11,14},{14,11},{15,15},{16,16},{1... | collective-permute-start | bytes 1966088 | tf_op jit(solution)/shard_map/ppermute | solution.py:64
  170.8 8.0 %collective-permute-start.8 = (bf16[256,1280]{1,0:T(8,128)(2,1)}, bf16[256,1280]{1,0:T(8,128)(2,1)}, u32[]{:S(2)}, u32[]{:S(2)}) collective-permute-start(bf16[256,1280]{1,0:T(8,128)(2,1)} %shard_map.122), channel_id=1, source_target_pairs={{2,8},{3,12},{6,9},{7,13},{8,2},{9,6},{12,3},{13,7},{18,24},{19,28... | collective-permute-start | bytes 1966088 | tf_op jit(solution)/shard_map/ppermute | solution.py:64
  174.7 53.4 %collective-permute-start.20 = (f16[256,2048]{1,0:T(8,128)(2,1)}, f16[256,2048]{1,0:T(8,128)(2,1)}, u32[]{:S(2)}, u32[]{:S(2)}) collective-permute-start(f16[256,2048]{1,0:T(8,128)(2,1)} %fusion.9), channel_id=1, source_target_pairs={{0,1},{1,0},{2,3},{3,2},{4,5},{5,4},{6,7},{7,6},{8,9},{9,8},{10,11... | collective-permute-start | bytes 3145736 | tf_op jit(solution)/shard_map/ppermute | solution.py:17
  176.0 54.5 %collective-permute-start.17 = (f16[256,2048]{1,0:T(8,128)(2,1)}, f16[256,2048]{1,0:T(8,128)(2,1)}, u32[]{:S(2)}, u32[]{:S(2)}) collective-permute-start(f16[256,2048]{1,0:T(8,128)(2,1)} %fusion.8), channel_id=1, source_target_pairs={{0,1},{1,0},{2,3},{3,2},{4,5},{5,4},{6,7},{7,6},{8,9},{9,8},{10,11... | collective-permute-start | bytes 3145736 | tf_op jit(solution)/shard_map/ppermute | solution.py:17
  178.8 48.0 %collective-permute-start.14 = (f16[128,2048]{1,0:T(8,128)(2,1)}, f16[128,2048]{1,0:T(8,128)(2,1)}, u32[]{:S(2)}, u32[]{:S(2)}) collective-permute-start(f16[128,2048]{1,0:T(8,128)(2,1)} %multiply_convert_fusion.14), channel_id=1, source_target_pairs={{0,2},{2,0},{1,3},{3,1},{4,6},{6,4},{5,7},{7,5},{8,10},{10,8},{9,1... | collective-permute-start | bytes 1572872 | tf_op jit(solution)/shard_map/ppermute | solution.py:17
  193.7 4.0 %copy-start.7 = (bf16[4096,1280]{1,0:T(8,128)(2,1)S(1)}, bf16[4096,1280]{1,0:T(8,128)(2,1)}, u32[]{:S(2)}) copy-start(bf16[4096,1280]{1,0:T(8,128)(2,1)} %refs_2_.9) | copy-start | bytes 31457284
  207.1 17.9 %collective-permute-start.22 = (f16[128,2048]{1,0:T(8,128)(2,1)}, f16[128,2048]{1,0:T(8,128)(2,1)}, u32[]{:S(2)}, u32[]{:S(2)}) collective-permute-start(f16[128,2048]{1,0:T(8,128)(2,1)} %multiply_convert_fusion.8), channel_id=1, source_target_pairs={{0,2},{2,0},{1,3},{3,1},{4,6},{6,4},{5,7},{7,5},{8,10},{10,8},{9,1... | collective-permute-start | bytes 1572872 | tf_op jit(solution)/shard_map/ppermute | solution.py:17
  207.1 31.0 %collective-permute-start.15 = (f16[256,2048]{1,0:T(8,128)(2,1)}, f16[256,2048]{1,0:T(8,128)(2,1)}, u32[]{:S(2)}, u32[]{:S(2)}) collective-permute-start(f16[256,2048]{1,0:T(8,128)(2,1)} %copy-done.32), channel_id=1, source_target_pairs={{0,1},{1,0},{2,3},{3,2},{4,5},{5,4},{6,7},{7,6},{8,9},{9,8},{10,11... | collective-permute-start | bytes 3145736 | tf_op jit(solution)/shard_map/ppermute | solution.py:17
  210.3 4.0 %copy-start.8 = (bf16[4096,1280]{1,0:T(8,128)(2,1)S(1)}, bf16[4096,1280]{1,0:T(8,128)(2,1)}, u32[]{:S(2)}) copy-start(bf16[4096,1280]{1,0:T(8,128)(2,1)} %refs_2_.9) | copy-start | bytes 31457284
  225.0 17.1 %collective-permute-start.10 = (f16[256,2048]{1,0:T(8,128)(2,1)}, f16[256,2048]{1,0:T(8,128)(2,1)}, u32[]{:S(2)}, u32[]{:S(2)}) collective-permute-start(f16[256,2048]{1,0:T(8,128)(2,1)} %fusion.7), channel_id=1, source_target_pairs={{0,1},{1,0},{2,3},{3,2},{4,5},{5,4},{6,7},{7,6},{8,9},{9,8},{10,11... | collective-permute-start | bytes 3145736 | tf_op jit(solution)/shard_map/ppermute | solution.py:17
  238.1 4.0 %copy-start.11 = (f32[256,2048]{1,0:T(8,128)S(1)}, f32[256,2048]{1,0:T(8,128)}, u32[]{:S(2)}) copy-start(f32[256,2048]{1,0:T(8,128)} %copy-done.10) | copy-start | bytes 6291460
  240.0 26.7 %collective-permute-start.23 = (f16[128,2048]{1,0:T(8,128)(2,1)S(1)}, f16[128,2048]{1,0:T(8,128)(2,1)S(1)}, u32[]{:S(2)}, u32[]{:S(2)}) collective-permute-start(f16[128,2048]{1,0:T(8,128)(2,1)S(1)} %get-tuple-element.48), channel_id=1, source_target_pairs={{0,2},{2,0},{1,3},{3,1},{4,6},{6,4},{5,7},{7,5},{8,10},{10,8},{9,1... | collective-permute-start | bytes 1572872 | tf_op jit(solution)/shard_map/ppermute | solution.py:17
  242.0 23.3 %collective-permute-start.16 = (f16[128,2048]{1,0:T(8,128)(2,1)S(1)}, f16[128,2048]{1,0:T(8,128)(2,1)S(1)}, u32[]{:S(2)}, u32[]{:S(2)}) collective-permute-start(f16[128,2048]{1,0:T(8,128)(2,1)S(1)} %get-tuple-element.49), channel_id=1, source_target_pairs={{0,2},{2,0},{1,3},{3,1},{4,6},{6,4},{5,7},{7,5},{8,10},{10,8},{9,1... | collective-permute-start | bytes 1572872 | tf_op jit(solution)/shard_map/ppermute | solution.py:17
  267.3 15.1 %copy-start.34 = (s32[2]{0:T(128)S(1)}, s32[2]{0:T(128)}, u32[]{:S(2)}) copy-start(s32[2]{0:T(128)} %param.19) | copy-start | bytes 28
  279.1 7.6 %all-to-all-start.1 = ((f32[4,1,6144]{2,1,0:T(1,128)}), f32[4,1,6144]{2,1,0:T(1,128)S(1)}, u32[]{:S(2)}, u32[]{:S(2)}) async-start(f32[4,1,6144]{2,1,0:T(1,128)} %reshape.222), calls=%async_computation.1 | async-start | bytes 196608 | tf_op jit(solution)/shard_map/all_to_all | solution.py:29
  282.4 10.7 %collective-permute-start.24 = (s32[2]{0:T(128)S(1)}, s32[2]{0:T(128)S(1)}, u32[]{:S(2)}, u32[]{:S(2)}) collective-permute-start(s32[2]{0:T(128)S(1)} %copy-done.34), channel_id=1, source_target_pairs={{0,2},{2,0},{1,3},{3,1},{4,6},{6,4},{5,7},{7,5},{8,10},{10,8},{9,1... | collective-permute-start | bytes 32 | tf_op jit(solution)/shard_map/ppermute | solution.py:17
  289.8 8.9 %all-to-all-start.2 = ((f32[4,4,512]{2,1,0:T(4,128)}), f32[4,4,512]{2,1,0:T(4,128)S(1)}, u32[]{:S(2)}, u32[]{:S(2)}) async-start(f32[4,4,512]{2,1,0:T(4,128)} %broadcast_in_dim.5), calls=%async_computation.2 | async-start | bytes 65536 | tf_op jit(solution)/shard_map/all_to_all | solution.py:29
  (16 other events, 29.8 us)
Sparse Core Ops, SparseCore 0:
  100.5 38.3 all-reduce.1

commit v5 on v4

--- a/solution.py
+++ b/solution.py
@@ -25,12 +25,29 @@
     return value.astype(F32) * (1.0 / SEND_SCALE)
 
 
-def exchange(blocks, axis):
-    return lax.all_to_all(blocks, axis, split_axis=0, concat_axis=0, tiled=True)
-
-
-def share(value, axis, n):
-    return exchange(jnp.broadcast_to(value[None], (n,) + value.shape), axis)
+def in_order(pieces, axis):
+    n = len(pieces)
+    back = pieces[:0:-1] + pieces[:1]
+    return lax.dynamic_slice_in_dim(jnp.stack(back + back), n - 1 - lax.axis_index(axis), n, 0)
+
+
+def gather_in_order(value, axis):
+    n = lax.axis_size(axis)
+    if n > 8:
+        return lax.all_gather(value, axis, axis=0)
+    return in_order([value] + [shift(value, axis, step) for step in range(1, n)], axis)
+
+
+def scatter_sum(blocks, axis):
+    n = lax.axis_size(axis)
+    if n > 8:
+        return lax.psum_scatter(blocks, axis, scatter_dimension=0, tiled=True)[0]
+    me = lax.axis_index(axis)
+    total = lax.dynamic_index_in_dim(blocks, me, 0, keepdims=False)
+    for step in range(1, n):
+        block = lax.dynamic_index_in_dim(blocks, lax.rem(me + step, n), 0, keepdims=False)
+        total = total + shift(block, axis, step)
+    return total
 
 
 def token(value):
@@ -51,7 +68,7 @@
     )(value, *earlier)
 
 
-def direct_features(starts, ex_step):
+def spread_features(starts, far, cross):
     pieces = []
     for turn in range(2):
         pairs = []
@@ -59,10 +76,16 @@
             example, core = block // 2, block % 2
             for source_core in range(2):
                 target = block ^ (2 * turn + (source_core ^ core))
-                source = block * 4 + (example ^ ex_step) * 2 + source_core
-                pairs.append((source, target * 4 + example * 2 + core))
+                source = block * 4 + (example ^ far) * 2 + source_core
+                landing = example if cross else example ^ far
+                pairs.append((source, target * 4 + landing * 2 + core))
         pieces.append(lax.ppermute(starts[turn], ("tensor", "example", "test"), pairs))
     return pieces
+
+
+def piece_index(across):
+    example = lax.axis_index("example") ^ across
+    return (lax.axis_index("tensor") ^ (example * 2 + lax.axis_index("test"))) // 2
 
 
 def gathered_features(flat, n_ex, n_cores):
@@ -117,8 +140,7 @@
         return (block, 0) if by_rows else (0, block)
 
     core = lax.axis_index("test")
-    holder = lax.axis_index("example") * n_cores + core
-    piece = (lax.axis_index("tensor") ^ holder) // 2 if len(pieces) == 2 else 0 * core
+    piece = piece_index(0) if len(pieces) == 2 else 0 * core
 
     def kept_block(turn, i, place_ref):
         return (0, jnp.where(turn == n_cores - 1, i, 0))
@@ -147,7 +169,7 @@
             * len(weights),
             scratch_shapes=[pltpu.VMEM((rows, depth), jnp.bfloat16)],
         ),
-        compiler_params=pltpu.CompilerParams(vmem_limit_bytes=24 * 2**20),
+        compiler_params=pltpu.CompilerParams(vmem_limit_bytes=48 * 2**20),
         cost_estimate=pl.CostEstimate(flops=1, bytes_accessed=1, transcendentals=0),
     )(jnp.stack([core, piece]), *pieces, *weights, *earlier)
     return list(zip(outs[::2], outs[1::2]))
@@ -208,46 +230,49 @@
     direct = (n_z, n_ex, n_cores) == (4, 2, 2)
     examples = [slice(e * seq_len, (e + 1) * seq_len) for e in range(ex_loc)]
     if direct:
-        acts_far = [[direct_features([activations[e]] * 2, 1) for e in range(ex_loc)]]
+        starts = [activations[0]] + [after(one, model_part) for one in activations[1:]]
+        acts_far = [[spread_features([start, start], 1, True) for start in starts]]
     else:
         acts_here = gathered_features(flat_acts, n_ex, n_cores)
         grad_here = gathered_features(flat_grad, n_ex, n_cores)
         acts_far = [[[block[rows]] for rows in examples] for block in acts_here[1:]]
-    earlier = []
-    marks = []
+    earlier, marks = [], []
     for e in range(ex_loc):
         for step in range(1, n_ex):
-            far = products(acts_far[step - 1][e], (w_gate, w_up), False, n_cores, *earlier)
-            swapped = [core_swap(one) for one in far]
-            earlier = [packed[-1] for _, packed, _ in swapped]
-            marks.append(earlier)
-            for which, (kept, _, got) in enumerate(swapped):
-                sent = send(which, e, step, kept, got)
+            sent = []
+            for which, weight in enumerate((w_gate, w_up)):
+                pieces = acts_far[step - 1][e]
+                (far,) = products(pieces, (weight,), False, n_cores, *earlier)
+                kept, packed, got = core_swap(far)
+                sent.append(send(which, e, step, kept, got))
+                earlier = earlier[-1:] + [packed[-1]]
+            earlier = [earlier[-1]] + sent[:1]
+            marks.append(sent)
     model_sum = lax.psum(after(model_part, marks[0][0]), "tensor")
     if direct:
         start = after(flat_grad, marks[0][1])
-        later = after(start, marks[-1][0])
-        grad_far = [direct_features([start, later], 1)]
-        start = after(flat_acts, marks[-1][1])
-        acts_near = direct_features([start, start], 0)
-        acts_near = [after(piece, *marks[-1]) for piece in acts_near]
+        pieces = spread_features([start, start], 1, False)
+        pieces = [after(piece, marks[-1][0]) for piece in pieces]
+        grad_far = [[shift(jnp.where(piece_index(1) == 0, *pieces), "example", 1)]]
+        start = after(flat_acts, marks[-1][0])
+        acts_near = spread_features([start, start], 0, False)
     else:
         grad_far = [[block] for block in grad_here[1:]]
         acts_near = acts_here[:1]
-    acts_near = products(acts_near, (w_gate, w_up), False, n_cores, *marks[-1])
-    grad_far = [[after(piece, acts_near[0][0]) for piece in pieces] for pieces in grad_far]
     for step in range(1, n_ex):
-        (far,) = products(grad_far[step - 1], (w_down,), True, n_cores)
+        (far,) = products(grad_far[step - 1], (w_down,), True, n_cores, *marks[-1])
         kept, packed, got = core_swap(far)
         for e, rows in enumerate(examples):
             sent = send(2, e, step, kept[rows], [one[rows] for one in got])
     if direct:
+        acts_near = [after(piece, packed[-1]) for piece in acts_near]
+    acts_near = products(acts_near, (w_gate, w_up), False, n_cores)
+    if direct:
         start = after(flat_grad, acts_near[0][0])
-        grad_near = direct_features([start, start], 0)
-        grad_near = [after(piece, packed[-1]) for piece in grad_near]
+        grad_near = spread_features([start, start], 0, False)
     else:
         grad_near = grad_here[:1]
-    (grad_near,) = products(grad_near, (w_down,), True, n_cores, packed[-1])
+    (grad_near,) = products(grad_near, (w_down,), True, n_cores, sent)
     model_sum = after(model_sum, grad_near[0])
     own = []
     for near in (*acts_near, grad_near):
@@ -291,20 +316,31 @@
             outer(out_up, masked[e, :, width : 2 * width]),
             hidden_grads[e],
         ]
-    grads = jnp.sum(exchange(jnp.stack(grads, 1), "tensor"), 0)
-    grads = share(grads, ("example", "test"), n_ex * n_cores)
-    grads = jnp.sum(grads.reshape((n_ex, n_cores) + grads.shape[1:]), 1)
+    grads = scatter_sum(jnp.stack(grads, 1), "tensor")
+    by_example = []
+    for ex_step in range(n_ex):
+        total = 0.0
+        for core_step in range(n_cores):
+            piece = grads
+            if ex_step or core_step:
+                pairs = [
+                    (i * n_cores + c, (i + ex_step) % n_ex * n_cores + (c + core_step) % n_cores)
+                    for i in range(n_ex)
+                    for c in range(n_cores)
+                ]
+                piece = lax.ppermute(piece, ("example", "test"), pairs)
+            total = total + piece
+        by_example.append(total)
+    grads = in_order(by_example, "example")
     partial_scores = lax.dot_general(
         grads.reshape(n_ex * ex_loc, -1),
         test_grads.astype(F32).reshape(-1, test_grads.shape[-1]),
         (((1,), (0,)), ((), ())),
         precision=lax.Precision.HIGHEST,
     )
-    all_scores = jnp.sum(share(partial_scores, "tensor", n_z), 0)
+    all_scores = jnp.sum(gather_in_order(partial_scores, "tensor"), 0)
     scores = lax.dynamic_slice_in_dim(all_scores, ex_index * ex_loc, ex_loc, 0)
-    all_groups = [groups] + [shift(groups, "example", step) for step in range(1, n_ex)]
-    owners = jnp.stack([lax.rem(ex_index + n_ex - step, n_ex) for step in range(n_ex)])
-    all_groups = jnp.zeros((n_ex, ex_loc), jnp.int32).at[owners].set(jnp.stack(all_groups))
+    all_groups = gather_in_order(groups, "example")
     group_onehot = (
         all_groups.reshape(-1)[:, None] == jnp.arange(NGROUP, dtype=jnp.int32)[None, :]
     ).astype(F32)

time: 309 us -> 271 us (0.88)
  local copies, waits for them, and re-layouts: 52.3 us -> 17.9 us
  Pallas kernels: 46.4 us -> 68 us
  starting transfers between devices: 86.3 us -> 77 us
  blocking collectives: 8.43 us -> 0 us
  waiting for transfers between devices: 44.1 us -> 37.1 us
  other arithmetic: 44 us -> 39.8 us
    unnamed x79 -> x68, local copies, waits for them, and re-layouts: 45.2 us -> 13.6 us
    pallas_call x5 -> x7, Pallas kernels: 46.4 us -> 68 us  [products(): pl.pallas_call(functools.partial(products_kernel, by_rows, len(pieces), l...]
    all_to_all x1 -> x0, blocking collectives: 8.43 us -> none  [exchange(): return lax.all_to_all(blocks, axis, split_axis=0, concat_axis=0, tiled=True)]
    all_to_all x2 -> x0, waiting for transfers between devices: 7.14 us -> none  [exchange(): return lax.all_to_all(blocks, axis, split_axis=0, concat_axis=0, tiled=True)]
    all_to_all x2 -> x0, starting transfers between devices: 6.56 us -> none  [exchange(): return lax.all_to_all(blocks, axis, split_axis=0, concat_axis=0, tiled=True)]
    ppermute x10 -> x13, starting transfers between devices: 39.6 us -> 34.8 us  [the longest x10 30.2 us: spread_features(): lax.ppermute(starts[turn], ('tensor', 'example', 'test'), pairs)]
    convert_element_type x13, other arithmetic: 21.6 us -> 16.9 us  [pack(): return (value * SEND_SCALE).astype(jnp.float16)]
    ppermute x15 -> x22, waiting for transfers between devices: 21.6 us -> 24.1 us  [shift(): return lax.ppermute(value, axis, [(i, (i + step) % n) for i in range(n)])]
  transfers between devices with their start and end apart: 28 -> 36, of which waited for: 5 -> 10; matrix products, arithmetic and copies ran while one was open for 19% -> 20% of each run, Pallas kernels for 15% -> 25%
where the time goes in v5:
time: 271 us; the launch traced here: 268 us
  starting transfers between devices  77 us (28%)
  Pallas kernels  68 us (25%)
  other arithmetic  39.8 us (15%)
  waiting for transfers between devices  37.1 us (14%)
  local copies, waits for them, and re-layouts  17.9 us (7%)
  between operations  14.8 us (5%)
  matrix products  13.8 us (5%)
    pallas_call x7, Pallas kernels, products(): pl.pallas_call(functools.partial(products_kernel, by_rows, len(pieces), l...  68 us
    ppermute x22, starting transfers between devices, shift(): return lax.ppermute(value, axis, [(i, (i + step) % n) for i in range(n)])  42.2 us
    ppermute x10, starting transfers between devices, spread_features(): lax.ppermute(starts[turn], ('tensor', 'example', 'test'), pairs)  30.2 us
    ppermute x22, waiting for transfers between devices, shift(): return lax.ppermute(value, axis, [(i, (i + step) % n) for i in range(n)])  24.1 us
    convert_element_type x13, other arithmetic, pack(): return (value * SEND_SCALE).astype(jnp.float16)  16.9 us
    unnamed x68, local copies, waits for them, and re-layouts  13.6 us
    convert_element_type x13, other arithmetic, token(): corner[:16, :128].astype(F32)  10.4 us
    ppermute x10, waiting for transfers between devices, spread_features(): lax.ppermute(starts[turn], ('tensor', 'example', 'test'), pairs)  8.91 us
  transfers between devices with their start and end apart: 36, of which 10 were waited for; matrix products, arithmetic and copies ran while one was open for 20% of the time, Pallas kernels for 25%

profile of v5, /device:TPU:0, one launch (start us, length us, event | category | flops | bytes accessed | tf_op | source)
XLA Modules:
  0.0 268.5 jit_solution(12049926809834472956)
XLA Ops:
  8.5 1.3 copy.61
  10.8 1.4 collective-permute-start.3
  16.8 2.0 copy.42.refs_0_
  18.9 8.9 %collective-permute-done.2.refs_0_ = bf16[128,1280]{1,0:T(8,128)(2,1)} collective-permute-done((bf16[128,1280]{1,0:T(8,128)(2,1)}, bf16[128,1280]{1,0:T(8,128)(2,1)}, u32[]{:S(2)}, u32[]{:S(2)}) %collective-permute-start.2) | collective-permute-done | bytes 327712 | tf_op jit(solution)/shard_map/ppermute | solution.py:82
  27.8 8.4 %shard_map.114 = (f32[128,2048]{1,0:T(8,128)S(1)}, f32[1,128,2048]{2,1,0:T(8,128)S(1)}) custom-call(s32[2]{0:T(128)S(1)} %pad_add_fusion.1.place_ref, bf16[128,1280]{1,0:T(8,128)(2,1)} %collective-permute-done.2.refs_0_, bf16[128,1280]{1,0:T(8,128)(2,1)} %collective-permute-done.3.refs_1_, bf16[1280,4096]{1,0:T(8,128)(2,1)} %refs_2_.10), custom_call_target="tpu_custom_call" | custom-call | flops 1 | bytes 1 | tf_op jit(solution)/shard_map/pallas_call | solution.py:151
  36.3 8.4 %shard_map.115 = (f32[128,2048]{1,0:T(8,128)S(1)}, f32[1,128,2048]{2,1,0:T(8,128)S(1)}) custom-call(s32[2]{0:T(128)S(1)} %pad_add_fusion.1.place_ref, bf16[128,1280]{1,0:T(8,128)(2,1)} %collective-permute-done.2.refs_0_, bf16[128,1280]{1,0:T(8,128)(2,1)} %collective-permute-done.3.refs_1_, bf16[1280,4096]{1,0:T(8,128)(2,1)} %refs_3_.1, ...), custom_call_target="tpu_custom_call" | custom-call | flops 1 | bytes 1 | tf_op jit(solution)/shard_map/pallas_call | solution.py:151
  47.8 14.5 %collective-permute-start.12 = (f16[128,2048]{1,0:T(8,128)(2,1)}, f16[128,2048]{1,0:T(8,128)(2,1)}, u32[]{:S(2)}, u32[]{:S(2)}) collective-permute-start(f16[128,2048]{1,0:T(8,128)(2,1)} %multiply_convert_fusion.14), channel_id=1, source_target_pairs={{0,2},{2,0},{1,3},{3,1},{4,6},{6,4},{5,7},{7,5},{8,10},{10,8},{9,1... | collective-permute-start | bytes 1572872 | tf_op jit(solution)/shard_map/ppermute | solution.py:17
  62.3 1.3 slice_convert_fusion.7.refs_1_
  66.6 1.5 collective-permute-start.9
  68.1 8.3 %shard_map.116 = (f32[128,2048]{1,0:T(8,128)S(1)}, f32[1,128,2048]{2,1,0:T(8,128)S(1)}) custom-call(s32[2]{0:T(128)S(1)} %pad_add_fusion.1.place_ref, bf16[128,1280]{1,0:T(8,128)(2,1)} %collective-permute-done.refs_0_, bf16[128,1280]{1,0:T(8,128)(2,1)S(1)} %collective-permute-done.1.refs_1_, bf16[1280,4096]{1,0:T(8,128)(2,1)} %refs_2_.10, ...), custom_call_target="tpu_custom_call" | custom-call | flops 1 | bytes 1 | tf_op jit(solution)/shard_map/pallas_call | solution.py:151
  78.4 8.3 %shard_map.122 = (f32[128,2048]{1,0:T(8,128)S(1)}, f32[1,128,2048]{2,1,0:T(8,128)S(1)}) custom-call(s32[2]{0:T(128)S(1)} %pad_add_fusion.1.place_ref, bf16[128,1280]{1,0:T(8,128)(2,1)} %collective-permute-done.refs_0_, bf16[128,1280]{1,0:T(8,128)(2,1)S(1)} %collective-permute-done.1.refs_1_, bf16[1280,4096]{1,0:T(8,128)(2,1)} %refs_3_.1, ...), custom_call_target="tpu_custom_call" | custom-call | flops 1 | bytes 1 | tf_op jit(solution)/shard_map/pallas_call | solution.py:151
  90.4 2.4 multiply_convert_fusion.15
  94.1 8.0 %collective-permute-start.20 = (f16[128,2048]{1,0:T(8,128)(2,1)}, f16[128,2048]{1,0:T(8,128)(2,1)}, u32[]{:S(2)}, u32[]{:S(2)}) collective-permute-start(f16[128,2048]{1,0:T(8,128)(2,1)} %multiply_convert_fusion.15), channel_id=1, source_target_pairs={{0,2},{2,0},{1,3},{3,1},{4,6},{6,4},{5,7},{7,5},{8,10},{10,8},{9,1... | collective-permute-start | bytes 1572872 | tf_op jit(solution)/shard_map/ppermute | solution.py:17
  102.1 4.3 %collective-permute-start.14 = (bf16[256,1280]{1,0:T(8,128)(2,1)}, bf16[256,1280]{1,0:T(8,128)(2,1)}, u32[]{:S(2)}, u32[]{:S(2)}) collective-permute-start(bf16[256,1280]{1,0:T(8,128)(2,1)} %shard_map.118), channel_id=1, source_target_pairs={{0,8},{1,12},{4,9},{5,13},{10,2},{11,6},{14,3},{15,7},{16,24},{17,... | collective-permute-start | bytes 1966088 | tf_op jit(solution)/shard_map/ppermute | solution.py:82
  107.6 6.5 %collective-permute-start.7 = (bf16[256,1280]{1,0:T(8,128)(2,1)}, bf16[256,1280]{1,0:T(8,128)(2,1)}, u32[]{:S(2)}, u32[]{:S(2)}) collective-permute-start(bf16[256,1280]{1,0:T(8,128)(2,1)} %shard_map.118), channel_id=1, source_target_pairs={{0,0},{1,4},{4,1},{5,5},{10,10},{11,14},{14,11},{15,15},{16,16},{1... | collective-permute-start | bytes 1966088 | tf_op jit(solution)/shard_map/ppermute | solution.py:82
  114.2 2.4 multiply_convert_fusion.12
  117.8 2.0 collective-permute-start.11
  121.8 10.0 %collective-permute-done.17 = f16[128,2048]{1,0:T(8,128)(2,1)} collective-permute-done((f16[128,2048]{1,0:T(8,128)(2,1)}, f16[128,2048]{1,0:T(8,128)(2,1)}, u32[]{:S(2)}, u32[]{:S(2)}) %collective-permute-start.17) | collective-permute-done | bytes 524320 | tf_op jit(solution)/shard_map/ppermute | solution.py:17
  133.0 7.3 %collective-permute-done.11.refs_0_ = bf16[256,1280]{1,0:T(8,128)(2,1)S(1)} collective-permute-done((bf16[256,1280]{1,0:T(8,128)(2,1)S(1)}, bf16[256,1280]{1,0:T(8,128)(2,1)S(1)}, u32[]{:S(2)}, u32[]{:S(2)}) %collective-permute-start.11) | collective-permute-done | bytes 655392 | tf_op jit(solution)/shard_map/ppermute | solution.py:17
  140.3 9.4 %shard_map.124 = (f32[256,2048]{1,0:T(8,128)S(1)}, f32[1,256,2048]{2,1,0:T(8,128)S(1)}) custom-call(s32[2]{0:T(128)S(1)} %pad_add_fusion.2.place_ref, bf16[256,1280]{1,0:T(8,128)(2,1)S(1)} %collective-permute-done.11.refs_0_, bf16[4096,1280]{1,0:T(8,128)(2,1)} %refs_2_.11, f32[16,128]{1,0:T(8,128)S(1)} %copy-done.10, f32[16,128]{1,0:T(8,128)S(1)} %slice_convert_fusion.4.refs_3_), custom_call_target="tpu_custom_call" | custom-call | flops 1 | bytes 1 | tf_op jit(solution)/shard_map/pallas_call | solution.py:151
  152.1 15.5 %shard_map.127 = (f32[256,2048]{1,0:T(8,128)S(1)}, f32[1,256,2048]{2,1,0:T(8,128)S(1)}, f32[256,2048]{1,0:T(8,128)}, f32[1,256,2048]{2,1,0:T(8,128)}) custom-call(s32[2]{0:T(128)S(1)} %pad_add_fusion.1.place_ref, bf16[256,1280]{1,0:T(8,128)(2,1)} %shard_map.125.refs_0_, bf16[256,1280]{1,0:T(8,128)(2,1)} %shard_map.126.refs_1_, bf16[1280,4096]{1,0:T(8,128)(2,1)} %refs_2_.10, ...), custom_call_target="tpu_custom_call" | custom-call | flops 1 | bytes 1 | tf_op jit(solution)/shard_map/pallas_call | solution.py:151
  167.6 1.3 copy-done.3
  170.2 5.5 %collective-permute-start.16 = (bf16[256,1280]{1,0:T(8,128)(2,1)}, bf16[256,1280]{1,0:T(8,128)(2,1)}, u32[]{:S(2)}, u32[]{:S(2)}) collective-permute-start(bf16[256,1280]{1,0:T(8,128)(2,1)} %shard_map.128), channel_id=1, source_target_pairs={{0,8},{1,12},{4,9},{5,13},{10,2},{11,6},{14,3},{15,7},{16,24},{17,... | collective-permute-start | bytes 1966088 | tf_op jit(solution)/shard_map/ppermute | solution.py:82
  175.7 6.6 %collective-permute-start.15 = (bf16[256,1280]{1,0:T(8,128)(2,1)}, bf16[256,1280]{1,0:T(8,128)(2,1)}, u32[]{:S(2)}, u32[]{:S(2)}) collective-permute-start(bf16[256,1280]{1,0:T(8,128)(2,1)} %shard_map.128), channel_id=1, source_target_pairs={{0,0},{1,4},{4,1},{5,5},{10,10},{11,14},{14,11},{15,15},{16,16},{1... | collective-permute-start | bytes 1966088 | tf_op jit(solution)/shard_map/ppermute | solution.py:82
  182.3 2.8 %fusion.9 = f16[256,2048]{1,0:T(8,128)(2,1)} fusion(f32[1,256,2048]{2,1,0:T(8,128)} %copy-done.7), kind=kLoop, calls=%fused_computation.24 | loop fusion | flops 1048576 | bytes 3145728 | tf_op jit(solution)/shard_map/convert_element_type | solution.py:21
  187.0 1.5 fusion.47
  188.5 3.4 %multiply_convert_fusion.11 = (f16[128,2048]{1,0:T(8,128)(2,1)}, f16[128,2048]{1,0:T(8,128)(2,1)}) fusion(f32[128,2048]{1,0:T(8,128)} %shard_map.129, f16[256,2048]{1,0:T(8,128)(2,1)} %collective-permute-done.18, f32[128,2048]{1,0:T(8,128)} %shard_map.131), kind=kLoop, calls=%fused_computation.44 | loop fusion | flops 2621440 | bytes 4194304 | tf_op jit(solution)/shard_map/convert_element_type | solution.py:21
  192.0 2.0 collective-permute-start.24
  194.0 1.6 multiply_add_fusion
  195.6 1.7 multiply_add_fusion.1
  198.0 9.7 %shard_map.130 = (f32[256,2048]{1,0:T(8,128)S(1)}, f32[1,256,2048]{2,1,0:T(8,128)S(1)}) custom-call(s32[2]{0:T(128)S(1)} %pad_add_fusion.1.place_ref, bf16[256,1280]{1,0:T(8,128)(2,1)} %collective-permute-done.15.refs_0_, bf16[256,1280]{1,0:T(8,128)(2,1)} %collective-permute-done.16.refs_1_, bf16[4096,1280]{1,0:T(8,128)(2,1)} %refs_2_.11, ...), custom_call_target="tpu_custom_call" | custom-call | flops 1 | bytes 1 | tf_op jit(solution)/shard_map/pallas_call | solution.py:151
  207.8 1.3 copy-done.1
  210.3 4.4 %add_multiply_fusion = (f32[128,2048]{1,0:T(8,128)}, f32[128,2048]{1,0:T(8,128)}, f32[128,2048]{1,0:T(8,128)}, f32[128,2048]{1,0:T(8,128)}) fusion(f16[128,2048]{1,0:T(8,128)(2,1)} %collective-permute-done.17, f32[256,2048]{1,0:T(8,128)S(1)} %multiply_add_fusion.1, f16[128,2048]{1,0:T(8,128)(2,1)} %collective-permute-done.20, ...), kind=kLoop, calls=%fused_computation.34 | loop fusion | flops 7864320 | bytes 10485760 | tf_op jit(solution)/shard_map/mul | solution.py:303
  215.8 2.2 convolution_bitcast_fusion.1
  218.2 1.9 convolution_bitcast_fusion.5
  220.4 1.8 multiply_add_fusion.2
  222.2 1.5 fusion.18
  223.8 1.5 fusion.19
  225.9 1.4 fusion.20
  227.5 1.4 fusion.21
  229.3 4.6 %collective-permute-start.25 = (f32[6,16,64]{2,1,0:T(8,128)S(1)}, f32[6,16,64]{2,1,0:T(8,128)S(1)}, u32[]{:S(2)}, u32[]{:S(2)}) collective-permute-start(f32[6,16,64]{2,1,0:T(8,128)S(1)} %get-tuple-element.52), channel_id=1, source_target_pairs={{0,4},{4,8},{8,12},{12,0},{1,5},{5,9},{9,13},{13,1},{2,6},{6,10},{... | collective-permute-start | bytes 73736 | tf_op jit(solution)/shard_map/ppermute | solution.py:17
  235.2 2.8 %collective-permute-start.26 = (f32[6,16,64]{2,1,0:T(8,128)S(1)}, f32[6,16,64]{2,1,0:T(8,128)}, u32[]{:S(2)}, u32[]{:S(2)}) collective-permute-start(f32[6,16,64]{2,1,0:T(8,128)S(1)} %get-tuple-element.54), channel_id=1, source_target_pairs={{0,8},{4,12},{8,0},{12,4},{1,9},{5,13},{9,1},{13,5},{2,10},{6,14},... | collective-permute-start | bytes 73736 | tf_op jit(solution)/shard_map/ppermute | solution.py:17
  238.0 2.6 collective-permute-start.34
  242.6 4.5 %collective-permute-start.29 = (f32[6,16,64]{2,1,0:T(8,128)S(1)}, f32[6,16,64]{2,1,0:T(8,128)S(1)}, u32[]{:S(2)}, u32[]{:S(2)}) collective-permute-start(f32[6,16,64]{2,1,0:T(8,128)S(1)} %fusion.36), channel_id=1, source_target_pairs={{0,3},{1,2},{2,1},{3,0},{4,7},{5,6},{6,5},{7,4},{8,11},{9,10},{10,... | collective-permute-start | bytes 73736 | tf_op jit(solution)/shard_map/ppermute | solution.py:331
  247.1 2.1 collective-permute-done.29
  249.1 2.0 collective-permute-done.28
  252.6 1.9 collective-permute-start.31
  256.3 3.0 %collective-permute-done.32 = f32[4,512]{1,0:T(4,128)S(1)} collective-permute-done((f32[4,512]{1,0:T(4,128)S(1)}, f32[4,512]{1,0:T(4,128)S(1)}, u32[]{:S(2)}, u32[]{:S(2)}) %collective-permute-start.32) | collective-permute-done | bytes 8224 | tf_op jit(solution)/shard_map/ppermute | solution.py:17
  (182 shorter events, 44.7 us)
Async XLA Ops:
  7.2 244.1 %copy-start = (bf16[3,16,64,512]{3,2,1,0:T(8,128)(2,1)S(1)}, bf16[3,16,64,512]{3,2,1,0:T(8,128)(2,1)}, u32[]{:S(2)}) copy-start(bf16[3,16,64,512]{3,2,1,0:T(8,128)(2,1)} %param.17) | copy-start | bytes 9437188
  7.2 207.5 %all-reduce.2.cloned.1.call-start = ((), (), s32[]{:S(2)}) async-start(), calls=%async_computation | async-start | bytes 524288 | tf_op jit(solution)/shard_map/psum | solution.py:251
  7.2 6.2 %copy-start.26 = (bf16[1280,192]{0,1:T(8,128)(2,1)S(1)}, bf16[1280,192]{0,1:T(8,128)(2,1)}, u32[]{:S(2)}) copy-start(bf16[1280,192]{0,1:T(8,128)(2,1)} %param.15) | copy-start | bytes 1474564
  8.5 5.6 %copy-start.15 = (bf16[2,128,1280]{2,1,0:T(8,128)(2,1)}, bf16[2,128,1280]{2,1,0:T(8,128)(2,1)S(1)}, u32[]{:S(2)}) copy-start(bf16[2,128,1280]{2,1,0:T(8,128)(2,1)S(1)} %copy.60) | copy-start | bytes 1966084
  9.8 5.0 %copy-start.16 = (bf16[2,128,1280]{2,1,0:T(8,128)(2,1)}, bf16[2,128,1280]{2,1,0:T(8,128)(2,1)S(1)}, u32[]{:S(2)}) copy-start(bf16[2,128,1280]{2,1,0:T(8,128)(2,1)S(1)} %copy.61) | copy-start | bytes 1966084
  10.8 8.1 %collective-permute-start.3 = (bf16[128,1280]{1,0:T(8,128)(2,1)}, bf16[128,1280]{1,0:T(8,128)(2,1)}, u32[]{:S(2)}, u32[]{:S(2)}) collective-permute-start(bf16[128,1280]{1,0:T(8,128)(2,1)} %get-tuple-element.51), channel_id=1, source_target_pairs={{2,8},{3,12},{6,9},{7,13},{8,2},{9,6},{12,3},{13,7},{18,24},{19,28... | collective-permute-start | bytes 983048 | tf_op jit(solution)/shard_map/ppermute | solution.py:82
  12.1 15.6 %collective-permute-start.2 = (bf16[128,1280]{1,0:T(8,128)(2,1)}, bf16[128,1280]{1,0:T(8,128)(2,1)}, u32[]{:S(2)}, u32[]{:S(2)}) collective-permute-start(bf16[128,1280]{1,0:T(8,128)(2,1)} %get-tuple-element.51), channel_id=1, source_target_pairs={{2,0},{3,4},{6,1},{7,5},{8,10},{9,14},{12,11},{13,15},{18,16},{19,... | collective-permute-start | bytes 983048 | tf_op jit(solution)/shard_map/ppermute | solution.py:82
  14.8 51.8 %collective-permute-start.1 = (bf16[128,1280]{1,0:T(8,128)(2,1)}, bf16[128,1280]{1,0:T(8,128)(2,1)S(1)}, u32[]{:S(2)}, u32[]{:S(2)}) collective-permute-start(bf16[128,1280]{1,0:T(8,128)(2,1)} %shard_map.113), channel_id=1, source_target_pairs={{2,8},{3,12},{6,9},{7,13},{8,2},{9,6},{12,3},{13,7},{18,24},{19,28... | collective-permute-start | bytes 983048 | tf_op jit(solution)/shard_map/ppermute | solution.py:82
  15.5 52.6 %collective-permute-start = (bf16[128,1280]{1,0:T(8,128)(2,1)}, bf16[128,1280]{1,0:T(8,128)(2,1)}, u32[]{:S(2)}, u32[]{:S(2)}) collective-permute-start(bf16[128,1280]{1,0:T(8,128)(2,1)} %shard_map.113), channel_id=1, source_target_pairs={{2,0},{3,4},{6,1},{7,5},{8,10},{9,14},{12,11},{13,15},{18,16},{19,... | collective-permute-start | bytes 983048 | tf_op jit(solution)/shard_map/ppermute | solution.py:82
  36.3 8.7 %copy-start.28 = (s32[2]{0:T(128)S(1)}, s32[2]{0:T(128)}, u32[]{:S(2)}) copy-start(s32[2]{0:T(128)} %param.18) | copy-start | bytes 28
  44.8 2.0 collective-permute-start.8
  45.1 18.6 %collective-permute-start.4 = (f16[128,2048]{1,0:T(8,128)(2,1)S(1)}, f16[128,2048]{1,0:T(8,128)(2,1)S(1)}, u32[]{:S(2)}, u32[]{:S(2)}) collective-permute-start(f16[128,2048]{1,0:T(8,128)(2,1)S(1)} %fusion.12), channel_id=1, source_target_pairs={{0,1},{1,0},{2,3},{3,2},{4,5},{5,4},{6,7},{7,6},{8,9},{9,8},{10,11... | collective-permute-start | bytes 1572872 | tf_op jit(solution)/shard_map/ppermute | solution.py:17
  47.8 54.2 %collective-permute-start.12 = (f16[128,2048]{1,0:T(8,128)(2,1)}, f16[128,2048]{1,0:T(8,128)(2,1)}, u32[]{:S(2)}, u32[]{:S(2)}) collective-permute-start(f16[128,2048]{1,0:T(8,128)(2,1)} %multiply_convert_fusion.14), channel_id=1, source_target_pairs={{0,2},{2,0},{1,3},{3,1},{4,6},{6,4},{5,7},{7,5},{8,10},{10,8},{9,1... | collective-permute-start | bytes 1572872 | tf_op jit(solution)/shard_map/ppermute | solution.py:17
  64.6 24.0 %collective-permute-start.5 = (f16[128,2048]{1,0:T(8,128)(2,1)}, f16[128,2048]{1,0:T(8,128)(2,1)}, u32[]{:S(2)}, u32[]{:S(2)}) collective-permute-start(f16[128,2048]{1,0:T(8,128)(2,1)} %multiply_convert_fusion.17), channel_id=1, source_target_pairs={{0,2},{2,0},{1,3},{3,1},{4,6},{6,4},{5,7},{7,5},{8,10},{10,8},{9,1... | collective-permute-start | bytes 1572872 | tf_op jit(solution)/shard_map/ppermute | solution.py:17
  64.7 51.9 %collective-permute-start.10 = (bf16[256,1280]{1,0:T(8,128)(2,1)}, bf16[256,1280]{1,0:T(8,128)(2,1)}, u32[]{:S(2)}, u32[]{:S(2)}) collective-permute-start(bf16[256,1280]{1,0:T(8,128)(2,1)} %shard_map.119), channel_id=1, source_target_pairs={{2,10},{3,14},{6,11},{7,15},{8,0},{9,4},{12,1},{13,5},{18,26},{19,... | collective-permute-start | bytes 1966088 | tf_op jit(solution)/shard_map/ppermute | solution.py:82
  66.6 9.8 %copy-start.11 = (f32[16,128]{1,0:T(8,128)}, f32[16,128]{1,0:T(8,128)S(1)}, u32[]{:S(2)}) copy-start(f32[16,128]{1,0:T(8,128)S(1)} %slice_convert_fusion.10.refs_4_.refs_3_.refs_1_) | copy-start | bytes 24580
  66.6 50.0 %collective-permute-start.9 = (bf16[256,1280]{1,0:T(8,128)(2,1)}, bf16[256,1280]{1,0:T(8,128)(2,1)}, u32[]{:S(2)}, u32[]{:S(2)}) collective-permute-start(bf16[256,1280]{1,0:T(8,128)(2,1)} %shard_map.119), channel_id=1, source_target_pairs={{2,2},{3,6},{6,3},{7,7},{8,8},{9,12},{12,9},{13,13},{18,18},{19,22... | collective-permute-start | bytes 1966088 | tf_op jit(solution)/shard_map/ppermute | solution.py:82
  78.4 12.1 %collective-permute-start.6 = (f16[128,2048]{1,0:T(8,128)(2,1)}, f16[128,2048]{1,0:T(8,128)(2,1)}, u32[]{:S(2)}, u32[]{:S(2)}) collective-permute-start(f16[128,2048]{1,0:T(8,128)(2,1)} %copy-done.25), channel_id=1, source_target_pairs={{0,1},{1,0},{2,3},{3,2},{4,5},{5,4},{6,7},{7,6},{8,9},{9,8},{10,11... | collective-permute-start | bytes 1572872 | tf_op jit(solution)/shard_map/ppermute | solution.py:17
  88.6 19.0 %collective-permute-start.13 = (f16[128,2048]{1,0:T(8,128)(2,1)}, f16[128,2048]{1,0:T(8,128)(2,1)}, u32[]{:S(2)}, u32[]{:S(2)}) collective-permute-start(f16[128,2048]{1,0:T(8,128)(2,1)} %fusion.15), channel_id=1, source_target_pairs={{0,1},{1,0},{2,3},{3,2},{4,5},{5,4},{6,7},{7,6},{8,9},{9,8},{10,11... | collective-permute-start | bytes 1572872 | tf_op jit(solution)/shard_map/ppermute | solution.py:17
  94.1 26.4 %collective-permute-start.20 = (f16[128,2048]{1,0:T(8,128)(2,1)}, f16[128,2048]{1,0:T(8,128)(2,1)}, u32[]{:S(2)}, u32[]{:S(2)}) collective-permute-start(f16[128,2048]{1,0:T(8,128)(2,1)} %multiply_convert_fusion.15), channel_id=1, source_target_pairs={{0,2},{2,0},{1,3},{3,1},{4,6},{6,4},{5,7},{7,5},{8,10},{10,8},{9,1... | collective-permute-start | bytes 1572872 | tf_op jit(solution)/shard_map/ppermute | solution.py:17
  102.1 50.0 %collective-permute-start.14 = (bf16[256,1280]{1,0:T(8,128)(2,1)}, bf16[256,1280]{1,0:T(8,128)(2,1)}, u32[]{:S(2)}, u32[]{:S(2)}) collective-permute-start(bf16[256,1280]{1,0:T(8,128)(2,1)} %shard_map.118), channel_id=1, source_target_pairs={{0,8},{1,12},{4,9},{5,13},{10,2},{11,6},{14,3},{15,7},{16,24},{17,... | collective-permute-start | bytes 1966088 | tf_op jit(solution)/shard_map/ppermute | solution.py:82
  107.6 44.4 %collective-permute-start.7 = (bf16[256,1280]{1,0:T(8,128)(2,1)}, bf16[256,1280]{1,0:T(8,128)(2,1)}, u32[]{:S(2)}, u32[]{:S(2)}) collective-permute-start(bf16[256,1280]{1,0:T(8,128)(2,1)} %shard_map.118), channel_id=1, source_target_pairs={{0,0},{1,4},{4,1},{5,5},{10,10},{11,14},{14,11},{15,15},{16,16},{1... | collective-permute-start | bytes 1966088 | tf_op jit(solution)/shard_map/ppermute | solution.py:82
  116.6 23.8 %copy-start.10 = (f32[16,128]{1,0:T(8,128)S(1)}, f32[16,128]{1,0:T(8,128)}, u32[]{:S(2)}) copy-start(f32[16,128]{1,0:T(8,128)} %slice_convert_fusion.8.refs_1_.refs_2_) | copy-start | bytes 24580
  116.6 15.2 %collective-permute-start.17 = (f16[128,2048]{1,0:T(8,128)(2,1)}, f16[128,2048]{1,0:T(8,128)(2,1)}, u32[]{:S(2)}, u32[]{:S(2)}) collective-permute-start(f16[128,2048]{1,0:T(8,128)(2,1)} %multiply_convert_fusion.12), channel_id=1, source_target_pairs={{0,2},{2,0},{1,3},{3,1},{4,6},{6,4},{5,7},{7,5},{8,10},{10,8},{9,1... | collective-permute-start | bytes 1572872 | tf_op jit(solution)/shard_map/ppermute | solution.py:17
  117.8 22.5 %collective-permute-start.11 = (bf16[256,1280]{1,0:T(8,128)(2,1)S(1)}, bf16[256,1280]{1,0:T(8,128)(2,1)S(1)}, u32[]{:S(2)}, u32[]{:S(2)}) collective-permute-start(bf16[256,1280]{1,0:T(8,128)(2,1)S(1)} %broadcast_select_fusion), channel_id=1, source_target_pairs={{0,2},{2,0},{1,3},{3,1},{4,6},{6,4},{5,7},{7,5},{8,10},{10,8},{9,1... | collective-permute-start | bytes 1966088 | tf_op jit(solution)/shard_map/ppermute | solution.py:17
  152.0 36.5 %collective-permute-start.18 = (f16[256,2048]{1,0:T(8,128)(2,1)}, f16[256,2048]{1,0:T(8,128)(2,1)}, u32[]{:S(2)}, u32[]{:S(2)}) collective-permute-start(f16[256,2048]{1,0:T(8,128)(2,1)} %copy-done.24), channel_id=1, source_target_pairs={{0,1},{1,0},{2,3},{3,2},{4,5},{5,4},{6,7},{7,6},{8,9},{9,8},{10,11... | collective-permute-start | bytes 3145736 | tf_op jit(solution)/shard_map/ppermute | solution.py:17
  170.2 14.8 %copy-start.21 = (f32[1,256,2048]{2,1,0:T(8,128)S(1)}, f32[1,256,2048]{2,1,0:T(8,128)}, u32[]{:S(2)}) copy-start(f32[1,256,2048]{2,1,0:T(8,128)} %get-tuple-element.36) | copy-start | bytes 6291460
  170.2 27.8 %collective-permute-start.16 = (bf16[256,1280]{1,0:T(8,128)(2,1)}, bf16[256,1280]{1,0:T(8,128)(2,1)}, u32[]{:S(2)}, u32[]{:S(2)}) collective-permute-start(bf16[256,1280]{1,0:T(8,128)(2,1)} %shard_map.128), channel_id=1, source_target_pairs={{0,8},{1,12},{4,9},{5,13},{10,2},{11,6},{14,3},{15,7},{16,24},{17,... | collective-permute-start | bytes 1966088 | tf_op jit(solution)/shard_map/ppermute | solution.py:82
  175.7 22.3 %collective-permute-start.15 = (bf16[256,1280]{1,0:T(8,128)(2,1)}, bf16[256,1280]{1,0:T(8,128)(2,1)}, u32[]{:S(2)}, u32[]{:S(2)}) collective-permute-start(bf16[256,1280]{1,0:T(8,128)(2,1)} %shard_map.128), channel_id=1, source_target_pairs={{0,0},{1,4},{4,1},{5,5},{10,10},{11,14},{14,11},{15,15},{16,16},{1... | collective-permute-start | bytes 1966088 | tf_op jit(solution)/shard_map/ppermute | solution.py:82
  185.0 6.9 %collective-permute-start.23 = (f16[256,2048]{1,0:T(8,128)(2,1)}, f16[256,2048]{1,0:T(8,128)(2,1)}, u32[]{:S(2)}, u32[]{:S(2)}) collective-permute-start(f16[256,2048]{1,0:T(8,128)(2,1)} %fusion.9), channel_id=1, source_target_pairs={{0,1},{1,0},{2,3},{3,2},{4,5},{5,4},{6,7},{7,6},{8,9},{9,8},{10,11... | collective-permute-start | bytes 3145736 | tf_op jit(solution)/shard_map/ppermute | solution.py:17
  186.3 9.3 %collective-permute-start.22 = (f16[256,2048]{1,0:T(8,128)(2,1)}, f16[256,2048]{1,0:T(8,128)(2,1)}, u32[]{:S(2)}, u32[]{:S(2)}) collective-permute-start(f16[256,2048]{1,0:T(8,128)(2,1)} %fusion.8), channel_id=1, source_target_pairs={{0,1},{1,0},{2,3},{3,2},{4,5},{5,4},{6,7},{7,6},{8,9},{9,8},{10,11... | collective-permute-start | bytes 3145736 | tf_op jit(solution)/shard_map/ppermute | solution.py:17
  188.5 5.5 %copy-start.4 = (f32[256,2048]{1,0:T(8,128)S(1)}, f32[256,2048]{1,0:T(8,128)}, u32[]{:S(2)}) copy-start(f32[256,2048]{1,0:T(8,128)} %copy-done.3) | copy-start | bytes 6291460
  192.0 30.2 %collective-permute-start.21 = (f16[128,2048]{1,0:T(8,128)(2,1)}, f16[128,2048]{1,0:T(8,128)(2,1)}, u32[]{:S(2)}, u32[]{:S(2)}) collective-permute-start(f16[128,2048]{1,0:T(8,128)(2,1)} %get-tuple-element.49), channel_id=1, source_target_pairs={{0,2},{2,0},{1,3},{3,1},{4,6},{6,4},{5,7},{7,5},{8,10},{10,8},{9,1... | collective-permute-start | bytes 1572872 | tf_op jit(solution)/shard_map/ppermute | solution.py:17
  192.0 3.6 %copy-start.22 = (f32[256,2048]{1,0:T(8,128)S(1)}, f32[256,2048]{1,0:T(8,128)}, u32[]{:S(2)}) copy-start(f32[256,2048]{1,0:T(8,128)} %get-tuple-element.35) | copy-start | bytes 6291460
  192.0 33.9 %collective-permute-start.24 = (f16[128,2048]{1,0:T(8,128)(2,1)}, f16[128,2048]{1,0:T(8,128)(2,1)}, u32[]{:S(2)}, u32[]{:S(2)}) collective-permute-start(f16[128,2048]{1,0:T(8,128)(2,1)} %get-tuple-element.48), channel_id=1, source_target_pairs={{0,2},{2,0},{1,3},{3,1},{4,6},{6,4},{5,7},{7,5},{8,10},{10,8},{9,1... | collective-permute-start | bytes 1572872 | tf_op jit(solution)/shard_map/ppermute | solution.py:17
  197.3 13.0 %copy-start.13 = (f32[256,2048]{1,0:T(8,128)}, f32[256,2048]{1,0:T(8,128)S(1)}, u32[]{:S(2)}) copy-start(f32[256,2048]{1,0:T(8,128)S(1)} %multiply_add_fusion.1) | copy-start | bytes 6291460
  210.3 9.9 %collective-permute-start.19 = (f16[256,2048]{1,0:T(8,128)(2,1)}, f16[256,2048]{1,0:T(8,128)(2,1)}, u32[]{:S(2)}, u32[]{:S(2)}) collective-permute-start(f16[256,2048]{1,0:T(8,128)(2,1)} %fusion.7), channel_id=1, source_target_pairs={{0,1},{1,0},{2,3},{3,2},{4,5},{5,4},{6,7},{7,6},{8,9},{9,8},{10,11... | collective-permute-start | bytes 3145736 | tf_op jit(solution)/shard_map/ppermute | solution.py:17
  227.3 10.7 %copy-start.27 = (s32[2]{0:T(128)S(1)}, s32[2]{0:T(128)}, u32[]{:S(2)}) copy-start(s32[2]{0:T(128)} %param.19) | copy-start | bytes 28
  229.3 11.3 %collective-permute-start.25 = (f32[6,16,64]{2,1,0:T(8,128)S(1)}, f32[6,16,64]{2,1,0:T(8,128)S(1)}, u32[]{:S(2)}, u32[]{:S(2)}) collective-permute-start(f32[6,16,64]{2,1,0:T(8,128)S(1)} %get-tuple-element.52), channel_id=1, source_target_pairs={{0,4},{4,8},{8,12},{12,0},{1,5},{5,9},{9,13},{13,1},{2,6},{6,10},{... | collective-permute-start | bytes 73736 | tf_op jit(solution)/shard_map/ppermute | solution.py:17
  234.0 6.6 %collective-permute-start.27 = (f32[6,16,64]{2,1,0:T(8,128)S(1)}, f32[6,16,64]{2,1,0:T(8,128)}, u32[]{:S(2)}, u32[]{:S(2)}) collective-permute-start(f32[6,16,64]{2,1,0:T(8,128)S(1)} %get-tuple-element.53), channel_id=1, source_target_pairs={{0,12},{4,0},{8,4},{12,8},{1,13},{5,1},{9,5},{13,9},{2,14},{6,2},{... | collective-permute-start | bytes 73736 | tf_op jit(solution)/shard_map/ppermute | solution.py:17
  235.2 6.4 %collective-permute-start.26 = (f32[6,16,64]{2,1,0:T(8,128)S(1)}, f32[6,16,64]{2,1,0:T(8,128)}, u32[]{:S(2)}, u32[]{:S(2)}) collective-permute-start(f32[6,16,64]{2,1,0:T(8,128)S(1)} %get-tuple-element.54), channel_id=1, source_target_pairs={{0,8},{4,12},{8,0},{12,4},{1,9},{5,13},{9,1},{13,5},{2,10},{6,14},... | collective-permute-start | bytes 73736 | tf_op jit(solution)/shard_map/ppermute | solution.py:17
  238.0 4.5 %collective-permute-start.34 = (s32[2]{0:T(128)S(1)}, s32[2]{0:T(128)S(1)}, u32[]{:S(2)}, u32[]{:S(2)}) collective-permute-start(s32[2]{0:T(128)S(1)} %copy-done.27), channel_id=1, source_target_pairs={{0,2},{2,0},{1,3},{3,1},{4,6},{6,4},{5,7},{7,5},{8,10},{10,8},{9,1... | collective-permute-start | bytes 32 | tf_op jit(solution)/shard_map/ppermute | solution.py:17
  242.4 4.6 %collective-permute-start.30 = (f32[6,16,64]{2,1,0:T(8,128)S(1)}, f32[6,16,64]{2,1,0:T(8,128)S(1)}, u32[]{:S(2)}, u32[]{:S(2)}) collective-permute-start(f32[6,16,64]{2,1,0:T(8,128)S(1)} %fusion.36), channel_id=1, source_target_pairs={{0,1},{1,0},{2,3},{3,2},{4,5},{5,4},{6,7},{7,6},{8,9},{9,8},{10,11... | collective-permute-start | bytes 73736 | tf_op jit(solution)/shard_map/ppermute | solution.py:331
  242.6 6.6 %collective-permute-start.29 = (f32[6,16,64]{2,1,0:T(8,128)S(1)}, f32[6,16,64]{2,1,0:T(8,128)S(1)}, u32[]{:S(2)}, u32[]{:S(2)}) collective-permute-start(f32[6,16,64]{2,1,0:T(8,128)S(1)} %fusion.36), channel_id=1, source_target_pairs={{0,3},{1,2},{2,1},{3,0},{4,7},{5,6},{6,5},{7,4},{8,11},{9,10},{10,... | collective-permute-start | bytes 73736 | tf_op jit(solution)/shard_map/ppermute | solution.py:331
  247.0 4.1 %collective-permute-start.28 = (f32[6,16,64]{2,1,0:T(8,128)S(1)}, f32[6,16,64]{2,1,0:T(8,128)S(1)}, u32[]{:S(2)}, u32[]{:S(2)}) collective-permute-start(f32[6,16,64]{2,1,0:T(8,128)S(1)} %fusion.36), channel_id=1, source_target_pairs={{0,2},{1,3},{2,0},{3,1},{4,6},{5,7},{6,4},{7,5},{8,10},{9,11},{10,... | collective-permute-start | bytes 73736 | tf_op jit(solution)/shard_map/ppermute | solution.py:331
  252.6 3.7 %collective-permute-start.31 = (f32[4,512]{1,0:T(4,128)S(1)}, f32[4,512]{1,0:T(4,128)S(1)}, u32[]{:S(2)}, u32[]{:S(2)}) collective-permute-start(f32[4,512]{1,0:T(4,128)S(1)} %fusion.49), channel_id=1, source_target_pairs={{0,12},{4,0},{8,4},{12,8},{1,13},{5,1},{9,5},{13,9},{2,14},{6,2},{... | collective-permute-start | bytes 24584 | tf_op jit(solution)/shard_map/ppermute | solution.py:17
  254.6 5.4 %collective-permute-start.33 = (f32[4,512]{1,0:T(4,128)S(1)}, f32[4,512]{1,0:T(4,128)S(1)}, u32[]{:S(2)}, u32[]{:S(2)}) collective-permute-start(f32[4,512]{1,0:T(4,128)S(1)} %fusion.49), channel_id=1, source_target_pairs={{0,4},{4,8},{8,12},{12,0},{1,5},{5,9},{9,13},{13,1},{2,6},{6,10},{... | collective-permute-start | bytes 24584 | tf_op jit(solution)/shard_map/ppermute | solution.py:17
  254.8 4.5 %collective-permute-start.32 = (f32[4,512]{1,0:T(4,128)S(1)}, f32[4,512]{1,0:T(4,128)S(1)}, u32[]{:S(2)}, u32[]{:S(2)}) collective-permute-start(f32[4,512]{1,0:T(4,128)S(1)} %fusion.49), channel_id=1, source_target_pairs={{0,8},{4,12},{8,0},{12,4},{1,9},{5,13},{9,1},{13,5},{2,10},{6,14},... | collective-permute-start | bytes 24584 | tf_op jit(solution)/shard_map/ppermute | solution.py:17
  (17 other events, 26.7 us)
Sparse Core Ops, SparseCore 0:
  78.5 46.9 all-reduce.1

commit v6 on v5

--- a/solution.py
+++ b/solution.py
@@ -50,13 +50,7 @@
     return total
 
 
-def token(value):
-    corner = value[(0,) * (value.ndim - 2)]
-    return corner[:16, :128].astype(F32) if value.dtype == jnp.float16 else value
-
-
 def after(value, *earlier):
-    earlier = [token(one) for one in earlier]
     anywhere = pl.BlockSpec(memory_space=pl.ANY)
     return pl.pallas_call(
         lambda *refs: None,
@@ -98,81 +92,29 @@
     return [lax.dynamic_slice_in_dim(whole, owner * rows, rows, 0) for owner in owners]
 
 
-def products_kernel(by_rows, n_pieces, n_weights, place_ref, *refs):
-    pieces, refs = refs[:n_pieces], refs[n_pieces:]
-    weight_refs, refs = refs[:n_weights], refs[n_weights:]
-    kept_refs, sent_refs = refs[-1 - 2 * n_weights : -1 : 2], refs[-2 * n_weights : -1 : 2]
-    tokens_ref = refs[-1]
-    keep = pl.program_id(0) == pl.num_programs(0) - 1
-
-    @pl.when((pl.program_id(0) == 0) & (pl.program_id(1) == 0))
-    def _():
-        for place, piece in enumerate(pieces):
-
-            @pl.when(place_ref[1] == place)
-            def _():
-                tokens_ref[...] = piece[...]
-
+def products_kernel(by_rows, tokens_ref, *refs):
     contract = (((1,), (1 if by_rows else 0,)), ((), ()))
-    for weight_ref, kept_ref, sent_ref in zip(weight_refs, kept_refs, sent_refs):
-        product = lax.dot_general(
+    for weight_ref, out_ref in zip(refs, refs[len(refs) // 2 :]):
+        out_ref[...] = lax.dot_general(
             tokens_ref[...], weight_ref[...], contract, preferred_element_type=F32
         )
 
-        @pl.when(keep)
-        def _():
-            kept_ref[...] = product
-
-        @pl.when(jnp.logical_not(keep))
-        def _():
-            sent_ref[0] = product
-
-
-def products(pieces, weights, by_rows, n_cores, *earlier):
-    earlier = [token(one) for one in earlier]
-    rows, depth = pieces[0].shape
-    hidden = weights[0].shape[0 if by_rows else 1] // n_cores
+
+def products(tokens, weights, by_rows, vmem_mib):
+    rows, depth = tokens.shape
+    hidden = weights[0].shape[0 if by_rows else 1]
     tile = min(512, hidden)
-    tiles = hidden // tile
-
-    def weight_block(turn, i, place_ref):
-        block = lax.rem(place_ref[0] + turn + 1, n_cores) * tiles + i
-        return (block, 0) if by_rows else (0, block)
-
-    core = lax.axis_index("test")
-    piece = piece_index(0) if len(pieces) == 2 else 0 * core
-
-    def kept_block(turn, i, place_ref):
-        return (0, jnp.where(turn == n_cores - 1, i, 0))
-
-    def sent_block(turn, i, place_ref):
-        return (jnp.minimum(turn, n_cores - 2), 0, jnp.where(turn == n_cores - 1, tiles - 1, i))
-
-    outs = pl.pallas_call(
-        functools.partial(products_kernel, by_rows, len(pieces), len(weights)),
-        out_shape=[
-            jax.ShapeDtypeStruct((rows, hidden), F32),
-            jax.ShapeDtypeStruct((n_cores - 1, rows, hidden), F32),
-        ]
-        * len(weights),
-        grid_spec=pltpu.PrefetchScalarGridSpec(
-            num_scalar_prefetch=1,
-            grid=(n_cores, tiles),
-            in_specs=[pl.BlockSpec((rows, depth), lambda turn, i, place_ref: (0, 0))] * len(pieces)
-            + [pl.BlockSpec((tile, depth) if by_rows else (depth, tile), weight_block)]
-            * len(weights)
-            + [pl.BlockSpec(memory_space=pl.ANY)] * len(earlier),
-            out_specs=[
-                pl.BlockSpec((rows, tile), kept_block),
-                pl.BlockSpec((1, rows, tile), sent_block),
-            ]
-            * len(weights),
-            scratch_shapes=[pltpu.VMEM((rows, depth), jnp.bfloat16)],
-        ),
-        compiler_params=pltpu.CompilerParams(vmem_limit_bytes=48 * 2**20),
+    block = ((tile, depth), lambda i: (i, 0)) if by_rows else ((depth, tile), lambda i: (0, i))
+    return pl.pallas_call(
+        functools.partial(products_kernel, by_rows),
+        out_shape=[jax.ShapeDtypeStruct((rows, hidden), F32)] * len(weights),
+        grid=(hidden // tile,),
+        in_specs=[pl.BlockSpec((rows, depth), lambda i: (0, 0))]
+        + [pl.BlockSpec(*block)] * len(weights),
+        out_specs=[pl.BlockSpec((rows, tile), lambda i: (0, i))] * len(weights),
+        compiler_params=pltpu.CompilerParams(vmem_limit_bytes=vmem_mib * 2**20),
         cost_estimate=pl.CostEstimate(flops=1, bytes_accessed=1, transcendentals=0),
-    )(jnp.stack([core, piece]), *pieces, *weights, *earlier)
-    return list(zip(outs[::2], outs[1::2]))
+    )(tokens, *weights)
 
 
 def on_device(
@@ -197,26 +139,16 @@
     ex_index = lax.axis_index("example")
     hid_part = w_gate.shape[1] // n_cores
 
-    def core_swap(product):
-        kept, others = product
-        packed = [pack(others[step - 1]) for step in range(1, n_cores)]
-        got = [shift(sent, "test", step + 1) for step, sent in enumerate(packed)]
-        return kept, packed, got
-
-    def core_sum(kept, got):
-        return kept + sum(unpack(one) for one in got)
-
-    arrived = [[[] for _ in range(ex_loc)] for _ in range(3)]
-    queue = []
-
-    def send(which, e, step, kept, got, *earlier):
-        earlier = queue[-2:-1] + list(earlier)
-        if earlier:
-            kept = after(kept, *earlier)
-        sent = pack(core_sum(kept, got))
-        queue.append(shift(sent, "example", step))
-        arrived[which][e].append(queue[-1])
-        return sent
+    def forward(tokens, weight):
+        return jnp.dot(tokens, weight, preferred_element_type=F32)
+
+    def core_sum(product):
+        kept = lax.dynamic_slice_in_dim(product, core * hid_part, hid_part, 1)
+        for step in range(1, n_cores):
+            to = lax.rem(core + step, n_cores)
+            sent = pack(lax.dynamic_slice_in_dim(product, to * hid_part, hid_part, 1))
+            kept = kept + unpack(shift(sent, "test", step))
+        return kept
 
     flat_acts = activations.reshape(tok_rows, d_local)
     flat_grad = out_grad.reshape(tok_rows, d_local)
@@ -227,61 +159,54 @@
         ],
         1,
     )
+
     direct = (n_z, n_ex, n_cores) == (4, 2, 2)
     examples = [slice(e * seq_len, (e + 1) * seq_len) for e in range(ex_loc)]
+    arrived = [[[] for _ in range(ex_loc)] for _ in range(3)]
     if direct:
-        starts = [activations[0]] + [after(one, model_part) for one in activations[1:]]
-        acts_far = [[spread_features([start, start], 1, True) for start in starts]]
+        acts_far = spread_features([flat_acts] * 2, 1, True)
+        acts_far = [jnp.where(piece_index(0) == 0, after(acts_far[0], model_part), acts_far[1])]
+        grad_across = spread_features([flat_grad] * 2, 1, False)
     else:
         acts_here = gathered_features(flat_acts, n_ex, n_cores)
         grad_here = gathered_features(flat_grad, n_ex, n_cores)
-        acts_far = [[[block[rows]] for rows in examples] for block in acts_here[1:]]
-    earlier, marks = [], []
-    for e in range(ex_loc):
-        for step in range(1, n_ex):
-            sent = []
-            for which, weight in enumerate((w_gate, w_up)):
-                pieces = acts_far[step - 1][e]
-                (far,) = products(pieces, (weight,), False, n_cores, *earlier)
-                kept, packed, got = core_swap(far)
-                sent.append(send(which, e, step, kept, got))
-                earlier = earlier[-1:] + [packed[-1]]
-            earlier = [earlier[-1]] + sent[:1]
-            marks.append(sent)
-    model_sum = lax.psum(after(model_part, marks[0][0]), "tensor")
+        acts_far, grad_far = acts_here[1:], grad_here[1:]
+    for step in range(1, n_ex):
+        gate_far = forward(acts_far[step - 1], w_gate)
+        up_far = forward(after(acts_far[step - 1], gate_far), w_up)
+        if direct:
+            grad_across = [after(piece, gate_far) for piece in grad_across]
+            grad_far = [shift(jnp.where(piece_index(1) == 0, *grad_across), "example", 1)]
+        both = jnp.stack([core_sum(gate_far), core_sum(up_far)])
+        received = unpack(shift(pack(both), "example", step))
+        for e, rows in enumerate(examples):
+            for which in range(2):
+                arrived[which][e].append(received[which, rows])
+        (down_far,) = products(after(grad_far[step - 1], both), [w_down], True, 16)
+        summed = core_sum(down_far)
+        for e, rows in enumerate(examples):
+            arrived[2][e].append(unpack(shift(pack(summed[rows]), "example", step)))
+    model_sum = lax.psum(after(model_part, gate_far), "tensor")
     if direct:
-        start = after(flat_grad, marks[0][1])
-        pieces = spread_features([start, start], 1, False)
-        pieces = [after(piece, marks[-1][0]) for piece in pieces]
-        grad_far = [[shift(jnp.where(piece_index(1) == 0, *pieces), "example", 1)]]
-        start = after(flat_acts, marks[-1][0])
+        start = after(flat_acts, summed)
         acts_near = spread_features([start, start], 0, False)
-    else:
-        grad_far = [[block] for block in grad_here[1:]]
-        acts_near = acts_here[:1]
-    for step in range(1, n_ex):
-        (far,) = products(grad_far[step - 1], (w_down,), True, n_cores, *marks[-1])
-        kept, packed, got = core_swap(far)
-        for e, rows in enumerate(examples):
-            sent = send(2, e, step, kept[rows], [one[rows] for one in got])
-    if direct:
-        acts_near = [after(piece, packed[-1]) for piece in acts_near]
-    acts_near = products(acts_near, (w_gate, w_up), False, n_cores)
-    if direct:
-        start = after(flat_grad, acts_near[0][0])
+        acts_near = jnp.where(piece_index(0) == 0, *acts_near)
+        start = after(flat_grad, acts_near)
         grad_near = spread_features([start, start], 0, False)
     else:
-        grad_near = grad_here[:1]
-    (grad_near,) = products(grad_near, (w_down,), True, n_cores, sent)
-    model_sum = after(model_sum, grad_near[0])
-    own = []
-    for near in (*acts_near, grad_near):
-        kept, _, got = core_swap(near)
-        own.append(lax.optimization_barrier(core_sum(kept, got)))
+        acts_near, grad_near = acts_here[0], grad_here[0]
+    (gate_near,) = products(acts_near, [w_gate], False, 48)
+    (up_near,) = products(after(acts_near, received), [w_up], False, 48)
+    if direct:
+        grad_near = [after(piece, gate_near) for piece in grad_near]
+        grad_near = jnp.where(piece_index(0) == 0, *grad_near)
+    (grad_near,) = products(grad_near, [w_down], True, 48)
+    model_sum = after(model_sum, grad_near)
+    own = [core_sum(near) for near in (gate_near, up_near, grad_near)]
 
     def total(which, e):
         kept = own[which][e * seq_len : (e + 1) * seq_len]
-        return kept + sum(unpack(one) for one in arrived[which][e])
+        return kept + sum(arrived[which][e])
 
     hid_proj = lax.dynamic_slice_in_dim(proj_hidden, core * hid_part, hid_part, 0)
     positions = jnp.arange(seq_len, dtype=jnp.int32)

time: 271 us -> 271 us (level)
  Pallas kernels: 68 us -> 30.8 us
  waiting for transfers between devices: 37.1 us -> 65.1 us
  matrix products: 13.8 us -> 26.6 us
  starting transfers between devices: 77 us -> 66.3 us
  local copies, waits for them, and re-layouts: 17.9 us -> 23.3 us
    pallas_call x7 -> x4, Pallas kernels: 68 us -> 30.8 us  [products(): pl.pallas_call(functools.partial(products_kernel, by_rows), out_shape=[ja...]
    ppermute x10 -> x8, waiting for transfers between devices: 8.91 us -> 44.9 us  [spread_features(): lax.ppermute(starts[turn], ('tensor', 'example', 'test'), pairs)]
    dot_general x0 -> x2, matrix products: none -> 14 us  [forward(): return jnp.dot(tokens, weight, preferred_element_type=F32)]
    convert_element_type x13 -> x0, other arithmetic: 10.4 us -> none  [token(): corner[:16, :128].astype(F32)]
    unnamed x68 -> x45, local copies, waits for them, and re-layouts: 13.6 us -> 21.4 us
    another operation x2 -> x3, other arithmetic: 0.15 us -> 7.3 us  [on_device(): both = jnp.stack([core_sum(gate_far), core_sum(up_far)])]
    ppermute x22 -> x17, waiting for transfers between devices: 24.1 us -> 17.3 us  [shift(): return lax.ppermute(value, axis, [(i, (i + step) % n) for i in range(n)])]
    ppermute x22 -> x17, starting transfers between devices: 42.2 us -> 36.1 us  [shift(): return lax.ppermute(value, axis, [(i, (i + step) % n) for i in range(n)])]
  transfers between devices with their start and end apart: 36 -> 29, of which waited for: 10 -> 12; matrix products, arithmetic and copies ran while one was open for 20% -> 23% of each run, Pallas kernels for 25% -> 9%
where the time goes in v6:
time: 271 us; the launch traced here: 268 us
  starting transfers between devices  66.3 us (24%)
  waiting for transfers between devices  65.1 us (24%)
  other arithmetic  41.6 us (15%)
  Pallas kernels  30.8 us (11%)
  matrix products  26.6 us (10%)
  local copies, waits for them, and re-layouts  23.3 us (9%)
  between operations  14.6 us (5%)
    ppermute x8, waiting for transfers between devices, spread_features(): lax.ppermute(starts[turn], ('tensor', 'example', 'test'), pairs)  44.9 us
    ppermute x17, starting transfers between devices, shift(): return lax.ppermute(value, axis, [(i, (i + step) % n) for i in range(n)])  36.1 us
    pallas_call x4, Pallas kernels, products(): pl.pallas_call(functools.partial(products_kernel, by_rows), out_shape=[ja...  30.8 us
    ppermute x8, starting transfers between devices, spread_features(): lax.ppermute(starts[turn], ('tensor', 'example', 'test'), pairs)  27.9 us
    unnamed x45, local copies, waits for them, and re-layouts  21.4 us
    ppermute x17, waiting for transfers between devices, shift(): return lax.ppermute(value, axis, [(i, (i + step) % n) for i in range(n)])  17.3 us
    dot_general x2, matrix products, forward(): return jnp.dot(tokens, weight, preferred_element_type=F32)  14 us
    convert_element_type x7, other arithmetic, pack(): return (value * SEND_SCALE).astype(jnp.float16)  11.6 us
  transfers between devices with their start and end apart: 29, of which 12 were waited for; matrix products, arithmetic and copies ran while one was open for 23% of the time, Pallas kernels for 9%

profile of v6, /device:TPU:0, one launch (start us, length us, event | category | flops | bytes accessed | tf_op | source)
XLA Modules:
  0.0 268.2 jit_solution(5754700314151280432)
XLA Ops:
  7.2 2.2 copy.56
  9.4 2.0 copy.57
  12.6 1.5 collective-permute-start.2
  15.5 1.5 collective-permute-start
  18.4 1.5 fusion.20
  20.6 10.8 %collective-permute-done.1.refs_0_ = bf16[256,1280]{1,0:T(8,128)(2,1)} collective-permute-done((bf16[256,1280]{1,0:T(8,128)(2,1)}, bf16[256,1280]{1,0:T(8,128)(2,1)}, u32[]{:S(2)}, u32[]{:S(2)}) %collective-permute-start.1) | collective-permute-done | bytes 655392 | tf_op jit(solution)/shard_map/ppermute | solution.py:76
  33.5 8.4 %fusion.44.refs_1_ = f32[256,4096]{1,0:T(8,128)} fusion(bf16[256,1280]{1,0:T(8,128)(2,1)S(1)} %broadcast_select_fusion.3.refs_0_, bf16[1280,4096]{1,0:T(8,128)(2,1)} %refs_0_.5), kind=kOutput, calls=%fused_computation.117 | convolution fusion | flops 2684354560 | bytes 15335424 | tf_op jit(solution)/shard_map/dot_general | solution.py:143
  41.9 2.8 %multiply_convert_fusion.6 = f16[256,2048]{1,0:T(8,128)(2,1)} fusion(f32[256,4096]{1,0:T(8,128)} %fusion.44.refs_1_, s32[]{:T(128)S(6)} %select_n.79), kind=kLoop, calls=%fused_computation.14 | loop fusion | flops 1048576 | bytes 3145732 | tf_op jit(solution)/shard_map/convert_element_type | solution.py:21
  44.7 5.6 %fusion.45 = f32[256,4096]{1,0:T(8,128)S(1)} fusion(bf16[256,1280]{1,0:T(8,128)(2,1)S(1)} %copy-done.14, bf16[1280,4096]{1,0:T(8,128)(2,1)} %refs_0_.7), kind=kOutput, calls=%fused_computation.118 | convolution fusion | flops 2684354560 | bytes 15335424 | tf_op jit(solution)/shard_map/dot_general | solution.py:143
  50.4 2.0 copy-done.11
  54.1 25.2 %collective-permute-done.3.refs_0_ = bf16[256,1280]{1,0:T(8,128)(2,1)} collective-permute-done((bf16[256,1280]{1,0:T(8,128)(2,1)}, bf16[256,1280]{1,0:T(8,128)(2,1)}, u32[]{:S(2)}, u32[]{:S(2)}) %collective-permute-start.3) | collective-permute-done | bytes 655392 | tf_op jit(solution)/shard_map/ppermute | solution.py:76
  80.5 10.2 %collective-permute-start.4 = (bf16[256,1280]{1,0:T(8,128)(2,1)S(1)}, bf16[256,1280]{1,0:T(8,128)(2,1)}, u32[]{:S(2)}, u32[]{:S(2)}) collective-permute-start(bf16[256,1280]{1,0:T(8,128)(2,1)S(1)} %broadcast_select_fusion), channel_id=1, source_target_pairs={{0,2},{2,0},{1,3},{3,1},{4,6},{6,4},{5,7},{7,5},{8,10},{10,8},{9,1... | collective-permute-start | bytes 1966088 | tf_op jit(solution)/shard_map/ppermute | solution.py:17
  90.7 2.2 add_bitcast_fusion.1
  92.9 1.6 add_bitcast_fusion
  94.6 3.4 %pad_maximum_fusion = (f32[2,256,2048]{2,1,0:T(8,128)}, f16[2,256,2048]{2,1,0:T(8,128)(2,1)}) fusion(f32[1,256,2048]{2,1,0:T(8,128)S(1)} %add_bitcast_fusion, f32[1,256,2048]{2,1,0:T(8,128)S(1)} %add_bitcast_fusion.1), kind=kLoop, calls=%fused_computation | loop fusion | flops 3145728 | bytes 10485760 | tf_op jit(solution)/shard_map/stack | solution.py:180
  98.0 7.7 %collective-permute-done.4.refs_0_ = bf16[256,1280]{1,0:T(8,128)(2,1)} collective-permute-done((bf16[256,1280]{1,0:T(8,128)(2,1)S(1)}, bf16[256,1280]{1,0:T(8,128)(2,1)}, u32[]{:S(2)}, u32[]{:S(2)}) %collective-permute-start.4) | collective-permute-done | bytes 655392 | tf_op jit(solution)/shard_map/ppermute | solution.py:17
  105.7 4.0 %copy-done.2 = bf16[4096,1280]{1,0:T(8,128)(2,1)S(1)} copy-done((bf16[4096,1280]{1,0:T(8,128)(2,1)S(1)}, bf16[4096,1280]{1,0:T(8,128)(2,1)}, u32[]{:S(2)}) %copy-start.2) | copy-done | bytes 10485784
  109.7 5.7 %shard_map.118 = f32[256,4096]{1,0:T(8,128)S(1)} custom-call(bf16[256,1280]{1,0:T(8,128)(2,1)} %shard_map.117.tokens_ref, bf16[4096,1280]{1,0:T(8,128)(2,1)S(1)} %copy-done.2), custom_call_target="tpu_custom_call" | custom-call | flops 1 | bytes 1 | tf_op jit(solution)/shard_map/pallas_call | solution.py:108
  115.4 2.0 copy-done.5
  118.6 1.7 collective-permute-start.14
  121.6 3.7 %multiply_add_fusion.3.refs_1_ = f32[256,2048]{1,0:T(8,128)} fusion(f16[256,2048]{1,0:T(8,128)(2,1)} %collective-permute-done.7, f32[256,4096]{1,0:T(8,128)} %copy-done.5, s32[]{:T(128)S(6)} %select_n.72), kind=kLoop, calls=%fused_computation.9 | loop fusion | flops 1572864 | bytes 5242884 | tf_op jit(solution)/shard_map/add | solution.py:150
  125.3 6.9 %collective-permute-start.9 = (bf16[256,1280]{1,0:T(8,128)(2,1)}, bf16[256,1280]{1,0:T(8,128)(2,1)}, u32[]{:S(2)}, u32[]{:S(2)}) collective-permute-start(bf16[256,1280]{1,0:T(8,128)(2,1)} %shard_map.119), channel_id=1, source_target_pairs={{0,8},{1,12},{4,9},{5,13},{10,2},{11,6},{14,3},{15,7},{16,24},{17,... | collective-permute-start | bytes 1966088 | tf_op jit(solution)/shard_map/ppermute | solution.py:76
  132.2 6.6 %collective-permute-start.8 = (bf16[256,1280]{1,0:T(8,128)(2,1)}, bf16[256,1280]{1,0:T(8,128)(2,1)}, u32[]{:S(2)}, u32[]{:S(2)}) collective-permute-start(bf16[256,1280]{1,0:T(8,128)(2,1)} %shard_map.119), channel_id=1, source_target_pairs={{0,0},{1,4},{4,1},{5,5},{10,10},{11,14},{14,11},{15,15},{16,16},{1... | collective-permute-start | bytes 1966088 | tf_op jit(solution)/shard_map/ppermute | solution.py:76
  138.8 2.7 %fusion.8 = (f16[128,2048]{1,0:T(8,128)(2,1)}, f16[128,2048]{1,0:T(8,128)(2,1)}) fusion(f32[256,2048]{1,0:T(8,128)} %multiply_add_fusion.3.refs_1_), kind=kLoop, calls=%fused_computation.34 | loop fusion | flops 1048576 | bytes 3145728 | tf_op jit(solution)/shard_map/convert_element_type | solution.py:21
  141.5 8.8 %collective-permute-done.9 = bf16[256,1280]{1,0:T(8,128)(2,1)} collective-permute-done((bf16[256,1280]{1,0:T(8,128)(2,1)}, bf16[256,1280]{1,0:T(8,128)(2,1)}, u32[]{:S(2)}, u32[]{:S(2)}) %collective-permute-start.9) | collective-permute-done | bytes 655392 | tf_op jit(solution)/shard_map/ppermute | solution.py:76
  150.3 2.0 broadcast_select_fusion.2.refs_1_.tokens_ref.refs_0_
  152.3 14.8 %collective-permute-start.13 = (f16[128,2048]{1,0:T(8,128)(2,1)}, f16[128,2048]{1,0:T(8,128)(2,1)}, u32[]{:S(2)}, u32[]{:S(2)}) collective-permute-start(f16[128,2048]{1,0:T(8,128)(2,1)} %get-tuple-element.17), channel_id=1, source_target_pairs={{0,2},{2,0},{1,3},{3,1},{4,6},{6,4},{5,7},{7,5},{8,10},{10,8},{9,1... | collective-permute-start | bytes 1572872 | tf_op jit(solution)/shard_map/ppermute | solution.py:17
  167.1 2.3 collective-permute-start.11
  169.5 6.6 %collective-permute-start.10 = (bf16[256,1280]{1,0:T(8,128)(2,1)}, bf16[256,1280]{1,0:T(8,128)(2,1)}, u32[]{:S(2)}, u32[]{:S(2)}) collective-permute-start(bf16[256,1280]{1,0:T(8,128)(2,1)} %shard_map.120), channel_id=1, source_target_pairs={{0,0},{1,4},{4,1},{5,5},{10,10},{11,14},{14,11},{15,15},{16,16},{1... | collective-permute-start | bytes 1966088 | tf_op jit(solution)/shard_map/ppermute | solution.py:76
  177.1 8.3 %shard_map.121.refs_1_ = f32[256,4096]{1,0:T(8,128)S(1)} custom-call(bf16[256,1280]{1,0:T(8,128)(2,1)S(1)} %copy-done.8, bf16[1280,4096]{1,0:T(8,128)(2,1)} %refs_0_.5), custom_call_target="tpu_custom_call" | custom-call | flops 1 | bytes 1 | tf_op jit(solution)/shard_map/pallas_call | solution.py:108
  185.4 5.6 %convert_multiply_fusion.refs_1_ = f32[2,256,2048]{2,1,0:T(8,128)} fusion(f16[2,256,2048]{2,1,0:T(8,128)(2,1)} %collective-permute-done.14), kind=kLoop, calls=%fused_computation.1 | loop fusion | flops 2097152 | bytes 6291456 | tf_op jit(solution)/shard_map/mul | solution.py:25
  193.3 8.3 %shard_map.126 = f32[256,4096]{1,0:T(8,128)S(1)} custom-call(bf16[256,1280]{1,0:T(8,128)(2,1)S(1)} %copy-done.9, bf16[1280,4096]{1,0:T(8,128)(2,1)} %refs_0_.7), custom_call_target="tpu_custom_call" | custom-call | flops 1 | bytes 1 | tf_op jit(solution)/shard_map/pallas_call | solution.py:108
  201.7 2.0 copy-done.6
  206.6 8.4 %shard_map.124.refs_1_ = f32[256,4096]{1,0:T(8,128)S(1)} custom-call(bf16[256,1280]{1,0:T(8,128)(2,1)S(1)} %broadcast_select_fusion.1.tokens_ref, bf16[4096,1280]{1,0:T(8,128)(2,1)} %refs_0_.6), custom_call_target="tpu_custom_call" | custom-call | flops 1 | bytes 1 | tf_op jit(solution)/shard_map/pallas_call | solution.py:108
  215.1 1.9 copy-done.3
  219.5 2.4 multiply_add_fusion
  222.6 2.0 multiply_add_fusion.1
  224.6 1.5 add_multiply_fusion
  226.8 1.4 copy-done.4
  230.1 1.4 fusion.15
  233.7 1.4 fusion.17
  235.8 3.6 %collective-permute-start.20 = (f32[6,16,64]{2,1,0:T(8,128)S(1)}, f32[6,16,64]{2,1,0:T(8,128)}, u32[]{:S(2)}, u32[]{:S(2)}) collective-permute-start(f32[6,16,64]{2,1,0:T(8,128)S(1)} %get-tuple-element.19), channel_id=1, source_target_pairs={{0,12},{4,0},{8,4},{12,8},{1,13},{5,1},{9,5},{13,9},{2,14},{6,2},{... | collective-permute-start | bytes 73736 | tf_op jit(solution)/shard_map/ppermute | solution.py:17
  239.5 1.6 collective-permute-start.27
  242.0 2.8 %collective-permute-done.19 = f32[6,16,64]{2,1,0:T(8,128)} collective-permute-done((f32[6,16,64]{2,1,0:T(8,128)S(1)}, f32[6,16,64]{2,1,0:T(8,128)}, u32[]{:S(2)}, u32[]{:S(2)}) %collective-permute-start.19) | collective-permute-done | bytes 24608 | tf_op jit(solution)/shard_map/ppermute | solution.py:17
  246.2 1.7 collective-permute-start.21
  249.3 1.6 collective-permute-done.21
  252.3 1.9 collective-permute-start.24
  256.0 3.0 %collective-permute-done.25 = f32[4,512]{1,0:T(4,128)S(1)} collective-permute-done((f32[4,512]{1,0:T(4,128)S(1)}, f32[4,512]{1,0:T(4,128)S(1)}, u32[]{:S(2)}, u32[]{:S(2)}) %collective-permute-start.25) | collective-permute-done | bytes 8224 | tf_op jit(solution)/shard_map/ppermute | solution.py:17
  (127 shorter events, 36.3 us)
Async XLA Ops:
  7.2 243.9 %copy-start = (bf16[3,16,64,512]{3,2,1,0:T(8,128)(2,1)S(1)}, bf16[3,16,64,512]{3,2,1,0:T(8,128)(2,1)}, u32[]{:S(2)}) copy-start(bf16[3,16,64,512]{3,2,1,0:T(8,128)(2,1)} %param.17) | copy-start | bytes 9437188
  7.2 211.0 %all-reduce.2.cloned.1.call-start = ((), (), s32[]{:S(2)}) async-start(), calls=%async_computation | async-start | bytes 524288 | tf_op jit(solution)/shard_map/psum | solution.py:189
  11.4 20.1 %collective-permute-start.1 = (bf16[256,1280]{1,0:T(8,128)(2,1)}, bf16[256,1280]{1,0:T(8,128)(2,1)}, u32[]{:S(2)}, u32[]{:S(2)}) collective-permute-start(bf16[256,1280]{1,0:T(8,128)(2,1)} %bitcast.1.refs_0_), channel_id=1, source_target_pairs={{2,0},{3,4},{6,1},{7,5},{8,10},{9,14},{12,11},{13,15},{18,16},{19,... | collective-permute-start | bytes 1966088 | tf_op jit(solution)/shard_map/ppermute | solution.py:76
  12.6 18.8 %collective-permute-start.2 = (bf16[256,1280]{1,0:T(8,128)(2,1)}, bf16[256,1280]{1,0:T(8,128)(2,1)}, u32[]{:S(2)}, u32[]{:S(2)}) collective-permute-start(bf16[256,1280]{1,0:T(8,128)(2,1)} %bitcast.1.refs_0_), channel_id=1, source_target_pairs={{2,8},{3,12},{6,9},{7,13},{8,2},{9,6},{12,3},{13,7},{18,24},{19,28... | collective-permute-start | bytes 1966088 | tf_op jit(solution)/shard_map/ppermute | solution.py:76
  14.2 65.2 %collective-permute-start.3 = (bf16[256,1280]{1,0:T(8,128)(2,1)}, bf16[256,1280]{1,0:T(8,128)(2,1)}, u32[]{:S(2)}, u32[]{:S(2)}) collective-permute-start(bf16[256,1280]{1,0:T(8,128)(2,1)} %bitcast.refs_0_), channel_id=1, source_target_pairs={{2,10},{3,14},{6,11},{7,15},{8,0},{9,4},{12,1},{13,5},{18,26},{19,... | collective-permute-start | bytes 1966088 | tf_op jit(solution)/shard_map/ppermute | solution.py:76
  15.5 63.9 %collective-permute-start = (bf16[256,1280]{1,0:T(8,128)(2,1)}, bf16[256,1280]{1,0:T(8,128)(2,1)}, u32[]{:S(2)}, u32[]{:S(2)}) collective-permute-start(bf16[256,1280]{1,0:T(8,128)(2,1)} %bitcast.refs_0_), channel_id=1, source_target_pairs={{2,2},{3,6},{6,3},{7,7},{8,8},{9,12},{12,9},{13,13},{18,18},{19,22... | collective-permute-start | bytes 1966088 | tf_op jit(solution)/shard_map/ppermute | solution.py:76
  32.6 0.9 copy-start.13
  41.9 2.9 %copy-start.14 = (bf16[256,1280]{1,0:T(8,128)(2,1)S(1)}, bf16[256,1280]{1,0:T(8,128)(2,1)}, u32[]{:S(2)}) copy-start(bf16[256,1280]{1,0:T(8,128)(2,1)} %shard_map.116) | copy-start | bytes 1966084
  44.7 45.9 %collective-permute-start.5 = (f16[256,2048]{1,0:T(8,128)(2,1)}, f16[256,2048]{1,0:T(8,128)(2,1)}, u32[]{:S(2)}, u32[]{:S(2)}) collective-permute-start(f16[256,2048]{1,0:T(8,128)(2,1)} %multiply_convert_fusion.6), channel_id=1, source_target_pairs={{0,1},{1,0},{2,3},{3,2},{4,5},{5,4},{6,7},{7,6},{8,9},{9,8},{10,11... | collective-permute-start | bytes 3145736 | tf_op jit(solution)/shard_map/ppermute | solution.py:17
  50.3 2.0 copy-start.11
  53.6 39.3 %collective-permute-start.6 = (f16[256,2048]{1,0:T(8,128)(2,1)}, f16[256,2048]{1,0:T(8,128)(2,1)}, u32[]{:S(2)}, u32[]{:S(2)}) collective-permute-start(f16[256,2048]{1,0:T(8,128)(2,1)} %multiply_convert_fusion.5), channel_id=1, source_target_pairs={{0,1},{1,0},{2,3},{3,2},{4,5},{5,4},{6,7},{7,6},{8,9},{9,8},{10,11... | collective-permute-start | bytes 3145736 | tf_op jit(solution)/shard_map/ppermute | solution.py:17
  80.5 12.4 %copy-start.12 = (f32[256,4096]{1,0:T(8,128)S(1)}, f32[256,4096]{1,0:T(8,128)}, u32[]{:S(2)}) copy-start(f32[256,4096]{1,0:T(8,128)} %copy-done.11) | copy-start | bytes 12582916
  80.5 25.2 %collective-permute-start.4 = (bf16[256,1280]{1,0:T(8,128)(2,1)S(1)}, bf16[256,1280]{1,0:T(8,128)(2,1)}, u32[]{:S(2)}, u32[]{:S(2)}) collective-permute-start(bf16[256,1280]{1,0:T(8,128)(2,1)S(1)} %broadcast_select_fusion), channel_id=1, source_target_pairs={{0,2},{2,0},{1,3},{3,1},{4,6},{6,4},{5,7},{7,5},{8,10},{10,8},{9,1... | collective-permute-start | bytes 1966088 | tf_op jit(solution)/shard_map/ppermute | solution.py:17
  105.7 4.0 %copy-start.2 = (bf16[4096,1280]{1,0:T(8,128)(2,1)S(1)}, bf16[4096,1280]{1,0:T(8,128)(2,1)}, u32[]{:S(2)}) copy-start(bf16[4096,1280]{1,0:T(8,128)(2,1)} %refs_0_.6) | copy-start | bytes 31457284
  115.4 2.0 copy-start.5
  118.6 3.0 %collective-permute-start.7 = (f16[256,2048]{1,0:T(8,128)(2,1)}, f16[256,2048]{1,0:T(8,128)(2,1)}, u32[]{:S(2)}, u32[]{:S(2)}) collective-permute-start(f16[256,2048]{1,0:T(8,128)(2,1)} %multiply_convert_fusion.4), channel_id=1, source_target_pairs={{0,1},{1,0},{2,3},{3,2},{4,5},{5,4},{6,7},{7,6},{8,9},{9,8},{10,11... | collective-permute-start | bytes 3145736 | tf_op jit(solution)/shard_map/ppermute | solution.py:17
  118.6 66.8 %collective-permute-start.14 = (f16[2,256,2048]{2,1,0:T(8,128)(2,1)}, f16[2,256,2048]{2,1,0:T(8,128)(2,1)}, u32[]{:S(2)}, u32[]{:S(2)}) collective-permute-start(f16[2,256,2048]{2,1,0:T(8,128)(2,1)} %get-tuple-element.15), channel_id=1, source_target_pairs={{0,2},{2,0},{1,3},{3,1},{4,6},{6,4},{5,7},{7,5},{8,10},{10,8},{9,1... | collective-permute-start | bytes 6291464 | tf_op jit(solution)/shard_map/ppermute | solution.py:17
  125.3 13.4 %copy-start.17 = (s32[2]{0:T(128)S(1)}, s32[2]{0:T(128)}, u32[]{:S(2)}) copy-start(s32[2]{0:T(128)} %param.18) | copy-start | bytes 28
  125.3 25.1 %collective-permute-start.9 = (bf16[256,1280]{1,0:T(8,128)(2,1)}, bf16[256,1280]{1,0:T(8,128)(2,1)}, u32[]{:S(2)}, u32[]{:S(2)}) collective-permute-start(bf16[256,1280]{1,0:T(8,128)(2,1)} %shard_map.119), channel_id=1, source_target_pairs={{0,8},{1,12},{4,9},{5,13},{10,2},{11,6},{14,3},{15,7},{16,24},{17,... | collective-permute-start | bytes 1966088 | tf_op jit(solution)/shard_map/ppermute | solution.py:76
  132.2 18.2 %collective-permute-start.8 = (bf16[256,1280]{1,0:T(8,128)(2,1)}, bf16[256,1280]{1,0:T(8,128)(2,1)}, u32[]{:S(2)}, u32[]{:S(2)}) collective-permute-start(bf16[256,1280]{1,0:T(8,128)(2,1)} %shard_map.119), channel_id=1, source_target_pairs={{0,0},{1,4},{4,1},{5,5},{10,10},{11,14},{14,11},{15,15},{16,16},{1... | collective-permute-start | bytes 1966088 | tf_op jit(solution)/shard_map/ppermute | solution.py:76
  141.5 90.6 %collective-permute-start.17 = (f16[128,2048]{1,0:T(8,128)(2,1)}, f16[128,2048]{1,0:T(8,128)(2,1)}, u32[]{:S(2)}, u32[]{:S(2)}) collective-permute-start(f16[128,2048]{1,0:T(8,128)(2,1)} %get-tuple-element.16), channel_id=1, source_target_pairs={{0,2},{2,0},{1,3},{3,1},{4,6},{6,4},{5,7},{7,5},{8,10},{10,8},{9,1... | collective-permute-start | bytes 1572872 | tf_op jit(solution)/shard_map/ppermute | solution.py:17
  152.3 76.3 %collective-permute-start.13 = (f16[128,2048]{1,0:T(8,128)(2,1)}, f16[128,2048]{1,0:T(8,128)(2,1)}, u32[]{:S(2)}, u32[]{:S(2)}) collective-permute-start(f16[128,2048]{1,0:T(8,128)(2,1)} %get-tuple-element.17), channel_id=1, source_target_pairs={{0,2},{2,0},{1,3},{3,1},{4,6},{6,4},{5,7},{7,5},{8,10},{10,8},{9,1... | collective-permute-start | bytes 1572872 | tf_op jit(solution)/shard_map/ppermute | solution.py:17
  167.1 37.7 %collective-permute-start.11 = (bf16[256,1280]{1,0:T(8,128)(2,1)}, bf16[256,1280]{1,0:T(8,128)(2,1)}, u32[]{:S(2)}, u32[]{:S(2)}) collective-permute-start(bf16[256,1280]{1,0:T(8,128)(2,1)} %shard_map.120), channel_id=1, source_target_pairs={{0,8},{1,12},{4,9},{5,13},{10,2},{11,6},{14,3},{15,7},{16,24},{17,... | collective-permute-start | bytes 1966088 | tf_op jit(solution)/shard_map/ppermute | solution.py:76
  169.5 35.4 %collective-permute-start.10 = (bf16[256,1280]{1,0:T(8,128)(2,1)}, bf16[256,1280]{1,0:T(8,128)(2,1)}, u32[]{:S(2)}, u32[]{:S(2)}) collective-permute-start(bf16[256,1280]{1,0:T(8,128)(2,1)} %shard_map.120), channel_id=1, source_target_pairs={{0,0},{1,4},{4,1},{5,5},{10,10},{11,14},{14,11},{15,15},{16,16},{1... | collective-permute-start | bytes 1966088 | tf_op jit(solution)/shard_map/ppermute | solution.py:76
  176.0 1.1 copy-start.8
  185.4 5.6 %copy-start.1 = (f32[256,4096]{1,0:T(8,128)}, f32[256,4096]{1,0:T(8,128)S(1)}, u32[]{:S(2)}) copy-start(f32[256,4096]{1,0:T(8,128)S(1)} %shard_map.121.refs_1_) | copy-start | bytes 12582916
  192.2 27.2 %collective-permute-start.16 = (f16[256,2048]{1,0:T(8,128)(2,1)}, f16[256,2048]{1,0:T(8,128)(2,1)}, u32[]{:S(2)}, u32[]{:S(2)}) collective-permute-start(f16[256,2048]{1,0:T(8,128)(2,1)} %multiply_convert_fusion.1), channel_id=1, source_target_pairs={{0,1},{1,0},{2,3},{3,2},{4,5},{5,4},{6,7},{7,6},{8,9},{9,8},{10,11... | collective-permute-start | bytes 3145736 | tf_op jit(solution)/shard_map/ppermute | solution.py:17
  192.3 1.1 copy-start.9
  201.6 2.1 copy-start.6
  206.1 15.8 %collective-permute-start.15 = (f16[256,2048]{1,0:T(8,128)(2,1)}, f16[256,2048]{1,0:T(8,128)(2,1)}, u32[]{:S(2)}, u32[]{:S(2)}) collective-permute-start(f16[256,2048]{1,0:T(8,128)(2,1)} %multiply_convert_fusion.2), channel_id=1, source_target_pairs={{0,1},{1,0},{2,3},{3,2},{4,5},{5,4},{6,7},{7,6},{8,9},{9,8},{10,11... | collective-permute-start | bytes 3145736 | tf_op jit(solution)/shard_map/ppermute | solution.py:17
  215.1 1.9 copy-start.3
  219.3 7.5 %collective-permute-start.12 = (f16[256,2048]{1,0:T(8,128)(2,1)}, f16[256,2048]{1,0:T(8,128)(2,1)S(1)}, u32[]{:S(2)}, u32[]{:S(2)}) collective-permute-start(f16[256,2048]{1,0:T(8,128)(2,1)} %multiply_convert_fusion.3), channel_id=1, source_target_pairs={{0,1},{1,0},{2,3},{3,2},{4,5},{5,4},{6,7},{7,6},{8,9},{9,8},{10,11... | collective-permute-start | bytes 3145736 | tf_op jit(solution)/shard_map/ppermute | solution.py:17
  219.4 3.1 %copy-start.7 = (f32[256,4096]{1,0:T(8,128)S(1)}, f32[256,4096]{1,0:T(8,128)}, u32[]{:S(2)}) copy-start(f32[256,4096]{1,0:T(8,128)} %copy-done.6) | copy-start | bytes 12582916
  221.8 2.7 %copy-start.10 = (f32[2,256,2048]{2,1,0:T(8,128)S(1)}, f32[2,256,2048]{2,1,0:T(8,128)}, u32[]{:S(2)}) copy-start(f32[2,256,2048]{2,1,0:T(8,128)} %convert_multiply_fusion.refs_1_) | copy-start | bytes 12582916
  224.5 1.5 copy-start.15
  226.0 2.2 copy-start.4
  233.5 5.9 %copy-start.16 = (s32[2]{0:T(128)S(1)}, s32[2]{0:T(128)}, u32[]{:S(2)}) copy-start(s32[2]{0:T(128)} %param.19) | copy-start | bytes 28
  235.6 6.4 %collective-permute-start.18 = (f32[6,16,64]{2,1,0:T(8,128)S(1)}, f32[6,16,64]{2,1,0:T(8,128)S(1)}, u32[]{:S(2)}, u32[]{:S(2)}) collective-permute-start(f32[6,16,64]{2,1,0:T(8,128)S(1)} %get-tuple-element.18), channel_id=1, source_target_pairs={{0,4},{4,8},{8,12},{12,0},{1,5},{5,9},{9,13},{13,1},{2,6},{6,10},{... | collective-permute-start | bytes 73736 | tf_op jit(solution)/shard_map/ppermute | solution.py:17
  235.8 6.2 %collective-permute-start.20 = (f32[6,16,64]{2,1,0:T(8,128)S(1)}, f32[6,16,64]{2,1,0:T(8,128)}, u32[]{:S(2)}, u32[]{:S(2)}) collective-permute-start(f32[6,16,64]{2,1,0:T(8,128)S(1)} %get-tuple-element.19), channel_id=1, source_target_pairs={{0,12},{4,0},{8,4},{12,8},{1,13},{5,1},{9,5},{13,9},{2,14},{6,2},{... | collective-permute-start | bytes 73736 | tf_op jit(solution)/shard_map/ppermute | solution.py:17
  239.5 5.3 %collective-permute-start.19 = (f32[6,16,64]{2,1,0:T(8,128)S(1)}, f32[6,16,64]{2,1,0:T(8,128)}, u32[]{:S(2)}, u32[]{:S(2)}) collective-permute-start(f32[6,16,64]{2,1,0:T(8,128)S(1)} %get-tuple-element.20), channel_id=1, source_target_pairs={{0,8},{4,12},{8,0},{12,4},{1,9},{5,13},{9,1},{13,5},{2,10},{6,14},... | collective-permute-start | bytes 73736 | tf_op jit(solution)/shard_map/ppermute | solution.py:17
  239.5 6.2 %collective-permute-start.27 = (s32[2]{0:T(128)S(1)}, s32[2]{0:T(128)S(1)}, u32[]{:S(2)}, u32[]{:S(2)}) collective-permute-start(s32[2]{0:T(128)S(1)} %copy-done.16), channel_id=1, source_target_pairs={{0,2},{2,0},{1,3},{3,1},{4,6},{6,4},{5,7},{7,5},{8,10},{10,8},{9,1... | collective-permute-start | bytes 32 | tf_op jit(solution)/shard_map/ppermute | solution.py:17
  245.6 2.3 collective-permute-start.23
  245.7 3.6 %collective-permute-start.22 = (f32[6,16,64]{2,1,0:T(8,128)S(1)}, f32[6,16,64]{2,1,0:T(8,128)S(1)}, u32[]{:S(2)}, u32[]{:S(2)}) collective-permute-start(f32[6,16,64]{2,1,0:T(8,128)S(1)} %fusion.34), channel_id=1, source_target_pairs={{0,3},{1,2},{2,1},{3,0},{4,7},{5,6},{6,5},{7,4},{8,11},{9,10},{10,... | collective-permute-start | bytes 73736 | tf_op jit(solution)/shard_map/ppermute | solution.py:256
  246.2 4.7 %collective-permute-start.21 = (f32[6,16,64]{2,1,0:T(8,128)S(1)}, f32[6,16,64]{2,1,0:T(8,128)S(1)}, u32[]{:S(2)}, u32[]{:S(2)}) collective-permute-start(f32[6,16,64]{2,1,0:T(8,128)S(1)} %fusion.34), channel_id=1, source_target_pairs={{0,2},{1,3},{2,0},{3,1},{4,6},{5,7},{6,4},{7,5},{8,10},{9,11},{10,... | collective-permute-start | bytes 73736 | tf_op jit(solution)/shard_map/ppermute | solution.py:256
  252.3 3.7 %collective-permute-start.24 = (f32[4,512]{1,0:T(4,128)S(1)}, f32[4,512]{1,0:T(4,128)S(1)}, u32[]{:S(2)}, u32[]{:S(2)}) collective-permute-start(f32[4,512]{1,0:T(4,128)S(1)} %fusion.46), channel_id=1, source_target_pairs={{0,12},{4,0},{8,4},{12,8},{1,13},{5,1},{9,5},{13,9},{2,14},{6,2},{... | collective-permute-start | bytes 24584 | tf_op jit(solution)/shard_map/ppermute | solution.py:17
  254.4 5.4 %collective-permute-start.26 = (f32[4,512]{1,0:T(4,128)S(1)}, f32[4,512]{1,0:T(4,128)S(1)}, u32[]{:S(2)}, u32[]{:S(2)}) collective-permute-start(f32[4,512]{1,0:T(4,128)S(1)} %fusion.46), channel_id=1, source_target_pairs={{0,4},{4,8},{8,12},{12,0},{1,5},{5,9},{9,13},{13,1},{2,6},{6,10},{... | collective-permute-start | bytes 24584 | tf_op jit(solution)/shard_map/ppermute | solution.py:17
  254.5 4.5 %collective-permute-start.25 = (f32[4,512]{1,0:T(4,128)S(1)}, f32[4,512]{1,0:T(4,128)S(1)}, u32[]{:S(2)}, u32[]{:S(2)}) collective-permute-start(f32[4,512]{1,0:T(4,128)S(1)} %fusion.46), channel_id=1, source_target_pairs={{0,8},{4,12},{8,0},{12,4},{1,9},{5,13},{9,1},{13,5},{2,10},{6,14},... | collective-permute-start | bytes 24584 | tf_op jit(solution)/shard_map/ppermute | solution.py:17
Sparse Core Ops, SparseCore 0:
  138.9 36.4 all-reduce.1

commit v7 on v6

--- a/solution.py
+++ b/solution.py
@@ -1,5 +1,3 @@
-import functools
-
 import jax
 import jax.numpy as jnp
 from jax import lax
@@ -51,18 +49,10 @@
 
 
 def after(value, *earlier):
-    anywhere = pl.BlockSpec(memory_space=pl.ANY)
-    return pl.pallas_call(
-        lambda *refs: None,
-        out_shape=jax.ShapeDtypeStruct(value.shape, value.dtype),
-        in_specs=[anywhere] * (1 + len(earlier)),
-        out_specs=anywhere,
-        input_output_aliases={0: 0},
-        cost_estimate=pl.CostEstimate(flops=1, bytes_accessed=1, transcendentals=0),
-    )(value, *earlier)
-
-
-def spread_features(starts, far, cross):
+    return lax.optimization_barrier((value,) + earlier)[0]
+
+
+def spread_features(flat, far, *earlier):
     pieces = []
     for turn in range(2):
         pairs = []
@@ -71,15 +61,12 @@
             for source_core in range(2):
                 target = block ^ (2 * turn + (source_core ^ core))
                 source = block * 4 + (example ^ far) * 2 + source_core
-                landing = example if cross else example ^ far
-                pairs.append((source, target * 4 + landing * 2 + core))
-        pieces.append(lax.ppermute(starts[turn], ("tensor", "example", "test"), pairs))
-    return pieces
-
-
-def piece_index(across):
-    example = lax.axis_index("example") ^ across
-    return (lax.axis_index("tensor") ^ (example * 2 + lax.axis_index("test"))) // 2
+                pairs.append((source, target * 4 + example * 2 + core))
+        pieces.append(lax.ppermute(flat, ("tensor", "example", "test"), pairs))
+    if earlier:
+        pieces = lax.optimization_barrier((*pieces, *earlier))
+    holder = lax.axis_index("example") * 2 + lax.axis_index("test")
+    return jnp.where((lax.axis_index("tensor") ^ holder) < 2, pieces[0], pieces[1])
 
 
 def gathered_features(flat, n_ex, n_cores):
@@ -92,29 +79,28 @@
     return [lax.dynamic_slice_in_dim(whole, owner * rows, rows, 0) for owner in owners]
 
 
-def products_kernel(by_rows, tokens_ref, *refs):
-    contract = (((1,), (1 if by_rows else 0,)), ((), ()))
-    for weight_ref, out_ref in zip(refs, refs[len(refs) // 2 :]):
-        out_ref[...] = lax.dot_general(
-            tokens_ref[...], weight_ref[...], contract, preferred_element_type=F32
-        )
-
-
-def products(tokens, weights, by_rows, vmem_mib):
+def dot_rows_kernel(tokens_ref, weight_ref, out_ref):
+    out_ref[...] = lax.dot_general(
+        tokens_ref[...], weight_ref[...], (((1,), (1,)), ((), ())), preferred_element_type=F32
+    )
+
+
+def dot_rows(tokens, weight):
     rows, depth = tokens.shape
-    hidden = weights[0].shape[0 if by_rows else 1]
+    hidden = weight.shape[0]
     tile = min(512, hidden)
-    block = ((tile, depth), lambda i: (i, 0)) if by_rows else ((depth, tile), lambda i: (0, i))
     return pl.pallas_call(
-        functools.partial(products_kernel, by_rows),
-        out_shape=[jax.ShapeDtypeStruct((rows, hidden), F32)] * len(weights),
+        dot_rows_kernel,
+        out_shape=jax.ShapeDtypeStruct((rows, hidden), F32),
         grid=(hidden // tile,),
-        in_specs=[pl.BlockSpec((rows, depth), lambda i: (0, 0))]
-        + [pl.BlockSpec(*block)] * len(weights),
-        out_specs=[pl.BlockSpec((rows, tile), lambda i: (0, i))] * len(weights),
-        compiler_params=pltpu.CompilerParams(vmem_limit_bytes=vmem_mib * 2**20),
+        in_specs=[
+            pl.BlockSpec((rows, depth), lambda i: (0, 0)),
+            pl.BlockSpec((tile, depth), lambda i: (i, 0)),
+        ],
+        out_specs=pl.BlockSpec((rows, tile), lambda i: (0, i)),
+        compiler_params=pltpu.CompilerParams(vmem_limit_bytes=16 * 2**20),
         cost_estimate=pl.CostEstimate(flops=1, bytes_accessed=1, transcendentals=0),
-    )(tokens, *weights)
+    )(tokens, weight)
 
 
 def on_device(
@@ -164,49 +150,41 @@
     examples = [slice(e * seq_len, (e + 1) * seq_len) for e in range(ex_loc)]
     arrived = [[[] for _ in range(ex_loc)] for _ in range(3)]
     if direct:
-        acts_far = spread_features([flat_acts] * 2, 1, True)
-        acts_far = [jnp.where(piece_index(0) == 0, after(acts_far[0], model_part), acts_far[1])]
-        grad_across = spread_features([flat_grad] * 2, 1, False)
+        acts_far = [spread_features(flat_acts, 1)]
     else:
-        acts_here = gathered_features(flat_acts, n_ex, n_cores)
-        grad_here = gathered_features(flat_grad, n_ex, n_cores)
-        acts_far, grad_far = acts_here[1:], grad_here[1:]
+        acts_near, *acts_far = gathered_features(flat_acts, n_ex, n_cores)
+        grad_near, *grad_far = gathered_features(flat_grad, n_ex, n_cores)
     for step in range(1, n_ex):
         gate_far = forward(acts_far[step - 1], w_gate)
         up_far = forward(after(acts_far[step - 1], gate_far), w_up)
-        if direct:
-            grad_across = [after(piece, gate_far) for piece in grad_across]
-            grad_far = [shift(jnp.where(piece_index(1) == 0, *grad_across), "example", 1)]
-        both = jnp.stack([core_sum(gate_far), core_sum(up_far)])
-        received = unpack(shift(pack(both), "example", step))
+        both = pack(jnp.stack([core_sum(gate_far), core_sum(up_far)]))
+        received = shift(both, "example", step)
         for e, rows in enumerate(examples):
             for which in range(2):
                 arrived[which][e].append(received[which, rows])
-        (down_far,) = products(after(grad_far[step - 1], both), [w_down], True, 16)
+    if direct:
+        acts_near = spread_features(flat_acts, 0, up_far)
+    gate_near = forward(after(acts_near, both), w_gate)
+    up_near = forward(after(acts_near, gate_near), w_up)
+    if direct:
+        grad_ready = after(flat_grad, acts_far[0])
+        grad_far = [spread_features(grad_ready, 1, up_near)]
+    for step in range(1, n_ex):
+        down_far = dot_rows(grad_far[step - 1], w_down)
         summed = core_sum(down_far)
         for e, rows in enumerate(examples):
-            arrived[2][e].append(unpack(shift(pack(summed[rows]), "example", step)))
-    model_sum = lax.psum(after(model_part, gate_far), "tensor")
-    if direct:
-        start = after(flat_acts, summed)
-        acts_near = spread_features([start, start], 0, False)
-        acts_near = jnp.where(piece_index(0) == 0, *acts_near)
-        start = after(flat_grad, acts_near)
-        grad_near = spread_features([start, start], 0, False)
-    else:
-        acts_near, grad_near = acts_here[0], grad_here[0]
-    (gate_near,) = products(acts_near, [w_gate], False, 48)
-    (up_near,) = products(after(acts_near, received), [w_up], False, 48)
-    if direct:
-        grad_near = [after(piece, gate_near) for piece in grad_near]
-        grad_near = jnp.where(piece_index(0) == 0, *grad_near)
-    (grad_near,) = products(grad_near, [w_down], True, 48)
+            sent = pack(summed[rows])
+            arrived[2][e].append(shift(sent, "example", step))
+    if direct:
+        grad_near = spread_features(grad_ready, 0, sent)
+    grad_near = dot_rows(grad_near, w_down)
+    model_sum = lax.psum(after(model_part, acts_far[0]), "tensor")
     model_sum = after(model_sum, grad_near)
     own = [core_sum(near) for near in (gate_near, up_near, grad_near)]
 
     def total(which, e):
         kept = own[which][e * seq_len : (e + 1) * seq_len]
-        return kept + sum(arrived[which][e])
+        return kept + sum(unpack(one) for one in arrived[which][e])
 
     hid_proj = lax.dynamic_slice_in_dim(proj_hidden, core * hid_part, hid_part, 0)
     positions = jnp.arange(seq_len, dtype=jnp.int32)

time: 271 us -> 211 us (0.78)
  Pallas kernels: 30.8 us -> 9.24 us
  waiting for transfers between devices: 65.1 us -> 46.8 us
  local copies, waits for them, and re-layouts: 23.3 us -> 9.97 us
  other arithmetic: 41.6 us -> 28.6 us
  matrix products: 26.6 us -> 32 us
    ppermute x8, waiting for transfers between devices: 44.9 us -> 11.2 us  [spread_features(): pieces.append(lax.ppermute(flat, ('tensor', 'example', 'test'), pairs))]
    pallas_call x16 -> x2, Pallas kernels: 30.8 us -> 9.24 us  [dot_rows(): pl.pallas_call(dot_rows_kernel, out_shape=jax.ShapeDtypeStruct((rows, hid...]
    ppermute x8, starting transfers between devices: 27.9 us -> 40.9 us  [spread_features(): pieces.append(lax.ppermute(flat, ('tensor', 'example', 'test'), pairs))]
    ppermute x17 -> x16, waiting for transfers between devices: 17.3 us -> 30.1 us  [shift(): return lax.ppermute(value, axis, [(i, (i + step) % n) for i in range(n)])]
    unnamed x45 -> x47, local copies, waits for them, and re-layouts: 21.4 us -> 9.14 us
    ppermute x17 -> x16, starting transfers between devices: 36.1 us -> 25.1 us  [shift(): return lax.ppermute(value, axis, [(i, (i + step) % n) for i in range(n)])]
    another operation x3 -> x2, other arithmetic: 7.3 us -> 0.78 us  [on_device(): both = pack(jnp.stack([core_sum(gate_far), core_sum(up_far)]))]
    mul x1 -> x0, other arithmetic: 5.6 us -> none  [unpack(): return value.astype(F32) * (1.0 / SEND_SCALE)]
  transfers between devices with their start and end apart: 29 -> 28, of which waited for: 12 -> 13; matrix products, arithmetic and copies ran while one was open for 23% -> 25% of each run, Pallas kernels for 9% -> 2%
where the time goes in v7:
time: 211 us; the launch traced here: 210 us
  starting transfers between devices  68.3 us (32%)
  waiting for transfers between devices  46.8 us (22%)
  matrix products  32 us (15%)
  other arithmetic  28.6 us (14%)
  between operations  14.7 us (7%)
  local copies, waits for them, and re-layouts  9.97 us (5%)
  Pallas kernels  9.24 us (4%)
    ppermute x8, starting transfers between devices, spread_features(): pieces.append(lax.ppermute(flat, ('tensor', 'example', 'test'), pairs))  40.9 us
    ppermute x16, waiting for transfers between devices, shift(): return lax.ppermute(value, axis, [(i, (i + step) % n) for i in range(n)])  30.1 us
    ppermute x16, starting transfers between devices, shift(): return lax.ppermute(value, axis, [(i, (i + step) % n) for i in range(n)])  25.1 us
    dot_general x4, matrix products, forward(): return jnp.dot(tokens, weight, preferred_element_type=F32)  17.3 us
    convert_element_type x8, other arithmetic, pack(): return (value * SEND_SCALE).astype(jnp.float16)  12.1 us
    ppermute x8, waiting for transfers between devices, spread_features(): pieces.append(lax.ppermute(flat, ('tensor', 'example', 'test'), pairs))  11.2 us
    pallas_call x2, Pallas kernels, dot_rows(): pl.pallas_call(dot_rows_kernel, out_shape=jax.ShapeDtypeStruct((rows, hid...  9.24 us
    unnamed x47, local copies, waits for them, and re-layouts  9.14 us
  transfers between devices with their start and end apart: 28, of which 13 were waited for; matrix products, arithmetic and copies ran while one was open for 25% of the time, Pallas kernels for 2%

profile of v7, /device:TPU:0, one launch (start us, length us, event | category | flops | bytes accessed | tf_op | source)
XLA Modules:
  0.0 209.6 jit_solution(16353805523725841271)
XLA Ops:
  7.2 1.7 collective-permute-start.1
  8.9 1.3 collective-permute-start
  10.2 9.7 %collective-permute-start.7 = (bf16[256,1280]{1,0:T(8,128)(2,1)}, bf16[256,1280]{1,0:T(8,128)(2,1)}, u32[]{:S(2)}, u32[]{:S(2)}) collective-permute-start(bf16[256,1280]{1,0:T(8,128)(2,1)} %bitcast.159), channel_id=1, source_target_pairs={{0,8},{1,12},{4,9},{5,13},{10,2},{11,6},{14,3},{15,7},{16,24},{17,... | collective-permute-start | bytes 1966088 | tf_op jit(solution)/shard_map/ppermute | solution.py:65
  19.9 6.5 %collective-permute-start.6 = (bf16[256,1280]{1,0:T(8,128)(2,1)}, bf16[256,1280]{1,0:T(8,128)(2,1)}, u32[]{:S(2)}, u32[]{:S(2)}) collective-permute-start(bf16[256,1280]{1,0:T(8,128)(2,1)} %bitcast.160), channel_id=1, source_target_pairs={{0,0},{1,4},{4,1},{5,5},{10,10},{11,14},{14,11},{15,15},{16,16},{1... | collective-permute-start | bytes 1966088 | tf_op jit(solution)/shard_map/ppermute | solution.py:65
  26.4 1.6 fusion.19
  28.0 3.5 %collective-permute-done = bf16[256,1280]{1,0:T(8,128)(2,1)} collective-permute-done((bf16[256,1280]{1,0:T(8,128)(2,1)}, bf16[256,1280]{1,0:T(8,128)(2,1)}, u32[]{:S(2)}, u32[]{:S(2)}) %collective-permute-start) | collective-permute-done | bytes 655392 | tf_op jit(solution)/shard_map/ppermute | solution.py:65
  31.5 1.3 broadcast_select_fusion.3
  33.7 1.6 collective-permute-start.4
  35.3 5.6 %fusion.45 = f32[256,4096]{1,0:T(8,128)S(1)} fusion(bf16[256,1280]{1,0:T(8,128)(2,1)S(1)} %broadcast_select_fusion.3, bf16[1280,4096]{1,0:T(8,128)(2,1)} %param.12), kind=kOutput, calls=%fused_computation.118 | convolution fusion | flops 2684354560 | bytes 15335424 | tf_op jit(solution)/shard_map/dot_general | solution.py:129
  41.2 2.9 %fusion.46 = f32[256,4096]{1,0:T(8,128)S(1)} fusion(bf16[256,1280]{1,0:T(8,128)(2,1)S(1)} %broadcast_select_fusion.3, bf16[1280,4096]{1,0:T(8,128)(2,1)S(1)} %bitcast.173), kind=kOutput, calls=%fused_computation.119 | convolution fusion | flops 2684354560 | bytes 15335424 | tf_op jit(solution)/shard_map/dot_general | solution.py:129
  44.9 1.5 broadcast_select_fusion.2
  47.6 1.8 fusion
  49.6 4.4 %fusion.47 = f32[256,4096]{1,0:T(8,128)} fusion(bf16[256,1280]{1,0:T(8,128)(2,1)S(1)} %broadcast_select_fusion.2, bf16[1280,4096]{1,0:T(8,128)(2,1)S(1)} %bitcast.171), kind=kOutput, calls=%fused_computation.120 | convolution fusion | flops 2684354560 | bytes 15335424 | tf_op jit(solution)/shard_map/dot_general | solution.py:129
  54.0 4.4 %fusion.48 = f32[256,4096]{1,0:T(8,128)} fusion(bf16[256,1280]{1,0:T(8,128)(2,1)S(1)} %broadcast_select_fusion.2, bf16[1280,4096]{1,0:T(8,128)(2,1)S(1)} %bitcast.173), kind=kOutput, calls=%fused_computation.121 | convolution fusion | flops 2684354560 | bytes 15335424 | tf_op jit(solution)/shard_map/dot_general | solution.py:129
  58.4 7.7 %collective-permute-done.4 = bf16[256,1280]{1,0:T(8,128)(2,1)S(1)} collective-permute-done((bf16[256,1280]{1,0:T(8,128)(2,1)S(1)}, bf16[256,1280]{1,0:T(8,128)(2,1)S(1)}, u32[]{:S(2)}, u32[]{:S(2)}) %collective-permute-start.4) | collective-permute-done | bytes 655392 | tf_op jit(solution)/shard_map/ppermute | solution.py:65
  66.3 4.6 %shard_map.113 = f32[256,4096]{1,0:T(8,128)S(1)} custom-call(bf16[256,1280]{1,0:T(8,128)(2,1)S(1)} %broadcast_select_fusion.1.tokens_ref, bf16[4096,1280]{1,0:T(8,128)(2,1)S(1)} %bitcast.151), custom_call_target="tpu_custom_call" | custom-call | flops 1 | bytes 1 | tf_op jit(solution)/shard_map/pallas_call | solution.py:92
  70.9 2.1 copy-done.2
  74.2 1.2 fusion.27
  76.2 12.8 %collective-permute-start.3 = (bf16[256,1280]{1,0:T(8,128)(2,1)}, bf16[256,1280]{1,0:T(8,128)(2,1)}, u32[]{:S(2)}, u32[]{:S(2)}) collective-permute-start(bf16[256,1280]{1,0:T(8,128)(2,1)} %bitcast.152), channel_id=1, source_target_pairs={{0,8},{1,12},{4,9},{5,13},{10,2},{11,6},{14,3},{15,7},{16,24},{17,... | collective-permute-start | bytes 1966088 | tf_op jit(solution)/shard_map/ppermute | solution.py:65
  89.0 6.5 %collective-permute-start.2 = (bf16[256,1280]{1,0:T(8,128)(2,1)}, bf16[256,1280]{1,0:T(8,128)(2,1)}, u32[]{:S(2)}, u32[]{:S(2)}) collective-permute-start(bf16[256,1280]{1,0:T(8,128)(2,1)} %bitcast.153), channel_id=1, source_target_pairs={{0,0},{1,4},{4,1},{5,5},{10,10},{11,14},{14,11},{15,15},{16,16},{1... | collective-permute-start | bytes 1966088 | tf_op jit(solution)/shard_map/ppermute | solution.py:65
  95.6 2.9 %multiply_convert_fusion = f16[256,2048]{1,0:T(8,128)(2,1)} fusion(f32[256,4096]{1,0:T(8,128)} %fusion.47, s32[]{:T(128)S(6)} %select_n.64), kind=kLoop, calls=%fused_computation.3 | loop fusion | flops 1048576 | bytes 3145732 | tf_op jit(solution)/shard_map/convert_element_type | solution.py:19
  99.7 2.8 %multiply_convert_fusion.1 = f16[256,2048]{1,0:T(8,128)(2,1)} fusion(f32[256,4096]{1,0:T(8,128)} %fusion.48, s32[]{:T(128)S(6)} %select_n.64), kind=kLoop, calls=%fused_computation.5 | loop fusion | flops 1048576 | bytes 3145732 | tf_op jit(solution)/shard_map/convert_element_type | solution.py:19
  102.5 1.7 multiply_add_fusion.3
  105.3 16.4 %collective-permute-start.16 = (f16[128,2048]{1,0:T(8,128)(2,1)}, f16[128,2048]{1,0:T(8,128)(2,1)}, u32[]{:S(2)}, u32[]{:S(2)}) collective-permute-start(f16[128,2048]{1,0:T(8,128)(2,1)} %get-tuple-element.38), channel_id=1, source_target_pairs={{0,2},{2,0},{1,3},{3,1},{4,6},{6,4},{5,7},{7,5},{8,10},{10,8},{9,1... | collective-permute-start | bytes 1572872 | tf_op jit(solution)/shard_map/ppermute | solution.py:15
  123.0 4.0 %copy-done.1 = bf16[4096,1280]{1,0:T(8,128)(2,1)S(1)} copy-done((bf16[4096,1280]{1,0:T(8,128)(2,1)S(1)}, bf16[4096,1280]{1,0:T(8,128)(2,1)}, u32[]{:S(2)}) %copy-start.1) | copy-done | bytes 10485784
  127.0 4.6 %shard_map.114 = f32[256,4096]{1,0:T(8,128)S(1)} custom-call(bf16[256,1280]{1,0:T(8,128)(2,1)S(1)} %broadcast_select_fusion.tokens_ref, bf16[4096,1280]{1,0:T(8,128)(2,1)S(1)} %copy-done.1), custom_call_target="tpu_custom_call" | custom-call | flops 1 | bytes 1 | tf_op jit(solution)/shard_map/pallas_call | solution.py:92
  131.7 2.1 copy-done.4
  133.7 2.5 %all-reduce.2.cloned.1.call-done = f32[256,192]{0,1:T(8,128)} async-done(((f32[256,192]{0,1:T(8,128)}), f32[256,192]{0,1:T(8,128)}) %all-reduce.2.cloned.1.call-update) | async-done | bytes 196624 | tf_op jit(solution)/shard_map/psum | solution.py:181
  137.1 1.8 multiply_convert_fusion.2
  139.0 2.4 %multiply_add_fusion = f32[256,2048]{1,0:T(8,128)S(1)} fusion(f16[256,2048]{1,0:T(8,128)(2,1)} %collective-permute-done.15, f32[256,4096]{1,0:T(8,128)} %fusion.47, s32[]{:T(128)S(6)} %select_n.60), kind=kLoop, calls=%fused_computation.2 | loop fusion | flops 1572864 | bytes 5242884 | tf_op jit(solution)/shard_map/add | solution.py:136
  142.1 1.6 multiply_add_fusion.1
  144.2 3.0 %add_multiply_fusion = (f32[128,2048]{1,0:T(8,128)S(1)}, f32[128,2048]{1,0:T(8,128)S(1)}, f32[128,2048]{1,0:T(8,128)S(1)}, f32[128,2048]{1,0:T(8,128)S(1)}) fusion(f32[256,2048]{1,0:T(8,128)S(1)} %multiply_add_fusion.1, f32[256,2048]{1,0:T(8,128)S(1)} %multiply_add_fusion, f16[2,256,2048]{2,1,0:T(8,128)(2,1)} %collective-permute-done.14), kind=kLoop, calls=%fused_computation.41 | loop fusion | flops 7864320 | bytes 10485760 | tf_op jit(solution)/shard_map/mul | solution.py:206
  147.6 19.1 %collective-permute-done.12 = f16[128,2048]{1,0:T(8,128)(2,1)} collective-permute-done((f16[128,2048]{1,0:T(8,128)(2,1)}, f16[128,2048]{1,0:T(8,128)(2,1)}, u32[]{:S(2)}, u32[]{:S(2)}) %collective-permute-start.12) | collective-permute-done | bytes 524320 | tf_op jit(solution)/shard_map/ppermute | solution.py:15
  166.7 1.4 fusion.13
  168.4 1.4 fusion.14
  169.8 1.4 convolution_bitcast_fusion.5
  171.6 1.4 fusion.15
  173.3 1.4 fusion.16
  174.9 1.4 convolution_bitcast_fusion.1
  177.3 3.2 %collective-permute-start.19 = (f32[6,16,64]{2,1,0:T(8,128)S(1)}, f32[6,16,64]{2,1,0:T(8,128)}, u32[]{:S(2)}, u32[]{:S(2)}) collective-permute-start(f32[6,16,64]{2,1,0:T(8,128)S(1)} %get-tuple-element.41), channel_id=1, source_target_pairs={{0,12},{4,0},{8,4},{12,8},{1,13},{5,1},{9,5},{13,9},{2,14},{6,2},{... | collective-permute-start | bytes 73736 | tf_op jit(solution)/shard_map/ppermute | solution.py:15
  180.5 2.4 %collective-permute-done.17 = f32[6,16,64]{2,1,0:T(8,128)S(1)} collective-permute-done((f32[6,16,64]{2,1,0:T(8,128)S(1)}, f32[6,16,64]{2,1,0:T(8,128)S(1)}, u32[]{:S(2)}, u32[]{:S(2)}) %collective-permute-start.17) | collective-permute-done | bytes 24608 | tf_op jit(solution)/shard_map/ppermute | solution.py:15
  182.9 2.8 %collective-permute-done.18 = f32[6,16,64]{2,1,0:T(8,128)} collective-permute-done((f32[6,16,64]{2,1,0:T(8,128)S(1)}, f32[6,16,64]{2,1,0:T(8,128)}, u32[]{:S(2)}, u32[]{:S(2)}) %collective-permute-start.18) | collective-permute-done | bytes 24608 | tf_op jit(solution)/shard_map/ppermute | solution.py:15
  187.4 1.4 collective-permute-start.20
  188.9 1.4 collective-permute-done.21
  190.2 1.6 collective-permute-done.20
  192.0 1.3 fusion.49
  193.3 2.3 %collective-permute-start.23 = (f32[4,512]{1,0:T(4,128)S(1)}, f32[4,512]{1,0:T(4,128)S(1)}, u32[]{:S(2)}, u32[]{:S(2)}) collective-permute-start(f32[4,512]{1,0:T(4,128)S(1)} %fusion.49), channel_id=1, source_target_pairs={{0,12},{4,0},{8,4},{12,8},{1,13},{5,1},{9,5},{13,9},{2,14},{6,2},{... | collective-permute-start | bytes 24584 | tf_op jit(solution)/shard_map/ppermute | solution.py:15
  197.0 3.3 %collective-permute-done.24 = f32[4,512]{1,0:T(4,128)S(1)} collective-permute-done((f32[4,512]{1,0:T(4,128)S(1)}, f32[4,512]{1,0:T(4,128)S(1)}, u32[]{:S(2)}, u32[]{:S(2)}) %collective-permute-start.24) | collective-permute-done | bytes 8224 | tf_op jit(solution)/shard_map/ppermute | solution.py:15
  (116 shorter events, 19.0 us)
Async XLA Ops:
  7.2 184.8 %copy-start = (bf16[3,16,64,512]{3,2,1,0:T(8,128)(2,1)S(1)}, bf16[3,16,64,512]{3,2,1,0:T(8,128)(2,1)}, u32[]{:S(2)}) copy-start(bf16[3,16,64,512]{3,2,1,0:T(8,128)(2,1)} %param.17) | copy-start | bytes 9437188
  7.2 129.0 %all-reduce.2.cloned.1.call-start = ((), (), s32[]{:S(2)}) async-start(), calls=%async_computation | async-start | bytes 393216 | tf_op jit(solution)/shard_map/psum | solution.py:181
  7.2 20.8 %collective-permute-start.1 = (bf16[256,1280]{1,0:T(8,128)(2,1)}, bf16[256,1280]{1,0:T(8,128)(2,1)}, u32[]{:S(2)}, u32[]{:S(2)}) collective-permute-start(bf16[256,1280]{1,0:T(8,128)(2,1)} %bitcast.157), channel_id=1, source_target_pairs={{2,8},{3,12},{6,9},{7,13},{8,2},{9,6},{12,3},{13,7},{18,24},{19,28... | collective-permute-start | bytes 1966088 | tf_op jit(solution)/shard_map/ppermute | solution.py:65
  8.9 22.6 %collective-permute-start = (bf16[256,1280]{1,0:T(8,128)(2,1)}, bf16[256,1280]{1,0:T(8,128)(2,1)}, u32[]{:S(2)}, u32[]{:S(2)}) collective-permute-start(bf16[256,1280]{1,0:T(8,128)(2,1)} %bitcast.158), channel_id=1, source_target_pairs={{2,0},{3,4},{6,1},{7,5},{8,10},{9,14},{12,11},{13,15},{18,16},{19,... | collective-permute-start | bytes 1966088 | tf_op jit(solution)/shard_map/ppermute | solution.py:65
  10.2 33.9 %collective-permute-start.7 = (bf16[256,1280]{1,0:T(8,128)(2,1)}, bf16[256,1280]{1,0:T(8,128)(2,1)}, u32[]{:S(2)}, u32[]{:S(2)}) collective-permute-start(bf16[256,1280]{1,0:T(8,128)(2,1)} %bitcast.159), channel_id=1, source_target_pairs={{0,8},{1,12},{4,9},{5,13},{10,2},{11,6},{14,3},{15,7},{16,24},{17,... | collective-permute-start | bytes 1966088 | tf_op jit(solution)/shard_map/ppermute | solution.py:65
  19.9 24.2 %collective-permute-start.6 = (bf16[256,1280]{1,0:T(8,128)(2,1)}, bf16[256,1280]{1,0:T(8,128)(2,1)}, u32[]{:S(2)}, u32[]{:S(2)}) collective-permute-start(bf16[256,1280]{1,0:T(8,128)(2,1)} %bitcast.160), channel_id=1, source_target_pairs={{0,0},{1,4},{4,1},{5,5},{10,10},{11,14},{14,11},{15,15},{16,16},{1... | collective-permute-start | bytes 1966088 | tf_op jit(solution)/shard_map/ppermute | solution.py:65
  26.4 6.4 %copy-start.8 = (bf16[2,128,1280]{2,1,0:T(8,128)(2,1)S(1)}, bf16[2,128,1280]{2,1,0:T(8,128)(2,1)}, u32[]{:S(2)}) copy-start(bf16[2,128,1280]{2,1,0:T(8,128)(2,1)} %param.11) | copy-start | bytes 1966084
  31.5 9.7 %slice-start.6 = ((s8[10485760]{0:T(1024)(128)(4,1)}), s8[4194304]{0:T(1024)(128)(4,1)S(1)}, s32[]{:S(2)}) async-start(s8[10485760]{0:T(1024)(128)(4,1)} %bitcast.172), calls=%async_computation.7 | async-start | bytes 8388608
  32.8 8.4 %slice-start.7 = ((s8[10485760]{0:T(1024)(128)(4,1)}), s8[4194304]{0:T(1024)(128)(4,1)S(1)}, s32[]{:S(2)}) async-start(s8[10485760]{0:T(1024)(128)(4,1)} %bitcast.172), calls=%async_computation.8 | async-start | bytes 8388608
  32.9 8.4 %slice-start.8 = ((s8[10485760]{0:T(1024)(128)(4,1)}), s8[2097152]{0:T(1024)(128)(4,1)S(1)}, s32[]{:S(2)}) async-start(s8[10485760]{0:T(1024)(128)(4,1)} %bitcast.172), calls=%async_computation.9 | async-start | bytes 4194304
  32.9 25.6 %collective-permute-start.5 = (bf16[256,1280]{1,0:T(8,128)(2,1)S(1)}, bf16[256,1280]{1,0:T(8,128)(2,1)S(1)}, u32[]{:S(2)}, u32[]{:S(2)}) collective-permute-start(bf16[256,1280]{1,0:T(8,128)(2,1)S(1)} %bitcast.154), channel_id=1, source_target_pairs={{2,8},{3,12},{6,9},{7,13},{8,2},{9,6},{12,3},{13,7},{18,24},{19,28... | collective-permute-start | bytes 1966088 | tf_op jit(solution)/shard_map/ppermute | solution.py:65
  33.7 32.5 %collective-permute-start.4 = (bf16[256,1280]{1,0:T(8,128)(2,1)S(1)}, bf16[256,1280]{1,0:T(8,128)(2,1)S(1)}, u32[]{:S(2)}, u32[]{:S(2)}) collective-permute-start(bf16[256,1280]{1,0:T(8,128)(2,1)S(1)} %bitcast.155), channel_id=1, source_target_pairs={{2,0},{3,4},{6,1},{7,5},{8,10},{9,14},{12,11},{13,15},{18,16},{19,... | collective-permute-start | bytes 1966088 | tf_op jit(solution)/shard_map/ppermute | solution.py:65
  41.1 5.3 %collective-permute-start.8 = (f16[256,2048]{1,0:T(8,128)(2,1)S(1)}, f16[256,2048]{1,0:T(8,128)(2,1)S(1)}, u32[]{:S(2)}, u32[]{:S(2)}) collective-permute-start(f16[256,2048]{1,0:T(8,128)(2,1)S(1)} %multiply_convert_fusion.5), channel_id=1, source_target_pairs={{0,1},{1,0},{2,3},{3,2},{4,5},{5,4},{6,7},{7,6},{8,9},{9,8},{10,11... | collective-permute-start | bytes 3145736 | tf_op jit(solution)/shard_map/ppermute | solution.py:15
  44.1 5.3 %slice-start.3 = ((s8[10485760]{0:T(1024)(128)(4,1)}), s8[4194304]{0:T(1024)(128)(4,1)S(1)}, s32[]{:S(2)}) async-start(s8[10485760]{0:T(1024)(128)(4,1)} %bitcast.170), calls=%async_computation.4 | async-start | bytes 8388608
  44.4 2.8 %collective-permute-start.9 = (f16[256,2048]{1,0:T(8,128)(2,1)S(1)}, f16[256,2048]{1,0:T(8,128)(2,1)S(1)}, u32[]{:S(2)}, u32[]{:S(2)}) collective-permute-start(f16[256,2048]{1,0:T(8,128)(2,1)S(1)} %multiply_convert_fusion.4), channel_id=1, source_target_pairs={{0,1},{1,0},{2,3},{3,2},{4,5},{5,4},{6,7},{7,6},{8,9},{9,8},{10,11... | collective-permute-start | bytes 3145736 | tf_op jit(solution)/shard_map/ppermute | solution.py:15
  46.4 3.0 %slice-start.4 = ((s8[10485760]{0:T(1024)(128)(4,1)}), s8[4194304]{0:T(1024)(128)(4,1)S(1)}, s32[]{:S(2)}) async-start(s8[10485760]{0:T(1024)(128)(4,1)} %bitcast.170), calls=%async_computation.5 | async-start | bytes 8388608
  46.9 2.8 %slice-start.5 = ((s8[10485760]{0:T(1024)(128)(4,1)}), s8[2097152]{0:T(1024)(128)(4,1)S(1)}, s32[]{:S(2)}) async-start(s8[10485760]{0:T(1024)(128)(4,1)} %bitcast.170), calls=%async_computation.6 | async-start | bytes 4194304
  49.6 16.6 %slice-start = ((s8[10485760]{0:T(1024)(128)(4,1)}), s8[4194304]{0:T(1024)(128)(4,1)S(1)}, s32[]{:S(2)}) async-start(s8[10485760]{0:T(1024)(128)(4,1)} %bitcast.150), calls=%async_computation.1 | async-start | bytes 8388608
  49.6 16.6 %slice-start.1 = ((s8[10485760]{0:T(1024)(128)(4,1)}), s8[4194304]{0:T(1024)(128)(4,1)S(1)}, s32[]{:S(2)}) async-start(s8[10485760]{0:T(1024)(128)(4,1)} %bitcast.150), calls=%async_computation.2 | async-start | bytes 8388608
  54.0 12.2 %slice-start.2 = ((s8[10485760]{0:T(1024)(128)(4,1)}), s8[2097152]{0:T(1024)(128)(4,1)S(1)}, s32[]{:S(2)}) async-start(s8[10485760]{0:T(1024)(128)(4,1)} %bitcast.150), calls=%async_computation.3 | async-start | bytes 4194304
  70.9 2.1 copy-start.2
  73.0 3.1 %copy-start.10 = (s32[2]{0:T(128)S(1)}, s32[2]{0:T(128)}, u32[]{:S(2)}) copy-start(s32[2]{0:T(128)} %param.18) | copy-start | bytes 28
  74.2 28.3 %collective-permute-start.10 = (f16[256,2048]{1,0:T(8,128)(2,1)}, f16[256,2048]{1,0:T(8,128)(2,1)}, u32[]{:S(2)}, u32[]{:S(2)}) collective-permute-start(f16[256,2048]{1,0:T(8,128)(2,1)} %multiply_convert_fusion.3), channel_id=1, source_target_pairs={{0,1},{1,0},{2,3},{3,2},{4,5},{5,4},{6,7},{7,6},{8,9},{9,8},{10,11... | collective-permute-start | bytes 3145736 | tf_op jit(solution)/shard_map/ppermute | solution.py:15
  76.2 29.1 %collective-permute-start.3 = (bf16[256,1280]{1,0:T(8,128)(2,1)}, bf16[256,1280]{1,0:T(8,128)(2,1)}, u32[]{:S(2)}, u32[]{:S(2)}) collective-permute-start(bf16[256,1280]{1,0:T(8,128)(2,1)} %bitcast.152), channel_id=1, source_target_pairs={{0,8},{1,12},{4,9},{5,13},{10,2},{11,6},{14,3},{15,7},{16,24},{17,... | collective-permute-start | bytes 1966088 | tf_op jit(solution)/shard_map/ppermute | solution.py:65
  89.0 32.8 %collective-permute-start.2 = (bf16[256,1280]{1,0:T(8,128)(2,1)}, bf16[256,1280]{1,0:T(8,128)(2,1)}, u32[]{:S(2)}, u32[]{:S(2)}) collective-permute-start(bf16[256,1280]{1,0:T(8,128)(2,1)} %bitcast.153), channel_id=1, source_target_pairs={{0,0},{1,4},{4,1},{5,5},{10,10},{11,14},{14,11},{15,15},{16,16},{1... | collective-permute-start | bytes 1966088 | tf_op jit(solution)/shard_map/ppermute | solution.py:65
  95.5 48.7 %collective-permute-start.14 = (f16[2,256,2048]{2,1,0:T(8,128)(2,1)}, f16[2,256,2048]{2,1,0:T(8,128)(2,1)}, u32[]{:S(2)}, u32[]{:S(2)}) collective-permute-start(f16[2,256,2048]{2,1,0:T(8,128)(2,1)} %fusion), channel_id=1, source_target_pairs={{0,2},{2,0},{1,3},{3,1},{4,6},{6,4},{5,7},{7,5},{8,10},{10,8},{9,1... | collective-permute-start | bytes 6291464 | tf_op jit(solution)/shard_map/ppermute | solution.py:15
  95.6 6.9 %copy-start.3 = (f32[256,4096]{1,0:T(8,128)S(1)}, f32[256,4096]{1,0:T(8,128)}, u32[]{:S(2)}) copy-start(f32[256,4096]{1,0:T(8,128)} %copy-done.2) | copy-start | bytes 12582916
  98.5 40.4 %collective-permute-start.15 = (f16[256,2048]{1,0:T(8,128)(2,1)}, f16[256,2048]{1,0:T(8,128)(2,1)}, u32[]{:S(2)}, u32[]{:S(2)}) collective-permute-start(f16[256,2048]{1,0:T(8,128)(2,1)} %multiply_convert_fusion), channel_id=1, source_target_pairs={{0,1},{1,0},{2,3},{3,2},{4,5},{5,4},{6,7},{7,6},{8,9},{9,8},{10,11... | collective-permute-start | bytes 3145736 | tf_op jit(solution)/shard_map/ppermute | solution.py:15
  102.5 38.9 %collective-permute-start.13 = (f16[256,2048]{1,0:T(8,128)(2,1)}, f16[256,2048]{1,0:T(8,128)(2,1)}, u32[]{:S(2)}, u32[]{:S(2)}) collective-permute-start(f16[256,2048]{1,0:T(8,128)(2,1)} %multiply_convert_fusion.1), channel_id=1, source_target_pairs={{0,1},{1,0},{2,3},{3,2},{4,5},{5,4},{6,7},{7,6},{8,9},{9,8},{10,11... | collective-permute-start | bytes 3145736 | tf_op jit(solution)/shard_map/ppermute | solution.py:15
  105.3 66.3 %collective-permute-start.16 = (f16[128,2048]{1,0:T(8,128)(2,1)}, f16[128,2048]{1,0:T(8,128)(2,1)}, u32[]{:S(2)}, u32[]{:S(2)}) collective-permute-start(f16[128,2048]{1,0:T(8,128)(2,1)} %get-tuple-element.38), channel_id=1, source_target_pairs={{0,2},{2,0},{1,3},{3,1},{4,6},{6,4},{5,7},{7,5},{8,10},{10,8},{9,1... | collective-permute-start | bytes 1572872 | tf_op jit(solution)/shard_map/ppermute | solution.py:15
  122.9 43.8 %collective-permute-start.12 = (f16[128,2048]{1,0:T(8,128)(2,1)}, f16[128,2048]{1,0:T(8,128)(2,1)}, u32[]{:S(2)}, u32[]{:S(2)}) collective-permute-start(f16[128,2048]{1,0:T(8,128)(2,1)} %get-tuple-element.39), channel_id=1, source_target_pairs={{0,2},{2,0},{1,3},{3,1},{4,6},{6,4},{5,7},{7,5},{8,10},{10,8},{9,1... | collective-permute-start | bytes 1572872 | tf_op jit(solution)/shard_map/ppermute | solution.py:15
  123.0 4.0 %copy-start.1 = (bf16[4096,1280]{1,0:T(8,128)(2,1)S(1)}, bf16[4096,1280]{1,0:T(8,128)(2,1)}, u32[]{:S(2)}) copy-start(bf16[4096,1280]{1,0:T(8,128)(2,1)} %weight_ref.3) | copy-start | bytes 31457284
  131.6 2.1 copy-start.4
  138.9 3.1 %copy-start.6 = (f32[256,4096]{1,0:T(8,128)S(1)}, f32[256,4096]{1,0:T(8,128)}, u32[]{:S(2)}) copy-start(f32[256,4096]{1,0:T(8,128)} %fusion.48) | copy-start | bytes 12582916
  138.9 8.3 %collective-permute-start.11 = (f16[256,2048]{1,0:T(8,128)(2,1)S(1)}, f16[256,2048]{1,0:T(8,128)(2,1)S(1)}, u32[]{:S(2)}, u32[]{:S(2)}) collective-permute-start(f16[256,2048]{1,0:T(8,128)(2,1)S(1)} %multiply_convert_fusion.2), channel_id=1, source_target_pairs={{0,1},{1,0},{2,3},{3,2},{4,5},{5,4},{6,7},{7,6},{8,9},{9,8},{10,11... | collective-permute-start | bytes 3145736 | tf_op jit(solution)/shard_map/ppermute | solution.py:15
  143.7 3.6 %copy-start.5 = (f32[256,4096]{1,0:T(8,128)S(1)}, f32[256,4096]{1,0:T(8,128)}, u32[]{:S(2)}) copy-start(f32[256,4096]{1,0:T(8,128)} %copy-done.4) | copy-start | bytes 12582916
  147.2 19.5 %copy-start.7 = (bf16[4096,192]{0,1:T(8,128)(2,1)S(1)}, bf16[4096,192]{0,1:T(8,128)(2,1)}, u32[]{:S(2)}) copy-start(bf16[4096,192]{0,1:T(8,128)(2,1)} %param.16) | copy-start | bytes 4718596
  174.7 5.7 %copy-start.9 = (s32[2]{0:T(128)S(1)}, s32[2]{0:T(128)}, u32[]{:S(2)}) copy-start(s32[2]{0:T(128)} %param.19) | copy-start | bytes 28
  176.6 6.3 %collective-permute-start.17 = (f32[6,16,64]{2,1,0:T(8,128)S(1)}, f32[6,16,64]{2,1,0:T(8,128)S(1)}, u32[]{:S(2)}, u32[]{:S(2)}) collective-permute-start(f32[6,16,64]{2,1,0:T(8,128)S(1)} %get-tuple-element.40), channel_id=1, source_target_pairs={{0,4},{4,8},{8,12},{12,0},{1,5},{5,9},{9,13},{13,1},{2,6},{6,10},{... | collective-permute-start | bytes 73736 | tf_op jit(solution)/shard_map/ppermute | solution.py:15
  177.3 5.6 %collective-permute-start.19 = (f32[6,16,64]{2,1,0:T(8,128)S(1)}, f32[6,16,64]{2,1,0:T(8,128)}, u32[]{:S(2)}, u32[]{:S(2)}) collective-permute-start(f32[6,16,64]{2,1,0:T(8,128)S(1)} %get-tuple-element.41), channel_id=1, source_target_pairs={{0,12},{4,0},{8,4},{12,8},{1,13},{5,1},{9,5},{13,9},{2,14},{6,2},{... | collective-permute-start | bytes 73736 | tf_op jit(solution)/shard_map/ppermute | solution.py:15
  180.5 5.3 %collective-permute-start.18 = (f32[6,16,64]{2,1,0:T(8,128)S(1)}, f32[6,16,64]{2,1,0:T(8,128)}, u32[]{:S(2)}, u32[]{:S(2)}) collective-permute-start(f32[6,16,64]{2,1,0:T(8,128)S(1)} %get-tuple-element.42), channel_id=1, source_target_pairs={{0,8},{4,12},{8,0},{12,4},{1,9},{5,13},{9,1},{13,5},{2,10},{6,14},... | collective-permute-start | bytes 73736 | tf_op jit(solution)/shard_map/ppermute | solution.py:15
  180.5 6.2 %collective-permute-start.26 = (s32[2]{0:T(128)S(1)}, s32[2]{0:T(128)S(1)}, u32[]{:S(2)}, u32[]{:S(2)}) collective-permute-start(s32[2]{0:T(128)S(1)} %copy-done.9), channel_id=1, source_target_pairs={{0,2},{2,0},{1,3},{3,1},{4,6},{6,4},{5,7},{7,5},{8,10},{10,8},{9,1... | collective-permute-start | bytes 32 | tf_op jit(solution)/shard_map/ppermute | solution.py:15
  186.6 2.3 %collective-permute-start.22 = (f32[6,16,64]{2,1,0:T(8,128)S(1)}, f32[6,16,64]{2,1,0:T(8,128)S(1)}, u32[]{:S(2)}, u32[]{:S(2)}) collective-permute-start(f32[6,16,64]{2,1,0:T(8,128)S(1)} %fusion.33), channel_id=1, source_target_pairs={{0,1},{1,0},{2,3},{3,2},{4,5},{5,4},{6,7},{7,6},{8,9},{9,8},{10,11... | collective-permute-start | bytes 73736 | tf_op jit(solution)/shard_map/ppermute | solution.py:234
  186.7 3.6 %collective-permute-start.21 = (f32[6,16,64]{2,1,0:T(8,128)S(1)}, f32[6,16,64]{2,1,0:T(8,128)S(1)}, u32[]{:S(2)}, u32[]{:S(2)}) collective-permute-start(f32[6,16,64]{2,1,0:T(8,128)S(1)} %fusion.33), channel_id=1, source_target_pairs={{0,3},{1,2},{2,1},{3,0},{4,7},{5,6},{6,5},{7,4},{8,11},{9,10},{10,... | collective-permute-start | bytes 73736 | tf_op jit(solution)/shard_map/ppermute | solution.py:234
  187.4 4.4 %collective-permute-start.20 = (f32[6,16,64]{2,1,0:T(8,128)S(1)}, f32[6,16,64]{2,1,0:T(8,128)S(1)}, u32[]{:S(2)}, u32[]{:S(2)}) collective-permute-start(f32[6,16,64]{2,1,0:T(8,128)S(1)} %fusion.33), channel_id=1, source_target_pairs={{0,2},{1,3},{2,0},{3,1},{4,6},{5,7},{6,4},{7,5},{8,10},{9,11},{10,... | collective-permute-start | bytes 73736 | tf_op jit(solution)/shard_map/ppermute | solution.py:234
  193.3 3.7 %collective-permute-start.23 = (f32[4,512]{1,0:T(4,128)S(1)}, f32[4,512]{1,0:T(4,128)S(1)}, u32[]{:S(2)}, u32[]{:S(2)}) collective-permute-start(f32[4,512]{1,0:T(4,128)S(1)} %fusion.49), channel_id=1, source_target_pairs={{0,12},{4,0},{8,4},{12,8},{1,13},{5,1},{9,5},{13,9},{2,14},{6,2},{... | collective-permute-start | bytes 24584 | tf_op jit(solution)/shard_map/ppermute | solution.py:15
  195.7 5.4 %collective-permute-start.25 = (f32[4,512]{1,0:T(4,128)S(1)}, f32[4,512]{1,0:T(4,128)S(1)}, u32[]{:S(2)}, u32[]{:S(2)}) collective-permute-start(f32[4,512]{1,0:T(4,128)S(1)} %fusion.49), channel_id=1, source_target_pairs={{0,4},{4,8},{8,12},{12,0},{1,5},{5,9},{9,13},{13,1},{2,6},{6,10},{... | collective-permute-start | bytes 24584 | tf_op jit(solution)/shard_map/ppermute | solution.py:15
  195.7 4.6 %collective-permute-start.24 = (f32[4,512]{1,0:T(4,128)S(1)}, f32[4,512]{1,0:T(4,128)S(1)}, u32[]{:S(2)}, u32[]{:S(2)}) collective-permute-start(f32[4,512]{1,0:T(4,128)S(1)} %fusion.49), channel_id=1, source_target_pairs={{0,8},{4,12},{8,0},{12,4},{1,9},{5,13},{9,1},{13,5},{2,10},{6,14},... | collective-permute-start | bytes 24584 | tf_op jit(solution)/shard_map/ppermute | solution.py:15
Sparse Core Ops, SparseCore 0:
  95.6 40.4 all-reduce.1

commit v8 on v7

--- a/solution.py
+++ b/solution.py
@@ -52,7 +52,7 @@
     return lax.optimization_barrier((value,) + earlier)[0]
 
 
-def spread_features(flat, far, *earlier):
+def spread_features(flat, far):
     pieces = []
     for turn in range(2):
         pairs = []
@@ -63,10 +63,16 @@
                 source = block * 4 + (example ^ far) * 2 + source_core
                 pairs.append((source, target * 4 + example * 2 + core))
         pieces.append(lax.ppermute(flat, ("tensor", "example", "test"), pairs))
-    if earlier:
-        pieces = lax.optimization_barrier((*pieces, *earlier))
+    return pieces
+
+
+def arrived_features(far, near, *earlier):
+    pieces = lax.optimization_barrier((*far, *near, *earlier))[:4]
     holder = lax.axis_index("example") * 2 + lax.axis_index("test")
-    return jnp.where((lax.axis_index("tensor") ^ holder) < 2, pieces[0], pieces[1])
+    first = (lax.axis_index("tensor") ^ holder) < 2
+    return jnp.concatenate(
+        [jnp.where(first, pieces[0], pieces[1]), jnp.where(first, pieces[2], pieces[3])]
+    )
 
 
 def gathered_features(flat, n_ex, n_cores):
@@ -75,8 +81,8 @@
     mine = lax.dynamic_slice_in_dim(flat, lax.axis_index("test") * part, part, 0)
     whole = lax.all_gather(mine, "tensor", axis=1, tiled=True)
     whole = lax.all_to_all(whole, ("example", "test"), split_axis=1, concat_axis=0, tiled=True)
-    owners = [lax.rem(lax.axis_index("example") + step, n_ex) for step in range(n_ex)]
-    return [lax.dynamic_slice_in_dim(whole, owner * rows, rows, 0) for owner in owners]
+    begin = lax.rem(lax.axis_index("example") + 1, n_ex) * rows
+    return lax.dynamic_slice_in_dim(jnp.concatenate([whole, whole]), begin, n_ex * rows, 0)
 
 
 def dot_rows_kernel(tokens_ref, weight_ref, out_ref):
@@ -101,6 +107,47 @@
         compiler_params=pltpu.CompilerParams(vmem_limit_bytes=16 * 2**20),
         cost_estimate=pl.CostEstimate(flops=1, bytes_accessed=1, transcendentals=0),
     )(tokens, weight)
+
+
+def gradients_kernel(down_ref, *refs):
+    factor_refs, proj_refs, (model_ref, hidden_ref, out_ref) = refs[:2], refs[2:4], refs[4:]
+    n_z, _, share, width = out_ref.shape
+    ex_loc, seq_len, _ = model_ref.shape
+    hidden = down_ref.shape[1]
+    chunk = min(512, hidden)
+    for layer in range(2):
+        outputs = jnp.zeros((ex_loc * seq_len, width), F32)
+        for begin in range(0, hidden, chunk):
+            part = pl.ds(begin, chunk)
+            rounded = (down_ref[:, part] * factor_refs[layer][:, part]).astype(jnp.bfloat16)
+            outputs += jnp.dot(rounded, proj_refs[layer][part, :], preferred_element_type=F32)
+        for e in range(ex_loc):
+            grad = lax.dot_general(
+                outputs[e * seq_len : (e + 1) * seq_len],
+                model_ref[e, :, layer * width : (layer + 1) * width],
+                (((0,), (0,)), ((), ())),
+                precision=lax.Precision.HIGHEST,
+                preferred_element_type=F32,
+            )
+            for z in range(n_z):
+                out_ref[z, 3 * e + layer] = grad[z * share : (z + 1) * share]
+    for e in range(ex_loc):
+        out_ref[:, 3 * e + 2] = hidden_ref[e]
+
+
+def gradients(d_hidden, factors, hid_proj, model, hidden_grads, n_z):
+    width = hid_proj.shape[1] // 3
+    rows, hidden = d_hidden.shape
+    ex_loc = model.shape[0]
+    projs = [hid_proj[:, :width], hid_proj[:, width : 2 * width]]
+    return pl.pallas_call(
+        gradients_kernel,
+        out_shape=jax.ShapeDtypeStruct((n_z, 3 * ex_loc, width // n_z, width), F32),
+        compiler_params=pltpu.CompilerParams(vmem_limit_bytes=32 * 2**20),
+        cost_estimate=pl.CostEstimate(
+            flops=4 * rows * hidden * width, bytes_accessed=12 * rows * hidden, transcendentals=0
+        ),
+    )(d_hidden, *factors, *projs, model, hidden_grads)
 
 
 def on_device(
@@ -128,12 +175,16 @@
     def forward(tokens, weight):
         return jnp.dot(tokens, weight, preferred_element_type=F32)
 
-    def core_sum(product):
-        kept = lax.dynamic_slice_in_dim(product, core * hid_part, hid_part, 1)
-        for step in range(1, n_cores):
-            to = lax.rem(core + step, n_cores)
-            sent = pack(lax.dynamic_slice_in_dim(product, to * hid_part, hid_part, 1))
-            kept = kept + unpack(shift(sent, "test", step))
+    def core_sum(product, step):
+        begin = (step - 1) % n_ex * tok_rows
+
+        def share_of(index):
+            return lax.dynamic_slice(product, (begin, index * hid_part), (tok_rows, hid_part))
+
+        kept = share_of(core)
+        for core_step in range(1, n_cores):
+            sent = pack(share_of(lax.rem(core + core_step, n_cores)))
+            kept = kept + unpack(shift(sent, "test", core_step))
         return kept
 
     flat_acts = activations.reshape(tok_rows, d_local)
@@ -148,43 +199,31 @@
 
     direct = (n_z, n_ex, n_cores) == (4, 2, 2)
     examples = [slice(e * seq_len, (e + 1) * seq_len) for e in range(ex_loc)]
-    arrived = [[[] for _ in range(ex_loc)] for _ in range(3)]
+    arrived, arrived_down = [], []
     if direct:
-        acts_far = [spread_features(flat_acts, 1)]
+        acts_all = arrived_features(
+            spread_features(flat_acts, 1), spread_features(flat_acts, 0), model_part
+        )
+        grad_ready = after(flat_grad, acts_all)
+        grad_all = spread_features(grad_ready, 1), spread_features(grad_ready, 0)
     else:
-        acts_near, *acts_far = gathered_features(flat_acts, n_ex, n_cores)
-        grad_near, *grad_far = gathered_features(flat_grad, n_ex, n_cores)
+        acts_all = gathered_features(flat_acts, n_ex, n_cores)
+        grad_all = gathered_features(flat_grad, n_ex, n_cores)
+    model_sum = lax.psum(after(model_part, acts_all), "tensor")
+    gate_all = forward(acts_all, w_gate)
+    up_all = forward(after(acts_all, gate_all), w_up)
     for step in range(1, n_ex):
-        gate_far = forward(acts_far[step - 1], w_gate)
-        up_far = forward(after(acts_far[step - 1], gate_far), w_up)
-        both = pack(jnp.stack([core_sum(gate_far), core_sum(up_far)]))
+        both = pack(jnp.stack([core_sum(gate_all, step), core_sum(up_all, step)]))
         received = shift(both, "example", step)
-        for e, rows in enumerate(examples):
-            for which in range(2):
-                arrived[which][e].append(received[which, rows])
+        arrived.append(received)
     if direct:
-        acts_near = spread_features(flat_acts, 0, up_far)
-    gate_near = forward(after(acts_near, both), w_gate)
-    up_near = forward(after(acts_near, gate_near), w_up)
-    if direct:
-        grad_ready = after(flat_grad, acts_far[0])
-        grad_far = [spread_features(grad_ready, 1, up_near)]
+        grad_all = arrived_features(*grad_all, both)
+    down_all = dot_rows(grad_all, w_down)
     for step in range(1, n_ex):
-        down_far = dot_rows(grad_far[step - 1], w_down)
-        summed = core_sum(down_far)
-        for e, rows in enumerate(examples):
-            sent = pack(summed[rows])
-            arrived[2][e].append(shift(sent, "example", step))
-    if direct:
-        grad_near = spread_features(grad_ready, 0, sent)
-    grad_near = dot_rows(grad_near, w_down)
-    model_sum = lax.psum(after(model_part, acts_far[0]), "tensor")
-    model_sum = after(model_sum, grad_near)
-    own = [core_sum(near) for near in (gate_near, up_near, grad_near)]
-
-    def total(which, e):
-        kept = own[which][e * seq_len : (e + 1) * seq_len]
-        return kept + sum(unpack(one) for one in arrived[which][e])
+        sent = pack(core_sum(down_all, step))
+        arrived_down.append(shift(sent, "example", step))
+    own = [core_sum(one, 0) for one in (gate_all, up_all, after(down_all, received))]
+    model_sum = after(model_sum, received)
 
     hid_proj = lax.dynamic_slice_in_dim(proj_hidden, core * hid_part, hid_part, 0)
     positions = jnp.arange(seq_len, dtype=jnp.int32)
@@ -197,29 +236,23 @@
         )
         return product.reshape(n_z, width // n_z, width)
 
-    factors, hidden_grads = [], []
-    for e in range(ex_loc):
-        gate_act, up_act = total(0, e), total(1, e)
-        sigmoid_gate = jax.nn.sigmoid(gate_act)
-        silu_gate = gate_act * sigmoid_gate
-        hidden = (silu_gate * up_act).astype(jnp.bfloat16)
-        gate_factor = up_act * sigmoid_gate * (1.0 + gate_act * (1.0 - sigmoid_gate))
-        factors.append(lax.optimization_barrier((gate_factor, silu_gate)))
-        in_hidden = jnp.dot(hidden, hid_proj[:, 2 * width :], preferred_element_type=F32)
-        hidden_grads.append(outer(masked[e, :, 2 * width :], in_hidden))
-    grads = []
-    for e in range(ex_loc):
-        d_hidden = total(2, e)
-        d_gate = (d_hidden * factors[e][0]).astype(jnp.bfloat16)
-        d_up = (d_hidden * factors[e][1]).astype(jnp.bfloat16)
-        out_gate = jnp.dot(d_gate, hid_proj[:, :width], preferred_element_type=F32)
-        out_up = jnp.dot(d_up, hid_proj[:, width : 2 * width], preferred_element_type=F32)
-        grads += [
-            outer(out_gate, masked[e, :, :width]),
-            outer(out_up, masked[e, :, width : 2 * width]),
-            hidden_grads[e],
-        ]
-    grads = scatter_sum(jnp.stack(grads, 1), "tensor")
+    gate_act, up_act = [
+        kept + sum(unpack(one[which]) for one in arrived) for which, kept in enumerate(own[:2])
+    ]
+    d_hidden = own[2] + sum(unpack(one) for one in arrived_down)
+    sigmoid_gate = jax.nn.sigmoid(gate_act)
+    silu_gate = gate_act * sigmoid_gate
+    hidden = (silu_gate * up_act).astype(jnp.bfloat16)
+    gate_factor = up_act * sigmoid_gate * (1.0 + gate_act * (1.0 - sigmoid_gate))
+    in_hidden = jnp.dot(hidden, hid_proj[:, 2 * width :], preferred_element_type=F32)
+    hidden_grads = jnp.stack(
+        [outer(masked[e, :, 2 * width :], in_hidden[rows]) for e, rows in enumerate(examples)]
+    )
+    factors = [gate_factor, silu_gate]
+    grads = gradients(
+        d_hidden, factors, hid_proj, masked[:, :, : 2 * width], hidden_grads, n_z
+    )
+    grads = scatter_sum(grads, "tensor")
     by_example = []
     for ex_step in range(n_ex):
         total = 0.0

time: 211 us -> 218 us (1.033)
  waiting for transfers between devices: 46.8 us -> 59.8 us
  matrix products: 32 us -> 22.7 us
  local copies, waits for them, and re-layouts: 9.97 us -> 15 us
    psum x1, waiting for transfers between devices: 2.45 us -> 30.7 us  [on_device(): model_sum = lax.psum(after(model_part, acts_all), 'tensor')]
    ppermute x16 -> x15, waiting for transfers between devices: 30.1 us -> 6.76 us  [shift(): return lax.ppermute(value, axis, [(i, (i + step) % n) for i in range(n)])]
    ppermute x8, waiting for transfers between devices: 11.2 us -> 19 us  [spread_features(): pieces.append(lax.ppermute(flat, ('tensor', 'example', 'test'), pairs))]
    dot_general x4 -> x0, matrix products: 5.78 us -> none  [the longest x2 2.89 us: on_device(): jnp.dot(d_up, hid_proj[:, width:2 * width], preferred_element_type=F32)]
    another operation x2 -> x3, other arithmetic: 0.78 us -> 4.75 us  [the longest x2 4.74 us: on_device(): both = pack(jnp.stack([core_sum(gate_all, step), core_sum(up_all, step)]))]
    add x4 -> x1, other arithmetic: 6 us -> 2.53 us  [on_device(): d_hidden = own[2] + sum((unpack(one) for one in arrived_down))]
    dot_general x4 -> x2, matrix products: 17.3 us -> 14.1 us  [forward(): return jnp.dot(tokens, weight, preferred_element_type=F32)]
    select_n x4 -> x3, other arithmetic: 4.07 us -> 1.56 us  [the longest x2 1.49 us: arrived_features(): jnp.where(first, pieces[2], pieces[3])]
  transfers between devices with their start and end apart: 28 -> 27, of which waited for: 13 -> 11; matrix products, arithmetic and copies ran while one was open for 25% -> 18% of each run, Pallas kernels for 2% -> 3%
where the time goes in v8:
time: 218 us; the launch traced here: 217 us
  starting transfers between devices  67.8 us (31%)
  waiting for transfers between devices  59.8 us (27%)
  other arithmetic  28.3 us (13%)
  matrix products  22.7 us (10%)
  local copies, waits for them, and re-layouts  15 us (7%)
  between operations  14.5 us (7%)
  Pallas kernels  8.77 us (4%)
    ppermute x8, starting transfers between devices, spread_features(): pieces.append(lax.ppermute(flat, ('tensor', 'example', 'test'), pairs))  41.1 us
    psum x1, waiting for transfers between devices, on_device(): model_sum = lax.psum(after(model_part, acts_all), 'tensor')  30.7 us
    ppermute x15, starting transfers between devices, shift(): return lax.ppermute(value, axis, [(i, (i + step) % n) for i in range(n)])  24.7 us
    ppermute x8, waiting for transfers between devices, spread_features(): pieces.append(lax.ppermute(flat, ('tensor', 'example', 'test'), pairs))  19 us
    dot_general x2, matrix products, forward(): return jnp.dot(tokens, weight, preferred_element_type=F32)  14.1 us
    convert_element_type x6, other arithmetic, pack(): return (value * SEND_SCALE).astype(jnp.float16)  12.5 us
    unnamed x37, local copies, waits for them, and re-layouts  11.2 us
    pallas_call x1, Pallas kernels, dot_rows(): pl.pallas_call(dot_rows_kernel, out_shape=jax.ShapeDtypeStruct((rows, hid...  7.51 us
  transfers between devices with their start and end apart: 27, of which 11 were waited for; matrix products, arithmetic and copies ran while one was open for 18% of the time, Pallas kernels for 3%

profile of v8, /device:TPU:0, one launch (start us, length us, event | category | flops | bytes accessed | tf_op | source)
XLA Modules:
  0.0 217.0 jit_solution(13460503411483564887)
XLA Ops:
  7.2 1.6 collective-permute-start
  8.8 1.5 collective-permute-start.1
  10.3 6.6 %collective-permute-start.2 = (bf16[256,1280]{1,0:T(8,128)(2,1)}, bf16[256,1280]{1,0:T(8,128)(2,1)}, u32[]{:S(2)}, u32[]{:S(2)}) collective-permute-start(bf16[256,1280]{1,0:T(8,128)(2,1)} %bitcast.94), channel_id=1, source_target_pairs={{0,0},{1,4},{4,1},{5,5},{10,10},{11,14},{14,11},{15,15},{16,16},{1... | collective-permute-start | bytes 1966088 | tf_op jit(solution)/shard_map/ppermute | solution.py:65
  16.8 5.1 %collective-permute-start.3 = (bf16[256,1280]{1,0:T(8,128)(2,1)}, bf16[256,1280]{1,0:T(8,128)(2,1)}, u32[]{:S(2)}, u32[]{:S(2)}) collective-permute-start(bf16[256,1280]{1,0:T(8,128)(2,1)} %bitcast.95), channel_id=1, source_target_pairs={{0,8},{1,12},{4,9},{5,13},{10,2},{11,6},{14,3},{15,7},{16,24},{17,... | collective-permute-start | bytes 1966088 | tf_op jit(solution)/shard_map/ppermute | solution.py:65
  22.0 1.4 fusion.6
  23.4 1.6 fusion.3
  25.7 1.9 collective-permute-done
  27.6 8.7 %collective-permute-done.3 = bf16[256,1280]{1,0:T(8,128)(2,1)} collective-permute-done((bf16[256,1280]{1,0:T(8,128)(2,1)}, bf16[256,1280]{1,0:T(8,128)(2,1)}, u32[]{:S(2)}, u32[]{:S(2)}) %collective-permute-start.3) | collective-permute-done | bytes 655392 | tf_op jit(solution)/shard_map/ppermute | solution.py:65
  36.3 1.4 broadcast_select_fusion.2
  37.8 8.6 %fusion.17 = f32[512,4096]{1,0:T(8,128)S(1)} fusion(bf16[1280,4096]{1,0:T(8,128)(2,1)} %param.12, bf16[256,1280]{1,0:T(8,128)(2,1)S(1)} %get-tuple-element.41, bf16[256,1280]{1,0:T(8,128)(2,1)S(1)} %get-tuple-element.42), kind=kOutput, calls=%fused_computation.73 | convolution fusion | flops 5371330560 | bytes 20185088 | tf_op jit(solution)/shard_map/dot_general | solution.py:176
  46.4 2.3 %multiply_convert_fusion.1 = (f16[256,2048]{1,0:T(8,128)(2,1)}, f16[256,2048]{1,0:T(8,128)(2,1)}) fusion(f32[512,4096]{1,0:T(8,128)S(1)} %fusion.17, s32[]{:T(128)S(6)} %select_n.64), kind=kLoop, calls=%fused_computation.8 | loop fusion | flops 2097152 | bytes 6291460 | tf_op jit(solution)/shard_map/convert_element_type | solution.py:19
  48.7 1.6 copy-done.5
  51.3 5.6 %fusion.19 = f32[512,4096]{1,0:T(8,128)S(1)} fusion(bf16[512,1280]{1,0:T(8,128)(2,1)S(1)} %pad_maximum_fusion, bf16[1280,4096]{1,0:T(8,128)(2,1)S(1)} %bitcast.102), kind=kOutput, calls=%fused_computation.75 | convolution fusion | flops 5368709120 | bytes 20185088 | tf_op jit(solution)/shard_map/dot_general | solution.py:176
  56.9 3.2 %copy-done.4 = f32[512,4096]{1,0:T(8,128)} copy-done((f32[512,4096]{1,0:T(8,128)}, f32[512,4096]{1,0:T(8,128)S(1)}, u32[]{:S(2)}) %copy-start.4) | copy-done | bytes 8388632
  60.1 1.9 multiply_convert_fusion.2
  62.0 1.3 collective-permute-start.4
  64.0 1.7 collective-permute-start.6
  65.7 22.6 %collective-permute-start.7 = (bf16[256,1280]{1,0:T(8,128)(2,1)}, bf16[256,1280]{1,0:T(8,128)(2,1)S(1)}, u32[]{:S(2)}, u32[]{:S(2)}) collective-permute-start(bf16[256,1280]{1,0:T(8,128)(2,1)} %bitcast.91), channel_id=1, source_target_pairs={{0,8},{1,12},{4,9},{5,13},{10,2},{11,6},{14,3},{15,7},{16,24},{17,... | collective-permute-start | bytes 1966088 | tf_op jit(solution)/shard_map/ppermute | solution.py:65
  88.4 2.4 %add_bitcast_fusion.1 = f32[1,256,2048]{2,1,0:T(8,128)S(1)} fusion(f16[256,2048]{1,0:T(8,128)(2,1)} %collective-permute-done.8, f32[512,4096]{1,0:T(8,128)} %copy-done.5, s32[]{:T(128)S(6)} %select_n.63), kind=kLoop, calls=%fused_computation.16 | loop fusion | flops 1572864 | bytes 5242884 | tf_op jit(solution)/shard_map/stack | solution.py:216
  90.8 2.4 %add_bitcast_fusion = f32[1,256,2048]{2,1,0:T(8,128)S(1)} fusion(f16[256,2048]{1,0:T(8,128)(2,1)} %collective-permute-done.9, f32[512,4096]{1,0:T(8,128)} %copy-done.4, s32[]{:T(128)S(6)} %select_n.63), kind=kLoop, calls=%fused_computation.14 | loop fusion | flops 1572864 | bytes 5242884 | tf_op jit(solution)/shard_map/stack | solution.py:216
  93.2 2.0 fusion
  95.2 1.4 collective-permute-done.4
  96.6 7.0 %collective-permute-done.7 = bf16[256,1280]{1,0:T(8,128)(2,1)S(1)} collective-permute-done((bf16[256,1280]{1,0:T(8,128)(2,1)}, bf16[256,1280]{1,0:T(8,128)(2,1)S(1)}, u32[]{:S(2)}, u32[]{:S(2)}) %collective-permute-start.7) | collective-permute-done | bytes 655392 | tf_op jit(solution)/shard_map/ppermute | solution.py:65
  103.9 7.5 %shard_map.113 = f32[512,4096]{1,0:T(8,128)S(1)} custom-call(bf16[512,1280]{1,0:T(8,128)(2,1)S(1)} %pad_maximum_fusion.1.tokens_ref, bf16[4096,1280]{1,0:T(8,128)(2,1)S(1)} %bitcast.85), custom_call_target="tpu_custom_call" | custom-call | flops 1 | bytes 1 | tf_op jit(solution)/shard_map/pallas_call | solution.py:98
  111.4 3.3 %copy-done.1 = f32[512,4096]{1,0:T(8,128)} copy-done((f32[512,4096]{1,0:T(8,128)}, f32[512,4096]{1,0:T(8,128)S(1)}, u32[]{:S(2)}) %copy-start.1) | copy-done | bytes 8388632
  114.7 1.2 multiply_convert_fusion.4
  116.0 1.8 fusion.18
  117.7 2.0 copy.21.refs_2_
  121.4 3.3 %multiply_convert_fusion.3 = f16[256,2048]{1,0:T(8,128)(2,1)} fusion(f16[256,2048]{1,0:T(8,128)(2,1)} %collective-permute-done.12, f32[512,4096]{1,0:T(8,128)} %copy-done.1, s32[]{:T(128)S(6)} %select_n.63), kind=kLoop, calls=%fused_computation.11 | loop fusion | flops 2621440 | bytes 4194308 | tf_op jit(solution)/shard_map/convert_element_type | solution.py:19
  124.7 13.1 %collective-permute-start.13 = (f16[256,2048]{1,0:T(8,128)(2,1)}, f16[256,2048]{1,0:T(8,128)(2,1)}, u32[]{:S(2)}, u32[]{:S(2)}) collective-permute-start(f16[256,2048]{1,0:T(8,128)(2,1)} %multiply_convert_fusion.3), channel_id=1, source_target_pairs={{0,2},{2,0},{1,3},{3,1},{4,6},{6,4},{5,7},{7,5},{8,10},{10,8},{9,1... | collective-permute-start | bytes 3145736 | tf_op jit(solution)/shard_map/ppermute | solution.py:15
  137.8 30.7 %all-reduce.2.cloned.1.call-done = f32[256,192]{0,1:T(8,128)} async-done(((f32[256,192]{0,1:T(8,128)}), f32[256,192]{0,1:T(8,128)}) %all-reduce.2.cloned.1.call-update) | async-done | bytes 196624 | tf_op jit(solution)/shard_map/psum | solution.py:212
  169.8 1.8 multiply_convert_fusion.5
  171.7 5.0 %fusion.1 = (f32[256,2048]{1,0:T(8,128)S(1)}, f32[256,2048]{1,0:T(8,128)S(1)}) fusion(f16[2,256,2048]{2,1,0:T(8,128)(2,1)} %collective-permute-done.10, f16[256,2048]{1,0:T(8,128)(2,1)} %collective-permute-done.15, f32[512,4096]{1,0:T(8,128)} %copy-done.5, s32[]{:T(128)S(6)} %select_n.63, f16[256,2048]{1,0:T(8,128)(2,1)} %collective-permute-done.14, ...), kind=kLoop, calls=%fused_computation.7 | loop fusion | flops 11010048 | bytes 12582916 | tf_op jit(solution)/shard_map/mul | solution.py:244
  176.7 3.0 %fusion.2 = f32[256,64]{0,1:T(8,128)S(1)} fusion(f32[256,2048]{1,0:T(8,128)S(1)} %get-tuple-element.28.refs_1_, f16[256,2048]{1,0:T(8,128)(2,1)} %collective-permute-done.14, f32[512,4096]{1,0:T(8,128)} %copy-done.4, s32[]{:T(128)S(6)} %select_n.63, f16[2,256,2048]{2,1,0:T(8,128)(2,1)} %collective-permute-done.10, bf16[4096,192]{0,1:T(8,128)(2,1)} %param.16, ...), kind=kOutput, calls=%fused_computation.22 | convolution fusion | flops 71303168 | bytes 6620672 | tf_op jit(solution)/shard_map/dot_general | solution.py:247
  180.2 2.5 %multiply_add_fusion.down_ref = f32[256,2048]{1,0:T(8,128)S(1)} fusion(f16[256,2048]{1,0:T(8,128)(2,1)} %collective-permute-done.13, f16[256,2048]{1,0:T(8,128)(2,1)S(1)} %collective-permute-done.11, f32[512,4096]{1,0:T(8,128)} %copy-done.1, s32[]{:T(128)S(6)} %select_n.63), kind=kLoop, calls=%fused_computation.10 | loop fusion | flops 3145728 | bytes 6291460 | tf_op jit(solution)/shard_map/add | solution.py:242
  182.7 1.3 shard_map.114
  184.0 1.4 collective-permute-start.16
  185.4 1.3 collective-permute-start.17
  186.8 2.3 %collective-permute-start.18 = (f32[6,16,64]{2,1,0:T(8,128)S(1)}, f32[6,16,64]{2,1,0:T(8,128)}, u32[]{:S(2)}, u32[]{:S(2)}) collective-permute-start(f32[6,16,64]{2,1,0:T(8,128)S(1)} %get-tuple-element.39), channel_id=1, source_target_pairs={{0,12},{4,0},{8,4},{12,8},{1,13},{5,1},{9,5},{13,9},{2,14},{6,2},{... | collective-permute-start | bytes 73736 | tf_op jit(solution)/shard_map/ppermute | solution.py:15
  189.1 1.5 collective-permute-start.25
  190.6 1.7 collective-permute-done.17
  193.2 1.5 collective-permute-start.19
  195.1 2.3 %collective-permute-done.19 = f32[6,16,64]{2,1,0:T(8,128)S(1)} collective-permute-done((f32[6,16,64]{2,1,0:T(8,128)S(1)}, f32[6,16,64]{2,1,0:T(8,128)S(1)}, u32[]{:S(2)}, u32[]{:S(2)}) %collective-permute-start.19) | collective-permute-done | bytes 24608 | tf_op jit(solution)/shard_map/ppermute | solution.py:267
  197.4 1.1 collective-permute-done.20
  198.7 1.3 fusion.20
  200.0 2.9 %collective-permute-start.22 = (f32[4,512]{1,0:T(4,128)S(1)}, f32[4,512]{1,0:T(4,128)S(1)}, u32[]{:S(2)}, u32[]{:S(2)}) collective-permute-start(f32[4,512]{1,0:T(4,128)S(1)} %fusion.20), channel_id=1, source_target_pairs={{0,12},{4,0},{8,4},{12,8},{1,13},{5,1},{9,5},{13,9},{2,14},{6,2},{... | collective-permute-start | bytes 24584 | tf_op jit(solution)/shard_map/ppermute | solution.py:15
  204.2 3.3 %collective-permute-done.23 = f32[4,512]{1,0:T(4,128)S(1)} collective-permute-done((f32[4,512]{1,0:T(4,128)S(1)}, f32[4,512]{1,0:T(4,128)S(1)}, u32[]{:S(2)}, u32[]{:S(2)}) %collective-permute-start.23) | collective-permute-done | bytes 8224 | tf_op jit(solution)/shard_map/ppermute | solution.py:15
  207.5 1.1 collective-permute-done.24
  (94 shorter events, 10.7 us)
Async XLA Ops:
  7.2 191.5 %copy-start = (bf16[3,16,64,512]{3,2,1,0:T(8,128)(2,1)S(1)}, bf16[3,16,64,512]{3,2,1,0:T(8,128)(2,1)}, u32[]{:S(2)}) copy-start(bf16[3,16,64,512]{3,2,1,0:T(8,128)(2,1)} %param.17) | copy-start | bytes 9437188
  7.2 161.3 %all-reduce.2.cloned.1.call-start = ((), (), s32[]{:S(2)}) async-start(), calls=%async_computation | async-start | bytes 393216 | tf_op jit(solution)/shard_map/psum | solution.py:212
  7.2 20.4 %collective-permute-start = (bf16[256,1280]{1,0:T(8,128)(2,1)}, bf16[256,1280]{1,0:T(8,128)(2,1)}, u32[]{:S(2)}, u32[]{:S(2)}) collective-permute-start(bf16[256,1280]{1,0:T(8,128)(2,1)} %bitcast.92), channel_id=1, source_target_pairs={{2,0},{3,4},{6,1},{7,5},{8,10},{9,14},{12,11},{13,15},{18,16},{19,... | collective-permute-start | bytes 1966088 | tf_op jit(solution)/shard_map/ppermute | solution.py:65
  8.8 18.8 %collective-permute-start.1 = (bf16[256,1280]{1,0:T(8,128)(2,1)}, bf16[256,1280]{1,0:T(8,128)(2,1)}, u32[]{:S(2)}, u32[]{:S(2)}) collective-permute-start(bf16[256,1280]{1,0:T(8,128)(2,1)} %bitcast.93), channel_id=1, source_target_pairs={{2,8},{3,12},{6,9},{7,13},{8,2},{9,6},{12,3},{13,7},{18,24},{19,28... | collective-permute-start | bytes 1966088 | tf_op jit(solution)/shard_map/ppermute | solution.py:65
  10.3 17.3 %collective-permute-start.2 = (bf16[256,1280]{1,0:T(8,128)(2,1)}, bf16[256,1280]{1,0:T(8,128)(2,1)}, u32[]{:S(2)}, u32[]{:S(2)}) collective-permute-start(bf16[256,1280]{1,0:T(8,128)(2,1)} %bitcast.94), channel_id=1, source_target_pairs={{0,0},{1,4},{4,1},{5,5},{10,10},{11,14},{14,11},{15,15},{16,16},{1... | collective-permute-start | bytes 1966088 | tf_op jit(solution)/shard_map/ppermute | solution.py:65
  16.8 19.4 %collective-permute-start.3 = (bf16[256,1280]{1,0:T(8,128)(2,1)}, bf16[256,1280]{1,0:T(8,128)(2,1)}, u32[]{:S(2)}, u32[]{:S(2)}) collective-permute-start(bf16[256,1280]{1,0:T(8,128)(2,1)} %bitcast.95), channel_id=1, source_target_pairs={{0,8},{1,12},{4,9},{5,13},{10,2},{11,6},{14,3},{15,7},{16,24},{17,... | collective-permute-start | bytes 1966088 | tf_op jit(solution)/shard_map/ppermute | solution.py:65
  37.7 13.6 %slice-start.3 = ((s8[10485760]{0:T(1024)(128)(4,1)}), s8[4194304]{0:T(1024)(128)(4,1)S(1)}, s32[]{:S(2)}) async-start(s8[10485760]{0:T(1024)(128)(4,1)} %bitcast.101), calls=%async_computation.4 | async-start | bytes 8388608
  37.8 13.5 %slice-start.4 = ((s8[10485760]{0:T(1024)(128)(4,1)}), s8[4194304]{0:T(1024)(128)(4,1)S(1)}, s32[]{:S(2)}) async-start(s8[10485760]{0:T(1024)(128)(4,1)} %bitcast.101), calls=%async_computation.5 | async-start | bytes 8388608
  37.8 13.5 %slice-start.5 = ((s8[10485760]{0:T(1024)(128)(4,1)}), s8[2097152]{0:T(1024)(128)(4,1)S(1)}, s32[]{:S(2)}) async-start(s8[10485760]{0:T(1024)(128)(4,1)} %bitcast.101), calls=%async_computation.6 | async-start | bytes 4194304
  46.4 3.9 %copy-start.5 = (f32[512,4096]{1,0:T(8,128)}, f32[512,4096]{1,0:T(8,128)S(1)}, u32[]{:S(2)}) copy-start(f32[512,4096]{1,0:T(8,128)S(1)} %fusion.17) | copy-start | bytes 25165828
  50.3 15.5 %collective-permute-start.8 = (f16[256,2048]{1,0:T(8,128)(2,1)}, f16[256,2048]{1,0:T(8,128)(2,1)}, u32[]{:S(2)}, u32[]{:S(2)}) collective-permute-start(f16[256,2048]{1,0:T(8,128)(2,1)} %get-tuple-element.31), channel_id=1, source_target_pairs={{0,1},{1,0},{2,3},{3,2},{4,5},{5,4},{6,7},{7,6},{8,9},{9,8},{10,11... | collective-permute-start | bytes 3145736 | tf_op jit(solution)/shard_map/ppermute | solution.py:15
  56.9 3.2 %copy-start.4 = (f32[512,4096]{1,0:T(8,128)}, f32[512,4096]{1,0:T(8,128)S(1)}, u32[]{:S(2)}) copy-start(f32[512,4096]{1,0:T(8,128)S(1)} %fusion.19) | copy-start | bytes 25165828
  62.0 28.8 %collective-permute-start.9 = (f16[256,2048]{1,0:T(8,128)(2,1)}, f16[256,2048]{1,0:T(8,128)(2,1)}, u32[]{:S(2)}, u32[]{:S(2)}) collective-permute-start(f16[256,2048]{1,0:T(8,128)(2,1)} %get-tuple-element.33), channel_id=1, source_target_pairs={{0,1},{1,0},{2,3},{3,2},{4,5},{5,4},{6,7},{7,6},{8,9},{9,8},{10,11... | collective-permute-start | bytes 3145736 | tf_op jit(solution)/shard_map/ppermute | solution.py:15
  62.0 34.6 %collective-permute-start.4 = (bf16[256,1280]{1,0:T(8,128)(2,1)}, bf16[256,1280]{1,0:T(8,128)(2,1)S(1)}, u32[]{:S(2)}, u32[]{:S(2)}) collective-permute-start(bf16[256,1280]{1,0:T(8,128)(2,1)} %bitcast.88), channel_id=1, source_target_pairs={{2,0},{3,4},{6,1},{7,5},{8,10},{9,14},{12,11},{13,15},{18,16},{19,... | collective-permute-start | bytes 1966088 | tf_op jit(solution)/shard_map/ppermute | solution.py:65
  63.3 33.3 %collective-permute-start.5 = (bf16[256,1280]{1,0:T(8,128)(2,1)}, bf16[256,1280]{1,0:T(8,128)(2,1)S(1)}, u32[]{:S(2)}, u32[]{:S(2)}) collective-permute-start(bf16[256,1280]{1,0:T(8,128)(2,1)} %bitcast.89), channel_id=1, source_target_pairs={{2,8},{3,12},{6,9},{7,13},{8,2},{9,6},{12,3},{13,7},{18,24},{19,28... | collective-permute-start | bytes 1966088 | tf_op jit(solution)/shard_map/ppermute | solution.py:65
  64.0 32.6 %collective-permute-start.6 = (bf16[256,1280]{1,0:T(8,128)(2,1)}, bf16[256,1280]{1,0:T(8,128)(2,1)S(1)}, u32[]{:S(2)}, u32[]{:S(2)}) collective-permute-start(bf16[256,1280]{1,0:T(8,128)(2,1)} %bitcast.90), channel_id=1, source_target_pairs={{0,0},{1,4},{4,1},{5,5},{10,10},{11,14},{14,11},{15,15},{16,16},{1... | collective-permute-start | bytes 1966088 | tf_op jit(solution)/shard_map/ppermute | solution.py:65
  65.7 37.8 %collective-permute-start.7 = (bf16[256,1280]{1,0:T(8,128)(2,1)}, bf16[256,1280]{1,0:T(8,128)(2,1)S(1)}, u32[]{:S(2)}, u32[]{:S(2)}) collective-permute-start(bf16[256,1280]{1,0:T(8,128)(2,1)} %bitcast.91), channel_id=1, source_target_pairs={{0,8},{1,12},{4,9},{5,13},{10,2},{11,6},{14,3},{15,7},{16,24},{17,... | collective-permute-start | bytes 1966088 | tf_op jit(solution)/shard_map/ppermute | solution.py:65
  88.4 15.4 %slice-start = ((s8[10485760]{0:T(1024)(128)(4,1)}), s8[4194304]{0:T(1024)(128)(4,1)S(1)}, s32[]{:S(2)}) async-start(s8[10485760]{0:T(1024)(128)(4,1)} %bitcast.84), calls=%async_computation.1 | async-start | bytes 8388608
  90.8 13.1 %slice-start.1 = ((s8[10485760]{0:T(1024)(128)(4,1)}), s8[4194304]{0:T(1024)(128)(4,1)S(1)}, s32[]{:S(2)}) async-start(s8[10485760]{0:T(1024)(128)(4,1)} %bitcast.84), calls=%async_computation.2 | async-start | bytes 8388608
  93.2 10.7 %slice-start.2 = ((s8[10485760]{0:T(1024)(128)(4,1)}), s8[2097152]{0:T(1024)(128)(4,1)S(1)}, s32[]{:S(2)}) async-start(s8[10485760]{0:T(1024)(128)(4,1)} %bitcast.84), calls=%async_computation.3 | async-start | bytes 4194304
  95.2 73.3 %collective-permute-start.10 = (f16[2,256,2048]{2,1,0:T(8,128)(2,1)}, f16[2,256,2048]{2,1,0:T(8,128)(2,1)}, u32[]{:S(2)}, u32[]{:S(2)}) collective-permute-start(f16[2,256,2048]{2,1,0:T(8,128)(2,1)} %fusion), channel_id=1, source_target_pairs={{0,2},{2,0},{1,3},{3,1},{4,6},{6,4},{5,7},{7,5},{8,10},{10,8},{9,1... | collective-permute-start | bytes 6291464 | tf_op jit(solution)/shard_map/ppermute | solution.py:15
  111.4 3.3 %copy-start.1 = (f32[512,4096]{1,0:T(8,128)}, f32[512,4096]{1,0:T(8,128)S(1)}, u32[]{:S(2)}) copy-start(f32[512,4096]{1,0:T(8,128)S(1)} %shard_map.113) | copy-start | bytes 25165828
  115.9 4.8 %copy-start.7 = (s32[2]{0:T(128)S(1)}, s32[2]{0:T(128)}, u32[]{:S(2)}) copy-start(s32[2]{0:T(128)} %param.18) | copy-start | bytes 28
  115.9 5.5 %collective-permute-start.12 = (f16[256,2048]{1,0:T(8,128)(2,1)}, f16[256,2048]{1,0:T(8,128)(2,1)}, u32[]{:S(2)}, u32[]{:S(2)}) collective-permute-start(f16[256,2048]{1,0:T(8,128)(2,1)} %multiply_convert_fusion.4), channel_id=1, source_target_pairs={{0,1},{1,0},{2,3},{3,2},{4,5},{5,4},{6,7},{7,6},{8,9},{9,8},{10,11... | collective-permute-start | bytes 3145736 | tf_op jit(solution)/shard_map/ppermute | solution.py:15
  120.8 50.9 %collective-permute-start.14 = (f16[256,2048]{1,0:T(8,128)(2,1)}, f16[256,2048]{1,0:T(8,128)(2,1)}, u32[]{:S(2)}, u32[]{:S(2)}) collective-permute-start(f16[256,2048]{1,0:T(8,128)(2,1)} %get-tuple-element.32), channel_id=1, source_target_pairs={{0,1},{1,0},{2,3},{3,2},{4,5},{5,4},{6,7},{7,6},{8,9},{9,8},{10,11... | collective-permute-start | bytes 3145736 | tf_op jit(solution)/shard_map/ppermute | solution.py:15
  121.3 50.4 %collective-permute-start.15 = (f16[256,2048]{1,0:T(8,128)(2,1)}, f16[256,2048]{1,0:T(8,128)(2,1)}, u32[]{:S(2)}, u32[]{:S(2)}) collective-permute-start(f16[256,2048]{1,0:T(8,128)(2,1)} %get-tuple-element.30), channel_id=1, source_target_pairs={{0,1},{1,0},{2,3},{3,2},{4,5},{5,4},{6,7},{7,6},{8,9},{9,8},{10,11... | collective-permute-start | bytes 3145736 | tf_op jit(solution)/shard_map/ppermute | solution.py:15
  124.7 55.4 %collective-permute-start.13 = (f16[256,2048]{1,0:T(8,128)(2,1)}, f16[256,2048]{1,0:T(8,128)(2,1)}, u32[]{:S(2)}, u32[]{:S(2)}) collective-permute-start(f16[256,2048]{1,0:T(8,128)(2,1)} %multiply_convert_fusion.3), channel_id=1, source_target_pairs={{0,2},{2,0},{1,3},{3,1},{4,6},{6,4},{5,7},{7,5},{8,10},{10,8},{9,1... | collective-permute-start | bytes 3145736 | tf_op jit(solution)/shard_map/ppermute | solution.py:15
  171.6 8.5 %collective-permute-start.11 = (f16[256,2048]{1,0:T(8,128)(2,1)S(1)}, f16[256,2048]{1,0:T(8,128)(2,1)S(1)}, u32[]{:S(2)}, u32[]{:S(2)}) collective-permute-start(f16[256,2048]{1,0:T(8,128)(2,1)S(1)} %multiply_convert_fusion.5), channel_id=1, source_target_pairs={{0,1},{1,0},{2,3},{3,2},{4,5},{5,4},{6,7},{7,6},{8,9},{9,8},{10,11... | collective-permute-start | bytes 3145736 | tf_op jit(solution)/shard_map/ppermute | solution.py:15
  180.1 2.6 %copy-start.2 = (bf16[2048,64]{1,0:T(8,128)(2,1)S(1)}, bf16[2048,64]{1,0:T(8,128)(2,1)}, u32[]{:S(2)}) copy-start(bf16[2048,64]{1,0:T(8,128)(2,1)} %copy.21.refs_2_) | copy-start | bytes 786436
  180.1 2.6 %copy-start.3 = (bf16[2048,64]{1,0:T(8,128)(2,1)S(1)}, bf16[2048,64]{1,0:T(8,128)(2,1)}, u32[]{:S(2)}) copy-start(bf16[2048,64]{1,0:T(8,128)(2,1)} %copy.22.refs_3_) | copy-start | bytes 786436
  182.7 6.4 %copy-start.6 = (s32[2]{0:T(128)S(1)}, s32[2]{0:T(128)}, u32[]{:S(2)}) copy-start(s32[2]{0:T(128)} %param.19) | copy-start | bytes 28
  184.0 6.6 %collective-permute-start.16 = (f32[6,16,64]{2,1,0:T(8,128)S(1)}, f32[6,16,64]{2,1,0:T(8,128)S(1)}, u32[]{:S(2)}, u32[]{:S(2)}) collective-permute-start(f32[6,16,64]{2,1,0:T(8,128)S(1)} %get-tuple-element.38), channel_id=1, source_target_pairs={{0,4},{4,8},{8,12},{12,0},{1,5},{5,9},{9,13},{13,1},{2,6},{6,10},{... | collective-permute-start | bytes 73736 | tf_op jit(solution)/shard_map/ppermute | solution.py:15
  185.4 6.8 %collective-permute-start.17 = (f32[6,16,64]{2,1,0:T(8,128)S(1)}, f32[6,16,64]{2,1,0:T(8,128)}, u32[]{:S(2)}, u32[]{:S(2)}) collective-permute-start(f32[6,16,64]{2,1,0:T(8,128)S(1)} %get-tuple-element.40), channel_id=1, source_target_pairs={{0,8},{4,12},{8,0},{12,4},{1,9},{5,13},{9,1},{13,5},{2,10},{6,14},... | collective-permute-start | bytes 73736 | tf_op jit(solution)/shard_map/ppermute | solution.py:15
  186.8 5.5 %collective-permute-start.18 = (f32[6,16,64]{2,1,0:T(8,128)S(1)}, f32[6,16,64]{2,1,0:T(8,128)}, u32[]{:S(2)}, u32[]{:S(2)}) collective-permute-start(f32[6,16,64]{2,1,0:T(8,128)S(1)} %get-tuple-element.39), channel_id=1, source_target_pairs={{0,12},{4,0},{8,4},{12,8},{1,13},{5,1},{9,5},{13,9},{2,14},{6,2},{... | collective-permute-start | bytes 73736 | tf_op jit(solution)/shard_map/ppermute | solution.py:15
  189.1 4.1 %collective-permute-start.25 = (s32[2]{0:T(128)S(1)}, s32[2]{0:T(128)S(1)}, u32[]{:S(2)}, u32[]{:S(2)}) collective-permute-start(s32[2]{0:T(128)S(1)} %copy-done.6), channel_id=1, source_target_pairs={{0,2},{2,0},{1,3},{3,1},{4,6},{6,4},{5,7},{7,5},{8,10},{10,8},{9,1... | collective-permute-start | bytes 32 | tf_op jit(solution)/shard_map/ppermute | solution.py:15
  193.1 2.0 collective-permute-start.21
  193.2 4.2 %collective-permute-start.19 = (f32[6,16,64]{2,1,0:T(8,128)S(1)}, f32[6,16,64]{2,1,0:T(8,128)S(1)}, u32[]{:S(2)}, u32[]{:S(2)}) collective-permute-start(f32[6,16,64]{2,1,0:T(8,128)S(1)} %fusion.12), channel_id=1, source_target_pairs={{0,2},{1,3},{2,0},{3,1},{4,6},{5,7},{6,4},{7,5},{8,10},{9,11},{10,... | collective-permute-start | bytes 73736 | tf_op jit(solution)/shard_map/ppermute | solution.py:267
  194.8 3.7 %collective-permute-start.20 = (f32[6,16,64]{2,1,0:T(8,128)S(1)}, f32[6,16,64]{2,1,0:T(8,128)S(1)}, u32[]{:S(2)}, u32[]{:S(2)}) collective-permute-start(f32[6,16,64]{2,1,0:T(8,128)S(1)} %fusion.12), channel_id=1, source_target_pairs={{0,3},{1,2},{2,1},{3,0},{4,7},{5,6},{6,5},{7,4},{8,11},{9,10},{10,... | collective-permute-start | bytes 73736 | tf_op jit(solution)/shard_map/ppermute | solution.py:267
  200.0 4.2 %collective-permute-start.22 = (f32[4,512]{1,0:T(4,128)S(1)}, f32[4,512]{1,0:T(4,128)S(1)}, u32[]{:S(2)}, u32[]{:S(2)}) collective-permute-start(f32[4,512]{1,0:T(4,128)S(1)} %fusion.20), channel_id=1, source_target_pairs={{0,12},{4,0},{8,4},{12,8},{1,13},{5,1},{9,5},{13,9},{2,14},{6,2},{... | collective-permute-start | bytes 24584 | tf_op jit(solution)/shard_map/ppermute | solution.py:15
  202.9 4.5 %collective-permute-start.23 = (f32[4,512]{1,0:T(4,128)S(1)}, f32[4,512]{1,0:T(4,128)S(1)}, u32[]{:S(2)}, u32[]{:S(2)}) collective-permute-start(f32[4,512]{1,0:T(4,128)S(1)} %fusion.20), channel_id=1, source_target_pairs={{0,8},{4,12},{8,0},{12,4},{1,9},{5,13},{9,1},{13,5},{2,10},{6,14},... | collective-permute-start | bytes 24584 | tf_op jit(solution)/shard_map/ppermute | solution.py:15
  203.1 5.4 %collective-permute-start.24 = (f32[4,512]{1,0:T(4,128)S(1)}, f32[4,512]{1,0:T(4,128)S(1)}, u32[]{:S(2)}, u32[]{:S(2)}) collective-permute-start(f32[4,512]{1,0:T(4,128)S(1)} %fusion.20), channel_id=1, source_target_pairs={{0,4},{4,8},{8,12},{12,0},{1,5},{5,9},{9,13},{13,1},{2,6},{6,10},{... | collective-permute-start | bytes 24584 | tf_op jit(solution)/shard_map/ppermute | solution.py:15
Sparse Core Ops, SparseCore 0:
  121.5 46.9 all-reduce.1

commit v9 on v8

--- a/solution.py
+++ b/solution.py
@@ -66,13 +66,10 @@
     return pieces
 
 
-def arrived_features(far, near, *earlier):
-    pieces = lax.optimization_barrier((*far, *near, *earlier))[:4]
+def arrived_features(pieces, *earlier):
+    pieces = lax.optimization_barrier((*pieces, *earlier))
     holder = lax.axis_index("example") * 2 + lax.axis_index("test")
-    first = (lax.axis_index("tensor") ^ holder) < 2
-    return jnp.concatenate(
-        [jnp.where(first, pieces[0], pieces[1]), jnp.where(first, pieces[2], pieces[3])]
-    )
+    return jnp.where((lax.axis_index("tensor") ^ holder) < 2, pieces[0], pieces[1])
 
 
 def gathered_features(flat, n_ex, n_cores):
@@ -81,8 +78,8 @@
     mine = lax.dynamic_slice_in_dim(flat, lax.axis_index("test") * part, part, 0)
     whole = lax.all_gather(mine, "tensor", axis=1, tiled=True)
     whole = lax.all_to_all(whole, ("example", "test"), split_axis=1, concat_axis=0, tiled=True)
-    begin = lax.rem(lax.axis_index("example") + 1, n_ex) * rows
-    return lax.dynamic_slice_in_dim(jnp.concatenate([whole, whole]), begin, n_ex * rows, 0)
+    owners = [lax.rem(lax.axis_index("example") + step, n_ex) for step in range(n_ex)]
+    return [lax.dynamic_slice_in_dim(whole, owner * rows, rows, 0) for owner in owners]
 
 
 def dot_rows_kernel(tokens_ref, weight_ref, out_ref):
@@ -135,11 +132,10 @@
         out_ref[:, 3 * e + 2] = hidden_ref[e]
 
 
-def gradients(d_hidden, factors, hid_proj, model, hidden_grads, n_z):
-    width = hid_proj.shape[1] // 3
+def gradients(d_hidden, factors, projs, model, hidden_grads, n_z):
+    width = projs[0].shape[1]
     rows, hidden = d_hidden.shape
     ex_loc = model.shape[0]
-    projs = [hid_proj[:, :width], hid_proj[:, width : 2 * width]]
     return pl.pallas_call(
         gradients_kernel,
         out_shape=jax.ShapeDtypeStruct((n_z, 3 * ex_loc, width // n_z, width), F32),
@@ -175,60 +171,71 @@
     def forward(tokens, weight):
         return jnp.dot(tokens, weight, preferred_element_type=F32)
 
-    def core_sum(product, step):
-        begin = (step - 1) % n_ex * tok_rows
-
+    def core_sum(product, begin, *earlier):
         def share_of(index):
             return lax.dynamic_slice(product, (begin, index * hid_part), (tok_rows, hid_part))
 
         kept = share_of(core)
-        for core_step in range(1, n_cores):
-            sent = pack(share_of(lax.rem(core + core_step, n_cores)))
-            kept = kept + unpack(shift(sent, "test", core_step))
+        for step in range(1, n_cores):
+            sent = pack(share_of(lax.rem(core + step, n_cores)))
+            kept = kept + unpack(after(shift(sent, "test", step), *earlier))
         return kept
 
     flat_acts = activations.reshape(tok_rows, d_local)
     flat_grad = out_grad.reshape(tok_rows, d_local)
-    model_part = jnp.concatenate(
-        [
-            jnp.dot(flat_acts, proj_model[:, : 2 * width], preferred_element_type=F32),
-            jnp.dot(flat_grad, proj_model[:, 2 * width :], preferred_element_type=F32),
-        ],
-        1,
-    )
+    model_acts = jnp.dot(flat_acts, proj_model[:, : 2 * width], preferred_element_type=F32)
+    model_grad = jnp.dot(flat_grad, proj_model[:, 2 * width :], preferred_element_type=F32)
+    model_part = jnp.concatenate([model_acts, model_grad], 1)
+
+    hid_proj = lax.dynamic_slice_in_dim(proj_hidden, core * hid_part, hid_part, 0)
+    projs = [hid_proj[:, layer * width : (layer + 1) * width] for layer in range(3)]
+    positions = jnp.arange(seq_len, dtype=jnp.int32)
+    token_mask = (positions[None, :] < lengths[:, None]).astype(F32)
+    early = (model_acts, model_grad, token_mask, *projs)
 
     direct = (n_z, n_ex, n_cores) == (4, 2, 2)
     examples = [slice(e * seq_len, (e + 1) * seq_len) for e in range(ex_loc)]
     arrived, arrived_down = [], []
     if direct:
-        acts_all = arrived_features(
-            spread_features(flat_acts, 1), spread_features(flat_acts, 0), model_part
-        )
-        grad_ready = after(flat_grad, acts_all)
-        grad_all = spread_features(grad_ready, 1), spread_features(grad_ready, 0)
+        acts_far = [arrived_features(spread_features(flat_acts, 1), *early)]
+        acts_near = spread_features(flat_acts, 0)
     else:
-        acts_all = gathered_features(flat_acts, n_ex, n_cores)
-        grad_all = gathered_features(flat_grad, n_ex, n_cores)
-    model_sum = lax.psum(after(model_part, acts_all), "tensor")
-    gate_all = forward(acts_all, w_gate)
-    up_all = forward(after(acts_all, gate_all), w_up)
-    for step in range(1, n_ex):
-        both = pack(jnp.stack([core_sum(gate_all, step), core_sum(up_all, step)]))
+        acts_near, *acts_far = gathered_features(flat_acts, n_ex, n_cores)
+        grad_near, *grad_far = gathered_features(flat_grad, n_ex, n_cores)
+    gate_far = [forward(one, w_gate) for one in acts_far]
+    up_far = [forward(after(one, *gate_far), w_up) for one in acts_far]
+    if direct:
+        grad_ready = after(flat_grad, *up_far)
+        grad_far, grad_near = spread_features(grad_ready, 1), spread_features(grad_ready, 0)
+        acts_near = arrived_features(acts_near, *up_far)
+    gate_near = forward(after(acts_near, *up_far), w_gate)
+    up_near = forward(after(acts_near, gate_near), w_up)
+    for step, (gate, up) in enumerate(zip(gate_far, up_far), 1):
+        both = pack(jnp.stack([core_sum(gate, 0, up_near), core_sum(up, 0, up_near)]))
         received = shift(both, "example", step)
         arrived.append(received)
     if direct:
-        grad_all = arrived_features(*grad_all, both)
-    down_all = dot_rows(grad_all, w_down)
+        grad_far = [arrived_features(grad_far, both)]
+        grad_near = arrived_features(grad_near, both)
+    down_all = dot_rows(jnp.concatenate([*grad_far, grad_near]), w_down)
     for step in range(1, n_ex):
-        sent = pack(core_sum(down_all, step))
+        sent = pack(core_sum(down_all, (step - 1) * tok_rows))
         arrived_down.append(shift(sent, "example", step))
-    own = [core_sum(one, 0) for one in (gate_all, up_all, after(down_all, received))]
-    model_sum = after(model_sum, received)
-
-    hid_proj = lax.dynamic_slice_in_dim(proj_hidden, core * hid_part, hid_part, 0)
-    positions = jnp.arange(seq_len, dtype=jnp.int32)
-    token_mask = (positions[None, :] < lengths[:, None]).astype(F32)[:, :, None]
-    masked = model_sum.reshape(ex_loc, seq_len, 3 * width) * token_mask
+    down_near = after(down_all, received)
+    own = [
+        core_sum(gate_near, 0),
+        core_sum(up_near, 0),
+        core_sum(down_near, (n_ex - 1) * tok_rows),
+    ]
+    if n_z > 8:
+        model_sum = lax.psum(model_part, "tensor")
+    else:
+        model_sent = after(pack(model_part), sent)
+        others = [shift(model_sent, "tensor", step) for step in range(1, n_z)]
+        others = lax.optimization_barrier((*others, received))[:-1]
+        model_sum = model_part + sum(unpack(one) for one in others)
+
+    masked = model_sum.reshape(ex_loc, seq_len, 3 * width) * token_mask[:, :, None]
 
     def outer(outputs, inputs):
         product = lax.dot_general(
@@ -244,13 +251,13 @@
     silu_gate = gate_act * sigmoid_gate
     hidden = (silu_gate * up_act).astype(jnp.bfloat16)
     gate_factor = up_act * sigmoid_gate * (1.0 + gate_act * (1.0 - sigmoid_gate))
-    in_hidden = jnp.dot(hidden, hid_proj[:, 2 * width :], preferred_element_type=F32)
+    in_hidden = jnp.dot(hidden, projs[2], preferred_element_type=F32)
     hidden_grads = jnp.stack(
         [outer(masked[e, :, 2 * width :], in_hidden[rows]) for e, rows in enumerate(examples)]
     )
     factors = [gate_factor, silu_gate]
     grads = gradients(
-        d_hidden, factors, hid_proj, masked[:, :, : 2 * width], hidden_grads, n_z
+        d_hidden, factors, projs[:2], masked[:, :, : 2 * width], hidden_grads, n_z
     )
     grads = scatter_sum(grads, "tensor")
     by_example = []

time: 218 us -> 178 us (0.82)
  waiting for transfers between devices: 59.8 us -> 34.2 us
  between operations: 14.5 us -> 1.24 us
  local copies, waits for them, and re-layouts: 15 us -> 7.95 us
  other arithmetic: 28.3 us -> 21.5 us
  matrix products: 22.7 us -> 29.1 us
  starting transfers between devices: 67.8 us -> 74 us
    psum x1 -> x0, waiting for transfers between devices: 30.7 us -> none  [on_device(): model_sum = lax.psum(after(model_part, acts_all), 'tensor')]
    ppermute x15 -> x18, waiting for transfers between devices: 6.76 us -> 20.3 us  [shift(): return lax.ppermute(value, axis, [(i, (i + step) % n) for i in range(n)])]
    ppermute x15 -> x18, starting transfers between devices: 24.7 us -> 33.8 us  [shift(): return lax.ppermute(value, axis, [(i, (i + step) % n) for i in range(n)])]
    ppermute x8, waiting for transfers between devices: 19 us -> 10.3 us  [spread_features(): pieces.append(lax.ppermute(flat, ('tensor', 'example', 'test'), pairs))]
    dot_general x2 -> x4, matrix products: 14.1 us -> 21.2 us  [forward(): return jnp.dot(tokens, weight, preferred_element_type=F32)]
    unnamed x37 -> x41, local copies, waits for them, and re-layouts: 11.2 us -> 4.16 us
    convert_element_type x6 -> x9, other arithmetic: 12.5 us -> 7.6 us  [pack(): return (value * SEND_SCALE).astype(jnp.float16)]
    another operation x2, other arithmetic: 4.74 us -> 0.83 us  [on_device(): jnp.stack([core_sum(gate, 0, up_near), core_sum(up, 0, up_near)])]
  transfers between devices with their start and end apart: 27 -> 29, of which waited for: 11 -> 14; matrix products, arithmetic and copies ran while one was open for 18% -> 29% of each run, Pallas kernels for 3% -> 4%
where the time goes in v9:
time: 178 us; the launch traced here: 177 us
  starting transfers between devices  74 us (42%)
  waiting for transfers between devices  34.2 us (19%)
  matrix products  29.1 us (16%)
  other arithmetic  21.5 us (12%)
  Pallas kernels  8.78 us (5%)
  local copies, waits for them, and re-layouts  7.95 us (4%)
    ppermute x8, starting transfers between devices, spread_features(): pieces.append(lax.ppermute(flat, ('tensor', 'example', 'test'), pairs))  38.8 us
    ppermute x18, starting transfers between devices, shift(): return lax.ppermute(value, axis, [(i, (i + step) % n) for i in range(n)])  33.8 us
    dot_general x4, matrix products, forward(): return jnp.dot(tokens, weight, preferred_element_type=F32)  21.2 us
    ppermute x18, waiting for transfers between devices, shift(): return lax.ppermute(value, axis, [(i, (i + step) % n) for i in range(n)])  20.3 us
    ppermute x8, waiting for transfers between devices, spread_features(): pieces.append(lax.ppermute(flat, ('tensor', 'example', 'test'), pairs))  10.3 us
    convert_element_type x9, other arithmetic, pack(): return (value * SEND_SCALE).astype(jnp.float16)  7.6 us
    pallas_call x1, Pallas kernels, dot_rows(): pl.pallas_call(dot_rows_kernel, out_shape=jax.ShapeDtypeStruct((rows, hid...  7.51 us
    mul x1, other arithmetic, on_device(): silu_gate = gate_act * sigmoid_gate  5.14 us
  transfers between devices with their start and end apart: 29, of which 14 were waited for; matrix products, arithmetic and copies ran while one was open for 29% of the time, Pallas kernels for 4%

profile of v9, /device:TPU:0, one launch (start us, length us, event | category | flops | bytes accessed | tf_op | source)
XLA Modules:
  0.0 176.9 jit_solution(186042579955004877)
XLA Ops:
  0.6 1.6 collective-permute-start
  2.2 1.5 collective-permute-start.1
  3.7 6.5 %collective-permute-start.5 = (bf16[256,1280]{1,0:T(8,128)(2,1)}, bf16[256,1280]{1,0:T(8,128)(2,1)}, u32[]{:S(2)}, u32[]{:S(2)}) collective-permute-start(bf16[256,1280]{1,0:T(8,128)(2,1)} %bitcast.99), channel_id=1, source_target_pairs={{0,0},{1,4},{4,1},{5,5},{10,10},{11,14},{14,11},{15,15},{16,16},{1... | collective-permute-start | bytes 1966088 | tf_op jit(solution)/shard_map/ppermute | solution.py:65
  10.2 5.1 %collective-permute-start.6 = (bf16[256,1280]{1,0:T(8,128)(2,1)}, bf16[256,1280]{1,0:T(8,128)(2,1)}, u32[]{:S(2)}, u32[]{:S(2)}) collective-permute-start(bf16[256,1280]{1,0:T(8,128)(2,1)} %bitcast.100), channel_id=1, source_target_pairs={{0,8},{1,12},{4,9},{5,13},{10,2},{11,6},{14,3},{15,7},{16,24},{17,... | collective-permute-start | bytes 1966088 | tf_op jit(solution)/shard_map/ppermute | solution.py:65
  15.4 1.8 fusion.17
  17.1 2.0 %copy.21.refs_2_ = bf16[2048,64]{1,0:T(8,128)(2,1)} copy(bf16[2048,64]{0,1:T(8,128)(2,1)} %get-tuple-element.43) | data formatting | bytes 524288
  19.1 1.0 copy.22.refs_3_
  20.1 1.4 fusion.6
  21.5 1.6 fusion.3
  23.1 1.3 broadcast_select_fusion.3
  24.5 5.7 %fusion.18 = f32[256,4096]{1,0:T(8,128)S(1)} fusion(bf16[256,1280]{1,0:T(8,128)(2,1)S(1)} %broadcast_select_fusion.3, bf16[1280,4096]{1,0:T(8,128)(2,1)} %param.12), kind=kOutput, calls=%fused_computation.75 | convolution fusion | flops 2684354560 | bytes 15335424 | tf_op jit(solution)/shard_map/dot_general | solution.py:172
  30.7 2.9 %fusion.19 = f32[256,4096]{1,0:T(8,128)S(1)} fusion(bf16[256,1280]{1,0:T(8,128)(2,1)S(1)} %broadcast_select_fusion.3, bf16[1280,4096]{1,0:T(8,128)(2,1)S(1)} %bitcast.107), kind=kOutput, calls=%fused_computation.76 | convolution fusion | flops 2684354560 | bytes 15335424 | tf_op jit(solution)/shard_map/dot_general | solution.py:172
  33.6 1.3 collective-permute-start.2
  36.7 1.2 broadcast_select_fusion.2
  37.9 3.3 %collective-permute-start.4 = (f16[256,2048]{1,0:T(8,128)(2,1)S(1)}, f16[256,2048]{1,0:T(8,128)(2,1)S(1)}, u32[]{:S(2)}, u32[]{:S(2)}) collective-permute-start(f16[256,2048]{1,0:T(8,128)(2,1)S(1)} %multiply_convert_fusion.7), channel_id=1, source_target_pairs={{0,1},{1,0},{2,3},{3,2},{4,5},{5,4},{6,7},{7,6},{8,9},{9,8},{10,11... | collective-permute-start | bytes 3145736 | tf_op jit(solution)/shard_map/ppermute | solution.py:15
  41.2 5.6 %fusion.20 = f32[256,4096]{1,0:T(8,128)S(1)} fusion(bf16[256,1280]{1,0:T(8,128)(2,1)S(1)} %broadcast_select_fusion.2, bf16[1280,4096]{1,0:T(8,128)(2,1)} %param.12), kind=kOutput, calls=%fused_computation.77 | convolution fusion | flops 2684354560 | bytes 15335424 | tf_op jit(solution)/shard_map/dot_general | solution.py:172
  46.9 7.0 %fusion.21 = f32[256,4096]{1,0:T(8,128)S(1)} fusion(bf16[256,1280]{1,0:T(8,128)(2,1)S(1)} %broadcast_select_fusion.2, bf16[1280,4096]{1,0:T(8,128)(2,1)} %param.13), kind=kOutput, calls=%fused_computation.78 | convolution fusion | flops 2684354560 | bytes 15335424 | tf_op jit(solution)/shard_map/dot_general | solution.py:172
  54.0 21.4 %collective-permute-start.9 = (bf16[256,1280]{1,0:T(8,128)(2,1)S(1)}, bf16[256,1280]{1,0:T(8,128)(2,1)S(1)}, u32[]{:S(2)}, u32[]{:S(2)}) collective-permute-start(bf16[256,1280]{1,0:T(8,128)(2,1)S(1)} %bitcast.96), channel_id=1, source_target_pairs={{0,8},{1,12},{4,9},{5,13},{10,2},{11,6},{14,3},{15,7},{16,24},{17,... | collective-permute-start | bytes 1966088 | tf_op jit(solution)/shard_map/ppermute | solution.py:65
  76.3 1.9 %fusion = f16[2,256,2048]{2,1,0:T(8,128)(2,1)} fusion(f32[1,256,2048]{2,1,0:T(8,128)S(1)} %add_bitcast_fusion, f32[1,256,2048]{2,1,0:T(8,128)S(1)} %add_bitcast_fusion.1), kind=kLoop, calls=%fused_computation.1 | loop fusion | flops 3145728 | bytes 6291456 | tf_op jit(solution)/shard_map/convert_element_type | solution.py:19
  78.2 10.3 %collective-permute-done.9 = bf16[256,1280]{1,0:T(8,128)(2,1)S(1)} collective-permute-done((bf16[256,1280]{1,0:T(8,128)(2,1)S(1)}, bf16[256,1280]{1,0:T(8,128)(2,1)S(1)}, u32[]{:S(2)}, u32[]{:S(2)}) %collective-permute-start.9) | collective-permute-done | bytes 655392 | tf_op jit(solution)/shard_map/ppermute | solution.py:65
  88.8 7.5 %shard_map.113 = f32[512,4096]{1,0:T(8,128)S(1)} custom-call(bf16[512,1280]{1,0:T(8,128)(2,1)S(1)} %pad_maximum_fusion.tokens_ref, bf16[4096,1280]{1,0:T(8,128)(2,1)S(1)} %bitcast.90), custom_call_target="tpu_custom_call" | custom-call | flops 1 | bytes 1 | tf_op jit(solution)/shard_map/pallas_call | solution.py:95
  97.4 1.6 multiply_convert_fusion.1
  99.9 1.4 multiply_convert_fusion.3
  101.3 14.2 %collective-permute-start.16 = (f16[256,192]{0,1:T(8,128)(2,1)S(1)}, f16[256,192]{0,1:T(8,128)(2,1)S(1)}, u32[]{:S(2)}, u32[]{:S(2)}) collective-permute-start(f16[256,192]{0,1:T(8,128)(2,1)S(1)} %multiply_convert_fusion.9), channel_id=1, source_target_pairs={{0,4},{4,8},{8,12},{12,0},{1,5},{5,9},{9,13},{13,1},{2,6},{6,10},{... | collective-permute-start | bytes 294920 | tf_op jit(solution)/shard_map/ppermute | solution.py:15
  115.5 1.3 collective-permute-start.17
  116.8 2.9 %collective-permute-start.18 = (f16[256,192]{0,1:T(8,128)(2,1)S(1)}, f16[256,192]{0,1:T(8,128)(2,1)}, u32[]{:S(2)}, u32[]{:S(2)}) collective-permute-start(f16[256,192]{0,1:T(8,128)(2,1)S(1)} %multiply_convert_fusion.9), channel_id=1, source_target_pairs={{0,12},{4,0},{8,4},{12,8},{1,13},{5,1},{9,5},{13,9},{2,14},{6,2},{... | collective-permute-start | bytes 294920 | tf_op jit(solution)/shard_map/ppermute | solution.py:15
  119.8 1.7 collective-permute-start.13
  121.5 2.8 %collective-permute-done.17 = f16[256,192]{0,1:T(8,128)(2,1)} collective-permute-done((f16[256,192]{0,1:T(8,128)(2,1)S(1)}, f16[256,192]{0,1:T(8,128)(2,1)}, u32[]{:S(2)}, u32[]{:S(2)}) %collective-permute-start.17) | collective-permute-done | bytes 98336 | tf_op jit(solution)/shard_map/ppermute | solution.py:15
  124.3 2.4 %collective-permute-done.10 = f16[2,256,2048]{2,1,0:T(8,128)(2,1)} collective-permute-done((f16[2,256,2048]{2,1,0:T(8,128)(2,1)}, f16[2,256,2048]{2,1,0:T(8,128)(2,1)}, u32[]{:S(2)}, u32[]{:S(2)}) %collective-permute-start.10) | collective-permute-done | bytes 2097184 | tf_op jit(solution)/shard_map/ppermute | solution.py:15
  126.8 1.7 multiply_add_fusion.1
  128.4 1.1 copy.17
  129.8 1.8 %multiply_convert_fusion.5 = f16[256,2048]{1,0:T(8,128)(2,1)S(1)} fusion(f32[512,4096]{1,0:T(8,128)} %copy-done.1, s32[]{:T(128)S(6)} %select_n.63), kind=kLoop, calls=%fused_computation.13 | loop fusion | flops 1048576 | bytes 3145732 | tf_op jit(solution)/shard_map/convert_element_type | solution.py:19
  131.7 5.1 %fusion.1 = (f32[256,2048]{1,0:T(8,128)S(1)}, f32[256,2048]{1,0:T(8,128)S(1)}) fusion(f16[2,256,2048]{2,1,0:T(8,128)(2,1)} %collective-permute-done.10, f16[256,2048]{1,0:T(8,128)(2,1)} %collective-permute-done.15, f32[256,4096]{1,0:T(8,128)} %copy-done.6, s32[]{:T(128)S(6)} %select_n.61, f16[256,2048]{1,0:T(8,128)(2,1)} %collective-permute-done.14, ...), kind=kLoop, calls=%fused_computation.7 | loop fusion | flops 11010048 | bytes 12582916 | tf_op jit(solution)/shard_map/mul | solution.py:251
  136.9 2.4 %fusion.2 = f32[256,64]{0,1:T(8,128)S(1)} fusion(f32[256,2048]{1,0:T(8,128)S(1)} %get-tuple-element.40.refs_1_, f16[256,2048]{1,0:T(8,128)(2,1)} %collective-permute-done.14, f32[256,4096]{1,0:T(8,128)S(1)} %copy-done.5, s32[]{:T(128)S(6)} %select_n.61, f16[2,256,2048]{2,1,0:T(8,128)(2,1)} %collective-permute-done.10, bf16[4096,192]{0,1:T(8,128)(2,1)} %param.16, ...), kind=kOutput, calls=%fused_computation.21 | convolution fusion | flops 71303168 | bytes 6620672 | tf_op jit(solution)/shard_map/dot_general | solution.py:254
  139.7 7.6 %collective-permute-done.13 = f16[256,2048]{1,0:T(8,128)(2,1)} collective-permute-done((f16[256,2048]{1,0:T(8,128)(2,1)}, f16[256,2048]{1,0:T(8,128)(2,1)}, u32[]{:S(2)}, u32[]{:S(2)}) %collective-permute-start.13) | collective-permute-done | bytes 1048608 | tf_op jit(solution)/shard_map/ppermute | solution.py:15
  147.2 2.5 %multiply_add_fusion.down_ref = f32[256,2048]{1,0:T(8,128)S(1)} fusion(f16[256,2048]{1,0:T(8,128)(2,1)} %collective-permute-done.13, f16[256,2048]{1,0:T(8,128)(2,1)S(1)} %collective-permute-done.11, f32[512,4096]{1,0:T(8,128)} %copy-done.1, s32[]{:T(128)S(6)} %select_n.61), kind=kLoop, calls=%fused_computation.10 | loop fusion | flops 3145728 | bytes 6291460 | tf_op jit(solution)/shard_map/add | solution.py:249
  149.7 1.3 shard_map.114
  151.2 3.1 %collective-permute-start.20 = (f32[6,16,64]{2,1,0:T(8,128)S(1)}, f32[6,16,64]{2,1,0:T(8,128)}, u32[]{:S(2)}, u32[]{:S(2)}) collective-permute-start(f32[6,16,64]{2,1,0:T(8,128)S(1)} %get-tuple-element.48), channel_id=1, source_target_pairs={{0,8},{4,12},{8,0},{12,4},{1,9},{5,13},{9,1},{13,5},{2,10},{6,14},... | collective-permute-start | bytes 73736 | tf_op jit(solution)/shard_map/ppermute | solution.py:15
  154.3 2.2 %collective-permute-start.21 = (f32[6,16,64]{2,1,0:T(8,128)S(1)}, f32[6,16,64]{2,1,0:T(8,128)}, u32[]{:S(2)}, u32[]{:S(2)}) collective-permute-start(f32[6,16,64]{2,1,0:T(8,128)S(1)} %get-tuple-element.47), channel_id=1, source_target_pairs={{0,12},{4,0},{8,4},{12,8},{1,13},{5,1},{9,5},{13,9},{2,14},{6,2},{... | collective-permute-start | bytes 73736 | tf_op jit(solution)/shard_map/ppermute | solution.py:15
  157.7 0.8 collective-permute-done.21
  158.5 0.8 fusion.12
  160.0 1.0 collective-permute-start.22
  161.4 3.0 %collective-permute-done.22 = f32[6,16,64]{2,1,0:T(8,128)S(1)} collective-permute-done((f32[6,16,64]{2,1,0:T(8,128)S(1)}, f32[6,16,64]{2,1,0:T(8,128)S(1)}, u32[]{:S(2)}, u32[]{:S(2)}) %collective-permute-start.22) | collective-permute-done | bytes 24608 | tf_op jit(solution)/shard_map/ppermute | solution.py:274
  165.1 1.3 fusion.22
  166.5 3.3 %collective-permute-start.25 = (f32[4,512]{1,0:T(4,128)S(1)}, f32[4,512]{1,0:T(4,128)S(1)}, u32[]{:S(2)}, u32[]{:S(2)}) collective-permute-start(f32[4,512]{1,0:T(4,128)S(1)} %fusion.22), channel_id=1, source_target_pairs={{0,12},{4,0},{8,4},{12,8},{1,13},{5,1},{9,5},{13,9},{2,14},{6,2},{... | collective-permute-start | bytes 24584 | tf_op jit(solution)/shard_map/ppermute | solution.py:15
  171.1 3.3 %collective-permute-done.26 = f32[4,512]{1,0:T(4,128)S(1)} collective-permute-done((f32[4,512]{1,0:T(4,128)S(1)}, f32[4,512]{1,0:T(4,128)S(1)}, u32[]{:S(2)}, u32[]{:S(2)}) %collective-permute-start.26) | collective-permute-done | bytes 8224 | tf_op jit(solution)/shard_map/ppermute | solution.py:15
  174.4 0.9 collective-permute-done.27
  175.4 0.9 fusion.14
  (105 shorter events, 11.4 us)
Async XLA Ops:
  0.6 164.5 %copy-start = (bf16[3,16,64,512]{3,2,1,0:T(8,128)(2,1)S(1)}, bf16[3,16,64,512]{3,2,1,0:T(8,128)(2,1)}, u32[]{:S(2)}) copy-start(bf16[3,16,64,512]{3,2,1,0:T(8,128)(2,1)} %param.17) | copy-start | bytes 9437188
  0.6 22.5 %collective-permute-start = (bf16[256,1280]{1,0:T(8,128)(2,1)}, bf16[256,1280]{1,0:T(8,128)(2,1)}, u32[]{:S(2)}, u32[]{:S(2)}) collective-permute-start(bf16[256,1280]{1,0:T(8,128)(2,1)} %bitcast.97), channel_id=1, source_target_pairs={{2,0},{3,4},{6,1},{7,5},{8,10},{9,14},{12,11},{13,15},{18,16},{19,... | collective-permute-start | bytes 1966088 | tf_op jit(solution)/shard_map/ppermute | solution.py:65
  2.2 20.9 %collective-permute-start.1 = (bf16[256,1280]{1,0:T(8,128)(2,1)}, bf16[256,1280]{1,0:T(8,128)(2,1)}, u32[]{:S(2)}, u32[]{:S(2)}) collective-permute-start(bf16[256,1280]{1,0:T(8,128)(2,1)} %bitcast.98), channel_id=1, source_target_pairs={{2,8},{3,12},{6,9},{7,13},{8,2},{9,6},{12,3},{13,7},{18,24},{19,28... | collective-permute-start | bytes 1966088 | tf_op jit(solution)/shard_map/ppermute | solution.py:65
  3.7 33.0 %collective-permute-start.5 = (bf16[256,1280]{1,0:T(8,128)(2,1)}, bf16[256,1280]{1,0:T(8,128)(2,1)}, u32[]{:S(2)}, u32[]{:S(2)}) collective-permute-start(bf16[256,1280]{1,0:T(8,128)(2,1)} %bitcast.99), channel_id=1, source_target_pairs={{0,0},{1,4},{4,1},{5,5},{10,10},{11,14},{14,11},{15,15},{16,16},{1... | collective-permute-start | bytes 1966088 | tf_op jit(solution)/shard_map/ppermute | solution.py:65
  10.2 26.5 %collective-permute-start.6 = (bf16[256,1280]{1,0:T(8,128)(2,1)}, bf16[256,1280]{1,0:T(8,128)(2,1)}, u32[]{:S(2)}, u32[]{:S(2)}) collective-permute-start(bf16[256,1280]{1,0:T(8,128)(2,1)} %bitcast.100), channel_id=1, source_target_pairs={{0,8},{1,12},{4,9},{5,13},{10,2},{11,6},{14,3},{15,7},{16,24},{17,... | collective-permute-start | bytes 1966088 | tf_op jit(solution)/shard_map/ppermute | solution.py:65
  23.1 7.1 %slice-start.3 = ((s8[10485760]{0:T(1024)(128)(4,1)}), s8[4194304]{0:T(1024)(128)(4,1)S(1)}, s32[]{:S(2)}) async-start(s8[10485760]{0:T(1024)(128)(4,1)} %bitcast.106), calls=%async_computation.3 | async-start | bytes 8388608
  24.5 5.8 %slice-start.4 = ((s8[10485760]{0:T(1024)(128)(4,1)}), s8[4194304]{0:T(1024)(128)(4,1)S(1)}, s32[]{:S(2)}) async-start(s8[10485760]{0:T(1024)(128)(4,1)} %bitcast.106), calls=%async_computation.4 | async-start | bytes 8388608
  24.5 6.2 %slice-start.5 = ((s8[10485760]{0:T(1024)(128)(4,1)}), s8[2097152]{0:T(1024)(128)(4,1)S(1)}, s32[]{:S(2)}) async-start(s8[10485760]{0:T(1024)(128)(4,1)} %bitcast.106), calls=%async_computation.5 | async-start | bytes 4194304
  30.7 2.9 %copy-start.7 = (bf16[2,128,1280]{2,1,0:T(8,128)(2,1)S(1)}, bf16[2,128,1280]{2,1,0:T(8,128)(2,1)}, u32[]{:S(2)}) copy-start(bf16[2,128,1280]{2,1,0:T(8,128)(2,1)} %param.11) | copy-start | bytes 1966084
  33.6 44.6 %collective-permute-start.2 = (bf16[256,1280]{1,0:T(8,128)(2,1)S(1)}, bf16[256,1280]{1,0:T(8,128)(2,1)S(1)}, u32[]{:S(2)}, u32[]{:S(2)}) collective-permute-start(bf16[256,1280]{1,0:T(8,128)(2,1)S(1)} %bitcast.93), channel_id=1, source_target_pairs={{2,0},{3,4},{6,1},{7,5},{8,10},{9,14},{12,11},{13,15},{18,16},{19,... | collective-permute-start | bytes 1966088 | tf_op jit(solution)/shard_map/ppermute | solution.py:65
  34.9 43.3 %collective-permute-start.3 = (bf16[256,1280]{1,0:T(8,128)(2,1)S(1)}, bf16[256,1280]{1,0:T(8,128)(2,1)S(1)}, u32[]{:S(2)}, u32[]{:S(2)}) collective-permute-start(bf16[256,1280]{1,0:T(8,128)(2,1)S(1)} %bitcast.94), channel_id=1, source_target_pairs={{2,8},{3,12},{6,9},{7,13},{8,2},{9,6},{12,3},{13,7},{18,24},{19,28... | collective-permute-start | bytes 1966088 | tf_op jit(solution)/shard_map/ppermute | solution.py:65
  35.6 42.6 %collective-permute-start.8 = (bf16[256,1280]{1,0:T(8,128)(2,1)S(1)}, bf16[256,1280]{1,0:T(8,128)(2,1)S(1)}, u32[]{:S(2)}, u32[]{:S(2)}) collective-permute-start(bf16[256,1280]{1,0:T(8,128)(2,1)S(1)} %bitcast.95), channel_id=1, source_target_pairs={{0,0},{1,4},{4,1},{5,5},{10,10},{11,14},{14,11},{15,15},{16,16},{1... | collective-permute-start | bytes 1966088 | tf_op jit(solution)/shard_map/ppermute | solution.py:65
  37.9 16.1 %collective-permute-start.4 = (f16[256,2048]{1,0:T(8,128)(2,1)S(1)}, f16[256,2048]{1,0:T(8,128)(2,1)S(1)}, u32[]{:S(2)}, u32[]{:S(2)}) collective-permute-start(f16[256,2048]{1,0:T(8,128)(2,1)S(1)} %multiply_convert_fusion.7), channel_id=1, source_target_pairs={{0,1},{1,0},{2,3},{3,2},{4,5},{5,4},{6,7},{7,6},{8,9},{9,8},{10,11... | collective-permute-start | bytes 3145736 | tf_op jit(solution)/shard_map/ppermute | solution.py:15
  46.8 50.6 %copy-start.6 = (f32[256,4096]{1,0:T(8,128)}, f32[256,4096]{1,0:T(8,128)S(1)}, u32[]{:S(2)}) copy-start(f32[256,4096]{1,0:T(8,128)S(1)} %fusion.20) | copy-start | bytes 12582916
  46.8 29.0 %collective-permute-start.7 = (f16[256,2048]{1,0:T(8,128)(2,1)S(1)}, f16[256,2048]{1,0:T(8,128)(2,1)S(1)}, u32[]{:S(2)}, u32[]{:S(2)}) collective-permute-start(f16[256,2048]{1,0:T(8,128)(2,1)S(1)} %multiply_convert_fusion.6), channel_id=1, source_target_pairs={{0,1},{1,0},{2,3},{3,2},{4,5},{5,4},{6,7},{7,6},{8,9},{9,8},{10,11... | collective-permute-start | bytes 3145736 | tf_op jit(solution)/shard_map/ppermute | solution.py:15
  54.0 42.7 %copy-start.4 = (f32[256,4096]{1,0:T(8,128)}, f32[256,4096]{1,0:T(8,128)S(1)}, u32[]{:S(2)}) copy-start(f32[256,4096]{1,0:T(8,128)S(1)} %fusion.21) | copy-start | bytes 12582916
  54.0 34.6 %collective-permute-start.9 = (bf16[256,1280]{1,0:T(8,128)(2,1)S(1)}, bf16[256,1280]{1,0:T(8,128)(2,1)S(1)}, u32[]{:S(2)}, u32[]{:S(2)}) collective-permute-start(bf16[256,1280]{1,0:T(8,128)(2,1)S(1)} %bitcast.96), channel_id=1, source_target_pairs={{0,8},{1,12},{4,9},{5,13},{10,2},{11,6},{14,3},{15,7},{16,24},{17,... | collective-permute-start | bytes 1966088 | tf_op jit(solution)/shard_map/ppermute | solution.py:65
  75.4 13.4 %slice-start = ((s8[10485760]{0:T(1024)(128)(4,1)}), s8[4194304]{0:T(1024)(128)(4,1)S(1)}, s32[]{:S(2)}) async-start(s8[10485760]{0:T(1024)(128)(4,1)} %bitcast.89), calls=%async_computation | async-start | bytes 8388608
  75.8 13.0 %slice-start.1 = ((s8[10485760]{0:T(1024)(128)(4,1)}), s8[4194304]{0:T(1024)(128)(4,1)S(1)}, s32[]{:S(2)}) async-start(s8[10485760]{0:T(1024)(128)(4,1)} %bitcast.89), calls=%async_computation.1 | async-start | bytes 8388608
  76.3 12.5 %slice-start.2 = ((s8[10485760]{0:T(1024)(128)(4,1)}), s8[2097152]{0:T(1024)(128)(4,1)S(1)}, s32[]{:S(2)}) async-start(s8[10485760]{0:T(1024)(128)(4,1)} %bitcast.89), calls=%async_computation.2 | async-start | bytes 4194304
  78.2 48.6 %collective-permute-start.10 = (f16[2,256,2048]{2,1,0:T(8,128)(2,1)}, f16[2,256,2048]{2,1,0:T(8,128)(2,1)}, u32[]{:S(2)}, u32[]{:S(2)}) collective-permute-start(f16[2,256,2048]{2,1,0:T(8,128)(2,1)} %fusion), channel_id=1, source_target_pairs={{0,2},{2,0},{1,3},{3,1},{4,6},{6,4},{5,7},{7,5},{8,10},{10,8},{9,1... | collective-permute-start | bytes 6291464 | tf_op jit(solution)/shard_map/ppermute | solution.py:15
  96.3 3.6 %copy-start.1 = (f32[512,4096]{1,0:T(8,128)}, f32[512,4096]{1,0:T(8,128)S(1)}, u32[]{:S(2)}) copy-start(f32[512,4096]{1,0:T(8,128)S(1)} %shard_map.113) | copy-start | bytes 25165828
  96.6 2.7 %collective-permute-start.12 = (f16[256,2048]{1,0:T(8,128)(2,1)S(1)}, f16[256,2048]{1,0:T(8,128)(2,1)S(1)}, u32[]{:S(2)}, u32[]{:S(2)}) collective-permute-start(f16[256,2048]{1,0:T(8,128)(2,1)S(1)} %multiply_convert_fusion.4), channel_id=1, source_target_pairs={{0,1},{1,0},{2,3},{3,2},{4,5},{5,4},{6,7},{7,6},{8,9},{9,8},{10,11... | collective-permute-start | bytes 3145736 | tf_op jit(solution)/shard_map/ppermute | solution.py:15
  96.9 19.9 %collective-permute-start.14 = (f16[256,2048]{1,0:T(8,128)(2,1)S(1)}, f16[256,2048]{1,0:T(8,128)(2,1)}, u32[]{:S(2)}, u32[]{:S(2)}) collective-permute-start(f16[256,2048]{1,0:T(8,128)(2,1)S(1)} %multiply_convert_fusion.2), channel_id=1, source_target_pairs={{0,1},{1,0},{2,3},{3,2},{4,5},{5,4},{6,7},{7,6},{8,9},{9,8},{10,11... | collective-permute-start | bytes 3145736 | tf_op jit(solution)/shard_map/ppermute | solution.py:15
  99.0 20.8 %collective-permute-start.15 = (f16[256,2048]{1,0:T(8,128)(2,1)}, f16[256,2048]{1,0:T(8,128)(2,1)}, u32[]{:S(2)}, u32[]{:S(2)}) collective-permute-start(f16[256,2048]{1,0:T(8,128)(2,1)} %multiply_convert_fusion.1), channel_id=1, source_target_pairs={{0,1},{1,0},{2,3},{3,2},{4,5},{5,4},{6,7},{7,6},{8,9},{9,8},{10,11... | collective-permute-start | bytes 3145736 | tf_op jit(solution)/shard_map/ppermute | solution.py:15
  99.1 20.7 %copy-start.9 = (s32[2]{0:T(128)S(1)}, s32[2]{0:T(128)}, u32[]{:S(2)}) copy-start(s32[2]{0:T(128)} %param.18) | copy-start | bytes 28
  101.3 20.2 %collective-permute-start.16 = (f16[256,192]{0,1:T(8,128)(2,1)S(1)}, f16[256,192]{0,1:T(8,128)(2,1)S(1)}, u32[]{:S(2)}, u32[]{:S(2)}) collective-permute-start(f16[256,192]{0,1:T(8,128)(2,1)S(1)} %multiply_convert_fusion.9), channel_id=1, source_target_pairs={{0,4},{4,8},{8,12},{12,0},{1,5},{5,9},{9,13},{13,1},{2,6},{6,10},{... | collective-permute-start | bytes 294920 | tf_op jit(solution)/shard_map/ppermute | solution.py:15
  115.5 8.8 %collective-permute-start.17 = (f16[256,192]{0,1:T(8,128)(2,1)S(1)}, f16[256,192]{0,1:T(8,128)(2,1)}, u32[]{:S(2)}, u32[]{:S(2)}) collective-permute-start(f16[256,192]{0,1:T(8,128)(2,1)S(1)} %multiply_convert_fusion.9), channel_id=1, source_target_pairs={{0,8},{4,12},{8,0},{12,4},{1,9},{5,13},{9,1},{13,5},{2,10},{6,14},... | collective-permute-start | bytes 294920 | tf_op jit(solution)/shard_map/ppermute | solution.py:15
  116.8 7.5 %collective-permute-start.18 = (f16[256,192]{0,1:T(8,128)(2,1)S(1)}, f16[256,192]{0,1:T(8,128)(2,1)}, u32[]{:S(2)}, u32[]{:S(2)}) collective-permute-start(f16[256,192]{0,1:T(8,128)(2,1)S(1)} %multiply_convert_fusion.9), channel_id=1, source_target_pairs={{0,12},{4,0},{8,4},{12,8},{1,13},{5,1},{9,5},{13,9},{2,14},{6,2},{... | collective-permute-start | bytes 294920 | tf_op jit(solution)/shard_map/ppermute | solution.py:15
  119.8 27.4 %collective-permute-start.13 = (f16[256,2048]{1,0:T(8,128)(2,1)}, f16[256,2048]{1,0:T(8,128)(2,1)}, u32[]{:S(2)}, u32[]{:S(2)}) collective-permute-start(f16[256,2048]{1,0:T(8,128)(2,1)} %multiply_convert_fusion.3), channel_id=1, source_target_pairs={{0,2},{2,0},{1,3},{3,1},{4,6},{6,4},{5,7},{7,5},{8,10},{10,8},{9,1... | collective-permute-start | bytes 3145736 | tf_op jit(solution)/shard_map/ppermute | solution.py:15
  131.6 5.2 %copy-start.5 = (f32[256,4096]{1,0:T(8,128)S(1)}, f32[256,4096]{1,0:T(8,128)}, u32[]{:S(2)}) copy-start(f32[256,4096]{1,0:T(8,128)} %copy-done.4) | copy-start | bytes 12582916
  131.6 8.1 %collective-permute-start.11 = (f16[256,2048]{1,0:T(8,128)(2,1)S(1)}, f16[256,2048]{1,0:T(8,128)(2,1)S(1)}, u32[]{:S(2)}, u32[]{:S(2)}) collective-permute-start(f16[256,2048]{1,0:T(8,128)(2,1)S(1)} %multiply_convert_fusion.5), channel_id=1, source_target_pairs={{0,1},{1,0},{2,3},{3,2},{4,5},{5,4},{6,7},{7,6},{8,9},{9,8},{10,11... | collective-permute-start | bytes 3145736 | tf_op jit(solution)/shard_map/ppermute | solution.py:15
  139.7 10.0 %copy-start.2 = (bf16[2048,64]{1,0:T(8,128)(2,1)S(1)}, bf16[2048,64]{1,0:T(8,128)(2,1)}, u32[]{:S(2)}) copy-start(bf16[2048,64]{1,0:T(8,128)(2,1)} %copy.21.refs_2_) | copy-start | bytes 786436
  139.7 10.0 %copy-start.3 = (bf16[2048,64]{1,0:T(8,128)(2,1)S(1)}, bf16[2048,64]{1,0:T(8,128)(2,1)}, u32[]{:S(2)}) copy-start(bf16[2048,64]{1,0:T(8,128)(2,1)} %copy.22.refs_3_) | copy-start | bytes 786436
  149.7 6.7 %copy-start.8 = (s32[2]{0:T(128)S(1)}, s32[2]{0:T(128)}, u32[]{:S(2)}) copy-start(s32[2]{0:T(128)} %param.19) | copy-start | bytes 28
  151.0 6.3 %collective-permute-start.19 = (f32[6,16,64]{2,1,0:T(8,128)S(1)}, f32[6,16,64]{2,1,0:T(8,128)S(1)}, u32[]{:S(2)}, u32[]{:S(2)}) collective-permute-start(f32[6,16,64]{2,1,0:T(8,128)S(1)} %get-tuple-element.46), channel_id=1, source_target_pairs={{0,4},{4,8},{8,12},{12,0},{1,5},{5,9},{9,13},{13,1},{2,6},{6,10},{... | collective-permute-start | bytes 73736 | tf_op jit(solution)/shard_map/ppermute | solution.py:15
  151.2 6.5 %collective-permute-start.20 = (f32[6,16,64]{2,1,0:T(8,128)S(1)}, f32[6,16,64]{2,1,0:T(8,128)}, u32[]{:S(2)}, u32[]{:S(2)}) collective-permute-start(f32[6,16,64]{2,1,0:T(8,128)S(1)} %get-tuple-element.48), channel_id=1, source_target_pairs={{0,8},{4,12},{8,0},{12,4},{1,9},{5,13},{9,1},{13,5},{2,10},{6,14},... | collective-permute-start | bytes 73736 | tf_op jit(solution)/shard_map/ppermute | solution.py:15
  154.3 4.2 %collective-permute-start.21 = (f32[6,16,64]{2,1,0:T(8,128)S(1)}, f32[6,16,64]{2,1,0:T(8,128)}, u32[]{:S(2)}, u32[]{:S(2)}) collective-permute-start(f32[6,16,64]{2,1,0:T(8,128)S(1)} %get-tuple-element.47), channel_id=1, source_target_pairs={{0,12},{4,0},{8,4},{12,8},{1,13},{5,1},{9,5},{13,9},{2,14},{6,2},{... | collective-permute-start | bytes 73736 | tf_op jit(solution)/shard_map/ppermute | solution.py:15
  156.5 3.5 %collective-permute-start.28 = (s32[2]{0:T(128)S(1)}, s32[2]{0:T(128)S(1)}, u32[]{:S(2)}, u32[]{:S(2)}) collective-permute-start(s32[2]{0:T(128)S(1)} %copy-done.8), channel_id=1, source_target_pairs={{0,2},{2,0},{1,3},{3,1},{4,6},{6,4},{5,7},{7,5},{8,10},{10,8},{9,1... | collective-permute-start | bytes 32 | tf_op jit(solution)/shard_map/ppermute | solution.py:15
  159.3 2.0 %collective-permute-start.24 = (f32[6,16,64]{2,1,0:T(8,128)S(1)}, f32[6,16,64]{2,1,0:T(8,128)S(1)}, u32[]{:S(2)}, u32[]{:S(2)}) collective-permute-start(f32[6,16,64]{2,1,0:T(8,128)S(1)} %fusion.12), channel_id=1, source_target_pairs={{0,1},{1,0},{2,3},{3,2},{4,5},{5,4},{6,7},{7,6},{8,9},{9,8},{10,11... | collective-permute-start | bytes 73736 | tf_op jit(solution)/shard_map/ppermute | solution.py:274
  160.0 4.4 %collective-permute-start.22 = (f32[6,16,64]{2,1,0:T(8,128)S(1)}, f32[6,16,64]{2,1,0:T(8,128)S(1)}, u32[]{:S(2)}, u32[]{:S(2)}) collective-permute-start(f32[6,16,64]{2,1,0:T(8,128)S(1)} %fusion.12), channel_id=1, source_target_pairs={{0,2},{1,3},{2,0},{3,1},{4,6},{5,7},{6,4},{7,5},{8,10},{9,11},{10,... | collective-permute-start | bytes 73736 | tf_op jit(solution)/shard_map/ppermute | solution.py:274
  161.1 3.9 %collective-permute-start.23 = (f32[6,16,64]{2,1,0:T(8,128)S(1)}, f32[6,16,64]{2,1,0:T(8,128)S(1)}, u32[]{:S(2)}, u32[]{:S(2)}) collective-permute-start(f32[6,16,64]{2,1,0:T(8,128)S(1)} %fusion.12), channel_id=1, source_target_pairs={{0,3},{1,2},{2,1},{3,0},{4,7},{5,6},{6,5},{7,4},{8,11},{9,10},{10,... | collective-permute-start | bytes 73736 | tf_op jit(solution)/shard_map/ppermute | solution.py:274
  166.5 4.7 %collective-permute-start.25 = (f32[4,512]{1,0:T(4,128)S(1)}, f32[4,512]{1,0:T(4,128)S(1)}, u32[]{:S(2)}, u32[]{:S(2)}) collective-permute-start(f32[4,512]{1,0:T(4,128)S(1)} %fusion.22), channel_id=1, source_target_pairs={{0,12},{4,0},{8,4},{12,8},{1,13},{5,1},{9,5},{13,9},{2,14},{6,2},{... | collective-permute-start | bytes 24584 | tf_op jit(solution)/shard_map/ppermute | solution.py:15
  169.8 4.6 %collective-permute-start.26 = (f32[4,512]{1,0:T(4,128)S(1)}, f32[4,512]{1,0:T(4,128)S(1)}, u32[]{:S(2)}, u32[]{:S(2)}) collective-permute-start(f32[4,512]{1,0:T(4,128)S(1)} %fusion.22), channel_id=1, source_target_pairs={{0,8},{4,12},{8,0},{12,4},{1,9},{5,13},{9,1},{13,5},{2,10},{6,14},... | collective-permute-start | bytes 24584 | tf_op jit(solution)/shard_map/ppermute | solution.py:15
  169.8 5.5 %collective-permute-start.27 = (f32[4,512]{1,0:T(4,128)S(1)}, f32[4,512]{1,0:T(4,128)S(1)}, u32[]{:S(2)}, u32[]{:S(2)}) collective-permute-start(f32[4,512]{1,0:T(4,128)S(1)} %fusion.22), channel_id=1, source_target_pairs={{0,4},{4,8},{8,12},{12,0},{1,5},{5,9},{9,13},{13,1},{2,6},{6,10},{... | collective-permute-start | bytes 24584 | tf_op jit(solution)/shard_map/ppermute | solution.py:15

commit v10 on v9

--- a/solution.py
+++ b/solution.py
@@ -1,3 +1,5 @@
+import functools
+
 import jax
 import jax.numpy as jnp
 from jax import lax
@@ -104,6 +106,41 @@
         compiler_params=pltpu.CompilerParams(vmem_limit_bytes=16 * 2**20),
         cost_estimate=pl.CostEstimate(flops=1, bytes_accessed=1, transcendentals=0),
     )(tokens, weight)
+
+
+def products_kernel(by_rows, tile, tokens_ref, *refs):
+    count = len(refs) // 2
+    contract = (((1,), (1 if by_rows else 0,)), ((), ()))
+
+    def step(*tiles):
+        for weight_ref, out_ref in zip(tiles, tiles[count:]):
+            out_ref[...] = lax.dot_general(
+                tokens_ref[...], weight_ref[...], contract, preferred_element_type=F32
+            )
+
+    rows, depth = tokens_ref.shape
+    hidden = refs[-1].shape[1]
+    block = ((tile, depth), lambda i: (i, 0)) if by_rows else ((depth, tile), lambda i: (0, i))
+    pltpu.emit_pipeline(
+        step,
+        grid=(hidden // tile,),
+        in_specs=[pl.BlockSpec(*block, pipeline_mode=pl.Buffered(3))] * count,
+        out_specs=[pl.BlockSpec((rows, tile), lambda i: (0, i))] * count,
+    )(*refs)
+
+
+def products(tokens, weights, by_rows):
+    rows, depth = tokens.shape
+    hidden = weights[0].shape[0 if by_rows else 1]
+    far_memory = pl.BlockSpec(memory_space=pltpu.HBM)
+    return pl.pallas_call(
+        functools.partial(products_kernel, by_rows, min(512, hidden)),
+        out_shape=[jax.ShapeDtypeStruct((rows, hidden), F32)] * len(weights),
+        in_specs=[pl.BlockSpec(memory_space=pltpu.VMEM)] + [far_memory] * len(weights),
+        out_specs=[pl.BlockSpec(memory_space=pl.ANY)] * len(weights),
+        compiler_params=pltpu.CompilerParams(vmem_limit_bytes=20 * 2**20),
+        cost_estimate=pl.CostEstimate(flops=1, bytes_accessed=1, transcendentals=0),
+    )(tokens, *weights)
 
 
 def gradients_kernel(down_ref, *refs):
@@ -208,10 +245,8 @@
         grad_ready = after(flat_grad, *up_far)
         grad_far, grad_near = spread_features(grad_ready, 1), spread_features(grad_ready, 0)
         acts_near = arrived_features(acts_near, *up_far)
-    gate_near = forward(after(acts_near, *up_far), w_gate)
-    up_near = forward(after(acts_near, gate_near), w_up)
     for step, (gate, up) in enumerate(zip(gate_far, up_far), 1):
-        both = pack(jnp.stack([core_sum(gate, 0, up_near), core_sum(up, 0, up_near)]))
+        both = pack(jnp.stack([core_sum(gate, 0, acts_near), core_sum(up, 0, acts_near)]))
         received = shift(both, "example", step)
         arrived.append(received)
     if direct:
@@ -221,6 +256,7 @@
     for step in range(1, n_ex):
         sent = pack(core_sum(down_all, (step - 1) * tok_rows))
         arrived_down.append(shift(sent, "example", step))
+    gate_near, up_near = products(after(acts_near, sent), [w_gate, w_up], False)
     down_near = after(down_all, received)
     own = [
         core_sum(gate_near, 0),

time: 178 us -> 186 us (1.045)
  starting transfers between devices: 74 us -> 58.1 us
  waiting for transfers between devices: 34.2 us -> 46.9 us
  matrix products: 29.1 us -> 17.5 us
  Pallas kernels: 8.78 us -> 20 us
  local copies, waits for them, and re-layouts: 7.95 us -> 14.4 us
  other arithmetic: 21.5 us -> 26.3 us
    ppermute x8, waiting for transfers between devices: 10.3 us -> 24.6 us  [spread_features(): pieces.append(lax.ppermute(flat, ('tensor', 'example', 'test'), pairs))]
    ppermute x18, starting transfers between devices: 33.8 us -> 20.5 us  [shift(): return lax.ppermute(value, axis, [(i, (i + step) % n) for i in range(n)])]
    dot_general x4 -> x2, matrix products: 21.2 us -> 8.67 us  [forward(): return jnp.dot(tokens, weight, preferred_element_type=F32)]
    pallas_call x0 -> x1, Pallas kernels: none -> 11.3 us  [products(): pl.pallas_call(functools.partial(products_kernel, by_rows, min(512, hidde...]
    unnamed x41 -> x51, local copies, waits for them, and re-layouts: 4.16 us -> 10.5 us
    ppermute x8, starting transfers between devices: 38.8 us -> 35.4 us  [spread_features(): pieces.append(lax.ppermute(flat, ('tensor', 'example', 'test'), pairs))]
    select_n x3 -> x4, other arithmetic: 2.62 us -> 4.8 us  [arrived_features(): jnp.where(lax.axis_index('tensor') ^ holder < 2, pieces[0], pieces[1])]
  transfers between devices with their start and end apart: 29 -> 29, of which waited for: 14 -> 12; matrix products, arithmetic and copies ran while one was open for 29% -> 24% of each run, Pallas kernels for 4% -> 10%
where the time goes in v10:
time: 186 us; the launch traced here: 184 us
  starting transfers between devices  58.1 us (31%)
  waiting for transfers between devices  46.9 us (25%)
  other arithmetic  26.3 us (14%)
  Pallas kernels  20 us (11%)
  matrix products  17.5 us (9%)
  local copies, waits for them, and re-layouts  14.4 us (8%)
    ppermute x8, starting transfers between devices, spread_features(): pieces.append(lax.ppermute(flat, ('tensor', 'example', 'test'), pairs))  35.4 us
    ppermute x8, waiting for transfers between devices, spread_features(): pieces.append(lax.ppermute(flat, ('tensor', 'example', 'test'), pairs))  24.6 us
    ppermute x18, starting transfers between devices, shift(): return lax.ppermute(value, axis, [(i, (i + step) % n) for i in range(n)])  20.5 us
    ppermute x18, waiting for transfers between devices, shift(): return lax.ppermute(value, axis, [(i, (i + step) % n) for i in range(n)])  18.6 us
    pallas_call x1, Pallas kernels, products(): pl.pallas_call(functools.partial(products_kernel, by_rows, min(512, hidde...  11.3 us
    unnamed x51, local copies, waits for them, and re-layouts  10.5 us
    convert_element_type x9, other arithmetic, pack(): return (value * SEND_SCALE).astype(jnp.float16)  8.87 us
    dot_general x2, matrix products, forward(): return jnp.dot(tokens, weight, preferred_element_type=F32)  8.67 us
  transfers between devices with their start and end apart: 29, of which 12 were waited for; matrix products, arithmetic and copies ran while one was open for 24% of the time, Pallas kernels for 10%

profile of v10, /device:TPU:0, one launch (start us, length us, event | category | flops | bytes accessed | tf_op | source)
XLA Modules:
  0.0 184.4 jit_solution(1023523766815994735)
XLA Ops:
  0.6 7.1 %collective-permute-start.6 = (bf16[256,1280]{1,0:T(8,128)(2,1)}, bf16[256,1280]{1,0:T(8,128)(2,1)}, u32[]{:S(2)}, u32[]{:S(2)}) collective-permute-start(bf16[256,1280]{1,0:T(8,128)(2,1)} %bitcast.90), channel_id=1, source_target_pairs={{0,8},{1,12},{4,9},{5,13},{10,2},{11,6},{14,3},{15,7},{16,24},{17,... | collective-permute-start | bytes 1966088 | tf_op jit(solution)/shard_map/ppermute | solution.py:67
  7.7 6.5 %collective-permute-start.5 = (bf16[256,1280]{1,0:T(8,128)(2,1)}, bf16[256,1280]{1,0:T(8,128)(2,1)}, u32[]{:S(2)}, u32[]{:S(2)}) collective-permute-start(bf16[256,1280]{1,0:T(8,128)(2,1)} %bitcast.91), channel_id=1, source_target_pairs={{0,0},{1,4},{4,1},{5,5},{10,10},{11,14},{14,11},{15,15},{16,16},{1... | collective-permute-start | bytes 1966088 | tf_op jit(solution)/shard_map/ppermute | solution.py:67
  14.2 1.5 collective-permute-start.1
  15.7 1.3 collective-permute-start
  17.0 1.8 fusion.17
  18.8 2.0 %copy.22.refs_3_ = bf16[2048,64]{1,0:T(8,128)(2,1)} copy(bf16[2048,64]{0,1:T(8,128)(2,1)} %get-tuple-element.44) | data formatting | bytes 524288
  21.8 2.1 %fusion.6 = f32[256,64]{0,1:T(8,128)} fusion(bf16[256,1280]{1,0:T(8,128)(2,1)} %bitcast, bf16[1280,192]{0,1:T(8,128)(2,1)} %param.15), kind=kOutput, calls=%fused_computation.36 | convolution fusion | flops 41943040 | bytes 884736 | tf_op jit(solution)/shard_map/dot_general | solution.py:224
  23.8 2.2 %fusion.3 = f32[256,128]{0,1:T(8,128)} fusion(bf16[256,1280]{1,0:T(8,128)(2,1)} %bitcast.94, bf16[1280,192]{0,1:T(8,128)(2,1)} %param.15), kind=kOutput, calls=%fused_computation.26 | convolution fusion | flops 83886080 | bytes 1114112 | tf_op jit(solution)/shard_map/dot_general | solution.py:223
  26.0 8.0 %collective-permute-done = bf16[256,1280]{1,0:T(8,128)(2,1)} collective-permute-done((bf16[256,1280]{1,0:T(8,128)(2,1)}, bf16[256,1280]{1,0:T(8,128)(2,1)}, u32[]{:S(2)}, u32[]{:S(2)}) %collective-permute-start) | collective-permute-done | bytes 655392 | tf_op jit(solution)/shard_map/ppermute | solution.py:67
  34.1 1.3 broadcast_select_fusion.3
  35.4 5.8 %fusion.18 = f32[256,4096]{1,0:T(8,128)S(1)} fusion(bf16[256,1280]{1,0:T(8,128)(2,1)S(1)} %broadcast_select_fusion.3, bf16[1280,4096]{1,0:T(8,128)(2,1)} %refs_0_.1), kind=kOutput, calls=%fused_computation.75 | convolution fusion | flops 2684354560 | bytes 15335424 | tf_op jit(solution)/shard_map/dot_general | solution.py:209
  41.6 2.9 %fusion.19 = f32[256,4096]{1,0:T(8,128)S(1)} fusion(bf16[256,1280]{1,0:T(8,128)(2,1)S(1)} %broadcast_select_fusion.3, bf16[1280,4096]{1,0:T(8,128)(2,1)S(1)} %bitcast.88), kind=kOutput, calls=%fused_computation.76 | convolution fusion | flops 2684354560 | bytes 15335424 | tf_op jit(solution)/shard_map/dot_general | solution.py:209
  45.2 9.7 %collective-permute-start.9 = (bf16[256,1280]{1,0:T(8,128)(2,1)}, bf16[256,1280]{1,0:T(8,128)(2,1)}, u32[]{:S(2)}, u32[]{:S(2)}) collective-permute-start(bf16[256,1280]{1,0:T(8,128)(2,1)} %bitcast), channel_id=1, source_target_pairs={{0,8},{1,12},{4,9},{5,13},{10,2},{11,6},{14,3},{15,7},{16,24},{17,... | collective-permute-start | bytes 1966088 | tf_op jit(solution)/shard_map/ppermute | solution.py:67
  54.9 6.5 %collective-permute-start.8 = (bf16[256,1280]{1,0:T(8,128)(2,1)}, bf16[256,1280]{1,0:T(8,128)(2,1)}, u32[]{:S(2)}, u32[]{:S(2)}) collective-permute-start(bf16[256,1280]{1,0:T(8,128)(2,1)} %bitcast), channel_id=1, source_target_pairs={{0,0},{1,4},{4,1},{5,5},{10,10},{11,14},{14,11},{15,15},{16,16},{1... | collective-permute-start | bytes 1966088 | tf_op jit(solution)/shard_map/ppermute | solution.py:67
  61.4 1.5 collective-permute-start.3
  64.1 1.3 collective-permute-start.2
  65.4 2.6 %add_bitcast_fusion = (f32[1,256,2048]{2,1,0:T(8,128)S(1)}, f32[1,256,2048]{2,1,0:T(8,128)S(1)}) fusion(f16[256,2048]{1,0:T(8,128)(2,1)S(1)} %collective-permute-done.7, f32[256,4096]{1,0:T(8,128)} %copy-done.10, s32[]{:T(128)S(6)} %select_n.61, f16[256,2048]{1,0:T(8,128)(2,1)S(1)} %collective-permute-done.4, f32[256,4096]{1,0:T(8,128)S(1)} %fusion.18), kind=kLoop, calls=%fused_computation.14 | loop fusion | flops 3145728 | bytes 10485764 | tf_op jit(solution)/shard_map/stack | solution.py:249
  68.6 3.5 %collective-permute-start.10 = (f16[2,256,2048]{2,1,0:T(8,128)(2,1)S(1)}, f16[2,256,2048]{2,1,0:T(8,128)(2,1)S(1)}, u32[]{:S(2)}, u32[]{:S(2)}) collective-permute-start(f16[2,256,2048]{2,1,0:T(8,128)(2,1)S(1)} %fusion), channel_id=1, source_target_pairs={{0,2},{2,0},{1,3},{3,1},{4,6},{6,4},{5,7},{7,5},{8,10},{10,8},{9,1... | collective-permute-start | bytes 6291464 | tf_op jit(solution)/shard_map/ppermute | solution.py:17
  72.1 16.5 %collective-permute-done.2 = bf16[256,1280]{1,0:T(8,128)(2,1)} collective-permute-done((bf16[256,1280]{1,0:T(8,128)(2,1)}, bf16[256,1280]{1,0:T(8,128)(2,1)}, u32[]{:S(2)}, u32[]{:S(2)}) %collective-permute-start.2) | collective-permute-done | bytes 655392 | tf_op jit(solution)/shard_map/ppermute | solution.py:67
  88.6 1.2 broadcast_select_fusion
  89.8 1.2 broadcast_select_fusion.1
  91.1 7.5 %shard_map.113 = f32[512,4096]{1,0:T(8,128)S(1)} custom-call(bf16[512,1280]{1,0:T(8,128)(2,1)S(1)} %pad_maximum_fusion.tokens_ref, bf16[4096,1280]{1,0:T(8,128)(2,1)S(1)} %bitcast.86), custom_call_target="tpu_custom_call" | custom-call | flops 1 | bytes 1 | tf_op jit(solution)/shard_map/pallas_call | solution.py:97
  99.8 1.2 multiply_convert_fusion.9
  102.0 1.4 multiply_convert_fusion.3
  104.5 2.4 %collective-permute-start.17 = (f16[256,192]{0,1:T(8,128)(2,1)}, f16[256,192]{0,1:T(8,128)(2,1)}, u32[]{:S(2)}, u32[]{:S(2)}) collective-permute-start(f16[256,192]{0,1:T(8,128)(2,1)} %multiply_convert_fusion.9), channel_id=1, source_target_pairs={{0,8},{4,12},{8,0},{12,4},{1,9},{5,13},{9,1},{13,5},{2,10},{6,14},... | collective-permute-start | bytes 294920 | tf_op jit(solution)/shard_map/ppermute | solution.py:17
  107.0 2.0 %collective-permute-start.16 = (f16[256,192]{0,1:T(8,128)(2,1)}, f16[256,192]{0,1:T(8,128)(2,1)}, u32[]{:S(2)}, u32[]{:S(2)}) collective-permute-start(f16[256,192]{0,1:T(8,128)(2,1)} %multiply_convert_fusion.9), channel_id=1, source_target_pairs={{0,4},{4,8},{8,12},{12,0},{1,5},{5,9},{9,13},{13,1},{2,6},{6,10},{... | collective-permute-start | bytes 294920 | tf_op jit(solution)/shard_map/ppermute | solution.py:17
  109.0 4.0 %copy-done.2 = bf16[1280,4096]{1,0:T(8,128)(2,1)S(1)} copy-done((bf16[1280,4096]{1,0:T(8,128)(2,1)S(1)}, bf16[1280,4096]{1,0:T(8,128)(2,1)}, u32[]{:S(2)}) %copy-start.2) | copy-done | bytes 10485784
  113.0 11.3 %shard_map.114 = (f32[256,4096]{1,0:T(8,128)S(1)}, f32[256,4096]{1,0:T(8,128)S(1)}) custom-call(bf16[256,1280]{1,0:T(8,128)(2,1)S(1)} %broadcast_select_fusion.2.tokens_ref, bf16[1280,4096]{1,0:T(8,128)(2,1)S(1)} %copy-done.2, bf16[1280,4096]{1,0:T(8,128)(2,1)S(1)} %bitcast.88), custom_call_target="tpu_custom_call" | custom-call | flops 1 | bytes 1 | tf_op jit(solution)/shard_map/pallas_call | solution.py:136
  124.3 1.4 multiply_convert_fusion.2
  125.6 1.7 multiply_convert_fusion.1
  128.1 1.3 copy-done.8
  129.6 2.5 %collective-permute-start.13 = (f16[256,2048]{1,0:T(8,128)(2,1)}, f16[256,2048]{1,0:T(8,128)(2,1)}, u32[]{:S(2)}, u32[]{:S(2)}) collective-permute-start(f16[256,2048]{1,0:T(8,128)(2,1)} %multiply_convert_fusion.3), channel_id=1, source_target_pairs={{0,2},{2,0},{1,3},{3,1},{4,6},{6,4},{5,7},{7,5},{8,10},{10,8},{9,1... | collective-permute-start | bytes 3145736 | tf_op jit(solution)/shard_map/ppermute | solution.py:17
  132.0 1.8 multiply_add_fusion.1
  135.2 1.9 %multiply_convert_fusion.5 = f16[256,2048]{1,0:T(8,128)(2,1)S(1)} fusion(f32[512,4096]{1,0:T(8,128)} %copy-done.1, s32[]{:T(128)S(6)} %select_n.63), kind=kLoop, calls=%fused_computation.13 | loop fusion | flops 1048576 | bytes 3145732 | tf_op jit(solution)/shard_map/convert_element_type | solution.py:21
  137.4 4.6 %fusion.1 = (f32[256,2048]{1,0:T(8,128)S(1)}, f32[256,2048]{1,0:T(8,128)S(1)}) fusion(f16[2,256,2048]{2,1,0:T(8,128)(2,1)S(1)} %copy-done.9, f16[256,2048]{1,0:T(8,128)(2,1)} %collective-permute-done.15, f32[256,4096]{1,0:T(8,128)} %copy-done.5, s32[]{:T(128)S(6)} %select_n.61, f16[256,2048]{1,0:T(8,128)(2,1)} %collective-permute-done.14, ...), kind=kLoop, calls=%fused_computation.7 | loop fusion | flops 11010048 | bytes 12582916 | tf_op jit(solution)/shard_map/mul | solution.py:287
  142.0 2.0 %fusion.2 = f32[256,64]{0,1:T(8,128)S(1)} fusion(f32[256,2048]{1,0:T(8,128)S(1)} %get-tuple-element.42.refs_1_, f16[256,2048]{1,0:T(8,128)(2,1)} %collective-permute-done.14, f32[256,4096]{1,0:T(8,128)S(1)} %copy-done.4, s32[]{:T(128)S(6)} %select_n.61, f16[2,256,2048]{2,1,0:T(8,128)(2,1)S(1)} %copy-done.9, bf16[4096,192]{0,1:T(8,128)(2,1)} %param.16, ...), kind=kOutput, calls=%fused_computation.21 | convolution fusion | flops 71303168 | bytes 6620672 | tf_op jit(solution)/shard_map/dot_general | solution.py:290
  144.4 10.5 %collective-permute-done.13 = f16[256,2048]{1,0:T(8,128)(2,1)} collective-permute-done((f16[256,2048]{1,0:T(8,128)(2,1)}, f16[256,2048]{1,0:T(8,128)(2,1)}, u32[]{:S(2)}, u32[]{:S(2)}) %collective-permute-start.13) | collective-permute-done | bytes 1048608 | tf_op jit(solution)/shard_map/ppermute | solution.py:17
  154.9 2.5 %multiply_add_fusion.down_ref = f32[256,2048]{1,0:T(8,128)S(1)} fusion(f16[256,2048]{1,0:T(8,128)(2,1)} %collective-permute-done.13, f16[256,2048]{1,0:T(8,128)(2,1)S(1)} %collective-permute-done.11, f32[512,4096]{1,0:T(8,128)} %copy-done.1, s32[]{:T(128)S(6)} %select_n.61), kind=kLoop, calls=%fused_computation.10 | loop fusion | flops 3145728 | bytes 6291460 | tf_op jit(solution)/shard_map/add | solution.py:285
  157.4 1.3 shard_map.115
  158.7 1.4 collective-permute-start.19
  160.2 2.4 %collective-permute-start.21 = (f32[6,16,64]{2,1,0:T(8,128)S(1)}, f32[6,16,64]{2,1,0:T(8,128)}, u32[]{:S(2)}, u32[]{:S(2)}) collective-permute-start(f32[6,16,64]{2,1,0:T(8,128)S(1)} %get-tuple-element.49), channel_id=1, source_target_pairs={{0,12},{4,0},{8,4},{12,8},{1,13},{5,1},{9,5},{13,9},{2,14},{6,2},{... | collective-permute-start | bytes 73736 | tf_op jit(solution)/shard_map/ppermute | solution.py:17
  162.6 1.7 collective-permute-start.28
  165.0 2.7 %collective-permute-done.20 = f32[6,16,64]{2,1,0:T(8,128)} collective-permute-done((f32[6,16,64]{2,1,0:T(8,128)S(1)}, f32[6,16,64]{2,1,0:T(8,128)}, u32[]{:S(2)}, u32[]{:S(2)}) %collective-permute-start.20) | collective-permute-done | bytes 24608 | tf_op jit(solution)/shard_map/ppermute | solution.py:17
  168.6 1.9 %collective-permute-start.23 = (f32[6,16,64]{2,1,0:T(8,128)S(1)}, f32[6,16,64]{2,1,0:T(8,128)S(1)}, u32[]{:S(2)}, u32[]{:S(2)}) collective-permute-start(f32[6,16,64]{2,1,0:T(8,128)S(1)} %fusion.12), channel_id=1, source_target_pairs={{0,3},{1,2},{2,1},{3,0},{4,7},{5,6},{6,5},{7,4},{8,11},{9,10},{10,... | collective-permute-start | bytes 73736 | tf_op jit(solution)/shard_map/ppermute | solution.py:310
  170.8 1.7 collective-permute-done.23
  172.5 2.1 %collective-permute-done.22 = f32[6,16,64]{2,1,0:T(8,128)S(1)} collective-permute-done((f32[6,16,64]{2,1,0:T(8,128)S(1)}, f32[6,16,64]{2,1,0:T(8,128)S(1)}, u32[]{:S(2)}, u32[]{:S(2)}) %collective-permute-start.22) | collective-permute-done | bytes 24608 | tf_op jit(solution)/shard_map/ppermute | solution.py:310
  174.8 1.3 fusion.20
  179.8 3.0 %collective-permute-done.26 = f32[4,512]{1,0:T(4,128)S(1)} collective-permute-done((f32[4,512]{1,0:T(4,128)S(1)}, f32[4,512]{1,0:T(4,128)S(1)}, u32[]{:S(2)}, u32[]{:S(2)}) %collective-permute-start.26) | collective-permute-done | bytes 8224 | tf_op jit(solution)/shard_map/ppermute | solution.py:17
  (114 shorter events, 17.1 us)
Async XLA Ops:
  0.6 174.2 %copy-start = (bf16[3,16,64,512]{3,2,1,0:T(8,128)(2,1)S(1)}, bf16[3,16,64,512]{3,2,1,0:T(8,128)(2,1)}, u32[]{:S(2)}) copy-start(bf16[3,16,64,512]{3,2,1,0:T(8,128)(2,1)} %param.17) | copy-start | bytes 9437188
  0.6 54.2 %collective-permute-start.6 = (bf16[256,1280]{1,0:T(8,128)(2,1)}, bf16[256,1280]{1,0:T(8,128)(2,1)}, u32[]{:S(2)}, u32[]{:S(2)}) collective-permute-start(bf16[256,1280]{1,0:T(8,128)(2,1)} %bitcast.90), channel_id=1, source_target_pairs={{0,8},{1,12},{4,9},{5,13},{10,2},{11,6},{14,3},{15,7},{16,24},{17,... | collective-permute-start | bytes 1966088 | tf_op jit(solution)/shard_map/ppermute | solution.py:67
  7.7 53.7 %collective-permute-start.5 = (bf16[256,1280]{1,0:T(8,128)(2,1)}, bf16[256,1280]{1,0:T(8,128)(2,1)}, u32[]{:S(2)}, u32[]{:S(2)}) collective-permute-start(bf16[256,1280]{1,0:T(8,128)(2,1)} %bitcast.91), channel_id=1, source_target_pairs={{0,0},{1,4},{4,1},{5,5},{10,10},{11,14},{14,11},{15,15},{16,16},{1... | collective-permute-start | bytes 1966088 | tf_op jit(solution)/shard_map/ppermute | solution.py:67
  14.2 11.8 %collective-permute-start.1 = (bf16[256,1280]{1,0:T(8,128)(2,1)}, bf16[256,1280]{1,0:T(8,128)(2,1)}, u32[]{:S(2)}, u32[]{:S(2)}) collective-permute-start(bf16[256,1280]{1,0:T(8,128)(2,1)} %bitcast.92), channel_id=1, source_target_pairs={{2,8},{3,12},{6,9},{7,13},{8,2},{9,6},{12,3},{13,7},{18,24},{19,28... | collective-permute-start | bytes 1966088 | tf_op jit(solution)/shard_map/ppermute | solution.py:67
  15.7 18.3 %collective-permute-start = (bf16[256,1280]{1,0:T(8,128)(2,1)}, bf16[256,1280]{1,0:T(8,128)(2,1)}, u32[]{:S(2)}, u32[]{:S(2)}) collective-permute-start(bf16[256,1280]{1,0:T(8,128)(2,1)} %bitcast.93), channel_id=1, source_target_pairs={{2,0},{3,4},{6,1},{7,5},{8,10},{9,14},{12,11},{13,15},{18,16},{19,... | collective-permute-start | bytes 1966088 | tf_op jit(solution)/shard_map/ppermute | solution.py:67
  34.1 7.4 %slice-start.3 = ((s8[10485760]{0:T(1024)(128)(4,1)}), s8[4194304]{0:T(1024)(128)(4,1)S(1)}, s32[]{:S(2)}) async-start(s8[10485760]{0:T(1024)(128)(4,1)} %bitcast.87), calls=%async_computation.3 | async-start | bytes 8388608
  35.4 6.1 %slice-start.4 = ((s8[10485760]{0:T(1024)(128)(4,1)}), s8[4194304]{0:T(1024)(128)(4,1)S(1)}, s32[]{:S(2)}) async-start(s8[10485760]{0:T(1024)(128)(4,1)} %bitcast.87), calls=%async_computation.4 | async-start | bytes 8388608
  35.4 6.2 %slice-start.5 = ((s8[10485760]{0:T(1024)(128)(4,1)}), s8[2097152]{0:T(1024)(128)(4,1)S(1)}, s32[]{:S(2)}) async-start(s8[10485760]{0:T(1024)(128)(4,1)} %bitcast.87), calls=%async_computation.5 | async-start | bytes 4194304
  41.4 22.7 %collective-permute-start.4 = (f16[256,2048]{1,0:T(8,128)(2,1)S(1)}, f16[256,2048]{1,0:T(8,128)(2,1)S(1)}, u32[]{:S(2)}, u32[]{:S(2)}) collective-permute-start(f16[256,2048]{1,0:T(8,128)(2,1)S(1)} %multiply_convert_fusion.7), channel_id=1, source_target_pairs={{0,1},{1,0},{2,3},{3,2},{4,5},{5,4},{6,7},{7,6},{8,9},{9,8},{10,11... | collective-permute-start | bytes 3145736 | tf_op jit(solution)/shard_map/ppermute | solution.py:17
  44.5 19.6 %copy-start.10 = (f32[256,4096]{1,0:T(8,128)}, f32[256,4096]{1,0:T(8,128)S(1)}, u32[]{:S(2)}) copy-start(f32[256,4096]{1,0:T(8,128)S(1)} %fusion.19) | copy-start | bytes 12582916
  44.7 20.7 %collective-permute-start.7 = (f16[256,2048]{1,0:T(8,128)(2,1)S(1)}, f16[256,2048]{1,0:T(8,128)(2,1)S(1)}, u32[]{:S(2)}, u32[]{:S(2)}) collective-permute-start(f16[256,2048]{1,0:T(8,128)(2,1)S(1)} %multiply_convert_fusion.6), channel_id=1, source_target_pairs={{0,1},{1,0},{2,3},{3,2},{4,5},{5,4},{6,7},{7,6},{8,9},{9,8},{10,11... | collective-permute-start | bytes 3145736 | tf_op jit(solution)/shard_map/ppermute | solution.py:17
  45.2 27.0 %collective-permute-start.9 = (bf16[256,1280]{1,0:T(8,128)(2,1)}, bf16[256,1280]{1,0:T(8,128)(2,1)}, u32[]{:S(2)}, u32[]{:S(2)}) collective-permute-start(bf16[256,1280]{1,0:T(8,128)(2,1)} %bitcast), channel_id=1, source_target_pairs={{0,8},{1,12},{4,9},{5,13},{10,2},{11,6},{14,3},{15,7},{16,24},{17,... | collective-permute-start | bytes 1966088 | tf_op jit(solution)/shard_map/ppermute | solution.py:67
  54.9 17.2 %collective-permute-start.8 = (bf16[256,1280]{1,0:T(8,128)(2,1)}, bf16[256,1280]{1,0:T(8,128)(2,1)}, u32[]{:S(2)}, u32[]{:S(2)}) collective-permute-start(bf16[256,1280]{1,0:T(8,128)(2,1)} %bitcast), channel_id=1, source_target_pairs={{0,0},{1,4},{4,1},{5,5},{10,10},{11,14},{14,11},{15,15},{16,16},{1... | collective-permute-start | bytes 1966088 | tf_op jit(solution)/shard_map/ppermute | solution.py:67
  61.4 10.7 %collective-permute-start.3 = (bf16[256,1280]{1,0:T(8,128)(2,1)}, bf16[256,1280]{1,0:T(8,128)(2,1)}, u32[]{:S(2)}, u32[]{:S(2)}) collective-permute-start(bf16[256,1280]{1,0:T(8,128)(2,1)} %bitcast), channel_id=1, source_target_pairs={{2,8},{3,12},{6,9},{7,13},{8,2},{9,6},{12,3},{13,7},{18,24},{19,28... | collective-permute-start | bytes 1966088 | tf_op jit(solution)/shard_map/ppermute | solution.py:67
  64.1 24.5 %collective-permute-start.2 = (bf16[256,1280]{1,0:T(8,128)(2,1)}, bf16[256,1280]{1,0:T(8,128)(2,1)}, u32[]{:S(2)}, u32[]{:S(2)}) collective-permute-start(bf16[256,1280]{1,0:T(8,128)(2,1)} %bitcast), channel_id=1, source_target_pairs={{2,0},{3,4},{6,1},{7,5},{8,10},{9,14},{12,11},{13,15},{18,16},{19,... | collective-permute-start | bytes 1966088 | tf_op jit(solution)/shard_map/ppermute | solution.py:67
  65.4 25.7 %slice-start = ((s8[10485760]{0:T(1024)(128)(4,1)}), s8[4194304]{0:T(1024)(128)(4,1)S(1)}, s32[]{:S(2)}) async-start(s8[10485760]{0:T(1024)(128)(4,1)} %bitcast.85), calls=%async_computation | async-start | bytes 8388608
  65.4 25.7 %slice-start.1 = ((s8[10485760]{0:T(1024)(128)(4,1)}), s8[4194304]{0:T(1024)(128)(4,1)S(1)}, s32[]{:S(2)}) async-start(s8[10485760]{0:T(1024)(128)(4,1)} %bitcast.85), calls=%async_computation.1 | async-start | bytes 8388608
  68.0 23.1 %slice-start.2 = ((s8[10485760]{0:T(1024)(128)(4,1)}), s8[2097152]{0:T(1024)(128)(4,1)S(1)}, s32[]{:S(2)}) async-start(s8[10485760]{0:T(1024)(128)(4,1)} %bitcast.85), calls=%async_computation.2 | async-start | bytes 4194304
  68.6 58.8 %collective-permute-start.10 = (f16[2,256,2048]{2,1,0:T(8,128)(2,1)S(1)}, f16[2,256,2048]{2,1,0:T(8,128)(2,1)S(1)}, u32[]{:S(2)}, u32[]{:S(2)}) collective-permute-start(f16[2,256,2048]{2,1,0:T(8,128)(2,1)S(1)} %fusion), channel_id=1, source_target_pairs={{0,2},{2,0},{1,3},{3,1},{4,6},{6,4},{5,7},{7,5},{8,10},{10,8},{9,1... | collective-permute-start | bytes 6291464 | tf_op jit(solution)/shard_map/ppermute | solution.py:17
  98.6 3.3 %copy-start.1 = (f32[512,4096]{1,0:T(8,128)}, f32[512,4096]{1,0:T(8,128)S(1)}, u32[]{:S(2)}) copy-start(f32[512,4096]{1,0:T(8,128)S(1)} %shard_map.113) | copy-start | bytes 25165828
  98.9 2.7 %collective-permute-start.12 = (f16[256,2048]{1,0:T(8,128)(2,1)S(1)}, f16[256,2048]{1,0:T(8,128)(2,1)S(1)}, u32[]{:S(2)}, u32[]{:S(2)}) collective-permute-start(f16[256,2048]{1,0:T(8,128)(2,1)S(1)} %multiply_convert_fusion.4), channel_id=1, source_target_pairs={{0,1},{1,0},{2,3},{3,2},{4,5},{5,4},{6,7},{7,6},{8,9},{9,8},{10,11... | collective-permute-start | bytes 3145736 | tf_op jit(solution)/shard_map/ppermute | solution.py:17
  103.4 26.2 %collective-permute-start.18 = (f16[256,192]{0,1:T(8,128)(2,1)}, f16[256,192]{0,1:T(8,128)(2,1)}, u32[]{:S(2)}, u32[]{:S(2)}) collective-permute-start(f16[256,192]{0,1:T(8,128)(2,1)} %multiply_convert_fusion.9), channel_id=1, source_target_pairs={{0,12},{4,0},{8,4},{12,8},{1,13},{5,1},{9,5},{13,9},{2,14},{6,2},{... | collective-permute-start | bytes 294920 | tf_op jit(solution)/shard_map/ppermute | solution.py:17
  104.5 27.5 %collective-permute-start.17 = (f16[256,192]{0,1:T(8,128)(2,1)}, f16[256,192]{0,1:T(8,128)(2,1)}, u32[]{:S(2)}, u32[]{:S(2)}) collective-permute-start(f16[256,192]{0,1:T(8,128)(2,1)} %multiply_convert_fusion.9), channel_id=1, source_target_pairs={{0,8},{4,12},{8,0},{12,4},{1,9},{5,13},{9,1},{13,5},{2,10},{6,14},... | collective-permute-start | bytes 294920 | tf_op jit(solution)/shard_map/ppermute | solution.py:17
  107.0 25.1 %collective-permute-start.16 = (f16[256,192]{0,1:T(8,128)(2,1)}, f16[256,192]{0,1:T(8,128)(2,1)}, u32[]{:S(2)}, u32[]{:S(2)}) collective-permute-start(f16[256,192]{0,1:T(8,128)(2,1)} %multiply_convert_fusion.9), channel_id=1, source_target_pairs={{0,4},{4,8},{8,12},{12,0},{1,5},{5,9},{9,13},{13,1},{2,6},{6,10},{... | collective-permute-start | bytes 294920 | tf_op jit(solution)/shard_map/ppermute | solution.py:17
  109.0 4.0 %copy-start.2 = (bf16[1280,4096]{1,0:T(8,128)(2,1)S(1)}, bf16[1280,4096]{1,0:T(8,128)(2,1)}, u32[]{:S(2)}) copy-start(bf16[1280,4096]{1,0:T(8,128)(2,1)} %refs_0_.1) | copy-start | bytes 31457284
  124.2 3.1 %copy-start.3 = (f32[256,4096]{1,0:T(8,128)}, f32[256,4096]{1,0:T(8,128)S(1)}, u32[]{:S(2)}) copy-start(f32[256,4096]{1,0:T(8,128)S(1)} %get-tuple-element.36) | copy-start | bytes 12582916
  124.2 3.9 %copy-start.5 = (f32[256,4096]{1,0:T(8,128)}, f32[256,4096]{1,0:T(8,128)S(1)}, u32[]{:S(2)}) copy-start(f32[256,4096]{1,0:T(8,128)S(1)} %get-tuple-element.37) | copy-start | bytes 12582916
  125.6 3.9 %copy-start.14 = (s32[2]{0:T(128)S(1)}, s32[2]{0:T(128)}, u32[]{:S(2)}) copy-start(s32[2]{0:T(128)} %param.18) | copy-start | bytes 28
  125.6 11.6 %collective-permute-start.14 = (f16[256,2048]{1,0:T(8,128)(2,1)}, f16[256,2048]{1,0:T(8,128)(2,1)}, u32[]{:S(2)}, u32[]{:S(2)}) collective-permute-start(f16[256,2048]{1,0:T(8,128)(2,1)} %multiply_convert_fusion.2), channel_id=1, source_target_pairs={{0,1},{1,0},{2,3},{3,2},{4,5},{5,4},{6,7},{7,6},{8,9},{9,8},{10,11... | collective-permute-start | bytes 3145736 | tf_op jit(solution)/shard_map/ppermute | solution.py:17
  128.1 1.4 copy-start.8
  128.1 9.1 %collective-permute-start.15 = (f16[256,2048]{1,0:T(8,128)(2,1)}, f16[256,2048]{1,0:T(8,128)(2,1)}, u32[]{:S(2)}, u32[]{:S(2)}) collective-permute-start(f16[256,2048]{1,0:T(8,128)(2,1)} %multiply_convert_fusion.1), channel_id=1, source_target_pairs={{0,1},{1,0},{2,3},{3,2},{4,5},{5,4},{6,7},{7,6},{8,9},{9,8},{10,11... | collective-permute-start | bytes 3145736 | tf_op jit(solution)/shard_map/ppermute | solution.py:17
  129.6 25.4 %collective-permute-start.13 = (f16[256,2048]{1,0:T(8,128)(2,1)}, f16[256,2048]{1,0:T(8,128)(2,1)}, u32[]{:S(2)}, u32[]{:S(2)}) collective-permute-start(f16[256,2048]{1,0:T(8,128)(2,1)} %multiply_convert_fusion.3), channel_id=1, source_target_pairs={{0,2},{2,0},{1,3},{3,1},{4,6},{6,4},{5,7},{7,5},{8,10},{10,8},{9,1... | collective-permute-start | bytes 3145736 | tf_op jit(solution)/shard_map/ppermute | solution.py:17
  135.2 2.2 %copy-start.9 = (f16[2,256,2048]{2,1,0:T(8,128)(2,1)S(1)}, f16[2,256,2048]{2,1,0:T(8,128)(2,1)}, u32[]{:S(2)}) copy-start(f16[2,256,2048]{2,1,0:T(8,128)(2,1)} %copy-done.8) | copy-start | bytes 6291460
  137.2 4.8 %copy-start.4 = (f32[256,4096]{1,0:T(8,128)S(1)}, f32[256,4096]{1,0:T(8,128)}, u32[]{:S(2)}) copy-start(f32[256,4096]{1,0:T(8,128)} %copy-done.3) | copy-start | bytes 12582916
  137.2 7.3 %collective-permute-start.11 = (f16[256,2048]{1,0:T(8,128)(2,1)S(1)}, f16[256,2048]{1,0:T(8,128)(2,1)S(1)}, u32[]{:S(2)}, u32[]{:S(2)}) collective-permute-start(f16[256,2048]{1,0:T(8,128)(2,1)S(1)} %multiply_convert_fusion.5), channel_id=1, source_target_pairs={{0,1},{1,0},{2,3},{3,2},{4,5},{5,4},{6,7},{7,6},{8,9},{9,8},{10,11... | collective-permute-start | bytes 3145736 | tf_op jit(solution)/shard_map/ppermute | solution.py:17
  144.4 13.0 %copy-start.6 = (bf16[2048,64]{1,0:T(8,128)(2,1)S(1)}, bf16[2048,64]{1,0:T(8,128)(2,1)}, u32[]{:S(2)}) copy-start(bf16[2048,64]{1,0:T(8,128)(2,1)} %copy.22.refs_3_) | copy-start | bytes 786436
  144.4 13.0 %copy-start.7 = (bf16[2048,64]{1,0:T(8,128)(2,1)S(1)}, bf16[2048,64]{1,0:T(8,128)(2,1)}, u32[]{:S(2)}) copy-start(bf16[2048,64]{1,0:T(8,128)(2,1)} %copy.21.refs_2_) | copy-start | bytes 786436
  157.4 5.2 %copy-start.13 = (s32[2]{0:T(128)S(1)}, s32[2]{0:T(128)}, u32[]{:S(2)}) copy-start(s32[2]{0:T(128)} %param.19) | copy-start | bytes 28
  158.7 6.1 %collective-permute-start.19 = (f32[6,16,64]{2,1,0:T(8,128)S(1)}, f32[6,16,64]{2,1,0:T(8,128)S(1)}, u32[]{:S(2)}, u32[]{:S(2)}) collective-permute-start(f32[6,16,64]{2,1,0:T(8,128)S(1)} %get-tuple-element.48), channel_id=1, source_target_pairs={{0,4},{4,8},{8,12},{12,0},{1,5},{5,9},{9,13},{13,1},{2,6},{6,10},{... | collective-permute-start | bytes 73736 | tf_op jit(solution)/shard_map/ppermute | solution.py:17
  160.2 4.8 %collective-permute-start.21 = (f32[6,16,64]{2,1,0:T(8,128)S(1)}, f32[6,16,64]{2,1,0:T(8,128)}, u32[]{:S(2)}, u32[]{:S(2)}) collective-permute-start(f32[6,16,64]{2,1,0:T(8,128)S(1)} %get-tuple-element.49), channel_id=1, source_target_pairs={{0,12},{4,0},{8,4},{12,8},{1,13},{5,1},{9,5},{13,9},{2,14},{6,2},{... | collective-permute-start | bytes 73736 | tf_op jit(solution)/shard_map/ppermute | solution.py:17
  162.6 5.1 %collective-permute-start.20 = (f32[6,16,64]{2,1,0:T(8,128)S(1)}, f32[6,16,64]{2,1,0:T(8,128)}, u32[]{:S(2)}, u32[]{:S(2)}) collective-permute-start(f32[6,16,64]{2,1,0:T(8,128)S(1)} %get-tuple-element.50), channel_id=1, source_target_pairs={{0,8},{4,12},{8,0},{12,4},{1,9},{5,13},{9,1},{13,5},{2,10},{6,14},... | collective-permute-start | bytes 73736 | tf_op jit(solution)/shard_map/ppermute | solution.py:17
  162.6 6.0 %collective-permute-start.28 = (s32[2]{0:T(128)S(1)}, s32[2]{0:T(128)S(1)}, u32[]{:S(2)}, u32[]{:S(2)}) collective-permute-start(s32[2]{0:T(128)S(1)} %copy-done.13), channel_id=1, source_target_pairs={{0,2},{2,0},{1,3},{3,1},{4,6},{6,4},{5,7},{7,5},{8,10},{10,8},{9,1... | collective-permute-start | bytes 32 | tf_op jit(solution)/shard_map/ppermute | solution.py:17
  168.5 2.3 %collective-permute-start.24 = (f32[6,16,64]{2,1,0:T(8,128)S(1)}, f32[6,16,64]{2,1,0:T(8,128)S(1)}, u32[]{:S(2)}, u32[]{:S(2)}) collective-permute-start(f32[6,16,64]{2,1,0:T(8,128)S(1)} %fusion.12), channel_id=1, source_target_pairs={{0,1},{1,0},{2,3},{3,2},{4,5},{5,4},{6,7},{7,6},{8,9},{9,8},{10,11... | collective-permute-start | bytes 73736 | tf_op jit(solution)/shard_map/ppermute | solution.py:310
  168.6 3.9 %collective-permute-start.23 = (f32[6,16,64]{2,1,0:T(8,128)S(1)}, f32[6,16,64]{2,1,0:T(8,128)S(1)}, u32[]{:S(2)}, u32[]{:S(2)}) collective-permute-start(f32[6,16,64]{2,1,0:T(8,128)S(1)} %fusion.12), channel_id=1, source_target_pairs={{0,3},{1,2},{2,1},{3,0},{4,7},{5,6},{6,5},{7,4},{8,11},{9,10},{10,... | collective-permute-start | bytes 73736 | tf_op jit(solution)/shard_map/ppermute | solution.py:310
  170.5 4.1 %collective-permute-start.22 = (f32[6,16,64]{2,1,0:T(8,128)S(1)}, f32[6,16,64]{2,1,0:T(8,128)S(1)}, u32[]{:S(2)}, u32[]{:S(2)}) collective-permute-start(f32[6,16,64]{2,1,0:T(8,128)S(1)} %fusion.12), channel_id=1, source_target_pairs={{0,2},{1,3},{2,0},{3,1},{4,6},{5,7},{6,4},{7,5},{8,10},{9,11},{10,... | collective-permute-start | bytes 73736 | tf_op jit(solution)/shard_map/ppermute | solution.py:310
  176.1 3.7 %collective-permute-start.25 = (f32[4,512]{1,0:T(4,128)S(1)}, f32[4,512]{1,0:T(4,128)S(1)}, u32[]{:S(2)}, u32[]{:S(2)}) collective-permute-start(f32[4,512]{1,0:T(4,128)S(1)} %fusion.20), channel_id=1, source_target_pairs={{0,12},{4,0},{8,4},{12,8},{1,13},{5,1},{9,5},{13,9},{2,14},{6,2},{... | collective-permute-start | bytes 24584 | tf_op jit(solution)/shard_map/ppermute | solution.py:17
  177.1 5.7 %collective-permute-start.27 = (f32[4,512]{1,0:T(4,128)S(1)}, f32[4,512]{1,0:T(4,128)S(1)}, u32[]{:S(2)}, u32[]{:S(2)}) collective-permute-start(f32[4,512]{1,0:T(4,128)S(1)} %fusion.20), channel_id=1, source_target_pairs={{0,4},{4,8},{8,12},{12,0},{1,5},{5,9},{9,13},{13,1},{2,6},{6,10},{... | collective-permute-start | bytes 24584 | tf_op jit(solution)/shard_map/ppermute | solution.py:17
  178.3 4.5 %collective-permute-start.26 = (f32[4,512]{1,0:T(4,128)S(1)}, f32[4,512]{1,0:T(4,128)S(1)}, u32[]{:S(2)}, u32[]{:S(2)}) collective-permute-start(f32[4,512]{1,0:T(4,128)S(1)} %fusion.20), channel_id=1, source_target_pairs={{0,8},{4,12},{8,0},{12,4},{1,9},{5,13},{9,1},{13,5},{2,10},{6,14},... | collective-permute-start | bytes 24584 | tf_op jit(solution)/shard_map/ppermute | solution.py:17
  (2 other events, 2.2 us)

commit v11 on v9

--- a/solution.py
+++ b/solution.py
@@ -52,16 +52,17 @@
     return lax.optimization_barrier((value,) + earlier)[0]
 
 
-def spread_features(flat, far):
+def spread_features(flat):
     pieces = []
     for turn in range(2):
         pairs = []
         for block in range(4):
             example, core = block // 2, block % 2
-            for source_core in range(2):
-                target = block ^ (2 * turn + (source_core ^ core))
-                source = block * 4 + (example ^ far) * 2 + source_core
-                pairs.append((source, target * 4 + example * 2 + core))
+            for far in range(2):
+                for source_core in range(2):
+                    target = block ^ (2 * (turn if far else 1 - turn) + (source_core ^ core))
+                    source = block * 4 + (example ^ far) * 2 + source_core
+                    pairs.append((source, target * 4 + example * 2 + core))
         pieces.append(lax.ppermute(flat, ("tensor", "example", "test"), pairs))
     return pieces
 
@@ -69,7 +70,8 @@
 def arrived_features(pieces, *earlier):
     pieces = lax.optimization_barrier((*pieces, *earlier))
     holder = lax.axis_index("example") * 2 + lax.axis_index("test")
-    return jnp.where((lax.axis_index("tensor") ^ holder) < 2, pieces[0], pieces[1])
+    far_first = (lax.axis_index("tensor") ^ holder) < 2
+    return [jnp.where(far_first, *pieces[:2]), jnp.where(far_first, *pieces[1::-1])]
 
 
 def gathered_features(flat, n_ex, n_cores):
@@ -169,16 +171,21 @@
     hid_part = w_gate.shape[1] // n_cores
 
     def forward(tokens, weight):
-        return jnp.dot(tokens, weight, preferred_element_type=F32)
+        return pack(jnp.dot(tokens, weight, preferred_element_type=F32))
 
     def core_sum(product, begin, *earlier):
+        packed = product.dtype == jnp.float16
+
         def share_of(index):
             return lax.dynamic_slice(product, (begin, index * hid_part), (tok_rows, hid_part))
 
         kept = share_of(core)
+        if packed:
+            kept = unpack(kept)
         for step in range(1, n_cores):
-            sent = pack(share_of(lax.rem(core + step, n_cores)))
-            kept = kept + unpack(after(shift(sent, "test", step), *earlier))
+            sent = share_of(lax.rem(core + step, n_cores))
+            got = shift(sent if packed else pack(sent), "test", step)
+            kept = kept + unpack(after(got, *earlier))
         return kept
 
     flat_acts = activations.reshape(tok_rows, d_local)
@@ -191,23 +198,22 @@
     projs = [hid_proj[:, layer * width : (layer + 1) * width] for layer in range(3)]
     positions = jnp.arange(seq_len, dtype=jnp.int32)
     token_mask = (positions[None, :] < lengths[:, None]).astype(F32)
-    early = (model_acts, model_grad, token_mask, *projs)
+    all_groups = gather_in_order(groups, "example")
+    early = (all_groups, model_acts, model_grad, token_mask, *projs)
 
     direct = (n_z, n_ex, n_cores) == (4, 2, 2)
     examples = [slice(e * seq_len, (e + 1) * seq_len) for e in range(ex_loc)]
     arrived, arrived_down = [], []
     if direct:
-        acts_far = [arrived_features(spread_features(flat_acts, 1), *early)]
-        acts_near = spread_features(flat_acts, 0)
+        acts_far, acts_near = arrived_features(spread_features(flat_acts), *early)
+        acts_far = [acts_far]
     else:
         acts_near, *acts_far = gathered_features(flat_acts, n_ex, n_cores)
         grad_near, *grad_far = gathered_features(flat_grad, n_ex, n_cores)
     gate_far = [forward(one, w_gate) for one in acts_far]
     up_far = [forward(after(one, *gate_far), w_up) for one in acts_far]
     if direct:
-        grad_ready = after(flat_grad, *up_far)
-        grad_far, grad_near = spread_features(grad_ready, 1), spread_features(grad_ready, 0)
-        acts_near = arrived_features(acts_near, *up_far)
+        grad_all = spread_features(after(flat_grad, *up_far))
     gate_near = forward(after(acts_near, *up_far), w_gate)
     up_near = forward(after(acts_near, gate_near), w_up)
     for step, (gate, up) in enumerate(zip(gate_far, up_far), 1):
@@ -215,9 +221,10 @@
         received = shift(both, "example", step)
         arrived.append(received)
     if direct:
-        grad_far = [arrived_features(grad_far, both)]
-        grad_near = arrived_features(grad_near, both)
-    down_all = dot_rows(jnp.concatenate([*grad_far, grad_near]), w_down)
+        grad_all = arrived_features(grad_all, both)
+    else:
+        grad_all = [*grad_far, grad_near]
+    down_all = dot_rows(jnp.concatenate(grad_all), w_down)
     for step in range(1, n_ex):
         sent = pack(core_sum(down_all, (step - 1) * tok_rows))
         arrived_down.append(shift(sent, "example", step))
@@ -283,7 +290,6 @@
     )
     all_scores = jnp.sum(gather_in_order(partial_scores, "tensor"), 0)
     scores = lax.dynamic_slice_in_dim(all_scores, ex_index * ex_loc, ex_loc, 0)
-    all_groups = gather_in_order(groups, "example")
     group_onehot = (
         all_groups.reshape(-1)[:, None] == jnp.arange(NGROUP, dtype=jnp.int32)[None, :]
     ).astype(F32)

time: 178 us -> 179 us (level)
  starting transfers between devices: 74 us -> 64.6 us
  waiting for transfers between devices: 34.2 us -> 41.1 us
  local copies, waits for them, and re-layouts: 7.95 us -> 12.5 us
  other arithmetic: 21.5 us -> 17.1 us
  matrix products: 29.1 us -> 32.7 us
    ppermute x18, waiting for transfers between devices: 20.3 us -> 37.1 us  [shift(): return lax.ppermute(value, axis, [(i, (i + step) % n) for i in range(n)])]
    ppermute x8 -> x4, waiting for transfers between devices: 10.3 us -> 0.29 us  [spread_features(): pieces.append(lax.ppermute(flat, ('tensor', 'example', 'test'), pairs))]
    ppermute x8 -> x4, starting transfers between devices: 38.8 us -> 29 us  [spread_features(): pieces.append(lax.ppermute(flat, ('tensor', 'example', 'test'), pairs))]
    dot_general x4, matrix products: 21.2 us -> 24.9 us  [forward(): return pack(jnp.dot(tokens, weight, preferred_element_type=F32))]
    dynamic_slice x0 -> x4, local copies, waits for them, and re-layouts: none -> 2.44 us  [share_of(): lax.dynamic_slice(product, (begin, index * hid_part), (tok_rows, hid_part))]
    convert_element_type x9 -> x5, other arithmetic: 7.6 us -> 5.42 us  [pack(): return (value * SEND_SCALE).astype(jnp.float16)]
    unnamed x41, local copies, waits for them, and re-layouts: 4.16 us -> 6.27 us
  transfers between devices with their start and end apart: 29 -> 25, of which waited for: 14 -> 13; matrix products, arithmetic and copies ran while one was open for 29% -> 21% of each run, Pallas kernels for 4% -> 4%
where the time goes in v11:
time: 179 us; the launch traced here: 178 us
  starting transfers between devices  64.6 us (36%)
  waiting for transfers between devices  41.1 us (23%)
  matrix products  32.7 us (18%)
  other arithmetic  17.1 us (10%)
  local copies, waits for them, and re-layouts  12.5 us (7%)
  Pallas kernels  8.69 us (5%)
    ppermute x18, waiting for transfers between devices, shift(): return lax.ppermute(value, axis, [(i, (i + step) % n) for i in range(n)])  37.1 us
    ppermute x18, starting transfers between devices, shift(): return lax.ppermute(value, axis, [(i, (i + step) % n) for i in range(n)])  32.9 us
    ppermute x4, starting transfers between devices, spread_features(): pieces.append(lax.ppermute(flat, ('tensor', 'example', 'test'), pairs))  29 us
    dot_general x4, matrix products, forward(): return pack(jnp.dot(tokens, weight, preferred_element_type=F32))  24.9 us
    pallas_call x1, Pallas kernels, dot_rows(): pl.pallas_call(dot_rows_kernel, out_shape=jax.ShapeDtypeStruct((rows, hid...  7.49 us
    unnamed x41, local copies, waits for them, and re-layouts  6.27 us
    convert_element_type x5, other arithmetic, pack(): return (value * SEND_SCALE).astype(jnp.float16)  5.42 us
    mul x1, other arithmetic, on_device(): silu_gate = gate_act * sigmoid_gate  4.11 us
  transfers between devices with their start and end apart: 25, of which 13 were waited for; matrix products, arithmetic and copies ran while one was open for 21% of the time, Pallas kernels for 4%

profile of v11, /device:TPU:0, one launch (start us, length us, event | category | flops | bytes accessed | tf_op | source)
XLA Modules:
  0.0 177.9 jit_solution(8638607743139528056)
XLA Ops:
  0.6 4.1 %collective-permute-start = (bf16[256,1280]{1,0:T(8,128)(2,1)}, bf16[256,1280]{1,0:T(8,128)(2,1)}, u32[]{:S(2)}, u32[]{:S(2)}) collective-permute-start(bf16[256,1280]{1,0:T(8,128)(2,1)} %bitcast.97), channel_id=1, source_target_pairs={{0,8},{1,12},{2,0},{3,4},{4,9},{5,13},{6,1},{7,5},{10,2},{11,6},{8... | collective-permute-start | bytes 1966088 | tf_op jit(solution)/shard_map/ppermute | solution.py:66
  4.7 6.6 %collective-permute-start.1 = (bf16[256,1280]{1,0:T(8,128)(2,1)}, bf16[256,1280]{1,0:T(8,128)(2,1)}, u32[]{:S(2)}, u32[]{:S(2)}) collective-permute-start(bf16[256,1280]{1,0:T(8,128)(2,1)} %bitcast.98), channel_id=1, source_target_pairs={{0,0},{1,4},{2,8},{3,12},{4,1},{5,5},{6,9},{7,13},{10,10},{11,14},... | collective-permute-start | bytes 1966088 | tf_op jit(solution)/shard_map/ppermute | solution.py:66
  11.3 1.8 %fusion.24 = (bf16[2048,64]{0,1:T(8,128)(2,1)S(1)}, bf16[2048,64]{0,1:T(8,128)(2,1)}) fusion(bf16[4096,192]{0,1:T(8,128)(2,1)} %param.16, s32[]{:T(128)S(6)} %select_n.62, s32[]{:T(128)S(6)} %add.164), kind=kLoop, calls=%fused_computation.87 | loop fusion | bytes 1048584 | tf_op jit(solution)/shard_map/slice | solution.py:198
  13.1 2.0 %copy.21.refs_2_ = bf16[2048,64]{1,0:T(8,128)(2,1)} copy(bf16[2048,64]{0,1:T(8,128)(2,1)} %get-tuple-element.35) | data formatting | bytes 524288
  15.1 1.0 copy.22.refs_3_
  16.1 1.4 fusion.13
  17.5 1.6 fusion.10
  19.9 1.4 broadcast_select_fusion.2
  21.3 7.3 %fusion = f16[256,4096]{1,0:T(8,128)(2,1)S(1)} fusion(bf16[256,1280]{1,0:T(8,128)(2,1)S(1)} %get-tuple-element.19, bf16[1280,4096]{1,0:T(8,128)(2,1)} %param.12), kind=kOutput, calls=%fused_computation.4 | convolution fusion | flops 2686451712 | bytes 13238272 | tf_op jit(solution)/shard_map/dot_general | solution.py:174
  28.6 7.3 %fusion.1 = f16[256,4096]{1,0:T(8,128)(2,1)S(1)} fusion(bf16[256,1280]{1,0:T(8,128)(2,1)S(1)} %get-tuple-element.19, bf16[1280,4096]{1,0:T(8,128)(2,1)} %param.13), kind=kOutput, calls=%fused_computation.5 | convolution fusion | flops 2686451712 | bytes 13238272 | tf_op jit(solution)/shard_map/dot_general | solution.py:174
  36.0 17.6 %collective-permute-start.3 = (bf16[256,1280]{1,0:T(8,128)(2,1)S(1)}, bf16[256,1280]{1,0:T(8,128)(2,1)S(1)}, u32[]{:S(2)}, u32[]{:S(2)}) collective-permute-start(bf16[256,1280]{1,0:T(8,128)(2,1)S(1)} %bitcast.95), channel_id=1, source_target_pairs={{0,8},{1,12},{2,0},{3,4},{4,9},{5,13},{6,1},{7,5},{10,2},{11,6},{8... | collective-permute-start | bytes 1966088 | tf_op jit(solution)/shard_map/ppermute | solution.py:66
  53.6 0.7 collective-permute-start.4
  54.3 3.1 %fusion.2 = f16[256,4096]{1,0:T(8,128)(2,1)S(1)} fusion(bf16[256,1280]{1,0:T(8,128)(2,1)S(1)} %get-tuple-element.22, bf16[1280,4096]{1,0:T(8,128)(2,1)S(1)} %bitcast.105), kind=kOutput, calls=%fused_computation.6 | convolution fusion | flops 2686451712 | bytes 13238272 | tf_op jit(solution)/shard_map/dot_general | solution.py:174
  57.7 4.6 %collective-permute-start.5 = (f16[256,2048]{1,0:T(8,128)(2,1)S(1)}, f16[256,2048]{1,0:T(8,128)(2,1)S(1)}, u32[]{:S(2)}, u32[]{:S(2)}) collective-permute-start(f16[256,2048]{1,0:T(8,128)(2,1)S(1)} %constant_dynamic-slice_fusion.5), channel_id=1, source_target_pairs={{0,1},{1,0},{2,3},{3,2},{4,5},{5,4},{6,7},{7,6},{8,9},{9,8},{10,11... | collective-permute-start | bytes 3145736 | tf_op jit(solution)/shard_map/ppermute | solution.py:15
  62.6 7.2 %fusion.3 = f16[256,4096]{1,0:T(8,128)(2,1)S(1)} fusion(bf16[256,1280]{1,0:T(8,128)(2,1)S(1)} %get-tuple-element.22, bf16[1280,4096]{1,0:T(8,128)(2,1)} %param.13), kind=kOutput, calls=%fused_computation.7 | convolution fusion | flops 2686451712 | bytes 13238272 | tf_op jit(solution)/shard_map/dot_general | solution.py:174
  70.6 1.8 %fusion.4 = f16[2,256,2048]{2,1,0:T(8,128)(2,1)} fusion(f32[1,256,2048]{2,1,0:T(8,128)S(1)} %multiply_bitcast_fusion, f32[1,256,2048]{2,1,0:T(8,128)S(1)} %multiply_bitcast_fusion.1), kind=kLoop, calls=%fused_computation.9 | loop fusion | flops 3145728 | bytes 6291456 | tf_op jit(solution)/shard_map/convert_element_type | solution.py:19
  72.7 0.8 slice-done
  73.5 1.3 slice-done.1
  75.4 7.5 %shard_map.113 = f32[512,4096]{1,0:T(8,128)S(1)} custom-call(bf16[512,1280]{1,0:T(8,128)(2,1)S(1)} %pad_maximum_fusion.tokens_ref, bf16[4096,1280]{1,0:T(8,128)(2,1)S(1)} %bitcast.92), custom_call_target="tpu_custom_call" | custom-call | flops 1 | bytes 1 | tf_op jit(solution)/shard_map/pallas_call | solution.py:97
  84.0 1.8 constant_dynamic-slice_fusion.2
  86.6 1.4 multiply_convert_fusion.1
  87.9 2.1 %collective-permute-start.13 = (f16[256,192]{0,1:T(8,128)(2,1)S(1)}, f16[256,192]{0,1:T(8,128)(2,1)S(1)}, u32[]{:S(2)}, u32[]{:S(2)}) collective-permute-start(f16[256,192]{0,1:T(8,128)(2,1)S(1)} %multiply_convert_fusion.5), channel_id=1, source_target_pairs={{0,4},{4,8},{8,12},{12,0},{1,5},{5,9},{9,13},{13,1},{2,6},{6,10},{... | collective-permute-start | bytes 294920 | tf_op jit(solution)/shard_map/ppermute | solution.py:15
  90.1 12.6 %collective-permute-start.14 = (f16[256,192]{0,1:T(8,128)(2,1)S(1)}, f16[256,192]{0,1:T(8,128)(2,1)}, u32[]{:S(2)}, u32[]{:S(2)}) collective-permute-start(f16[256,192]{0,1:T(8,128)(2,1)S(1)} %multiply_convert_fusion.5), channel_id=1, source_target_pairs={{0,8},{4,12},{8,0},{12,4},{1,9},{5,13},{9,1},{13,5},{2,10},{6,14},... | collective-permute-start | bytes 294920 | tf_op jit(solution)/shard_map/ppermute | solution.py:15
  102.7 1.9 %collective-permute-start.15 = (f16[256,192]{0,1:T(8,128)(2,1)S(1)}, f16[256,192]{0,1:T(8,128)(2,1)}, u32[]{:S(2)}, u32[]{:S(2)}) collective-permute-start(f16[256,192]{0,1:T(8,128)(2,1)S(1)} %multiply_convert_fusion.5), channel_id=1, source_target_pairs={{0,12},{4,0},{8,4},{12,8},{1,13},{5,1},{9,5},{13,9},{2,14},{6,2},{... | collective-permute-start | bytes 294920 | tf_op jit(solution)/shard_map/ppermute | solution.py:15
  104.7 1.3 collective-permute-start.10
  106.0 4.1 %collective-permute-done.14 = f16[256,192]{0,1:T(8,128)(2,1)} collective-permute-done((f16[256,192]{0,1:T(8,128)(2,1)S(1)}, f16[256,192]{0,1:T(8,128)(2,1)}, u32[]{:S(2)}, u32[]{:S(2)}) %collective-permute-start.14) | collective-permute-done | bytes 98336 | tf_op jit(solution)/shard_map/ppermute | solution.py:15
  110.1 15.5 %collective-permute-done.7 = f16[2,256,2048]{2,1,0:T(8,128)(2,1)} collective-permute-done((f16[2,256,2048]{2,1,0:T(8,128)(2,1)}, f16[2,256,2048]{2,1,0:T(8,128)(2,1)}, u32[]{:S(2)}, u32[]{:S(2)}) %collective-permute-start.7) | collective-permute-done | bytes 2097184 | tf_op jit(solution)/shard_map/ppermute | solution.py:15
  125.6 1.7 multiply_add_fusion.1
  127.3 1.1 copy.17
  128.7 1.9 %multiply_convert_fusion.3 = f16[256,2048]{1,0:T(8,128)(2,1)S(1)} fusion(f32[512,4096]{1,0:T(8,128)} %copy-done.1, s32[]{:T(128)S(6)} %select_n.64), kind=kLoop, calls=%fused_computation.21 | loop fusion | flops 1048576 | bytes 3145732 | tf_op jit(solution)/shard_map/convert_element_type | solution.py:19
  130.9 4.1 %fusion.7 = (f32[256,2048]{1,0:T(8,128)S(1)}, f32[256,2048]{1,0:T(8,128)S(1)}) fusion(f16[256,2048]{1,0:T(8,128)(2,1)} %collective-permute-done.12, f16[2,256,2048]{2,1,0:T(8,128)(2,1)} %collective-permute-done.7, f16[256,4096]{1,0:T(8,128)(2,1)} %copy-done.6, s32[]{:T(128)S(6)} %select_n.62, f16[256,2048]{1,0:T(8,128)(2,1)} %collective-permute-done.11, ...), kind=kLoop, calls=%fused_computation.17 | loop fusion | flops 11010048 | bytes 10485764 | tf_op jit(solution)/shard_map/mul | solution.py:258
  135.0 2.3 %fusion.8 = f32[256,64]{0,1:T(8,128)S(1)} fusion(f32[256,2048]{1,0:T(8,128)S(1)} %get-tuple-element.32.refs_1_, f16[256,2048]{1,0:T(8,128)(2,1)} %collective-permute-done.11, f16[2,256,2048]{2,1,0:T(8,128)(2,1)} %collective-permute-done.7, f16[256,4096]{1,0:T(8,128)(2,1)S(1)} %copy-done.5, s32[]{:T(128)S(6)} %select_n.62, bf16[4096,192]{0,1:T(8,128)(2,1)} %param.16, ...), kind=kOutput, calls=%fused_computation.29 | convolution fusion | flops 71303168 | bytes 5572096 | tf_op jit(solution)/shard_map/dot_general | solution.py:261
  137.7 10.4 %collective-permute-done.10 = f16[256,2048]{1,0:T(8,128)(2,1)} collective-permute-done((f16[256,2048]{1,0:T(8,128)(2,1)}, f16[256,2048]{1,0:T(8,128)(2,1)}, u32[]{:S(2)}, u32[]{:S(2)}) %collective-permute-start.10) | collective-permute-done | bytes 1048608 | tf_op jit(solution)/shard_map/ppermute | solution.py:15
  148.1 2.5 %multiply_add_fusion.down_ref = f32[256,2048]{1,0:T(8,128)S(1)} fusion(f16[256,2048]{1,0:T(8,128)(2,1)} %collective-permute-done.10, f16[256,2048]{1,0:T(8,128)(2,1)S(1)} %collective-permute-done.8, f32[512,4096]{1,0:T(8,128)} %copy-done.1, s32[]{:T(128)S(6)} %select_n.62), kind=kLoop, calls=%fused_computation.18 | loop fusion | flops 3145728 | bytes 6291460 | tf_op jit(solution)/shard_map/add | solution.py:256
  150.6 1.2 shard_map.114
  151.9 3.3 %collective-permute-start.17 = (f32[6,16,64]{2,1,0:T(8,128)S(1)}, f32[6,16,64]{2,1,0:T(8,128)}, u32[]{:S(2)}, u32[]{:S(2)}) collective-permute-start(f32[6,16,64]{2,1,0:T(8,128)S(1)} %get-tuple-element.44), channel_id=1, source_target_pairs={{0,8},{4,12},{8,0},{12,4},{1,9},{5,13},{9,1},{13,5},{2,10},{6,14},... | collective-permute-start | bytes 73736 | tf_op jit(solution)/shard_map/ppermute | solution.py:15
  155.3 2.4 %collective-permute-start.18 = (f32[6,16,64]{2,1,0:T(8,128)S(1)}, f32[6,16,64]{2,1,0:T(8,128)}, u32[]{:S(2)}, u32[]{:S(2)}) collective-permute-start(f32[6,16,64]{2,1,0:T(8,128)S(1)} %get-tuple-element.43), channel_id=1, source_target_pairs={{0,12},{4,0},{8,4},{12,8},{1,13},{5,1},{9,5},{13,9},{2,14},{6,2},{... | collective-permute-start | bytes 73736 | tf_op jit(solution)/shard_map/ppermute | solution.py:15
  158.7 0.7 collective-permute-done.18
  159.4 0.9 fusion.19
  160.4 2.6 %collective-permute-start.19 = (f32[6,16,64]{2,1,0:T(8,128)S(1)}, f32[6,16,64]{2,1,0:T(8,128)S(1)}, u32[]{:S(2)}, u32[]{:S(2)}) collective-permute-start(f32[6,16,64]{2,1,0:T(8,128)S(1)} %fusion.19), channel_id=1, source_target_pairs={{0,2},{1,3},{2,0},{3,1},{4,6},{5,7},{6,4},{7,5},{8,10},{9,11},{10,... | collective-permute-start | bytes 73736 | tf_op jit(solution)/shard_map/ppermute | solution.py:281
  163.1 2.3 %collective-permute-done.19 = f32[6,16,64]{2,1,0:T(8,128)S(1)} collective-permute-done((f32[6,16,64]{2,1,0:T(8,128)S(1)}, f32[6,16,64]{2,1,0:T(8,128)S(1)}, u32[]{:S(2)}, u32[]{:S(2)}) %collective-permute-start.19) | collective-permute-done | bytes 24608 | tf_op jit(solution)/shard_map/ppermute | solution.py:281
  165.3 1.4 collective-permute-done.20
  166.9 1.3 fusion.25
  168.2 2.6 %collective-permute-start.22 = (f32[4,512]{1,0:T(4,128)S(1)}, f32[4,512]{1,0:T(4,128)S(1)}, u32[]{:S(2)}, u32[]{:S(2)}) collective-permute-start(f32[4,512]{1,0:T(4,128)S(1)} %fusion.25), channel_id=1, source_target_pairs={{0,12},{4,0},{8,4},{12,8},{1,13},{5,1},{9,5},{13,9},{2,14},{6,2},{... | collective-permute-start | bytes 24584 | tf_op jit(solution)/shard_map/ppermute | solution.py:15
  171.5 0.7 collective-permute-done.22
  172.2 3.3 %collective-permute-done.23 = f32[4,512]{1,0:T(4,128)S(1)} collective-permute-done((f32[4,512]{1,0:T(4,128)S(1)}, f32[4,512]{1,0:T(4,128)S(1)}, u32[]{:S(2)}, u32[]{:S(2)}) %collective-permute-start.23) | collective-permute-done | bytes 8224 | tf_op jit(solution)/shard_map/ppermute | solution.py:15
  175.5 0.9 collective-permute-done.24
  176.5 0.9 fusion.21
  (96 shorter events, 8.7 us)
Async XLA Ops:
  0.6 166.2 %copy-start = (bf16[3,16,64,512]{3,2,1,0:T(8,128)(2,1)S(1)}, bf16[3,16,64,512]{3,2,1,0:T(8,128)(2,1)}, u32[]{:S(2)}) copy-start(bf16[3,16,64,512]{3,2,1,0:T(8,128)(2,1)} %param.17) | copy-start | bytes 9437188
  0.6 19.2 %collective-permute-start = (bf16[256,1280]{1,0:T(8,128)(2,1)}, bf16[256,1280]{1,0:T(8,128)(2,1)}, u32[]{:S(2)}, u32[]{:S(2)}) collective-permute-start(bf16[256,1280]{1,0:T(8,128)(2,1)} %bitcast.97), channel_id=1, source_target_pairs={{0,8},{1,12},{2,0},{3,4},{4,9},{5,13},{6,1},{7,5},{10,2},{11,6},{8... | collective-permute-start | bytes 1966088 | tf_op jit(solution)/shard_map/ppermute | solution.py:66
  4.7 15.1 %collective-permute-start.1 = (bf16[256,1280]{1,0:T(8,128)(2,1)}, bf16[256,1280]{1,0:T(8,128)(2,1)}, u32[]{:S(2)}, u32[]{:S(2)}) collective-permute-start(bf16[256,1280]{1,0:T(8,128)(2,1)} %bitcast.98), channel_id=1, source_target_pairs={{0,0},{1,4},{2,8},{3,12},{4,1},{5,5},{6,9},{7,13},{10,10},{11,14},... | collective-permute-start | bytes 1966088 | tf_op jit(solution)/shard_map/ppermute | solution.py:66
  11.3 8.3 %collective-permute-start.2 = (s32[2]{0:T(128)}, s32[2]{0:T(128)S(1)}, u32[]{:S(2)}, u32[]{:S(2)}) collective-permute-start(s32[2]{0:T(128)} %param.19), channel_id=1, source_target_pairs={{0,2},{2,0},{1,3},{3,1},{4,6},{6,4},{5,7},{7,5},{8,10},{10,8},{9,1... | collective-permute-start | bytes 32 | tf_op jit(solution)/shard_map/ppermute | solution.py:15
  11.3 8.3 %copy-start.8 = (s32[2]{0:T(128)S(1)}, s32[2]{0:T(128)}, u32[]{:S(2)}) copy-start(s32[2]{0:T(128)} %param.19) | copy-start | bytes 28
  21.2 33.1 %slice-start.3 = ((s8[10485760]{0:T(1024)(128)(4,1)}), s8[4194304]{0:T(1024)(128)(4,1)S(1)}, s32[]{:S(2)}) async-start(s8[10485760]{0:T(1024)(128)(4,1)} %bitcast.104), calls=%async_computation.3 | async-start | bytes 8388608
  21.3 33.1 %slice-start.4 = ((s8[10485760]{0:T(1024)(128)(4,1)}), s8[4194304]{0:T(1024)(128)(4,1)S(1)}, s32[]{:S(2)}) async-start(s8[10485760]{0:T(1024)(128)(4,1)} %bitcast.104), calls=%async_computation.4 | async-start | bytes 8388608
  28.6 7.4 %copy-start.7 = (bf16[2,128,1280]{2,1,0:T(8,128)(2,1)S(1)}, bf16[2,128,1280]{2,1,0:T(8,128)(2,1)}, u32[]{:S(2)}) copy-start(bf16[2,128,1280]{2,1,0:T(8,128)(2,1)} %param.11) | copy-start | bytes 1966084
  28.6 25.7 %slice-start.5 = ((s8[10485760]{0:T(1024)(128)(4,1)}), s8[2097152]{0:T(1024)(128)(4,1)S(1)}, s32[]{:S(2)}) async-start(s8[10485760]{0:T(1024)(128)(4,1)} %bitcast.104), calls=%async_computation.5 | async-start | bytes 4194304
  36.0 36.5 %collective-permute-start.3 = (bf16[256,1280]{1,0:T(8,128)(2,1)S(1)}, bf16[256,1280]{1,0:T(8,128)(2,1)S(1)}, u32[]{:S(2)}, u32[]{:S(2)}) collective-permute-start(bf16[256,1280]{1,0:T(8,128)(2,1)S(1)} %bitcast.95), channel_id=1, source_target_pairs={{0,8},{1,12},{2,0},{3,4},{4,9},{5,13},{6,1},{7,5},{10,2},{11,6},{8... | collective-permute-start | bytes 1966088 | tf_op jit(solution)/shard_map/ppermute | solution.py:66
  53.6 18.8 %collective-permute-start.4 = (bf16[256,1280]{1,0:T(8,128)(2,1)S(1)}, bf16[256,1280]{1,0:T(8,128)(2,1)S(1)}, u32[]{:S(2)}, u32[]{:S(2)}) collective-permute-start(bf16[256,1280]{1,0:T(8,128)(2,1)S(1)} %bitcast.96), channel_id=1, source_target_pairs={{0,0},{1,4},{2,8},{3,12},{4,1},{5,5},{6,9},{7,13},{10,10},{11,14},... | collective-permute-start | bytes 1966088 | tf_op jit(solution)/shard_map/ppermute | solution.py:66
  57.5 26.5 %copy-start.6 = (f16[256,4096]{1,0:T(8,128)(2,1)}, f16[256,4096]{1,0:T(8,128)(2,1)S(1)}, u32[]{:S(2)}) copy-start(f16[256,4096]{1,0:T(8,128)(2,1)S(1)} %fusion.2) | copy-start | bytes 6291460
  57.7 12.1 %collective-permute-start.5 = (f16[256,2048]{1,0:T(8,128)(2,1)S(1)}, f16[256,2048]{1,0:T(8,128)(2,1)S(1)}, u32[]{:S(2)}, u32[]{:S(2)}) collective-permute-start(f16[256,2048]{1,0:T(8,128)(2,1)S(1)} %constant_dynamic-slice_fusion.5), channel_id=1, source_target_pairs={{0,1},{1,0},{2,3},{3,2},{4,5},{5,4},{6,7},{7,6},{8,9},{9,8},{10,11... | collective-permute-start | bytes 3145736 | tf_op jit(solution)/shard_map/ppermute | solution.py:15
  62.5 7.7 %collective-permute-start.6 = (f16[256,2048]{1,0:T(8,128)(2,1)S(1)}, f16[256,2048]{1,0:T(8,128)(2,1)S(1)}, u32[]{:S(2)}, u32[]{:S(2)}) collective-permute-start(f16[256,2048]{1,0:T(8,128)(2,1)S(1)} %constant_dynamic-slice_fusion.4), channel_id=1, source_target_pairs={{0,1},{1,0},{2,3},{3,2},{4,5},{5,4},{6,7},{7,6},{8,9},{9,8},{10,11... | collective-permute-start | bytes 3145736 | tf_op jit(solution)/shard_map/ppermute | solution.py:15
  69.8 13.9 %copy-start.4 = (f16[256,4096]{1,0:T(8,128)(2,1)}, f16[256,4096]{1,0:T(8,128)(2,1)S(1)}, u32[]{:S(2)}) copy-start(f16[256,4096]{1,0:T(8,128)(2,1)S(1)} %fusion.3) | copy-start | bytes 6291460
  69.8 3.7 %slice-start = ((s8[10485760]{0:T(1024)(128)(4,1)}), s8[4194304]{0:T(1024)(128)(4,1)S(1)}, s32[]{:S(2)}) async-start(s8[10485760]{0:T(1024)(128)(4,1)} %bitcast.91), calls=%async_computation | async-start | bytes 8388608
  70.2 4.6 %slice-start.1 = ((s8[10485760]{0:T(1024)(128)(4,1)}), s8[4194304]{0:T(1024)(128)(4,1)S(1)}, s32[]{:S(2)}) async-start(s8[10485760]{0:T(1024)(128)(4,1)} %bitcast.91), calls=%async_computation.1 | async-start | bytes 8388608
  70.6 4.8 %slice-start.2 = ((s8[10485760]{0:T(1024)(128)(4,1)}), s8[2097152]{0:T(1024)(128)(4,1)S(1)}, s32[]{:S(2)}) async-start(s8[10485760]{0:T(1024)(128)(4,1)} %bitcast.91), calls=%async_computation.2 | async-start | bytes 4194304
  72.5 53.2 %collective-permute-start.7 = (f16[2,256,2048]{2,1,0:T(8,128)(2,1)}, f16[2,256,2048]{2,1,0:T(8,128)(2,1)}, u32[]{:S(2)}, u32[]{:S(2)}) collective-permute-start(f16[2,256,2048]{2,1,0:T(8,128)(2,1)} %fusion.4), channel_id=1, source_target_pairs={{0,2},{2,0},{1,3},{3,1},{4,6},{6,4},{5,7},{7,5},{8,10},{10,8},{9,1... | collective-permute-start | bytes 6291464 | tf_op jit(solution)/shard_map/ppermute | solution.py:15
  82.9 3.7 %copy-start.1 = (f32[512,4096]{1,0:T(8,128)}, f32[512,4096]{1,0:T(8,128)S(1)}, u32[]{:S(2)}) copy-start(f32[512,4096]{1,0:T(8,128)S(1)} %shard_map.113) | copy-start | bytes 25165828
  83.1 3.2 %collective-permute-start.9 = (f16[256,2048]{1,0:T(8,128)(2,1)S(1)}, f16[256,2048]{1,0:T(8,128)(2,1)S(1)}, u32[]{:S(2)}, u32[]{:S(2)}) collective-permute-start(f16[256,2048]{1,0:T(8,128)(2,1)S(1)} %multiply_convert_fusion.2), channel_id=1, source_target_pairs={{0,1},{1,0},{2,3},{3,2},{4,5},{5,4},{6,7},{7,6},{8,9},{9,8},{10,11... | collective-permute-start | bytes 3145736 | tf_op jit(solution)/shard_map/ppermute | solution.py:15
  83.9 18.8 %collective-permute-start.11 = (f16[256,2048]{1,0:T(8,128)(2,1)S(1)}, f16[256,2048]{1,0:T(8,128)(2,1)}, u32[]{:S(2)}, u32[]{:S(2)}) collective-permute-start(f16[256,2048]{1,0:T(8,128)(2,1)S(1)} %constant_dynamic-slice_fusion.3), channel_id=1, source_target_pairs={{0,1},{1,0},{2,3},{3,2},{4,5},{5,4},{6,7},{7,6},{8,9},{9,8},{10,11... | collective-permute-start | bytes 3145736 | tf_op jit(solution)/shard_map/ppermute | solution.py:15
  85.7 19.0 %collective-permute-start.12 = (f16[256,2048]{1,0:T(8,128)(2,1)}, f16[256,2048]{1,0:T(8,128)(2,1)}, u32[]{:S(2)}, u32[]{:S(2)}) collective-permute-start(f16[256,2048]{1,0:T(8,128)(2,1)} %constant_dynamic-slice_fusion.2), channel_id=1, source_target_pairs={{0,1},{1,0},{2,3},{3,2},{4,5},{5,4},{6,7},{7,6},{8,9},{9,8},{10,11... | collective-permute-start | bytes 3145736 | tf_op jit(solution)/shard_map/ppermute | solution.py:15
  86.2 18.4 %copy-start.9 = (s32[2]{0:T(128)S(1)}, s32[2]{0:T(128)}, u32[]{:S(2)}) copy-start(s32[2]{0:T(128)} %param.18) | copy-start | bytes 28
  87.9 18.1 %collective-permute-start.13 = (f16[256,192]{0,1:T(8,128)(2,1)S(1)}, f16[256,192]{0,1:T(8,128)(2,1)S(1)}, u32[]{:S(2)}, u32[]{:S(2)}) collective-permute-start(f16[256,192]{0,1:T(8,128)(2,1)S(1)} %multiply_convert_fusion.5), channel_id=1, source_target_pairs={{0,4},{4,8},{8,12},{12,0},{1,5},{5,9},{9,13},{13,1},{2,6},{6,10},{... | collective-permute-start | bytes 294920 | tf_op jit(solution)/shard_map/ppermute | solution.py:15
  90.1 20.1 %collective-permute-start.14 = (f16[256,192]{0,1:T(8,128)(2,1)S(1)}, f16[256,192]{0,1:T(8,128)(2,1)}, u32[]{:S(2)}, u32[]{:S(2)}) collective-permute-start(f16[256,192]{0,1:T(8,128)(2,1)S(1)} %multiply_convert_fusion.5), channel_id=1, source_target_pairs={{0,8},{4,12},{8,0},{12,4},{1,9},{5,13},{9,1},{13,5},{2,10},{6,14},... | collective-permute-start | bytes 294920 | tf_op jit(solution)/shard_map/ppermute | solution.py:15
  102.7 7.4 %collective-permute-start.15 = (f16[256,192]{0,1:T(8,128)(2,1)S(1)}, f16[256,192]{0,1:T(8,128)(2,1)}, u32[]{:S(2)}, u32[]{:S(2)}) collective-permute-start(f16[256,192]{0,1:T(8,128)(2,1)S(1)} %multiply_convert_fusion.5), channel_id=1, source_target_pairs={{0,12},{4,0},{8,4},{12,8},{1,13},{5,1},{9,5},{13,9},{2,14},{6,2},{... | collective-permute-start | bytes 294920 | tf_op jit(solution)/shard_map/ppermute | solution.py:15
  104.7 43.4 %collective-permute-start.10 = (f16[256,2048]{1,0:T(8,128)(2,1)}, f16[256,2048]{1,0:T(8,128)(2,1)}, u32[]{:S(2)}, u32[]{:S(2)}) collective-permute-start(f16[256,2048]{1,0:T(8,128)(2,1)} %multiply_convert_fusion.1), channel_id=1, source_target_pairs={{0,2},{2,0},{1,3},{3,1},{4,6},{6,4},{5,7},{7,5},{8,10},{10,8},{9,1... | collective-permute-start | bytes 3145736 | tf_op jit(solution)/shard_map/ppermute | solution.py:15
  128.6 2.2 %copy-start.5 = (f16[256,4096]{1,0:T(8,128)(2,1)S(1)}, f16[256,4096]{1,0:T(8,128)(2,1)}, u32[]{:S(2)}) copy-start(f16[256,4096]{1,0:T(8,128)(2,1)} %copy-done.4) | copy-start | bytes 6291460
  130.6 7.1 %collective-permute-start.8 = (f16[256,2048]{1,0:T(8,128)(2,1)S(1)}, f16[256,2048]{1,0:T(8,128)(2,1)S(1)}, u32[]{:S(2)}, u32[]{:S(2)}) collective-permute-start(f16[256,2048]{1,0:T(8,128)(2,1)S(1)} %multiply_convert_fusion.3), channel_id=1, source_target_pairs={{0,1},{1,0},{2,3},{3,2},{4,5},{5,4},{6,7},{7,6},{8,9},{9,8},{10,11... | collective-permute-start | bytes 3145736 | tf_op jit(solution)/shard_map/ppermute | solution.py:15
  137.7 12.9 %copy-start.2 = (bf16[2048,64]{1,0:T(8,128)(2,1)S(1)}, bf16[2048,64]{1,0:T(8,128)(2,1)}, u32[]{:S(2)}) copy-start(bf16[2048,64]{1,0:T(8,128)(2,1)} %copy.21.refs_2_) | copy-start | bytes 786436
  137.7 12.9 %copy-start.3 = (bf16[2048,64]{1,0:T(8,128)(2,1)S(1)}, bf16[2048,64]{1,0:T(8,128)(2,1)}, u32[]{:S(2)}) copy-start(bf16[2048,64]{1,0:T(8,128)(2,1)} %copy.22.refs_3_) | copy-start | bytes 786436
  151.8 6.3 %collective-permute-start.16 = (f32[6,16,64]{2,1,0:T(8,128)S(1)}, f32[6,16,64]{2,1,0:T(8,128)}, u32[]{:S(2)}, u32[]{:S(2)}) collective-permute-start(f32[6,16,64]{2,1,0:T(8,128)S(1)} %get-tuple-element.42), channel_id=1, source_target_pairs={{0,4},{4,8},{8,12},{12,0},{1,5},{5,9},{9,13},{13,1},{2,6},{6,10},{... | collective-permute-start | bytes 73736 | tf_op jit(solution)/shard_map/ppermute | solution.py:15
  151.9 6.8 %collective-permute-start.17 = (f32[6,16,64]{2,1,0:T(8,128)S(1)}, f32[6,16,64]{2,1,0:T(8,128)}, u32[]{:S(2)}, u32[]{:S(2)}) collective-permute-start(f32[6,16,64]{2,1,0:T(8,128)S(1)} %get-tuple-element.44), channel_id=1, source_target_pairs={{0,8},{4,12},{8,0},{12,4},{1,9},{5,13},{9,1},{13,5},{2,10},{6,14},... | collective-permute-start | bytes 73736 | tf_op jit(solution)/shard_map/ppermute | solution.py:15
  155.3 4.2 %collective-permute-start.18 = (f32[6,16,64]{2,1,0:T(8,128)S(1)}, f32[6,16,64]{2,1,0:T(8,128)}, u32[]{:S(2)}, u32[]{:S(2)}) collective-permute-start(f32[6,16,64]{2,1,0:T(8,128)S(1)} %get-tuple-element.43), channel_id=1, source_target_pairs={{0,12},{4,0},{8,4},{12,8},{1,13},{5,1},{9,5},{13,9},{2,14},{6,2},{... | collective-permute-start | bytes 73736 | tf_op jit(solution)/shard_map/ppermute | solution.py:15
  160.3 2.8 %collective-permute-start.21 = (f32[6,16,64]{2,1,0:T(8,128)S(1)}, f32[6,16,64]{2,1,0:T(8,128)S(1)}, u32[]{:S(2)}, u32[]{:S(2)}) collective-permute-start(f32[6,16,64]{2,1,0:T(8,128)S(1)} %fusion.19), channel_id=1, source_target_pairs={{0,1},{1,0},{2,3},{3,2},{4,5},{5,4},{6,7},{7,6},{8,9},{9,8},{10,11... | collective-permute-start | bytes 73736 | tf_op jit(solution)/shard_map/ppermute | solution.py:281
  160.4 5.0 %collective-permute-start.19 = (f32[6,16,64]{2,1,0:T(8,128)S(1)}, f32[6,16,64]{2,1,0:T(8,128)S(1)}, u32[]{:S(2)}, u32[]{:S(2)}) collective-permute-start(f32[6,16,64]{2,1,0:T(8,128)S(1)} %fusion.19), channel_id=1, source_target_pairs={{0,2},{1,3},{2,0},{3,1},{4,6},{5,7},{6,4},{7,5},{8,10},{9,11},{10,... | collective-permute-start | bytes 73736 | tf_op jit(solution)/shard_map/ppermute | solution.py:281
  163.0 3.7 %collective-permute-start.20 = (f32[6,16,64]{2,1,0:T(8,128)S(1)}, f32[6,16,64]{2,1,0:T(8,128)S(1)}, u32[]{:S(2)}, u32[]{:S(2)}) collective-permute-start(f32[6,16,64]{2,1,0:T(8,128)S(1)} %fusion.19), channel_id=1, source_target_pairs={{0,3},{1,2},{2,1},{3,0},{4,7},{5,6},{6,5},{7,4},{8,11},{9,10},{10,... | collective-permute-start | bytes 73736 | tf_op jit(solution)/shard_map/ppermute | solution.py:281
  168.2 4.0 %collective-permute-start.22 = (f32[4,512]{1,0:T(4,128)S(1)}, f32[4,512]{1,0:T(4,128)S(1)}, u32[]{:S(2)}, u32[]{:S(2)}) collective-permute-start(f32[4,512]{1,0:T(4,128)S(1)} %fusion.25), channel_id=1, source_target_pairs={{0,12},{4,0},{8,4},{12,8},{1,13},{5,1},{9,5},{13,9},{2,14},{6,2},{... | collective-permute-start | bytes 24584 | tf_op jit(solution)/shard_map/ppermute | solution.py:15
  170.9 4.6 %collective-permute-start.23 = (f32[4,512]{1,0:T(4,128)S(1)}, f32[4,512]{1,0:T(4,128)S(1)}, u32[]{:S(2)}, u32[]{:S(2)}) collective-permute-start(f32[4,512]{1,0:T(4,128)S(1)} %fusion.25), channel_id=1, source_target_pairs={{0,8},{4,12},{8,0},{12,4},{1,9},{5,13},{9,1},{13,5},{2,10},{6,14},... | collective-permute-start | bytes 24584 | tf_op jit(solution)/shard_map/ppermute | solution.py:15
  170.9 5.4 %collective-permute-start.24 = (f32[4,512]{1,0:T(4,128)S(1)}, f32[4,512]{1,0:T(4,128)S(1)}, u32[]{:S(2)}, u32[]{:S(2)}) collective-permute-start(f32[4,512]{1,0:T(4,128)S(1)} %fusion.25), channel_id=1, source_target_pairs={{0,4},{4,8},{8,12},{12,0},{1,5},{5,9},{9,13},{13,1},{2,6},{6,10},{... | collective-permute-start | bytes 24584 | tf_op jit(solution)/shard_map/ppermute | solution.py:15

commit v12 on v11

--- a/solution.py
+++ b/solution.py
@@ -72,6 +72,34 @@
     holder = lax.axis_index("example") * 2 + lax.axis_index("test")
     far_first = (lax.axis_index("tensor") ^ holder) < 2
     return [jnp.where(far_first, *pieces[:2]), jnp.where(far_first, *pieces[1::-1])]
+
+
+def cross_features(rows):
+    pairs = []
+    for block in range(4):
+        for core in range(2):
+            line = block * 4 + core
+            pairs.append((line + 2 * (1 - block // 2), line + 2 * (block // 2)))
+    return lax.ppermute(rows, ("tensor", "example", "test"), pairs)
+
+
+def spread_on_line(rows):
+    pieces = []
+    for turn in range(2):
+        pairs = []
+        for block in range(4):
+            for source_core in range(2):
+                line = block // 2 * 2
+                target = block ^ (2 * turn + (source_core ^ (block % 2)))
+                pairs.append((block * 4 + line + source_core, target * 4 + line + block % 2))
+        pieces.append(lax.ppermute(rows, ("tensor", "example", "test"), pairs))
+    return pieces
+
+
+def arrived_on_line(pieces, *earlier):
+    pieces = lax.optimization_barrier((*pieces, *earlier))
+    holder = lax.axis_index("example") * 2 + lax.axis_index("test")
+    return jnp.where((lax.axis_index("tensor") ^ holder) < 2, *pieces[:2])
 
 
 def gathered_features(flat, n_ex, n_cores):
@@ -205,41 +233,43 @@
     examples = [slice(e * seq_len, (e + 1) * seq_len) for e in range(ex_loc)]
     arrived, arrived_down = [], []
     if direct:
-        acts_far, acts_near = arrived_features(spread_features(flat_acts), *early)
-        acts_far = [acts_far]
+        grad_crossed = cross_features(flat_grad)
+        acts_all = arrived_features(spread_features(flat_acts), *early, grad_crossed)
     else:
-        acts_near, *acts_far = gathered_features(flat_acts, n_ex, n_cores)
+        near, *acts_all = gathered_features(flat_acts, n_ex, n_cores)
+        acts_all.append(near)
         grad_near, *grad_far = gathered_features(flat_grad, n_ex, n_cores)
-    gate_far = [forward(one, w_gate) for one in acts_far]
-    up_far = [forward(after(one, *gate_far), w_up) for one in acts_far]
+    acts_all = jnp.concatenate(acts_all)
+    gate_all = forward(acts_all, w_gate)
+    up_all = forward(after(acts_all, gate_all), w_up)
     if direct:
-        grad_all = spread_features(after(flat_grad, *up_far))
-    gate_near = forward(after(acts_near, *up_far), w_gate)
-    up_near = forward(after(acts_near, gate_near), w_up)
-    for step, (gate, up) in enumerate(zip(gate_far, up_far), 1):
-        both = pack(jnp.stack([core_sum(gate, 0, up_near), core_sum(up, 0, up_near)]))
+        grad_far = spread_on_line(after(grad_crossed, up_all))
+    for step in range(1, n_ex):
+        begin = (step - 1) * tok_rows
+        both = pack(jnp.stack([core_sum(gate_all, begin), core_sum(up_all, begin)]))
         received = shift(both, "example", step)
         arrived.append(received)
     if direct:
-        grad_all = arrived_features(grad_all, both)
-    else:
-        grad_all = [*grad_far, grad_near]
-    down_all = dot_rows(jnp.concatenate(grad_all), w_down)
-    for step in range(1, n_ex):
-        sent = pack(core_sum(down_all, (step - 1) * tok_rows))
+        grad_far = [arrived_on_line(grad_far, both)]
+    for step, one in enumerate(grad_far, 1):
+        down_far = dot_rows(one, w_down)
+        sent = pack(core_sum(down_far, 0))
         arrived_down.append(shift(sent, "example", step))
-    down_near = after(down_all, received)
+    if direct:
+        grad_near = spread_on_line(after(flat_grad, one))
+        grad_near = arrived_on_line(grad_near, received)
+    down_near = dot_rows(grad_near, w_down)
+    begin = (n_ex - 1) * tok_rows
     own = [
-        core_sum(gate_near, 0),
-        core_sum(up_near, 0),
-        core_sum(down_near, (n_ex - 1) * tok_rows),
+        core_sum(gate_all, begin),
+        core_sum(up_all, begin),
+        core_sum(down_near, 0),
     ]
     if n_z > 8:
         model_sum = lax.psum(model_part, "tensor")
     else:
-        model_sent = after(pack(model_part), sent)
+        model_sent = after(pack(model_part), received)
         others = [shift(model_sent, "tensor", step) for step in range(1, n_z)]
-        others = lax.optimization_barrier((*others, received))[:-1]
         model_sum = model_part + sum(unpack(one) for one in others)
 
     masked = model_sum.reshape(ex_loc, seq_len, 3 * width) * token_mask[:, :, None]

time: 179 us -> 196 us (1.095)
  matrix products: 32.7 us -> 24.8 us
  starting transfers between devices: 64.6 us -> 72.1 us
  waiting for transfers between devices: 41.1 us -> 46.8 us
  local copies, waits for them, and re-layouts: 12.5 us -> 18.1 us
  other arithmetic: 17.1 us -> 20.9 us
    ppermute x0 -> x5, starting transfers between devices: none -> 27.3 us  [the longest x4 26 us: spread_on_line(): pieces.append(lax.ppermute(rows, ('tensor', 'example', 'test'), pairs))]
    ppermute x4 -> x2, starting transfers between devices: 29 us -> 7.53 us  [spread_features(): pieces.append(lax.ppermute(flat, ('tensor', 'example', 'test'), pairs))]
    ppermute x0 -> x5, waiting for transfers between devices: none -> 17.7 us  [the longest x4 10.7 us: spread_on_line(): pieces.append(lax.ppermute(rows, ('tensor', 'example', 'test'), pairs))]
    ppermute x18, waiting for transfers between devices: 37.1 us -> 25 us  [shift(): return lax.ppermute(value, axis, [(i, (i + step) % n) for i in range(n)])]
    dot_general x4 -> x2, matrix products: 24.9 us -> 16.2 us  [forward(): return pack(jnp.dot(tokens, weight, preferred_element_type=F32))]
    unnamed x41 -> x53, local copies, waits for them, and re-layouts: 6.27 us -> 12.1 us
    convert_element_type x5, other arithmetic: 5.42 us -> 7.6 us  [pack(): return (value * SEND_SCALE).astype(jnp.float16)]
    pallas_call x1 -> x2, Pallas kernels: 7.49 us -> 9.26 us  [dot_rows(): pl.pallas_call(dot_rows_kernel, out_shape=jax.ShapeDtypeStruct((rows, hid...]
  transfers between devices with their start and end apart: 25 -> 28, of which waited for: 13 -> 13; matrix products, arithmetic and copies ran while one was open for 21% -> 18% of each run, Pallas kernels for 4% -> 5%
where the time goes in v12:
time: 196 us; the launch traced here: 194 us
  starting transfers between devices  72.1 us (37%)
  waiting for transfers between devices  46.8 us (24%)
  matrix products  24.8 us (13%)
  other arithmetic  20.9 us (11%)
  local copies, waits for them, and re-layouts  18.1 us (9%)
  Pallas kernels  10.5 us (5%)
    ppermute x18, starting transfers between devices, shift(): return lax.ppermute(value, axis, [(i, (i + step) % n) for i in range(n)])  34.8 us
    ppermute x4, starting transfers between devices, spread_on_line(): pieces.append(lax.ppermute(rows, ('tensor', 'example', 'test'), pairs))  26 us
    ppermute x18, waiting for transfers between devices, shift(): return lax.ppermute(value, axis, [(i, (i + step) % n) for i in range(n)])  25 us
    dot_general x2, matrix products, forward(): return pack(jnp.dot(tokens, weight, preferred_element_type=F32))  16.2 us
    unnamed x53, local copies, waits for them, and re-layouts  12.1 us
    ppermute x4, waiting for transfers between devices, spread_on_line(): pieces.append(lax.ppermute(rows, ('tensor', 'example', 'test'), pairs))  10.7 us
    pallas_call x2, Pallas kernels, dot_rows(): pl.pallas_call(dot_rows_kernel, out_shape=jax.ShapeDtypeStruct((rows, hid...  9.26 us
    convert_element_type x5, other arithmetic, pack(): return (value * SEND_SCALE).astype(jnp.float16)  7.6 us
  transfers between devices with their start and end apart: 28, of which 13 were waited for; matrix products, arithmetic and copies ran while one was open for 18% of the time, Pallas kernels for 5%

profile of v12, /device:TPU:0, one launch (start us, length us, event | category | flops | bytes accessed | tf_op | source)
XLA Modules:
  0.0 194.4 jit_solution(12868105210391960104)
XLA Ops:
  0.6 6.8 %collective-permute-start.2 = (bf16[256,1280]{1,0:T(8,128)(2,1)}, bf16[256,1280]{1,0:T(8,128)(2,1)}, u32[]{:S(2)}, u32[]{:S(2)}) collective-permute-start(bf16[256,1280]{1,0:T(8,128)(2,1)} %bitcast.89), channel_id=1, source_target_pairs={{0,0},{1,4},{2,8},{3,12},{4,1},{5,5},{6,9},{7,13},{10,10},{11,14},... | collective-permute-start | bytes 1966088 | tf_op jit(solution)/shard_map/ppermute | solution.py:66
  8.2 1.3 collective-permute-start.3
  9.5 1.3 collective-permute-start
  10.8 1.8 fusion.20
  12.6 2.0 %copy.22.refs_3_ = bf16[2048,64]{1,0:T(8,128)(2,1)} copy(bf16[2048,64]{0,1:T(8,128)(2,1)} %get-tuple-element.28) | data formatting | bytes 524288
  14.5 1.1 copy.21.refs_2_
  15.6 1.4 fusion.9
  17.0 1.6 fusion.6
  18.6 12.8 %collective-permute-done.3 = s32[2]{0:T(128)S(1)} collective-permute-done((s32[2]{0:T(128)}, s32[2]{0:T(128)S(1)}, u32[]{:S(2)}, u32[]{:S(2)}) %collective-permute-start.3) | collective-permute-done | bytes 40 | tf_op jit(solution)/shard_map/ppermute | solution.py:15
  31.4 7.1 %collective-permute-done = bf16[256,1280]{1,0:T(8,128)(2,1)} collective-permute-done((bf16[256,1280]{1,0:T(8,128)(2,1)}, bf16[256,1280]{1,0:T(8,128)(2,1)}, u32[]{:S(2)}, u32[]{:S(2)}) %collective-permute-start) | collective-permute-done | bytes 655392 | tf_op jit(solution)/shard_map/ppermute | solution.py:83
  38.5 1.4 broadcast_select_fusion.3
  40.0 10.4 %multiply_convert_fusion.1 = f16[512,4096]{1,0:T(8,128)(2,1)S(1)} fusion(bf16[1280,4096]{1,0:T(8,128)(2,1)} %param.12, bf16[256,1280]{1,0:T(8,128)(2,1)S(1)} %get-tuple-element.31, bf16[256,1280]{1,0:T(8,128)(2,1)S(1)} %get-tuple-element.30), kind=kOutput, calls=%fused_computation.1 | convolution fusion | flops 5375524864 | bytes 15990784 | tf_op jit(solution)/shard_map/dot_general | solution.py:202
  51.2 5.8 %multiply_convert_fusion = f16[512,4096]{1,0:T(8,128)(2,1)S(1)} fusion(bf16[512,1280]{1,0:T(8,128)(2,1)S(1)} %pad_maximum_fusion, bf16[1280,4096]{1,0:T(8,128)(2,1)S(1)} %bitcast.97), kind=kOutput, calls=%fused_computation | convolution fusion | flops 5372903424 | bytes 15990784 | tf_op jit(solution)/shard_map/dot_general | solution.py:202
  57.1 1.5 constant_dynamic-slice_fusion.6
  59.1 5.4 %collective-permute-start.5 = (bf16[256,1280]{1,0:T(8,128)(2,1)}, bf16[256,1280]{1,0:T(8,128)(2,1)S(1)}, u32[]{:S(2)}, u32[]{:S(2)}) collective-permute-start(bf16[256,1280]{1,0:T(8,128)(2,1)} %collective-permute-done), channel_id=1, source_target_pairs={{0,8},{1,12},{4,9},{5,13},{10,2},{11,6},{14,3},{15,7},{16,24},{17,... | collective-permute-start | bytes 1966088 | tf_op jit(solution)/shard_map/ppermute | solution.py:95
  64.5 1.7 collective-permute-start.4
  67.7 1.8 fusion
  69.5 10.4 %collective-permute-done.5 = bf16[256,1280]{1,0:T(8,128)(2,1)S(1)} collective-permute-done((bf16[256,1280]{1,0:T(8,128)(2,1)}, bf16[256,1280]{1,0:T(8,128)(2,1)S(1)}, u32[]{:S(2)}, u32[]{:S(2)}) %collective-permute-start.5) | collective-permute-done | bytes 655392 | tf_op jit(solution)/shard_map/ppermute | solution.py:95
  80.0 4.6 %shard_map.114 = f32[256,4096]{1,0:T(8,128)S(1)} custom-call(bf16[256,1280]{1,0:T(8,128)(2,1)S(1)} %broadcast_select_fusion.1.tokens_ref, bf16[4096,1280]{1,0:T(8,128)(2,1)S(1)} %bitcast.87), custom_call_target="tpu_custom_call" | custom-call | flops 1 | bytes 1 | tf_op jit(solution)/shard_map/pallas_call | solution.py:125
  84.7 2.1 %copy-done.5 = f32[256,4096]{1,0:T(8,128)} copy-done((f32[256,4096]{1,0:T(8,128)}, f32[256,4096]{1,0:T(8,128)S(1)}, u32[]{:S(2)}) %copy-start.5) | copy-done | bytes 4194328
  86.7 1.2 multiply_convert_fusion.4
  88.0 5.1 %collective-permute-start.12 = (f16[256,2048]{1,0:T(8,128)(2,1)}, f16[256,2048]{1,0:T(8,128)(2,1)}, u32[]{:S(2)}, u32[]{:S(2)}) collective-permute-start(f16[256,2048]{1,0:T(8,128)(2,1)} %multiply_convert_fusion.4), channel_id=1, source_target_pairs={{0,1},{1,0},{2,3},{3,2},{4,5},{5,4},{6,7},{7,6},{8,9},{9,8},{10,11... | collective-permute-start | bytes 3145736 | tf_op jit(solution)/shard_map/ppermute | solution.py:15
  93.0 12.3 %collective-permute-start.9 = (bf16[256,1280]{1,0:T(8,128)(2,1)}, bf16[256,1280]{1,0:T(8,128)(2,1)}, u32[]{:S(2)}, u32[]{:S(2)}) collective-permute-start(bf16[256,1280]{1,0:T(8,128)(2,1)} %bitcast), channel_id=1, source_target_pairs={{0,8},{1,12},{4,9},{5,13},{10,2},{11,6},{14,3},{15,7},{16,24},{17,... | collective-permute-start | bytes 1966088 | tf_op jit(solution)/shard_map/ppermute | solution.py:95
  105.3 1.0 copy-done.12
  106.3 6.5 %collective-permute-start.8 = (bf16[256,1280]{1,0:T(8,128)(2,1)}, bf16[256,1280]{1,0:T(8,128)(2,1)}, u32[]{:S(2)}, u32[]{:S(2)}) collective-permute-start(bf16[256,1280]{1,0:T(8,128)(2,1)} %bitcast), channel_id=1, source_target_pairs={{0,0},{1,4},{4,1},{5,5},{10,10},{11,14},{14,11},{15,15},{16,16},{1... | collective-permute-start | bytes 1966088 | tf_op jit(solution)/shard_map/ppermute | solution.py:95
  113.0 3.3 %multiply_convert_fusion.3 = f16[256,2048]{1,0:T(8,128)(2,1)} fusion(f16[256,2048]{1,0:T(8,128)(2,1)} %collective-permute-done.12, f32[256,4096]{1,0:T(8,128)} %copy-done.5, s32[]{:T(128)S(6)} %select_n.62), kind=kLoop, calls=%fused_computation.13 | loop fusion | flops 2621440 | bytes 4194308 | tf_op jit(solution)/shard_map/convert_element_type | solution.py:19
  116.3 1.9 %collective-permute-done.10 = f16[2,256,2048]{2,1,0:T(8,128)(2,1)} collective-permute-done((f16[2,256,2048]{2,1,0:T(8,128)(2,1)}, f16[2,256,2048]{2,1,0:T(8,128)(2,1)}, u32[]{:S(2)}, u32[]{:S(2)}) %collective-permute-start.10) | collective-permute-done | bytes 2097184 | tf_op jit(solution)/shard_map/ppermute | solution.py:15
  119.9 1.2 broadcast_select_fusion.tokens_ref
  121.1 18.6 %collective-permute-start.16 = (f16[256,192]{0,1:T(8,128)(2,1)S(1)}, f16[256,192]{0,1:T(8,128)(2,1)S(1)}, u32[]{:S(2)}, u32[]{:S(2)}) collective-permute-start(f16[256,192]{0,1:T(8,128)(2,1)S(1)} %multiply_convert_fusion.7), channel_id=1, source_target_pairs={{0,4},{4,8},{8,12},{12,0},{1,5},{5,9},{9,13},{13,1},{2,6},{6,10},{... | collective-permute-start | bytes 294920 | tf_op jit(solution)/shard_map/ppermute | solution.py:15
  139.7 4.0 %copy-done.1 = bf16[4096,1280]{1,0:T(8,128)(2,1)S(1)} copy-done((bf16[4096,1280]{1,0:T(8,128)(2,1)S(1)}, bf16[4096,1280]{1,0:T(8,128)(2,1)}, u32[]{:S(2)}) %copy-start.1) | copy-done | bytes 10485784
  143.7 4.6 %shard_map.113 = f32[256,4096]{1,0:T(8,128)S(1)} custom-call(bf16[256,1280]{1,0:T(8,128)(2,1)S(1)} %broadcast_select_fusion.tokens_ref, bf16[4096,1280]{1,0:T(8,128)(2,1)S(1)} %copy-done.1), custom_call_target="tpu_custom_call" | custom-call | flops 1 | bytes 1 | tf_op jit(solution)/shard_map/pallas_call | solution.py:125
  148.3 1.2 multiply_convert_fusion.5
  149.5 1.2 copy-done.4
  150.7 5.1 %fusion.3 = (f32[256,2048]{1,0:T(8,128)S(1)}, f32[256,2048]{1,0:T(8,128)}) fusion(f16[256,2048]{1,0:T(8,128)(2,1)S(1)} %copy-done.13, f16[2,256,2048]{2,1,0:T(8,128)(2,1)} %collective-permute-done.10, f16[512,4096]{1,0:T(8,128)(2,1)} %copy-done.11, s32[]{:T(128)S(6)} %select_n.62, f16[256,2048]{1,0:T(8,128)(2,1)} %collective-permute-done.14, ...), kind=kLoop, calls=%fused_computation.11 | loop fusion | flops 11010048 | bytes 10485764 | tf_op jit(solution)/shard_map/mul | solution.py:288
  155.8 3.1 %fusion.4 = f32[256,64]{0,1:T(8,128)S(1)} fusion(f32[256,2048]{1,0:T(8,128)S(1)} %get-tuple-element.22.refs_1_, f16[256,2048]{1,0:T(8,128)(2,1)} %collective-permute-done.14, f16[2,256,2048]{2,1,0:T(8,128)(2,1)} %collective-permute-done.10, f16[512,4096]{1,0:T(8,128)(2,1)S(1)} %copy-done.10, s32[]{:T(128)S(6)} %select_n.62, bf16[4096,192]{0,1:T(8,128)(2,1)} %param.16, ...), kind=kOutput, calls=%fused_computation.23 | convolution fusion | flops 71303168 | bytes 5572096 | tf_op jit(solution)/shard_map/dot_general | solution.py:291
  159.7 1.1 copy.17
  161.5 2.9 %multiply_add_fusion.down_ref = f32[256,2048]{1,0:T(8,128)S(1)} fusion(f16[256,2048]{1,0:T(8,128)(2,1)} %collective-permute-done.13, f16[256,2048]{1,0:T(8,128)(2,1)} %collective-permute-done.11, f32[256,4096]{1,0:T(8,128)} %copy-done.4, s32[]{:T(128)S(6)} %select_n.62), kind=kLoop, calls=%fused_computation.12 | loop fusion | flops 3145728 | bytes 6291460 | tf_op jit(solution)/shard_map/add | solution.py:286
  165.2 1.2 shard_map.115
  166.4 2.4 %collective-permute-start.19 = (f32[6,16,64]{2,1,0:T(8,128)S(1)}, f32[6,16,64]{2,1,0:T(8,128)}, u32[]{:S(2)}, u32[]{:S(2)}) collective-permute-start(f32[6,16,64]{2,1,0:T(8,128)S(1)} %get-tuple-element.34), channel_id=1, source_target_pairs={{0,4},{4,8},{8,12},{12,0},{1,5},{5,9},{9,13},{13,1},{2,6},{6,10},{... | collective-permute-start | bytes 73736 | tf_op jit(solution)/shard_map/ppermute | solution.py:15
  168.8 1.5 collective-permute-start.21
  170.5 2.4 %collective-permute-done.19 = f32[6,16,64]{2,1,0:T(8,128)} collective-permute-done((f32[6,16,64]{2,1,0:T(8,128)S(1)}, f32[6,16,64]{2,1,0:T(8,128)}, u32[]{:S(2)}, u32[]{:S(2)}) %collective-permute-start.19) | collective-permute-done | bytes 24608 | tf_op jit(solution)/shard_map/ppermute | solution.py:15
  173.3 2.5 %collective-permute-done.20 = f32[6,16,64]{2,1,0:T(8,128)} collective-permute-done((f32[6,16,64]{2,1,0:T(8,128)S(1)}, f32[6,16,64]{2,1,0:T(8,128)}, u32[]{:S(2)}, u32[]{:S(2)}) %collective-permute-start.20) | collective-permute-done | bytes 24608 | tf_op jit(solution)/shard_map/ppermute | solution.py:15
  176.8 2.4 %collective-permute-start.23 = (f32[6,16,64]{2,1,0:T(8,128)S(1)}, f32[6,16,64]{2,1,0:T(8,128)S(1)}, u32[]{:S(2)}, u32[]{:S(2)}) collective-permute-start(f32[6,16,64]{2,1,0:T(8,128)S(1)} %fusion.15), channel_id=1, source_target_pairs={{0,3},{1,2},{2,1},{3,0},{4,7},{5,6},{6,5},{7,4},{8,11},{9,10},{10,... | collective-permute-start | bytes 73736 | tf_op jit(solution)/shard_map/ppermute | solution.py:311
  179.3 2.0 %collective-permute-done.23 = f32[6,16,64]{2,1,0:T(8,128)S(1)} collective-permute-done((f32[6,16,64]{2,1,0:T(8,128)S(1)}, f32[6,16,64]{2,1,0:T(8,128)S(1)}, u32[]{:S(2)}, u32[]{:S(2)}) %collective-permute-start.23) | collective-permute-done | bytes 24608 | tf_op jit(solution)/shard_map/ppermute | solution.py:311
  181.3 2.0 %collective-permute-done.22 = f32[6,16,64]{2,1,0:T(8,128)S(1)} collective-permute-done((f32[6,16,64]{2,1,0:T(8,128)S(1)}, f32[6,16,64]{2,1,0:T(8,128)S(1)}, u32[]{:S(2)}, u32[]{:S(2)}) %collective-permute-start.22) | collective-permute-done | bytes 24608 | tf_op jit(solution)/shard_map/ppermute | solution.py:311
  183.5 1.3 fusion.21
  184.8 2.6 %collective-permute-start.25 = (f32[4,512]{1,0:T(4,128)S(1)}, f32[4,512]{1,0:T(4,128)S(1)}, u32[]{:S(2)}, u32[]{:S(2)}) collective-permute-start(f32[4,512]{1,0:T(4,128)S(1)} %fusion.21), channel_id=1, source_target_pairs={{0,12},{4,0},{8,4},{12,8},{1,13},{5,1},{9,5},{13,9},{2,14},{6,2},{... | collective-permute-start | bytes 24584 | tf_op jit(solution)/shard_map/ppermute | solution.py:15
  188.7 3.3 %collective-permute-done.26 = f32[4,512]{1,0:T(4,128)S(1)} collective-permute-done((f32[4,512]{1,0:T(4,128)S(1)}, f32[4,512]{1,0:T(4,128)S(1)}, u32[]{:S(2)}, u32[]{:S(2)}) %collective-permute-start.26) | collective-permute-done | bytes 8224 | tf_op jit(solution)/shard_map/ppermute | solution.py:15
  (112 shorter events, 13.1 us)
Async XLA Ops:
  0.6 182.8 %copy-start = (bf16[3,16,64,512]{3,2,1,0:T(8,128)(2,1)S(1)}, bf16[3,16,64,512]{3,2,1,0:T(8,128)(2,1)}, u32[]{:S(2)}) copy-start(bf16[3,16,64,512]{3,2,1,0:T(8,128)(2,1)} %param.17) | copy-start | bytes 9437188
  0.6 30.8 %collective-permute-start.2 = (bf16[256,1280]{1,0:T(8,128)(2,1)}, bf16[256,1280]{1,0:T(8,128)(2,1)}, u32[]{:S(2)}, u32[]{:S(2)}) collective-permute-start(bf16[256,1280]{1,0:T(8,128)(2,1)} %bitcast.89), channel_id=1, source_target_pairs={{0,0},{1,4},{2,8},{3,12},{4,1},{5,5},{6,9},{7,13},{10,10},{11,14},... | collective-permute-start | bytes 1966088 | tf_op jit(solution)/shard_map/ppermute | solution.py:66
  7.4 24.0 %collective-permute-start.1 = (bf16[256,1280]{1,0:T(8,128)(2,1)}, bf16[256,1280]{1,0:T(8,128)(2,1)}, u32[]{:S(2)}, u32[]{:S(2)}) collective-permute-start(bf16[256,1280]{1,0:T(8,128)(2,1)} %bitcast.90), channel_id=1, source_target_pairs={{0,8},{1,12},{2,0},{3,4},{4,9},{5,13},{6,1},{7,5},{10,2},{11,6},{8... | collective-permute-start | bytes 1966088 | tf_op jit(solution)/shard_map/ppermute | solution.py:66
  8.2 23.2 %collective-permute-start.3 = (s32[2]{0:T(128)}, s32[2]{0:T(128)S(1)}, u32[]{:S(2)}, u32[]{:S(2)}) collective-permute-start(s32[2]{0:T(128)} %param.19), channel_id=1, source_target_pairs={{0,2},{2,0},{1,3},{3,1},{4,6},{6,4},{5,7},{7,5},{8,10},{10,8},{9,1... | collective-permute-start | bytes 32 | tf_op jit(solution)/shard_map/ppermute | solution.py:15
  9.5 29.0 %collective-permute-start = (bf16[256,1280]{1,0:T(8,128)(2,1)}, bf16[256,1280]{1,0:T(8,128)(2,1)}, u32[]{:S(2)}, u32[]{:S(2)}) collective-permute-start(bf16[256,1280]{1,0:T(8,128)(2,1)} %bitcast), channel_id=1, source_target_pairs={{2,0},{3,1},{6,4},{7,5},{8,10},{9,11},{12,14},{13,15},{18,16},{19,... | collective-permute-start | bytes 1966088 | tf_op jit(solution)/shard_map/ppermute | solution.py:83
  10.8 20.6 %copy-start.14 = (s32[2]{0:T(128)S(1)}, s32[2]{0:T(128)}, u32[]{:S(2)}) copy-start(s32[2]{0:T(128)} %param.19) | copy-start | bytes 28
  39.9 11.3 %slice-start.3 = ((s8[10485760]{0:T(1024)(128)(4,1)}), s8[4194304]{0:T(1024)(128)(4,1)S(1)}, s32[]{:S(2)}) async-start(s8[10485760]{0:T(1024)(128)(4,1)} %bitcast.96), calls=%async_computation.3 | async-start | bytes 8388608
  40.0 11.2 %slice-start.4 = ((s8[10485760]{0:T(1024)(128)(4,1)}), s8[4194304]{0:T(1024)(128)(4,1)S(1)}, s32[]{:S(2)}) async-start(s8[10485760]{0:T(1024)(128)(4,1)} %bitcast.96), calls=%async_computation.4 | async-start | bytes 8388608
  40.0 11.2 %slice-start.5 = ((s8[10485760]{0:T(1024)(128)(4,1)}), s8[2097152]{0:T(1024)(128)(4,1)S(1)}, s32[]{:S(2)}) async-start(s8[10485760]{0:T(1024)(128)(4,1)} %bitcast.96), calls=%async_computation.5 | async-start | bytes 4194304
  50.4 16.5 %copy-start.11 = (f16[512,4096]{1,0:T(8,128)(2,1)}, f16[512,4096]{1,0:T(8,128)(2,1)S(1)}, u32[]{:S(2)}) copy-start(f16[512,4096]{1,0:T(8,128)(2,1)S(1)} %multiply_convert_fusion.1) | copy-start | bytes 12582916
  51.1 15.7 %collective-permute-start.6 = (f16[256,2048]{1,0:T(8,128)(2,1)S(1)}, f16[256,2048]{1,0:T(8,128)(2,1)S(1)}, u32[]{:S(2)}, u32[]{:S(2)}) collective-permute-start(f16[256,2048]{1,0:T(8,128)(2,1)S(1)} %get-tuple-element.25), channel_id=1, source_target_pairs={{0,1},{1,0},{2,3},{3,2},{4,5},{5,4},{6,7},{7,6},{8,9},{9,8},{10,11... | collective-permute-start | bytes 3145736 | tf_op jit(solution)/shard_map/ppermute | solution.py:15
  57.0 10.2 %copy-start.9 = (f16[512,4096]{1,0:T(8,128)(2,1)}, f16[512,4096]{1,0:T(8,128)(2,1)S(1)}, u32[]{:S(2)}) copy-start(f16[512,4096]{1,0:T(8,128)(2,1)S(1)} %multiply_convert_fusion) | copy-start | bytes 12582916
  57.0 22.9 %slice-start = ((s8[10485760]{0:T(1024)(128)(4,1)}), s8[4194304]{0:T(1024)(128)(4,1)S(1)}, s32[]{:S(2)}) async-start(s8[10485760]{0:T(1024)(128)(4,1)} %bitcast.86), calls=%async_computation | async-start | bytes 8388608
  58.6 8.7 %collective-permute-start.7 = (f16[256,2048]{1,0:T(8,128)(2,1)S(1)}, f16[256,2048]{1,0:T(8,128)(2,1)S(1)}, u32[]{:S(2)}, u32[]{:S(2)}) collective-permute-start(f16[256,2048]{1,0:T(8,128)(2,1)S(1)} %get-tuple-element.27), channel_id=1, source_target_pairs={{0,1},{1,0},{2,3},{3,2},{4,5},{5,4},{6,7},{7,6},{8,9},{9,8},{10,11... | collective-permute-start | bytes 3145736 | tf_op jit(solution)/shard_map/ppermute | solution.py:15
  59.1 20.8 %collective-permute-start.5 = (bf16[256,1280]{1,0:T(8,128)(2,1)}, bf16[256,1280]{1,0:T(8,128)(2,1)S(1)}, u32[]{:S(2)}, u32[]{:S(2)}) collective-permute-start(bf16[256,1280]{1,0:T(8,128)(2,1)} %collective-permute-done), channel_id=1, source_target_pairs={{0,8},{1,12},{4,9},{5,13},{10,2},{11,6},{14,3},{15,7},{16,24},{17,... | collective-permute-start | bytes 1966088 | tf_op jit(solution)/shard_map/ppermute | solution.py:95
  64.5 15.5 %collective-permute-start.4 = (bf16[256,1280]{1,0:T(8,128)(2,1)}, bf16[256,1280]{1,0:T(8,128)(2,1)S(1)}, u32[]{:S(2)}, u32[]{:S(2)}) collective-permute-start(bf16[256,1280]{1,0:T(8,128)(2,1)} %collective-permute-done), channel_id=1, source_target_pairs={{0,0},{1,4},{4,1},{5,5},{10,10},{11,14},{14,11},{15,15},{16,16},{1... | collective-permute-start | bytes 1966088 | tf_op jit(solution)/shard_map/ppermute | solution.py:95
  66.2 39.1 %collective-permute-start.15 = (f16[256,2048]{1,0:T(8,128)(2,1)S(1)}, f16[256,2048]{1,0:T(8,128)(2,1)S(1)}, u32[]{:S(2)}, u32[]{:S(2)}) collective-permute-start(f16[256,2048]{1,0:T(8,128)(2,1)S(1)} %get-tuple-element.24), channel_id=1, source_target_pairs={{0,1},{1,0},{2,3},{3,2},{4,5},{5,4},{6,7},{7,6},{8,9},{9,8},{10,11... | collective-permute-start | bytes 3145736 | tf_op jit(solution)/shard_map/ppermute | solution.py:15
  66.8 13.2 %slice-start.1 = ((s8[10485760]{0:T(1024)(128)(4,1)}), s8[4194304]{0:T(1024)(128)(4,1)S(1)}, s32[]{:S(2)}) async-start(s8[10485760]{0:T(1024)(128)(4,1)} %bitcast.86), calls=%async_computation.1 | async-start | bytes 8388608
  66.8 46.2 %collective-permute-start.14 = (f16[256,2048]{1,0:T(8,128)(2,1)}, f16[256,2048]{1,0:T(8,128)(2,1)}, u32[]{:S(2)}, u32[]{:S(2)}) collective-permute-start(f16[256,2048]{1,0:T(8,128)(2,1)} %get-tuple-element.26), channel_id=1, source_target_pairs={{0,1},{1,0},{2,3},{3,2},{4,5},{5,4},{6,7},{7,6},{8,9},{9,8},{10,11... | collective-permute-start | bytes 3145736 | tf_op jit(solution)/shard_map/ppermute | solution.py:15
  67.7 12.3 %slice-start.2 = ((s8[10485760]{0:T(1024)(128)(4,1)}), s8[2097152]{0:T(1024)(128)(4,1)S(1)}, s32[]{:S(2)}) async-start(s8[10485760]{0:T(1024)(128)(4,1)} %bitcast.86), calls=%async_computation.2 | async-start | bytes 4194304
  69.5 48.8 %collective-permute-start.10 = (f16[2,256,2048]{2,1,0:T(8,128)(2,1)}, f16[2,256,2048]{2,1,0:T(8,128)(2,1)}, u32[]{:S(2)}, u32[]{:S(2)}) collective-permute-start(f16[2,256,2048]{2,1,0:T(8,128)(2,1)} %fusion), channel_id=1, source_target_pairs={{0,2},{2,0},{1,3},{3,1},{4,6},{6,4},{5,7},{7,5},{8,10},{10,8},{9,1... | collective-permute-start | bytes 6291464 | tf_op jit(solution)/shard_map/ppermute | solution.py:15
  86.7 26.1 %copy-start.15 = (s32[2]{0:T(128)S(1)}, s32[2]{0:T(128)}, u32[]{:S(2)}) copy-start(s32[2]{0:T(128)} %param.18) | copy-start | bytes 28
  88.0 25.0 %collective-permute-start.12 = (f16[256,2048]{1,0:T(8,128)(2,1)}, f16[256,2048]{1,0:T(8,128)(2,1)}, u32[]{:S(2)}, u32[]{:S(2)}) collective-permute-start(f16[256,2048]{1,0:T(8,128)(2,1)} %multiply_convert_fusion.4), channel_id=1, source_target_pairs={{0,1},{1,0},{2,3},{3,2},{4,5},{5,4},{6,7},{7,6},{8,9},{9,8},{10,11... | collective-permute-start | bytes 3145736 | tf_op jit(solution)/shard_map/ppermute | solution.py:15
  93.0 26.9 %collective-permute-start.9 = (bf16[256,1280]{1,0:T(8,128)(2,1)}, bf16[256,1280]{1,0:T(8,128)(2,1)}, u32[]{:S(2)}, u32[]{:S(2)}) collective-permute-start(bf16[256,1280]{1,0:T(8,128)(2,1)} %bitcast), channel_id=1, source_target_pairs={{0,8},{1,12},{4,9},{5,13},{10,2},{11,6},{14,3},{15,7},{16,24},{17,... | collective-permute-start | bytes 1966088 | tf_op jit(solution)/shard_map/ppermute | solution.py:95
  106.3 13.6 %collective-permute-start.8 = (bf16[256,1280]{1,0:T(8,128)(2,1)}, bf16[256,1280]{1,0:T(8,128)(2,1)}, u32[]{:S(2)}, u32[]{:S(2)}) collective-permute-start(bf16[256,1280]{1,0:T(8,128)(2,1)} %bitcast), channel_id=1, source_target_pairs={{0,0},{1,4},{4,1},{5,5},{10,10},{11,14},{14,11},{15,15},{16,16},{1... | collective-permute-start | bytes 1966088 | tf_op jit(solution)/shard_map/ppermute | solution.py:95
  116.3 45.2 %collective-permute-start.13 = (f16[256,2048]{1,0:T(8,128)(2,1)}, f16[256,2048]{1,0:T(8,128)(2,1)}, u32[]{:S(2)}, u32[]{:S(2)}) collective-permute-start(f16[256,2048]{1,0:T(8,128)(2,1)} %multiply_convert_fusion.3), channel_id=1, source_target_pairs={{0,2},{2,0},{1,3},{3,1},{4,6},{6,4},{5,7},{7,5},{8,10},{10,8},{9,1... | collective-permute-start | bytes 3145736 | tf_op jit(solution)/shard_map/ppermute | solution.py:15
  118.3 40.7 %collective-permute-start.18 = (f16[256,192]{0,1:T(8,128)(2,1)S(1)}, f16[256,192]{0,1:T(8,128)(2,1)S(1)}, u32[]{:S(2)}, u32[]{:S(2)}) collective-permute-start(f16[256,192]{0,1:T(8,128)(2,1)S(1)} %multiply_convert_fusion.7), channel_id=1, source_target_pairs={{0,12},{4,0},{8,4},{12,8},{1,13},{5,1},{9,5},{13,9},{2,14},{6,2},{... | collective-permute-start | bytes 294920 | tf_op jit(solution)/shard_map/ppermute | solution.py:15
  118.8 40.2 %collective-permute-start.17 = (f16[256,192]{0,1:T(8,128)(2,1)S(1)}, f16[256,192]{0,1:T(8,128)(2,1)S(1)}, u32[]{:S(2)}, u32[]{:S(2)}) collective-permute-start(f16[256,192]{0,1:T(8,128)(2,1)S(1)} %multiply_convert_fusion.7), channel_id=1, source_target_pairs={{0,8},{4,12},{8,0},{12,4},{1,9},{5,13},{9,1},{13,5},{2,10},{6,14},... | collective-permute-start | bytes 294920 | tf_op jit(solution)/shard_map/ppermute | solution.py:15
  121.1 37.9 %collective-permute-start.16 = (f16[256,192]{0,1:T(8,128)(2,1)S(1)}, f16[256,192]{0,1:T(8,128)(2,1)S(1)}, u32[]{:S(2)}, u32[]{:S(2)}) collective-permute-start(f16[256,192]{0,1:T(8,128)(2,1)S(1)} %multiply_convert_fusion.7), channel_id=1, source_target_pairs={{0,4},{4,8},{8,12},{12,0},{1,5},{5,9},{9,13},{13,1},{2,6},{6,10},{... | collective-permute-start | bytes 294920 | tf_op jit(solution)/shard_map/ppermute | solution.py:15
  139.7 4.0 %copy-start.1 = (bf16[4096,1280]{1,0:T(8,128)(2,1)S(1)}, bf16[4096,1280]{1,0:T(8,128)(2,1)}, u32[]{:S(2)}) copy-start(bf16[4096,1280]{1,0:T(8,128)(2,1)} %weight_ref.3) | copy-start | bytes 31457284
  143.7 7.0 %copy-start.10 = (f16[512,4096]{1,0:T(8,128)(2,1)S(1)}, f16[512,4096]{1,0:T(8,128)(2,1)}, u32[]{:S(2)}) copy-start(f16[512,4096]{1,0:T(8,128)(2,1)} %copy-done.9) | copy-start | bytes 12582916
  148.3 2.4 %copy-start.4 = (f32[256,4096]{1,0:T(8,128)}, f32[256,4096]{1,0:T(8,128)S(1)}, u32[]{:S(2)}) copy-start(f32[256,4096]{1,0:T(8,128)S(1)} %shard_map.113) | copy-start | bytes 12582916
  148.3 2.4 %copy-start.13 = (f16[256,2048]{1,0:T(8,128)(2,1)S(1)}, f16[256,2048]{1,0:T(8,128)(2,1)}, u32[]{:S(2)}) copy-start(f16[256,2048]{1,0:T(8,128)(2,1)} %copy-done.12) | copy-start | bytes 3145732
  150.7 10.8 %collective-permute-start.11 = (f16[256,2048]{1,0:T(8,128)(2,1)}, f16[256,2048]{1,0:T(8,128)(2,1)}, u32[]{:S(2)}, u32[]{:S(2)}) collective-permute-start(f16[256,2048]{1,0:T(8,128)(2,1)} %multiply_convert_fusion.5), channel_id=1, source_target_pairs={{0,1},{1,0},{2,3},{3,2},{4,5},{5,4},{6,7},{7,6},{8,9},{9,8},{10,11... | collective-permute-start | bytes 3145736 | tf_op jit(solution)/shard_map/ppermute | solution.py:15
  155.8 3.1 %copy-start.2 = (f32[256,2048]{1,0:T(8,128)}, f32[256,2048]{1,0:T(8,128)S(1)}, u32[]{:S(2)}) copy-start(f32[256,2048]{1,0:T(8,128)S(1)} %get-tuple-element.22.refs_1_) | copy-start | bytes 6291460
  161.5 3.0 %copy-start.3 = (f32[256,2048]{1,0:T(8,128)S(1)}, f32[256,2048]{1,0:T(8,128)}, u32[]{:S(2)}) copy-start(f32[256,2048]{1,0:T(8,128)} %copy-done.2) | copy-start | bytes 6291460
  161.5 3.5 %copy-start.6 = (f32[256,2048]{1,0:T(8,128)S(1)}, f32[256,2048]{1,0:T(8,128)}, u32[]{:S(2)}) copy-start(f32[256,2048]{1,0:T(8,128)} %get-tuple-element.23.refs_0_) | copy-start | bytes 6291460
  161.5 3.5 %copy-start.7 = (bf16[2048,64]{1,0:T(8,128)(2,1)S(1)}, bf16[2048,64]{1,0:T(8,128)(2,1)}, u32[]{:S(2)}) copy-start(bf16[2048,64]{1,0:T(8,128)(2,1)} %copy.22.refs_3_) | copy-start | bytes 786436
  161.5 3.7 %copy-start.8 = (bf16[2048,64]{1,0:T(8,128)(2,1)S(1)}, bf16[2048,64]{1,0:T(8,128)(2,1)}, u32[]{:S(2)}) copy-start(bf16[2048,64]{1,0:T(8,128)(2,1)} %copy.21.refs_2_) | copy-start | bytes 786436
  166.4 6.5 %collective-permute-start.19 = (f32[6,16,64]{2,1,0:T(8,128)S(1)}, f32[6,16,64]{2,1,0:T(8,128)}, u32[]{:S(2)}, u32[]{:S(2)}) collective-permute-start(f32[6,16,64]{2,1,0:T(8,128)S(1)} %get-tuple-element.34), channel_id=1, source_target_pairs={{0,4},{4,8},{8,12},{12,0},{1,5},{5,9},{9,13},{13,1},{2,6},{6,10},{... | collective-permute-start | bytes 73736 | tf_op jit(solution)/shard_map/ppermute | solution.py:15
  168.8 4.5 %collective-permute-start.21 = (f32[6,16,64]{2,1,0:T(8,128)S(1)}, f32[6,16,64]{2,1,0:T(8,128)}, u32[]{:S(2)}, u32[]{:S(2)}) collective-permute-start(f32[6,16,64]{2,1,0:T(8,128)S(1)} %get-tuple-element.35), channel_id=1, source_target_pairs={{0,12},{4,0},{8,4},{12,8},{1,13},{5,1},{9,5},{13,9},{2,14},{6,2},{... | collective-permute-start | bytes 73736 | tf_op jit(solution)/shard_map/ppermute | solution.py:15
  170.3 5.6 %collective-permute-start.20 = (f32[6,16,64]{2,1,0:T(8,128)S(1)}, f32[6,16,64]{2,1,0:T(8,128)}, u32[]{:S(2)}, u32[]{:S(2)}) collective-permute-start(f32[6,16,64]{2,1,0:T(8,128)S(1)} %get-tuple-element.36), channel_id=1, source_target_pairs={{0,8},{4,12},{8,0},{12,4},{1,9},{5,13},{9,1},{13,5},{2,10},{6,14},... | collective-permute-start | bytes 73736 | tf_op jit(solution)/shard_map/ppermute | solution.py:15
  176.7 2.5 %collective-permute-start.24 = (f32[6,16,64]{2,1,0:T(8,128)S(1)}, f32[6,16,64]{2,1,0:T(8,128)S(1)}, u32[]{:S(2)}, u32[]{:S(2)}) collective-permute-start(f32[6,16,64]{2,1,0:T(8,128)S(1)} %fusion.15), channel_id=1, source_target_pairs={{0,1},{1,0},{2,3},{3,2},{4,5},{5,4},{6,7},{7,6},{8,9},{9,8},{10,11... | collective-permute-start | bytes 73736 | tf_op jit(solution)/shard_map/ppermute | solution.py:311
  176.8 4.5 %collective-permute-start.23 = (f32[6,16,64]{2,1,0:T(8,128)S(1)}, f32[6,16,64]{2,1,0:T(8,128)S(1)}, u32[]{:S(2)}, u32[]{:S(2)}) collective-permute-start(f32[6,16,64]{2,1,0:T(8,128)S(1)} %fusion.15), channel_id=1, source_target_pairs={{0,3},{1,2},{2,1},{3,0},{4,7},{5,6},{6,5},{7,4},{8,11},{9,10},{10,... | collective-permute-start | bytes 73736 | tf_op jit(solution)/shard_map/ppermute | solution.py:311
  179.2 4.1 %collective-permute-start.22 = (f32[6,16,64]{2,1,0:T(8,128)S(1)}, f32[6,16,64]{2,1,0:T(8,128)S(1)}, u32[]{:S(2)}, u32[]{:S(2)}) collective-permute-start(f32[6,16,64]{2,1,0:T(8,128)S(1)} %fusion.15), channel_id=1, source_target_pairs={{0,2},{1,3},{2,0},{3,1},{4,6},{5,7},{6,4},{7,5},{8,10},{9,11},{10,... | collective-permute-start | bytes 73736 | tf_op jit(solution)/shard_map/ppermute | solution.py:311
  184.8 3.9 %collective-permute-start.25 = (f32[4,512]{1,0:T(4,128)S(1)}, f32[4,512]{1,0:T(4,128)S(1)}, u32[]{:S(2)}, u32[]{:S(2)}) collective-permute-start(f32[4,512]{1,0:T(4,128)S(1)} %fusion.21), channel_id=1, source_target_pairs={{0,12},{4,0},{8,4},{12,8},{1,13},{5,1},{9,5},{13,9},{2,14},{6,2},{... | collective-permute-start | bytes 24584 | tf_op jit(solution)/shard_map/ppermute | solution.py:15
  187.4 5.4 %collective-permute-start.27 = (f32[4,512]{1,0:T(4,128)S(1)}, f32[4,512]{1,0:T(4,128)S(1)}, u32[]{:S(2)}, u32[]{:S(2)}) collective-permute-start(f32[4,512]{1,0:T(4,128)S(1)} %fusion.21), channel_id=1, source_target_pairs={{0,4},{4,8},{8,12},{12,0},{1,5},{5,9},{9,13},{13,1},{2,6},{6,10},{... | collective-permute-start | bytes 24584 | tf_op jit(solution)/shard_map/ppermute | solution.py:15
  187.4 4.5 %collective-permute-start.26 = (f32[4,512]{1,0:T(4,128)S(1)}, f32[4,512]{1,0:T(4,128)S(1)}, u32[]{:S(2)}, u32[]{:S(2)}) collective-permute-start(f32[4,512]{1,0:T(4,128)S(1)} %fusion.21), channel_id=1, source_target_pairs={{0,8},{4,12},{8,0},{12,4},{1,9},{5,13},{9,1},{13,5},{2,10},{6,14},... | collective-permute-start | bytes 24584 | tf_op jit(solution)/shard_map/ppermute | solution.py:15
  (2 other events, 3.0 us)

commit v13 on v11

--- a/solution.py
+++ b/solution.py
@@ -205,34 +205,33 @@
     examples = [slice(e * seq_len, (e + 1) * seq_len) for e in range(ex_loc)]
     arrived, arrived_down = [], []
     if direct:
-        acts_far, acts_near = arrived_features(spread_features(flat_acts), *early)
-        acts_far = [acts_far]
+        acts_all = arrived_features(spread_features(flat_acts), *early)
     else:
-        acts_near, *acts_far = gathered_features(flat_acts, n_ex, n_cores)
-        grad_near, *grad_far = gathered_features(flat_grad, n_ex, n_cores)
-    gate_far = [forward(one, w_gate) for one in acts_far]
-    up_far = [forward(after(one, *gate_far), w_up) for one in acts_far]
+        near, *acts_all = gathered_features(flat_acts, n_ex, n_cores)
+        acts_all.append(near)
+        near, *grad_all = gathered_features(flat_grad, n_ex, n_cores)
+        grad_all.append(near)
+    acts_all = jnp.concatenate(acts_all)
+    gate_all = forward(acts_all, w_gate)
+    up_all = forward(after(acts_all, gate_all), w_up)
     if direct:
-        grad_all = spread_features(after(flat_grad, *up_far))
-    gate_near = forward(after(acts_near, *up_far), w_gate)
-    up_near = forward(after(acts_near, gate_near), w_up)
-    for step, (gate, up) in enumerate(zip(gate_far, up_far), 1):
-        both = pack(jnp.stack([core_sum(gate, 0, up_near), core_sum(up, 0, up_near)]))
+        grad_all = spread_features(after(flat_grad, up_all))
+    for step in range(1, n_ex):
+        begin = (step - 1) * tok_rows
+        both = pack(jnp.stack([core_sum(gate_all, begin), core_sum(up_all, begin)]))
         received = shift(both, "example", step)
         arrived.append(received)
     if direct:
         grad_all = arrived_features(grad_all, both)
-    else:
-        grad_all = [*grad_far, grad_near]
     down_all = dot_rows(jnp.concatenate(grad_all), w_down)
     for step in range(1, n_ex):
         sent = pack(core_sum(down_all, (step - 1) * tok_rows))
         arrived_down.append(shift(sent, "example", step))
-    down_near = after(down_all, received)
+    begin = (n_ex - 1) * tok_rows
     own = [
-        core_sum(gate_near, 0),
-        core_sum(up_near, 0),
-        core_sum(down_near, (n_ex - 1) * tok_rows),
+        core_sum(gate_all, begin),
+        core_sum(up_all, begin),
+        core_sum(after(down_all, received), begin),
     ]
     if n_z > 8:
         model_sum = lax.psum(model_part, "tensor")

time: 179 us -> 180 us (level)
  waiting for transfers between devices: 41.1 us -> 64.7 us
  starting transfers between devices: 64.6 us -> 51.3 us
  matrix products: 32.7 us -> 24.3 us
  local copies, waits for them, and re-layouts: 12.5 us -> 10.4 us
    ppermute x4, waiting for transfers between devices: 0.29 us -> 15.8 us  [spread_features(): pieces.append(lax.ppermute(flat, ('tensor', 'example', 'test'), pairs))]
    dot_general x4 -> x2, matrix products: 24.9 us -> 16.2 us  [forward(): return pack(jnp.dot(tokens, weight, preferred_element_type=F32))]
    ppermute x18, starting transfers between devices: 32.9 us -> 24.8 us  [shift(): return lax.ppermute(value, axis, [(i, (i + step) % n) for i in range(n)])]
    ppermute x18, waiting for transfers between devices: 37.1 us -> 44.9 us  [shift(): return lax.ppermute(value, axis, [(i, (i + step) % n) for i in range(n)])]
    ppermute x4, starting transfers between devices: 29 us -> 23.8 us  [spread_features(): pieces.append(lax.ppermute(flat, ('tensor', 'example', 'test'), pairs))]
  transfers between devices with their start and end apart: 25 -> 25, of which waited for: 13 -> 14; matrix products, arithmetic and copies ran while one was open for 21% -> 18% of each run, Pallas kernels for 4% -> 4%
where the time goes in v13:
time: 180 us; the launch traced here: 179 us
  waiting for transfers between devices  64.7 us (36%)
  starting transfers between devices  51.3 us (28%)
  matrix products  24.3 us (14%)
  other arithmetic  18.4 us (10%)
  local copies, waits for them, and re-layouts  10.4 us (6%)
  Pallas kernels  8.71 us (5%)
    ppermute x18, waiting for transfers between devices, shift(): return lax.ppermute(value, axis, [(i, (i + step) % n) for i in range(n)])  44.9 us
    ppermute x18, starting transfers between devices, shift(): return lax.ppermute(value, axis, [(i, (i + step) % n) for i in range(n)])  24.8 us
    ppermute x4, starting transfers between devices, spread_features(): pieces.append(lax.ppermute(flat, ('tensor', 'example', 'test'), pairs))  23.8 us
    dot_general x2, matrix products, forward(): return pack(jnp.dot(tokens, weight, preferred_element_type=F32))  16.2 us
    ppermute x4, waiting for transfers between devices, spread_features(): pieces.append(lax.ppermute(flat, ('tensor', 'example', 'test'), pairs))  15.8 us
    pallas_call x1, Pallas kernels, dot_rows(): pl.pallas_call(dot_rows_kernel, out_shape=jax.ShapeDtypeStruct((rows, hid...  7.51 us
    convert_element_type x5, other arithmetic, pack(): return (value * SEND_SCALE).astype(jnp.float16)  6.34 us
    unnamed x41, local copies, waits for them, and re-layouts  4.48 us
  transfers between devices with their start and end apart: 25, of which 14 were waited for; matrix products, arithmetic and copies ran while one was open for 18% of the time, Pallas kernels for 4%

profile of v13, /device:TPU:0, one launch (start us, length us, event | category | flops | bytes accessed | tf_op | source)
XLA Modules:
  0.0 179.0 jit_solution(17338237358249419007)
XLA Ops:
  0.6 6.8 %collective-permute-start.1 = (bf16[256,1280]{1,0:T(8,128)(2,1)}, bf16[256,1280]{1,0:T(8,128)(2,1)}, u32[]{:S(2)}, u32[]{:S(2)}) collective-permute-start(bf16[256,1280]{1,0:T(8,128)(2,1)} %bitcast.92), channel_id=1, source_target_pairs={{0,0},{1,4},{2,8},{3,12},{4,1},{5,5},{6,9},{7,13},{10,10},{11,14},... | collective-permute-start | bytes 1966088 | tf_op jit(solution)/shard_map/ppermute | solution.py:66
  7.5 0.7 collective-permute-start
  8.2 1.3 collective-permute-start.2
  9.5 1.8 %fusion.20 = (bf16[2048,64]{0,1:T(8,128)(2,1)}, bf16[2048,64]{0,1:T(8,128)(2,1)S(1)}) fusion(bf16[4096,192]{0,1:T(8,128)(2,1)} %param.16, s32[]{:T(128)S(6)} %select_n.62, s32[]{:T(128)S(6)} %add.164), kind=kLoop, calls=%fused_computation.82 | loop fusion | bytes 1048584 | tf_op jit(solution)/shard_map/slice | solution.py:198
  11.3 2.0 %copy.22.refs_3_ = bf16[2048,64]{1,0:T(8,128)(2,1)} copy(bf16[2048,64]{0,1:T(8,128)(2,1)} %get-tuple-element.30) | data formatting | bytes 524288
  13.3 1.0 copy.21.refs_2_
  14.3 1.4 fusion.9
  15.7 1.6 fusion.6
  17.3 7.2 %collective-permute-done.2 = s32[2]{0:T(128)S(1)} collective-permute-done((s32[2]{0:T(128)}, s32[2]{0:T(128)S(1)}, u32[]{:S(2)}, u32[]{:S(2)}) %collective-permute-start.2) | collective-permute-done | bytes 40 | tf_op jit(solution)/shard_map/ppermute | solution.py:15
  24.5 1.4 broadcast_select_fusion.3
  26.0 10.4 %multiply_convert_fusion.1 = f16[512,4096]{1,0:T(8,128)(2,1)S(1)} fusion(bf16[1280,4096]{1,0:T(8,128)(2,1)} %param.12, bf16[256,1280]{1,0:T(8,128)(2,1)S(1)} %get-tuple-element.35, bf16[256,1280]{1,0:T(8,128)(2,1)S(1)} %get-tuple-element.34), kind=kOutput, calls=%fused_computation.1 | convolution fusion | flops 5375524864 | bytes 15990784 | tf_op jit(solution)/shard_map/dot_general | solution.py:174
  37.0 3.4 %collective-permute-start.5 = (f16[256,2048]{1,0:T(8,128)(2,1)S(1)}, f16[256,2048]{1,0:T(8,128)(2,1)S(1)}, u32[]{:S(2)}, u32[]{:S(2)}) collective-permute-start(f16[256,2048]{1,0:T(8,128)(2,1)S(1)} %get-tuple-element.27), channel_id=1, source_target_pairs={{0,1},{1,0},{2,3},{3,2},{4,5},{5,4},{6,7},{7,6},{8,9},{9,8},{10,11... | collective-permute-start | bytes 3145736 | tf_op jit(solution)/shard_map/ppermute | solution.py:15
  40.5 5.8 %multiply_convert_fusion = f16[512,4096]{1,0:T(8,128)(2,1)S(1)} fusion(bf16[512,1280]{1,0:T(8,128)(2,1)S(1)} %pad_maximum_fusion, bf16[1280,4096]{1,0:T(8,128)(2,1)S(1)} %bitcast.100), kind=kOutput, calls=%fused_computation | convolution fusion | flops 5372903424 | bytes 15990784 | tf_op jit(solution)/shard_map/dot_general | solution.py:174
  46.3 1.5 constant_dynamic-slice_fusion.6
  47.9 0.7 collective-permute-start.4
  48.6 15.6 %collective-permute-start.3 = (bf16[256,1280]{1,0:T(8,128)(2,1)S(1)}, bf16[256,1280]{1,0:T(8,128)(2,1)S(1)}, u32[]{:S(2)}, u32[]{:S(2)}) collective-permute-start(bf16[256,1280]{1,0:T(8,128)(2,1)S(1)} %bitcast.91), channel_id=1, source_target_pairs={{0,8},{1,12},{2,0},{3,4},{4,9},{5,13},{6,1},{7,5},{10,2},{11,6},{8... | collective-permute-start | bytes 1966088 | tf_op jit(solution)/shard_map/ppermute | solution.py:66
  65.0 1.9 %fusion = f16[2,256,2048]{2,1,0:T(8,128)(2,1)} fusion(f32[1,256,2048]{2,1,0:T(8,128)S(1)} %multiply_bitcast_fusion, f32[1,256,2048]{2,1,0:T(8,128)S(1)} %multiply_bitcast_fusion.1), kind=kLoop, calls=%fused_computation.3 | loop fusion | flops 3145728 | bytes 6291456 | tf_op jit(solution)/shard_map/convert_element_type | solution.py:19
  66.9 15.8 %collective-permute-done.3 = bf16[256,1280]{1,0:T(8,128)(2,1)S(1)} collective-permute-done((bf16[256,1280]{1,0:T(8,128)(2,1)S(1)}, bf16[256,1280]{1,0:T(8,128)(2,1)S(1)}, u32[]{:S(2)}, u32[]{:S(2)}) %collective-permute-start.3) | collective-permute-done | bytes 655392 | tf_op jit(solution)/shard_map/ppermute | solution.py:66
  82.9 7.5 %shard_map.113 = f32[512,4096]{1,0:T(8,128)S(1)} custom-call(bf16[512,1280]{1,0:T(8,128)(2,1)S(1)} %pad_maximum_fusion.1.tokens_ref, bf16[4096,1280]{1,0:T(8,128)(2,1)S(1)} %bitcast.87), custom_call_target="tpu_custom_call" | custom-call | flops 1 | bytes 1 | tf_op jit(solution)/shard_map/pallas_call | solution.py:97
  91.3 2.0 %collective-permute-done.9 = f16[256,2048]{1,0:T(8,128)(2,1)S(1)} collective-permute-done((f16[256,2048]{1,0:T(8,128)(2,1)S(1)}, f16[256,2048]{1,0:T(8,128)(2,1)S(1)}, u32[]{:S(2)}, u32[]{:S(2)}) %collective-permute-start.9) | collective-permute-done | bytes 1048608 | tf_op jit(solution)/shard_map/ppermute | solution.py:15
  93.7 1.4 multiply_convert_fusion.3
  95.1 11.2 %collective-permute-start.15 = (f16[256,192]{0,1:T(8,128)(2,1)S(1)}, f16[256,192]{0,1:T(8,128)(2,1)S(1)}, u32[]{:S(2)}, u32[]{:S(2)}) collective-permute-start(f16[256,192]{0,1:T(8,128)(2,1)S(1)} %multiply_convert_fusion.7), channel_id=1, source_target_pairs={{0,12},{4,0},{8,4},{12,8},{1,13},{5,1},{9,5},{13,9},{2,14},{6,2},{... | collective-permute-start | bytes 294920 | tf_op jit(solution)/shard_map/ppermute | solution.py:15
  106.4 1.0 copy-done.6
  107.4 1.6 collective-permute-start.13
  109.6 7.1 %collective-permute-done.14 = f16[256,192]{0,1:T(8,128)(2,1)} collective-permute-done((f16[256,192]{0,1:T(8,128)(2,1)S(1)}, f16[256,192]{0,1:T(8,128)(2,1)}, u32[]{:S(2)}, u32[]{:S(2)}) %collective-permute-start.14) | collective-permute-done | bytes 98336 | tf_op jit(solution)/shard_map/ppermute | solution.py:15
  116.7 11.0 %collective-permute-done.7 = f16[2,256,2048]{2,1,0:T(8,128)(2,1)} collective-permute-done((f16[2,256,2048]{2,1,0:T(8,128)(2,1)}, f16[2,256,2048]{2,1,0:T(8,128)(2,1)}, u32[]{:S(2)}, u32[]{:S(2)}) %collective-permute-start.7) | collective-permute-done | bytes 2097184 | tf_op jit(solution)/shard_map/ppermute | solution.py:15
  127.7 1.7 multiply_add_fusion.1
  129.4 1.1 copy.17
  130.6 2.8 %multiply_convert_fusion.5 = f16[256,2048]{1,0:T(8,128)(2,1)} fusion(f32[512,4096]{1,0:T(8,128)} %copy-done.1, s32[]{:T(128)S(6)} %select_n.65), kind=kLoop, calls=%fused_computation.15 | loop fusion | flops 1048576 | bytes 3145732 | tf_op jit(solution)/shard_map/convert_element_type | solution.py:19
  133.6 4.4 %fusion.3 = (f32[256,2048]{1,0:T(8,128)S(1)}, f32[256,2048]{1,0:T(8,128)S(1)}) fusion(f16[256,2048]{1,0:T(8,128)(2,1)} %copy-done.6, f16[2,256,2048]{2,1,0:T(8,128)(2,1)} %collective-permute-done.7, f16[512,4096]{1,0:T(8,128)(2,1)} %copy-done.5, s32[]{:T(128)S(6)} %select_n.62, f16[256,2048]{1,0:T(8,128)(2,1)} %collective-permute-done.11, ...), kind=kLoop, calls=%fused_computation.11 | loop fusion | flops 11010048 | bytes 10485764 | tf_op jit(solution)/shard_map/mul | solution.py:257
  138.0 2.6 %fusion.4 = f32[256,64]{0,1:T(8,128)S(1)} fusion(f32[256,2048]{1,0:T(8,128)S(1)} %get-tuple-element.24.refs_1_, f16[256,2048]{1,0:T(8,128)(2,1)} %collective-permute-done.11, f16[2,256,2048]{2,1,0:T(8,128)(2,1)} %collective-permute-done.7, f16[512,4096]{1,0:T(8,128)(2,1)} %copy-done.4, s32[]{:T(128)S(6)} %select_n.62, bf16[4096,192]{0,1:T(8,128)(2,1)} %param.16, ...), kind=kOutput, calls=%fused_computation.24 | convolution fusion | flops 71303168 | bytes 5572096 | tf_op jit(solution)/shard_map/dot_general | solution.py:260
  141.0 7.2 %collective-permute-done.10 = f16[256,2048]{1,0:T(8,128)(2,1)} collective-permute-done((f16[256,2048]{1,0:T(8,128)(2,1)}, f16[256,2048]{1,0:T(8,128)(2,1)}, u32[]{:S(2)}, u32[]{:S(2)}) %collective-permute-start.10) | collective-permute-done | bytes 1048608 | tf_op jit(solution)/shard_map/ppermute | solution.py:15
  148.2 2.5 %multiply_add_fusion.down_ref = f32[256,2048]{1,0:T(8,128)S(1)} fusion(f16[256,2048]{1,0:T(8,128)(2,1)} %collective-permute-done.10, f16[256,2048]{1,0:T(8,128)(2,1)S(1)} %collective-permute-done.8, f32[512,4096]{1,0:T(8,128)} %copy-done.1, s32[]{:T(128)S(6)} %select_n.62), kind=kLoop, calls=%fused_computation.12 | loop fusion | flops 3145728 | bytes 6291460 | tf_op jit(solution)/shard_map/add | solution.py:255
  150.7 1.2 shard_map.114
  152.0 3.8 %collective-permute-start.18 = (f32[6,16,64]{2,1,0:T(8,128)S(1)}, f32[6,16,64]{2,1,0:T(8,128)}, u32[]{:S(2)}, u32[]{:S(2)}) collective-permute-start(f32[6,16,64]{2,1,0:T(8,128)S(1)} %get-tuple-element.39), channel_id=1, source_target_pairs={{0,12},{4,0},{8,4},{12,8},{1,13},{5,1},{9,5},{13,9},{2,14},{6,2},{... | collective-permute-start | bytes 73736 | tf_op jit(solution)/shard_map/ppermute | solution.py:15
  155.8 2.7 %collective-permute-done.16 = f32[6,16,64]{2,1,0:T(8,128)} collective-permute-done((f32[6,16,64]{2,1,0:T(8,128)S(1)}, f32[6,16,64]{2,1,0:T(8,128)}, u32[]{:S(2)}, u32[]{:S(2)}) %collective-permute-start.16) | collective-permute-done | bytes 24608 | tf_op jit(solution)/shard_map/ppermute | solution.py:15
  158.5 2.4 %collective-permute-done.17 = f32[6,16,64]{2,1,0:T(8,128)} collective-permute-done((f32[6,16,64]{2,1,0:T(8,128)S(1)}, f32[6,16,64]{2,1,0:T(8,128)}, u32[]{:S(2)}, u32[]{:S(2)}) %collective-permute-start.17) | collective-permute-done | bytes 24608 | tf_op jit(solution)/shard_map/ppermute | solution.py:15
  160.9 0.9 fusion.15
  161.9 2.6 %collective-permute-start.20 = (f32[6,16,64]{2,1,0:T(8,128)S(1)}, f32[6,16,64]{2,1,0:T(8,128)S(1)}, u32[]{:S(2)}, u32[]{:S(2)}) collective-permute-start(f32[6,16,64]{2,1,0:T(8,128)S(1)} %fusion.15), channel_id=1, source_target_pairs={{0,3},{1,2},{2,1},{3,0},{4,7},{5,6},{6,5},{7,4},{8,11},{9,10},{10,... | collective-permute-start | bytes 73736 | tf_op jit(solution)/shard_map/ppermute | solution.py:280
  164.5 2.0 %collective-permute-done.20 = f32[6,16,64]{2,1,0:T(8,128)S(1)} collective-permute-done((f32[6,16,64]{2,1,0:T(8,128)S(1)}, f32[6,16,64]{2,1,0:T(8,128)S(1)}, u32[]{:S(2)}, u32[]{:S(2)}) %collective-permute-start.20) | collective-permute-done | bytes 24608 | tf_op jit(solution)/shard_map/ppermute | solution.py:280
  166.5 2.0 %collective-permute-done.19 = f32[6,16,64]{2,1,0:T(8,128)S(1)} collective-permute-done((f32[6,16,64]{2,1,0:T(8,128)S(1)}, f32[6,16,64]{2,1,0:T(8,128)S(1)}, u32[]{:S(2)}, u32[]{:S(2)}) %collective-permute-start.19) | collective-permute-done | bytes 24608 | tf_op jit(solution)/shard_map/ppermute | solution.py:280
  168.7 1.3 fusion.21
  170.1 1.9 %collective-permute-start.22 = (f32[4,512]{1,0:T(4,128)S(1)}, f32[4,512]{1,0:T(4,128)S(1)}, u32[]{:S(2)}, u32[]{:S(2)}) collective-permute-start(f32[4,512]{1,0:T(4,128)S(1)} %fusion.21), channel_id=1, source_target_pairs={{0,12},{4,0},{8,4},{12,8},{1,13},{5,1},{9,5},{13,9},{2,14},{6,2},{... | collective-permute-start | bytes 24584 | tf_op jit(solution)/shard_map/ppermute | solution.py:15
  172.7 1.0 collective-permute-done.22
  173.7 3.0 %collective-permute-done.23 = f32[4,512]{1,0:T(4,128)S(1)} collective-permute-done((f32[4,512]{1,0:T(4,128)S(1)}, f32[4,512]{1,0:T(4,128)S(1)}, u32[]{:S(2)}, u32[]{:S(2)}) %collective-permute-start.23) | collective-permute-done | bytes 8224 | tf_op jit(solution)/shard_map/ppermute | solution.py:15
  176.7 0.7 collective-permute-done.24
  177.5 0.6 constant_dynamic-slice_fusion.1
  178.1 0.9 fusion.16
  (93 shorter events, 5.5 us)
Async XLA Ops:
  0.6 168.1 %copy-start = (bf16[3,16,64,512]{3,2,1,0:T(8,128)(2,1)S(1)}, bf16[3,16,64,512]{3,2,1,0:T(8,128)(2,1)}, u32[]{:S(2)}) copy-start(bf16[3,16,64,512]{3,2,1,0:T(8,128)(2,1)} %param.17) | copy-start | bytes 9437188
  0.6 23.8 %collective-permute-start.1 = (bf16[256,1280]{1,0:T(8,128)(2,1)}, bf16[256,1280]{1,0:T(8,128)(2,1)}, u32[]{:S(2)}, u32[]{:S(2)}) collective-permute-start(bf16[256,1280]{1,0:T(8,128)(2,1)} %bitcast.92), channel_id=1, source_target_pairs={{0,0},{1,4},{2,8},{3,12},{4,1},{5,5},{6,9},{7,13},{10,10},{11,14},... | collective-permute-start | bytes 1966088 | tf_op jit(solution)/shard_map/ppermute | solution.py:66
  7.5 17.0 %collective-permute-start = (bf16[256,1280]{1,0:T(8,128)(2,1)}, bf16[256,1280]{1,0:T(8,128)(2,1)}, u32[]{:S(2)}, u32[]{:S(2)}) collective-permute-start(bf16[256,1280]{1,0:T(8,128)(2,1)} %bitcast.93), channel_id=1, source_target_pairs={{0,8},{1,12},{2,0},{3,4},{4,9},{5,13},{6,1},{7,5},{10,2},{11,6},{8... | collective-permute-start | bytes 1966088 | tf_op jit(solution)/shard_map/ppermute | solution.py:66
  8.2 16.3 %collective-permute-start.2 = (s32[2]{0:T(128)}, s32[2]{0:T(128)S(1)}, u32[]{:S(2)}, u32[]{:S(2)}) collective-permute-start(s32[2]{0:T(128)} %param.19), channel_id=1, source_target_pairs={{0,2},{2,0},{1,3},{3,1},{4,6},{6,4},{5,7},{7,5},{8,10},{10,8},{9,1... | collective-permute-start | bytes 32 | tf_op jit(solution)/shard_map/ppermute | solution.py:15
  9.5 14.9 %copy-start.8 = (s32[2]{0:T(128)S(1)}, s32[2]{0:T(128)}, u32[]{:S(2)}) copy-start(s32[2]{0:T(128)} %param.19) | copy-start | bytes 28
  25.9 14.6 %slice-start.3 = ((s8[10485760]{0:T(1024)(128)(4,1)}), s8[4194304]{0:T(1024)(128)(4,1)S(1)}, s32[]{:S(2)}) async-start(s8[10485760]{0:T(1024)(128)(4,1)} %bitcast.99), calls=%async_computation.3 | async-start | bytes 8388608
  26.0 14.5 %slice-start.4 = ((s8[10485760]{0:T(1024)(128)(4,1)}), s8[4194304]{0:T(1024)(128)(4,1)S(1)}, s32[]{:S(2)}) async-start(s8[10485760]{0:T(1024)(128)(4,1)} %bitcast.99), calls=%async_computation.4 | async-start | bytes 8388608
  26.0 14.5 %slice-start.5 = ((s8[10485760]{0:T(1024)(128)(4,1)}), s8[2097152]{0:T(1024)(128)(4,1)S(1)}, s32[]{:S(2)}) async-start(s8[10485760]{0:T(1024)(128)(4,1)} %bitcast.99), calls=%async_computation.5 | async-start | bytes 4194304
  36.4 27.7 %copy-start.5 = (f16[512,4096]{1,0:T(8,128)(2,1)}, f16[512,4096]{1,0:T(8,128)(2,1)S(1)}, u32[]{:S(2)}) copy-start(f16[512,4096]{1,0:T(8,128)(2,1)S(1)} %multiply_convert_fusion.1) | copy-start | bytes 12582916
  37.0 27.1 %collective-permute-start.5 = (f16[256,2048]{1,0:T(8,128)(2,1)S(1)}, f16[256,2048]{1,0:T(8,128)(2,1)S(1)}, u32[]{:S(2)}, u32[]{:S(2)}) collective-permute-start(f16[256,2048]{1,0:T(8,128)(2,1)S(1)} %get-tuple-element.27), channel_id=1, source_target_pairs={{0,1},{1,0},{2,3},{3,2},{4,5},{5,4},{6,7},{7,6},{8,9},{9,8},{10,11... | collective-permute-start | bytes 3145736 | tf_op jit(solution)/shard_map/ppermute | solution.py:15
  46.3 18.3 %copy-start.4 = (f16[512,4096]{1,0:T(8,128)(2,1)}, f16[512,4096]{1,0:T(8,128)(2,1)S(1)}, u32[]{:S(2)}) copy-start(f16[512,4096]{1,0:T(8,128)(2,1)S(1)} %multiply_convert_fusion) | copy-start | bytes 12582916
  46.3 1.6 copy-start.7
  47.8 16.7 %collective-permute-start.6 = (f16[256,2048]{1,0:T(8,128)(2,1)S(1)}, f16[256,2048]{1,0:T(8,128)(2,1)S(1)}, u32[]{:S(2)}, u32[]{:S(2)}) collective-permute-start(f16[256,2048]{1,0:T(8,128)(2,1)S(1)} %get-tuple-element.29), channel_id=1, source_target_pairs={{0,1},{1,0},{2,3},{3,2},{4,5},{5,4},{6,7},{7,6},{8,9},{9,8},{10,11... | collective-permute-start | bytes 3145736 | tf_op jit(solution)/shard_map/ppermute | solution.py:15
  47.9 19.0 %collective-permute-start.4 = (bf16[256,1280]{1,0:T(8,128)(2,1)S(1)}, bf16[256,1280]{1,0:T(8,128)(2,1)S(1)}, u32[]{:S(2)}, u32[]{:S(2)}) collective-permute-start(bf16[256,1280]{1,0:T(8,128)(2,1)S(1)} %bitcast.90), channel_id=1, source_target_pairs={{0,0},{1,4},{2,8},{3,12},{4,1},{5,5},{6,9},{7,13},{10,10},{11,14},... | collective-permute-start | bytes 1966088 | tf_op jit(solution)/shard_map/ppermute | solution.py:66
  48.6 34.1 %collective-permute-start.3 = (bf16[256,1280]{1,0:T(8,128)(2,1)S(1)}, bf16[256,1280]{1,0:T(8,128)(2,1)S(1)}, u32[]{:S(2)}, u32[]{:S(2)}) collective-permute-start(bf16[256,1280]{1,0:T(8,128)(2,1)S(1)} %bitcast.91), channel_id=1, source_target_pairs={{0,8},{1,12},{2,0},{3,4},{4,9},{5,13},{6,1},{7,5},{10,2},{11,6},{8... | collective-permute-start | bytes 1966088 | tf_op jit(solution)/shard_map/ppermute | solution.py:66
  64.1 18.7 %slice-start = ((s8[10485760]{0:T(1024)(128)(4,1)}), s8[4194304]{0:T(1024)(128)(4,1)S(1)}, s32[]{:S(2)}) async-start(s8[10485760]{0:T(1024)(128)(4,1)} %bitcast.86), calls=%async_computation | async-start | bytes 8388608
  64.5 18.3 %slice-start.1 = ((s8[10485760]{0:T(1024)(128)(4,1)}), s8[4194304]{0:T(1024)(128)(4,1)S(1)}, s32[]{:S(2)}) async-start(s8[10485760]{0:T(1024)(128)(4,1)} %bitcast.86), calls=%async_computation.1 | async-start | bytes 8388608
  64.9 17.9 %slice-start.2 = ((s8[10485760]{0:T(1024)(128)(4,1)}), s8[2097152]{0:T(1024)(128)(4,1)S(1)}, s32[]{:S(2)}) async-start(s8[10485760]{0:T(1024)(128)(4,1)} %bitcast.86), calls=%async_computation.2 | async-start | bytes 4194304
  66.8 60.9 %collective-permute-start.7 = (f16[2,256,2048]{2,1,0:T(8,128)(2,1)}, f16[2,256,2048]{2,1,0:T(8,128)(2,1)}, u32[]{:S(2)}, u32[]{:S(2)}) collective-permute-start(f16[2,256,2048]{2,1,0:T(8,128)(2,1)} %fusion), channel_id=1, source_target_pairs={{0,2},{2,0},{1,3},{3,1},{4,6},{6,4},{5,7},{7,5},{8,10},{10,8},{9,1... | collective-permute-start | bytes 6291464 | tf_op jit(solution)/shard_map/ppermute | solution.py:15
  90.4 3.3 %copy-start.1 = (f32[512,4096]{1,0:T(8,128)}, f32[512,4096]{1,0:T(8,128)S(1)}, u32[]{:S(2)}) copy-start(f32[512,4096]{1,0:T(8,128)S(1)} %shard_map.113) | copy-start | bytes 25165828
  90.6 2.7 %collective-permute-start.9 = (f16[256,2048]{1,0:T(8,128)(2,1)S(1)}, f16[256,2048]{1,0:T(8,128)(2,1)S(1)}, u32[]{:S(2)}, u32[]{:S(2)}) collective-permute-start(f16[256,2048]{1,0:T(8,128)(2,1)S(1)} %multiply_convert_fusion.4), channel_id=1, source_target_pairs={{0,1},{1,0},{2,3},{3,2},{4,5},{5,4},{6,7},{7,6},{8,9},{9,8},{10,11... | collective-permute-start | bytes 3145736 | tf_op jit(solution)/shard_map/ppermute | solution.py:15
  90.7 15.7 %collective-permute-start.12 = (f16[256,2048]{1,0:T(8,128)(2,1)S(1)}, f16[256,2048]{1,0:T(8,128)(2,1)S(1)}, u32[]{:S(2)}, u32[]{:S(2)}) collective-permute-start(f16[256,2048]{1,0:T(8,128)(2,1)S(1)} %get-tuple-element.26), channel_id=1, source_target_pairs={{0,1},{1,0},{2,3},{3,2},{4,5},{5,4},{6,7},{7,6},{8,9},{9,8},{10,11... | collective-permute-start | bytes 3145736 | tf_op jit(solution)/shard_map/ppermute | solution.py:15
  91.2 17.8 %collective-permute-start.11 = (f16[256,2048]{1,0:T(8,128)(2,1)}, f16[256,2048]{1,0:T(8,128)(2,1)}, u32[]{:S(2)}, u32[]{:S(2)}) collective-permute-start(f16[256,2048]{1,0:T(8,128)(2,1)} %get-tuple-element.28), channel_id=1, source_target_pairs={{0,1},{1,0},{2,3},{3,2},{4,5},{5,4},{6,7},{7,6},{8,9},{9,8},{10,11... | collective-permute-start | bytes 3145736 | tf_op jit(solution)/shard_map/ppermute | solution.py:15
  91.3 17.7 %copy-start.9 = (s32[2]{0:T(128)S(1)}, s32[2]{0:T(128)}, u32[]{:S(2)}) copy-start(s32[2]{0:T(128)} %param.18) | copy-start | bytes 28
  95.1 14.5 %collective-permute-start.15 = (f16[256,192]{0,1:T(8,128)(2,1)S(1)}, f16[256,192]{0,1:T(8,128)(2,1)S(1)}, u32[]{:S(2)}, u32[]{:S(2)}) collective-permute-start(f16[256,192]{0,1:T(8,128)(2,1)S(1)} %multiply_convert_fusion.7), channel_id=1, source_target_pairs={{0,12},{4,0},{8,4},{12,8},{1,13},{5,1},{9,5},{13,9},{2,14},{6,2},{... | collective-permute-start | bytes 294920 | tf_op jit(solution)/shard_map/ppermute | solution.py:15
  106.4 10.4 %collective-permute-start.14 = (f16[256,192]{0,1:T(8,128)(2,1)S(1)}, f16[256,192]{0,1:T(8,128)(2,1)}, u32[]{:S(2)}, u32[]{:S(2)}) collective-permute-start(f16[256,192]{0,1:T(8,128)(2,1)S(1)} %multiply_convert_fusion.7), channel_id=1, source_target_pairs={{0,8},{4,12},{8,0},{12,4},{1,9},{5,13},{9,1},{13,5},{2,10},{6,14},... | collective-permute-start | bytes 294920 | tf_op jit(solution)/shard_map/ppermute | solution.py:15
  106.4 1.0 copy-start.6
  107.4 9.3 %collective-permute-start.13 = (f16[256,192]{0,1:T(8,128)(2,1)S(1)}, f16[256,192]{0,1:T(8,128)(2,1)}, u32[]{:S(2)}, u32[]{:S(2)}) collective-permute-start(f16[256,192]{0,1:T(8,128)(2,1)S(1)} %multiply_convert_fusion.7), channel_id=1, source_target_pairs={{0,4},{4,8},{8,12},{12,0},{1,5},{5,9},{9,13},{13,1},{2,6},{6,10},{... | collective-permute-start | bytes 294920 | tf_op jit(solution)/shard_map/ppermute | solution.py:15
  109.0 39.2 %collective-permute-start.10 = (f16[256,2048]{1,0:T(8,128)(2,1)}, f16[256,2048]{1,0:T(8,128)(2,1)}, u32[]{:S(2)}, u32[]{:S(2)}) collective-permute-start(f16[256,2048]{1,0:T(8,128)(2,1)} %multiply_convert_fusion.3), channel_id=1, source_target_pairs={{0,2},{2,0},{1,3},{3,1},{4,6},{6,4},{5,7},{7,5},{8,10},{10,8},{9,1... | collective-permute-start | bytes 3145736 | tf_op jit(solution)/shard_map/ppermute | solution.py:15
  133.5 7.5 %collective-permute-start.8 = (f16[256,2048]{1,0:T(8,128)(2,1)}, f16[256,2048]{1,0:T(8,128)(2,1)S(1)}, u32[]{:S(2)}, u32[]{:S(2)}) collective-permute-start(f16[256,2048]{1,0:T(8,128)(2,1)} %multiply_convert_fusion.5), channel_id=1, source_target_pairs={{0,1},{1,0},{2,3},{3,2},{4,5},{5,4},{6,7},{7,6},{8,9},{9,8},{10,11... | collective-permute-start | bytes 3145736 | tf_op jit(solution)/shard_map/ppermute | solution.py:15
  141.0 9.7 %copy-start.2 = (bf16[2048,64]{1,0:T(8,128)(2,1)S(1)}, bf16[2048,64]{1,0:T(8,128)(2,1)}, u32[]{:S(2)}) copy-start(bf16[2048,64]{1,0:T(8,128)(2,1)} %copy.22.refs_3_) | copy-start | bytes 786436
  141.0 9.7 %copy-start.3 = (bf16[2048,64]{1,0:T(8,128)(2,1)S(1)}, bf16[2048,64]{1,0:T(8,128)(2,1)}, u32[]{:S(2)}) copy-start(bf16[2048,64]{1,0:T(8,128)(2,1)} %copy.21.refs_2_) | copy-start | bytes 786436
  152.0 6.5 %collective-permute-start.16 = (f32[6,16,64]{2,1,0:T(8,128)S(1)}, f32[6,16,64]{2,1,0:T(8,128)}, u32[]{:S(2)}, u32[]{:S(2)}) collective-permute-start(f32[6,16,64]{2,1,0:T(8,128)S(1)} %get-tuple-element.38), channel_id=1, source_target_pairs={{0,4},{4,8},{8,12},{12,0},{1,5},{5,9},{9,13},{13,1},{2,6},{6,10},{... | collective-permute-start | bytes 73736 | tf_op jit(solution)/shard_map/ppermute | solution.py:15
  152.0 6.5 %collective-permute-start.18 = (f32[6,16,64]{2,1,0:T(8,128)S(1)}, f32[6,16,64]{2,1,0:T(8,128)}, u32[]{:S(2)}, u32[]{:S(2)}) collective-permute-start(f32[6,16,64]{2,1,0:T(8,128)S(1)} %get-tuple-element.39), channel_id=1, source_target_pairs={{0,12},{4,0},{8,4},{12,8},{1,13},{5,1},{9,5},{13,9},{2,14},{6,2},{... | collective-permute-start | bytes 73736 | tf_op jit(solution)/shard_map/ppermute | solution.py:15
  155.8 5.1 %collective-permute-start.17 = (f32[6,16,64]{2,1,0:T(8,128)S(1)}, f32[6,16,64]{2,1,0:T(8,128)}, u32[]{:S(2)}, u32[]{:S(2)}) collective-permute-start(f32[6,16,64]{2,1,0:T(8,128)S(1)} %get-tuple-element.40), channel_id=1, source_target_pairs={{0,8},{4,12},{8,0},{12,4},{1,9},{5,13},{9,1},{13,5},{2,10},{6,14},... | collective-permute-start | bytes 73736 | tf_op jit(solution)/shard_map/ppermute | solution.py:15
  161.8 2.7 %collective-permute-start.21 = (f32[6,16,64]{2,1,0:T(8,128)S(1)}, f32[6,16,64]{2,1,0:T(8,128)S(1)}, u32[]{:S(2)}, u32[]{:S(2)}) collective-permute-start(f32[6,16,64]{2,1,0:T(8,128)S(1)} %fusion.15), channel_id=1, source_target_pairs={{0,1},{1,0},{2,3},{3,2},{4,5},{5,4},{6,7},{7,6},{8,9},{9,8},{10,11... | collective-permute-start | bytes 73736 | tf_op jit(solution)/shard_map/ppermute | solution.py:280
  161.9 4.7 %collective-permute-start.20 = (f32[6,16,64]{2,1,0:T(8,128)S(1)}, f32[6,16,64]{2,1,0:T(8,128)S(1)}, u32[]{:S(2)}, u32[]{:S(2)}) collective-permute-start(f32[6,16,64]{2,1,0:T(8,128)S(1)} %fusion.15), channel_id=1, source_target_pairs={{0,3},{1,2},{2,1},{3,0},{4,7},{5,6},{6,5},{7,4},{8,11},{9,10},{10,... | collective-permute-start | bytes 73736 | tf_op jit(solution)/shard_map/ppermute | solution.py:280
  164.5 4.1 %collective-permute-start.19 = (f32[6,16,64]{2,1,0:T(8,128)S(1)}, f32[6,16,64]{2,1,0:T(8,128)S(1)}, u32[]{:S(2)}, u32[]{:S(2)}) collective-permute-start(f32[6,16,64]{2,1,0:T(8,128)S(1)} %fusion.15), channel_id=1, source_target_pairs={{0,2},{1,3},{2,0},{3,1},{4,6},{5,7},{6,4},{7,5},{8,10},{9,11},{10,... | collective-permute-start | bytes 73736 | tf_op jit(solution)/shard_map/ppermute | solution.py:280
  170.1 3.7 %collective-permute-start.22 = (f32[4,512]{1,0:T(4,128)S(1)}, f32[4,512]{1,0:T(4,128)S(1)}, u32[]{:S(2)}, u32[]{:S(2)}) collective-permute-start(f32[4,512]{1,0:T(4,128)S(1)} %fusion.21), channel_id=1, source_target_pairs={{0,12},{4,0},{8,4},{12,8},{1,13},{5,1},{9,5},{13,9},{2,14},{6,2},{... | collective-permute-start | bytes 24584 | tf_op jit(solution)/shard_map/ppermute | solution.py:15
  172.0 5.4 %collective-permute-start.24 = (f32[4,512]{1,0:T(4,128)S(1)}, f32[4,512]{1,0:T(4,128)S(1)}, u32[]{:S(2)}, u32[]{:S(2)}) collective-permute-start(f32[4,512]{1,0:T(4,128)S(1)} %fusion.21), channel_id=1, source_target_pairs={{0,4},{4,8},{8,12},{12,0},{1,5},{5,9},{9,13},{13,1},{2,6},{6,10},{... | collective-permute-start | bytes 24584 | tf_op jit(solution)/shard_map/ppermute | solution.py:15
  172.2 4.5 %collective-permute-start.23 = (f32[4,512]{1,0:T(4,128)S(1)}, f32[4,512]{1,0:T(4,128)S(1)}, u32[]{:S(2)}, u32[]{:S(2)}) collective-permute-start(f32[4,512]{1,0:T(4,128)S(1)} %fusion.21), channel_id=1, source_target_pairs={{0,8},{4,12},{8,0},{12,4},{1,9},{5,13},{9,1},{13,5},{2,10},{6,14},... | collective-permute-start | bytes 24584 | tf_op jit(solution)/shard_map/ppermute | solution.py:15

commit v14 on v13

--- a/solution.py
+++ b/solution.py
@@ -214,14 +214,13 @@
     acts_all = jnp.concatenate(acts_all)
     gate_all = forward(acts_all, w_gate)
     up_all = forward(after(acts_all, gate_all), w_up)
-    if direct:
-        grad_all = spread_features(after(flat_grad, up_all))
     for step in range(1, n_ex):
         begin = (step - 1) * tok_rows
         both = pack(jnp.stack([core_sum(gate_all, begin), core_sum(up_all, begin)]))
         received = shift(both, "example", step)
         arrived.append(received)
     if direct:
+        grad_all = spread_features(after(flat_grad, both))
         grad_all = arrived_features(grad_all, both)
     down_all = dot_rows(jnp.concatenate(grad_all), w_down)
     for step in range(1, n_ex):
@@ -252,7 +251,7 @@
     gate_act, up_act = [
         kept + sum(unpack(one[which]) for one in arrived) for which, kept in enumerate(own[:2])
     ]
-    d_hidden = own[2] + sum(unpack(one) for one in arrived_down)
+    d_hidden = lax.optimization_barrier(own[2]) + sum(unpack(one) for one in arrived_down)
     sigmoid_gate = jax.nn.sigmoid(gate_act)
     silu_gate = gate_act * sigmoid_gate
     hidden = (silu_gate * up_act).astype(jnp.bfloat16)

time: 180 us -> 182 us (1.011)
  waiting for transfers between devices: 64.7 us -> 67.4 us
    ppermute x4, waiting for transfers between devices: 15.8 us -> 19.6 us  [spread_features(): pieces.append(lax.ppermute(flat, ('tensor', 'example', 'test'), pairs))]
  transfers between devices with their start and end apart: 25 -> 25, of which waited for: 14 -> 15; matrix products, arithmetic and copies ran while one was open for 18% -> 18% of each run, Pallas kernels for 4% -> 4%
where the time goes in v14:
time: 182 us
  waiting for transfers between devices  67.4 us (37%)
  starting transfers between devices  49.7 us (27%)
  matrix products  24.3 us (13%)
  other arithmetic  19.6 us (11%)
  local copies, waits for them, and re-layouts  10.8 us (6%)
  Pallas kernels  8.71 us (5%)
    ppermute x18, waiting for transfers between devices, shift(): return lax.ppermute(value, axis, [(i, (i + step) % n) for i in range(n)])  43.8 us
    ppermute x18, starting transfers between devices, shift(): return lax.ppermute(value, axis, [(i, (i + step) % n) for i in range(n)])  23.6 us
    ppermute x4, starting transfers between devices, spread_features(): pieces.append(lax.ppermute(flat, ('tensor', 'example', 'test'), pairs))  23.5 us
    ppermute x4, waiting for transfers between devices, spread_features(): pieces.append(lax.ppermute(flat, ('tensor', 'example', 'test'), pairs))  19.6 us
    dot_general x2, matrix products, forward(): return pack(jnp.dot(tokens, weight, preferred_element_type=F32))  16.2 us
    pallas_call x1, Pallas kernels, dot_rows(): pl.pallas_call(dot_rows_kernel, out_shape=jax.ShapeDtypeStruct((rows, hid...  7.51 us
    convert_element_type x5, other arithmetic, pack(): return (value * SEND_SCALE).astype(jnp.float16)  6.34 us
    unnamed x41, local copies, waits for them, and re-layouts  4.48 us
  transfers between devices with their start and end apart: 25, of which 15 were waited for; matrix products, arithmetic and copies ran while one was open for 18% of the time, Pallas kernels for 4%

profile of v14, /device:TPU:0, one launch (start us, length us, event | category | flops | bytes accessed | tf_op | source)
XLA Modules:
  0.0 181.6 jit_solution(16090868490243236213)
XLA Ops:
  0.6 6.8 %collective-permute-start.1 = (bf16[256,1280]{1,0:T(8,128)(2,1)}, bf16[256,1280]{1,0:T(8,128)(2,1)}, u32[]{:S(2)}, u32[]{:S(2)}) collective-permute-start(bf16[256,1280]{1,0:T(8,128)(2,1)} %bitcast.92), channel_id=1, source_target_pairs={{0,0},{1,4},{2,8},{3,12},{4,1},{5,5},{6,9},{7,13},{10,10},{11,14},... | collective-permute-start | bytes 1966088 | tf_op jit(solution)/shard_map/ppermute | solution.py:66
  8.2 1.3 collective-permute-start.2
  9.5 1.8 fusion.20
  11.3 2.0 %copy.22.refs_3_ = bf16[2048,64]{1,0:T(8,128)(2,1)} copy(bf16[2048,64]{0,1:T(8,128)(2,1)} %get-tuple-element.30) | data formatting | bytes 524288
  13.3 1.0 copy.21.refs_2_
  14.3 1.4 fusion.9
  15.7 1.6 fusion.6
  17.3 7.2 %collective-permute-done.2 = s32[2]{0:T(128)S(1)} collective-permute-done((s32[2]{0:T(128)}, s32[2]{0:T(128)S(1)}, u32[]{:S(2)}, u32[]{:S(2)}) %collective-permute-start.2) | collective-permute-done | bytes 40 | tf_op jit(solution)/shard_map/ppermute | solution.py:15
  24.5 1.4 broadcast_select_fusion.3
  26.0 10.4 %multiply_convert_fusion.1 = f16[512,4096]{1,0:T(8,128)(2,1)S(1)} fusion(bf16[1280,4096]{1,0:T(8,128)(2,1)} %param.12, bf16[256,1280]{1,0:T(8,128)(2,1)S(1)} %get-tuple-element.35, bf16[256,1280]{1,0:T(8,128)(2,1)S(1)} %get-tuple-element.34), kind=kOutput, calls=%fused_computation.1 | convolution fusion | flops 5375524864 | bytes 15990784 | tf_op jit(solution)/shard_map/dot_general | solution.py:174
  37.0 3.4 %collective-permute-start.3 = (f16[256,2048]{1,0:T(8,128)(2,1)S(1)}, f16[256,2048]{1,0:T(8,128)(2,1)S(1)}, u32[]{:S(2)}, u32[]{:S(2)}) collective-permute-start(f16[256,2048]{1,0:T(8,128)(2,1)S(1)} %get-tuple-element.27), channel_id=1, source_target_pairs={{0,1},{1,0},{2,3},{3,2},{4,5},{5,4},{6,7},{7,6},{8,9},{9,8},{10,11... | collective-permute-start | bytes 3145736 | tf_op jit(solution)/shard_map/ppermute | solution.py:15
  40.5 5.8 %multiply_convert_fusion = f16[512,4096]{1,0:T(8,128)(2,1)S(1)} fusion(bf16[512,1280]{1,0:T(8,128)(2,1)S(1)} %pad_maximum_fusion, bf16[1280,4096]{1,0:T(8,128)(2,1)S(1)} %bitcast.100), kind=kOutput, calls=%fused_computation | convolution fusion | flops 5372903424 | bytes 15990784 | tf_op jit(solution)/shard_map/dot_general | solution.py:174
  46.3 1.9 %constant_dynamic-slice_fusion.6 = (f16[256,2048]{1,0:T(8,128)(2,1)}, f16[256,2048]{1,0:T(8,128)(2,1)S(1)}) fusion(f16[512,4096]{1,0:T(8,128)(2,1)S(1)} %multiply_convert_fusion, s32[]{:T(128)S(6)} %select_n.65), kind=kLoop, calls=%fused_computation.79 | loop fusion | bytes 4194308 | tf_op jit(solution)/shard_map/dynamic_slice | solution.py:180
  48.7 2.2 %collective-permute-done.4 = f16[256,2048]{1,0:T(8,128)(2,1)S(1)} collective-permute-done((f16[256,2048]{1,0:T(8,128)(2,1)S(1)}, f16[256,2048]{1,0:T(8,128)(2,1)S(1)}, u32[]{:S(2)}, u32[]{:S(2)}) %collective-permute-start.4) | collective-permute-done | bytes 1048608 | tf_op jit(solution)/shard_map/ppermute | solution.py:15
  51.3 1.9 %fusion = f16[2,256,2048]{2,1,0:T(8,128)(2,1)} fusion(f32[1,256,2048]{2,1,0:T(8,128)S(1)} %multiply_bitcast_fusion, f32[1,256,2048]{2,1,0:T(8,128)S(1)} %multiply_bitcast_fusion.1), kind=kLoop, calls=%fused_computation.3 | loop fusion | flops 3145728 | bytes 6291456 | tf_op jit(solution)/shard_map/convert_element_type | solution.py:19
  53.9 15.2 %collective-permute-start.5 = (bf16[256,1280]{1,0:T(8,128)(2,1)S(1)}, bf16[256,1280]{1,0:T(8,128)(2,1)S(1)}, u32[]{:S(2)}, u32[]{:S(2)}) collective-permute-start(bf16[256,1280]{1,0:T(8,128)(2,1)S(1)} %bitcast.91), channel_id=1, source_target_pairs={{0,8},{1,12},{2,0},{3,4},{4,9},{5,13},{6,1},{7,5},{10,2},{11,6},{8... | collective-permute-start | bytes 1966088 | tf_op jit(solution)/shard_map/ppermute | solution.py:66
  69.1 19.6 %collective-permute-done.5 = bf16[256,1280]{1,0:T(8,128)(2,1)S(1)} collective-permute-done((bf16[256,1280]{1,0:T(8,128)(2,1)S(1)}, bf16[256,1280]{1,0:T(8,128)(2,1)S(1)}, u32[]{:S(2)}, u32[]{:S(2)}) %collective-permute-start.5) | collective-permute-done | bytes 655392 | tf_op jit(solution)/shard_map/ppermute | solution.py:66
  88.9 7.5 %shard_map.113 = f32[512,4096]{1,0:T(8,128)S(1)} custom-call(bf16[512,1280]{1,0:T(8,128)(2,1)S(1)} %pad_maximum_fusion.1.tokens_ref, bf16[4096,1280]{1,0:T(8,128)(2,1)S(1)} %bitcast.87), custom_call_target="tpu_custom_call" | custom-call | flops 1 | bytes 1 | tf_op jit(solution)/shard_map/pallas_call | solution.py:97
  97.4 2.0 %collective-permute-done.9 = f16[256,2048]{1,0:T(8,128)(2,1)S(1)} collective-permute-done((f16[256,2048]{1,0:T(8,128)(2,1)S(1)}, f16[256,2048]{1,0:T(8,128)(2,1)S(1)}, u32[]{:S(2)}, u32[]{:S(2)}) %collective-permute-start.9) | collective-permute-done | bytes 1048608 | tf_op jit(solution)/shard_map/ppermute | solution.py:15
  99.7 1.4 multiply_convert_fusion.3
  101.2 10.2 %collective-permute-start.15 = (f16[256,192]{0,1:T(8,128)(2,1)S(1)}, f16[256,192]{0,1:T(8,128)(2,1)S(1)}, u32[]{:S(2)}, u32[]{:S(2)}) collective-permute-start(f16[256,192]{0,1:T(8,128)(2,1)S(1)} %multiply_convert_fusion.7), channel_id=1, source_target_pairs={{0,12},{4,0},{8,4},{12,8},{1,13},{5,1},{9,5},{13,9},{2,14},{6,2},{... | collective-permute-start | bytes 294920 | tf_op jit(solution)/shard_map/ppermute | solution.py:15
  111.4 1.0 copy-done.6
  112.4 1.2 collective-permute-start.13
  113.9 0.7 collective-permute-done.15
  114.6 7.0 %collective-permute-done.14 = f16[256,192]{0,1:T(8,128)(2,1)} collective-permute-done((f16[256,192]{0,1:T(8,128)(2,1)S(1)}, f16[256,192]{0,1:T(8,128)(2,1)}, u32[]{:S(2)}, u32[]{:S(2)}) %collective-permute-start.14) | collective-permute-done | bytes 98336 | tf_op jit(solution)/shard_map/ppermute | solution.py:15
  121.7 12.1 %collective-permute-done.7 = f16[2,256,2048]{2,1,0:T(8,128)(2,1)} collective-permute-done((f16[2,256,2048]{2,1,0:T(8,128)(2,1)}, f16[2,256,2048]{2,1,0:T(8,128)(2,1)}, u32[]{:S(2)}, u32[]{:S(2)}) %collective-permute-start.7) | collective-permute-done | bytes 2097184 | tf_op jit(solution)/shard_map/ppermute | solution.py:15
  133.8 1.7 multiply_add_fusion.2
  135.4 1.1 copy.17
  136.6 2.8 %multiply_convert_fusion.5 = f16[256,2048]{1,0:T(8,128)(2,1)} fusion(f32[512,4096]{1,0:T(8,128)} %copy-done.1, s32[]{:T(128)S(6)} %select_n.65), kind=kLoop, calls=%fused_computation.16 | loop fusion | flops 1048576 | bytes 3145732 | tf_op jit(solution)/shard_map/convert_element_type | solution.py:19
  139.6 4.4 %fusion.3 = (f32[256,2048]{1,0:T(8,128)S(1)}, f32[256,2048]{1,0:T(8,128)S(1)}) fusion(f16[256,2048]{1,0:T(8,128)(2,1)} %copy-done.6, f16[2,256,2048]{2,1,0:T(8,128)(2,1)} %collective-permute-done.7, f16[512,4096]{1,0:T(8,128)(2,1)} %copy-done.5, s32[]{:T(128)S(6)} %select_n.62, f16[256,2048]{1,0:T(8,128)(2,1)} %collective-permute-done.11, ...), kind=kLoop, calls=%fused_computation.11 | loop fusion | flops 11010048 | bytes 10485764 | tf_op jit(solution)/shard_map/mul | solution.py:256
  144.1 2.6 %fusion.4 = f32[256,64]{0,1:T(8,128)S(1)} fusion(f32[256,2048]{1,0:T(8,128)S(1)} %get-tuple-element.24.refs_1_, f16[256,2048]{1,0:T(8,128)(2,1)} %collective-permute-done.11, f16[2,256,2048]{2,1,0:T(8,128)(2,1)} %collective-permute-done.7, f16[512,4096]{1,0:T(8,128)(2,1)} %copy-done.4, s32[]{:T(128)S(6)} %select_n.62, bf16[4096,192]{0,1:T(8,128)(2,1)} %param.16, ...), kind=kOutput, calls=%fused_computation.25 | convolution fusion | flops 71303168 | bytes 5572096 | tf_op jit(solution)/shard_map/dot_general | solution.py:259
  147.1 2.0 %multiply_add_fusion.1 = f32[256,2048]{1,0:T(8,128)S(1)} fusion(f16[256,2048]{1,0:T(8,128)(2,1)S(1)} %collective-permute-done.8, f32[512,4096]{1,0:T(8,128)} %copy-done.1, s32[]{:T(128)S(6)} %select_n.62), kind=kLoop, calls=%fused_computation.15 | loop fusion | flops 1572864 | bytes 5242884 | tf_op jit(solution)/shard_map/add | solution.py:188
  149.1 2.6 %collective-permute-done.10 = f16[256,2048]{1,0:T(8,128)(2,1)} collective-permute-done((f16[256,2048]{1,0:T(8,128)(2,1)}, f16[256,2048]{1,0:T(8,128)(2,1)}, u32[]{:S(2)}, u32[]{:S(2)}) %collective-permute-start.10) | collective-permute-done | bytes 1048608 | tf_op jit(solution)/shard_map/ppermute | solution.py:15
  151.7 1.6 multiply_add_fusion.down_ref
  153.3 1.2 shard_map.114
  154.6 3.8 %collective-permute-start.18 = (f32[6,16,64]{2,1,0:T(8,128)S(1)}, f32[6,16,64]{2,1,0:T(8,128)}, u32[]{:S(2)}, u32[]{:S(2)}) collective-permute-start(f32[6,16,64]{2,1,0:T(8,128)S(1)} %get-tuple-element.39), channel_id=1, source_target_pairs={{0,12},{4,0},{8,4},{12,8},{1,13},{5,1},{9,5},{13,9},{2,14},{6,2},{... | collective-permute-start | bytes 73736 | tf_op jit(solution)/shard_map/ppermute | solution.py:15
  158.4 2.6 %collective-permute-done.16 = f32[6,16,64]{2,1,0:T(8,128)} collective-permute-done((f32[6,16,64]{2,1,0:T(8,128)S(1)}, f32[6,16,64]{2,1,0:T(8,128)}, u32[]{:S(2)}, u32[]{:S(2)}) %collective-permute-start.16) | collective-permute-done | bytes 24608 | tf_op jit(solution)/shard_map/ppermute | solution.py:15
  161.1 2.5 %collective-permute-done.17 = f32[6,16,64]{2,1,0:T(8,128)} collective-permute-done((f32[6,16,64]{2,1,0:T(8,128)S(1)}, f32[6,16,64]{2,1,0:T(8,128)}, u32[]{:S(2)}, u32[]{:S(2)}) %collective-permute-start.17) | collective-permute-done | bytes 24608 | tf_op jit(solution)/shard_map/ppermute | solution.py:15
  163.5 0.9 fusion.15
  164.5 2.6 %collective-permute-start.20 = (f32[6,16,64]{2,1,0:T(8,128)S(1)}, f32[6,16,64]{2,1,0:T(8,128)S(1)}, u32[]{:S(2)}, u32[]{:S(2)}) collective-permute-start(f32[6,16,64]{2,1,0:T(8,128)S(1)} %fusion.15), channel_id=1, source_target_pairs={{0,3},{1,2},{2,1},{3,0},{4,7},{5,6},{6,5},{7,4},{8,11},{9,10},{10,... | collective-permute-start | bytes 73736 | tf_op jit(solution)/shard_map/ppermute | solution.py:279
  167.1 2.0 %collective-permute-done.20 = f32[6,16,64]{2,1,0:T(8,128)S(1)} collective-permute-done((f32[6,16,64]{2,1,0:T(8,128)S(1)}, f32[6,16,64]{2,1,0:T(8,128)S(1)}, u32[]{:S(2)}, u32[]{:S(2)}) %collective-permute-start.20) | collective-permute-done | bytes 24608 | tf_op jit(solution)/shard_map/ppermute | solution.py:279
  169.1 2.0 %collective-permute-done.19 = f32[6,16,64]{2,1,0:T(8,128)S(1)} collective-permute-done((f32[6,16,64]{2,1,0:T(8,128)S(1)}, f32[6,16,64]{2,1,0:T(8,128)S(1)}, u32[]{:S(2)}, u32[]{:S(2)}) %collective-permute-start.19) | collective-permute-done | bytes 24608 | tf_op jit(solution)/shard_map/ppermute | solution.py:279
  171.3 1.3 fusion.21
  172.7 1.9 %collective-permute-start.22 = (f32[4,512]{1,0:T(4,128)S(1)}, f32[4,512]{1,0:T(4,128)S(1)}, u32[]{:S(2)}, u32[]{:S(2)}) collective-permute-start(f32[4,512]{1,0:T(4,128)S(1)} %fusion.21), channel_id=1, source_target_pairs={{0,12},{4,0},{8,4},{12,8},{1,13},{5,1},{9,5},{13,9},{2,14},{6,2},{... | collective-permute-start | bytes 24584 | tf_op jit(solution)/shard_map/ppermute | solution.py:15
  175.3 1.0 collective-permute-done.22
  176.3 3.0 %collective-permute-done.23 = f32[4,512]{1,0:T(4,128)S(1)} collective-permute-done((f32[4,512]{1,0:T(4,128)S(1)}, f32[4,512]{1,0:T(4,128)S(1)}, u32[]{:S(2)}, u32[]{:S(2)}) %collective-permute-start.23) | collective-permute-done | bytes 8224 | tf_op jit(solution)/shard_map/ppermute | solution.py:15
  179.3 0.7 collective-permute-done.24
  180.8 0.9 fusion.16
  (94 shorter events, 7.1 us)
Async XLA Ops:
  0.6 170.7 %copy-start = (bf16[3,16,64,512]{3,2,1,0:T(8,128)(2,1)S(1)}, bf16[3,16,64,512]{3,2,1,0:T(8,128)(2,1)}, u32[]{:S(2)}) copy-start(bf16[3,16,64,512]{3,2,1,0:T(8,128)(2,1)} %param.17) | copy-start | bytes 9437188
  0.6 23.8 %collective-permute-start.1 = (bf16[256,1280]{1,0:T(8,128)(2,1)}, bf16[256,1280]{1,0:T(8,128)(2,1)}, u32[]{:S(2)}, u32[]{:S(2)}) collective-permute-start(bf16[256,1280]{1,0:T(8,128)(2,1)} %bitcast.92), channel_id=1, source_target_pairs={{0,0},{1,4},{2,8},{3,12},{4,1},{5,5},{6,9},{7,13},{10,10},{11,14},... | collective-permute-start | bytes 1966088 | tf_op jit(solution)/shard_map/ppermute | solution.py:66
  7.5 17.0 %collective-permute-start = (bf16[256,1280]{1,0:T(8,128)(2,1)}, bf16[256,1280]{1,0:T(8,128)(2,1)}, u32[]{:S(2)}, u32[]{:S(2)}) collective-permute-start(bf16[256,1280]{1,0:T(8,128)(2,1)} %bitcast.93), channel_id=1, source_target_pairs={{0,8},{1,12},{2,0},{3,4},{4,9},{5,13},{6,1},{7,5},{10,2},{11,6},{8... | collective-permute-start | bytes 1966088 | tf_op jit(solution)/shard_map/ppermute | solution.py:66
  8.2 16.3 %collective-permute-start.2 = (s32[2]{0:T(128)}, s32[2]{0:T(128)S(1)}, u32[]{:S(2)}, u32[]{:S(2)}) collective-permute-start(s32[2]{0:T(128)} %param.19), channel_id=1, source_target_pairs={{0,2},{2,0},{1,3},{3,1},{4,6},{6,4},{5,7},{7,5},{8,10},{10,8},{9,1... | collective-permute-start | bytes 32 | tf_op jit(solution)/shard_map/ppermute | solution.py:15
  9.5 14.9 %copy-start.8 = (s32[2]{0:T(128)S(1)}, s32[2]{0:T(128)}, u32[]{:S(2)}) copy-start(s32[2]{0:T(128)} %param.19) | copy-start | bytes 28
  25.9 14.6 %slice-start.3 = ((s8[10485760]{0:T(1024)(128)(4,1)}), s8[4194304]{0:T(1024)(128)(4,1)S(1)}, s32[]{:S(2)}) async-start(s8[10485760]{0:T(1024)(128)(4,1)} %bitcast.99), calls=%async_computation.3 | async-start | bytes 8388608
  26.0 14.5 %slice-start.4 = ((s8[10485760]{0:T(1024)(128)(4,1)}), s8[4194304]{0:T(1024)(128)(4,1)S(1)}, s32[]{:S(2)}) async-start(s8[10485760]{0:T(1024)(128)(4,1)} %bitcast.99), calls=%async_computation.4 | async-start | bytes 8388608
  26.0 14.5 %slice-start.5 = ((s8[10485760]{0:T(1024)(128)(4,1)}), s8[2097152]{0:T(1024)(128)(4,1)S(1)}, s32[]{:S(2)}) async-start(s8[10485760]{0:T(1024)(128)(4,1)} %bitcast.99), calls=%async_computation.5 | async-start | bytes 4194304
  36.4 11.8 %copy-start.5 = (f16[512,4096]{1,0:T(8,128)(2,1)}, f16[512,4096]{1,0:T(8,128)(2,1)S(1)}, u32[]{:S(2)}) copy-start(f16[512,4096]{1,0:T(8,128)(2,1)S(1)} %multiply_convert_fusion.1) | copy-start | bytes 12582916
  37.0 11.3 %collective-permute-start.3 = (f16[256,2048]{1,0:T(8,128)(2,1)S(1)}, f16[256,2048]{1,0:T(8,128)(2,1)S(1)}, u32[]{:S(2)}, u32[]{:S(2)}) collective-permute-start(f16[256,2048]{1,0:T(8,128)(2,1)S(1)} %get-tuple-element.27), channel_id=1, source_target_pairs={{0,1},{1,0},{2,3},{3,2},{4,5},{5,4},{6,7},{7,6},{8,9},{9,8},{10,11... | collective-permute-start | bytes 3145736 | tf_op jit(solution)/shard_map/ppermute | solution.py:15
  46.3 4.6 %copy-start.4 = (f16[512,4096]{1,0:T(8,128)(2,1)}, f16[512,4096]{1,0:T(8,128)(2,1)S(1)}, u32[]{:S(2)}) copy-start(f16[512,4096]{1,0:T(8,128)(2,1)S(1)} %multiply_convert_fusion) | copy-start | bytes 12582916
  48.2 2.7 %collective-permute-start.4 = (f16[256,2048]{1,0:T(8,128)(2,1)S(1)}, f16[256,2048]{1,0:T(8,128)(2,1)S(1)}, u32[]{:S(2)}, u32[]{:S(2)}) collective-permute-start(f16[256,2048]{1,0:T(8,128)(2,1)S(1)} %get-tuple-element.29), channel_id=1, source_target_pairs={{0,1},{1,0},{2,3},{3,2},{4,5},{5,4},{6,7},{7,6},{8,9},{9,8},{10,11... | collective-permute-start | bytes 3145736 | tf_op jit(solution)/shard_map/ppermute | solution.py:15
  48.3 40.6 %slice-start = ((s8[10485760]{0:T(1024)(128)(4,1)}), s8[4194304]{0:T(1024)(128)(4,1)S(1)}, s32[]{:S(2)}) async-start(s8[10485760]{0:T(1024)(128)(4,1)} %bitcast.86), calls=%async_computation | async-start | bytes 8388608
  48.6 40.3 %slice-start.1 = ((s8[10485760]{0:T(1024)(128)(4,1)}), s8[4194304]{0:T(1024)(128)(4,1)S(1)}, s32[]{:S(2)}) async-start(s8[10485760]{0:T(1024)(128)(4,1)} %bitcast.86), calls=%async_computation.1 | async-start | bytes 8388608
  51.2 1.9 %copy-start.7 = (bf16[2,128,1280]{2,1,0:T(8,128)(2,1)S(1)}, bf16[2,128,1280]{2,1,0:T(8,128)(2,1)}, u32[]{:S(2)}) copy-start(bf16[2,128,1280]{2,1,0:T(8,128)(2,1)} %param.11) | copy-start | bytes 1966084
  51.3 37.7 %slice-start.2 = ((s8[10485760]{0:T(1024)(128)(4,1)}), s8[2097152]{0:T(1024)(128)(4,1)S(1)}, s32[]{:S(2)}) async-start(s8[10485760]{0:T(1024)(128)(4,1)} %bitcast.86), calls=%async_computation.2 | async-start | bytes 4194304
  53.2 15.9 %collective-permute-start.6 = (bf16[256,1280]{1,0:T(8,128)(2,1)S(1)}, bf16[256,1280]{1,0:T(8,128)(2,1)S(1)}, u32[]{:S(2)}, u32[]{:S(2)}) collective-permute-start(bf16[256,1280]{1,0:T(8,128)(2,1)S(1)} %bitcast.90), channel_id=1, source_target_pairs={{0,0},{1,4},{2,8},{3,12},{4,1},{5,5},{6,9},{7,13},{10,10},{11,14},... | collective-permute-start | bytes 1966088 | tf_op jit(solution)/shard_map/ppermute | solution.py:66
  53.9 34.8 %collective-permute-start.5 = (bf16[256,1280]{1,0:T(8,128)(2,1)S(1)}, bf16[256,1280]{1,0:T(8,128)(2,1)S(1)}, u32[]{:S(2)}, u32[]{:S(2)}) collective-permute-start(bf16[256,1280]{1,0:T(8,128)(2,1)S(1)} %bitcast.91), channel_id=1, source_target_pairs={{0,8},{1,12},{2,0},{3,4},{4,9},{5,13},{6,1},{7,5},{10,2},{11,6},{8... | collective-permute-start | bytes 1966088 | tf_op jit(solution)/shard_map/ppermute | solution.py:66
  69.1 64.7 %collective-permute-start.7 = (f16[2,256,2048]{2,1,0:T(8,128)(2,1)}, f16[2,256,2048]{2,1,0:T(8,128)(2,1)}, u32[]{:S(2)}, u32[]{:S(2)}) collective-permute-start(f16[2,256,2048]{2,1,0:T(8,128)(2,1)} %fusion), channel_id=1, source_target_pairs={{0,2},{2,0},{1,3},{3,1},{4,6},{6,4},{5,7},{7,5},{8,10},{10,8},{9,1... | collective-permute-start | bytes 6291464 | tf_op jit(solution)/shard_map/ppermute | solution.py:15
  96.4 3.3 %copy-start.1 = (f32[512,4096]{1,0:T(8,128)}, f32[512,4096]{1,0:T(8,128)S(1)}, u32[]{:S(2)}) copy-start(f32[512,4096]{1,0:T(8,128)S(1)} %shard_map.113) | copy-start | bytes 25165828
  96.7 2.7 %collective-permute-start.9 = (f16[256,2048]{1,0:T(8,128)(2,1)S(1)}, f16[256,2048]{1,0:T(8,128)(2,1)S(1)}, u32[]{:S(2)}, u32[]{:S(2)}) collective-permute-start(f16[256,2048]{1,0:T(8,128)(2,1)S(1)} %multiply_convert_fusion.4), channel_id=1, source_target_pairs={{0,1},{1,0},{2,3},{3,2},{4,5},{5,4},{6,7},{7,6},{8,9},{9,8},{10,11... | collective-permute-start | bytes 3145736 | tf_op jit(solution)/shard_map/ppermute | solution.py:15
  96.8 14.6 %collective-permute-start.12 = (f16[256,2048]{1,0:T(8,128)(2,1)S(1)}, f16[256,2048]{1,0:T(8,128)(2,1)S(1)}, u32[]{:S(2)}, u32[]{:S(2)}) collective-permute-start(f16[256,2048]{1,0:T(8,128)(2,1)S(1)} %get-tuple-element.26), channel_id=1, source_target_pairs={{0,1},{1,0},{2,3},{3,2},{4,5},{5,4},{6,7},{7,6},{8,9},{9,8},{10,11... | collective-permute-start | bytes 3145736 | tf_op jit(solution)/shard_map/ppermute | solution.py:15
  97.3 16.5 %collective-permute-start.11 = (f16[256,2048]{1,0:T(8,128)(2,1)}, f16[256,2048]{1,0:T(8,128)(2,1)}, u32[]{:S(2)}, u32[]{:S(2)}) collective-permute-start(f16[256,2048]{1,0:T(8,128)(2,1)} %get-tuple-element.28), channel_id=1, source_target_pairs={{0,1},{1,0},{2,3},{3,2},{4,5},{5,4},{6,7},{7,6},{8,9},{9,8},{10,11... | collective-permute-start | bytes 3145736 | tf_op jit(solution)/shard_map/ppermute | solution.py:15
  97.4 16.3 %copy-start.9 = (s32[2]{0:T(128)S(1)}, s32[2]{0:T(128)}, u32[]{:S(2)}) copy-start(s32[2]{0:T(128)} %param.18) | copy-start | bytes 28
  101.2 13.4 %collective-permute-start.15 = (f16[256,192]{0,1:T(8,128)(2,1)S(1)}, f16[256,192]{0,1:T(8,128)(2,1)S(1)}, u32[]{:S(2)}, u32[]{:S(2)}) collective-permute-start(f16[256,192]{0,1:T(8,128)(2,1)S(1)} %multiply_convert_fusion.7), channel_id=1, source_target_pairs={{0,12},{4,0},{8,4},{12,8},{1,13},{5,1},{9,5},{13,9},{2,14},{6,2},{... | collective-permute-start | bytes 294920 | tf_op jit(solution)/shard_map/ppermute | solution.py:15
  111.4 10.3 %collective-permute-start.14 = (f16[256,192]{0,1:T(8,128)(2,1)S(1)}, f16[256,192]{0,1:T(8,128)(2,1)}, u32[]{:S(2)}, u32[]{:S(2)}) collective-permute-start(f16[256,192]{0,1:T(8,128)(2,1)S(1)} %multiply_convert_fusion.7), channel_id=1, source_target_pairs={{0,8},{4,12},{8,0},{12,4},{1,9},{5,13},{9,1},{13,5},{2,10},{6,14},... | collective-permute-start | bytes 294920 | tf_op jit(solution)/shard_map/ppermute | solution.py:15
  111.4 1.0 copy-start.6
  112.4 9.2 %collective-permute-start.13 = (f16[256,192]{0,1:T(8,128)(2,1)S(1)}, f16[256,192]{0,1:T(8,128)(2,1)}, u32[]{:S(2)}, u32[]{:S(2)}) collective-permute-start(f16[256,192]{0,1:T(8,128)(2,1)S(1)} %multiply_convert_fusion.7), channel_id=1, source_target_pairs={{0,4},{4,8},{8,12},{12,0},{1,5},{5,9},{9,13},{13,1},{2,6},{6,10},{... | collective-permute-start | bytes 294920 | tf_op jit(solution)/shard_map/ppermute | solution.py:15
  113.7 38.0 %collective-permute-start.10 = (f16[256,2048]{1,0:T(8,128)(2,1)}, f16[256,2048]{1,0:T(8,128)(2,1)}, u32[]{:S(2)}, u32[]{:S(2)}) collective-permute-start(f16[256,2048]{1,0:T(8,128)(2,1)} %multiply_convert_fusion.3), channel_id=1, source_target_pairs={{0,2},{2,0},{1,3},{3,1},{4,6},{6,4},{5,7},{7,5},{8,10},{10,8},{9,1... | collective-permute-start | bytes 3145736 | tf_op jit(solution)/shard_map/ppermute | solution.py:15
  139.6 7.5 %collective-permute-start.8 = (f16[256,2048]{1,0:T(8,128)(2,1)}, f16[256,2048]{1,0:T(8,128)(2,1)S(1)}, u32[]{:S(2)}, u32[]{:S(2)}) collective-permute-start(f16[256,2048]{1,0:T(8,128)(2,1)} %multiply_convert_fusion.5), channel_id=1, source_target_pairs={{0,1},{1,0},{2,3},{3,2},{4,5},{5,4},{6,7},{7,6},{8,9},{9,8},{10,11... | collective-permute-start | bytes 3145736 | tf_op jit(solution)/shard_map/ppermute | solution.py:15
  149.1 4.2 %copy-start.2 = (bf16[2048,64]{1,0:T(8,128)(2,1)S(1)}, bf16[2048,64]{1,0:T(8,128)(2,1)}, u32[]{:S(2)}) copy-start(bf16[2048,64]{1,0:T(8,128)(2,1)} %copy.22.refs_3_) | copy-start | bytes 786436
  149.1 4.2 %copy-start.3 = (bf16[2048,64]{1,0:T(8,128)(2,1)S(1)}, bf16[2048,64]{1,0:T(8,128)(2,1)}, u32[]{:S(2)}) copy-start(bf16[2048,64]{1,0:T(8,128)(2,1)} %copy.21.refs_2_) | copy-start | bytes 786436
  154.6 6.5 %collective-permute-start.16 = (f32[6,16,64]{2,1,0:T(8,128)S(1)}, f32[6,16,64]{2,1,0:T(8,128)}, u32[]{:S(2)}, u32[]{:S(2)}) collective-permute-start(f32[6,16,64]{2,1,0:T(8,128)S(1)} %get-tuple-element.38), channel_id=1, source_target_pairs={{0,4},{4,8},{8,12},{12,0},{1,5},{5,9},{9,13},{13,1},{2,6},{6,10},{... | collective-permute-start | bytes 73736 | tf_op jit(solution)/shard_map/ppermute | solution.py:15
  154.6 6.5 %collective-permute-start.18 = (f32[6,16,64]{2,1,0:T(8,128)S(1)}, f32[6,16,64]{2,1,0:T(8,128)}, u32[]{:S(2)}, u32[]{:S(2)}) collective-permute-start(f32[6,16,64]{2,1,0:T(8,128)S(1)} %get-tuple-element.39), channel_id=1, source_target_pairs={{0,12},{4,0},{8,4},{12,8},{1,13},{5,1},{9,5},{13,9},{2,14},{6,2},{... | collective-permute-start | bytes 73736 | tf_op jit(solution)/shard_map/ppermute | solution.py:15
  158.4 5.1 %collective-permute-start.17 = (f32[6,16,64]{2,1,0:T(8,128)S(1)}, f32[6,16,64]{2,1,0:T(8,128)}, u32[]{:S(2)}, u32[]{:S(2)}) collective-permute-start(f32[6,16,64]{2,1,0:T(8,128)S(1)} %get-tuple-element.40), channel_id=1, source_target_pairs={{0,8},{4,12},{8,0},{12,4},{1,9},{5,13},{9,1},{13,5},{2,10},{6,14},... | collective-permute-start | bytes 73736 | tf_op jit(solution)/shard_map/ppermute | solution.py:15
  164.4 2.7 %collective-permute-start.21 = (f32[6,16,64]{2,1,0:T(8,128)S(1)}, f32[6,16,64]{2,1,0:T(8,128)S(1)}, u32[]{:S(2)}, u32[]{:S(2)}) collective-permute-start(f32[6,16,64]{2,1,0:T(8,128)S(1)} %fusion.15), channel_id=1, source_target_pairs={{0,1},{1,0},{2,3},{3,2},{4,5},{5,4},{6,7},{7,6},{8,9},{9,8},{10,11... | collective-permute-start | bytes 73736 | tf_op jit(solution)/shard_map/ppermute | solution.py:279
  164.5 4.7 %collective-permute-start.20 = (f32[6,16,64]{2,1,0:T(8,128)S(1)}, f32[6,16,64]{2,1,0:T(8,128)S(1)}, u32[]{:S(2)}, u32[]{:S(2)}) collective-permute-start(f32[6,16,64]{2,1,0:T(8,128)S(1)} %fusion.15), channel_id=1, source_target_pairs={{0,3},{1,2},{2,1},{3,0},{4,7},{5,6},{6,5},{7,4},{8,11},{9,10},{10,... | collective-permute-start | bytes 73736 | tf_op jit(solution)/shard_map/ppermute | solution.py:279
  167.1 4.1 %collective-permute-start.19 = (f32[6,16,64]{2,1,0:T(8,128)S(1)}, f32[6,16,64]{2,1,0:T(8,128)S(1)}, u32[]{:S(2)}, u32[]{:S(2)}) collective-permute-start(f32[6,16,64]{2,1,0:T(8,128)S(1)} %fusion.15), channel_id=1, source_target_pairs={{0,2},{1,3},{2,0},{3,1},{4,6},{5,7},{6,4},{7,5},{8,10},{9,11},{10,... | collective-permute-start | bytes 73736 | tf_op jit(solution)/shard_map/ppermute | solution.py:279
  172.7 3.7 %collective-permute-start.22 = (f32[4,512]{1,0:T(4,128)S(1)}, f32[4,512]{1,0:T(4,128)S(1)}, u32[]{:S(2)}, u32[]{:S(2)}) collective-permute-start(f32[4,512]{1,0:T(4,128)S(1)} %fusion.21), channel_id=1, source_target_pairs={{0,12},{4,0},{8,4},{12,8},{1,13},{5,1},{9,5},{13,9},{2,14},{6,2},{... | collective-permute-start | bytes 24584 | tf_op jit(solution)/shard_map/ppermute | solution.py:15
  174.6 5.4 %collective-permute-start.24 = (f32[4,512]{1,0:T(4,128)S(1)}, f32[4,512]{1,0:T(4,128)S(1)}, u32[]{:S(2)}, u32[]{:S(2)}) collective-permute-start(f32[4,512]{1,0:T(4,128)S(1)} %fusion.21), channel_id=1, source_target_pairs={{0,4},{4,8},{8,12},{12,0},{1,5},{5,9},{9,13},{13,1},{2,6},{6,10},{... | collective-permute-start | bytes 24584 | tf_op jit(solution)/shard_map/ppermute | solution.py:15
  174.8 4.5 %collective-permute-start.23 = (f32[4,512]{1,0:T(4,128)S(1)}, f32[4,512]{1,0:T(4,128)S(1)}, u32[]{:S(2)}, u32[]{:S(2)}) collective-permute-start(f32[4,512]{1,0:T(4,128)S(1)} %fusion.21), channel_id=1, source_target_pairs={{0,8},{4,12},{8,0},{12,4},{1,9},{5,13},{9,1},{13,5},{2,10},{6,14},... | collective-permute-start | bytes 24584 | tf_op jit(solution)/shard_map/ppermute | solution.py:15

commit v15 on v9

--- a/solution.py
+++ b/solution.py
@@ -191,7 +191,8 @@
     projs = [hid_proj[:, layer * width : (layer + 1) * width] for layer in range(3)]
     positions = jnp.arange(seq_len, dtype=jnp.int32)
     token_mask = (positions[None, :] < lengths[:, None]).astype(F32)
-    early = (model_acts, model_grad, token_mask, *projs)
+    all_groups = gather_in_order(groups, "example")
+    early = (all_groups, model_acts, model_grad, token_mask, *projs)
 
     direct = (n_z, n_ex, n_cores) == (4, 2, 2)
     examples = [slice(e * seq_len, (e + 1) * seq_len) for e in range(ex_loc)]
@@ -246,7 +247,7 @@
     gate_act, up_act = [
         kept + sum(unpack(one[which]) for one in arrived) for which, kept in enumerate(own[:2])
     ]
-    d_hidden = own[2] + sum(unpack(one) for one in arrived_down)
+    d_hidden = lax.optimization_barrier(own[2]) + sum(unpack(one) for one in arrived_down)
     sigmoid_gate = jax.nn.sigmoid(gate_act)
     silu_gate = gate_act * sigmoid_gate
     hidden = (silu_gate * up_act).astype(jnp.bfloat16)
@@ -283,7 +284,6 @@
     )
     all_scores = jnp.sum(gather_in_order(partial_scores, "tensor"), 0)
     scores = lax.dynamic_slice_in_dim(all_scores, ex_index * ex_loc, ex_loc, 0)
-    all_groups = gather_in_order(groups, "example")
     group_onehot = (
         all_groups.reshape(-1)[:, None] == jnp.arange(NGROUP, dtype=jnp.int32)[None, :]
     ).astype(F32)

time: 178 us -> 178 us (level)
  starting transfers between devices: 74 us -> 65.7 us
  waiting for transfers between devices: 34.2 us -> 40.3 us
  local copies, waits for them, and re-layouts: 7.95 us -> 9.84 us
    ppermute x18, waiting for transfers between devices: 20.3 us -> 37.2 us  [shift(): return lax.ppermute(value, axis, [(i, (i + step) % n) for i in range(n)])]
    ppermute x18, starting transfers between devices: 33.8 us -> 21.8 us  [shift(): return lax.ppermute(value, axis, [(i, (i + step) % n) for i in range(n)])]
    ppermute x8, waiting for transfers between devices: 10.3 us -> 0.02 us  [spread_features(): pieces.append(lax.ppermute(flat, ('tensor', 'example', 'test'), pairs))]
    ppermute x8, starting transfers between devices: 38.8 us -> 42 us  [spread_features(): pieces.append(lax.ppermute(flat, ('tensor', 'example', 'test'), pairs))]
    unnamed x41, local copies, waits for them, and re-layouts: 4.16 us -> 6.04 us
    add x1 -> x2, other arithmetic: 2.46 us -> 3.62 us  [the longest x1 1.96 us: core_sum(): kept = kept + unpack(after(shift(sent, 'test', step), *earlier))]
  transfers between devices with their start and end apart: 29 -> 29, of which waited for: 14 -> 11; matrix products, arithmetic and copies ran while one was open for 29% -> 29% of each run, Pallas kernels for 4% -> 4%
where the time goes in v15:
time: 178 us; the launch traced here: 177 us
  starting transfers between devices  65.7 us (37%)
  waiting for transfers between devices  40.3 us (23%)
  matrix products  28.6 us (16%)
  other arithmetic  22.1 us (12%)
  local copies, waits for them, and re-layouts  9.84 us (6%)
  Pallas kernels  8.75 us (5%)
    ppermute x8, starting transfers between devices, spread_features(): pieces.append(lax.ppermute(flat, ('tensor', 'example', 'test'), pairs))  42 us
    ppermute x18, waiting for transfers between devices, shift(): return lax.ppermute(value, axis, [(i, (i + step) % n) for i in range(n)])  37.2 us
    ppermute x18, starting transfers between devices, shift(): return lax.ppermute(value, axis, [(i, (i + step) % n) for i in range(n)])  21.8 us
    dot_general x4, matrix products, forward(): return jnp.dot(tokens, weight, preferred_element_type=F32)  20.7 us
    pallas_call x1, Pallas kernels, dot_rows(): pl.pallas_call(dot_rows_kernel, out_shape=jax.ShapeDtypeStruct((rows, hid...  7.49 us
    convert_element_type x9, other arithmetic, pack(): return (value * SEND_SCALE).astype(jnp.float16)  7.15 us
    unnamed x41, local copies, waits for them, and re-layouts  6.04 us
    mul x1, other arithmetic, on_device(): silu_gate = gate_act * sigmoid_gate  5 us
  transfers between devices with their start and end apart: 29, of which 11 were waited for; matrix products, arithmetic and copies ran while one was open for 29% of the time, Pallas kernels for 4%

profile of v15, /device:TPU:0, one launch (start us, length us, event | category | flops | bytes accessed | tf_op | source)
XLA Modules:
  0.0 176.7 jit_solution(17493479302370243632)
XLA Ops:
  0.6 1.6 collective-permute-start
  2.2 1.5 collective-permute-start.1
  3.7 6.5 %collective-permute-start.6 = (bf16[256,1280]{1,0:T(8,128)(2,1)}, bf16[256,1280]{1,0:T(8,128)(2,1)}, u32[]{:S(2)}, u32[]{:S(2)}) collective-permute-start(bf16[256,1280]{1,0:T(8,128)(2,1)} %bitcast.99), channel_id=1, source_target_pairs={{0,0},{1,4},{4,1},{5,5},{10,10},{11,14},{14,11},{15,15},{16,16},{1... | collective-permute-start | bytes 1966088 | tf_op jit(solution)/shard_map/ppermute | solution.py:65
  10.2 5.1 %collective-permute-start.7 = (bf16[256,1280]{1,0:T(8,128)(2,1)}, bf16[256,1280]{1,0:T(8,128)(2,1)}, u32[]{:S(2)}, u32[]{:S(2)}) collective-permute-start(bf16[256,1280]{1,0:T(8,128)(2,1)} %bitcast.100), channel_id=1, source_target_pairs={{0,8},{1,12},{4,9},{5,13},{10,2},{11,6},{14,3},{15,7},{16,24},{17,... | collective-permute-start | bytes 1966088 | tf_op jit(solution)/shard_map/ppermute | solution.py:65
  15.5 1.8 %fusion.17 = (bf16[2048,64]{0,1:T(8,128)(2,1)S(1)}, bf16[2048,64]{0,1:T(8,128)(2,1)}) fusion(bf16[4096,192]{0,1:T(8,128)(2,1)} %param.16, s32[]{:T(128)S(6)} %select_n.62, s32[]{:T(128)S(6)} %add.160), kind=kLoop, calls=%fused_computation.75 | loop fusion | bytes 1048584 | tf_op jit(solution)/shard_map/slice | solution.py:191
  17.2 2.0 %copy.21.refs_2_ = bf16[2048,64]{1,0:T(8,128)(2,1)} copy(bf16[2048,64]{0,1:T(8,128)(2,1)} %get-tuple-element.43) | data formatting | bytes 524288
  19.2 1.0 copy.22.refs_3_
  20.2 1.4 fusion.6
  21.6 1.6 fusion.3
  23.3 1.3 broadcast_select_fusion.3
  24.6 5.7 %fusion.18 = f32[256,4096]{1,0:T(8,128)S(1)} fusion(bf16[256,1280]{1,0:T(8,128)(2,1)S(1)} %broadcast_select_fusion.3, bf16[1280,4096]{1,0:T(8,128)(2,1)} %param.12), kind=kOutput, calls=%fused_computation.76 | convolution fusion | flops 2684354560 | bytes 15335424 | tf_op jit(solution)/shard_map/dot_general | solution.py:172
  30.8 2.9 %fusion.19 = f32[256,4096]{1,0:T(8,128)S(1)} fusion(bf16[256,1280]{1,0:T(8,128)(2,1)S(1)} %broadcast_select_fusion.3, bf16[1280,4096]{1,0:T(8,128)(2,1)S(1)} %bitcast.107), kind=kOutput, calls=%fused_computation.77 | convolution fusion | flops 2684354560 | bytes 15335424 | tf_op jit(solution)/shard_map/dot_general | solution.py:172
  33.7 1.3 collective-permute-start.3
  35.7 24.6 %collective-permute-start.10 = (bf16[256,1280]{1,0:T(8,128)(2,1)S(1)}, bf16[256,1280]{1,0:T(8,128)(2,1)S(1)}, u32[]{:S(2)}, u32[]{:S(2)}) collective-permute-start(bf16[256,1280]{1,0:T(8,128)(2,1)S(1)} %bitcast.95), channel_id=1, source_target_pairs={{0,8},{1,12},{4,9},{5,13},{10,2},{11,6},{14,3},{15,7},{16,24},{17,... | collective-permute-start | bytes 1966088 | tf_op jit(solution)/shard_map/ppermute | solution.py:65
  60.7 1.2 broadcast_select_fusion.2
  62.0 5.6 %fusion.20 = f32[256,4096]{1,0:T(8,128)S(1)} fusion(bf16[256,1280]{1,0:T(8,128)(2,1)S(1)} %broadcast_select_fusion.2, bf16[1280,4096]{1,0:T(8,128)(2,1)} %param.12), kind=kOutput, calls=%fused_computation.78 | convolution fusion | flops 2684354560 | bytes 15335424 | tf_op jit(solution)/shard_map/dot_general | solution.py:172
  68.1 6.5 %fusion.21 = f32[256,4096]{1,0:T(8,128)S(1)} fusion(bf16[256,1280]{1,0:T(8,128)(2,1)S(1)} %broadcast_select_fusion.2, bf16[1280,4096]{1,0:T(8,128)(2,1)} %param.13), kind=kOutput, calls=%fused_computation.79 | convolution fusion | flops 2684354560 | bytes 15335424 | tf_op jit(solution)/shard_map/dot_general | solution.py:172
  76.3 1.9 %fusion = f16[2,256,2048]{2,1,0:T(8,128)(2,1)} fusion(f32[1,256,2048]{2,1,0:T(8,128)S(1)} %add_bitcast_fusion, f32[1,256,2048]{2,1,0:T(8,128)S(1)} %add_bitcast_fusion.1), kind=kLoop, calls=%fused_computation.1 | loop fusion | flops 3145728 | bytes 6291456 | tf_op jit(solution)/shard_map/convert_element_type | solution.py:19
  79.1 1.3 slice-done.1
  81.0 7.5 %shard_map.113 = f32[512,4096]{1,0:T(8,128)S(1)} custom-call(bf16[512,1280]{1,0:T(8,128)(2,1)S(1)} %pad_maximum_fusion.tokens_ref, bf16[4096,1280]{1,0:T(8,128)(2,1)S(1)} %bitcast.90), custom_call_target="tpu_custom_call" | custom-call | flops 1 | bytes 1 | tf_op jit(solution)/shard_map/pallas_call | solution.py:95
  88.7 7.5 %collective-permute-start.13 = (f16[256,2048]{1,0:T(8,128)(2,1)S(1)}, f16[256,2048]{1,0:T(8,128)(2,1)S(1)}, u32[]{:S(2)}, u32[]{:S(2)}) collective-permute-start(f16[256,2048]{1,0:T(8,128)(2,1)S(1)} %multiply_convert_fusion.4), channel_id=1, source_target_pairs={{0,1},{1,0},{2,3},{3,2},{4,5},{5,4},{6,7},{7,6},{8,9},{9,8},{10,11... | collective-permute-start | bytes 3145736 | tf_op jit(solution)/shard_map/ppermute | solution.py:15
  96.5 1.2 multiply_convert_fusion.1
  97.7 0.9 collective-permute-start.16
  98.7 1.4 multiply_convert_fusion.3
  100.2 3.7 %collective-permute-start.19 = (f16[256,192]{0,1:T(8,128)(2,1)S(1)}, f16[256,192]{0,1:T(8,128)(2,1)}, u32[]{:S(2)}, u32[]{:S(2)}) collective-permute-start(f16[256,192]{0,1:T(8,128)(2,1)S(1)} %multiply_convert_fusion.9), channel_id=1, source_target_pairs={{0,12},{4,0},{8,4},{12,8},{1,13},{5,1},{9,5},{13,9},{2,14},{6,2},{... | collective-permute-start | bytes 294920 | tf_op jit(solution)/shard_map/ppermute | solution.py:15
  104.0 3.7 %collective-permute-done.17 = f16[256,192]{0,1:T(8,128)(2,1)S(1)} collective-permute-done((f16[256,192]{0,1:T(8,128)(2,1)S(1)}, f16[256,192]{0,1:T(8,128)(2,1)S(1)}, u32[]{:S(2)}, u32[]{:S(2)}) %collective-permute-start.17) | collective-permute-done | bytes 98336 | tf_op jit(solution)/shard_map/ppermute | solution.py:15
  107.7 3.5 %collective-permute-done.18 = f16[256,192]{0,1:T(8,128)(2,1)} collective-permute-done((f16[256,192]{0,1:T(8,128)(2,1)S(1)}, f16[256,192]{0,1:T(8,128)(2,1)}, u32[]{:S(2)}, u32[]{:S(2)}) %collective-permute-start.18) | collective-permute-done | bytes 98336 | tf_op jit(solution)/shard_map/ppermute | solution.py:15
  111.2 15.1 %collective-permute-done.11 = f16[2,256,2048]{2,1,0:T(8,128)(2,1)} collective-permute-done((f16[2,256,2048]{2,1,0:T(8,128)(2,1)}, f16[2,256,2048]{2,1,0:T(8,128)(2,1)}, u32[]{:S(2)}, u32[]{:S(2)}) %collective-permute-start.11) | collective-permute-done | bytes 2097184 | tf_op jit(solution)/shard_map/ppermute | solution.py:15
  126.3 1.7 multiply_add_fusion.2
  127.9 1.1 copy.17
  129.3 1.8 %multiply_convert_fusion.5 = f16[256,2048]{1,0:T(8,128)(2,1)S(1)} fusion(f32[512,4096]{1,0:T(8,128)} %copy-done.1, s32[]{:T(128)S(6)} %select_n.64), kind=kLoop, calls=%fused_computation.14 | loop fusion | flops 1048576 | bytes 3145732 | tf_op jit(solution)/shard_map/convert_element_type | solution.py:19
  131.1 1.7 collective-permute-start.12
  132.8 5.0 %fusion.1 = (f32[256,2048]{1,0:T(8,128)S(1)}, f32[256,2048]{1,0:T(8,128)S(1)}) fusion(f16[2,256,2048]{2,1,0:T(8,128)(2,1)} %collective-permute-done.11, f16[256,2048]{1,0:T(8,128)(2,1)} %collective-permute-done.16, f32[256,4096]{1,0:T(8,128)} %copy-done.6, s32[]{:T(128)S(6)} %select_n.62, f16[256,2048]{1,0:T(8,128)(2,1)} %collective-permute-done.15, ...), kind=kLoop, calls=%fused_computation.7 | loop fusion | flops 11010048 | bytes 12582916 | tf_op jit(solution)/shard_map/mul | solution.py:252
  137.8 2.4 %fusion.2 = f32[256,64]{0,1:T(8,128)S(1)} fusion(f32[256,2048]{1,0:T(8,128)S(1)} %get-tuple-element.40.refs_1_, f16[256,2048]{1,0:T(8,128)(2,1)} %collective-permute-done.15, f32[256,4096]{1,0:T(8,128)S(1)} %copy-done.5, s32[]{:T(128)S(6)} %select_n.62, f16[2,256,2048]{2,1,0:T(8,128)(2,1)} %collective-permute-done.11, bf16[4096,192]{0,1:T(8,128)(2,1)} %param.16, ...), kind=kOutput, calls=%fused_computation.22 | convolution fusion | flops 71303168 | bytes 6620672 | tf_op jit(solution)/shard_map/dot_general | solution.py:255
  140.6 2.0 %multiply_add_fusion.1 = f32[256,2048]{1,0:T(8,128)S(1)} fusion(f16[256,2048]{1,0:T(8,128)(2,1)S(1)} %collective-permute-done.12, f32[512,4096]{1,0:T(8,128)} %copy-done.1, s32[]{:T(128)S(6)} %select_n.62), kind=kLoop, calls=%fused_computation.13 | loop fusion | flops 1572864 | bytes 5242884 | tf_op jit(solution)/shard_map/add | solution.py:181
  142.6 6.1 %collective-permute-done.14 = f16[256,2048]{1,0:T(8,128)(2,1)} collective-permute-done((f16[256,2048]{1,0:T(8,128)(2,1)}, f16[256,2048]{1,0:T(8,128)(2,1)}, u32[]{:S(2)}, u32[]{:S(2)}) %collective-permute-start.14) | collective-permute-done | bytes 1048608 | tf_op jit(solution)/shard_map/ppermute | solution.py:15
  148.7 1.7 multiply_add_fusion.down_ref
  150.4 1.3 shard_map.114
  151.8 2.1 %collective-permute-start.21 = (f32[6,16,64]{2,1,0:T(8,128)S(1)}, f32[6,16,64]{2,1,0:T(8,128)}, u32[]{:S(2)}, u32[]{:S(2)}) collective-permute-start(f32[6,16,64]{2,1,0:T(8,128)S(1)} %get-tuple-element.48), channel_id=1, source_target_pairs={{0,8},{4,12},{8,0},{12,4},{1,9},{5,13},{9,1},{13,5},{2,10},{6,14},... | collective-permute-start | bytes 73736 | tf_op jit(solution)/shard_map/ppermute | solution.py:15
  153.9 1.7 collective-permute-start.22
  155.6 2.7 %collective-permute-done.20 = f32[6,16,64]{2,1,0:T(8,128)} collective-permute-done((f32[6,16,64]{2,1,0:T(8,128)S(1)}, f32[6,16,64]{2,1,0:T(8,128)}, u32[]{:S(2)}, u32[]{:S(2)}) %collective-permute-start.20) | collective-permute-done | bytes 24608 | tf_op jit(solution)/shard_map/ppermute | solution.py:15
  160.1 1.3 collective-permute-start.23
  162.0 2.3 %collective-permute-done.23 = f32[6,16,64]{2,1,0:T(8,128)S(1)} collective-permute-done((f32[6,16,64]{2,1,0:T(8,128)S(1)}, f32[6,16,64]{2,1,0:T(8,128)S(1)}, u32[]{:S(2)}, u32[]{:S(2)}) %collective-permute-start.23) | collective-permute-done | bytes 24608 | tf_op jit(solution)/shard_map/ppermute | solution.py:275
  165.3 1.3 fusion.22
  166.6 2.6 %collective-permute-start.26 = (f32[4,512]{1,0:T(4,128)S(1)}, f32[4,512]{1,0:T(4,128)S(1)}, u32[]{:S(2)}, u32[]{:S(2)}) collective-permute-start(f32[4,512]{1,0:T(4,128)S(1)} %fusion.22), channel_id=1, source_target_pairs={{0,12},{4,0},{8,4},{12,8},{1,13},{5,1},{9,5},{13,9},{2,14},{6,2},{... | collective-permute-start | bytes 24584 | tf_op jit(solution)/shard_map/ppermute | solution.py:15
  170.5 3.3 %collective-permute-done.27 = f32[4,512]{1,0:T(4,128)S(1)} collective-permute-done((f32[4,512]{1,0:T(4,128)S(1)}, f32[4,512]{1,0:T(4,128)S(1)}, u32[]{:S(2)}, u32[]{:S(2)}) %collective-permute-start.27) | collective-permute-done | bytes 8224 | tf_op jit(solution)/shard_map/ppermute | solution.py:15
  173.8 1.3 collective-permute-done.28
  175.2 0.9 fusion.14
  (106 shorter events, 12.3 us)
Async XLA Ops:
  0.6 164.6 %copy-start = (bf16[3,16,64,512]{3,2,1,0:T(8,128)(2,1)S(1)}, bf16[3,16,64,512]{3,2,1,0:T(8,128)(2,1)}, u32[]{:S(2)}) copy-start(bf16[3,16,64,512]{3,2,1,0:T(8,128)(2,1)} %param.17) | copy-start | bytes 9437188
  0.6 22.6 %collective-permute-start = (bf16[256,1280]{1,0:T(8,128)(2,1)}, bf16[256,1280]{1,0:T(8,128)(2,1)}, u32[]{:S(2)}, u32[]{:S(2)}) collective-permute-start(bf16[256,1280]{1,0:T(8,128)(2,1)} %bitcast.97), channel_id=1, source_target_pairs={{2,0},{3,4},{6,1},{7,5},{8,10},{9,14},{12,11},{13,15},{18,16},{19,... | collective-permute-start | bytes 1966088 | tf_op jit(solution)/shard_map/ppermute | solution.py:65
  2.2 21.1 %collective-permute-start.1 = (bf16[256,1280]{1,0:T(8,128)(2,1)}, bf16[256,1280]{1,0:T(8,128)(2,1)}, u32[]{:S(2)}, u32[]{:S(2)}) collective-permute-start(bf16[256,1280]{1,0:T(8,128)(2,1)} %bitcast.98), channel_id=1, source_target_pairs={{2,8},{3,12},{6,9},{7,13},{8,2},{9,6},{12,3},{13,7},{18,24},{19,28... | collective-permute-start | bytes 1966088 | tf_op jit(solution)/shard_map/ppermute | solution.py:65
  3.7 57.0 %collective-permute-start.6 = (bf16[256,1280]{1,0:T(8,128)(2,1)}, bf16[256,1280]{1,0:T(8,128)(2,1)}, u32[]{:S(2)}, u32[]{:S(2)}) collective-permute-start(bf16[256,1280]{1,0:T(8,128)(2,1)} %bitcast.99), channel_id=1, source_target_pairs={{0,0},{1,4},{4,1},{5,5},{10,10},{11,14},{14,11},{15,15},{16,16},{1... | collective-permute-start | bytes 1966088 | tf_op jit(solution)/shard_map/ppermute | solution.py:65
  10.2 50.5 %collective-permute-start.7 = (bf16[256,1280]{1,0:T(8,128)(2,1)}, bf16[256,1280]{1,0:T(8,128)(2,1)}, u32[]{:S(2)}, u32[]{:S(2)}) collective-permute-start(bf16[256,1280]{1,0:T(8,128)(2,1)} %bitcast.100), channel_id=1, source_target_pairs={{0,8},{1,12},{4,9},{5,13},{10,2},{11,6},{14,3},{15,7},{16,24},{17,... | collective-permute-start | bytes 1966088 | tf_op jit(solution)/shard_map/ppermute | solution.py:65
  15.4 7.8 %collective-permute-start.2 = (s32[2]{0:T(128)}, s32[2]{0:T(128)S(1)}, u32[]{:S(2)}, u32[]{:S(2)}) collective-permute-start(s32[2]{0:T(128)} %param.19), channel_id=1, source_target_pairs={{0,2},{2,0},{1,3},{3,1},{4,6},{6,4},{5,7},{7,5},{8,10},{10,8},{9,1... | collective-permute-start | bytes 32 | tf_op jit(solution)/shard_map/ppermute | solution.py:15
  15.5 7.7 %copy-start.8 = (s32[2]{0:T(128)S(1)}, s32[2]{0:T(128)}, u32[]{:S(2)}) copy-start(s32[2]{0:T(128)} %param.19) | copy-start | bytes 28
  23.3 7.1 %slice-start.3 = ((s8[10485760]{0:T(1024)(128)(4,1)}), s8[4194304]{0:T(1024)(128)(4,1)S(1)}, s32[]{:S(2)}) async-start(s8[10485760]{0:T(1024)(128)(4,1)} %bitcast.106), calls=%async_computation.3 | async-start | bytes 8388608
  24.6 5.8 %slice-start.4 = ((s8[10485760]{0:T(1024)(128)(4,1)}), s8[4194304]{0:T(1024)(128)(4,1)S(1)}, s32[]{:S(2)}) async-start(s8[10485760]{0:T(1024)(128)(4,1)} %bitcast.106), calls=%async_computation.4 | async-start | bytes 8388608
  24.6 6.2 %slice-start.5 = ((s8[10485760]{0:T(1024)(128)(4,1)}), s8[2097152]{0:T(1024)(128)(4,1)S(1)}, s32[]{:S(2)}) async-start(s8[10485760]{0:T(1024)(128)(4,1)} %bitcast.106), calls=%async_computation.5 | async-start | bytes 4194304
  30.8 2.9 %copy-start.7 = (bf16[2,128,1280]{2,1,0:T(8,128)(2,1)S(1)}, bf16[2,128,1280]{2,1,0:T(8,128)(2,1)}, u32[]{:S(2)}) copy-start(bf16[2,128,1280]{2,1,0:T(8,128)(2,1)} %param.11) | copy-start | bytes 1966084
  33.7 44.5 %collective-permute-start.3 = (bf16[256,1280]{1,0:T(8,128)(2,1)S(1)}, bf16[256,1280]{1,0:T(8,128)(2,1)S(1)}, u32[]{:S(2)}, u32[]{:S(2)}) collective-permute-start(bf16[256,1280]{1,0:T(8,128)(2,1)S(1)} %bitcast.93), channel_id=1, source_target_pairs={{2,0},{3,4},{6,1},{7,5},{8,10},{9,14},{12,11},{13,15},{18,16},{19,... | collective-permute-start | bytes 1966088 | tf_op jit(solution)/shard_map/ppermute | solution.py:65
  35.0 43.2 %collective-permute-start.4 = (bf16[256,1280]{1,0:T(8,128)(2,1)S(1)}, bf16[256,1280]{1,0:T(8,128)(2,1)S(1)}, u32[]{:S(2)}, u32[]{:S(2)}) collective-permute-start(bf16[256,1280]{1,0:T(8,128)(2,1)S(1)} %bitcast.94), channel_id=1, source_target_pairs={{2,8},{3,12},{6,9},{7,13},{8,2},{9,6},{12,3},{13,7},{18,24},{19,28... | collective-permute-start | bytes 1966088 | tf_op jit(solution)/shard_map/ppermute | solution.py:65
  35.7 42.5 %collective-permute-start.10 = (bf16[256,1280]{1,0:T(8,128)(2,1)S(1)}, bf16[256,1280]{1,0:T(8,128)(2,1)S(1)}, u32[]{:S(2)}, u32[]{:S(2)}) collective-permute-start(bf16[256,1280]{1,0:T(8,128)(2,1)S(1)} %bitcast.95), channel_id=1, source_target_pairs={{0,8},{1,12},{4,9},{5,13},{10,2},{11,6},{14,3},{15,7},{16,24},{17,... | collective-permute-start | bytes 1966088 | tf_op jit(solution)/shard_map/ppermute | solution.py:65
  61.9 12.8 %collective-permute-start.5 = (f16[256,2048]{1,0:T(8,128)(2,1)S(1)}, f16[256,2048]{1,0:T(8,128)(2,1)S(1)}, u32[]{:S(2)}, u32[]{:S(2)}) collective-permute-start(f16[256,2048]{1,0:T(8,128)(2,1)S(1)} %multiply_convert_fusion.7), channel_id=1, source_target_pairs={{0,1},{1,0},{2,3},{3,2},{4,5},{5,4},{6,7},{7,6},{8,9},{9,8},{10,11... | collective-permute-start | bytes 3145736 | tf_op jit(solution)/shard_map/ppermute | solution.py:15
  67.6 28.9 %copy-start.6 = (f32[256,4096]{1,0:T(8,128)}, f32[256,4096]{1,0:T(8,128)S(1)}, u32[]{:S(2)}) copy-start(f32[256,4096]{1,0:T(8,128)S(1)} %fusion.20) | copy-start | bytes 12582916
  67.6 8.2 %collective-permute-start.8 = (f16[256,2048]{1,0:T(8,128)(2,1)S(1)}, f16[256,2048]{1,0:T(8,128)(2,1)S(1)}, u32[]{:S(2)}, u32[]{:S(2)}) collective-permute-start(f16[256,2048]{1,0:T(8,128)(2,1)S(1)} %multiply_convert_fusion.6), channel_id=1, source_target_pairs={{0,1},{1,0},{2,3},{3,2},{4,5},{5,4},{6,7},{7,6},{8,9},{9,8},{10,11... | collective-permute-start | bytes 3145736 | tf_op jit(solution)/shard_map/ppermute | solution.py:15
  74.7 21.5 %copy-start.4 = (f32[256,4096]{1,0:T(8,128)}, f32[256,4096]{1,0:T(8,128)S(1)}, u32[]{:S(2)}) copy-start(f32[256,4096]{1,0:T(8,128)S(1)} %fusion.21) | copy-start | bytes 12582916
  74.7 3.5 %collective-permute-start.9 = (bf16[256,1280]{1,0:T(8,128)(2,1)S(1)}, bf16[256,1280]{1,0:T(8,128)(2,1)S(1)}, u32[]{:S(2)}, u32[]{:S(2)}) collective-permute-start(bf16[256,1280]{1,0:T(8,128)(2,1)S(1)} %bitcast.96), channel_id=1, source_target_pairs={{0,0},{1,4},{4,1},{5,5},{10,10},{11,14},{14,11},{15,15},{16,16},{1... | collective-permute-start | bytes 1966088 | tf_op jit(solution)/shard_map/ppermute | solution.py:65
  75.4 3.7 %slice-start = ((s8[10485760]{0:T(1024)(128)(4,1)}), s8[4194304]{0:T(1024)(128)(4,1)S(1)}, s32[]{:S(2)}) async-start(s8[10485760]{0:T(1024)(128)(4,1)} %bitcast.89), calls=%async_computation | async-start | bytes 8388608
  75.8 4.5 %slice-start.1 = ((s8[10485760]{0:T(1024)(128)(4,1)}), s8[4194304]{0:T(1024)(128)(4,1)S(1)}, s32[]{:S(2)}) async-start(s8[10485760]{0:T(1024)(128)(4,1)} %bitcast.89), calls=%async_computation.1 | async-start | bytes 8388608
  76.3 4.7 %slice-start.2 = ((s8[10485760]{0:T(1024)(128)(4,1)}), s8[2097152]{0:T(1024)(128)(4,1)S(1)}, s32[]{:S(2)}) async-start(s8[10485760]{0:T(1024)(128)(4,1)} %bitcast.89), calls=%async_computation.2 | async-start | bytes 4194304
  78.2 48.1 %collective-permute-start.11 = (f16[2,256,2048]{2,1,0:T(8,128)(2,1)}, f16[2,256,2048]{2,1,0:T(8,128)(2,1)}, u32[]{:S(2)}, u32[]{:S(2)}) collective-permute-start(f16[2,256,2048]{2,1,0:T(8,128)(2,1)} %fusion), channel_id=1, source_target_pairs={{0,2},{2,0},{1,3},{3,1},{4,6},{6,4},{5,7},{7,5},{8,10},{10,8},{9,1... | collective-permute-start | bytes 6291464 | tf_op jit(solution)/shard_map/ppermute | solution.py:15
  88.5 10.2 %copy-start.1 = (f32[512,4096]{1,0:T(8,128)}, f32[512,4096]{1,0:T(8,128)S(1)}, u32[]{:S(2)}) copy-start(f32[512,4096]{1,0:T(8,128)S(1)} %shard_map.113) | copy-start | bytes 25165828
  88.7 10.0 %collective-permute-start.13 = (f16[256,2048]{1,0:T(8,128)(2,1)S(1)}, f16[256,2048]{1,0:T(8,128)(2,1)S(1)}, u32[]{:S(2)}, u32[]{:S(2)}) collective-permute-start(f16[256,2048]{1,0:T(8,128)(2,1)S(1)} %multiply_convert_fusion.4), channel_id=1, source_target_pairs={{0,1},{1,0},{2,3},{3,2},{4,5},{5,4},{6,7},{7,6},{8,9},{9,8},{10,11... | collective-permute-start | bytes 3145736 | tf_op jit(solution)/shard_map/ppermute | solution.py:15
  96.4 3.8 %collective-permute-start.15 = (f16[256,2048]{1,0:T(8,128)(2,1)S(1)}, f16[256,2048]{1,0:T(8,128)(2,1)}, u32[]{:S(2)}, u32[]{:S(2)}) collective-permute-start(f16[256,2048]{1,0:T(8,128)(2,1)S(1)} %multiply_convert_fusion.2), channel_id=1, source_target_pairs={{0,1},{1,0},{2,3},{3,2},{4,5},{5,4},{6,7},{7,6},{8,9},{9,8},{10,11... | collective-permute-start | bytes 3145736 | tf_op jit(solution)/shard_map/ppermute | solution.py:15
  97.7 6.3 %collective-permute-start.16 = (f16[256,2048]{1,0:T(8,128)(2,1)}, f16[256,2048]{1,0:T(8,128)(2,1)}, u32[]{:S(2)}, u32[]{:S(2)}) collective-permute-start(f16[256,2048]{1,0:T(8,128)(2,1)} %multiply_convert_fusion.1), channel_id=1, source_target_pairs={{0,1},{1,0},{2,3},{3,2},{4,5},{5,4},{6,7},{7,6},{8,9},{9,8},{10,11... | collective-permute-start | bytes 3145736 | tf_op jit(solution)/shard_map/ppermute | solution.py:15
  98.6 5.3 %copy-start.9 = (s32[2]{0:T(128)S(1)}, s32[2]{0:T(128)}, u32[]{:S(2)}) copy-start(s32[2]{0:T(128)} %param.18) | copy-start | bytes 28
  100.1 7.6 %collective-permute-start.17 = (f16[256,192]{0,1:T(8,128)(2,1)S(1)}, f16[256,192]{0,1:T(8,128)(2,1)S(1)}, u32[]{:S(2)}, u32[]{:S(2)}) collective-permute-start(f16[256,192]{0,1:T(8,128)(2,1)S(1)} %multiply_convert_fusion.9), channel_id=1, source_target_pairs={{0,4},{4,8},{8,12},{12,0},{1,5},{5,9},{9,13},{13,1},{2,6},{6,10},{... | collective-permute-start | bytes 294920 | tf_op jit(solution)/shard_map/ppermute | solution.py:15
  100.2 10.9 %collective-permute-start.18 = (f16[256,192]{0,1:T(8,128)(2,1)S(1)}, f16[256,192]{0,1:T(8,128)(2,1)}, u32[]{:S(2)}, u32[]{:S(2)}) collective-permute-start(f16[256,192]{0,1:T(8,128)(2,1)S(1)} %multiply_convert_fusion.9), channel_id=1, source_target_pairs={{0,8},{4,12},{8,0},{12,4},{1,9},{5,13},{9,1},{13,5},{2,10},{6,14},... | collective-permute-start | bytes 294920 | tf_op jit(solution)/shard_map/ppermute | solution.py:15
  100.2 10.9 %collective-permute-start.19 = (f16[256,192]{0,1:T(8,128)(2,1)S(1)}, f16[256,192]{0,1:T(8,128)(2,1)}, u32[]{:S(2)}, u32[]{:S(2)}) collective-permute-start(f16[256,192]{0,1:T(8,128)(2,1)S(1)} %multiply_convert_fusion.9), channel_id=1, source_target_pairs={{0,12},{4,0},{8,4},{12,8},{1,13},{5,1},{9,5},{13,9},{2,14},{6,2},{... | collective-permute-start | bytes 294920 | tf_op jit(solution)/shard_map/ppermute | solution.py:15
  104.0 44.7 %collective-permute-start.14 = (f16[256,2048]{1,0:T(8,128)(2,1)}, f16[256,2048]{1,0:T(8,128)(2,1)}, u32[]{:S(2)}, u32[]{:S(2)}) collective-permute-start(f16[256,2048]{1,0:T(8,128)(2,1)} %multiply_convert_fusion.3), channel_id=1, source_target_pairs={{0,2},{2,0},{1,3},{3,1},{4,6},{6,4},{5,7},{7,5},{8,10},{10,8},{9,1... | collective-permute-start | bytes 3145736 | tf_op jit(solution)/shard_map/ppermute | solution.py:15
  131.1 6.7 %copy-start.5 = (f32[256,4096]{1,0:T(8,128)S(1)}, f32[256,4096]{1,0:T(8,128)}, u32[]{:S(2)}) copy-start(f32[256,4096]{1,0:T(8,128)} %copy-done.4) | copy-start | bytes 12582916
  131.1 9.5 %collective-permute-start.12 = (f16[256,2048]{1,0:T(8,128)(2,1)S(1)}, f16[256,2048]{1,0:T(8,128)(2,1)S(1)}, u32[]{:S(2)}, u32[]{:S(2)}) collective-permute-start(f16[256,2048]{1,0:T(8,128)(2,1)S(1)} %multiply_convert_fusion.5), channel_id=1, source_target_pairs={{0,1},{1,0},{2,3},{3,2},{4,5},{5,4},{6,7},{7,6},{8,9},{9,8},{10,11... | collective-permute-start | bytes 3145736 | tf_op jit(solution)/shard_map/ppermute | solution.py:15
  142.6 7.8 %copy-start.2 = (bf16[2048,64]{1,0:T(8,128)(2,1)S(1)}, bf16[2048,64]{1,0:T(8,128)(2,1)}, u32[]{:S(2)}) copy-start(bf16[2048,64]{1,0:T(8,128)(2,1)} %copy.21.refs_2_) | copy-start | bytes 786436
  142.6 7.8 %copy-start.3 = (bf16[2048,64]{1,0:T(8,128)(2,1)S(1)}, bf16[2048,64]{1,0:T(8,128)(2,1)}, u32[]{:S(2)}) copy-start(bf16[2048,64]{1,0:T(8,128)(2,1)} %copy.22.refs_3_) | copy-start | bytes 786436
  151.7 6.6 %collective-permute-start.20 = (f32[6,16,64]{2,1,0:T(8,128)S(1)}, f32[6,16,64]{2,1,0:T(8,128)}, u32[]{:S(2)}, u32[]{:S(2)}) collective-permute-start(f32[6,16,64]{2,1,0:T(8,128)S(1)} %get-tuple-element.46), channel_id=1, source_target_pairs={{0,4},{4,8},{8,12},{12,0},{1,5},{5,9},{9,13},{13,1},{2,6},{6,10},{... | collective-permute-start | bytes 73736 | tf_op jit(solution)/shard_map/ppermute | solution.py:15
  151.8 7.4 %collective-permute-start.21 = (f32[6,16,64]{2,1,0:T(8,128)S(1)}, f32[6,16,64]{2,1,0:T(8,128)}, u32[]{:S(2)}, u32[]{:S(2)}) collective-permute-start(f32[6,16,64]{2,1,0:T(8,128)S(1)} %get-tuple-element.48), channel_id=1, source_target_pairs={{0,8},{4,12},{8,0},{12,4},{1,9},{5,13},{9,1},{13,5},{2,10},{6,14},... | collective-permute-start | bytes 73736 | tf_op jit(solution)/shard_map/ppermute | solution.py:15
  153.9 5.3 %collective-permute-start.22 = (f32[6,16,64]{2,1,0:T(8,128)S(1)}, f32[6,16,64]{2,1,0:T(8,128)}, u32[]{:S(2)}, u32[]{:S(2)}) collective-permute-start(f32[6,16,64]{2,1,0:T(8,128)S(1)} %get-tuple-element.47), channel_id=1, source_target_pairs={{0,12},{4,0},{8,4},{12,8},{1,13},{5,1},{9,5},{13,9},{2,14},{6,2},{... | collective-permute-start | bytes 73736 | tf_op jit(solution)/shard_map/ppermute | solution.py:15
  160.0 1.9 %collective-permute-start.25 = (f32[6,16,64]{2,1,0:T(8,128)S(1)}, f32[6,16,64]{2,1,0:T(8,128)S(1)}, u32[]{:S(2)}, u32[]{:S(2)}) collective-permute-start(f32[6,16,64]{2,1,0:T(8,128)S(1)} %fusion.12), channel_id=1, source_target_pairs={{0,1},{1,0},{2,3},{3,2},{4,5},{5,4},{6,7},{7,6},{8,9},{9,8},{10,11... | collective-permute-start | bytes 73736 | tf_op jit(solution)/shard_map/ppermute | solution.py:275
  160.1 4.2 %collective-permute-start.23 = (f32[6,16,64]{2,1,0:T(8,128)S(1)}, f32[6,16,64]{2,1,0:T(8,128)S(1)}, u32[]{:S(2)}, u32[]{:S(2)}) collective-permute-start(f32[6,16,64]{2,1,0:T(8,128)S(1)} %fusion.12), channel_id=1, source_target_pairs={{0,2},{1,3},{2,0},{3,1},{4,6},{5,7},{6,4},{7,5},{8,10},{9,11},{10,... | collective-permute-start | bytes 73736 | tf_op jit(solution)/shard_map/ppermute | solution.py:275
  161.4 3.7 %collective-permute-start.24 = (f32[6,16,64]{2,1,0:T(8,128)S(1)}, f32[6,16,64]{2,1,0:T(8,128)S(1)}, u32[]{:S(2)}, u32[]{:S(2)}) collective-permute-start(f32[6,16,64]{2,1,0:T(8,128)S(1)} %fusion.12), channel_id=1, source_target_pairs={{0,3},{1,2},{2,1},{3,0},{4,7},{5,6},{6,5},{7,4},{8,11},{9,10},{10,... | collective-permute-start | bytes 73736 | tf_op jit(solution)/shard_map/ppermute | solution.py:275
  166.6 3.9 %collective-permute-start.26 = (f32[4,512]{1,0:T(4,128)S(1)}, f32[4,512]{1,0:T(4,128)S(1)}, u32[]{:S(2)}, u32[]{:S(2)}) collective-permute-start(f32[4,512]{1,0:T(4,128)S(1)} %fusion.22), channel_id=1, source_target_pairs={{0,12},{4,0},{8,4},{12,8},{1,13},{5,1},{9,5},{13,9},{2,14},{6,2},{... | collective-permute-start | bytes 24584 | tf_op jit(solution)/shard_map/ppermute | solution.py:15
  169.3 4.6 %collective-permute-start.27 = (f32[4,512]{1,0:T(4,128)S(1)}, f32[4,512]{1,0:T(4,128)S(1)}, u32[]{:S(2)}, u32[]{:S(2)}) collective-permute-start(f32[4,512]{1,0:T(4,128)S(1)} %fusion.22), channel_id=1, source_target_pairs={{0,8},{4,12},{8,0},{12,4},{1,9},{5,13},{9,1},{13,5},{2,10},{6,14},... | collective-permute-start | bytes 24584 | tf_op jit(solution)/shard_map/ppermute | solution.py:15
  169.7 5.4 %collective-permute-start.28 = (f32[4,512]{1,0:T(4,128)S(1)}, f32[4,512]{1,0:T(4,128)S(1)}, u32[]{:S(2)}, u32[]{:S(2)}) collective-permute-start(f32[4,512]{1,0:T(4,128)S(1)} %fusion.22), channel_id=1, source_target_pairs={{0,4},{4,8},{8,12},{12,0},{1,5},{5,9},{9,13},{13,1},{2,6},{6,10},{... | collective-permute-start | bytes 24584 | tf_op jit(solution)/shard_map/ppermute | solution.py:15

commit v16 on v15

--- a/solution.py
+++ b/solution.py
@@ -169,16 +169,21 @@
     hid_part = w_gate.shape[1] // n_cores
 
     def forward(tokens, weight):
-        return jnp.dot(tokens, weight, preferred_element_type=F32)
+        return pack(jnp.dot(tokens, weight, preferred_element_type=F32))
 
     def core_sum(product, begin, *earlier):
+        packed = product.dtype == jnp.float16
+
         def share_of(index):
             return lax.dynamic_slice(product, (begin, index * hid_part), (tok_rows, hid_part))
 
         kept = share_of(core)
+        if packed:
+            kept = unpack(kept)
         for step in range(1, n_cores):
-            sent = pack(share_of(lax.rem(core + step, n_cores)))
-            kept = kept + unpack(after(shift(sent, "test", step), *earlier))
+            sent = share_of(lax.rem(core + step, n_cores))
+            got = shift(sent if packed else pack(sent), "test", step)
+            kept = kept + unpack(after(got, *earlier))
         return kept
 
     flat_acts = activations.reshape(tok_rows, d_local)

time: 178 us -> 178 us (level)
  other arithmetic: 22.1 us -> 19.2 us
  waiting for transfers between devices: 40.3 us -> 42.3 us
    dynamic_slice x0 -> x4, local copies, waits for them, and re-layouts: none -> 1.83 us  [share_of(): lax.dynamic_slice(product, (begin, index * hid_part), (tok_rows, hid_part))]
    ppermute x18, waiting for transfers between devices: 37.2 us -> 39 us  [shift(): return lax.ppermute(value, axis, [(i, (i + step) % n) for i in range(n)])]
    convert_element_type x9 -> x5, other arithmetic: 7.15 us -> 5.43 us  [pack(): return (value * SEND_SCALE).astype(jnp.float16)]
    unnamed x41 -> x43, local copies, waits for them, and re-layouts: 6.04 us -> 5.16 us
where the time goes in v16:
time: 178 us; the launch traced here: 177 us
  starting transfers between devices  65.7 us (37%)
  waiting for transfers between devices  42.3 us (24%)
  matrix products  28.5 us (16%)
  other arithmetic  19.2 us (11%)
  local copies, waits for them, and re-layouts  10.8 us (6%)
  Pallas kernels  8.69 us (5%)
    ppermute x8, starting transfers between devices, spread_features(): pieces.append(lax.ppermute(flat, ('tensor', 'example', 'test'), pairs))  42 us
    ppermute x18, waiting for transfers between devices, shift(): return lax.ppermute(value, axis, [(i, (i + step) % n) for i in range(n)])  39 us
    ppermute x18, starting transfers between devices, shift(): return lax.ppermute(value, axis, [(i, (i + step) % n) for i in range(n)])  21.8 us
    dot_general x4, matrix products, forward(): return pack(jnp.dot(tokens, weight, preferred_element_type=F32))  20.7 us
    pallas_call x1, Pallas kernels, dot_rows(): pl.pallas_call(dot_rows_kernel, out_shape=jax.ShapeDtypeStruct((rows, hid...  7.49 us
    convert_element_type x5, other arithmetic, pack(): return (value * SEND_SCALE).astype(jnp.float16)  5.43 us
    unnamed x43, local copies, waits for them, and re-layouts  5.16 us
    mul x1, other arithmetic, on_device(): silu_gate = gate_act * sigmoid_gate  4.11 us
  transfers between devices with their start and end apart: 29, of which 11 were waited for; matrix products, arithmetic and copies ran while one was open for 29% of the time, Pallas kernels for 4%

profile of v16, /device:TPU:0, one launch (start us, length us, event | category | flops | bytes accessed | tf_op | source)
XLA Modules:
  0.0 176.5 jit_solution(15751104984867379448)
XLA Ops:
  0.6 1.6 collective-permute-start
  2.2 1.5 collective-permute-start.1
  3.7 6.5 %collective-permute-start.6 = (bf16[256,1280]{1,0:T(8,128)(2,1)}, bf16[256,1280]{1,0:T(8,128)(2,1)}, u32[]{:S(2)}, u32[]{:S(2)}) collective-permute-start(bf16[256,1280]{1,0:T(8,128)(2,1)} %bitcast.101), channel_id=1, source_target_pairs={{0,0},{1,4},{4,1},{5,5},{10,10},{11,14},{14,11},{15,15},{16,16},{1... | collective-permute-start | bytes 1966088 | tf_op jit(solution)/shard_map/ppermute | solution.py:65
  10.3 5.2 %collective-permute-start.7 = (bf16[256,1280]{1,0:T(8,128)(2,1)}, bf16[256,1280]{1,0:T(8,128)(2,1)}, u32[]{:S(2)}, u32[]{:S(2)}) collective-permute-start(bf16[256,1280]{1,0:T(8,128)(2,1)} %bitcast.102), channel_id=1, source_target_pairs={{0,8},{1,12},{4,9},{5,13},{10,2},{11,6},{14,3},{15,7},{16,24},{17,... | collective-permute-start | bytes 1966088 | tf_op jit(solution)/shard_map/ppermute | solution.py:65
  15.4 1.8 %fusion.24 = (bf16[2048,64]{0,1:T(8,128)(2,1)S(1)}, bf16[2048,64]{0,1:T(8,128)(2,1)}) fusion(bf16[4096,192]{0,1:T(8,128)(2,1)} %param.16, s32[]{:T(128)S(6)} %select_n.62, s32[]{:T(128)S(6)} %add.166), kind=kLoop, calls=%fused_computation.88 | loop fusion | bytes 1048584 | tf_op jit(solution)/shard_map/slice | solution.py:196
  17.2 1.9 %copy.21.refs_2_ = bf16[2048,64]{1,0:T(8,128)(2,1)} copy(bf16[2048,64]{0,1:T(8,128)(2,1)} %get-tuple-element.43) | data formatting | bytes 524288
  19.2 1.0 copy.22.refs_3_
  20.2 1.4 fusion.13
  21.6 1.6 fusion.10
  23.2 1.2 broadcast_select_fusion.3
  24.4 7.3 %fusion = f16[256,4096]{1,0:T(8,128)(2,1)S(1)} fusion(bf16[256,1280]{1,0:T(8,128)(2,1)S(1)} %broadcast_select_fusion.3, bf16[1280,4096]{1,0:T(8,128)(2,1)} %param.12), kind=kOutput, calls=%fused_computation.4 | convolution fusion | flops 2686451712 | bytes 13238272 | tf_op jit(solution)/shard_map/dot_general | solution.py:172
  31.8 3.1 %fusion.1 = f16[256,4096]{1,0:T(8,128)(2,1)S(1)} fusion(bf16[256,1280]{1,0:T(8,128)(2,1)S(1)} %broadcast_select_fusion.3, bf16[1280,4096]{1,0:T(8,128)(2,1)S(1)} %copy-done.9), kind=kOutput, calls=%fused_computation.5 | convolution fusion | flops 2686451712 | bytes 13238272 | tf_op jit(solution)/shard_map/dot_general | solution.py:172
  34.9 1.3 collective-permute-start.3
  37.0 24.6 %collective-permute-start.10 = (bf16[256,1280]{1,0:T(8,128)(2,1)S(1)}, bf16[256,1280]{1,0:T(8,128)(2,1)S(1)}, u32[]{:S(2)}, u32[]{:S(2)}) collective-permute-start(bf16[256,1280]{1,0:T(8,128)(2,1)S(1)} %bitcast.97), channel_id=1, source_target_pairs={{0,8},{1,12},{4,9},{5,13},{10,2},{11,6},{14,3},{15,7},{16,24},{17,... | collective-permute-start | bytes 1966088 | tf_op jit(solution)/shard_map/ppermute | solution.py:65
  61.5 1.2 broadcast_select_fusion.2
  62.8 3.1 %fusion.2 = f16[256,4096]{1,0:T(8,128)(2,1)S(1)} fusion(bf16[256,1280]{1,0:T(8,128)(2,1)S(1)} %broadcast_select_fusion.2, bf16[1280,4096]{1,0:T(8,128)(2,1)S(1)} %bitcast.109), kind=kOutput, calls=%fused_computation.6 | convolution fusion | flops 2686451712 | bytes 13238272 | tf_op jit(solution)/shard_map/dot_general | solution.py:172
  67.0 7.2 %fusion.3 = f16[256,4096]{1,0:T(8,128)(2,1)S(1)} fusion(bf16[256,1280]{1,0:T(8,128)(2,1)S(1)} %broadcast_select_fusion.2, bf16[1280,4096]{1,0:T(8,128)(2,1)} %param.13), kind=kOutput, calls=%fused_computation.7 | convolution fusion | flops 2686451712 | bytes 13238272 | tf_op jit(solution)/shard_map/dot_general | solution.py:172
  75.7 1.9 %fusion.4 = f16[2,256,2048]{2,1,0:T(8,128)(2,1)} fusion(f32[1,256,2048]{2,1,0:T(8,128)S(1)} %multiply_bitcast_fusion, f32[1,256,2048]{2,1,0:T(8,128)S(1)} %multiply_bitcast_fusion.1), kind=kLoop, calls=%fused_computation.9 | loop fusion | flops 3145728 | bytes 6291456 | tf_op jit(solution)/shard_map/convert_element_type | solution.py:19
  77.9 1.4 slice-done.1
  79.9 7.5 %shard_map.113 = f32[512,4096]{1,0:T(8,128)S(1)} custom-call(bf16[512,1280]{1,0:T(8,128)(2,1)S(1)} %pad_maximum_fusion.tokens_ref, bf16[4096,1280]{1,0:T(8,128)(2,1)S(1)} %bitcast.92), custom_call_target="tpu_custom_call" | custom-call | flops 1 | bytes 1 | tf_op jit(solution)/shard_map/pallas_call | solution.py:95
  87.6 8.7 %collective-permute-start.13 = (f16[256,2048]{1,0:T(8,128)(2,1)S(1)}, f16[256,2048]{1,0:T(8,128)(2,1)S(1)}, u32[]{:S(2)}, u32[]{:S(2)}) collective-permute-start(f16[256,2048]{1,0:T(8,128)(2,1)S(1)} %multiply_convert_fusion.2), channel_id=1, source_target_pairs={{0,1},{1,0},{2,3},{3,2},{4,5},{5,4},{6,7},{7,6},{8,9},{9,8},{10,11... | collective-permute-start | bytes 3145736 | tf_op jit(solution)/shard_map/ppermute | solution.py:15
  96.7 1.1 constant_dynamic-slice_fusion.2
  97.8 1.1 collective-permute-start.16
  99.0 1.4 multiply_convert_fusion.1
  100.4 3.8 %collective-permute-start.19 = (f16[256,192]{0,1:T(8,128)(2,1)S(1)}, f16[256,192]{0,1:T(8,128)(2,1)}, u32[]{:S(2)}, u32[]{:S(2)}) collective-permute-start(f16[256,192]{0,1:T(8,128)(2,1)S(1)} %multiply_convert_fusion.5), channel_id=1, source_target_pairs={{0,12},{4,0},{8,4},{12,8},{1,13},{5,1},{9,5},{13,9},{2,14},{6,2},{... | collective-permute-start | bytes 294920 | tf_op jit(solution)/shard_map/ppermute | solution.py:15
  104.3 3.7 %collective-permute-done.17 = f16[256,192]{0,1:T(8,128)(2,1)S(1)} collective-permute-done((f16[256,192]{0,1:T(8,128)(2,1)S(1)}, f16[256,192]{0,1:T(8,128)(2,1)S(1)}, u32[]{:S(2)}, u32[]{:S(2)}) %collective-permute-start.17) | collective-permute-done | bytes 98336 | tf_op jit(solution)/shard_map/ppermute | solution.py:15
  108.0 3.4 %collective-permute-done.18 = f16[256,192]{0,1:T(8,128)(2,1)} collective-permute-done((f16[256,192]{0,1:T(8,128)(2,1)S(1)}, f16[256,192]{0,1:T(8,128)(2,1)}, u32[]{:S(2)}, u32[]{:S(2)}) %collective-permute-start.18) | collective-permute-done | bytes 98336 | tf_op jit(solution)/shard_map/ppermute | solution.py:15
  111.3 14.8 %collective-permute-done.11 = f16[2,256,2048]{2,1,0:T(8,128)(2,1)} collective-permute-done((f16[2,256,2048]{2,1,0:T(8,128)(2,1)}, f16[2,256,2048]{2,1,0:T(8,128)(2,1)}, u32[]{:S(2)}, u32[]{:S(2)}) %collective-permute-start.11) | collective-permute-done | bytes 2097184 | tf_op jit(solution)/shard_map/ppermute | solution.py:15
  126.1 1.7 multiply_add_fusion.2
  127.8 1.1 copy.17
  129.2 1.9 %multiply_convert_fusion.3 = f16[256,2048]{1,0:T(8,128)(2,1)S(1)} fusion(f32[512,4096]{1,0:T(8,128)} %copy-done.1, s32[]{:T(128)S(6)} %select_n.64), kind=kLoop, calls=%fused_computation.22 | loop fusion | flops 1048576 | bytes 3145732 | tf_op jit(solution)/shard_map/convert_element_type | solution.py:19
  131.9 4.1 %fusion.7 = (f32[256,2048]{1,0:T(8,128)S(1)}, f32[256,2048]{1,0:T(8,128)S(1)}) fusion(f16[256,2048]{1,0:T(8,128)(2,1)} %collective-permute-done.16, f16[2,256,2048]{2,1,0:T(8,128)(2,1)} %collective-permute-done.11, f16[256,4096]{1,0:T(8,128)(2,1)} %copy-done.6, s32[]{:T(128)S(6)} %select_n.62, f16[256,2048]{1,0:T(8,128)(2,1)} %collective-permute-done.15, ...), kind=kLoop, calls=%fused_computation.17 | loop fusion | flops 11010048 | bytes 10485764 | tf_op jit(solution)/shard_map/mul | solution.py:257
  136.0 2.3 %fusion.8 = f32[256,64]{0,1:T(8,128)S(1)} fusion(f32[256,2048]{1,0:T(8,128)S(1)} %get-tuple-element.40.refs_1_, f16[256,2048]{1,0:T(8,128)(2,1)} %collective-permute-done.15, f16[2,256,2048]{2,1,0:T(8,128)(2,1)} %collective-permute-done.11, f16[256,4096]{1,0:T(8,128)(2,1)S(1)} %copy-done.5, s32[]{:T(128)S(6)} %select_n.62, bf16[4096,192]{0,1:T(8,128)(2,1)} %param.16, ...), kind=kOutput, calls=%fused_computation.30 | convolution fusion | flops 71303168 | bytes 5572096 | tf_op jit(solution)/shard_map/dot_general | solution.py:260
  138.7 1.9 %multiply_add_fusion.1 = f32[256,2048]{1,0:T(8,128)S(1)} fusion(f16[256,2048]{1,0:T(8,128)(2,1)S(1)} %collective-permute-done.12, f32[512,4096]{1,0:T(8,128)} %copy-done.1, s32[]{:T(128)S(6)} %select_n.62), kind=kLoop, calls=%fused_computation.21 | loop fusion | flops 1572864 | bytes 5242884 | tf_op jit(solution)/shard_map/add | solution.py:186
  140.6 8.0 %collective-permute-done.14 = f16[256,2048]{1,0:T(8,128)(2,1)} collective-permute-done((f16[256,2048]{1,0:T(8,128)(2,1)}, f16[256,2048]{1,0:T(8,128)(2,1)}, u32[]{:S(2)}, u32[]{:S(2)}) %collective-permute-start.14) | collective-permute-done | bytes 1048608 | tf_op jit(solution)/shard_map/ppermute | solution.py:15
  148.6 1.6 multiply_add_fusion.down_ref
  150.2 1.2 shard_map.114
  151.5 2.6 %collective-permute-start.21 = (f32[6,16,64]{2,1,0:T(8,128)S(1)}, f32[6,16,64]{2,1,0:T(8,128)}, u32[]{:S(2)}, u32[]{:S(2)}) collective-permute-start(f32[6,16,64]{2,1,0:T(8,128)S(1)} %get-tuple-element.48), channel_id=1, source_target_pairs={{0,8},{4,12},{8,0},{12,4},{1,9},{5,13},{9,1},{13,5},{2,10},{6,14},... | collective-permute-start | bytes 73736 | tf_op jit(solution)/shard_map/ppermute | solution.py:15
  154.1 1.2 collective-permute-start.22
  155.3 2.7 %collective-permute-done.20 = f32[6,16,64]{2,1,0:T(8,128)} collective-permute-done((f32[6,16,64]{2,1,0:T(8,128)S(1)}, f32[6,16,64]{2,1,0:T(8,128)}, u32[]{:S(2)}, u32[]{:S(2)}) %collective-permute-start.20) | collective-permute-done | bytes 24608 | tf_op jit(solution)/shard_map/ppermute | solution.py:15
  158.0 1.2 collective-permute-done.21
  160.1 1.5 collective-permute-start.23
  162.0 2.3 %collective-permute-done.23 = f32[6,16,64]{2,1,0:T(8,128)S(1)} collective-permute-done((f32[6,16,64]{2,1,0:T(8,128)S(1)}, f32[6,16,64]{2,1,0:T(8,128)S(1)}, u32[]{:S(2)}, u32[]{:S(2)}) %collective-permute-start.23) | collective-permute-done | bytes 24608 | tf_op jit(solution)/shard_map/ppermute | solution.py:280
  164.3 1.0 collective-permute-done.24
  165.5 1.3 fusion.25
  166.8 2.2 %collective-permute-start.26 = (f32[4,512]{1,0:T(4,128)S(1)}, f32[4,512]{1,0:T(4,128)S(1)}, u32[]{:S(2)}, u32[]{:S(2)}) collective-permute-start(f32[4,512]{1,0:T(4,128)S(1)} %fusion.25), channel_id=1, source_target_pairs={{0,12},{4,0},{8,4},{12,8},{1,13},{5,1},{9,5},{13,9},{2,14},{6,2},{... | collective-permute-start | bytes 24584 | tf_op jit(solution)/shard_map/ppermute | solution.py:15
  170.5 3.2 %collective-permute-done.27 = f32[4,512]{1,0:T(4,128)S(1)} collective-permute-done((f32[4,512]{1,0:T(4,128)S(1)}, f32[4,512]{1,0:T(4,128)S(1)}, u32[]{:S(2)}, u32[]{:S(2)}) %collective-permute-start.27) | collective-permute-done | bytes 8224 | tf_op jit(solution)/shard_map/ppermute | solution.py:15
  173.6 1.4 collective-permute-done.28
  (108 shorter events, 11.0 us)
Async XLA Ops:
  0.6 164.8 %copy-start = (bf16[3,16,64,512]{3,2,1,0:T(8,128)(2,1)S(1)}, bf16[3,16,64,512]{3,2,1,0:T(8,128)(2,1)}, u32[]{:S(2)}) copy-start(bf16[3,16,64,512]{3,2,1,0:T(8,128)(2,1)} %param.17) | copy-start | bytes 9437188
  0.6 22.6 %collective-permute-start = (bf16[256,1280]{1,0:T(8,128)(2,1)}, bf16[256,1280]{1,0:T(8,128)(2,1)}, u32[]{:S(2)}, u32[]{:S(2)}) collective-permute-start(bf16[256,1280]{1,0:T(8,128)(2,1)} %bitcast.99), channel_id=1, source_target_pairs={{2,0},{3,4},{6,1},{7,5},{8,10},{9,14},{12,11},{13,15},{18,16},{19,... | collective-permute-start | bytes 1966088 | tf_op jit(solution)/shard_map/ppermute | solution.py:65
  2.2 21.0 %collective-permute-start.1 = (bf16[256,1280]{1,0:T(8,128)(2,1)}, bf16[256,1280]{1,0:T(8,128)(2,1)}, u32[]{:S(2)}, u32[]{:S(2)}) collective-permute-start(bf16[256,1280]{1,0:T(8,128)(2,1)} %bitcast.100), channel_id=1, source_target_pairs={{2,8},{3,12},{6,9},{7,13},{8,2},{9,6},{12,3},{13,7},{18,24},{19,28... | collective-permute-start | bytes 1966088 | tf_op jit(solution)/shard_map/ppermute | solution.py:65
  3.7 57.8 %collective-permute-start.6 = (bf16[256,1280]{1,0:T(8,128)(2,1)}, bf16[256,1280]{1,0:T(8,128)(2,1)}, u32[]{:S(2)}, u32[]{:S(2)}) collective-permute-start(bf16[256,1280]{1,0:T(8,128)(2,1)} %bitcast.101), channel_id=1, source_target_pairs={{0,0},{1,4},{4,1},{5,5},{10,10},{11,14},{14,11},{15,15},{16,16},{1... | collective-permute-start | bytes 1966088 | tf_op jit(solution)/shard_map/ppermute | solution.py:65
  10.3 51.3 %collective-permute-start.7 = (bf16[256,1280]{1,0:T(8,128)(2,1)}, bf16[256,1280]{1,0:T(8,128)(2,1)}, u32[]{:S(2)}, u32[]{:S(2)}) collective-permute-start(bf16[256,1280]{1,0:T(8,128)(2,1)} %bitcast.102), channel_id=1, source_target_pairs={{0,8},{1,12},{4,9},{5,13},{10,2},{11,6},{14,3},{15,7},{16,24},{17,... | collective-permute-start | bytes 1966088 | tf_op jit(solution)/shard_map/ppermute | solution.py:65
  15.4 7.8 %collective-permute-start.2 = (s32[2]{0:T(128)}, s32[2]{0:T(128)S(1)}, u32[]{:S(2)}, u32[]{:S(2)}) collective-permute-start(s32[2]{0:T(128)} %param.19), channel_id=1, source_target_pairs={{0,2},{2,0},{1,3},{3,1},{4,6},{6,4},{5,7},{7,5},{8,10},{10,8},{9,1... | collective-permute-start | bytes 32 | tf_op jit(solution)/shard_map/ppermute | solution.py:15
  15.4 7.7 %copy-start.8 = (s32[2]{0:T(128)S(1)}, s32[2]{0:T(128)}, u32[]{:S(2)}) copy-start(s32[2]{0:T(128)} %param.19) | copy-start | bytes 28
  24.4 7.4 %copy-start.9 = (bf16[1280,4096]{1,0:T(8,128)(2,1)S(1)}, bf16[1280,4096]{1,0:T(8,128)(2,1)}, u32[]{:S(2)}) copy-start(bf16[1280,4096]{1,0:T(8,128)(2,1)} %param.13) | copy-start | bytes 31457284
  24.4 38.3 %slice-start.3 = ((s8[10485760]{0:T(1024)(128)(4,1)}), s8[4194304]{0:T(1024)(128)(4,1)S(1)}, s32[]{:S(2)}) async-start(s8[10485760]{0:T(1024)(128)(4,1)} %bitcast.108), calls=%async_computation.3 | async-start | bytes 8388608
  24.4 38.3 %slice-start.4 = ((s8[10485760]{0:T(1024)(128)(4,1)}), s8[4194304]{0:T(1024)(128)(4,1)S(1)}, s32[]{:S(2)}) async-start(s8[10485760]{0:T(1024)(128)(4,1)} %bitcast.108), calls=%async_computation.4 | async-start | bytes 8388608
  31.8 3.1 %copy-start.7 = (bf16[2,128,1280]{2,1,0:T(8,128)(2,1)S(1)}, bf16[2,128,1280]{2,1,0:T(8,128)(2,1)}, u32[]{:S(2)}) copy-start(bf16[2,128,1280]{2,1,0:T(8,128)(2,1)} %param.11) | copy-start | bytes 1966084
  31.8 30.9 %slice-start.5 = ((s8[10485760]{0:T(1024)(128)(4,1)}), s8[2097152]{0:T(1024)(128)(4,1)S(1)}, s32[]{:S(2)}) async-start(s8[10485760]{0:T(1024)(128)(4,1)} %bitcast.108), calls=%async_computation.5 | async-start | bytes 4194304
  34.9 42.6 %collective-permute-start.3 = (bf16[256,1280]{1,0:T(8,128)(2,1)S(1)}, bf16[256,1280]{1,0:T(8,128)(2,1)S(1)}, u32[]{:S(2)}, u32[]{:S(2)}) collective-permute-start(bf16[256,1280]{1,0:T(8,128)(2,1)S(1)} %bitcast.95), channel_id=1, source_target_pairs={{2,0},{3,4},{6,1},{7,5},{8,10},{9,14},{12,11},{13,15},{18,16},{19,... | collective-permute-start | bytes 1966088 | tf_op jit(solution)/shard_map/ppermute | solution.py:65
  36.2 41.3 %collective-permute-start.4 = (bf16[256,1280]{1,0:T(8,128)(2,1)S(1)}, bf16[256,1280]{1,0:T(8,128)(2,1)S(1)}, u32[]{:S(2)}, u32[]{:S(2)}) collective-permute-start(bf16[256,1280]{1,0:T(8,128)(2,1)S(1)} %bitcast.96), channel_id=1, source_target_pairs={{2,8},{3,12},{6,9},{7,13},{8,2},{9,6},{12,3},{13,7},{18,24},{19,28... | collective-permute-start | bytes 1966088 | tf_op jit(solution)/shard_map/ppermute | solution.py:65
  37.0 40.6 %collective-permute-start.10 = (bf16[256,1280]{1,0:T(8,128)(2,1)S(1)}, bf16[256,1280]{1,0:T(8,128)(2,1)S(1)}, u32[]{:S(2)}, u32[]{:S(2)}) collective-permute-start(bf16[256,1280]{1,0:T(8,128)(2,1)S(1)} %bitcast.97), channel_id=1, source_target_pairs={{0,8},{1,12},{4,9},{5,13},{10,2},{11,6},{14,3},{15,7},{16,24},{17,... | collective-permute-start | bytes 1966088 | tf_op jit(solution)/shard_map/ppermute | solution.py:65
  65.9 30.8 %copy-start.6 = (f16[256,4096]{1,0:T(8,128)(2,1)}, f16[256,4096]{1,0:T(8,128)(2,1)S(1)}, u32[]{:S(2)}) copy-start(f16[256,4096]{1,0:T(8,128)(2,1)S(1)} %fusion.2) | copy-start | bytes 6291460
  66.1 8.1 %collective-permute-start.5 = (f16[256,2048]{1,0:T(8,128)(2,1)S(1)}, f16[256,2048]{1,0:T(8,128)(2,1)S(1)}, u32[]{:S(2)}, u32[]{:S(2)}) collective-permute-start(f16[256,2048]{1,0:T(8,128)(2,1)S(1)} %constant_dynamic-slice_fusion.5), channel_id=1, source_target_pairs={{0,1},{1,0},{2,3},{3,2},{4,5},{5,4},{6,7},{7,6},{8,9},{9,8},{10,11... | collective-permute-start | bytes 3145736 | tf_op jit(solution)/shard_map/ppermute | solution.py:15
  66.4 8.9 %collective-permute-start.8 = (f16[256,2048]{1,0:T(8,128)(2,1)S(1)}, f16[256,2048]{1,0:T(8,128)(2,1)S(1)}, u32[]{:S(2)}, u32[]{:S(2)}) collective-permute-start(f16[256,2048]{1,0:T(8,128)(2,1)S(1)} %constant_dynamic-slice_fusion.4), channel_id=1, source_target_pairs={{0,1},{1,0},{2,3},{3,2},{4,5},{5,4},{6,7},{7,6},{8,9},{9,8},{10,11... | collective-permute-start | bytes 3145736 | tf_op jit(solution)/shard_map/ppermute | solution.py:15
  74.2 22.2 %copy-start.4 = (f16[256,4096]{1,0:T(8,128)(2,1)}, f16[256,4096]{1,0:T(8,128)(2,1)S(1)}, u32[]{:S(2)}) copy-start(f16[256,4096]{1,0:T(8,128)(2,1)S(1)} %fusion.3) | copy-start | bytes 6291460
  74.2 3.4 %collective-permute-start.9 = (bf16[256,1280]{1,0:T(8,128)(2,1)S(1)}, bf16[256,1280]{1,0:T(8,128)(2,1)S(1)}, u32[]{:S(2)}, u32[]{:S(2)}) collective-permute-start(bf16[256,1280]{1,0:T(8,128)(2,1)S(1)} %bitcast.98), channel_id=1, source_target_pairs={{0,0},{1,4},{4,1},{5,5},{10,10},{11,14},{14,11},{15,15},{16,16},{1... | collective-permute-start | bytes 1966088 | tf_op jit(solution)/shard_map/ppermute | solution.py:65
  74.9 3.0 %slice-start = ((s8[10485760]{0:T(1024)(128)(4,1)}), s8[4194304]{0:T(1024)(128)(4,1)S(1)}, s32[]{:S(2)}) async-start(s8[10485760]{0:T(1024)(128)(4,1)} %bitcast.91), calls=%async_computation | async-start | bytes 8388608
  75.3 3.9 %slice-start.1 = ((s8[10485760]{0:T(1024)(128)(4,1)}), s8[4194304]{0:T(1024)(128)(4,1)S(1)}, s32[]{:S(2)}) async-start(s8[10485760]{0:T(1024)(128)(4,1)} %bitcast.91), calls=%async_computation.1 | async-start | bytes 8388608
  75.7 4.2 %slice-start.2 = ((s8[10485760]{0:T(1024)(128)(4,1)}), s8[2097152]{0:T(1024)(128)(4,1)S(1)}, s32[]{:S(2)}) async-start(s8[10485760]{0:T(1024)(128)(4,1)} %bitcast.91), calls=%async_computation.2 | async-start | bytes 4194304
  77.6 48.5 %collective-permute-start.11 = (f16[2,256,2048]{2,1,0:T(8,128)(2,1)}, f16[2,256,2048]{2,1,0:T(8,128)(2,1)}, u32[]{:S(2)}, u32[]{:S(2)}) collective-permute-start(f16[2,256,2048]{2,1,0:T(8,128)(2,1)} %fusion.4), channel_id=1, source_target_pairs={{0,2},{2,0},{1,3},{3,1},{4,6},{6,4},{5,7},{7,5},{8,10},{10,8},{9,1... | collective-permute-start | bytes 6291464 | tf_op jit(solution)/shard_map/ppermute | solution.py:15
  87.4 11.6 %copy-start.1 = (f32[512,4096]{1,0:T(8,128)}, f32[512,4096]{1,0:T(8,128)S(1)}, u32[]{:S(2)}) copy-start(f32[512,4096]{1,0:T(8,128)S(1)} %shard_map.113) | copy-start | bytes 25165828
  87.6 11.3 %collective-permute-start.13 = (f16[256,2048]{1,0:T(8,128)(2,1)S(1)}, f16[256,2048]{1,0:T(8,128)(2,1)S(1)}, u32[]{:S(2)}, u32[]{:S(2)}) collective-permute-start(f16[256,2048]{1,0:T(8,128)(2,1)S(1)} %multiply_convert_fusion.2), channel_id=1, source_target_pairs={{0,1},{1,0},{2,3},{3,2},{4,5},{5,4},{6,7},{7,6},{8,9},{9,8},{10,11... | collective-permute-start | bytes 3145736 | tf_op jit(solution)/shard_map/ppermute | solution.py:15
  96.6 3.9 %collective-permute-start.15 = (f16[256,2048]{1,0:T(8,128)(2,1)S(1)}, f16[256,2048]{1,0:T(8,128)(2,1)}, u32[]{:S(2)}, u32[]{:S(2)}) collective-permute-start(f16[256,2048]{1,0:T(8,128)(2,1)S(1)} %constant_dynamic-slice_fusion.3), channel_id=1, source_target_pairs={{0,1},{1,0},{2,3},{3,2},{4,5},{5,4},{6,7},{7,6},{8,9},{9,8},{10,11... | collective-permute-start | bytes 3145736 | tf_op jit(solution)/shard_map/ppermute | solution.py:15
  97.8 6.5 %collective-permute-start.16 = (f16[256,2048]{1,0:T(8,128)(2,1)}, f16[256,2048]{1,0:T(8,128)(2,1)}, u32[]{:S(2)}, u32[]{:S(2)}) collective-permute-start(f16[256,2048]{1,0:T(8,128)(2,1)} %constant_dynamic-slice_fusion.2), channel_id=1, source_target_pairs={{0,1},{1,0},{2,3},{3,2},{4,5},{5,4},{6,7},{7,6},{8,9},{9,8},{10,11... | collective-permute-start | bytes 3145736 | tf_op jit(solution)/shard_map/ppermute | solution.py:15
  98.9 5.3 %copy-start.10 = (s32[2]{0:T(128)S(1)}, s32[2]{0:T(128)}, u32[]{:S(2)}) copy-start(s32[2]{0:T(128)} %param.18) | copy-start | bytes 28
  100.4 7.6 %collective-permute-start.17 = (f16[256,192]{0,1:T(8,128)(2,1)S(1)}, f16[256,192]{0,1:T(8,128)(2,1)S(1)}, u32[]{:S(2)}, u32[]{:S(2)}) collective-permute-start(f16[256,192]{0,1:T(8,128)(2,1)S(1)} %multiply_convert_fusion.5), channel_id=1, source_target_pairs={{0,4},{4,8},{8,12},{12,0},{1,5},{5,9},{9,13},{13,1},{2,6},{6,10},{... | collective-permute-start | bytes 294920 | tf_op jit(solution)/shard_map/ppermute | solution.py:15
  100.4 10.9 %collective-permute-start.18 = (f16[256,192]{0,1:T(8,128)(2,1)S(1)}, f16[256,192]{0,1:T(8,128)(2,1)}, u32[]{:S(2)}, u32[]{:S(2)}) collective-permute-start(f16[256,192]{0,1:T(8,128)(2,1)S(1)} %multiply_convert_fusion.5), channel_id=1, source_target_pairs={{0,8},{4,12},{8,0},{12,4},{1,9},{5,13},{9,1},{13,5},{2,10},{6,14},... | collective-permute-start | bytes 294920 | tf_op jit(solution)/shard_map/ppermute | solution.py:15
  100.4 10.9 %collective-permute-start.19 = (f16[256,192]{0,1:T(8,128)(2,1)S(1)}, f16[256,192]{0,1:T(8,128)(2,1)}, u32[]{:S(2)}, u32[]{:S(2)}) collective-permute-start(f16[256,192]{0,1:T(8,128)(2,1)S(1)} %multiply_convert_fusion.5), channel_id=1, source_target_pairs={{0,12},{4,0},{8,4},{12,8},{1,13},{5,1},{9,5},{13,9},{2,14},{6,2},{... | collective-permute-start | bytes 294920 | tf_op jit(solution)/shard_map/ppermute | solution.py:15
  104.3 44.3 %collective-permute-start.14 = (f16[256,2048]{1,0:T(8,128)(2,1)}, f16[256,2048]{1,0:T(8,128)(2,1)}, u32[]{:S(2)}, u32[]{:S(2)}) collective-permute-start(f16[256,2048]{1,0:T(8,128)(2,1)} %multiply_convert_fusion.1), channel_id=1, source_target_pairs={{0,2},{2,0},{1,3},{3,1},{4,6},{6,4},{5,7},{7,5},{8,10},{10,8},{9,1... | collective-permute-start | bytes 3145736 | tf_op jit(solution)/shard_map/ppermute | solution.py:15
  129.1 2.7 %copy-start.5 = (f16[256,4096]{1,0:T(8,128)(2,1)S(1)}, f16[256,4096]{1,0:T(8,128)(2,1)}, u32[]{:S(2)}) copy-start(f16[256,4096]{1,0:T(8,128)(2,1)} %copy-done.4) | copy-start | bytes 6291460
  131.1 7.5 %collective-permute-start.12 = (f16[256,2048]{1,0:T(8,128)(2,1)S(1)}, f16[256,2048]{1,0:T(8,128)(2,1)S(1)}, u32[]{:S(2)}, u32[]{:S(2)}) collective-permute-start(f16[256,2048]{1,0:T(8,128)(2,1)S(1)} %multiply_convert_fusion.3), channel_id=1, source_target_pairs={{0,1},{1,0},{2,3},{3,2},{4,5},{5,4},{6,7},{7,6},{8,9},{9,8},{10,11... | collective-permute-start | bytes 3145736 | tf_op jit(solution)/shard_map/ppermute | solution.py:15
  140.6 9.6 %copy-start.2 = (bf16[2048,64]{1,0:T(8,128)(2,1)S(1)}, bf16[2048,64]{1,0:T(8,128)(2,1)}, u32[]{:S(2)}) copy-start(bf16[2048,64]{1,0:T(8,128)(2,1)} %copy.21.refs_2_) | copy-start | bytes 786436
  140.6 9.6 %copy-start.3 = (bf16[2048,64]{1,0:T(8,128)(2,1)S(1)}, bf16[2048,64]{1,0:T(8,128)(2,1)}, u32[]{:S(2)}) copy-start(bf16[2048,64]{1,0:T(8,128)(2,1)} %copy.22.refs_3_) | copy-start | bytes 786436
  151.4 6.5 %collective-permute-start.20 = (f32[6,16,64]{2,1,0:T(8,128)S(1)}, f32[6,16,64]{2,1,0:T(8,128)}, u32[]{:S(2)}, u32[]{:S(2)}) collective-permute-start(f32[6,16,64]{2,1,0:T(8,128)S(1)} %get-tuple-element.46), channel_id=1, source_target_pairs={{0,4},{4,8},{8,12},{12,0},{1,5},{5,9},{9,13},{13,1},{2,6},{6,10},{... | collective-permute-start | bytes 73736 | tf_op jit(solution)/shard_map/ppermute | solution.py:15
  151.5 7.7 %collective-permute-start.21 = (f32[6,16,64]{2,1,0:T(8,128)S(1)}, f32[6,16,64]{2,1,0:T(8,128)}, u32[]{:S(2)}, u32[]{:S(2)}) collective-permute-start(f32[6,16,64]{2,1,0:T(8,128)S(1)} %get-tuple-element.48), channel_id=1, source_target_pairs={{0,8},{4,12},{8,0},{12,4},{1,9},{5,13},{9,1},{13,5},{2,10},{6,14},... | collective-permute-start | bytes 73736 | tf_op jit(solution)/shard_map/ppermute | solution.py:15
  154.1 5.1 %collective-permute-start.22 = (f32[6,16,64]{2,1,0:T(8,128)S(1)}, f32[6,16,64]{2,1,0:T(8,128)}, u32[]{:S(2)}, u32[]{:S(2)}) collective-permute-start(f32[6,16,64]{2,1,0:T(8,128)S(1)} %get-tuple-element.47), channel_id=1, source_target_pairs={{0,12},{4,0},{8,4},{12,8},{1,13},{5,1},{9,5},{13,9},{2,14},{6,2},{... | collective-permute-start | bytes 73736 | tf_op jit(solution)/shard_map/ppermute | solution.py:15
  160.0 1.9 %collective-permute-start.25 = (f32[6,16,64]{2,1,0:T(8,128)S(1)}, f32[6,16,64]{2,1,0:T(8,128)S(1)}, u32[]{:S(2)}, u32[]{:S(2)}) collective-permute-start(f32[6,16,64]{2,1,0:T(8,128)S(1)} %fusion.19), channel_id=1, source_target_pairs={{0,1},{1,0},{2,3},{3,2},{4,5},{5,4},{6,7},{7,6},{8,9},{9,8},{10,11... | collective-permute-start | bytes 73736 | tf_op jit(solution)/shard_map/ppermute | solution.py:280
  160.1 4.2 %collective-permute-start.23 = (f32[6,16,64]{2,1,0:T(8,128)S(1)}, f32[6,16,64]{2,1,0:T(8,128)S(1)}, u32[]{:S(2)}, u32[]{:S(2)}) collective-permute-start(f32[6,16,64]{2,1,0:T(8,128)S(1)} %fusion.19), channel_id=1, source_target_pairs={{0,2},{1,3},{2,0},{3,1},{4,6},{5,7},{6,4},{7,5},{8,10},{9,11},{10,... | collective-permute-start | bytes 73736 | tf_op jit(solution)/shard_map/ppermute | solution.py:280
  161.6 3.7 %collective-permute-start.24 = (f32[6,16,64]{2,1,0:T(8,128)S(1)}, f32[6,16,64]{2,1,0:T(8,128)S(1)}, u32[]{:S(2)}, u32[]{:S(2)}) collective-permute-start(f32[6,16,64]{2,1,0:T(8,128)S(1)} %fusion.19), channel_id=1, source_target_pairs={{0,3},{1,2},{2,1},{3,0},{4,7},{5,6},{6,5},{7,4},{8,11},{9,10},{10,... | collective-permute-start | bytes 73736 | tf_op jit(solution)/shard_map/ppermute | solution.py:280
  166.8 3.7 %collective-permute-start.26 = (f32[4,512]{1,0:T(4,128)S(1)}, f32[4,512]{1,0:T(4,128)S(1)}, u32[]{:S(2)}, u32[]{:S(2)}) collective-permute-start(f32[4,512]{1,0:T(4,128)S(1)} %fusion.25), channel_id=1, source_target_pairs={{0,12},{4,0},{8,4},{12,8},{1,13},{5,1},{9,5},{13,9},{2,14},{6,2},{... | collective-permute-start | bytes 24584 | tf_op jit(solution)/shard_map/ppermute | solution.py:15
  169.1 4.6 %collective-permute-start.27 = (f32[4,512]{1,0:T(4,128)S(1)}, f32[4,512]{1,0:T(4,128)S(1)}, u32[]{:S(2)}, u32[]{:S(2)}) collective-permute-start(f32[4,512]{1,0:T(4,128)S(1)} %fusion.25), channel_id=1, source_target_pairs={{0,8},{4,12},{8,0},{12,4},{1,9},{5,13},{9,1},{13,5},{2,10},{6,14},... | collective-permute-start | bytes 24584 | tf_op jit(solution)/shard_map/ppermute | solution.py:15
  169.5 5.4 %collective-permute-start.28 = (f32[4,512]{1,0:T(4,128)S(1)}, f32[4,512]{1,0:T(4,128)S(1)}, u32[]{:S(2)}, u32[]{:S(2)}) collective-permute-start(f32[4,512]{1,0:T(4,128)S(1)} %fusion.25), channel_id=1, source_target_pairs={{0,4},{4,8},{8,12},{12,0},{1,5},{5,9},{9,13},{13,1},{2,6},{6,10},{... | collective-permute-start | bytes 24584 | tf_op jit(solution)/shard_map/ppermute | solution.py:15

commit v17 on v16

--- a/solution.py
+++ b/solution.py
@@ -214,10 +214,10 @@
         grad_ready = after(flat_grad, *up_far)
         grad_far, grad_near = spread_features(grad_ready, 1), spread_features(grad_ready, 0)
         acts_near = arrived_features(acts_near, *up_far)
-    gate_near = forward(after(acts_near, *up_far), w_gate)
-    up_near = forward(after(acts_near, gate_near), w_up)
+    up_near = forward(after(acts_near, *up_far), w_up)
+    gate_near = forward(after(acts_near, up_near), w_gate)
     for step, (gate, up) in enumerate(zip(gate_far, up_far), 1):
-        both = pack(jnp.stack([core_sum(gate, 0, up_near), core_sum(up, 0, up_near)]))
+        both = pack(jnp.stack([core_sum(gate, 0, gate_near), core_sum(up, 0, gate_near)]))
         received = shift(both, "example", step)
         arrived.append(received)
     if direct:

time: 178 us -> 178 us (level)
    unnamed x43 -> x45, local copies, waits for them, and re-layouts: 5.16 us -> 6.13 us
where the time goes in v17:
time: 178 us; the launch traced here: 177 us
  starting transfers between devices  65.7 us (37%)
  waiting for transfers between devices  41.7 us (23%)
  matrix products  28.5 us (16%)
  other arithmetic  19 us (11%)
  local copies, waits for them, and re-layouts  11.8 us (7%)
  Pallas kernels  8.69 us (5%)
    ppermute x8, starting transfers between devices, spread_features(): pieces.append(lax.ppermute(flat, ('tensor', 'example', 'test'), pairs))  42 us
    ppermute x18, waiting for transfers between devices, shift(): return lax.ppermute(value, axis, [(i, (i + step) % n) for i in range(n)])  38.3 us
    ppermute x18, starting transfers between devices, shift(): return lax.ppermute(value, axis, [(i, (i + step) % n) for i in range(n)])  21.8 us
    dot_general x4, matrix products, forward(): return pack(jnp.dot(tokens, weight, preferred_element_type=F32))  20.7 us
    pallas_call x1, Pallas kernels, dot_rows(): pl.pallas_call(dot_rows_kernel, out_shape=jax.ShapeDtypeStruct((rows, hid...  7.48 us
    unnamed x45, local copies, waits for them, and re-layouts  6.13 us
    convert_element_type x5, other arithmetic, pack(): return (value * SEND_SCALE).astype(jnp.float16)  5.45 us
    mul x1, other arithmetic, on_device(): silu_gate = gate_act * sigmoid_gate  3.79 us
  transfers between devices with their start and end apart: 29, of which 11 were waited for; matrix products, arithmetic and copies ran while one was open for 29% of the time, Pallas kernels for 4%

profile of v17, /device:TPU:0, one launch (start us, length us, event | category | flops | bytes accessed | tf_op | source)
XLA Modules:
  0.0 176.7 jit_solution(18043212011717312421)
XLA Ops:
  0.6 1.6 collective-permute-start
  2.2 1.5 collective-permute-start.1
  3.7 6.5 %collective-permute-start.6 = (bf16[256,1280]{1,0:T(8,128)(2,1)}, bf16[256,1280]{1,0:T(8,128)(2,1)}, u32[]{:S(2)}, u32[]{:S(2)}) collective-permute-start(bf16[256,1280]{1,0:T(8,128)(2,1)} %bitcast.101), channel_id=1, source_target_pairs={{0,0},{1,4},{4,1},{5,5},{10,10},{11,14},{14,11},{15,15},{16,16},{1... | collective-permute-start | bytes 1966088 | tf_op jit(solution)/shard_map/ppermute | solution.py:65
  10.2 5.2 %collective-permute-start.7 = (bf16[256,1280]{1,0:T(8,128)(2,1)}, bf16[256,1280]{1,0:T(8,128)(2,1)}, u32[]{:S(2)}, u32[]{:S(2)}) collective-permute-start(bf16[256,1280]{1,0:T(8,128)(2,1)} %bitcast.102), channel_id=1, source_target_pairs={{0,8},{1,12},{4,9},{5,13},{10,2},{11,6},{14,3},{15,7},{16,24},{17,... | collective-permute-start | bytes 1966088 | tf_op jit(solution)/shard_map/ppermute | solution.py:65
  15.5 1.8 fusion.24
  17.2 1.9 %copy.21.refs_2_ = bf16[2048,64]{1,0:T(8,128)(2,1)} copy(bf16[2048,64]{0,1:T(8,128)(2,1)} %get-tuple-element.43) | data formatting | bytes 524288
  19.2 1.0 copy.22.refs_3_
  20.2 1.4 fusion.13
  21.6 1.6 fusion.10
  23.3 1.3 broadcast_select_fusion.3
  24.6 7.3 %fusion = f16[256,4096]{1,0:T(8,128)(2,1)S(1)} fusion(bf16[256,1280]{1,0:T(8,128)(2,1)S(1)} %broadcast_select_fusion.3, bf16[1280,4096]{1,0:T(8,128)(2,1)} %param.12), kind=kOutput, calls=%fused_computation.4 | convolution fusion | flops 2686451712 | bytes 13238272 | tf_op jit(solution)/shard_map/dot_general | solution.py:172
  32.0 3.1 %fusion.1 = f16[256,4096]{1,0:T(8,128)(2,1)S(1)} fusion(bf16[256,1280]{1,0:T(8,128)(2,1)S(1)} %broadcast_select_fusion.3, bf16[1280,4096]{1,0:T(8,128)(2,1)S(1)} %bitcast.109), kind=kOutput, calls=%fused_computation.5 | convolution fusion | flops 2686451712 | bytes 13238272 | tf_op jit(solution)/shard_map/dot_general | solution.py:172
  35.1 1.3 collective-permute-start.3
  37.1 24.6 %collective-permute-start.10 = (bf16[256,1280]{1,0:T(8,128)(2,1)S(1)}, bf16[256,1280]{1,0:T(8,128)(2,1)S(1)}, u32[]{:S(2)}, u32[]{:S(2)}) collective-permute-start(bf16[256,1280]{1,0:T(8,128)(2,1)S(1)} %bitcast.97), channel_id=1, source_target_pairs={{0,8},{1,12},{4,9},{5,13},{10,2},{11,6},{14,3},{15,7},{16,24},{17,... | collective-permute-start | bytes 1966088 | tf_op jit(solution)/shard_map/ppermute | solution.py:65
  61.7 1.2 broadcast_select_fusion.2
  62.9 3.1 %fusion.2 = f16[256,4096]{1,0:T(8,128)(2,1)S(1)} fusion(bf16[256,1280]{1,0:T(8,128)(2,1)S(1)} %broadcast_select_fusion.2, bf16[1280,4096]{1,0:T(8,128)(2,1)S(1)} %bitcast.109), kind=kOutput, calls=%fused_computation.6 | convolution fusion | flops 2686451712 | bytes 13238272 | tf_op jit(solution)/shard_map/dot_general | solution.py:172
  67.1 7.2 %fusion.3 = f16[256,4096]{1,0:T(8,128)(2,1)S(1)} fusion(bf16[256,1280]{1,0:T(8,128)(2,1)S(1)} %broadcast_select_fusion.2, bf16[1280,4096]{1,0:T(8,128)(2,1)} %param.12), kind=kOutput, calls=%fused_computation.7 | convolution fusion | flops 2686451712 | bytes 13238272 | tf_op jit(solution)/shard_map/dot_general | solution.py:172
  75.8 1.9 %fusion.4 = f16[2,256,2048]{2,1,0:T(8,128)(2,1)} fusion(f32[1,256,2048]{2,1,0:T(8,128)S(1)} %multiply_bitcast_fusion, f32[1,256,2048]{2,1,0:T(8,128)S(1)} %multiply_bitcast_fusion.1), kind=kLoop, calls=%fused_computation.9 | loop fusion | flops 3145728 | bytes 6291456 | tf_op jit(solution)/shard_map/convert_element_type | solution.py:19
  78.0 1.4 slice-done.1
  80.0 7.5 %shard_map.113 = f32[512,4096]{1,0:T(8,128)S(1)} custom-call(bf16[512,1280]{1,0:T(8,128)(2,1)S(1)} %pad_maximum_fusion.tokens_ref, bf16[4096,1280]{1,0:T(8,128)(2,1)S(1)} %bitcast.92), custom_call_target="tpu_custom_call" | custom-call | flops 1 | bytes 1 | tf_op jit(solution)/shard_map/pallas_call | solution.py:95
  87.7 8.7 %collective-permute-start.13 = (f16[256,2048]{1,0:T(8,128)(2,1)S(1)}, f16[256,2048]{1,0:T(8,128)(2,1)S(1)}, u32[]{:S(2)}, u32[]{:S(2)}) collective-permute-start(f16[256,2048]{1,0:T(8,128)(2,1)S(1)} %multiply_convert_fusion.2), channel_id=1, source_target_pairs={{0,1},{1,0},{2,3},{3,2},{4,5},{5,4},{6,7},{7,6},{8,9},{9,8},{10,11... | collective-permute-start | bytes 3145736 | tf_op jit(solution)/shard_map/ppermute | solution.py:15
  96.8 1.2 constant_dynamic-slice_fusion.3
  98.0 1.1 collective-permute-start.15
  99.1 1.4 multiply_convert_fusion.1
  101.6 3.7 %collective-permute-start.19 = (f16[256,192]{0,1:T(8,128)(2,1)S(1)}, f16[256,192]{0,1:T(8,128)(2,1)}, u32[]{:S(2)}, u32[]{:S(2)}) collective-permute-start(f16[256,192]{0,1:T(8,128)(2,1)S(1)} %multiply_convert_fusion.5), channel_id=1, source_target_pairs={{0,12},{4,0},{8,4},{12,8},{1,13},{5,1},{9,5},{13,9},{2,14},{6,2},{... | collective-permute-start | bytes 294920 | tf_op jit(solution)/shard_map/ppermute | solution.py:15
  105.4 2.7 %collective-permute-done.17 = f16[256,192]{0,1:T(8,128)(2,1)S(1)} collective-permute-done((f16[256,192]{0,1:T(8,128)(2,1)S(1)}, f16[256,192]{0,1:T(8,128)(2,1)S(1)}, u32[]{:S(2)}, u32[]{:S(2)}) %collective-permute-start.17) | collective-permute-done | bytes 98336 | tf_op jit(solution)/shard_map/ppermute | solution.py:15
  108.1 3.4 %collective-permute-done.18 = f16[256,192]{0,1:T(8,128)(2,1)} collective-permute-done((f16[256,192]{0,1:T(8,128)(2,1)S(1)}, f16[256,192]{0,1:T(8,128)(2,1)}, u32[]{:S(2)}, u32[]{:S(2)}) %collective-permute-start.18) | collective-permute-done | bytes 98336 | tf_op jit(solution)/shard_map/ppermute | solution.py:15
  111.5 14.7 %collective-permute-done.11 = f16[2,256,2048]{2,1,0:T(8,128)(2,1)} collective-permute-done((f16[2,256,2048]{2,1,0:T(8,128)(2,1)}, f16[2,256,2048]{2,1,0:T(8,128)(2,1)}, u32[]{:S(2)}, u32[]{:S(2)}) %collective-permute-start.11) | collective-permute-done | bytes 2097184 | tf_op jit(solution)/shard_map/ppermute | solution.py:15
  126.2 1.7 multiply_add_fusion.2
  127.9 1.1 copy.17
  129.3 1.9 %multiply_convert_fusion.3 = f16[256,2048]{1,0:T(8,128)(2,1)S(1)} fusion(f32[512,4096]{1,0:T(8,128)} %copy-done.1, s32[]{:T(128)S(6)} %select_n.64), kind=kLoop, calls=%fused_computation.22 | loop fusion | flops 1048576 | bytes 3145732 | tf_op jit(solution)/shard_map/convert_element_type | solution.py:19
  132.0 3.8 %fusion.7 = (f32[256,2048]{1,0:T(8,128)S(1)}, f32[256,2048]{1,0:T(8,128)S(1)}) fusion(f16[256,2048]{1,0:T(8,128)(2,1)S(1)} %copy-done.8, f16[2,256,2048]{2,1,0:T(8,128)(2,1)} %collective-permute-done.11, f16[256,4096]{1,0:T(8,128)(2,1)} %copy-done.6, s32[]{:T(128)S(6)} %select_n.62, f16[256,2048]{1,0:T(8,128)(2,1)} %collective-permute-done.15, ...), kind=kLoop, calls=%fused_computation.17 | loop fusion | flops 11010048 | bytes 10485764 | tf_op jit(solution)/shard_map/mul | solution.py:257
  135.8 2.3 %fusion.8 = f32[256,64]{0,1:T(8,128)S(1)} fusion(f32[256,2048]{1,0:T(8,128)S(1)} %get-tuple-element.40.refs_1_, f16[256,2048]{1,0:T(8,128)(2,1)} %collective-permute-done.15, f16[2,256,2048]{2,1,0:T(8,128)(2,1)} %collective-permute-done.11, f16[256,4096]{1,0:T(8,128)(2,1)S(1)} %copy-done.5, s32[]{:T(128)S(6)} %select_n.62, bf16[4096,192]{0,1:T(8,128)(2,1)} %param.16, ...), kind=kOutput, calls=%fused_computation.30 | convolution fusion | flops 71303168 | bytes 5572096 | tf_op jit(solution)/shard_map/dot_general | solution.py:260
  138.5 1.9 %multiply_add_fusion.1 = f32[256,2048]{1,0:T(8,128)S(1)} fusion(f16[256,2048]{1,0:T(8,128)(2,1)S(1)} %collective-permute-done.12, f32[512,4096]{1,0:T(8,128)} %copy-done.1, s32[]{:T(128)S(6)} %select_n.62), kind=kLoop, calls=%fused_computation.21 | loop fusion | flops 1572864 | bytes 5242884 | tf_op jit(solution)/shard_map/add | solution.py:186
  140.4 8.3 %collective-permute-done.14 = f16[256,2048]{1,0:T(8,128)(2,1)} collective-permute-done((f16[256,2048]{1,0:T(8,128)(2,1)}, f16[256,2048]{1,0:T(8,128)(2,1)}, u32[]{:S(2)}, u32[]{:S(2)}) %collective-permute-start.14) | collective-permute-done | bytes 1048608 | tf_op jit(solution)/shard_map/ppermute | solution.py:15
  148.7 1.6 multiply_add_fusion.down_ref
  150.3 1.2 shard_map.114
  151.6 2.6 %collective-permute-start.21 = (f32[6,16,64]{2,1,0:T(8,128)S(1)}, f32[6,16,64]{2,1,0:T(8,128)}, u32[]{:S(2)}, u32[]{:S(2)}) collective-permute-start(f32[6,16,64]{2,1,0:T(8,128)S(1)} %get-tuple-element.48), channel_id=1, source_target_pairs={{0,8},{4,12},{8,0},{12,4},{1,9},{5,13},{9,1},{13,5},{2,10},{6,14},... | collective-permute-start | bytes 73736 | tf_op jit(solution)/shard_map/ppermute | solution.py:15
  154.2 1.2 collective-permute-start.22
  155.4 2.7 %collective-permute-done.20 = f32[6,16,64]{2,1,0:T(8,128)} collective-permute-done((f32[6,16,64]{2,1,0:T(8,128)S(1)}, f32[6,16,64]{2,1,0:T(8,128)}, u32[]{:S(2)}, u32[]{:S(2)}) %collective-permute-start.20) | collective-permute-done | bytes 24608 | tf_op jit(solution)/shard_map/ppermute | solution.py:15
  158.1 1.2 collective-permute-done.21
  160.2 1.5 collective-permute-start.23
  162.1 2.3 %collective-permute-done.23 = f32[6,16,64]{2,1,0:T(8,128)S(1)} collective-permute-done((f32[6,16,64]{2,1,0:T(8,128)S(1)}, f32[6,16,64]{2,1,0:T(8,128)S(1)}, u32[]{:S(2)}, u32[]{:S(2)}) %collective-permute-start.23) | collective-permute-done | bytes 24608 | tf_op jit(solution)/shard_map/ppermute | solution.py:280
  164.4 1.1 collective-permute-done.24
  165.6 1.3 fusion.25
  166.9 2.2 %collective-permute-start.26 = (f32[4,512]{1,0:T(4,128)S(1)}, f32[4,512]{1,0:T(4,128)S(1)}, u32[]{:S(2)}, u32[]{:S(2)}) collective-permute-start(f32[4,512]{1,0:T(4,128)S(1)} %fusion.25), channel_id=1, source_target_pairs={{0,12},{4,0},{8,4},{12,8},{1,13},{5,1},{9,5},{13,9},{2,14},{6,2},{... | collective-permute-start | bytes 24584 | tf_op jit(solution)/shard_map/ppermute | solution.py:15
  170.6 3.2 %collective-permute-done.27 = f32[4,512]{1,0:T(4,128)S(1)} collective-permute-done((f32[4,512]{1,0:T(4,128)S(1)}, f32[4,512]{1,0:T(4,128)S(1)}, u32[]{:S(2)}, u32[]{:S(2)}) %collective-permute-start.27) | collective-permute-done | bytes 8224 | tf_op jit(solution)/shard_map/ppermute | solution.py:15
  173.8 1.4 collective-permute-done.28
  (110 shorter events, 12.0 us)
Async XLA Ops:
  0.6 165.0 %copy-start = (bf16[3,16,64,512]{3,2,1,0:T(8,128)(2,1)S(1)}, bf16[3,16,64,512]{3,2,1,0:T(8,128)(2,1)}, u32[]{:S(2)}) copy-start(bf16[3,16,64,512]{3,2,1,0:T(8,128)(2,1)} %param.17) | copy-start | bytes 9437188
  0.6 22.6 %collective-permute-start = (bf16[256,1280]{1,0:T(8,128)(2,1)}, bf16[256,1280]{1,0:T(8,128)(2,1)}, u32[]{:S(2)}, u32[]{:S(2)}) collective-permute-start(bf16[256,1280]{1,0:T(8,128)(2,1)} %bitcast.99), channel_id=1, source_target_pairs={{2,0},{3,4},{6,1},{7,5},{8,10},{9,14},{12,11},{13,15},{18,16},{19,... | collective-permute-start | bytes 1966088 | tf_op jit(solution)/shard_map/ppermute | solution.py:65
  2.2 21.0 %collective-permute-start.1 = (bf16[256,1280]{1,0:T(8,128)(2,1)}, bf16[256,1280]{1,0:T(8,128)(2,1)}, u32[]{:S(2)}, u32[]{:S(2)}) collective-permute-start(bf16[256,1280]{1,0:T(8,128)(2,1)} %bitcast.100), channel_id=1, source_target_pairs={{2,8},{3,12},{6,9},{7,13},{8,2},{9,6},{12,3},{13,7},{18,24},{19,28... | collective-permute-start | bytes 1966088 | tf_op jit(solution)/shard_map/ppermute | solution.py:65
  3.7 58.0 %collective-permute-start.6 = (bf16[256,1280]{1,0:T(8,128)(2,1)}, bf16[256,1280]{1,0:T(8,128)(2,1)}, u32[]{:S(2)}, u32[]{:S(2)}) collective-permute-start(bf16[256,1280]{1,0:T(8,128)(2,1)} %bitcast.101), channel_id=1, source_target_pairs={{0,0},{1,4},{4,1},{5,5},{10,10},{11,14},{14,11},{15,15},{16,16},{1... | collective-permute-start | bytes 1966088 | tf_op jit(solution)/shard_map/ppermute | solution.py:65
  10.2 51.5 %collective-permute-start.7 = (bf16[256,1280]{1,0:T(8,128)(2,1)}, bf16[256,1280]{1,0:T(8,128)(2,1)}, u32[]{:S(2)}, u32[]{:S(2)}) collective-permute-start(bf16[256,1280]{1,0:T(8,128)(2,1)} %bitcast.102), channel_id=1, source_target_pairs={{0,8},{1,12},{4,9},{5,13},{10,2},{11,6},{14,3},{15,7},{16,24},{17,... | collective-permute-start | bytes 1966088 | tf_op jit(solution)/shard_map/ppermute | solution.py:65
  15.4 7.8 %collective-permute-start.2 = (s32[2]{0:T(128)}, s32[2]{0:T(128)S(1)}, u32[]{:S(2)}, u32[]{:S(2)}) collective-permute-start(s32[2]{0:T(128)} %param.19), channel_id=1, source_target_pairs={{0,2},{2,0},{1,3},{3,1},{4,6},{6,4},{5,7},{7,5},{8,10},{10,8},{9,1... | collective-permute-start | bytes 32 | tf_op jit(solution)/shard_map/ppermute | solution.py:15
  15.5 7.7 %copy-start.10 = (s32[2]{0:T(128)S(1)}, s32[2]{0:T(128)}, u32[]{:S(2)}) copy-start(s32[2]{0:T(128)} %param.19) | copy-start | bytes 28
  23.2 8.7 %slice-start.3 = ((s8[10485760]{0:T(1024)(128)(4,1)}), s8[4194304]{0:T(1024)(128)(4,1)S(1)}, s32[]{:S(2)}) async-start(s8[10485760]{0:T(1024)(128)(4,1)} %bitcast.108), calls=%async_computation.3 | async-start | bytes 8388608
  24.6 7.4 %slice-start.4 = ((s8[10485760]{0:T(1024)(128)(4,1)}), s8[4194304]{0:T(1024)(128)(4,1)S(1)}, s32[]{:S(2)}) async-start(s8[10485760]{0:T(1024)(128)(4,1)} %bitcast.108), calls=%async_computation.4 | async-start | bytes 8388608
  24.6 7.4 %slice-start.5 = ((s8[10485760]{0:T(1024)(128)(4,1)}), s8[2097152]{0:T(1024)(128)(4,1)S(1)}, s32[]{:S(2)}) async-start(s8[10485760]{0:T(1024)(128)(4,1)} %bitcast.108), calls=%async_computation.5 | async-start | bytes 4194304
  32.0 3.1 %copy-start.9 = (bf16[2,128,1280]{2,1,0:T(8,128)(2,1)S(1)}, bf16[2,128,1280]{2,1,0:T(8,128)(2,1)}, u32[]{:S(2)}) copy-start(bf16[2,128,1280]{2,1,0:T(8,128)(2,1)} %param.11) | copy-start | bytes 1966084
  35.1 42.6 %collective-permute-start.3 = (bf16[256,1280]{1,0:T(8,128)(2,1)S(1)}, bf16[256,1280]{1,0:T(8,128)(2,1)S(1)}, u32[]{:S(2)}, u32[]{:S(2)}) collective-permute-start(bf16[256,1280]{1,0:T(8,128)(2,1)S(1)} %bitcast.95), channel_id=1, source_target_pairs={{2,0},{3,4},{6,1},{7,5},{8,10},{9,14},{12,11},{13,15},{18,16},{19,... | collective-permute-start | bytes 1966088 | tf_op jit(solution)/shard_map/ppermute | solution.py:65
  36.4 41.3 %collective-permute-start.4 = (bf16[256,1280]{1,0:T(8,128)(2,1)S(1)}, bf16[256,1280]{1,0:T(8,128)(2,1)S(1)}, u32[]{:S(2)}, u32[]{:S(2)}) collective-permute-start(bf16[256,1280]{1,0:T(8,128)(2,1)S(1)} %bitcast.96), channel_id=1, source_target_pairs={{2,8},{3,12},{6,9},{7,13},{8,2},{9,6},{12,3},{13,7},{18,24},{19,28... | collective-permute-start | bytes 1966088 | tf_op jit(solution)/shard_map/ppermute | solution.py:65
  37.1 40.6 %collective-permute-start.10 = (bf16[256,1280]{1,0:T(8,128)(2,1)S(1)}, bf16[256,1280]{1,0:T(8,128)(2,1)S(1)}, u32[]{:S(2)}, u32[]{:S(2)}) collective-permute-start(bf16[256,1280]{1,0:T(8,128)(2,1)S(1)} %bitcast.97), channel_id=1, source_target_pairs={{0,8},{1,12},{4,9},{5,13},{10,2},{11,6},{14,3},{15,7},{16,24},{17,... | collective-permute-start | bytes 1966088 | tf_op jit(solution)/shard_map/ppermute | solution.py:65
  66.0 30.8 %copy-start.4 = (f16[256,4096]{1,0:T(8,128)(2,1)}, f16[256,4096]{1,0:T(8,128)(2,1)S(1)}, u32[]{:S(2)}) copy-start(f16[256,4096]{1,0:T(8,128)(2,1)S(1)} %fusion.2) | copy-start | bytes 6291460
  66.2 8.1 %collective-permute-start.5 = (f16[256,2048]{1,0:T(8,128)(2,1)S(1)}, f16[256,2048]{1,0:T(8,128)(2,1)S(1)}, u32[]{:S(2)}, u32[]{:S(2)}) collective-permute-start(f16[256,2048]{1,0:T(8,128)(2,1)S(1)} %constant_dynamic-slice_fusion.5), channel_id=1, source_target_pairs={{0,1},{1,0},{2,3},{3,2},{4,5},{5,4},{6,7},{7,6},{8,9},{9,8},{10,11... | collective-permute-start | bytes 3145736 | tf_op jit(solution)/shard_map/ppermute | solution.py:15
  66.5 8.9 %collective-permute-start.8 = (f16[256,2048]{1,0:T(8,128)(2,1)S(1)}, f16[256,2048]{1,0:T(8,128)(2,1)S(1)}, u32[]{:S(2)}, u32[]{:S(2)}) collective-permute-start(f16[256,2048]{1,0:T(8,128)(2,1)S(1)} %constant_dynamic-slice_fusion.4), channel_id=1, source_target_pairs={{0,1},{1,0},{2,3},{3,2},{4,5},{5,4},{6,7},{7,6},{8,9},{9,8},{10,11... | collective-permute-start | bytes 3145736 | tf_op jit(solution)/shard_map/ppermute | solution.py:15
  74.3 22.2 %copy-start.6 = (f16[256,4096]{1,0:T(8,128)(2,1)}, f16[256,4096]{1,0:T(8,128)(2,1)S(1)}, u32[]{:S(2)}) copy-start(f16[256,4096]{1,0:T(8,128)(2,1)S(1)} %fusion.3) | copy-start | bytes 6291460
  74.3 3.4 %collective-permute-start.9 = (bf16[256,1280]{1,0:T(8,128)(2,1)S(1)}, bf16[256,1280]{1,0:T(8,128)(2,1)S(1)}, u32[]{:S(2)}, u32[]{:S(2)}) collective-permute-start(bf16[256,1280]{1,0:T(8,128)(2,1)S(1)} %bitcast.98), channel_id=1, source_target_pairs={{0,0},{1,4},{4,1},{5,5},{10,10},{11,14},{14,11},{15,15},{16,16},{1... | collective-permute-start | bytes 1966088 | tf_op jit(solution)/shard_map/ppermute | solution.py:65
  75.0 3.0 %slice-start = ((s8[10485760]{0:T(1024)(128)(4,1)}), s8[4194304]{0:T(1024)(128)(4,1)S(1)}, s32[]{:S(2)}) async-start(s8[10485760]{0:T(1024)(128)(4,1)} %bitcast.91), calls=%async_computation | async-start | bytes 8388608
  75.4 3.9 %slice-start.1 = ((s8[10485760]{0:T(1024)(128)(4,1)}), s8[4194304]{0:T(1024)(128)(4,1)S(1)}, s32[]{:S(2)}) async-start(s8[10485760]{0:T(1024)(128)(4,1)} %bitcast.91), calls=%async_computation.1 | async-start | bytes 8388608
  75.8 4.2 %slice-start.2 = ((s8[10485760]{0:T(1024)(128)(4,1)}), s8[2097152]{0:T(1024)(128)(4,1)S(1)}, s32[]{:S(2)}) async-start(s8[10485760]{0:T(1024)(128)(4,1)} %bitcast.91), calls=%async_computation.2 | async-start | bytes 4194304
  77.7 48.5 %collective-permute-start.11 = (f16[2,256,2048]{2,1,0:T(8,128)(2,1)}, f16[2,256,2048]{2,1,0:T(8,128)(2,1)}, u32[]{:S(2)}, u32[]{:S(2)}) collective-permute-start(f16[2,256,2048]{2,1,0:T(8,128)(2,1)} %fusion.4), channel_id=1, source_target_pairs={{0,2},{2,0},{1,3},{3,1},{4,6},{6,4},{5,7},{7,5},{8,10},{10,8},{9,1... | collective-permute-start | bytes 6291464 | tf_op jit(solution)/shard_map/ppermute | solution.py:15
  87.5 11.6 %copy-start.1 = (f32[512,4096]{1,0:T(8,128)}, f32[512,4096]{1,0:T(8,128)S(1)}, u32[]{:S(2)}) copy-start(f32[512,4096]{1,0:T(8,128)S(1)} %shard_map.113) | copy-start | bytes 25165828
  87.7 11.4 %collective-permute-start.13 = (f16[256,2048]{1,0:T(8,128)(2,1)S(1)}, f16[256,2048]{1,0:T(8,128)(2,1)S(1)}, u32[]{:S(2)}, u32[]{:S(2)}) collective-permute-start(f16[256,2048]{1,0:T(8,128)(2,1)S(1)} %multiply_convert_fusion.2), channel_id=1, source_target_pairs={{0,1},{1,0},{2,3},{3,2},{4,5},{5,4},{6,7},{7,6},{8,9},{9,8},{10,11... | collective-permute-start | bytes 3145736 | tf_op jit(solution)/shard_map/ppermute | solution.py:15
  96.7 3.9 %collective-permute-start.16 = (f16[256,2048]{1,0:T(8,128)(2,1)S(1)}, f16[256,2048]{1,0:T(8,128)(2,1)S(1)}, u32[]{:S(2)}, u32[]{:S(2)}) collective-permute-start(f16[256,2048]{1,0:T(8,128)(2,1)S(1)} %constant_dynamic-slice_fusion.2), channel_id=1, source_target_pairs={{0,1},{1,0},{2,3},{3,2},{4,5},{5,4},{6,7},{7,6},{8,9},{9,8},{10,11... | collective-permute-start | bytes 3145736 | tf_op jit(solution)/shard_map/ppermute | solution.py:15
  98.0 7.5 %collective-permute-start.15 = (f16[256,2048]{1,0:T(8,128)(2,1)}, f16[256,2048]{1,0:T(8,128)(2,1)}, u32[]{:S(2)}, u32[]{:S(2)}) collective-permute-start(f16[256,2048]{1,0:T(8,128)(2,1)} %constant_dynamic-slice_fusion.3), channel_id=1, source_target_pairs={{0,1},{1,0},{2,3},{3,2},{4,5},{5,4},{6,7},{7,6},{8,9},{9,8},{10,11... | collective-permute-start | bytes 3145736 | tf_op jit(solution)/shard_map/ppermute | solution.py:15
  99.1 6.3 %copy-start.11 = (s32[2]{0:T(128)S(1)}, s32[2]{0:T(128)}, u32[]{:S(2)}) copy-start(s32[2]{0:T(128)} %param.18) | copy-start | bytes 28
  100.5 7.6 %collective-permute-start.17 = (f16[256,192]{0,1:T(8,128)(2,1)S(1)}, f16[256,192]{0,1:T(8,128)(2,1)S(1)}, u32[]{:S(2)}, u32[]{:S(2)}) collective-permute-start(f16[256,192]{0,1:T(8,128)(2,1)S(1)} %multiply_convert_fusion.5), channel_id=1, source_target_pairs={{0,4},{4,8},{8,12},{12,0},{1,5},{5,9},{9,13},{13,1},{2,6},{6,10},{... | collective-permute-start | bytes 294920 | tf_op jit(solution)/shard_map/ppermute | solution.py:15
  100.6 10.9 %collective-permute-start.18 = (f16[256,192]{0,1:T(8,128)(2,1)S(1)}, f16[256,192]{0,1:T(8,128)(2,1)}, u32[]{:S(2)}, u32[]{:S(2)}) collective-permute-start(f16[256,192]{0,1:T(8,128)(2,1)S(1)} %multiply_convert_fusion.5), channel_id=1, source_target_pairs={{0,8},{4,12},{8,0},{12,4},{1,9},{5,13},{9,1},{13,5},{2,10},{6,14},... | collective-permute-start | bytes 294920 | tf_op jit(solution)/shard_map/ppermute | solution.py:15
  100.6 1.0 copy-start.7
  101.6 9.9 %collective-permute-start.19 = (f16[256,192]{0,1:T(8,128)(2,1)S(1)}, f16[256,192]{0,1:T(8,128)(2,1)}, u32[]{:S(2)}, u32[]{:S(2)}) collective-permute-start(f16[256,192]{0,1:T(8,128)(2,1)S(1)} %multiply_convert_fusion.5), channel_id=1, source_target_pairs={{0,12},{4,0},{8,4},{12,8},{1,13},{5,1},{9,5},{13,9},{2,14},{6,2},{... | collective-permute-start | bytes 294920 | tf_op jit(solution)/shard_map/ppermute | solution.py:15
  105.4 43.3 %collective-permute-start.14 = (f16[256,2048]{1,0:T(8,128)(2,1)}, f16[256,2048]{1,0:T(8,128)(2,1)}, u32[]{:S(2)}, u32[]{:S(2)}) collective-permute-start(f16[256,2048]{1,0:T(8,128)(2,1)} %multiply_convert_fusion.1), channel_id=1, source_target_pairs={{0,2},{2,0},{1,3},{3,1},{4,6},{6,4},{5,7},{7,5},{8,10},{10,8},{9,1... | collective-permute-start | bytes 3145736 | tf_op jit(solution)/shard_map/ppermute | solution.py:15
  129.3 2.7 %copy-start.5 = (f16[256,4096]{1,0:T(8,128)(2,1)S(1)}, f16[256,4096]{1,0:T(8,128)(2,1)}, u32[]{:S(2)}) copy-start(f16[256,4096]{1,0:T(8,128)(2,1)} %copy-done.4) | copy-start | bytes 6291460
  129.3 2.7 %copy-start.8 = (f16[256,2048]{1,0:T(8,128)(2,1)S(1)}, f16[256,2048]{1,0:T(8,128)(2,1)}, u32[]{:S(2)}) copy-start(f16[256,2048]{1,0:T(8,128)(2,1)} %copy-done.7) | copy-start | bytes 3145732
  131.2 7.2 %collective-permute-start.12 = (f16[256,2048]{1,0:T(8,128)(2,1)S(1)}, f16[256,2048]{1,0:T(8,128)(2,1)S(1)}, u32[]{:S(2)}, u32[]{:S(2)}) collective-permute-start(f16[256,2048]{1,0:T(8,128)(2,1)S(1)} %multiply_convert_fusion.3), channel_id=1, source_target_pairs={{0,1},{1,0},{2,3},{3,2},{4,5},{5,4},{6,7},{7,6},{8,9},{9,8},{10,11... | collective-permute-start | bytes 3145736 | tf_op jit(solution)/shard_map/ppermute | solution.py:15
  140.4 9.9 %copy-start.2 = (bf16[2048,64]{1,0:T(8,128)(2,1)S(1)}, bf16[2048,64]{1,0:T(8,128)(2,1)}, u32[]{:S(2)}) copy-start(bf16[2048,64]{1,0:T(8,128)(2,1)} %copy.21.refs_2_) | copy-start | bytes 786436
  140.4 9.9 %copy-start.3 = (bf16[2048,64]{1,0:T(8,128)(2,1)S(1)}, bf16[2048,64]{1,0:T(8,128)(2,1)}, u32[]{:S(2)}) copy-start(bf16[2048,64]{1,0:T(8,128)(2,1)} %copy.22.refs_3_) | copy-start | bytes 786436
  151.6 6.5 %collective-permute-start.20 = (f32[6,16,64]{2,1,0:T(8,128)S(1)}, f32[6,16,64]{2,1,0:T(8,128)}, u32[]{:S(2)}, u32[]{:S(2)}) collective-permute-start(f32[6,16,64]{2,1,0:T(8,128)S(1)} %get-tuple-element.46), channel_id=1, source_target_pairs={{0,4},{4,8},{8,12},{12,0},{1,5},{5,9},{9,13},{13,1},{2,6},{6,10},{... | collective-permute-start | bytes 73736 | tf_op jit(solution)/shard_map/ppermute | solution.py:15
  151.6 7.7 %collective-permute-start.21 = (f32[6,16,64]{2,1,0:T(8,128)S(1)}, f32[6,16,64]{2,1,0:T(8,128)}, u32[]{:S(2)}, u32[]{:S(2)}) collective-permute-start(f32[6,16,64]{2,1,0:T(8,128)S(1)} %get-tuple-element.48), channel_id=1, source_target_pairs={{0,8},{4,12},{8,0},{12,4},{1,9},{5,13},{9,1},{13,5},{2,10},{6,14},... | collective-permute-start | bytes 73736 | tf_op jit(solution)/shard_map/ppermute | solution.py:15
  154.2 5.1 %collective-permute-start.22 = (f32[6,16,64]{2,1,0:T(8,128)S(1)}, f32[6,16,64]{2,1,0:T(8,128)}, u32[]{:S(2)}, u32[]{:S(2)}) collective-permute-start(f32[6,16,64]{2,1,0:T(8,128)S(1)} %get-tuple-element.47), channel_id=1, source_target_pairs={{0,12},{4,0},{8,4},{12,8},{1,13},{5,1},{9,5},{13,9},{2,14},{6,2},{... | collective-permute-start | bytes 73736 | tf_op jit(solution)/shard_map/ppermute | solution.py:15
  160.1 1.9 %collective-permute-start.25 = (f32[6,16,64]{2,1,0:T(8,128)S(1)}, f32[6,16,64]{2,1,0:T(8,128)S(1)}, u32[]{:S(2)}, u32[]{:S(2)}) collective-permute-start(f32[6,16,64]{2,1,0:T(8,128)S(1)} %fusion.19), channel_id=1, source_target_pairs={{0,1},{1,0},{2,3},{3,2},{4,5},{5,4},{6,7},{7,6},{8,9},{9,8},{10,11... | collective-permute-start | bytes 73736 | tf_op jit(solution)/shard_map/ppermute | solution.py:280
  160.2 4.2 %collective-permute-start.23 = (f32[6,16,64]{2,1,0:T(8,128)S(1)}, f32[6,16,64]{2,1,0:T(8,128)S(1)}, u32[]{:S(2)}, u32[]{:S(2)}) collective-permute-start(f32[6,16,64]{2,1,0:T(8,128)S(1)} %fusion.19), channel_id=1, source_target_pairs={{0,2},{1,3},{2,0},{3,1},{4,6},{5,7},{6,4},{7,5},{8,10},{9,11},{10,... | collective-permute-start | bytes 73736 | tf_op jit(solution)/shard_map/ppermute | solution.py:280
  161.8 3.7 %collective-permute-start.24 = (f32[6,16,64]{2,1,0:T(8,128)S(1)}, f32[6,16,64]{2,1,0:T(8,128)S(1)}, u32[]{:S(2)}, u32[]{:S(2)}) collective-permute-start(f32[6,16,64]{2,1,0:T(8,128)S(1)} %fusion.19), channel_id=1, source_target_pairs={{0,3},{1,2},{2,1},{3,0},{4,7},{5,6},{6,5},{7,4},{8,11},{9,10},{10,... | collective-permute-start | bytes 73736 | tf_op jit(solution)/shard_map/ppermute | solution.py:280
  166.9 3.7 %collective-permute-start.26 = (f32[4,512]{1,0:T(4,128)S(1)}, f32[4,512]{1,0:T(4,128)S(1)}, u32[]{:S(2)}, u32[]{:S(2)}) collective-permute-start(f32[4,512]{1,0:T(4,128)S(1)} %fusion.25), channel_id=1, source_target_pairs={{0,12},{4,0},{8,4},{12,8},{1,13},{5,1},{9,5},{13,9},{2,14},{6,2},{... | collective-permute-start | bytes 24584 | tf_op jit(solution)/shard_map/ppermute | solution.py:15
  169.2 4.6 %collective-permute-start.27 = (f32[4,512]{1,0:T(4,128)S(1)}, f32[4,512]{1,0:T(4,128)S(1)}, u32[]{:S(2)}, u32[]{:S(2)}) collective-permute-start(f32[4,512]{1,0:T(4,128)S(1)} %fusion.25), channel_id=1, source_target_pairs={{0,8},{4,12},{8,0},{12,4},{1,9},{5,13},{9,1},{13,5},{2,10},{6,14},... | collective-permute-start | bytes 24584 | tf_op jit(solution)/shard_map/ppermute | solution.py:15
  169.7 5.4 %collective-permute-start.28 = (f32[4,512]{1,0:T(4,128)S(1)}, f32[4,512]{1,0:T(4,128)S(1)}, u32[]{:S(2)}, u32[]{:S(2)}) collective-permute-start(f32[4,512]{1,0:T(4,128)S(1)} %fusion.25), channel_id=1, source_target_pairs={{0,4},{4,8},{8,12},{12,0},{1,5},{5,9},{9,13},{13,1},{2,6},{6,10},{... | collective-permute-start | bytes 24584 | tf_op jit(solution)/shard_map/ppermute | solution.py:15

commit v18 on v11

--- a/solution.py
+++ b/solution.py
@@ -214,12 +214,12 @@
     up_far = [forward(after(one, *gate_far), w_up) for one in acts_far]
     if direct:
         grad_all = spread_features(after(flat_grad, *up_far))
-    gate_near = forward(after(acts_near, *up_far), w_gate)
-    up_near = forward(after(acts_near, gate_near), w_up)
     for step, (gate, up) in enumerate(zip(gate_far, up_far), 1):
-        both = pack(jnp.stack([core_sum(gate, 0, up_near), core_sum(up, 0, up_near)]))
+        both = pack(jnp.stack([core_sum(gate, 0), core_sum(up, 0)]))
         received = shift(both, "example", step)
         arrived.append(received)
+    gate_near = forward(after(acts_near, both), w_gate)
+    up_near = forward(after(acts_near, gate_near), w_up)
     if direct:
         grad_all = arrived_features(grad_all, both)
     else:

time: 179 us -> 172 us (0.961)
  matrix products: 32.7 us -> 24.4 us
  waiting for transfers between devices: 41.1 us -> 45.6 us
  local copies, waits for them, and re-layouts: 12.5 us -> 9.87 us
    ppermute x4, waiting for transfers between devices: 0.29 us -> 10.3 us  [spread_features(): pieces.append(lax.ppermute(flat, ('tensor', 'example', 'test'), pairs))]
    dot_general x4, matrix products: 24.9 us -> 16.6 us  [forward(): return pack(jnp.dot(tokens, weight, preferred_element_type=F32))]
    ppermute x18, waiting for transfers between devices: 37.1 us -> 31.7 us  [shift(): return lax.ppermute(value, axis, [(i, (i + step) % n) for i in range(n)])]
    ppermute x4, starting transfers between devices: 29 us -> 24.4 us  [spread_features(): pieces.append(lax.ppermute(flat, ('tensor', 'example', 'test'), pairs))]
    ppermute x18, starting transfers between devices: 32.9 us -> 37.1 us  [shift(): return lax.ppermute(value, axis, [(i, (i + step) % n) for i in range(n)])]
    unnamed x41 -> x53, local copies, waits for them, and re-layouts: 6.27 us -> 4.06 us
where the time goes in v18:
time: 172 us; the launch traced here: 171 us
  starting transfers between devices  63.7 us (37%)
  waiting for transfers between devices  45.6 us (27%)
  matrix products  24.4 us (14%)
  other arithmetic  17.3 us (10%)
  local copies, waits for them, and re-layouts  9.87 us (6%)
  Pallas kernels  8.71 us (5%)
    ppermute x18, starting transfers between devices, shift(): return lax.ppermute(value, axis, [(i, (i + step) % n) for i in range(n)])  37.1 us
    ppermute x18, waiting for transfers between devices, shift(): return lax.ppermute(value, axis, [(i, (i + step) % n) for i in range(n)])  31.7 us
    ppermute x4, starting transfers between devices, spread_features(): pieces.append(lax.ppermute(flat, ('tensor', 'example', 'test'), pairs))  24.4 us
    dot_general x4, matrix products, forward(): return pack(jnp.dot(tokens, weight, preferred_element_type=F32))  16.6 us
    ppermute x4, waiting for transfers between devices, spread_features(): pieces.append(lax.ppermute(flat, ('tensor', 'example', 'test'), pairs))  10.3 us
    pallas_call x1, Pallas kernels, dot_rows(): pl.pallas_call(dot_rows_kernel, out_shape=jax.ShapeDtypeStruct((rows, hid...  7.51 us
    convert_element_type x5, other arithmetic, pack(): return (value * SEND_SCALE).astype(jnp.float16)  5.43 us
    mul x1, other arithmetic, on_device(): silu_gate = gate_act * sigmoid_gate  4.11 us
  transfers between devices with their start and end apart: 25, of which 13 were waited for; matrix products, arithmetic and copies ran while one was open for 21% of the time, Pallas kernels for 4%

profile of v18, /device:TPU:0, one launch (start us, length us, event | category | flops | bytes accessed | tf_op | source)
XLA Modules:
  0.0 170.8 jit_solution(2724644627751072665)
XLA Ops:
  0.6 4.1 %collective-permute-start = (bf16[256,1280]{1,0:T(8,128)(2,1)}, bf16[256,1280]{1,0:T(8,128)(2,1)}, u32[]{:S(2)}, u32[]{:S(2)}) collective-permute-start(bf16[256,1280]{1,0:T(8,128)(2,1)} %bitcast.97), channel_id=1, source_target_pairs={{0,8},{1,12},{2,0},{3,4},{4,9},{5,13},{6,1},{7,5},{10,2},{11,6},{8... | collective-permute-start | bytes 1966088 | tf_op jit(solution)/shard_map/ppermute | solution.py:66
  4.7 6.5 %collective-permute-start.1 = (bf16[256,1280]{1,0:T(8,128)(2,1)}, bf16[256,1280]{1,0:T(8,128)(2,1)}, u32[]{:S(2)}, u32[]{:S(2)}) collective-permute-start(bf16[256,1280]{1,0:T(8,128)(2,1)} %bitcast.98), channel_id=1, source_target_pairs={{0,0},{1,4},{2,8},{3,12},{4,1},{5,5},{6,9},{7,13},{10,10},{11,14},... | collective-permute-start | bytes 1966088 | tf_op jit(solution)/shard_map/ppermute | solution.py:66
  11.3 1.8 %fusion.24 = (bf16[2048,64]{0,1:T(8,128)(2,1)S(1)}, bf16[2048,64]{0,1:T(8,128)(2,1)}) fusion(bf16[4096,192]{0,1:T(8,128)(2,1)} %param.16, s32[]{:T(128)S(6)} %select_n.62, s32[]{:T(128)S(6)} %add.164), kind=kLoop, calls=%fused_computation.87 | loop fusion | bytes 1048584 | tf_op jit(solution)/shard_map/slice | solution.py:198
  13.1 2.0 %copy.21.refs_2_ = bf16[2048,64]{1,0:T(8,128)(2,1)} copy(bf16[2048,64]{0,1:T(8,128)(2,1)} %get-tuple-element.31) | data formatting | bytes 524288
  15.1 1.0 copy.22.refs_3_
  16.1 1.4 fusion.13
  17.5 1.6 fusion.10
  19.9 1.5 broadcast_select_fusion
  21.4 7.3 %fusion = f16[256,4096]{1,0:T(8,128)(2,1)S(1)} fusion(bf16[256,1280]{1,0:T(8,128)(2,1)S(1)} %get-tuple-element.17, bf16[1280,4096]{1,0:T(8,128)(2,1)} %param.12), kind=kOutput, calls=%fused_computation.4 | convolution fusion | flops 2686451712 | bytes 13238272 | tf_op jit(solution)/shard_map/dot_general | solution.py:174
  29.0 7.6 %collective-permute-start.5 = (f16[256,2048]{1,0:T(8,128)(2,1)S(1)}, f16[256,2048]{1,0:T(8,128)(2,1)S(1)}, u32[]{:S(2)}, u32[]{:S(2)}) collective-permute-start(f16[256,2048]{1,0:T(8,128)(2,1)S(1)} %constant_dynamic-slice_fusion.5), channel_id=1, source_target_pairs={{0,1},{1,0},{2,3},{3,2},{4,5},{5,4},{6,7},{7,6},{8,9},{9,8},{10,11... | collective-permute-start | bytes 3145736 | tf_op jit(solution)/shard_map/ppermute | solution.py:15
  36.6 3.1 %fusion.1 = f16[256,4096]{1,0:T(8,128)(2,1)S(1)} fusion(bf16[256,1280]{1,0:T(8,128)(2,1)S(1)} %get-tuple-element.17, bf16[1280,4096]{1,0:T(8,128)(2,1)S(1)} %bitcast.107), kind=kOutput, calls=%fused_computation.5 | convolution fusion | flops 2686451712 | bytes 13238272 | tf_op jit(solution)/shard_map/dot_general | solution.py:174
  40.8 13.1 %collective-permute-start.3 = (bf16[256,1280]{1,0:T(8,128)(2,1)S(1)}, bf16[256,1280]{1,0:T(8,128)(2,1)S(1)}, u32[]{:S(2)}, u32[]{:S(2)}) collective-permute-start(bf16[256,1280]{1,0:T(8,128)(2,1)S(1)} %bitcast.95), channel_id=1, source_target_pairs={{0,8},{1,12},{2,0},{3,4},{4,9},{5,13},{6,1},{7,5},{10,2},{11,6},{8... | collective-permute-start | bytes 1966088 | tf_op jit(solution)/shard_map/ppermute | solution.py:66
  55.4 1.9 %fusion.4 = f16[2,256,2048]{2,1,0:T(8,128)(2,1)} fusion(f32[1,256,2048]{2,1,0:T(8,128)S(1)} %multiply_bitcast_fusion, f32[1,256,2048]{2,1,0:T(8,128)S(1)} %multiply_bitcast_fusion.1), kind=kLoop, calls=%fused_computation.9 | loop fusion | flops 3145728 | bytes 6291456 | tf_op jit(solution)/shard_map/convert_element_type | solution.py:19
  57.2 2.8 %collective-permute-start.7 = (f16[2,256,2048]{2,1,0:T(8,128)(2,1)}, f16[2,256,2048]{2,1,0:T(8,128)(2,1)}, u32[]{:S(2)}, u32[]{:S(2)}) collective-permute-start(f16[2,256,2048]{2,1,0:T(8,128)(2,1)} %fusion.4), channel_id=1, source_target_pairs={{0,2},{2,0},{1,3},{3,1},{4,6},{6,4},{5,7},{7,5},{8,10},{10,8},{9,1... | collective-permute-start | bytes 6291464 | tf_op jit(solution)/shard_map/ppermute | solution.py:15
  60.1 3.1 %fusion.2 = f16[256,4096]{1,0:T(8,128)(2,1)S(1)} fusion(bf16[256,1280]{1,0:T(8,128)(2,1)S(1)} %get-tuple-element.23, bf16[1280,4096]{1,0:T(8,128)(2,1)S(1)} %bitcast.105), kind=kOutput, calls=%fused_computation.6 | convolution fusion | flops 2686451712 | bytes 13238272 | tf_op jit(solution)/shard_map/dot_general | solution.py:174
  63.2 10.0 %collective-permute-done.3 = bf16[256,1280]{1,0:T(8,128)(2,1)S(1)} collective-permute-done((bf16[256,1280]{1,0:T(8,128)(2,1)S(1)}, bf16[256,1280]{1,0:T(8,128)(2,1)S(1)}, u32[]{:S(2)}, u32[]{:S(2)}) %collective-permute-start.3) | collective-permute-done | bytes 655392 | tf_op jit(solution)/shard_map/ppermute | solution.py:66
  73.5 7.5 %shard_map.113 = f32[512,4096]{1,0:T(8,128)S(1)} custom-call(bf16[512,1280]{1,0:T(8,128)(2,1)S(1)} %pad_maximum_fusion.tokens_ref, bf16[4096,1280]{1,0:T(8,128)(2,1)S(1)} %bitcast.92), custom_call_target="tpu_custom_call" | custom-call | flops 1 | bytes 1 | tf_op jit(solution)/shard_map/pallas_call | solution.py:97
  81.2 2.2 %collective-permute-start.9 = (f16[256,2048]{1,0:T(8,128)(2,1)S(1)}, f16[256,2048]{1,0:T(8,128)(2,1)S(1)}, u32[]{:S(2)}, u32[]{:S(2)}) collective-permute-start(f16[256,2048]{1,0:T(8,128)(2,1)S(1)} %multiply_convert_fusion.2), channel_id=1, source_target_pairs={{0,1},{1,0},{2,3},{3,2},{4,5},{5,4},{6,7},{7,6},{8,9},{9,8},{10,11... | collective-permute-start | bytes 3145736 | tf_op jit(solution)/shard_map/ppermute | solution.py:15
  83.5 3.1 %fusion.3 = f16[256,4096]{1,0:T(8,128)(2,1)S(1)} fusion(bf16[256,1280]{1,0:T(8,128)(2,1)S(1)} %get-tuple-element.23, bf16[1280,4096]{1,0:T(8,128)(2,1)S(1)} %bitcast.109), kind=kOutput, calls=%fused_computation.7 | convolution fusion | flops 2686451712 | bytes 13238272 | tf_op jit(solution)/shard_map/dot_general | solution.py:174
  86.9 1.3 constant_dynamic-slice_fusion.2
  88.6 1.4 multiply_convert_fusion.1
  90.0 7.3 %collective-permute-start.13 = (f16[256,192]{0,1:T(8,128)(2,1)S(1)}, f16[256,192]{0,1:T(8,128)(2,1)S(1)}, u32[]{:S(2)}, u32[]{:S(2)}) collective-permute-start(f16[256,192]{0,1:T(8,128)(2,1)S(1)} %multiply_convert_fusion.5), channel_id=1, source_target_pairs={{0,4},{4,8},{8,12},{12,0},{1,5},{5,9},{9,13},{13,1},{2,6},{6,10},{... | collective-permute-start | bytes 294920 | tf_op jit(solution)/shard_map/ppermute | solution.py:15
  97.3 5.2 %collective-permute-start.14 = (f16[256,192]{0,1:T(8,128)(2,1)S(1)}, f16[256,192]{0,1:T(8,128)(2,1)}, u32[]{:S(2)}, u32[]{:S(2)}) collective-permute-start(f16[256,192]{0,1:T(8,128)(2,1)S(1)} %multiply_convert_fusion.5), channel_id=1, source_target_pairs={{0,8},{4,12},{8,0},{12,4},{1,9},{5,13},{9,1},{13,5},{2,10},{6,14},... | collective-permute-start | bytes 294920 | tf_op jit(solution)/shard_map/ppermute | solution.py:15
  102.4 2.3 %collective-permute-start.15 = (f16[256,192]{0,1:T(8,128)(2,1)S(1)}, f16[256,192]{0,1:T(8,128)(2,1)}, u32[]{:S(2)}, u32[]{:S(2)}) collective-permute-start(f16[256,192]{0,1:T(8,128)(2,1)S(1)} %multiply_convert_fusion.5), channel_id=1, source_target_pairs={{0,12},{4,0},{8,4},{12,8},{1,13},{5,1},{9,5},{13,9},{2,14},{6,2},{... | collective-permute-start | bytes 294920 | tf_op jit(solution)/shard_map/ppermute | solution.py:15
  104.8 1.0 collective-permute-start.10
  105.8 3.6 %collective-permute-done.14 = f16[256,192]{0,1:T(8,128)(2,1)} collective-permute-done((f16[256,192]{0,1:T(8,128)(2,1)S(1)}, f16[256,192]{0,1:T(8,128)(2,1)}, u32[]{:S(2)}, u32[]{:S(2)}) %collective-permute-start.14) | collective-permute-done | bytes 98336 | tf_op jit(solution)/shard_map/ppermute | solution.py:15
  109.4 10.1 %collective-permute-done.7 = f16[2,256,2048]{2,1,0:T(8,128)(2,1)} collective-permute-done((f16[2,256,2048]{2,1,0:T(8,128)(2,1)}, f16[2,256,2048]{2,1,0:T(8,128)(2,1)}, u32[]{:S(2)}, u32[]{:S(2)}) %collective-permute-start.7) | collective-permute-done | bytes 2097184 | tf_op jit(solution)/shard_map/ppermute | solution.py:15
  119.5 1.7 multiply_add_fusion.1
  121.2 1.1 copy.17
  122.6 1.9 %multiply_convert_fusion.3 = f16[256,2048]{1,0:T(8,128)(2,1)S(1)} fusion(f32[512,4096]{1,0:T(8,128)} %copy-done.1, s32[]{:T(128)S(6)} %select_n.64), kind=kLoop, calls=%fused_computation.21 | loop fusion | flops 1048576 | bytes 3145732 | tf_op jit(solution)/shard_map/convert_element_type | solution.py:19
  124.8 4.1 %fusion.7 = (f32[256,2048]{1,0:T(8,128)S(1)}, f32[256,2048]{1,0:T(8,128)S(1)}) fusion(f16[256,2048]{1,0:T(8,128)(2,1)} %collective-permute-done.12, f16[2,256,2048]{2,1,0:T(8,128)(2,1)} %collective-permute-done.7, f16[256,4096]{1,0:T(8,128)(2,1)} %copy-done.6, s32[]{:T(128)S(6)} %select_n.62, f16[256,2048]{1,0:T(8,128)(2,1)} %collective-permute-done.11, ...), kind=kLoop, calls=%fused_computation.17 | loop fusion | flops 11010048 | bytes 10485764 | tf_op jit(solution)/shard_map/mul | solution.py:258
  128.9 2.3 %fusion.8 = f32[256,64]{0,1:T(8,128)S(1)} fusion(f32[256,2048]{1,0:T(8,128)S(1)} %get-tuple-element.28.refs_1_, f16[256,2048]{1,0:T(8,128)(2,1)} %collective-permute-done.11, f16[2,256,2048]{2,1,0:T(8,128)(2,1)} %collective-permute-done.7, f16[256,4096]{1,0:T(8,128)(2,1)S(1)} %copy-done.5, s32[]{:T(128)S(6)} %select_n.62, bf16[4096,192]{0,1:T(8,128)(2,1)} %param.16, ...), kind=kOutput, calls=%fused_computation.29 | convolution fusion | flops 71303168 | bytes 5572096 | tf_op jit(solution)/shard_map/dot_general | solution.py:261
  131.6 9.6 %collective-permute-done.10 = f16[256,2048]{1,0:T(8,128)(2,1)} collective-permute-done((f16[256,2048]{1,0:T(8,128)(2,1)}, f16[256,2048]{1,0:T(8,128)(2,1)}, u32[]{:S(2)}, u32[]{:S(2)}) %collective-permute-start.10) | collective-permute-done | bytes 1048608 | tf_op jit(solution)/shard_map/ppermute | solution.py:15
  141.2 2.5 %multiply_add_fusion.down_ref = f32[256,2048]{1,0:T(8,128)S(1)} fusion(f16[256,2048]{1,0:T(8,128)(2,1)} %collective-permute-done.10, f16[256,2048]{1,0:T(8,128)(2,1)S(1)} %collective-permute-done.8, f32[512,4096]{1,0:T(8,128)} %copy-done.1, s32[]{:T(128)S(6)} %select_n.62), kind=kLoop, calls=%fused_computation.18 | loop fusion | flops 3145728 | bytes 6291460 | tf_op jit(solution)/shard_map/add | solution.py:256
  143.7 1.2 shard_map.114
  145.0 2.4 %collective-permute-start.17 = (f32[6,16,64]{2,1,0:T(8,128)S(1)}, f32[6,16,64]{2,1,0:T(8,128)}, u32[]{:S(2)}, u32[]{:S(2)}) collective-permute-start(f32[6,16,64]{2,1,0:T(8,128)S(1)} %get-tuple-element.40), channel_id=1, source_target_pairs={{0,8},{4,12},{8,0},{12,4},{1,9},{5,13},{9,1},{13,5},{2,10},{6,14},... | collective-permute-start | bytes 73736 | tf_op jit(solution)/shard_map/ppermute | solution.py:15
  147.4 2.0 %collective-permute-start.18 = (f32[6,16,64]{2,1,0:T(8,128)S(1)}, f32[6,16,64]{2,1,0:T(8,128)}, u32[]{:S(2)}, u32[]{:S(2)}) collective-permute-start(f32[6,16,64]{2,1,0:T(8,128)S(1)} %get-tuple-element.39), channel_id=1, source_target_pairs={{0,12},{4,0},{8,4},{12,8},{1,13},{5,1},{9,5},{13,9},{2,14},{6,2},{... | collective-permute-start | bytes 73736 | tf_op jit(solution)/shard_map/ppermute | solution.py:15
  149.3 2.0 %collective-permute-done.16 = f32[6,16,64]{2,1,0:T(8,128)} collective-permute-done((f32[6,16,64]{2,1,0:T(8,128)S(1)}, f32[6,16,64]{2,1,0:T(8,128)}, u32[]{:S(2)}, u32[]{:S(2)}) %collective-permute-start.16) | collective-permute-done | bytes 24608 | tf_op jit(solution)/shard_map/ppermute | solution.py:15
  151.4 0.7 collective-permute-done.17
  152.1 0.9 fusion.19
  153.1 2.0 %collective-permute-start.19 = (f32[6,16,64]{2,1,0:T(8,128)S(1)}, f32[6,16,64]{2,1,0:T(8,128)S(1)}, u32[]{:S(2)}, u32[]{:S(2)}) collective-permute-start(f32[6,16,64]{2,1,0:T(8,128)S(1)} %fusion.19), channel_id=1, source_target_pairs={{0,2},{1,3},{2,0},{3,1},{4,6},{5,7},{6,4},{7,5},{8,10},{9,11},{10,... | collective-permute-start | bytes 73736 | tf_op jit(solution)/shard_map/ppermute | solution.py:281
  155.2 2.3 %collective-permute-done.19 = f32[6,16,64]{2,1,0:T(8,128)S(1)} collective-permute-done((f32[6,16,64]{2,1,0:T(8,128)S(1)}, f32[6,16,64]{2,1,0:T(8,128)S(1)}, u32[]{:S(2)}, u32[]{:S(2)}) %collective-permute-start.19) | collective-permute-done | bytes 24608 | tf_op jit(solution)/shard_map/ppermute | solution.py:281
  157.4 1.4 collective-permute-done.20
  159.0 1.3 fusion.25
  160.3 3.2 %collective-permute-start.22 = (f32[4,512]{1,0:T(4,128)S(1)}, f32[4,512]{1,0:T(4,128)S(1)}, u32[]{:S(2)}, u32[]{:S(2)}) collective-permute-start(f32[4,512]{1,0:T(4,128)S(1)} %fusion.25), channel_id=1, source_target_pairs={{0,12},{4,0},{8,4},{12,8},{1,13},{5,1},{9,5},{13,9},{2,14},{6,2},{... | collective-permute-start | bytes 24584 | tf_op jit(solution)/shard_map/ppermute | solution.py:15
  164.9 3.3 %collective-permute-done.23 = f32[4,512]{1,0:T(4,128)S(1)} collective-permute-done((f32[4,512]{1,0:T(4,128)S(1)}, f32[4,512]{1,0:T(4,128)S(1)}, u32[]{:S(2)}, u32[]{:S(2)}) %collective-permute-start.23) | collective-permute-done | bytes 8224 | tf_op jit(solution)/shard_map/ppermute | solution.py:15
  168.1 1.1 collective-permute-done.24
  169.3 0.9 fusion.21
  (110 shorter events, 8.1 us)
Async XLA Ops:
  0.6 158.3 %copy-start = (bf16[3,16,64,512]{3,2,1,0:T(8,128)(2,1)S(1)}, bf16[3,16,64,512]{3,2,1,0:T(8,128)(2,1)}, u32[]{:S(2)}) copy-start(bf16[3,16,64,512]{3,2,1,0:T(8,128)(2,1)} %param.17) | copy-start | bytes 9437188
  0.6 19.2 %collective-permute-start = (bf16[256,1280]{1,0:T(8,128)(2,1)}, bf16[256,1280]{1,0:T(8,128)(2,1)}, u32[]{:S(2)}, u32[]{:S(2)}) collective-permute-start(bf16[256,1280]{1,0:T(8,128)(2,1)} %bitcast.97), channel_id=1, source_target_pairs={{0,8},{1,12},{2,0},{3,4},{4,9},{5,13},{6,1},{7,5},{10,2},{11,6},{8... | collective-permute-start | bytes 1966088 | tf_op jit(solution)/shard_map/ppermute | solution.py:66
  4.7 15.1 %collective-permute-start.1 = (bf16[256,1280]{1,0:T(8,128)(2,1)}, bf16[256,1280]{1,0:T(8,128)(2,1)}, u32[]{:S(2)}, u32[]{:S(2)}) collective-permute-start(bf16[256,1280]{1,0:T(8,128)(2,1)} %bitcast.98), channel_id=1, source_target_pairs={{0,0},{1,4},{2,8},{3,12},{4,1},{5,5},{6,9},{7,13},{10,10},{11,14},... | collective-permute-start | bytes 1966088 | tf_op jit(solution)/shard_map/ppermute | solution.py:66
  11.3 8.3 %collective-permute-start.2 = (s32[2]{0:T(128)}, s32[2]{0:T(128)S(1)}, u32[]{:S(2)}, u32[]{:S(2)}) collective-permute-start(s32[2]{0:T(128)} %param.19), channel_id=1, source_target_pairs={{0,2},{2,0},{1,3},{3,1},{4,6},{6,4},{5,7},{7,5},{8,10},{10,8},{9,1... | collective-permute-start | bytes 32 | tf_op jit(solution)/shard_map/ppermute | solution.py:15
  11.3 8.3 %copy-start.8 = (s32[2]{0:T(128)S(1)}, s32[2]{0:T(128)}, u32[]{:S(2)}) copy-start(s32[2]{0:T(128)} %param.19) | copy-start | bytes 28
  19.9 16.7 %slice-start.6 = ((s8[10485760]{0:T(1024)(128)(4,1)}), s8[4194304]{0:T(1024)(128)(4,1)S(1)}, s32[]{:S(2)}) async-start(s8[10485760]{0:T(1024)(128)(4,1)} %bitcast.106), calls=%async_computation.6 | async-start | bytes 8388608
  21.4 15.2 %slice-start.7 = ((s8[10485760]{0:T(1024)(128)(4,1)}), s8[4194304]{0:T(1024)(128)(4,1)S(1)}, s32[]{:S(2)}) async-start(s8[10485760]{0:T(1024)(128)(4,1)} %bitcast.106), calls=%async_computation.7 | async-start | bytes 8388608
  21.4 15.2 %slice-start.8 = ((s8[10485760]{0:T(1024)(128)(4,1)}), s8[2097152]{0:T(1024)(128)(4,1)S(1)}, s32[]{:S(2)}) async-start(s8[10485760]{0:T(1024)(128)(4,1)} %bitcast.106), calls=%async_computation.8 | async-start | bytes 4194304
  29.0 25.6 %collective-permute-start.5 = (f16[256,2048]{1,0:T(8,128)(2,1)S(1)}, f16[256,2048]{1,0:T(8,128)(2,1)S(1)}, u32[]{:S(2)}, u32[]{:S(2)}) collective-permute-start(f16[256,2048]{1,0:T(8,128)(2,1)S(1)} %constant_dynamic-slice_fusion.5), channel_id=1, source_target_pairs={{0,1},{1,0},{2,3},{3,2},{4,5},{5,4},{6,7},{7,6},{8,9},{9,8},{10,11... | collective-permute-start | bytes 3145736 | tf_op jit(solution)/shard_map/ppermute | solution.py:15
  36.6 23.5 %slice-start.3 = ((s8[10485760]{0:T(1024)(128)(4,1)}), s8[2097152]{0:T(1024)(128)(4,1)S(1)}, s32[]{:S(2)}) async-start(s8[10485760]{0:T(1024)(128)(4,1)} %bitcast.104), calls=%async_computation.3 | async-start | bytes 4194304
  36.6 23.5 %slice-start.4 = ((s8[10485760]{0:T(1024)(128)(4,1)}), s8[4194304]{0:T(1024)(128)(4,1)S(1)}, s32[]{:S(2)}) async-start(s8[10485760]{0:T(1024)(128)(4,1)} %bitcast.104), calls=%async_computation.4 | async-start | bytes 8388608
  39.7 1.1 copy-start.7
  40.0 20.1 %slice-start.5 = ((s8[10485760]{0:T(1024)(128)(4,1)}), s8[4194304]{0:T(1024)(128)(4,1)S(1)}, s32[]{:S(2)}) async-start(s8[10485760]{0:T(1024)(128)(4,1)} %bitcast.104), calls=%async_computation.5 | async-start | bytes 8388608
  40.0 15.0 %collective-permute-start.6 = (f16[256,2048]{1,0:T(8,128)(2,1)S(1)}, f16[256,2048]{1,0:T(8,128)(2,1)S(1)}, u32[]{:S(2)}, u32[]{:S(2)}) collective-permute-start(f16[256,2048]{1,0:T(8,128)(2,1)S(1)} %constant_dynamic-slice_fusion.4), channel_id=1, source_target_pairs={{0,1},{1,0},{2,3},{3,2},{4,5},{5,4},{6,7},{7,6},{8,9},{9,8},{10,11... | collective-permute-start | bytes 3145736 | tf_op jit(solution)/shard_map/ppermute | solution.py:15
  40.8 32.4 %collective-permute-start.3 = (bf16[256,1280]{1,0:T(8,128)(2,1)S(1)}, bf16[256,1280]{1,0:T(8,128)(2,1)S(1)}, u32[]{:S(2)}, u32[]{:S(2)}) collective-permute-start(bf16[256,1280]{1,0:T(8,128)(2,1)S(1)} %bitcast.95), channel_id=1, source_target_pairs={{0,8},{1,12},{2,0},{3,4},{4,9},{5,13},{6,1},{7,5},{10,2},{11,6},{8... | collective-permute-start | bytes 1966088 | tf_op jit(solution)/shard_map/ppermute | solution.py:66
  53.9 19.4 %collective-permute-start.4 = (bf16[256,1280]{1,0:T(8,128)(2,1)S(1)}, bf16[256,1280]{1,0:T(8,128)(2,1)S(1)}, u32[]{:S(2)}, u32[]{:S(2)}) collective-permute-start(bf16[256,1280]{1,0:T(8,128)(2,1)S(1)} %bitcast.96), channel_id=1, source_target_pairs={{0,0},{1,4},{2,8},{3,12},{4,1},{5,5},{6,9},{7,13},{10,10},{11,14},... | collective-permute-start | bytes 1966088 | tf_op jit(solution)/shard_map/ppermute | solution.py:66
  57.2 62.3 %collective-permute-start.7 = (f16[2,256,2048]{2,1,0:T(8,128)(2,1)}, f16[2,256,2048]{2,1,0:T(8,128)(2,1)}, u32[]{:S(2)}, u32[]{:S(2)}) collective-permute-start(f16[2,256,2048]{2,1,0:T(8,128)(2,1)} %fusion.4), channel_id=1, source_target_pairs={{0,2},{2,0},{1,3},{3,1},{4,6},{6,4},{5,7},{7,5},{8,10},{10,8},{9,1... | collective-permute-start | bytes 6291464 | tf_op jit(solution)/shard_map/ppermute | solution.py:15
  60.0 13.4 %slice-start = ((s8[10485760]{0:T(1024)(128)(4,1)}), s8[4194304]{0:T(1024)(128)(4,1)S(1)}, s32[]{:S(2)}) async-start(s8[10485760]{0:T(1024)(128)(4,1)} %bitcast.91), calls=%async_computation | async-start | bytes 8388608
  60.1 13.4 %slice-start.1 = ((s8[10485760]{0:T(1024)(128)(4,1)}), s8[4194304]{0:T(1024)(128)(4,1)S(1)}, s32[]{:S(2)}) async-start(s8[10485760]{0:T(1024)(128)(4,1)} %bitcast.91), calls=%async_computation.1 | async-start | bytes 8388608
  60.1 13.4 %slice-start.2 = ((s8[10485760]{0:T(1024)(128)(4,1)}), s8[2097152]{0:T(1024)(128)(4,1)S(1)}, s32[]{:S(2)}) async-start(s8[10485760]{0:T(1024)(128)(4,1)} %bitcast.91), calls=%async_computation.2 | async-start | bytes 4194304
  63.2 23.7 %copy-start.6 = (f16[256,4096]{1,0:T(8,128)(2,1)}, f16[256,4096]{1,0:T(8,128)(2,1)S(1)}, u32[]{:S(2)}) copy-start(f16[256,4096]{1,0:T(8,128)(2,1)S(1)} %fusion.2) | copy-start | bytes 6291460
  73.3 10.1 %slice-start.9 = ((s8[10485760]{0:T(1024)(128)(4,1)}), s8[4194304]{0:T(1024)(128)(4,1)S(1)}, s32[]{:S(2)}) async-start(s8[10485760]{0:T(1024)(128)(4,1)} %bitcast.108), calls=%async_computation.9 | async-start | bytes 8388608
  73.5 10.0 %slice-start.10 = ((s8[10485760]{0:T(1024)(128)(4,1)}), s8[4194304]{0:T(1024)(128)(4,1)S(1)}, s32[]{:S(2)}) async-start(s8[10485760]{0:T(1024)(128)(4,1)} %bitcast.108), calls=%async_computation.10 | async-start | bytes 8388608
  73.5 10.0 %slice-start.11 = ((s8[10485760]{0:T(1024)(128)(4,1)}), s8[2097152]{0:T(1024)(128)(4,1)S(1)}, s32[]{:S(2)}) async-start(s8[10485760]{0:T(1024)(128)(4,1)} %bitcast.108), calls=%async_computation.11 | async-start | bytes 4194304
  81.0 7.6 %copy-start.1 = (f32[512,4096]{1,0:T(8,128)}, f32[512,4096]{1,0:T(8,128)S(1)}, u32[]{:S(2)}) copy-start(f32[512,4096]{1,0:T(8,128)S(1)} %shard_map.113) | copy-start | bytes 25165828
  81.2 7.3 %collective-permute-start.9 = (f16[256,2048]{1,0:T(8,128)(2,1)S(1)}, f16[256,2048]{1,0:T(8,128)(2,1)S(1)}, u32[]{:S(2)}, u32[]{:S(2)}) collective-permute-start(f16[256,2048]{1,0:T(8,128)(2,1)S(1)} %multiply_convert_fusion.2), channel_id=1, source_target_pairs={{0,1},{1,0},{2,3},{3,2},{4,5},{5,4},{6,7},{7,6},{8,9},{9,8},{10,11... | collective-permute-start | bytes 3145736 | tf_op jit(solution)/shard_map/ppermute | solution.py:15
  86.6 1.6 copy-start.4
  86.8 15.6 %collective-permute-start.11 = (f16[256,2048]{1,0:T(8,128)(2,1)S(1)}, f16[256,2048]{1,0:T(8,128)(2,1)}, u32[]{:S(2)}, u32[]{:S(2)}) collective-permute-start(f16[256,2048]{1,0:T(8,128)(2,1)S(1)} %constant_dynamic-slice_fusion.3), channel_id=1, source_target_pairs={{0,1},{1,0},{2,3},{3,2},{4,5},{5,4},{6,7},{7,6},{8,9},{9,8},{10,11... | collective-permute-start | bytes 3145736 | tf_op jit(solution)/shard_map/ppermute | solution.py:15
  88.2 16.6 %collective-permute-start.12 = (f16[256,2048]{1,0:T(8,128)(2,1)}, f16[256,2048]{1,0:T(8,128)(2,1)}, u32[]{:S(2)}, u32[]{:S(2)}) collective-permute-start(f16[256,2048]{1,0:T(8,128)(2,1)} %constant_dynamic-slice_fusion.2), channel_id=1, source_target_pairs={{0,1},{1,0},{2,3},{3,2},{4,5},{5,4},{6,7},{7,6},{8,9},{9,8},{10,11... | collective-permute-start | bytes 3145736 | tf_op jit(solution)/shard_map/ppermute | solution.py:15
  88.6 16.2 %copy-start.9 = (s32[2]{0:T(128)S(1)}, s32[2]{0:T(128)}, u32[]{:S(2)}) copy-start(s32[2]{0:T(128)} %param.18) | copy-start | bytes 28
  90.0 15.8 %collective-permute-start.13 = (f16[256,192]{0,1:T(8,128)(2,1)S(1)}, f16[256,192]{0,1:T(8,128)(2,1)S(1)}, u32[]{:S(2)}, u32[]{:S(2)}) collective-permute-start(f16[256,192]{0,1:T(8,128)(2,1)S(1)} %multiply_convert_fusion.5), channel_id=1, source_target_pairs={{0,4},{4,8},{8,12},{12,0},{1,5},{5,9},{9,13},{13,1},{2,6},{6,10},{... | collective-permute-start | bytes 294920 | tf_op jit(solution)/shard_map/ppermute | solution.py:15
  97.3 12.1 %collective-permute-start.14 = (f16[256,192]{0,1:T(8,128)(2,1)S(1)}, f16[256,192]{0,1:T(8,128)(2,1)}, u32[]{:S(2)}, u32[]{:S(2)}) collective-permute-start(f16[256,192]{0,1:T(8,128)(2,1)S(1)} %multiply_convert_fusion.5), channel_id=1, source_target_pairs={{0,8},{4,12},{8,0},{12,4},{1,9},{5,13},{9,1},{13,5},{2,10},{6,14},... | collective-permute-start | bytes 294920 | tf_op jit(solution)/shard_map/ppermute | solution.py:15
  102.4 7.0 %collective-permute-start.15 = (f16[256,192]{0,1:T(8,128)(2,1)S(1)}, f16[256,192]{0,1:T(8,128)(2,1)}, u32[]{:S(2)}, u32[]{:S(2)}) collective-permute-start(f16[256,192]{0,1:T(8,128)(2,1)S(1)} %multiply_convert_fusion.5), channel_id=1, source_target_pairs={{0,12},{4,0},{8,4},{12,8},{1,13},{5,1},{9,5},{13,9},{2,14},{6,2},{... | collective-permute-start | bytes 294920 | tf_op jit(solution)/shard_map/ppermute | solution.py:15
  104.8 36.4 %collective-permute-start.10 = (f16[256,2048]{1,0:T(8,128)(2,1)}, f16[256,2048]{1,0:T(8,128)(2,1)}, u32[]{:S(2)}, u32[]{:S(2)}) collective-permute-start(f16[256,2048]{1,0:T(8,128)(2,1)} %multiply_convert_fusion.1), channel_id=1, source_target_pairs={{0,2},{2,0},{1,3},{3,1},{4,6},{6,4},{5,7},{7,5},{8,10},{10,8},{9,1... | collective-permute-start | bytes 3145736 | tf_op jit(solution)/shard_map/ppermute | solution.py:15
  122.6 2.2 %copy-start.5 = (f16[256,4096]{1,0:T(8,128)(2,1)S(1)}, f16[256,4096]{1,0:T(8,128)(2,1)}, u32[]{:S(2)}) copy-start(f16[256,4096]{1,0:T(8,128)(2,1)} %copy-done.4) | copy-start | bytes 6291460
  124.5 7.1 %collective-permute-start.8 = (f16[256,2048]{1,0:T(8,128)(2,1)S(1)}, f16[256,2048]{1,0:T(8,128)(2,1)S(1)}, u32[]{:S(2)}, u32[]{:S(2)}) collective-permute-start(f16[256,2048]{1,0:T(8,128)(2,1)S(1)} %multiply_convert_fusion.3), channel_id=1, source_target_pairs={{0,1},{1,0},{2,3},{3,2},{4,5},{5,4},{6,7},{7,6},{8,9},{9,8},{10,11... | collective-permute-start | bytes 3145736 | tf_op jit(solution)/shard_map/ppermute | solution.py:15
  131.6 12.1 %copy-start.2 = (bf16[2048,64]{1,0:T(8,128)(2,1)S(1)}, bf16[2048,64]{1,0:T(8,128)(2,1)}, u32[]{:S(2)}) copy-start(bf16[2048,64]{1,0:T(8,128)(2,1)} %copy.21.refs_2_) | copy-start | bytes 786436
  131.6 12.1 %copy-start.3 = (bf16[2048,64]{1,0:T(8,128)(2,1)S(1)}, bf16[2048,64]{1,0:T(8,128)(2,1)}, u32[]{:S(2)}) copy-start(bf16[2048,64]{1,0:T(8,128)(2,1)} %copy.22.refs_3_) | copy-start | bytes 786436
  144.9 6.4 %collective-permute-start.16 = (f32[6,16,64]{2,1,0:T(8,128)S(1)}, f32[6,16,64]{2,1,0:T(8,128)}, u32[]{:S(2)}, u32[]{:S(2)}) collective-permute-start(f32[6,16,64]{2,1,0:T(8,128)S(1)} %get-tuple-element.38), channel_id=1, source_target_pairs={{0,4},{4,8},{8,12},{12,0},{1,5},{5,9},{9,13},{13,1},{2,6},{6,10},{... | collective-permute-start | bytes 73736 | tf_op jit(solution)/shard_map/ppermute | solution.py:15
  145.0 7.1 %collective-permute-start.17 = (f32[6,16,64]{2,1,0:T(8,128)S(1)}, f32[6,16,64]{2,1,0:T(8,128)}, u32[]{:S(2)}, u32[]{:S(2)}) collective-permute-start(f32[6,16,64]{2,1,0:T(8,128)S(1)} %get-tuple-element.40), channel_id=1, source_target_pairs={{0,8},{4,12},{8,0},{12,4},{1,9},{5,13},{9,1},{13,5},{2,10},{6,14},... | collective-permute-start | bytes 73736 | tf_op jit(solution)/shard_map/ppermute | solution.py:15
  147.4 4.8 %collective-permute-start.18 = (f32[6,16,64]{2,1,0:T(8,128)S(1)}, f32[6,16,64]{2,1,0:T(8,128)}, u32[]{:S(2)}, u32[]{:S(2)}) collective-permute-start(f32[6,16,64]{2,1,0:T(8,128)S(1)} %get-tuple-element.39), channel_id=1, source_target_pairs={{0,12},{4,0},{8,4},{12,8},{1,13},{5,1},{9,5},{13,9},{2,14},{6,2},{... | collective-permute-start | bytes 73736 | tf_op jit(solution)/shard_map/ppermute | solution.py:15
  153.0 2.2 %collective-permute-start.21 = (f32[6,16,64]{2,1,0:T(8,128)S(1)}, f32[6,16,64]{2,1,0:T(8,128)S(1)}, u32[]{:S(2)}, u32[]{:S(2)}) collective-permute-start(f32[6,16,64]{2,1,0:T(8,128)S(1)} %fusion.19), channel_id=1, source_target_pairs={{0,1},{1,0},{2,3},{3,2},{4,5},{5,4},{6,7},{7,6},{8,9},{9,8},{10,11... | collective-permute-start | bytes 73736 | tf_op jit(solution)/shard_map/ppermute | solution.py:281
  153.1 4.4 %collective-permute-start.19 = (f32[6,16,64]{2,1,0:T(8,128)S(1)}, f32[6,16,64]{2,1,0:T(8,128)S(1)}, u32[]{:S(2)}, u32[]{:S(2)}) collective-permute-start(f32[6,16,64]{2,1,0:T(8,128)S(1)} %fusion.19), channel_id=1, source_target_pairs={{0,2},{1,3},{2,0},{3,1},{4,6},{5,7},{6,4},{7,5},{8,10},{9,11},{10,... | collective-permute-start | bytes 73736 | tf_op jit(solution)/shard_map/ppermute | solution.py:281
  155.1 3.7 %collective-permute-start.20 = (f32[6,16,64]{2,1,0:T(8,128)S(1)}, f32[6,16,64]{2,1,0:T(8,128)S(1)}, u32[]{:S(2)}, u32[]{:S(2)}) collective-permute-start(f32[6,16,64]{2,1,0:T(8,128)S(1)} %fusion.19), channel_id=1, source_target_pairs={{0,3},{1,2},{2,1},{3,0},{4,7},{5,6},{6,5},{7,4},{8,11},{9,10},{10,... | collective-permute-start | bytes 73736 | tf_op jit(solution)/shard_map/ppermute | solution.py:281
  160.3 4.6 %collective-permute-start.22 = (f32[4,512]{1,0:T(4,128)S(1)}, f32[4,512]{1,0:T(4,128)S(1)}, u32[]{:S(2)}, u32[]{:S(2)}) collective-permute-start(f32[4,512]{1,0:T(4,128)S(1)} %fusion.25), channel_id=1, source_target_pairs={{0,12},{4,0},{8,4},{12,8},{1,13},{5,1},{9,5},{13,9},{2,14},{6,2},{... | collective-permute-start | bytes 24584 | tf_op jit(solution)/shard_map/ppermute | solution.py:15
  163.6 4.5 %collective-permute-start.23 = (f32[4,512]{1,0:T(4,128)S(1)}, f32[4,512]{1,0:T(4,128)S(1)}, u32[]{:S(2)}, u32[]{:S(2)}) collective-permute-start(f32[4,512]{1,0:T(4,128)S(1)} %fusion.25), channel_id=1, source_target_pairs={{0,8},{4,12},{8,0},{12,4},{1,9},{5,13},{9,1},{13,5},{2,10},{6,14},... | collective-permute-start | bytes 24584 | tf_op jit(solution)/shard_map/ppermute | solution.py:15
  163.8 5.4 %collective-permute-start.24 = (f32[4,512]{1,0:T(4,128)S(1)}, f32[4,512]{1,0:T(4,128)S(1)}, u32[]{:S(2)}, u32[]{:S(2)}) collective-permute-start(f32[4,512]{1,0:T(4,128)S(1)} %fusion.25), channel_id=1, source_target_pairs={{0,4},{4,8},{8,12},{12,0},{1,5},{5,9},{9,13},{13,1},{2,6},{6,10},{... | collective-permute-start | bytes 24584 | tf_op jit(solution)/shard_map/ppermute | solution.py:15
